TPU v7x, 32 devices: a whole 2x2x4 slice. The times are simulated.
32 devices in a mesh: shard: 16 (over z, y, x), rep: 2 (over core).
Axes of the slice: x: 2, y: 2, z: 4, core: 2. Of those that a mesh axis runs over, the one named last changes fastest.
Arguments:
- images: bfloat16 [32, 8, 16, 768], P(('shard', 'rep')), may hold values from -6 to 6
- cotangent: bfloat16 [32, 8, 16, 1536], P(('shard', 'rep')), may hold values from -6 to 6
- depthwise_weight: bfloat16 [768, 49], P('shard'), may hold values from -0.875 to 0.875
- norm_gain: bfloat16 [768], P('shard'), may hold values from 0.5 to 1.5
- norm_bias: bfloat16 [768], P('shard'), may hold values from -3 to 3
- up_weight: bfloat16 [768, 1536], P('shard'), may hold values from -0.21875 to 0.21875
Outputs:
- grad_images: bfloat16 [32, 8, 16, 768], P(('shard', 'rep'))
- grad_up: float32 [768, 1536], P('shard')
- grad_depthwise: float32 [768, 49], P('shard')
- grad_gain: float32 [768], P('shard')
- grad_bias: float32 [768], P('shard')
All inputs are finite; a program needn't handle non-finite values.
Results may differ from a plain program's by a relative error of at most 0.0056.
Values may be sent and summed in bfloat16 or wider, within the bound.
No kernel may reach another device: no remote copies, remote signals or barrier semaphores. Data moves between devices by JAX's collectives and lax.ppermute only.
A program may use at most 128 MiB of HBM per device.

v0:
```python
import math

import jax
import jax.numpy as jnp
from jax import lax
from jax.sharding import PartitionSpec as P

KS = 7


norm_eps = 1e-06


def gelu_slope(inputs):
    cumulative = 0.5 * (1.0 + lax.erf(inputs * 0.7071067811865476))
    return cumulative + inputs * jnp.exp(-0.5 * inputs * inputs) * 0.3989422804014327


def pad_tile(source, margin):
    return jnp.pad(source, ((0, 0), (margin, margin), (margin, margin), (0, 0)))


def depthwise(source, kernel, extent):
    margin = extent // 2
    height, breadth = (source.shape[1], source.shape[2])
    padded = pad_tile(source, margin)
    running = jnp.zeros_like(source)
    for down_step in range(extent):
        for across in range(extent):
            running = (
                running
                + padded[:, down_step : down_step + height, across : across + breadth, :]
                * kernel[:, down_step * extent + across]
            )
    return running


def depthwise_back(grad_conv, kernel, extent):
    margin = extent // 2
    height, breadth = (grad_conv.shape[1], grad_conv.shape[2])
    padded = pad_tile(grad_conv, margin)
    running = jnp.zeros_like(grad_conv)
    for down_step in range(extent):
        for across in range(extent):
            top = 2 * margin - down_step
            left = 2 * margin - across
            running = (
                running
                + padded[:, top : top + height, left : left + breadth, :]
                * kernel[:, down_step * extent + across]
            )
    return running


def kernel_grad(source, grad_conv, extent):
    margin = extent // 2
    height, breadth = (source.shape[1], source.shape[2])
    padded = pad_tile(source, margin)
    columns = []
    for down_step in range(extent):
        for across in range(extent):
            columns.append(
                jnp.sum(
                    grad_conv
                    * padded[:, down_step : down_step + height, across : across + breadth, :],
                    axis=(0, 1, 2),
                )
            )
    return jnp.stack(columns, axis=1)


def local_pass(x_tile, cot_tile, dw_weight, gain, bias, weight, extent):
    source = x_tile.astype(jnp.float32)
    kernel = dw_weight.astype(jnp.float32)
    conv_out = depthwise(source, kernel, extent)
    average = jnp.mean(conv_out, axis=-1, keepdims=True)
    centered = conv_out - average
    inv_std = lax.rsqrt(jnp.mean(centered * centered, axis=-1, keepdims=True) + norm_eps)
    whitened = centered * inv_std
    gain_f = gain.astype(jnp.float32)
    normed = (whitened * gain_f + bias.astype(jnp.float32)).astype(jnp.bfloat16)
    depth = source.shape[-1]
    hidden = weight.shape[1]
    flattened = normed.reshape(-1, depth)
    pre_act = jnp.dot(flattened, weight, preferred_element_type=jnp.float32)
    grad_pre = (cot_tile.reshape(-1, hidden).astype(jnp.float32) * gelu_slope(pre_act)).astype(
        jnp.bfloat16
    )
    grad_normed = lax.dot_general(
        grad_pre, weight, (((1,), (1,)), ((), ())), preferred_element_type=jnp.float32
    ).reshape(conv_out.shape)
    weight_term = lax.dot_general(
        flattened, grad_pre, (((0,), (0,)), ((), ())), preferred_element_type=jnp.float32
    )
    gain_term = jnp.sum(grad_normed * whitened, axis=(0, 1, 2))
    bias_term = jnp.sum(grad_normed, axis=(0, 1, 2))
    grad_white = grad_normed * gain_f
    grad_conv = inv_std * (
        grad_white
        - jnp.mean(grad_white, axis=-1, keepdims=True)
        - whitened * jnp.mean(grad_white * whitened, axis=-1, keepdims=True)
    )
    kernel_term = kernel_grad(source, grad_conv, extent)
    grad_input = depthwise_back(grad_conv, kernel, extent).astype(jnp.bfloat16)
    return (grad_input, weight_term, kernel_term, gain_term, bias_term)


def body(images, cotangent, depthwise_weight, norm_gain, norm_bias, up_weight):
    weight, kernel_rows, gain_rows, bias_rows = (
        lax.all_gather(up_weight, "shard", axis=0, tiled=True),
        lax.all_gather(depthwise_weight, "shard", axis=0, tiled=True),
        lax.all_gather(norm_gain, "shard", axis=0, tiled=True),
        lax.all_gather(norm_bias, "shard", axis=0, tiled=True),
    )
    grad_input, weight_term, kernel_term, gain_term, bias_term = local_pass(
        images, cotangent, kernel_rows, gain_rows, bias_rows, weight, KS
    )
    depth = weight.shape[0]
    hidden = weight.shape[1]
    taps = KS * KS
    padding = jnp.zeros((depth, 64 - taps - 2), jnp.float32)
    small_term = jnp.concatenate(
        [kernel_term, gain_term[:, None], bias_term[:, None], padding], axis=1
    )
    pixels = (
        images.shape[0]
        * images.shape[1]
        * images.shape[2]
        * lax.axis_size("shard")
        * lax.axis_size("rep")
    )
    factor = 1.0 / math.sqrt(pixels)
    own_rows = depth // lax.axis_size("shard")
    weight_lines = weight_term.reshape(depth * hidden // 128, 128)
    weight_lines, small_share = (
        lax.psum_scatter(weight_lines, "shard", scatter_dimension=0, tiled=True),
        lax.psum_scatter(small_term, "shard", scatter_dimension=0, tiled=True),
    )
    weight_lines, small_share = lax.psum((weight_lines, small_share), "rep")
    weight_share = weight_lines.reshape(own_rows, hidden)
    grad_up = weight_share * factor
    grad_depthwise = small_share[:, :taps] * factor
    grad_gain = small_share[:, taps] * factor
    grad_bias = small_share[:, taps + 1] * factor
    return (grad_input, grad_up, grad_depthwise, grad_gain, grad_bias)


def solution(mesh):
    placed = (
        P(("shard", "rep"), None, None, None),
        P(("shard", "rep"), None, None, None),
        P("shard", None),
        P("shard"),
        P("shard"),
        P("shard", None),
    )
    return jax.shard_map(
        body,
        mesh=mesh,
        in_specs=placed,
        out_specs=(
            P(("shard", "rep"), None, None, None),
            P("shard", None),
            P("shard", None),
            P("shard"),
            P("shard"),
        ),
        check_vma=False,
    )
```

profile of v0, /device:TPU:0, one launch (start us, length us, event | category | flops | bytes accessed | tf_op | source)
XLA Modules:
  0.0 461.8 jit_solution(14171042898868137138)
XLA Ops:
  8.0 1.0 convert_element_type.31
  8.9 44.0 %all_gather.12 = bf16[768,49]{1,0:T(8,128)(2,1)S(1)} all-gather(bf16[48,49]{1,0:T(8,128)(2,1)} %param.8), channel_id=1, replica_groups=mesh['shard'=16,'rep'=2] {'shard'}, dimensions={0}, use_global_device_ids=true | all-gather | bytes 79968 | tf_op jit(solution)/shard_map/all_gather | solution.py:111
  53.0 1.2 dynamic-slice
  54.9 0.8 dynamic-update-slice.1
  55.7 0.8 dynamic-update-slice
  56.6 37.0 %all-reduce.4 = (bf16[768]{0:T(1024)(128)(2,1)S(1)}, bf16[768]{0:T(1024)(128)(2,1)S(1)}) all-reduce(bf16[768]{0:T(1024)(128)(2,1)S(1)} %dynamic-update-slice.1, bf16[768]{0:T(1024)(128)(2,1)S(1)} %dynamic-update-slice), channel_id=1, replica_groups=mesh['shard'=16,'rep'=2] {'shard'}, use_global_device_ids=true, to_apply=%add.3 | all-reduce | flops 1536 | bytes 6144
  93.6 2.3 slice_reduce_fusion.46
  95.9 3.8 slice_reduce_fusion.48
  100.0 4.5 slice_reduce_fusion.47
  104.9 4.2 fusion.106
  110.2 2.5 fusion.5
  112.7 1.5 fusion.105
  118.4 0.9 stack.204
  119.3 0.9 stack.205
  120.2 0.9 stack.206
  121.2 0.9 stack.207
  122.1 0.9 stack.208
  123.0 0.9 stack.209
  123.9 0.9 stack.210
  124.8 0.9 stack.211
  125.7 0.9 stack.212
  126.7 0.9 stack.213
  127.6 0.9 stack.214
  128.5 0.9 stack.215
  129.4 0.9 stack.216
  130.3 0.9 stack.217
  131.3 0.9 stack.218
  132.2 0.9 stack.219
  133.1 0.9 stack.220
  134.0 0.9 stack.221
  135.0 0.9 stack.222
  135.9 0.9 stack.223
  136.8 1.0 stack.224
  137.8 0.9 stack.225
  138.7 1.0 stack.226
  139.6 0.9 stack.227
  140.6 0.9 stack.228
  141.5 0.9 stack.229
  142.4 0.9 stack.230
  143.3 0.9 stack.231
  144.3 0.9 stack.232
  145.2 0.9 stack.233
  146.1 0.9 stack.234
  147.0 0.9 stack.235
  148.0 0.9 stack.236
  148.9 0.9 stack.237
  149.8 0.9 stack.238
  150.7 0.9 stack.239
  151.7 0.9 stack.240
  152.6 0.9 stack.241
  153.5 0.9 stack.242
  154.4 0.9 stack.243
  155.3 0.9 stack.244
  156.3 0.9 broadcast_in_dim.9
  157.2 0.9 broadcast_in_dim.20
  158.9 13.1 %concatenate.3 = f32[768,64]{1,0:T(8,128)} concatenate(f32[768,1]{1,0:T(8,128)S(1)} %stack.196, f32[768,1]{1,0:T(8,128)S(1)} %stack.197, f32[768,1]{1,0:T(8,128)S(1)} %stack.198, f32[768,1]{1,0:T(8,128)S(1)} %stack.199, f32[768,1]{1,0:T(8,128)S(1)} %stack.200, f32[768,1]{1,0:T(8,128)S(1)} %stack.201, f32[768,1]{1,0:T(8,128)S(1)} %stack.202, f32[768,1]{1,0:T(8,128)S(1)} %stack.203, ...), dimensions={1} | concatenate | bytes 393216 | tf_op jit(solution)/shard_map/concatenate | solution.py:122
  172.1 4.1 fusion.107
  176.2 5.6 %reshape.248 = f32[9216,128]{1,0:T(8,128)} reshape(f32[768,1536]{1,0:T(8,128)} %fusion.107) | data formatting | bytes 9437184 | tf_op jit(solution)/shard_map/reshape | solution.py:134
  182.8 3.8 fusion.97
  186.6 104.9 %reduce-scatter.5.cloned.1.call-done = f32[48,64]{1,0:T(8,128)} async-done(((f32[768,64]{1,0:T(8,128)}), f32[48,64]{1,0:T(8,128)}) %reduce-scatter.5.cloned.1.call-update) | async-done | bytes 12304 | tf_op jit(solution)/shard_map/reduce_scatter | solution.py:137
  291.5 4.0 psum.15
  295.6 138.3 %reduce-scatter.3.cloned.1.call-done = f32[576,128]{1,0:T(8,128)} async-done(((f32[9216,128]{1,0:T(8,128)}), f32[576,128]{1,0:T(8,128)}) %reduce-scatter.3.cloned.1.call-update) | async-done | bytes 294928 | tf_op jit(solution)/shard_map/reduce_scatter | solution.py:136
  435.2 18.3 %all-reduce.7.cloned.1.call-done = f32[576,128]{1,0:T(8,128)} async-done(((f32[576,128]{1,0:T(8,128)}), f32[576,128]{1,0:T(8,128)}) %all-reduce.7.cloned.1.call-update) | async-done | bytes 294928 | tf_op jit(solution)/shard_map/psum | solution.py:139
  453.5 1.0 broadcast_multiply_fusion
  (207 shorter events, 9.7 us)
Async XLA Ops:
  7.2 102.4 %all-gather.2.cloned.1.call-start = ((), (), s32[]{:S(2)}) async-start(), calls=%async_computation.2 | async-start | bytes 2506752 | tf_op jit(solution)/shard_map/all_gather | solution.py:110
  7.9 283.6 %reduce-scatter.5.cloned.1.call-start = ((), (), s32[]{:S(2)}) async-start(), calls=%async_computation.5 | async-start | bytes 417792 | tf_op jit(solution)/shard_map/reduce_scatter | solution.py:137
  95.9 8.7 %copy-start.4 = (f32[768]{0:T(1024)}, f32[768]{0:T(1024)S(1)}, u32[]{:S(2)}) copy-start(f32[768]{0:T(1024)S(1)} %get-tuple-element.100) | copy-start | bytes 9220
  95.9 8.7 %copy-start.6 = (f32[768]{0:T(1024)}, f32[768]{0:T(1024)S(1)}, u32[]{:S(2)}) copy-start(f32[768]{0:T(1024)S(1)} %get-tuple-element.101) | copy-start | bytes 9220
  95.9 8.7 %copy-start.8 = (f32[768]{0:T(1024)}, f32[768]{0:T(1024)S(1)}, u32[]{:S(2)}) copy-start(f32[768]{0:T(1024)S(1)} %get-tuple-element.102) | copy-start | bytes 9220
  95.9 8.7 %copy-start.10 = (f32[768]{0:T(1024)}, f32[768]{0:T(1024)S(1)}, u32[]{:S(2)}) copy-start(f32[768]{0:T(1024)S(1)} %get-tuple-element.103) | copy-start | bytes 9220
  95.9 8.7 %copy-start.12 = (f32[768]{0:T(1024)}, f32[768]{0:T(1024)S(1)}, u32[]{:S(2)}) copy-start(f32[768]{0:T(1024)S(1)} %get-tuple-element.104) | copy-start | bytes 9220
  95.9 8.7 %copy-start.14 = (f32[768]{0:T(1024)}, f32[768]{0:T(1024)S(1)}, u32[]{:S(2)}) copy-start(f32[768]{0:T(1024)S(1)} %get-tuple-element.105) | copy-start | bytes 9220
  95.9 8.7 %copy-start.16 = (f32[768]{0:T(1024)}, f32[768]{0:T(1024)S(1)}, u32[]{:S(2)}) copy-start(f32[768]{0:T(1024)S(1)} %get-tuple-element.106) | copy-start | bytes 9220
  99.8 4.9 %copy-start.18 = (f32[768]{0:T(1024)}, f32[768]{0:T(1024)S(1)}, u32[]{:S(2)}) copy-start(f32[768]{0:T(1024)S(1)} %get-tuple-element.58) | copy-start | bytes 9220
  99.8 4.9 %copy-start.20 = (f32[768]{0:T(1024)}, f32[768]{0:T(1024)S(1)}, u32[]{:S(2)}) copy-start(f32[768]{0:T(1024)S(1)} %get-tuple-element.59) | copy-start | bytes 9220
  99.8 4.9 %copy-start.22 = (f32[768]{0:T(1024)}, f32[768]{0:T(1024)S(1)}, u32[]{:S(2)}) copy-start(f32[768]{0:T(1024)S(1)} %get-tuple-element.60) | copy-start | bytes 9220
  99.8 4.9 %copy-start.24 = (f32[768]{0:T(1024)}, f32[768]{0:T(1024)S(1)}, u32[]{:S(2)}) copy-start(f32[768]{0:T(1024)S(1)} %get-tuple-element.61) | copy-start | bytes 9220
  99.8 4.9 %copy-start.26 = (f32[768]{0:T(1024)}, f32[768]{0:T(1024)S(1)}, u32[]{:S(2)}) copy-start(f32[768]{0:T(1024)S(1)} %get-tuple-element.62) | copy-start | bytes 9220
  99.8 4.9 %copy-start.28 = (f32[768]{0:T(1024)}, f32[768]{0:T(1024)S(1)}, u32[]{:S(2)}) copy-start(f32[768]{0:T(1024)S(1)} %get-tuple-element.63) | copy-start | bytes 9220
  99.8 4.9 %copy-start.30 = (f32[768]{0:T(1024)}, f32[768]{0:T(1024)S(1)}, u32[]{:S(2)}) copy-start(f32[768]{0:T(1024)S(1)} %get-tuple-element.64) | copy-start | bytes 9220
  99.9 4.9 %copy-start.32 = (f32[768]{0:T(1024)}, f32[768]{0:T(1024)S(1)}, u32[]{:S(2)}) copy-start(f32[768]{0:T(1024)S(1)} %get-tuple-element.65) | copy-start | bytes 9220
  99.9 4.9 %copy-start.34 = (f32[768]{0:T(1024)}, f32[768]{0:T(1024)S(1)}, u32[]{:S(2)}) copy-start(f32[768]{0:T(1024)S(1)} %get-tuple-element.66) | copy-start | bytes 9220
  99.9 4.9 %copy-start.36 = (f32[768]{0:T(1024)}, f32[768]{0:T(1024)S(1)}, u32[]{:S(2)}) copy-start(f32[768]{0:T(1024)S(1)} %get-tuple-element.67) | copy-start | bytes 9220
  99.9 4.9 %copy-start.38 = (f32[768]{0:T(1024)}, f32[768]{0:T(1024)S(1)}, u32[]{:S(2)}) copy-start(f32[768]{0:T(1024)S(1)} %get-tuple-element.68) | copy-start | bytes 9220
  99.9 4.9 %copy-start.40 = (f32[768]{0:T(1024)}, f32[768]{0:T(1024)S(1)}, u32[]{:S(2)}) copy-start(f32[768]{0:T(1024)S(1)} %get-tuple-element.69) | copy-start | bytes 9220
  99.9 4.9 %copy-start.42 = (f32[768]{0:T(1024)}, f32[768]{0:T(1024)S(1)}, u32[]{:S(2)}) copy-start(f32[768]{0:T(1024)S(1)} %get-tuple-element.70) | copy-start | bytes 9220
  99.9 4.9 %copy-start.44 = (f32[768]{0:T(1024)}, f32[768]{0:T(1024)S(1)}, u32[]{:S(2)}) copy-start(f32[768]{0:T(1024)S(1)} %get-tuple-element.71) | copy-start | bytes 9220
  99.9 4.9 %copy-start.46 = (f32[768]{0:T(1024)}, f32[768]{0:T(1024)S(1)}, u32[]{:S(2)}) copy-start(f32[768]{0:T(1024)S(1)} %get-tuple-element.72) | copy-start | bytes 9220
  99.9 4.9 %copy-start.48 = (f32[768]{0:T(1024)}, f32[768]{0:T(1024)S(1)}, u32[]{:S(2)}) copy-start(f32[768]{0:T(1024)S(1)} %get-tuple-element.73) | copy-start | bytes 9220
  99.9 4.9 %copy-start.50 = (f32[768]{0:T(1024)}, f32[768]{0:T(1024)S(1)}, u32[]{:S(2)}) copy-start(f32[768]{0:T(1024)S(1)} %get-tuple-element.74) | copy-start | bytes 9220
  100.0 4.9 %copy-start.52 = (f32[768]{0:T(1024)}, f32[768]{0:T(1024)S(1)}, u32[]{:S(2)}) copy-start(f32[768]{0:T(1024)S(1)} %get-tuple-element.75) | copy-start | bytes 9220
  100.0 4.9 %copy-start.54 = (f32[768]{0:T(1024)}, f32[768]{0:T(1024)S(1)}, u32[]{:S(2)}) copy-start(f32[768]{0:T(1024)S(1)} %get-tuple-element.76) | copy-start | bytes 9220
  100.0 10.3 %copy-start.84 = (bf16[1,8,16,1536]{3,2,1,0:T(8,128)(2,1)S(1)}, bf16[1,8,16,1536]{3,2,1,0:T(8,128)(2,1)}, u32[]{:S(2)}) copy-start(bf16[1,8,16,1536]{3,2,1,0:T(8,128)(2,1)} %param.7) | copy-start | bytes 1179652
  104.5 4.8 %copy-start.56 = (f32[768]{0:T(1024)}, f32[768]{0:T(1024)S(1)}, u32[]{:S(2)}) copy-start(f32[768]{0:T(1024)S(1)} %get-tuple-element.77) | copy-start | bytes 9220
  104.5 4.8 %copy-start.58 = (f32[768]{0:T(1024)}, f32[768]{0:T(1024)S(1)}, u32[]{:S(2)}) copy-start(f32[768]{0:T(1024)S(1)} %get-tuple-element.78) | copy-start | bytes 9220
  104.5 4.8 %copy-start.60 = (f32[768]{0:T(1024)}, f32[768]{0:T(1024)S(1)}, u32[]{:S(2)}) copy-start(f32[768]{0:T(1024)S(1)} %get-tuple-element.79) | copy-start | bytes 9220
  104.5 4.8 %copy-start.62 = (f32[768]{0:T(1024)}, f32[768]{0:T(1024)S(1)}, u32[]{:S(2)}) copy-start(f32[768]{0:T(1024)S(1)} %get-tuple-element.80) | copy-start | bytes 9220
  104.5 4.8 %copy-start.64 = (f32[768]{0:T(1024)}, f32[768]{0:T(1024)S(1)}, u32[]{:S(2)}) copy-start(f32[768]{0:T(1024)S(1)} %get-tuple-element.81) | copy-start | bytes 9220
  104.5 4.8 %copy-start.66 = (f32[768]{0:T(1024)}, f32[768]{0:T(1024)S(1)}, u32[]{:S(2)}) copy-start(f32[768]{0:T(1024)S(1)} %get-tuple-element.82) | copy-start | bytes 9220
  104.5 4.8 %copy-start.68 = (f32[768]{0:T(1024)}, f32[768]{0:T(1024)S(1)}, u32[]{:S(2)}) copy-start(f32[768]{0:T(1024)S(1)} %get-tuple-element.83) | copy-start | bytes 9220
  104.5 4.8 %copy-start.70 = (f32[768]{0:T(1024)}, f32[768]{0:T(1024)S(1)}, u32[]{:S(2)}) copy-start(f32[768]{0:T(1024)S(1)} %get-tuple-element.84) | copy-start | bytes 9220
  104.6 4.8 %copy-start.72 = (f32[768]{0:T(1024)}, f32[768]{0:T(1024)S(1)}, u32[]{:S(2)}) copy-start(f32[768]{0:T(1024)S(1)} %get-tuple-element.85) | copy-start | bytes 9220
  104.6 4.8 %copy-start.74 = (f32[768]{0:T(1024)}, f32[768]{0:T(1024)S(1)}, u32[]{:S(2)}) copy-start(f32[768]{0:T(1024)S(1)} %get-tuple-element.86) | copy-start | bytes 9220
  104.6 4.8 %copy-start.76 = (f32[768]{0:T(1024)}, f32[768]{0:T(1024)S(1)}, u32[]{:S(2)}) copy-start(f32[768]{0:T(1024)S(1)} %get-tuple-element.87) | copy-start | bytes 9220
  104.6 4.8 %copy-start.78 = (f32[768]{0:T(1024)}, f32[768]{0:T(1024)S(1)}, u32[]{:S(2)}) copy-start(f32[768]{0:T(1024)S(1)} %get-tuple-element.88) | copy-start | bytes 9220
  104.6 4.8 %copy-start.80 = (f32[768]{0:T(1024)}, f32[768]{0:T(1024)S(1)}, u32[]{:S(2)}) copy-start(f32[768]{0:T(1024)S(1)} %get-tuple-element.89) | copy-start | bytes 9220
  109.6 3.1 copy-start
  112.7 2.3 copy-start.1
  112.7 3.1 copy-start.2
  145.2 11.1 %copy-start.83 = (f32[768]{0:T(1024)S(1)}, f32[768]{0:T(1024)}, u32[]{:S(2)}) copy-start(f32[768]{0:T(1024)} %get-tuple-element.53) | copy-start | bytes 9220
  146.1 11.1 %copy-start.82 = (f32[768]{0:T(1024)S(1)}, f32[768]{0:T(1024)}, u32[]{:S(2)}) copy-start(f32[768]{0:T(1024)} %get-tuple-element.55) | copy-start | bytes 9220
  172.0 261.9 %reduce-scatter.3.cloned.1.call-start = ((), (), s32[]{:S(2)}) async-start(), calls=%async_computation.3 | async-start | bytes 5013504 | tf_op jit(solution)/shard_map/reduce_scatter | solution.py:136
  181.8 0.7 copy-start.13
  181.8 0.7 copy-start.15
  181.8 0.7 copy-start.19
  181.8 0.7 copy-start.21
  181.8 0.7 copy-start.23
  181.8 0.7 copy-start.25
  181.8 0.7 copy-start.27
  182.0 0.7 copy-start.53
  182.0 0.7 copy-start.59
  182.1 0.7 copy-start.69
  182.1 0.7 copy-start.73
  182.1 0.7 copy-start.75
  182.1 0.7 copy-start.77
  182.1 0.7 copy-start.79
  182.1 0.7 copy-start.81
  182.1 271.4 %all-reduce.7.cloned.1.call-start = ((), (), s32[]{:S(2)}) async-start(), calls=%async_computation.4 | async-start | bytes 589824 | tf_op jit(solution)/shard_map/psum | solution.py:139
  (25 other events, 17.1 us)
Sparse Core Ops, SparseCore 0:
  10.8 65.8 all-gather.1
  172.2 119.3 reduce-scatter.4
  297.5 136.3 reduce-scatter.2
  436.1 17.3 all-reduce.6
where the time goes:
time: 463 us; the launch traced here: 462 us
  waiting for transfers between devices  262 us (57%)
  blocking collectives  85 us (18%)
  local copies, waits for them, and re-layouts  76.4 us (17%)
  between operations  15.6 us (3%)
  other arithmetic  14.4 us (3%)
  matrix products  8.01 us (2%)
    reduce_scatter x1, waiting for transfers between devices, body(): lax.psum_scatter(weight_lines, 'shard', scatter_dimension=0, tiled=True)  138 us
    reduce_scatter x1, waiting for transfers between devices, body(): lax.psum_scatter(small_term, 'shard', scatter_dimension=0, tiled=True)  105 us
    all_gather x1, blocking collectives, body(): lax.all_gather(depthwise_weight, 'shard', axis=0, tiled=True)  44 us
    another operation x49, local copies, waits for them, and re-layouts, kernel_grad(): return jnp.stack(columns, axis=1)  39.1 us
    unnamed x1, blocking collectives  37 us
    psum x1, waiting for transfers between devices, body(): weight_lines, small_share = lax.psum((weight_lines, small_share), 'rep')  18.3 us
    concatenate x1, local copies, waits for them, and re-layouts, body(): jnp.concatenate([kernel_term, gain_term[:, None], bias_term[:, None], pad...  13.1 us
    slice x3, local copies, waits for them, and re-layouts, depthwise(): kernel[:, down_step * extent + across]  10.7 us
  transfers between devices with their start and end apart: 4, of which 3 were waited for; matrix products, arithmetic and copies ran while one was open for 7% of the time, Pallas kernels for 0%

commit v1 on v0

v1 whole, which is shorter than its diff:
```python
import functools
import math

import jax
import jax.numpy as jnp
from jax import lax
from jax.experimental import pallas as pl
from jax.experimental.pallas import tpu as pltpu
from jax.sharding import PartitionSpec as P

KS = 7
TAPS = KS * KS
MARGIN = KS // 2
LANES = 128
INNER = 4
NORM_EPS = 1e-06
BF16 = jnp.bfloat16
F32 = jnp.float32
VMEM = pl.BlockSpec(memory_space=pltpu.VMEM)


def params():
    return pltpu.CompilerParams(vmem_limit_bytes=48 * 1024 * 1024)


def gelu_slope(inputs):
    cumulative = 0.5 * (1.0 + lax.erf(inputs * 0.7071067811865476))
    return cumulative + inputs * jnp.exp(-0.5 * inputs * inputs) * 0.3989422804014327


def block_rows(relative, group, line, own, lines):
    if relative:
        place = lax.axis_index("shard") ^ (line * INNER + group)
        return pl.multiple_of(place * own, 16)
    return (group * lines + line) * own


def place_rows(pieces, target, own, relative, cast=None):
    for group, piece in enumerate(pieces):
        lines = piece.shape[0] // own
        if not relative:
            target[group * piece.shape[0] : (group + 1) * piece.shape[0], :] = (
                piece[...] if cast is None else piece[...].astype(cast)
            )
            continue
        for line in range(lines):
            rows = piece[line * own : (line + 1) * own, :]
            start = block_rows(True, group, line, own, lines)
            target[pl.ds(start, own), :] = rows if cast is None else rows.astype(cast)


def split_rows(source, pieces, own, relative):
    for group, piece in enumerate(pieces):
        lines = piece.shape[0] // own
        if not relative:
            piece[...] = source[group * piece.shape[0] : (group + 1) * piece.shape[0], :].astype(
                piece.dtype
            )
            continue
        for line in range(lines):
            start = block_rows(True, group, line, own, lines)
            piece[line * own : (line + 1) * own, :] = source[pl.ds(start, own), :].astype(
                piece.dtype
            )


def correlate(padded, tile, tap_row, height, breadth):
    sums = [None] * height
    for across in range(KS):
        shifted = padded[tile, :, 8 - MARGIN + across : 8 - MARGIN + across + breadth, :]
        for down in range(KS):
            row = tap_row(down, across)
            for line in range(height):
                origin = line + down - MARGIN
                if 0 <= origin < height:
                    term = shifted[origin] * row
                    sums[line] = term if sums[line] is None else sums[line] + term
    return sums


def conv_norm_kernel(relative, own, *refs):
    small = refs[:INNER]
    x_ref, normed_ref, white_ref, inv_ref, taps_ref, gathered, padded, conv = refs[INNER:]
    height, breadth, depth = x_ref.shape[1:]
    tiles = depth // LANES
    pixels = height * breadth
    place_rows(small, gathered, own, relative, F32)
    padded[...] = jnp.zeros_like(padded)
    for tile in range(tiles):
        lanes = slice(tile * LANES, (tile + 1) * LANES)
        taps_ref[tile] = gathered[lanes, :].T
        padded[tile, :, 8 : 8 + breadth, :] = x_ref[0, :, :, lanes].astype(F32)

    def one_tile(tile, carry):
        sums = correlate(
            padded,
            tile,
            lambda down, across: taps_ref[tile, pl.ds(down * KS + across, 1), :],
            height,
            breadth,
        )
        for line in range(height):
            conv[tile, line * breadth : (line + 1) * breadth, :] = sums[line]
        return carry

    lax.fori_loop(0, tiles, one_tile, 0)
    total = conv[0]
    for tile in range(1, tiles):
        total = total + conv[tile]
    average = jnp.sum(total, axis=-1, keepdims=True) / depth
    squares = None
    for tile in range(tiles):
        centered = conv[tile] - average
        squares = centered * centered if squares is None else squares + centered * centered
    variance = jnp.sum(squares, axis=-1, keepdims=True) / depth
    inv_std = lax.rsqrt(variance + NORM_EPS)
    inv_ref[...] = jnp.broadcast_to(inv_std, (pixels, LANES))
    for tile in range(tiles):
        lanes = slice(tile * LANES, (tile + 1) * LANES)
        whitened = (conv[tile] - average) * inv_std
        white_ref[:, lanes] = whitened
        gain = taps_ref[tile, TAPS : TAPS + 1, :]
        bias = taps_ref[tile, TAPS + 1 : TAPS + 2, :]
        normed_ref[:, lanes] = (whitened * gain + bias).astype(BF16)


def project_kernel(relative, own, *refs):
    weights = refs[:INNER]
    n_own, n_other, c_own, c_other = refs[INNER : INNER + 4]
    pieces = refs[INNER + 4 : 2 * INNER + 4]
    gp_ref, weight, normed, grad = refs[2 * INNER + 4 :]
    pixels = n_own.shape[0]
    hidden = weight.shape[1]
    place_rows(weights, weight, own, relative)
    normed[:pixels, :] = n_own[...]
    normed[pixels:, :] = n_other[...]
    step = 256 if hidden % 256 == 0 else hidden
    for start in range(0, hidden, step):
        columns = slice(start, start + step)
        pre_act = jnp.dot(normed[...], weight[:, columns], preferred_element_type=F32)
        slope = gelu_slope(pre_act)
        gp_ref[:pixels, columns] = (c_own[:, columns].astype(F32) * slope[:pixels]).astype(BF16)
        gp_ref[pixels:, columns] = (c_other[:, columns].astype(F32) * slope[pixels:]).astype(BF16)
        grad[:, columns] = lax.dot_general(
            normed[...], gp_ref[:, columns], (((0,), (0,)), ((), ())), preferred_element_type=F32
        )
    split_rows(grad, pieces, own, relative)


def back_project_kernel(relative, own, *refs):
    weights = refs[:INNER]
    gp_ref, own_ref, other_ref, weight = refs[INNER:]
    pixels = own_ref.shape[0]
    place_rows(weights, weight, own, relative)
    grad_normed = lax.dot_general(
        gp_ref[...], weight[...], (((1,), (1,)), ((), ())), preferred_element_type=F32
    )
    own_ref[...] = grad_normed[:pixels]
    other_ref[...] = grad_normed[pixels:]


def norm_back_kernel(relative, own, *refs):
    gn_own, gn_other, white_ref, inv_ref, taps_ref, x_ref = refs[:6]
    pieces = refs[6 : 6 + INNER]
    grad_ref, padded, rows, small = refs[6 + INNER :]
    height, breadth, depth = x_ref.shape[1:]
    tiles = depth // LANES
    pixels = height * breadth
    padded[...] = jnp.zeros_like(padded)
    rows[...] = jnp.zeros_like(rows)
    first = None
    second = None
    for tile in range(tiles):
        lanes = slice(tile * LANES, (tile + 1) * LANES)
        padded[tile, :, 8 : 8 + breadth, :] = x_ref[0, :, :, lanes].astype(F32)
        grad_normed = gn_own[:, lanes] + gn_other[:, lanes]
        whitened = white_ref[:, lanes]
        product = grad_normed * whitened
        gain = taps_ref[tile, TAPS : TAPS + 1, :]
        rows[tile, TAPS : TAPS + 1, :] = jnp.sum(product, axis=0, keepdims=True)
        rows[tile, TAPS + 1 : TAPS + 2, :] = jnp.sum(grad_normed, axis=0, keepdims=True)
        one, two = grad_normed * gain, product * gain
        first = one if first is None else first + one
        second = two if second is None else second + two
    mean_first = jnp.sum(first, axis=-1, keepdims=True) / depth
    mean_second = jnp.sum(second, axis=-1, keepdims=True) / depth
    for tile in range(tiles):
        lanes = slice(tile * LANES, (tile + 1) * LANES)
        gain = taps_ref[tile, TAPS : TAPS + 1, :]
        grad_white = (gn_own[:, lanes] + gn_other[:, lanes]) * gain
        grad_conv = inv_ref[...] * (grad_white - mean_first - white_ref[:, lanes] * mean_second)
        grad_ref[tile] = grad_conv.reshape(height, breadth, LANES)

    def one_tile(tile, carry):
        grads = [grad_ref[tile, line] for line in range(height)]
        for across in range(KS):
            shifted = padded[tile, :, 8 - MARGIN + across : 8 - MARGIN + across + breadth, :]
            for down in range(KS):
                total = None
                for line in range(height):
                    origin = line + down - MARGIN
                    if 0 <= origin < height:
                        term = grads[line] * shifted[origin]
                        total = term if total is None else total + term
                rows[tile, pl.ds(down * KS + across, 1), :] = jnp.sum(total, axis=0, keepdims=True)
        return carry

    lax.fori_loop(0, tiles, one_tile, 0)
    for tile in range(tiles):
        small[tile * LANES : (tile + 1) * LANES, :] = rows[tile].T
    split_rows(small, pieces, own, relative)


def conv_back_kernel(grad_ref, taps_ref, out_ref, padded):
    tiles, height, breadth, _ = grad_ref.shape
    padded[...] = jnp.zeros_like(padded)
    padded[:, :, 8 : 8 + breadth, :] = grad_ref[...]

    def one_tile(tile, carry):
        sums = correlate(
            padded,
            tile,
            lambda down, across: taps_ref[tile, pl.ds(TAPS - 1 - down * KS - across, 1), :],
            height,
            breadth,
        )
        start = pl.multiple_of(tile * LANES, LANES)
        for line in range(height):
            out_ref[0, line, :, pl.ds(start, LANES)] = sums[line].astype(BF16)
        return carry

    lax.fori_loop(0, tiles, one_tile, 0)


def call(kernel, name, outs, scratch, flops, *args):
    moved = sum(math.prod(a.shape) * a.dtype.itemsize for a in args)
    moved += sum(math.prod(o.shape) * o.dtype.itemsize for o in outs)
    return pl.pallas_call(
        kernel,
        out_shape=outs,
        in_specs=[VMEM] * len(args),
        out_specs=[VMEM] * len(outs),
        scratch_shapes=scratch,
        compiler_params=params(),
        cost_estimate=pl.CostEstimate(flops=flops, bytes_accessed=moved, transcendentals=0),
        name=name,
    )(*args)


def body(images, cotangent, depthwise_weight, norm_gain, norm_bias, up_weight):
    shards, reps = lax.axis_size("shard"), lax.axis_size("rep")
    own, hidden = up_weight.shape
    depth = own * shards
    lines = shards // INNER
    half = hidden // 2
    height, breadth = images.shape[1:3]
    pixels = height * breadth
    tiles = depth // LANES
    me = lax.axis_index("shard")
    side = lax.axis_index("rep") % 2
    relative = own % 16 == 0

    def over_shard(array, flip):
        return lax.ppermute(array, "shard", [(i, i ^ flip) for i in range(shards)])

    def over_core(array):
        return lax.ppermute(array, "rep", [(i, i ^ 1) for i in range(reps)])

    def true_order(pieces):
        if relative:
            return pieces
        stacked = jnp.stack(pieces).reshape(shards, own, -1)
        flips = jnp.arange(shards) ^ me
        places = (flips % INNER) * lines + flips // INNER
        return list(jnp.take(stacked, places, axis=0).reshape(INNER, lines * own, -1))

    def relative_order(pieces):
        if relative:
            return pieces
        stacked = jnp.concatenate([p.astype(F32) for p in pieces]).reshape(shards, own, -1)
        flips = (jnp.arange(lines)[None, :] * INNER + jnp.arange(INNER)[:, None]).reshape(-1)
        moved = jnp.take(stacked, flips ^ me, axis=0).reshape(INNER, lines * own, -1)
        return [moved[0]] + [moved[i].astype(BF16) for i in range(1, INNER)]

    columns = lax.dynamic_slice(up_weight, (0, side * half), (own, half))
    extras = jnp.concatenate(
        [
            depthwise_weight,
            norm_gain[:, None],
            norm_bias[:, None],
            jnp.zeros((own, LANES - TAPS - 2), BF16),
        ],
        axis=1,
    )
    packed = jnp.concatenate([columns, extras], axis=1)
    gathered = [packed] + [over_shard(packed, INNER * line) for line in range(1, lines)]
    weight_lines = jnp.concatenate([g[:, :half] for g in gathered])
    extra_lines = jnp.concatenate([g[:, half:] for g in gathered])
    weights = [weight_lines] + [over_shard(weight_lines, flip) for flip in range(1, INNER)]
    extras = [extra_lines] + [over_shard(extra_lines, flip) for flip in range(1, INNER)]
    weights, extras = true_order(weights), true_order(extras)

    cotangent = cotangent.reshape(pixels, hidden)
    cot_own = lax.dynamic_slice(cotangent, (0, side * half), (pixels, half))
    cot_other = over_core(lax.dynamic_slice(cotangent, (0, (1 - side) * half), (pixels, half)))

    shape = jax.ShapeDtypeStruct
    padded = pltpu.VMEM((tiles, height, breadth + 16, LANES), F32)
    conv_flops = 2 * TAPS * pixels * depth
    normed, whitened, inv_std, taps = call(
        functools.partial(conv_norm_kernel, relative, own),
        "conv_norm",
        [
            shape((pixels, depth), BF16),
            shape((pixels, depth), F32),
            shape((pixels, LANES), F32),
            shape((tiles, LANES, LANES), F32),
        ],
        [
            pltpu.VMEM((depth, LANES), F32),
            padded,
            pltpu.VMEM((tiles, pixels, LANES), F32),
        ],
        conv_flops,
        *extras,
        images,
    )
    normed_other = over_core(normed)

    rows = lines * own
    *pieces, grad_pre = call(
        functools.partial(project_kernel, relative, own),
        "project",
        [shape((rows, half), F32)]
        + [shape((rows, half), BF16)] * (INNER - 1)
        + [shape((2 * pixels, half), BF16)],
        [
            pltpu.VMEM((depth, half), BF16),
            pltpu.VMEM((2 * pixels, depth), BF16),
            pltpu.VMEM((depth, half), F32),
        ],
        8 * pixels * depth * half,
        *weights,
        normed,
        normed_other,
        cot_own,
        cot_other,
    )
    pieces = relative_order(pieces)
    arrived = [over_shard(piece, flip) for flip, piece in enumerate(pieces) if flip]

    gn_own, gn_send = call(
        functools.partial(back_project_kernel, relative, own),
        "back_project",
        [shape((pixels, depth), F32)] * 2,
        [pltpu.VMEM((depth, half), BF16)],
        4 * pixels * depth * half,
        *weights,
        grad_pre,
    )
    gn_other = over_core(gn_send)
    *small, grad_conv = call(
        functools.partial(norm_back_kernel, relative, own),
        "norm_back",
        [shape((rows, LANES), F32)]
        + [shape((rows, LANES), BF16)] * (INNER - 1)
        + [shape((tiles, height, breadth, LANES), F32)],
        [
            padded,
            pltpu.VMEM((tiles, LANES, LANES), F32),
            pltpu.VMEM((depth, LANES), F32),
        ],
        conv_flops,
        gn_own,
        gn_other,
        whitened,
        inv_std,
        taps,
        images,
    )
    small = relative_order(small)
    small_arrived = [over_shard(piece, flip) for flip, piece in enumerate(small) if flip]
    (grad_images,) = call(
        conv_back_kernel,
        "conv_back",
        [shape(images.shape, BF16)],
        [padded],
        conv_flops,
        grad_conv,
        taps,
    )

    plane = pieces[0] + sum(piece.astype(F32) for piece in arrived)
    small_plane = small[0] + sum(piece.astype(F32) for piece in small_arrived)
    merged = jnp.concatenate([plane, small_plane], axis=1).reshape(lines, own, half + LANES)
    total = merged[0]
    for line in range(1, lines):
        total = total + over_shard(merged[line].astype(BF16), INNER * line).astype(F32)
    if reps > 2:
        groups = [[i for i in range(reps) if i % 2 == s] for s in range(2)]
        total = lax.psum(total, "rep", axis_index_groups=groups)
    other = over_core(total)
    factor = 1.0 / math.sqrt(images.shape[0] * pixels * shards * reps)
    total, other = total * factor, other * factor
    grad_up = jnp.where(
        side == 0,
        jnp.concatenate([total[:, :half], other[:, :half]], axis=1),
        jnp.concatenate([other[:, :half], total[:, :half]], axis=1),
    )
    sums = total[:, half:] + other[:, half:]
    return (grad_images, grad_up, sums[:, :TAPS], sums[:, TAPS], sums[:, TAPS + 1])


def solution(mesh):
    placed = (
        P(("shard", "rep"), None, None, None),
        P(("shard", "rep"), None, None, None),
        P("shard", None),
        P("shard"),
        P("shard"),
        P("shard", None),
    )
    return jax.shard_map(
        body,
        mesh=mesh,
        in_specs=placed,
        out_specs=(
            P(("shard", "rep"), None, None, None),
            P("shard", None),
            P("shard", None),
            P("shard"),
            P("shard"),
        ),
        check_vma=False,
    )
```

time: 463 us -> 71.2 us (0.15)
  waiting for transfers between devices: 262 us -> 32.7 us
  blocking collectives: 85 us -> 0 us
  local copies, waits for them, and re-layouts: 76.4 us -> 5.39 us
  starting transfers between devices: 0.16 us -> 23.7 us
  between operations: 15.6 us -> 0.91 us
  other arithmetic: 14.4 us -> 1.09 us
  matrix products: 8.01 us -> 0 us
  Pallas kernels: 0 us -> 7.06 us
    reduce_scatter x2 -> x0, waiting for transfers between devices: 243 us -> none  [the longest x1 138 us: body(): lax.psum_scatter(weight_lines, 'shard', scatter_dimension=0, tiled=True)]
    all_gather x1 -> x0, blocking collectives: 44 us -> none  [body(): lax.all_gather(depthwise_weight, 'shard', axis=0, tiled=True)]
    another operation x49 -> x0, local copies, waits for them, and re-layouts: 39.1 us -> none  [kernel_grad(): return jnp.stack(columns, axis=1)]
    unnamed x1 -> x0, blocking collectives: 37 us -> none
    ppermute x0 -> x22, waiting for transfers between devices: none -> 32.7 us  [the longest x18 31.3 us: over_shard(): return lax.ppermute(array, 'shard', [(i, i ^ flip) for i in range(shards)])]
    ppermute x0 -> x22, starting transfers between devices: none -> 23.7 us  [the longest x18 23.5 us: over_shard(): return lax.ppermute(array, 'shard', [(i, i ^ flip) for i in range(shards)])]
    psum x1 -> x0, waiting for transfers between devices: 18.3 us -> none  [body(): weight_lines, small_share = lax.psum((weight_lines, small_share), 'rep')]
    concatenate x1, local copies, waits for them, and re-layouts: 13.1 us -> 0.1 us  [body(): packed = jnp.concatenate([columns, extras], axis=1)]
  transfers between devices with their start and end apart: 4 -> 22, of which waited for: 3 -> 13; matrix products, arithmetic and copies ran while one was open for 7% -> 0% of each run, Pallas kernels for 0% -> 7%
where the time goes in v1:
time: 71.2 us; the launch traced here: 70.9 us
  waiting for transfers between devices  32.7 us (46%)
  starting transfers between devices  23.7 us (33%)
  Pallas kernels  7.06 us (10%)
  local copies, waits for them, and re-layouts  5.39 us (8%)
  other arithmetic  1.09 us (2%)
  between operations  0.91 us (1%)
    ppermute x18, waiting for transfers between devices, over_shard(): return lax.ppermute(array, 'shard', [(i, i ^ flip) for i in range(shards)])  31.3 us
    ppermute x18, starting transfers between devices, over_shard(): return lax.ppermute(array, 'shard', [(i, i ^ flip) for i in range(shards)])  23.5 us
    pallas_call x5, Pallas kernels, call(): pl.pallas_call(kernel, out_shape=outs, in_specs=[VMEM] * len(args), out_s...  7.06 us
    unnamed x16, local copies, waits for them, and re-layouts  3.43 us
    ppermute x4, waiting for transfers between devices, over_core(): return lax.ppermute(array, 'rep', [(i, i ^ 1) for i in range(reps)])  1.43 us
  transfers between devices with their start and end apart: 22, of which 13 were waited for; matrix products, arithmetic and copies ran while one was open for 0% of the time, Pallas kernels for 7%

profile of v1, /device:TPU:0, one launch (start us, length us, event | category | flops | bytes accessed | tf_op | source)
XLA Modules:
  0.0 70.9 jit_solution(15681114832725243216)
XLA Ops:
  0.6 0.0 copy-start
  0.7 0.7 copy-done.6
  1.4 0.1 copy.15
  1.5 0.7 copy-done.7
  2.1 0.1 copy.16
  2.2 0.0 copy-start.5
  2.3 0.7 copy-done.5
  2.9 0.1 concatenate.22
  3.1 5.1 %collective-permute-start.2 = (bf16[48,896]{1,0:T(8,128)(2,1)S(1)}, bf16[48,896]{1,0:T(8,128)(2,1)S(1)}, u32[]{:S(2)}, u32[]{:S(2)}) collective-permute-start(bf16[48,896]{1,0:T(8,128)(2,1)S(1)} %concatenate.22), channel_id=1, source_target_pairs={{0,24},{2,26},{4,28},{6,30},{8,16},{10,18},{12,20},{14,22},{16,8},... | collective-permute-start | bytes 258056 | tf_op jit(solution)/shard_map/ppermute | solution.py:264
  8.2 0.0 collective-permute-start.1
  8.2 0.6 collective-permute-start
  8.8 2.6 %collective-permute-done.2 = bf16[48,896]{1,0:T(8,128)(2,1)S(1)} collective-permute-done((bf16[48,896]{1,0:T(8,128)(2,1)S(1)}, bf16[48,896]{1,0:T(8,128)(2,1)S(1)}, u32[]{:S(2)}, u32[]{:S(2)}) %collective-permute-start.2) | collective-permute-done | bytes 86048 | tf_op jit(solution)/shard_map/ppermute | solution.py:264
  11.4 4.0 %collective-permute-done.1 = bf16[48,896]{1,0:T(8,128)(2,1)S(1)} collective-permute-done((bf16[48,896]{1,0:T(8,128)(2,1)S(1)}, bf16[48,896]{1,0:T(8,128)(2,1)S(1)}, u32[]{:S(2)}, u32[]{:S(2)}) %collective-permute-start.1) | collective-permute-done | bytes 86048 | tf_op jit(solution)/shard_map/ppermute | solution.py:264
  15.4 0.0 collective-permute-done
  15.4 0.1 pad_maximum_fusion.2.refs_0_
  15.5 2.5 %collective-permute-start.8 = (bf16[192,128]{1,0:T(8,128)(2,1)S(1)}, bf16[192,128]{1,0:T(8,128)(2,1)S(1)}, u32[]{:S(2)}, u32[]{:S(2)}) collective-permute-start(bf16[192,128]{1,0:T(8,128)(2,1)S(1)} %pad_maximum_fusion.2.refs_0_), channel_id=1, source_target_pairs={{0,6},{2,4},{4,2},{6,0},{8,14},{10,12},{12,10},{14,8},{16,22},{18,... | collective-permute-start | bytes 147464 | tf_op jit(solution)/shard_map/ppermute | solution.py:264
  18.0 0.5 collective-permute-start.7
  18.5 0.5 collective-permute-start.6
  19.0 0.0 copy-start.2
  19.1 0.8 %slice-done = bf16[48,768]{1,0:T(8,128)(2,1)S(1)} async-done(((bf16[48,896]{1,0:T(8,128)(2,1)}), bf16[48,768]{1,0:T(8,128)(2,1)S(1)}, s32[]{:S(2)}) %slice-start) | async-done | bytes 73752 | tf_op jit(solution)/shard_map/slice | solution.py:297
  19.9 2.5 %collective-permute-start.5 = (bf16[192,768]{1,0:T(8,128)(2,1)S(1)}, bf16[192,768]{1,0:T(8,128)(2,1)S(1)}, u32[]{:S(2)}, u32[]{:S(2)}) collective-permute-start(bf16[192,768]{1,0:T(8,128)(2,1)S(1)} %pad_maximum_fusion.1.refs_0_), channel_id=1, source_target_pairs={{0,6},{2,4},{4,2},{6,0},{8,14},{10,12},{12,10},{14,8},{16,22},{18,... | collective-permute-start | bytes 884744 | tf_op jit(solution)/shard_map/ppermute | solution.py:264
  22.5 0.5 collective-permute-start.4
  23.0 0.0 collective-permute-done.8.refs_3_
  23.0 0.5 collective-permute-start.3
  23.5 0.0 collective-permute-done.7.refs_2_
  23.5 0.1 collective-permute-start.10
  23.6 0.0 collective-permute-done.6.refs_1_
  23.6 0.8 %copy-done.1 = bf16[1,8,16,768]{3,2,1,0:T(8,128)(2,1)S(1)} copy-done((bf16[1,8,16,768]{3,2,1,0:T(8,128)(2,1)S(1)}, bf16[1,8,16,768]{3,2,1,0:T(8,128)(2,1)}, u32[]{:S(2)}) %copy-start.1) | copy-done | bytes 196632
  24.4 1.6 %conv_norm.1 = (bf16[128,768]{1,0:T(8,128)(2,1)S(1)}, f32[128,768]{1,0:T(8,128)S(1)}, f32[128,128]{1,0:T(8,128)S(1)}, f32[6,128,128]{2,1,0:T(8,128)S(1)}) custom-call(bf16[192,128]{1,0:T(8,128)(2,1)S(1)} %pad_maximum_fusion.2.refs_0_, bf16[192,128]{1,0:T(8,128)(2,1)S(1)} %collective-permute-done.6.refs_1_, ...), custom_call_target="tpu_custom_call" | custom-call | flops 9633792 | bytes 1441792 | tf_op jit(solution)/shard_map/conv_norm/pallas_call | solution.py:238
  26.0 0.1 collective-permute-start.9
  26.1 0.0 collective-permute-done.10.refs_7_
  26.1 1.4 %collective-permute-done.9.refs_5_ = bf16[128,768]{1,0:T(8,128)(2,1)S(1)} collective-permute-done((bf16[128,768]{1,0:T(8,128)(2,1)S(1)}, bf16[128,768]{1,0:T(8,128)(2,1)S(1)}, u32[]{:S(2)}, u32[]{:S(2)}) %collective-permute-start.9) | collective-permute-done | bytes 196640 | tf_op jit(solution)/shard_map/ppermute | solution.py:267
  27.5 3.3 %collective-permute-done.5.refs_3_ = bf16[192,768]{1,0:T(8,128)(2,1)S(1)} collective-permute-done((bf16[192,768]{1,0:T(8,128)(2,1)S(1)}, bf16[192,768]{1,0:T(8,128)(2,1)S(1)}, u32[]{:S(2)}, u32[]{:S(2)}) %collective-permute-start.5) | collective-permute-done | bytes 294944 | tf_op jit(solution)/shard_map/ppermute | solution.py:264
  30.9 3.9 %collective-permute-done.4.refs_2_ = bf16[192,768]{1,0:T(8,128)(2,1)S(1)} collective-permute-done((bf16[192,768]{1,0:T(8,128)(2,1)S(1)}, bf16[192,768]{1,0:T(8,128)(2,1)S(1)}, u32[]{:S(2)}, u32[]{:S(2)}) %collective-permute-start.4) | collective-permute-done | bytes 294944 | tf_op jit(solution)/shard_map/ppermute | solution.py:264
  34.7 0.5 collective-permute-done.3.refs_1_
  35.2 1.4 %project.1 = (f32[192,768]{1,0:T(8,128)S(1)}, bf16[192,768]{1,0:T(8,128)(2,1)S(1)}, bf16[192,768]{1,0:T(8,128)(2,1)S(1)}, bf16[192,768]{1,0:T(8,128)(2,1)S(1)}, bf16[256,768]{1,0:T(8,128)(2,1)S(1)}) custom-call(bf16[192,768]{1,0:T(8,128)(2,1)S(1)} %pad_maximum_fusion.1.refs_0_, bf16[192,768]{1,0:T(8,128)(2,1)S(1)} %collective-permute-done.3.refs_1_, ...), custom_call_target="tpu_custom_call" | custom-call | flops 603979776 | bytes 3833856 | tf_op jit(solution)/shard_map/project/pallas_call | solution.py:238
  36.6 0.6 back_project.1
  37.2 0.1 collective-permute-start.11
  37.3 1.0 %collective-permute-start.12 = (bf16[192,768]{1,0:T(8,128)(2,1)S(1)}, bf16[192,768]{1,0:T(8,128)(2,1)S(1)}, u32[]{:S(2)}, u32[]{:S(2)}) collective-permute-start(bf16[192,768]{1,0:T(8,128)(2,1)S(1)} %get-tuple-element.30), channel_id=1, source_target_pairs={{0,2},{2,0},{4,6},{6,4},{8,10},{10,8},{12,14},{14,12},{16,18},{18,... | collective-permute-start | bytes 884744 | tf_op jit(solution)/shard_map/ppermute | solution.py:264
  38.3 1.0 %collective-permute-start.13 = (bf16[192,768]{1,0:T(8,128)(2,1)S(1)}, bf16[192,768]{1,0:T(8,128)(2,1)S(1)}, u32[]{:S(2)}, u32[]{:S(2)}) collective-permute-start(bf16[192,768]{1,0:T(8,128)(2,1)S(1)} %get-tuple-element.31), channel_id=1, source_target_pairs={{0,4},{2,6},{4,0},{6,2},{8,12},{10,14},{12,8},{14,10},{16,20},{18,... | collective-permute-start | bytes 884744 | tf_op jit(solution)/shard_map/ppermute | solution.py:264
  39.4 1.5 %collective-permute-start.14 = (bf16[192,768]{1,0:T(8,128)(2,1)S(1)}, bf16[192,768]{1,0:T(8,128)(2,1)S(1)}, u32[]{:S(2)}, u32[]{:S(2)}) collective-permute-start(bf16[192,768]{1,0:T(8,128)(2,1)S(1)} %get-tuple-element.32), channel_id=1, source_target_pairs={{0,6},{2,4},{4,2},{6,0},{8,14},{10,12},{12,10},{14,8},{16,22},{18,... | collective-permute-start | bytes 884744 | tf_op jit(solution)/shard_map/ppermute | solution.py:264
  40.9 1.7 %norm_back.1 = (f32[192,128]{1,0:T(8,128)S(1)}, bf16[192,128]{1,0:T(8,128)(2,1)S(1)}, bf16[192,128]{1,0:T(8,128)(2,1)S(1)}, bf16[192,128]{1,0:T(8,128)(2,1)S(1)}, f32[6,8,16,128]{3,2,1,0:T(8,128)S(1)}) custom-call(f32[128,768]{1,0:T(8,128)S(1)} %get-tuple-element.23.refs_0_, f32[128,768]{1,0:T(8,128)S(1)} %collective-permute-done.11.refs_1_, ...), custom_call_target="tpu_custom_call" | custom-call | flops 9633792 | bytes 2473984 | tf_op jit(solution)/shard_map/norm_back/pallas_call | solution.py:238
  42.5 1.1 %collective-permute-start.15 = (bf16[192,128]{1,0:T(8,128)(2,1)S(1)}, bf16[192,128]{1,0:T(8,128)(2,1)S(1)}, u32[]{:S(2)}, u32[]{:S(2)}) collective-permute-start(bf16[192,128]{1,0:T(8,128)(2,1)S(1)} %get-tuple-element.34), channel_id=1, source_target_pairs={{0,2},{2,0},{4,6},{6,4},{8,10},{10,8},{12,14},{14,12},{16,18},{18,... | collective-permute-start | bytes 147464 | tf_op jit(solution)/shard_map/ppermute | solution.py:264
  43.6 1.0 %collective-permute-start.16 = (bf16[192,128]{1,0:T(8,128)(2,1)S(1)}, bf16[192,128]{1,0:T(8,128)(2,1)S(1)}, u32[]{:S(2)}, u32[]{:S(2)}) collective-permute-start(bf16[192,128]{1,0:T(8,128)(2,1)S(1)} %get-tuple-element.35), channel_id=1, source_target_pairs={{0,4},{2,6},{4,0},{6,2},{8,12},{10,14},{12,8},{14,10},{16,20},{18,... | collective-permute-start | bytes 147464 | tf_op jit(solution)/shard_map/ppermute | solution.py:264
  44.6 2.6 %collective-permute-done.12 = bf16[192,768]{1,0:T(8,128)(2,1)S(1)} collective-permute-done((bf16[192,768]{1,0:T(8,128)(2,1)S(1)}, bf16[192,768]{1,0:T(8,128)(2,1)S(1)}, u32[]{:S(2)}, u32[]{:S(2)}) %collective-permute-start.12) | collective-permute-done | bytes 294944 | tf_op jit(solution)/shard_map/ppermute | solution.py:264
  47.2 1.4 %collective-permute-start.17 = (bf16[192,128]{1,0:T(8,128)(2,1)S(1)}, bf16[192,128]{1,0:T(8,128)(2,1)S(1)}, u32[]{:S(2)}, u32[]{:S(2)}) collective-permute-start(bf16[192,128]{1,0:T(8,128)(2,1)S(1)} %get-tuple-element.36), channel_id=1, source_target_pairs={{0,6},{2,4},{4,2},{6,0},{8,14},{10,12},{12,10},{14,8},{16,22},{18,... | collective-permute-start | bytes 147464 | tf_op jit(solution)/shard_map/ppermute | solution.py:264
  48.6 5.8 %collective-permute-done.13 = bf16[192,768]{1,0:T(8,128)(2,1)S(1)} collective-permute-done((bf16[192,768]{1,0:T(8,128)(2,1)S(1)}, bf16[192,768]{1,0:T(8,128)(2,1)S(1)}, u32[]{:S(2)}, u32[]{:S(2)}) %collective-permute-start.13) | collective-permute-done | bytes 294944 | tf_op jit(solution)/shard_map/ppermute | solution.py:264
  54.4 0.1 add_add_fusion
  54.5 0.1 collective-permute-done.15
  54.6 1.3 %collective-permute-done.16 = bf16[192,128]{1,0:T(8,128)(2,1)S(1)} collective-permute-done((bf16[192,128]{1,0:T(8,128)(2,1)S(1)}, bf16[192,128]{1,0:T(8,128)(2,1)S(1)}, u32[]{:S(2)}, u32[]{:S(2)}) %collective-permute-start.16) | collective-permute-done | bytes 49184 | tf_op jit(solution)/shard_map/ppermute | solution.py:264
  56.0 0.4 collective-permute-start.18
  56.3 1.9 %collective-permute-start.20 = (bf16[48,896]{1,0:T(8,128)(2,1)S(1)}, bf16[48,896]{1,0:T(8,128)(2,1)S(1)}, u32[]{:S(2)}, u32[]{:S(2)}) collective-permute-start(bf16[48,896]{1,0:T(8,128)(2,1)S(1)} %get-tuple-element.44), channel_id=1, source_target_pairs={{0,24},{2,26},{4,28},{6,30},{8,16},{10,18},{12,20},{14,22},{16,8},... | collective-permute-start | bytes 258056 | tf_op jit(solution)/shard_map/ppermute | solution.py:264
  58.3 1.2 %collective-permute-start.19 = (bf16[48,896]{1,0:T(8,128)(2,1)S(1)}, bf16[48,896]{1,0:T(8,128)(2,1)S(1)}, u32[]{:S(2)}, u32[]{:S(2)}) collective-permute-start(bf16[48,896]{1,0:T(8,128)(2,1)S(1)} %get-tuple-element.45), channel_id=1, source_target_pairs={{0,16},{2,18},{4,20},{6,22},{8,24},{10,26},{12,28},{14,30},{16,0},... | collective-permute-start | bytes 258056 | tf_op jit(solution)/shard_map/ppermute | solution.py:264
  59.5 2.0 %collective-permute-done.18 = bf16[48,896]{1,0:T(8,128)(2,1)S(1)} collective-permute-done((bf16[48,896]{1,0:T(8,128)(2,1)S(1)}, bf16[48,896]{1,0:T(8,128)(2,1)S(1)}, u32[]{:S(2)}, u32[]{:S(2)}) %collective-permute-start.18) | collective-permute-done | bytes 86048 | tf_op jit(solution)/shard_map/ppermute | solution.py:264
  61.5 2.1 %collective-permute-done.20 = bf16[48,896]{1,0:T(8,128)(2,1)S(1)} collective-permute-done((bf16[48,896]{1,0:T(8,128)(2,1)S(1)}, bf16[48,896]{1,0:T(8,128)(2,1)S(1)}, u32[]{:S(2)}, u32[]{:S(2)}) %collective-permute-start.20) | collective-permute-done | bytes 86048 | tf_op jit(solution)/shard_map/ppermute | solution.py:264
  63.5 3.3 %collective-permute-done.19 = bf16[48,896]{1,0:T(8,128)(2,1)S(1)} collective-permute-done((bf16[48,896]{1,0:T(8,128)(2,1)S(1)}, bf16[48,896]{1,0:T(8,128)(2,1)S(1)}, u32[]{:S(2)}, u32[]{:S(2)}) %collective-permute-start.19) | collective-permute-done | bytes 86048 | tf_op jit(solution)/shard_map/ppermute | solution.py:264
  66.8 0.1 broadcast_multiply_fusion.1
  66.9 0.1 collective-permute-start.21
  67.0 1.9 %conv_back.1 = bf16[1,8,16,768]{3,2,1,0:T(8,128)(2,1)} custom-call(f32[6,8,16,128]{3,2,1,0:T(8,128)S(1)} %get-tuple-element.28.grad_ref, f32[6,128,128]{2,1,0:T(8,128)S(1)} %get-tuple-element.27.refs_4_.taps_ref), custom_call_target="tpu_custom_call" | custom-call | flops 9633792 | bytes 983040 | tf_op jit(solution)/shard_map/conv_back/pallas_call | solution.py:238
  68.8 0.0 collective-permute-done.21
  68.9 0.0 copy-start.4
  68.9 0.6 copy-done.4
  69.5 0.7 slice_reduce_fusion
  70.2 0.7 %maximum_select_fusion = f32[48,1536]{1,0:T(8,128)} fusion(f32[48,768]{1,0:T(8,128)S(1)} %slice.89, f32[48,768]{1,0:T(8,128)S(1)} %slice.88, pred[]{:T(512)S(6)} %eq.5), kind=kLoop, calls=%fused_computation.6 | loop fusion | flops 221184 | bytes 589825 | tf_op jit(solution)/shard_map/jit(_where)/select_n | solution.py:405
  (27 shorter events, 0.2 us)
Async XLA Ops:
  0.6 1.6 %copy-start = (bf16[48,1536]{1,0:T(8,128)(2,1)S(1)}, bf16[48,1536]{1,0:T(8,128)(2,1)}, u32[]{:S(2)}) copy-start(bf16[48,1536]{1,0:T(8,128)(2,1)} %param.11) | copy-start | bytes 442372
  0.7 0.7 copy-start.6
  1.5 0.7 copy-start.7
  2.2 0.7 %copy-start.5 = (bf16[48,49]{1,0:T(8,128)(2,1)S(1)}, bf16[48,49]{1,0:T(8,128)(2,1)}, u32[]{:S(2)}) copy-start(bf16[48,49]{1,0:T(8,128)(2,1)} %param.8) | copy-start | bytes 14116
  3.1 8.3 %collective-permute-start.2 = (bf16[48,896]{1,0:T(8,128)(2,1)S(1)}, bf16[48,896]{1,0:T(8,128)(2,1)S(1)}, u32[]{:S(2)}, u32[]{:S(2)}) collective-permute-start(bf16[48,896]{1,0:T(8,128)(2,1)S(1)} %concatenate.22), channel_id=1, source_target_pairs={{0,24},{2,26},{4,28},{6,30},{8,16},{10,18},{12,20},{14,22},{16,8},... | collective-permute-start | bytes 258056 | tf_op jit(solution)/shard_map/ppermute | solution.py:264
  8.2 7.2 %collective-permute-start.1 = (bf16[48,896]{1,0:T(8,128)(2,1)S(1)}, bf16[48,896]{1,0:T(8,128)(2,1)S(1)}, u32[]{:S(2)}, u32[]{:S(2)}) collective-permute-start(bf16[48,896]{1,0:T(8,128)(2,1)S(1)} %concatenate.22), channel_id=1, source_target_pairs={{0,16},{2,18},{4,20},{6,22},{8,24},{10,26},{12,28},{14,30},{16,0},... | collective-permute-start | bytes 258056 | tf_op jit(solution)/shard_map/ppermute | solution.py:264
  8.2 7.2 %collective-permute-start = (bf16[48,896]{1,0:T(8,128)(2,1)S(1)}, bf16[48,896]{1,0:T(8,128)(2,1)S(1)}, u32[]{:S(2)}, u32[]{:S(2)}) collective-permute-start(bf16[48,896]{1,0:T(8,128)(2,1)S(1)} %concatenate.22), channel_id=1, source_target_pairs={{0,8},{2,10},{4,12},{6,14},{8,0},{10,2},{12,4},{14,6},{16,24},{18,... | collective-permute-start | bytes 258056 | tf_op jit(solution)/shard_map/ppermute | solution.py:264
  11.4 7.6 %copy-start.3 = (bf16[48,896]{1,0:T(8,128)(2,1)}, bf16[48,896]{1,0:T(8,128)(2,1)S(1)}, u32[]{:S(2)}) copy-start(bf16[48,896]{1,0:T(8,128)(2,1)S(1)} %collective-permute-done.2) | copy-start | bytes 258052
  15.5 7.5 %collective-permute-start.8 = (bf16[192,128]{1,0:T(8,128)(2,1)S(1)}, bf16[192,128]{1,0:T(8,128)(2,1)S(1)}, u32[]{:S(2)}, u32[]{:S(2)}) collective-permute-start(bf16[192,128]{1,0:T(8,128)(2,1)S(1)} %pad_maximum_fusion.2.refs_0_), channel_id=1, source_target_pairs={{0,6},{2,4},{4,2},{6,0},{8,14},{10,12},{12,10},{14,8},{16,22},{18,... | collective-permute-start | bytes 147464 | tf_op jit(solution)/shard_map/ppermute | solution.py:264
  18.0 5.5 %collective-permute-start.7 = (bf16[192,128]{1,0:T(8,128)(2,1)S(1)}, bf16[192,128]{1,0:T(8,128)(2,1)S(1)}, u32[]{:S(2)}, u32[]{:S(2)}) collective-permute-start(bf16[192,128]{1,0:T(8,128)(2,1)S(1)} %pad_maximum_fusion.2.refs_0_), channel_id=1, source_target_pairs={{0,4},{2,6},{4,0},{6,2},{8,12},{10,14},{12,8},{14,10},{16,20},{18,... | collective-permute-start | bytes 147464 | tf_op jit(solution)/shard_map/ppermute | solution.py:264
  18.5 5.1 %collective-permute-start.6 = (bf16[192,128]{1,0:T(8,128)(2,1)S(1)}, bf16[192,128]{1,0:T(8,128)(2,1)S(1)}, u32[]{:S(2)}, u32[]{:S(2)}) collective-permute-start(bf16[192,128]{1,0:T(8,128)(2,1)S(1)} %pad_maximum_fusion.2.refs_0_), channel_id=1, source_target_pairs={{0,2},{2,0},{4,6},{6,4},{8,10},{10,8},{12,14},{14,12},{16,18},{18,... | collective-permute-start | bytes 147464 | tf_op jit(solution)/shard_map/ppermute | solution.py:264
  19.0 0.9 %slice-start = ((bf16[48,896]{1,0:T(8,128)(2,1)}), bf16[48,768]{1,0:T(8,128)(2,1)S(1)}, s32[]{:S(2)}) async-start(bf16[48,896]{1,0:T(8,128)(2,1)} %copy-done.3), calls=%async_computation | async-start | bytes 147456 | tf_op jit(solution)/shard_map/slice | solution.py:297
  19.0 4.5 %copy-start.2 = (bf16[1,8,16,1536]{3,2,1,0:T(8,128)(2,1)S(1)}, bf16[1,8,16,1536]{3,2,1,0:T(8,128)(2,1)}, u32[]{:S(2)}) copy-start(bf16[1,8,16,1536]{3,2,1,0:T(8,128)(2,1)} %param.7) | copy-start | bytes 1179652
  19.9 10.9 %collective-permute-start.5 = (bf16[192,768]{1,0:T(8,128)(2,1)S(1)}, bf16[192,768]{1,0:T(8,128)(2,1)S(1)}, u32[]{:S(2)}, u32[]{:S(2)}) collective-permute-start(bf16[192,768]{1,0:T(8,128)(2,1)S(1)} %pad_maximum_fusion.1.refs_0_), channel_id=1, source_target_pairs={{0,6},{2,4},{4,2},{6,0},{8,14},{10,12},{12,10},{14,8},{16,22},{18,... | collective-permute-start | bytes 884744 | tf_op jit(solution)/shard_map/ppermute | solution.py:264
  22.5 12.3 %collective-permute-start.4 = (bf16[192,768]{1,0:T(8,128)(2,1)S(1)}, bf16[192,768]{1,0:T(8,128)(2,1)S(1)}, u32[]{:S(2)}, u32[]{:S(2)}) collective-permute-start(bf16[192,768]{1,0:T(8,128)(2,1)S(1)} %pad_maximum_fusion.1.refs_0_), channel_id=1, source_target_pairs={{0,4},{2,6},{4,0},{6,2},{8,12},{10,14},{12,8},{14,10},{16,20},{18,... | collective-permute-start | bytes 884744 | tf_op jit(solution)/shard_map/ppermute | solution.py:264
  23.0 12.3 %collective-permute-start.3 = (bf16[192,768]{1,0:T(8,128)(2,1)S(1)}, bf16[192,768]{1,0:T(8,128)(2,1)S(1)}, u32[]{:S(2)}, u32[]{:S(2)}) collective-permute-start(bf16[192,768]{1,0:T(8,128)(2,1)S(1)} %pad_maximum_fusion.1.refs_0_), channel_id=1, source_target_pairs={{0,2},{2,0},{4,6},{6,4},{8,10},{10,8},{12,14},{14,12},{16,18},{18,... | collective-permute-start | bytes 884744 | tf_op jit(solution)/shard_map/ppermute | solution.py:264
  23.5 0.9 %copy-start.1 = (bf16[1,8,16,768]{3,2,1,0:T(8,128)(2,1)S(1)}, bf16[1,8,16,768]{3,2,1,0:T(8,128)(2,1)}, u32[]{:S(2)}) copy-start(bf16[1,8,16,768]{3,2,1,0:T(8,128)(2,1)} %refs_5_.1) | copy-start | bytes 589828
  23.5 2.5 %collective-permute-start.10 = (bf16[128,768]{1,0:T(8,128)(2,1)S(1)}, bf16[128,768]{1,0:T(8,128)(2,1)S(1)}, u32[]{:S(2)}, u32[]{:S(2)}) collective-permute-start(bf16[128,768]{1,0:T(8,128)(2,1)S(1)} %get-tuple-element.41), channel_id=1, source_target_pairs={{0,1},{1,0},{2,3},{3,2},{4,5},{5,4},{6,7},{7,6},{8,9},{9,8},{10,11... | collective-permute-start | bytes 589832 | tf_op jit(solution)/shard_map/ppermute | solution.py:267
  26.0 1.5 %collective-permute-start.9 = (bf16[128,768]{1,0:T(8,128)(2,1)S(1)}, bf16[128,768]{1,0:T(8,128)(2,1)S(1)}, u32[]{:S(2)}, u32[]{:S(2)}) collective-permute-start(bf16[128,768]{1,0:T(8,128)(2,1)S(1)} %get-tuple-element.21.refs_4_), channel_id=1, source_target_pairs={{0,1},{1,0},{2,3},{3,2},{4,5},{5,4},{6,7},{7,6},{8,9},{9,8},{10,11... | collective-permute-start | bytes 589832 | tf_op jit(solution)/shard_map/ppermute | solution.py:267
  37.2 3.6 %collective-permute-start.11 = (f32[128,768]{1,0:T(8,128)S(1)}, f32[128,768]{1,0:T(8,128)S(1)}, u32[]{:S(2)}, u32[]{:S(2)}) collective-permute-start(f32[128,768]{1,0:T(8,128)S(1)} %get-tuple-element.24), channel_id=1, source_target_pairs={{0,1},{1,0},{2,3},{3,2},{4,5},{5,4},{6,7},{7,6},{8,9},{9,8},{10,11... | collective-permute-start | bytes 1179656 | tf_op jit(solution)/shard_map/ppermute | solution.py:267
  37.3 9.9 %collective-permute-start.12 = (bf16[192,768]{1,0:T(8,128)(2,1)S(1)}, bf16[192,768]{1,0:T(8,128)(2,1)S(1)}, u32[]{:S(2)}, u32[]{:S(2)}) collective-permute-start(bf16[192,768]{1,0:T(8,128)(2,1)S(1)} %get-tuple-element.30), channel_id=1, source_target_pairs={{0,2},{2,0},{4,6},{6,4},{8,10},{10,8},{12,14},{14,12},{16,18},{18,... | collective-permute-start | bytes 884744 | tf_op jit(solution)/shard_map/ppermute | solution.py:264
  38.3 16.1 %collective-permute-start.13 = (bf16[192,768]{1,0:T(8,128)(2,1)S(1)}, bf16[192,768]{1,0:T(8,128)(2,1)S(1)}, u32[]{:S(2)}, u32[]{:S(2)}) collective-permute-start(bf16[192,768]{1,0:T(8,128)(2,1)S(1)} %get-tuple-element.31), channel_id=1, source_target_pairs={{0,4},{2,6},{4,0},{6,2},{8,12},{10,14},{12,8},{14,10},{16,20},{18,... | collective-permute-start | bytes 884744 | tf_op jit(solution)/shard_map/ppermute | solution.py:264
  39.4 15.0 %collective-permute-start.14 = (bf16[192,768]{1,0:T(8,128)(2,1)S(1)}, bf16[192,768]{1,0:T(8,128)(2,1)S(1)}, u32[]{:S(2)}, u32[]{:S(2)}) collective-permute-start(bf16[192,768]{1,0:T(8,128)(2,1)S(1)} %get-tuple-element.32), channel_id=1, source_target_pairs={{0,6},{2,4},{4,2},{6,0},{8,14},{10,12},{12,10},{14,8},{16,22},{18,... | collective-permute-start | bytes 884744 | tf_op jit(solution)/shard_map/ppermute | solution.py:264
  42.5 12.0 %collective-permute-start.15 = (bf16[192,128]{1,0:T(8,128)(2,1)S(1)}, bf16[192,128]{1,0:T(8,128)(2,1)S(1)}, u32[]{:S(2)}, u32[]{:S(2)}) collective-permute-start(bf16[192,128]{1,0:T(8,128)(2,1)S(1)} %get-tuple-element.34), channel_id=1, source_target_pairs={{0,2},{2,0},{4,6},{6,4},{8,10},{10,8},{12,14},{14,12},{16,18},{18,... | collective-permute-start | bytes 147464 | tf_op jit(solution)/shard_map/ppermute | solution.py:264
  43.6 12.3 %collective-permute-start.16 = (bf16[192,128]{1,0:T(8,128)(2,1)S(1)}, bf16[192,128]{1,0:T(8,128)(2,1)S(1)}, u32[]{:S(2)}, u32[]{:S(2)}) collective-permute-start(bf16[192,128]{1,0:T(8,128)(2,1)S(1)} %get-tuple-element.35), channel_id=1, source_target_pairs={{0,4},{2,6},{4,0},{6,2},{8,12},{10,14},{12,8},{14,10},{16,20},{18,... | collective-permute-start | bytes 147464 | tf_op jit(solution)/shard_map/ppermute | solution.py:264
  47.2 8.7 %collective-permute-start.17 = (bf16[192,128]{1,0:T(8,128)(2,1)S(1)}, bf16[192,128]{1,0:T(8,128)(2,1)S(1)}, u32[]{:S(2)}, u32[]{:S(2)}) collective-permute-start(bf16[192,128]{1,0:T(8,128)(2,1)S(1)} %get-tuple-element.36), channel_id=1, source_target_pairs={{0,6},{2,4},{4,2},{6,0},{8,14},{10,12},{12,10},{14,8},{16,22},{18,... | collective-permute-start | bytes 147464 | tf_op jit(solution)/shard_map/ppermute | solution.py:264
  56.0 5.5 %collective-permute-start.18 = (bf16[48,896]{1,0:T(8,128)(2,1)S(1)}, bf16[48,896]{1,0:T(8,128)(2,1)S(1)}, u32[]{:S(2)}, u32[]{:S(2)}) collective-permute-start(bf16[48,896]{1,0:T(8,128)(2,1)S(1)} %get-tuple-element.43), channel_id=1, source_target_pairs={{0,8},{2,10},{4,12},{6,14},{8,0},{10,2},{12,4},{14,6},{16,24},{18,... | collective-permute-start | bytes 258056 | tf_op jit(solution)/shard_map/ppermute | solution.py:264
  56.3 7.2 %collective-permute-start.20 = (bf16[48,896]{1,0:T(8,128)(2,1)S(1)}, bf16[48,896]{1,0:T(8,128)(2,1)S(1)}, u32[]{:S(2)}, u32[]{:S(2)}) collective-permute-start(bf16[48,896]{1,0:T(8,128)(2,1)S(1)} %get-tuple-element.44), channel_id=1, source_target_pairs={{0,24},{2,26},{4,28},{6,30},{8,16},{10,18},{12,20},{14,22},{16,8},... | collective-permute-start | bytes 258056 | tf_op jit(solution)/shard_map/ppermute | solution.py:264
  58.3 8.6 %collective-permute-start.19 = (bf16[48,896]{1,0:T(8,128)(2,1)S(1)}, bf16[48,896]{1,0:T(8,128)(2,1)S(1)}, u32[]{:S(2)}, u32[]{:S(2)}) collective-permute-start(bf16[48,896]{1,0:T(8,128)(2,1)S(1)} %get-tuple-element.45), channel_id=1, source_target_pairs={{0,16},{2,18},{4,20},{6,22},{8,24},{10,26},{12,28},{14,30},{16,0},... | collective-permute-start | bytes 258056 | tf_op jit(solution)/shard_map/ppermute | solution.py:264
  66.9 2.0 %collective-permute-start.21 = (f32[48,896]{1,0:T(8,128)S(1)}, f32[48,896]{1,0:T(8,128)S(1)}, u32[]{:S(2)}, u32[]{:S(2)}) collective-permute-start(f32[48,896]{1,0:T(8,128)S(1)} %get-tuple-element.40), channel_id=1, source_target_pairs={{0,1},{1,0},{2,3},{3,2},{4,5},{5,4},{6,7},{7,6},{8,9},{9,8},{10,11... | collective-permute-start | bytes 516104 | tf_op jit(solution)/shard_map/ppermute | solution.py:267
  68.9 0.6 copy-start.4

commit v2 on v1

--- a/solution.py
+++ b/solution.py
@@ -78,9 +78,27 @@
     return sums
 
 
+def pack_kernel(w_ref, dw_ref, gain_ref, bias_ref, near_ref, far_ref, turned, wide):
+    own, hidden = w_ref.shape
+    quarter = hidden // 4
+    side = lax.axis_index("rep") % 2
+    parity = (lax.axis_index("shard") // INNER) % 2
+    turned[...] = jnp.zeros_like(turned)
+    turned[TAPS : TAPS + 1, :own] = gain_ref[...].astype(F32)
+    turned[TAPS + 1 : TAPS + 2, :own] = bias_ref[...].astype(F32)
+    wide[...] = jnp.zeros_like(wide)
+    wide[:, :TAPS] = dw_ref[...].astype(F32)
+    extras = (wide[...] + turned[...].T[:own]).astype(BF16)
+    for ref, which in ((near_ref, parity), (far_ref, 1 - parity)):
+        start = pl.multiple_of(side * (2 * quarter) + which * quarter, LANES)
+        ref[:, :quarter] = w_ref[:, pl.ds(start, quarter)]
+        ref[:, quarter:] = extras
+
+
 def conv_norm_kernel(relative, own, *refs):
     small = refs[:INNER]
-    x_ref, normed_ref, white_ref, inv_ref, taps_ref, gathered, padded, conv = refs[INNER:]
+    x_ref, other_ref = refs[INNER : INNER + 2]
+    normed_ref, white_ref, inv_ref, taps_ref, gathered, padded, conv = refs[INNER + 2 :]
     height, breadth, depth = x_ref.shape[1:]
     tiles = depth // LANES
     pixels = height * breadth
@@ -89,74 +107,104 @@
     for tile in range(tiles):
         lanes = slice(tile * LANES, (tile + 1) * LANES)
         taps_ref[tile] = gathered[lanes, :].T
-        padded[tile, :, 8 : 8 + breadth, :] = x_ref[0, :, :, lanes].astype(F32)
-
-    def one_tile(tile, carry):
-        sums = correlate(
-            padded,
-            tile,
-            lambda down, across: taps_ref[tile, pl.ds(down * KS + across, 1), :],
-            height,
-            breadth,
-        )
-        for line in range(height):
-            conv[tile, line * breadth : (line + 1) * breadth, :] = sums[line]
-        return carry
-
-    lax.fori_loop(0, tiles, one_tile, 0)
-    total = conv[0]
-    for tile in range(1, tiles):
-        total = total + conv[tile]
-    average = jnp.sum(total, axis=-1, keepdims=True) / depth
-    squares = None
-    for tile in range(tiles):
-        centered = conv[tile] - average
-        squares = centered * centered if squares is None else squares + centered * centered
-    variance = jnp.sum(squares, axis=-1, keepdims=True) / depth
-    inv_std = lax.rsqrt(variance + NORM_EPS)
-    inv_ref[...] = jnp.broadcast_to(inv_std, (pixels, LANES))
-    for tile in range(tiles):
-        lanes = slice(tile * LANES, (tile + 1) * LANES)
-        whitened = (conv[tile] - average) * inv_std
-        white_ref[:, lanes] = whitened
-        gain = taps_ref[tile, TAPS : TAPS + 1, :]
-        bias = taps_ref[tile, TAPS + 1 : TAPS + 2, :]
-        normed_ref[:, lanes] = (whitened * gain + bias).astype(BF16)
+
+    for image, source in enumerate((x_ref, other_ref)):
+        for tile in range(tiles):
+            lanes = slice(tile * LANES, (tile + 1) * LANES)
+            padded[tile, :, 8 : 8 + breadth, :] = source[0, :, :, lanes].astype(F32)
+
+        def one_tile(tile, carry):
+            sums = correlate(
+                padded,
+                tile,
+                lambda down, across: taps_ref[tile, pl.ds(down * KS + across, 1), :],
+                height,
+                breadth,
+            )
+            for line in range(height):
+                conv[tile, line * breadth : (line + 1) * breadth, :] = sums[line]
+            return carry
+
+        lax.fori_loop(0, tiles, one_tile, 0)
+        total = conv[0]
+        for tile in range(1, tiles):
+            total = total + conv[tile]
+        average = jnp.sum(total, axis=-1, keepdims=True) / depth
+        squares = None
+        for tile in range(tiles):
+            centered = conv[tile] - average
+            squares = centered * centered if squares is None else squares + centered * centered
+        variance = jnp.sum(squares, axis=-1, keepdims=True) / depth
+        inv_std = lax.rsqrt(variance + NORM_EPS)
+        if image == 0:
+            inv_ref[...] = jnp.broadcast_to(inv_std, (pixels, LANES))
+        for tile in range(tiles):
+            lanes = slice(tile * LANES, (tile + 1) * LANES)
+            whitened = (conv[tile] - average) * inv_std
+            if image == 0:
+                white_ref[:, lanes] = whitened
+            gain = taps_ref[tile, TAPS : TAPS + 1, :]
+            bias = taps_ref[tile, TAPS + 1 : TAPS + 2, :]
+            normed_ref[image * pixels : (image + 1) * pixels, lanes] = (
+                whitened * gain + bias
+            ).astype(BF16)
+
+
+def cot_pack_kernel(cot_ref, sibling_ref, out_ref):
+    pixels, half = sibling_ref.shape
+    quarter = half // 2
+    side = lax.axis_index("rep") % 2
+    parity = (lax.axis_index("shard") // INNER) % 2
+    start = pl.multiple_of(side * half + (1 - parity) * quarter, LANES)
+    out_ref[:pixels, :] = cot_ref[:, pl.ds(start, quarter)]
+    start = pl.multiple_of((1 - parity) * quarter, LANES)
+    out_ref[pixels:, :] = sibling_ref[:, pl.ds(start, quarter)]
 
 
 def project_kernel(relative, own, *refs):
     weights = refs[:INNER]
-    n_own, n_other, c_own, c_other = refs[INNER : INNER + 4]
-    pieces = refs[INNER + 4 : 2 * INNER + 4]
-    gp_ref, weight, normed, grad = refs[2 * INNER + 4 :]
-    pixels = n_own.shape[0]
-    hidden = weight.shape[1]
+    n_own, n_sibling, cot_ref, sibling_ref, far_ref = refs[INNER : INNER + 5]
+    pieces = refs[INNER + 5 : 2 * INNER + 5]
+    gp_ref, weight, normed, cot, grad = refs[2 * INNER + 5 :]
+    pixels, half = sibling_ref.shape
+    quarter = half // 2
+    side = lax.axis_index("rep") % 2
+    parity = (lax.axis_index("shard") // INNER) % 2
     place_rows(weights, weight, own, relative)
-    normed[:pixels, :] = n_own[...]
-    normed[pixels:, :] = n_other[...]
-    step = 256 if hidden % 256 == 0 else hidden
-    for start in range(0, hidden, step):
-        columns = slice(start, start + step)
+    normed[: 2 * pixels, :] = n_own[...]
+    normed[2 * pixels :, :] = n_sibling[...]
+    start = pl.multiple_of(side * half + parity * quarter, LANES)
+    cot[:pixels, :] = cot_ref[:, pl.ds(start, quarter)]
+    cot[pixels : 2 * pixels, :] = far_ref[:pixels, :]
+    start = pl.multiple_of(parity * quarter, LANES)
+    cot[2 * pixels : 3 * pixels, :] = sibling_ref[:, pl.ds(start, quarter)]
+    cot[3 * pixels :, :] = far_ref[pixels:, :]
+    for start in range(0, quarter, LANES):
+        columns = slice(start, start + LANES)
         pre_act = jnp.dot(normed[...], weight[:, columns], preferred_element_type=F32)
-        slope = gelu_slope(pre_act)
-        gp_ref[:pixels, columns] = (c_own[:, columns].astype(F32) * slope[:pixels]).astype(BF16)
-        gp_ref[pixels:, columns] = (c_other[:, columns].astype(F32) * slope[pixels:]).astype(BF16)
-        grad[:, columns] = lax.dot_general(
-            normed[...], gp_ref[:, columns], (((0,), (0,)), ((), ())), preferred_element_type=F32
-        )
+        gp_ref[:, columns] = (cot[:, columns].astype(F32) * gelu_slope(pre_act)).astype(BF16)
+    grad[...] = lax.dot_general(
+        normed[...], gp_ref[...], (((0,), (0,)), ((), ())), preferred_element_type=F32
+    )
     split_rows(grad, pieces, own, relative)
 
 
 def back_project_kernel(relative, own, *refs):
     weights = refs[:INNER]
     gp_ref, own_ref, other_ref, weight = refs[INNER:]
-    pixels = own_ref.shape[0]
+    rows = own_ref.shape[0]
     place_rows(weights, weight, own, relative)
     grad_normed = lax.dot_general(
         gp_ref[...], weight[...], (((1,), (1,)), ((), ())), preferred_element_type=F32
     )
-    own_ref[...] = grad_normed[:pixels]
-    other_ref[...] = grad_normed[pixels:]
+    own_ref[...] = grad_normed[:rows]
+    other_ref[...] = grad_normed[rows:]
+
+
+def core_sum_kernel(own_ref, other_ref, kept_ref, sent_ref):
+    pixels = kept_ref.shape[0]
+    kept_ref[...] = own_ref[:pixels] + other_ref[:pixels]
+    sent_ref[...] = (own_ref[pixels:] + other_ref[pixels:]).astype(BF16)
 
 
 def norm_back_kernel(relative, own, *refs):
@@ -173,7 +221,7 @@
     for tile in range(tiles):
         lanes = slice(tile * LANES, (tile + 1) * LANES)
         padded[tile, :, 8 : 8 + breadth, :] = x_ref[0, :, :, lanes].astype(F32)
-        grad_normed = gn_own[:, lanes] + gn_other[:, lanes]
+        grad_normed = gn_own[:, lanes] + gn_other[:, lanes].astype(F32)
         whitened = white_ref[:, lanes]
         product = grad_normed * whitened
         gain = taps_ref[tile, TAPS : TAPS + 1, :]
@@ -187,7 +235,7 @@
     for tile in range(tiles):
         lanes = slice(tile * LANES, (tile + 1) * LANES)
         gain = taps_ref[tile, TAPS : TAPS + 1, :]
-        grad_white = (gn_own[:, lanes] + gn_other[:, lanes]) * gain
+        grad_white = (gn_own[:, lanes] + gn_other[:, lanes].astype(F32)) * gain
         grad_conv = inv_ref[...] * (grad_white - mean_first - white_ref[:, lanes] * mean_second)
         grad_ref[tile] = grad_conv.reshape(height, breadth, LANES)
 
@@ -252,12 +300,13 @@
     own, hidden = up_weight.shape
     depth = own * shards
     lines = shards // INNER
-    half = hidden // 2
+    half, quarter = hidden // 2, hidden // 4
     height, breadth = images.shape[1:3]
     pixels = height * breadth
     tiles = depth // LANES
     me = lax.axis_index("shard")
     side = lax.axis_index("rep") % 2
+    parity = (me // INNER) % 2
     relative = own % 16 == 0
 
     def over_shard(array, flip):
@@ -282,36 +331,48 @@
         moved = jnp.take(stacked, flips ^ me, axis=0).reshape(INNER, lines * own, -1)
         return [moved[0]] + [moved[i].astype(BF16) for i in range(1, INNER)]
 
-    columns = lax.dynamic_slice(up_weight, (0, side * half), (own, half))
-    extras = jnp.concatenate(
-        [
-            depthwise_weight,
-            norm_gain[:, None],
-            norm_bias[:, None],
-            jnp.zeros((own, LANES - TAPS - 2), BF16),
-        ],
-        axis=1,
-    )
-    packed = jnp.concatenate([columns, extras], axis=1)
-    gathered = [packed] + [over_shard(packed, INNER * line) for line in range(1, lines)]
-    weight_lines = jnp.concatenate([g[:, :half] for g in gathered])
-    extra_lines = jnp.concatenate([g[:, half:] for g in gathered])
+    shape = jax.ShapeDtypeStruct
+    near, far = call(
+        pack_kernel,
+        "pack",
+        [shape((own, quarter + LANES), BF16)] * 2,
+        [pltpu.VMEM((LANES, LANES), F32), pltpu.VMEM((own, LANES), F32)],
+        0,
+        up_weight,
+        depthwise_weight,
+        norm_gain[None, :],
+        norm_bias[None, :],
+    )
+    gathered = [near] + [
+        over_shard(far if line % 2 else near, INNER * line) for line in range(1, lines)
+    ]
+    weight_lines = jnp.concatenate([g[:, :quarter] for g in gathered])
+    extra_lines = jnp.concatenate([g[:, quarter:] for g in gathered])
     weights = [weight_lines] + [over_shard(weight_lines, flip) for flip in range(1, INNER)]
     extras = [extra_lines] + [over_shard(extra_lines, flip) for flip in range(1, INNER)]
     weights, extras = true_order(weights), true_order(extras)
 
+    images_far = over_shard(images, INNER)
     cotangent = cotangent.reshape(pixels, hidden)
-    cot_own = lax.dynamic_slice(cotangent, (0, side * half), (pixels, half))
-    cot_other = over_core(lax.dynamic_slice(cotangent, (0, (1 - side) * half), (pixels, half)))
-
-    shape = jax.ShapeDtypeStruct
+    cot_sibling = over_core(lax.dynamic_slice(cotangent, (0, (1 - side) * half), (pixels, half)))
+    (cot_sent,) = call(
+        cot_pack_kernel,
+        "cot_pack",
+        [shape((2 * pixels, quarter), BF16)],
+        [],
+        0,
+        cotangent,
+        cot_sibling,
+    )
+    cot_far = over_shard(cot_sent, INNER)
+
     padded = pltpu.VMEM((tiles, height, breadth + 16, LANES), F32)
     conv_flops = 2 * TAPS * pixels * depth
     normed, whitened, inv_std, taps = call(
         functools.partial(conv_norm_kernel, relative, own),
         "conv_norm",
         [
-            shape((pixels, depth), BF16),
+            shape((2 * pixels, depth), BF16),
             shape((pixels, depth), F32),
             shape((pixels, LANES), F32),
             shape((tiles, LANES, LANES), F32),
@@ -321,44 +382,56 @@
             padded,
             pltpu.VMEM((tiles, pixels, LANES), F32),
         ],
-        conv_flops,
+        2 * conv_flops,
         *extras,
         images,
-    )
-    normed_other = over_core(normed)
+        images_far,
+    )
+    normed_sibling = over_core(normed)
 
     rows = lines * own
     *pieces, grad_pre = call(
         functools.partial(project_kernel, relative, own),
         "project",
-        [shape((rows, half), F32)]
-        + [shape((rows, half), BF16)] * (INNER - 1)
-        + [shape((2 * pixels, half), BF16)],
+        [shape((rows, quarter), F32)]
+        + [shape((rows, quarter), BF16)] * (INNER - 1)
+        + [shape((4 * pixels, quarter), BF16)],
         [
-            pltpu.VMEM((depth, half), BF16),
-            pltpu.VMEM((2 * pixels, depth), BF16),
-            pltpu.VMEM((depth, half), F32),
+            pltpu.VMEM((depth, quarter), BF16),
+            pltpu.VMEM((4 * pixels, depth), BF16),
+            pltpu.VMEM((4 * pixels, quarter), BF16),
+            pltpu.VMEM((depth, quarter), F32),
         ],
-        8 * pixels * depth * half,
+        16 * pixels * depth * quarter,
         *weights,
         normed,
-        normed_other,
-        cot_own,
-        cot_other,
+        normed_sibling,
+        cotangent,
+        cot_sibling,
+        cot_far,
     )
     pieces = relative_order(pieces)
     arrived = [over_shard(piece, flip) for flip, piece in enumerate(pieces) if flip]
 
-    gn_own, gn_send = call(
+    gn_kept, gn_sent = call(
         functools.partial(back_project_kernel, relative, own),
         "back_project",
-        [shape((pixels, depth), F32)] * 2,
-        [pltpu.VMEM((depth, half), BF16)],
-        4 * pixels * depth * half,
+        [shape((2 * pixels, depth), F32)] * 2,
+        [pltpu.VMEM((depth, quarter), BF16)],
+        8 * pixels * depth * quarter,
         *weights,
         grad_pre,
     )
-    gn_other = over_core(gn_send)
+    gn_kept, gn_sent = call(
+        core_sum_kernel,
+        "core_sum",
+        [shape((pixels, depth), F32), shape((pixels, depth), BF16)],
+        [],
+        2 * pixels * depth,
+        gn_kept,
+        over_core(gn_sent),
+    )
+    gn_other = over_shard(gn_sent, INNER)
     *small, grad_conv = call(
         functools.partial(norm_back_kernel, relative, own),
         "norm_back",
@@ -371,7 +444,7 @@
             pltpu.VMEM((depth, LANES), F32),
         ],
         conv_flops,
-        gn_own,
+        gn_kept,
         gn_other,
         whitened,
         inv_std,
@@ -392,20 +465,33 @@
 
     plane = pieces[0] + sum(piece.astype(F32) for piece in arrived)
     small_plane = small[0] + sum(piece.astype(F32) for piece in small_arrived)
-    merged = jnp.concatenate([plane, small_plane], axis=1).reshape(lines, own, half + LANES)
-    total = merged[0]
+    merged = jnp.concatenate([plane, small_plane], axis=1).reshape(lines, own, quarter + LANES)
+    merged, grad_images = lax.optimization_barrier((merged, grad_images))
+    same, cross = merged[0], None
     for line in range(1, lines):
-        total = total + over_shard(merged[line].astype(BF16), INNER * line).astype(F32)
+        came = over_shard(merged[line].astype(BF16), INNER * line).astype(F32)
+        if line % 2 == 0:
+            same = same + came
+        else:
+            cross = came if cross is None else cross + came
+    total = jnp.concatenate(
+        [same[:, :quarter], cross[:, :quarter], same[:, quarter:] + cross[:, quarter:]], axis=1
+    )
     if reps > 2:
         groups = [[i for i in range(reps) if i % 2 == s] for s in range(2)]
         total = lax.psum(total, "rep", axis_index_groups=groups)
     other = over_core(total)
     factor = 1.0 / math.sqrt(images.shape[0] * pixels * shards * reps)
     total, other = total * factor, other * factor
-    grad_up = jnp.where(
-        side == 0,
-        jnp.concatenate([total[:, :half], other[:, :half]], axis=1),
-        jnp.concatenate([other[:, :half], total[:, :half]], axis=1),
+    first = jnp.where(side == 0, total, other)
+    second = jnp.where(side == 0, other, total)
+    grad_up = jnp.concatenate(
+        [
+            jnp.where(parity == 0, part[:, low : low + quarter], part[:, quarter - low : half - low])
+            for part in (first, second)
+            for low in (0, quarter)
+        ],
+        axis=1,
     )
     sums = total[:, half:] + other[:, half:]
     return (grad_images, grad_up, sums[:, :TAPS], sums[:, TAPS], sums[:, TAPS + 1])

time: 71.2 us -> 67.6 us (0.949)
  waiting for transfers between devices: 32.7 us -> 24 us
  starting transfers between devices: 23.7 us -> 28.4 us
  Pallas kernels: 7.06 us -> 8.92 us
  local copies, waits for them, and re-layouts: 5.39 us -> 4.04 us
    ppermute x18 -> x21, waiting for transfers between devices: 31.3 us -> 20.4 us  [over_shard(): return lax.ppermute(array, 'shard', [(i, i ^ flip) for i in range(shards)])]
    ppermute x18 -> x21, starting transfers between devices: 23.5 us -> 28.1 us  [over_shard(): return lax.ppermute(array, 'shard', [(i, i ^ flip) for i in range(shards)])]
    ppermute x4, waiting for transfers between devices: 1.43 us -> 3.63 us  [over_core(): return lax.ppermute(array, 'rep', [(i, i ^ 1) for i in range(reps)])]
    pallas_call x5 -> x8, Pallas kernels: 7.06 us -> 8.92 us  [call(): pl.pallas_call(kernel, out_shape=outs, in_specs=[VMEM] * len(args), out_s...]
    unnamed x16 -> x20, local copies, waits for them, and re-layouts: 3.43 us -> 2.3 us
    dynamic_slice x1, local copies, waits for them, and re-layouts: 0.03 us -> 0.98 us  [body(): lax.dynamic_slice(cotangent, (0, (1 - side) * half), (pixels, half))]
    slice x10 -> x13, local copies, waits for them, and re-layouts: 0.91 us -> 0.05 us  [the longest x7 0.02 us: body(): weight_lines = jnp.concatenate([g[:, :quarter] for g in gathered])]
  transfers between devices with their start and end apart: 22 -> 25, of which waited for: 13 -> 15; matrix products, arithmetic and copies ran while one was open for 0% -> 2% of each run, Pallas kernels for 7% -> 10%
where the time goes in v2:
time: 67.6 us; the launch traced here: 67.4 us
  starting transfers between devices  28.4 us (42%)
  waiting for transfers between devices  24 us (36%)
  Pallas kernels  8.92 us (13%)
  local copies, waits for them, and re-layouts  4.04 us (6%)
  other arithmetic  1.03 us (2%)
  between operations  1.01 us (1%)
    ppermute x21, starting transfers between devices, over_shard(): return lax.ppermute(array, 'shard', [(i, i ^ flip) for i in range(shards)])  28.1 us
    ppermute x21, waiting for transfers between devices, over_shard(): return lax.ppermute(array, 'shard', [(i, i ^ flip) for i in range(shards)])  20.4 us
    pallas_call x8, Pallas kernels, call(): pl.pallas_call(kernel, out_shape=outs, in_specs=[VMEM] * len(args), out_s...  8.92 us
    ppermute x4, waiting for transfers between devices, over_core(): return lax.ppermute(array, 'rep', [(i, i ^ 1) for i in range(reps)])  3.63 us
    unnamed x20, local copies, waits for them, and re-layouts  2.3 us
  transfers between devices with their start and end apart: 25, of which 15 were waited for; matrix products, arithmetic and copies ran while one was open for 2% of the time, Pallas kernels for 10%

profile of v2, /device:TPU:0, one launch (start us, length us, event | category | flops | bytes accessed | tf_op | source)
XLA Modules:
  0.0 67.4 jit_solution(17768187046486037981)
XLA Ops:
  0.7 0.6 copy-done.4
  1.3 0.0 copy-done.5
  1.3 0.9 %copy-done.2 = bf16[48,1536]{1,0:T(8,128)(2,1)S(1)} copy-done((bf16[48,1536]{1,0:T(8,128)(2,1)S(1)}, bf16[48,1536]{1,0:T(8,128)(2,1)}, u32[]{:S(2)}) %copy-start.2) | copy-done | bytes 147480
  2.2 0.7 %copy-done.3 = bf16[48,49]{1,0:T(8,128)(2,1)S(1)} copy-done((bf16[48,49]{1,0:T(8,128)(2,1)S(1)}, bf16[48,49]{1,0:T(8,128)(2,1)}, u32[]{:S(2)}) %copy-start.3) | copy-done | bytes 4728
  2.9 0.1 pack.1
  3.0 5.1 %collective-permute-start.2 = (bf16[48,512]{1,0:T(8,128)(2,1)S(1)}, bf16[48,512]{1,0:T(8,128)(2,1)S(1)}, u32[]{:S(2)}, u32[]{:S(2)}) collective-permute-start(bf16[48,512]{1,0:T(8,128)(2,1)S(1)} %get-tuple-element.28), channel_id=1, source_target_pairs={{0,24},{2,26},{4,28},{6,30},{8,16},{10,18},{12,20},{14,22},{16,8},... | collective-permute-start | bytes 147464 | tf_op jit(solution)/shard_map/ppermute | solution.py:313
  8.1 0.6 collective-permute-start.1
  8.8 1.4 %collective-permute-start.9 = (bf16[1,8,16,768]{3,2,1,0:T(8,128)(2,1)}, bf16[1,8,16,768]{3,2,1,0:T(8,128)(2,1)S(1)}, u32[]{:S(2)}, u32[]{:S(2)}) collective-permute-start(bf16[1,8,16,768]{3,2,1,0:T(8,128)(2,1)} %refs_5_.1), channel_id=1, source_target_pairs={{0,8},{2,10},{4,12},{6,14},{8,0},{10,2},{12,4},{14,6},{16,24},{18,... | collective-permute-start | bytes 589832 | tf_op jit(solution)/shard_map/ppermute | solution.py:313
  10.2 1.0 %constant_dynamic-slice_fusion = bf16[128,768]{1,0:T(8,128)(2,1)S(1)} fusion(bf16[128,1536]{1,0:T(8,128)(2,1)} %bitcast.13, s32[]{:T(128)S(6)} %select_n.51), kind=kLoop, calls=%fused_computation.24 | loop fusion | bytes 393220 | tf_op jit(solution)/shard_map/dynamic_slice | solution.py:357
  11.1 0.1 collective-permute-start.11
  11.2 0.0 copy-start.7
  11.3 1.7 %collective-permute-done = bf16[48,512]{1,0:T(8,128)(2,1)S(1)} collective-permute-done((bf16[48,512]{1,0:T(8,128)(2,1)S(1)}, bf16[48,512]{1,0:T(8,128)(2,1)S(1)}, u32[]{:S(2)}, u32[]{:S(2)}) %collective-permute-start) | collective-permute-done | bytes 49184 | tf_op jit(solution)/shard_map/ppermute | solution.py:313
  12.9 0.6 collective-permute-done.1
  13.5 0.0 copy-start
  13.5 2.5 %collective-permute-start.8 = (bf16[192,128]{1,0:T(8,128)(2,1)S(1)}, bf16[192,128]{1,0:T(8,128)(2,1)S(1)}, u32[]{:S(2)}, u32[]{:S(2)}) collective-permute-start(bf16[192,128]{1,0:T(8,128)(2,1)S(1)} %pad_maximum_fusion.4.refs_0_), channel_id=1, source_target_pairs={{0,6},{2,4},{4,2},{6,0},{8,14},{10,12},{12,10},{14,8},{16,22},{18,... | collective-permute-start | bytes 147464 | tf_op jit(solution)/shard_map/ppermute | solution.py:313
  16.0 0.5 collective-permute-start.7
  16.6 0.5 collective-permute-start.6
  17.1 1.8 %collective-permute-done.8.refs_3_ = bf16[192,128]{1,0:T(8,128)(2,1)S(1)} collective-permute-done((bf16[192,128]{1,0:T(8,128)(2,1)S(1)}, bf16[192,128]{1,0:T(8,128)(2,1)S(1)}, u32[]{:S(2)}, u32[]{:S(2)}) %collective-permute-start.8) | collective-permute-done | bytes 49184 | tf_op jit(solution)/shard_map/ppermute | solution.py:313
  18.9 1.3 %collective-permute-done.7.refs_2_ = bf16[192,128]{1,0:T(8,128)(2,1)S(1)} collective-permute-done((bf16[192,128]{1,0:T(8,128)(2,1)S(1)}, bf16[192,128]{1,0:T(8,128)(2,1)S(1)}, u32[]{:S(2)}, u32[]{:S(2)}) %collective-permute-start.7) | collective-permute-done | bytes 49184 | tf_op jit(solution)/shard_map/ppermute | solution.py:313
  20.1 0.5 collective-permute-done.6.refs_1_
  20.7 2.9 %conv_norm.1 = (bf16[256,768]{1,0:T(8,128)(2,1)S(1)}, f32[128,768]{1,0:T(8,128)S(1)}, f32[128,128]{1,0:T(8,128)S(1)}, f32[6,128,128]{2,1,0:T(8,128)S(1)}) custom-call(bf16[192,128]{1,0:T(8,128)(2,1)S(1)} %pad_maximum_fusion.4.refs_0_, bf16[192,128]{1,0:T(8,128)(2,1)S(1)} %collective-permute-done.6.refs_1_, ...), custom_call_target="tpu_custom_call" | custom-call | flops 19267584 | bytes 1835008 | tf_op jit(solution)/shard_map/conv_norm/pallas_call | solution.py:286
  23.6 0.1 collective-permute-start.10
  23.7 0.0 slice-start
  23.7 0.0 slice-start.1
  23.7 0.0 slice-start.2
  23.7 0.0 collective-permute-done.11.sibling_ref.refs_7_
  23.8 2.3 %collective-permute-start.12 = (bf16[256,384]{1,0:T(8,128)(2,1)S(1)}, bf16[256,384]{1,0:T(8,128)(2,1)S(1)}, u32[]{:S(2)}, u32[]{:S(2)}) collective-permute-start(bf16[256,384]{1,0:T(8,128)(2,1)S(1)} %cot_pack.1), channel_id=1, source_target_pairs={{0,8},{2,10},{4,12},{6,14},{8,0},{10,2},{12,4},{14,6},{16,24},{18,... | collective-permute-start | bytes 589832 | tf_op jit(solution)/shard_map/ppermute | solution.py:313
  26.1 1.6 %collective-permute-start.5 = (bf16[192,384]{1,0:T(8,128)(2,1)S(1)}, bf16[192,384]{1,0:T(8,128)(2,1)S(1)}, u32[]{:S(2)}, u32[]{:S(2)}) collective-permute-start(bf16[192,384]{1,0:T(8,128)(2,1)S(1)} %pad_maximum_fusion.3.refs_0_), channel_id=1, source_target_pairs={{0,6},{2,4},{4,2},{6,0},{8,14},{10,12},{12,10},{14,8},{16,22},{18,... | collective-permute-start | bytes 442376 | tf_op jit(solution)/shard_map/ppermute | solution.py:313
  27.7 0.5 collective-permute-start.4
  28.2 1.5 %collective-permute-start.3 = (bf16[192,384]{1,0:T(8,128)(2,1)S(1)}, bf16[192,384]{1,0:T(8,128)(2,1)S(1)}, u32[]{:S(2)}, u32[]{:S(2)}) collective-permute-start(bf16[192,384]{1,0:T(8,128)(2,1)S(1)} %pad_maximum_fusion.3.refs_0_), channel_id=1, source_target_pairs={{0,2},{2,0},{4,6},{6,4},{8,10},{10,8},{12,14},{14,12},{16,18},{18,... | collective-permute-start | bytes 442376 | tf_op jit(solution)/shard_map/ppermute | solution.py:313
  29.7 4.1 %collective-permute-done.5.refs_3_ = bf16[192,384]{1,0:T(8,128)(2,1)S(1)} collective-permute-done((bf16[192,384]{1,0:T(8,128)(2,1)S(1)}, bf16[192,384]{1,0:T(8,128)(2,1)S(1)}, u32[]{:S(2)}, u32[]{:S(2)}) %collective-permute-start.5) | collective-permute-done | bytes 147488 | tf_op jit(solution)/shard_map/ppermute | solution.py:313
  33.8 2.4 %collective-permute-done.4.refs_2_ = bf16[192,384]{1,0:T(8,128)(2,1)S(1)} collective-permute-done((bf16[192,384]{1,0:T(8,128)(2,1)S(1)}, bf16[192,384]{1,0:T(8,128)(2,1)S(1)}, u32[]{:S(2)}, u32[]{:S(2)}) %collective-permute-start.4) | collective-permute-done | bytes 147488 | tf_op jit(solution)/shard_map/ppermute | solution.py:313
  36.2 0.1 collective-permute-done.3.refs_1_
  36.3 1.6 %project.1 = (f32[192,384]{1,0:T(8,128)S(1)}, bf16[192,384]{1,0:T(8,128)(2,1)S(1)}, bf16[192,384]{1,0:T(8,128)(2,1)S(1)}, bf16[192,384]{1,0:T(8,128)(2,1)S(1)}, bf16[512,384]{1,0:T(8,128)(2,1)S(1)}) custom-call(bf16[192,384]{1,0:T(8,128)(2,1)S(1)} %pad_maximum_fusion.3.refs_0_, bf16[192,384]{1,0:T(8,128)(2,1)S(1)} %collective-permute-done.3.refs_1_, ...), custom_call_target="tpu_custom_call" | custom-call | flops 603979776 | bytes 3293184 | tf_op jit(solution)/shard_map/project/pallas_call | solution.py:286
  37.9 0.7 back_project.1
  38.6 0.1 collective-permute-start.16
  38.6 2.3 %collective-permute-done.16.other_ref = f32[256,768]{1,0:T(8,128)S(1)} collective-permute-done((f32[256,768]{1,0:T(8,128)S(1)}, f32[256,768]{1,0:T(8,128)S(1)}, u32[]{:S(2)}, u32[]{:S(2)}) %collective-permute-start.16) | collective-permute-done | bytes 786464 | tf_op jit(solution)/shard_map/ppermute | solution.py:316
  40.9 0.1 core_sum.1
  41.0 1.0 %collective-permute-start.17 = (bf16[128,768]{1,0:T(8,128)(2,1)S(1)}, bf16[128,768]{1,0:T(8,128)(2,1)S(1)}, u32[]{:S(2)}, u32[]{:S(2)}) collective-permute-start(bf16[128,768]{1,0:T(8,128)(2,1)S(1)} %get-tuple-element.38), channel_id=1, source_target_pairs={{0,8},{2,10},{4,12},{6,14},{8,0},{10,2},{12,4},{14,6},{16,24},{18,... | collective-permute-start | bytes 589832 | tf_op jit(solution)/shard_map/ppermute | solution.py:313
  42.0 0.5 collective-permute-start.13
  42.5 1.4 %collective-permute-start.14 = (bf16[192,384]{1,0:T(8,128)(2,1)S(1)}, bf16[192,384]{1,0:T(8,128)(2,1)S(1)}, u32[]{:S(2)}, u32[]{:S(2)}) collective-permute-start(bf16[192,384]{1,0:T(8,128)(2,1)S(1)} %get-tuple-element.32), channel_id=1, source_target_pairs={{0,4},{2,6},{4,0},{6,2},{8,12},{10,14},{12,8},{14,10},{16,20},{18,... | collective-permute-start | bytes 442376 | tf_op jit(solution)/shard_map/ppermute | solution.py:313
  43.9 1.5 %collective-permute-start.15 = (bf16[192,384]{1,0:T(8,128)(2,1)S(1)}, bf16[192,384]{1,0:T(8,128)(2,1)S(1)}, u32[]{:S(2)}, u32[]{:S(2)}) collective-permute-start(bf16[192,384]{1,0:T(8,128)(2,1)S(1)} %get-tuple-element.33), channel_id=1, source_target_pairs={{0,6},{2,4},{4,2},{6,0},{8,14},{10,12},{12,10},{14,8},{16,22},{18,... | collective-permute-start | bytes 442376 | tf_op jit(solution)/shard_map/ppermute | solution.py:313
  45.5 2.5 %collective-permute-done.17.refs_1_ = bf16[128,768]{1,0:T(8,128)(2,1)S(1)} collective-permute-done((bf16[128,768]{1,0:T(8,128)(2,1)S(1)}, bf16[128,768]{1,0:T(8,128)(2,1)S(1)}, u32[]{:S(2)}, u32[]{:S(2)}) %collective-permute-start.17) | collective-permute-done | bytes 196640 | tf_op jit(solution)/shard_map/ppermute | solution.py:313
  48.0 1.7 %norm_back.1 = (f32[192,128]{1,0:T(8,128)S(1)}, bf16[192,128]{1,0:T(8,128)(2,1)S(1)}, bf16[192,128]{1,0:T(8,128)(2,1)S(1)}, bf16[192,128]{1,0:T(8,128)(2,1)S(1)}, f32[6,8,16,128]{3,2,1,0:T(8,128)S(1)}) custom-call(f32[128,768]{1,0:T(8,128)S(1)} %get-tuple-element.37.refs_0_, bf16[128,768]{1,0:T(8,128)(2,1)S(1)} %collective-permute-done.17.refs_1_, ...), custom_call_target="tpu_custom_call" | custom-call | flops 9633792 | bytes 2277376 | tf_op jit(solution)/shard_map/norm_back/pallas_call | solution.py:286
  49.7 0.6 collective-permute-start.18
  50.3 1.4 %collective-permute-start.19 = (bf16[192,128]{1,0:T(8,128)(2,1)S(1)}, bf16[192,128]{1,0:T(8,128)(2,1)S(1)}, u32[]{:S(2)}, u32[]{:S(2)}) collective-permute-start(bf16[192,128]{1,0:T(8,128)(2,1)S(1)} %get-tuple-element.44), channel_id=1, source_target_pairs={{0,4},{2,6},{4,0},{6,2},{8,12},{10,14},{12,8},{14,10},{16,20},{18,... | collective-permute-start | bytes 147464 | tf_op jit(solution)/shard_map/ppermute | solution.py:313
  51.7 0.0 collective-permute-done.13
  51.7 1.5 %collective-permute-start.20 = (bf16[192,128]{1,0:T(8,128)(2,1)S(1)}, bf16[192,128]{1,0:T(8,128)(2,1)S(1)}, u32[]{:S(2)}, u32[]{:S(2)}) collective-permute-start(bf16[192,128]{1,0:T(8,128)(2,1)S(1)} %get-tuple-element.45), channel_id=1, source_target_pairs={{0,6},{2,4},{4,2},{6,0},{8,14},{10,12},{12,10},{14,8},{16,22},{18,... | collective-permute-start | bytes 147464 | tf_op jit(solution)/shard_map/ppermute | solution.py:313
  53.3 0.0 collective-permute-done.14
  53.3 0.0 collective-permute-done.15
  53.3 0.1 add_add_fusion
  53.3 1.9 %conv_back.1 = bf16[1,8,16,768]{3,2,1,0:T(8,128)(2,1)} custom-call(f32[6,8,16,128]{3,2,1,0:T(8,128)S(1)} %get-tuple-element.46.grad_ref, f32[6,128,128]{2,1,0:T(8,128)S(1)} %get-tuple-element.41.refs_4_.taps_ref), custom_call_target="tpu_custom_call" | custom-call | flops 9633792 | bytes 983040 | tf_op jit(solution)/shard_map/conv_back/pallas_call | solution.py:286
  55.2 1.5 %collective-permute-done.20 = bf16[192,128]{1,0:T(8,128)(2,1)S(1)} collective-permute-done((bf16[192,128]{1,0:T(8,128)(2,1)S(1)}, bf16[192,128]{1,0:T(8,128)(2,1)S(1)}, u32[]{:S(2)}, u32[]{:S(2)}) %collective-permute-start.20) | collective-permute-done | bytes 49184 | tf_op jit(solution)/shard_map/ppermute | solution.py:313
  56.9 1.0 %collective-permute-start.21 = (bf16[48,512]{1,0:T(8,128)(2,1)S(1)}, bf16[48,512]{1,0:T(8,128)(2,1)S(1)}, u32[]{:S(2)}, u32[]{:S(2)}) collective-permute-start(bf16[48,512]{1,0:T(8,128)(2,1)S(1)} %get-tuple-element.53), channel_id=1, source_target_pairs={{0,16},{2,18},{4,20},{6,22},{8,24},{10,26},{12,28},{14,30},{16,0},... | collective-permute-start | bytes 147464 | tf_op jit(solution)/shard_map/ppermute | solution.py:313
  57.9 2.3 %collective-permute-start.23 = (bf16[48,512]{1,0:T(8,128)(2,1)S(1)}, bf16[48,512]{1,0:T(8,128)(2,1)S(1)}, u32[]{:S(2)}, u32[]{:S(2)}) collective-permute-start(bf16[48,512]{1,0:T(8,128)(2,1)S(1)} %get-tuple-element.54), channel_id=1, source_target_pairs={{0,24},{2,26},{4,28},{6,30},{8,16},{10,18},{12,20},{14,22},{16,8},... | collective-permute-start | bytes 147464 | tf_op jit(solution)/shard_map/ppermute | solution.py:313
  60.2 0.2 collective-permute-start.22
  60.4 2.0 %collective-permute-done.21 = bf16[48,512]{1,0:T(8,128)(2,1)S(1)} collective-permute-done((bf16[48,512]{1,0:T(8,128)(2,1)S(1)}, bf16[48,512]{1,0:T(8,128)(2,1)S(1)}, u32[]{:S(2)}, u32[]{:S(2)}) %collective-permute-start.21) | collective-permute-done | bytes 49184 | tf_op jit(solution)/shard_map/ppermute | solution.py:313
  62.5 1.3 %collective-permute-done.23 = bf16[48,512]{1,0:T(8,128)(2,1)S(1)} collective-permute-done((bf16[48,512]{1,0:T(8,128)(2,1)S(1)}, bf16[48,512]{1,0:T(8,128)(2,1)S(1)}, u32[]{:S(2)}, u32[]{:S(2)}) %collective-permute-start.23) | collective-permute-done | bytes 49184 | tf_op jit(solution)/shard_map/ppermute | solution.py:313
  63.7 0.5 collective-permute-done.22
  64.4 0.1 collective-permute-start.24
  64.5 1.4 %collective-permute-done.24 = f32[48,896]{1,0:T(8,128)S(1)} collective-permute-done((f32[48,896]{1,0:T(8,128)S(1)}, f32[48,896]{1,0:T(8,128)S(1)}, u32[]{:S(2)}, u32[]{:S(2)}) %collective-permute-start.24) | collective-permute-done | bytes 172064 | tf_op jit(solution)/shard_map/ppermute | solution.py:316
  65.9 0.0 copy-start.6
  65.9 0.7 %slice_reduce_fusion = (f32[48]{0:T(128)}, f32[48]{0:T(128)}) fusion(f32[48,128]{1,0:T(8,128)S(1)} %slice_add_fusion), kind=kLoop, calls=%fused_computation.20 | loop fusion | bytes 768 | tf_op jit(solution)/shard_map/slice | solution.py:497
  66.6 0.7 %pad_maximum_fusion.1 = f32[48,1536]{1,0:T(8,128)} fusion(f32[48,384]{1,0:T(8,128)S(1)} %get-tuple-element.61, f32[48,384]{1,0:T(8,128)S(1)} %get-tuple-element.60, f32[48,384]{1,0:T(8,128)S(1)} %get-tuple-element.62, f32[48,384]{1,0:T(8,128)S(1)} %get-tuple-element.63), kind=kLoop, calls=%fused_computation.1 | loop fusion | flops 221184 | bytes 589824 | tf_op jit(solution)/shard_map/concatenate | solution.py:488
  (44 shorter events, 0.4 us)
Async XLA Ops:
  0.6 0.7 copy-start.4
  0.6 0.7 copy-start.5
  1.3 0.9 %copy-start.2 = (bf16[48,1536]{1,0:T(8,128)(2,1)S(1)}, bf16[48,1536]{1,0:T(8,128)(2,1)}, u32[]{:S(2)}) copy-start(bf16[48,1536]{1,0:T(8,128)(2,1)} %w_ref.1) | copy-start | bytes 442372
  2.2 0.7 %copy-start.3 = (bf16[48,49]{1,0:T(8,128)(2,1)S(1)}, bf16[48,49]{1,0:T(8,128)(2,1)}, u32[]{:S(2)}) copy-start(bf16[48,49]{1,0:T(8,128)(2,1)} %dw_ref.1) | copy-start | bytes 14116
  3.0 8.2 %collective-permute-start.2 = (bf16[48,512]{1,0:T(8,128)(2,1)S(1)}, bf16[48,512]{1,0:T(8,128)(2,1)S(1)}, u32[]{:S(2)}, u32[]{:S(2)}) collective-permute-start(bf16[48,512]{1,0:T(8,128)(2,1)S(1)} %get-tuple-element.28), channel_id=1, source_target_pairs={{0,24},{2,26},{4,28},{6,30},{8,16},{10,18},{12,20},{14,22},{16,8},... | collective-permute-start | bytes 147464 | tf_op jit(solution)/shard_map/ppermute | solution.py:313
  8.1 4.8 %collective-permute-start = (bf16[48,512]{1,0:T(8,128)(2,1)S(1)}, bf16[48,512]{1,0:T(8,128)(2,1)S(1)}, u32[]{:S(2)}, u32[]{:S(2)}) collective-permute-start(bf16[48,512]{1,0:T(8,128)(2,1)S(1)} %get-tuple-element.28), channel_id=1, source_target_pairs={{0,8},{2,10},{4,12},{6,14},{8,0},{10,2},{12,4},{14,6},{16,24},{18,... | collective-permute-start | bytes 147464 | tf_op jit(solution)/shard_map/ppermute | solution.py:313
  8.1 5.4 %collective-permute-start.1 = (bf16[48,512]{1,0:T(8,128)(2,1)S(1)}, bf16[48,512]{1,0:T(8,128)(2,1)S(1)}, u32[]{:S(2)}, u32[]{:S(2)}) collective-permute-start(bf16[48,512]{1,0:T(8,128)(2,1)S(1)} %get-tuple-element.27), channel_id=1, source_target_pairs={{0,16},{2,18},{4,20},{6,22},{8,24},{10,26},{12,28},{14,30},{16,0},... | collective-permute-start | bytes 147464 | tf_op jit(solution)/shard_map/ppermute | solution.py:313
  8.8 11.9 %collective-permute-start.9 = (bf16[1,8,16,768]{3,2,1,0:T(8,128)(2,1)}, bf16[1,8,16,768]{3,2,1,0:T(8,128)(2,1)S(1)}, u32[]{:S(2)}, u32[]{:S(2)}) collective-permute-start(bf16[1,8,16,768]{3,2,1,0:T(8,128)(2,1)} %refs_5_.1), channel_id=1, source_target_pairs={{0,8},{2,10},{4,12},{6,14},{8,0},{10,2},{12,4},{14,6},{16,24},{18,... | collective-permute-start | bytes 589832 | tf_op jit(solution)/shard_map/ppermute | solution.py:313
  10.2 10.5 %copy-start.1 = (bf16[1,8,16,768]{3,2,1,0:T(8,128)(2,1)S(1)}, bf16[1,8,16,768]{3,2,1,0:T(8,128)(2,1)}, u32[]{:S(2)}) copy-start(bf16[1,8,16,768]{3,2,1,0:T(8,128)(2,1)} %refs_5_.1) | copy-start | bytes 589828
  11.1 12.6 %collective-permute-start.11 = (bf16[128,768]{1,0:T(8,128)(2,1)S(1)}, bf16[128,768]{1,0:T(8,128)(2,1)S(1)}, u32[]{:S(2)}, u32[]{:S(2)}) collective-permute-start(bf16[128,768]{1,0:T(8,128)(2,1)S(1)} %constant_dynamic-slice_fusion), channel_id=1, source_target_pairs={{0,1},{1,0},{2,3},{3,2},{4,5},{5,4},{6,7},{7,6},{8,9},{9,8},{10,11... | collective-permute-start | bytes 589832 | tf_op jit(solution)/shard_map/ppermute | solution.py:316
  11.2 12.4 %copy-start.7 = (bf16[48,512]{1,0:T(8,128)(2,1)}, bf16[48,512]{1,0:T(8,128)(2,1)S(1)}, u32[]{:S(2)}) copy-start(bf16[48,512]{1,0:T(8,128)(2,1)S(1)} %collective-permute-done.2) | copy-start | bytes 147460
  12.9 10.7 %copy-start.8 = (bf16[48,512]{1,0:T(8,128)(2,1)}, bf16[48,512]{1,0:T(8,128)(2,1)S(1)}, u32[]{:S(2)}) copy-start(bf16[48,512]{1,0:T(8,128)(2,1)S(1)} %collective-permute-done) | copy-start | bytes 147460
  13.5 10.2 %copy-start.9 = (bf16[48,512]{1,0:T(8,128)(2,1)}, bf16[48,512]{1,0:T(8,128)(2,1)S(1)}, u32[]{:S(2)}) copy-start(bf16[48,512]{1,0:T(8,128)(2,1)S(1)} %collective-permute-done.1) | copy-start | bytes 147460
  13.5 10.2 %copy-start = (bf16[1,8,16,1536]{3,2,1,0:T(8,128)(2,1)S(1)}, bf16[1,8,16,1536]{3,2,1,0:T(8,128)(2,1)}, u32[]{:S(2)}) copy-start(bf16[1,8,16,1536]{3,2,1,0:T(8,128)(2,1)} %param.7) | copy-start | bytes 1179652
  13.5 5.4 %collective-permute-start.8 = (bf16[192,128]{1,0:T(8,128)(2,1)S(1)}, bf16[192,128]{1,0:T(8,128)(2,1)S(1)}, u32[]{:S(2)}, u32[]{:S(2)}) collective-permute-start(bf16[192,128]{1,0:T(8,128)(2,1)S(1)} %pad_maximum_fusion.4.refs_0_), channel_id=1, source_target_pairs={{0,6},{2,4},{4,2},{6,0},{8,14},{10,12},{12,10},{14,8},{16,22},{18,... | collective-permute-start | bytes 147464 | tf_op jit(solution)/shard_map/ppermute | solution.py:313
  16.0 4.1 %collective-permute-start.7 = (bf16[192,128]{1,0:T(8,128)(2,1)S(1)}, bf16[192,128]{1,0:T(8,128)(2,1)S(1)}, u32[]{:S(2)}, u32[]{:S(2)}) collective-permute-start(bf16[192,128]{1,0:T(8,128)(2,1)S(1)} %pad_maximum_fusion.4.refs_0_), channel_id=1, source_target_pairs={{0,4},{2,6},{4,0},{6,2},{8,12},{10,14},{12,8},{14,10},{16,20},{18,... | collective-permute-start | bytes 147464 | tf_op jit(solution)/shard_map/ppermute | solution.py:313
  16.6 4.1 %collective-permute-start.6 = (bf16[192,128]{1,0:T(8,128)(2,1)S(1)}, bf16[192,128]{1,0:T(8,128)(2,1)S(1)}, u32[]{:S(2)}, u32[]{:S(2)}) collective-permute-start(bf16[192,128]{1,0:T(8,128)(2,1)S(1)} %pad_maximum_fusion.4.refs_0_), channel_id=1, source_target_pairs={{0,2},{2,0},{4,6},{6,4},{8,10},{10,8},{12,14},{14,12},{16,18},{18,... | collective-permute-start | bytes 147464 | tf_op jit(solution)/shard_map/ppermute | solution.py:313
  23.6 12.7 %collective-permute-start.10 = (bf16[256,768]{1,0:T(8,128)(2,1)S(1)}, bf16[256,768]{1,0:T(8,128)(2,1)S(1)}, u32[]{:S(2)}, u32[]{:S(2)}) collective-permute-start(bf16[256,768]{1,0:T(8,128)(2,1)S(1)} %get-tuple-element.29.refs_4_), channel_id=1, source_target_pairs={{0,1},{1,0},{2,3},{3,2},{4,5},{5,4},{6,7},{7,6},{8,9},{9,8},{10,11... | collective-permute-start | bytes 1179656 | tf_op jit(solution)/shard_map/ppermute | solution.py:316
  23.7 2.4 %slice-start = ((bf16[48,512]{1,0:T(8,128)(2,1)}), bf16[48,384]{1,0:T(8,128)(2,1)S(1)}, s32[]{:S(2)}) async-start(bf16[48,512]{1,0:T(8,128)(2,1)} %copy-done.7), calls=%async_computation | async-start | bytes 73728 | tf_op jit(solution)/shard_map/slice | solution.py:349
  23.7 2.4 %slice-start.1 = ((bf16[48,512]{1,0:T(8,128)(2,1)}), bf16[48,384]{1,0:T(8,128)(2,1)S(1)}, s32[]{:S(2)}) async-start(bf16[48,512]{1,0:T(8,128)(2,1)} %copy-done.8), calls=%async_computation.1 | async-start | bytes 73728 | tf_op jit(solution)/shard_map/slice | solution.py:349
  23.7 2.4 %slice-start.2 = ((bf16[48,512]{1,0:T(8,128)(2,1)}), bf16[48,384]{1,0:T(8,128)(2,1)S(1)}, s32[]{:S(2)}) async-start(bf16[48,512]{1,0:T(8,128)(2,1)} %copy-done.9), calls=%async_computation.2 | async-start | bytes 73728 | tf_op jit(solution)/shard_map/slice | solution.py:349
  23.8 12.5 %collective-permute-start.12 = (bf16[256,384]{1,0:T(8,128)(2,1)S(1)}, bf16[256,384]{1,0:T(8,128)(2,1)S(1)}, u32[]{:S(2)}, u32[]{:S(2)}) collective-permute-start(bf16[256,384]{1,0:T(8,128)(2,1)S(1)} %cot_pack.1), channel_id=1, source_target_pairs={{0,8},{2,10},{4,12},{6,14},{8,0},{10,2},{12,4},{14,6},{16,24},{18,... | collective-permute-start | bytes 589832 | tf_op jit(solution)/shard_map/ppermute | solution.py:313
  26.1 7.7 %collective-permute-start.5 = (bf16[192,384]{1,0:T(8,128)(2,1)S(1)}, bf16[192,384]{1,0:T(8,128)(2,1)S(1)}, u32[]{:S(2)}, u32[]{:S(2)}) collective-permute-start(bf16[192,384]{1,0:T(8,128)(2,1)S(1)} %pad_maximum_fusion.3.refs_0_), channel_id=1, source_target_pairs={{0,6},{2,4},{4,2},{6,0},{8,14},{10,12},{12,10},{14,8},{16,22},{18,... | collective-permute-start | bytes 442376 | tf_op jit(solution)/shard_map/ppermute | solution.py:313
  27.7 8.5 %collective-permute-start.4 = (bf16[192,384]{1,0:T(8,128)(2,1)S(1)}, bf16[192,384]{1,0:T(8,128)(2,1)S(1)}, u32[]{:S(2)}, u32[]{:S(2)}) collective-permute-start(bf16[192,384]{1,0:T(8,128)(2,1)S(1)} %pad_maximum_fusion.3.refs_0_), channel_id=1, source_target_pairs={{0,4},{2,6},{4,0},{6,2},{8,12},{10,14},{12,8},{14,10},{16,20},{18,... | collective-permute-start | bytes 442376 | tf_op jit(solution)/shard_map/ppermute | solution.py:313
  28.2 8.1 %collective-permute-start.3 = (bf16[192,384]{1,0:T(8,128)(2,1)S(1)}, bf16[192,384]{1,0:T(8,128)(2,1)S(1)}, u32[]{:S(2)}, u32[]{:S(2)}) collective-permute-start(bf16[192,384]{1,0:T(8,128)(2,1)S(1)} %pad_maximum_fusion.3.refs_0_), channel_id=1, source_target_pairs={{0,2},{2,0},{4,6},{6,4},{8,10},{10,8},{12,14},{14,12},{16,18},{18,... | collective-permute-start | bytes 442376 | tf_op jit(solution)/shard_map/ppermute | solution.py:313
  38.6 2.4 %collective-permute-start.16 = (f32[256,768]{1,0:T(8,128)S(1)}, f32[256,768]{1,0:T(8,128)S(1)}, u32[]{:S(2)}, u32[]{:S(2)}) collective-permute-start(f32[256,768]{1,0:T(8,128)S(1)} %get-tuple-element.36), channel_id=1, source_target_pairs={{0,1},{1,0},{2,3},{3,2},{4,5},{5,4},{6,7},{7,6},{8,9},{9,8},{10,11... | collective-permute-start | bytes 2359304 | tf_op jit(solution)/shard_map/ppermute | solution.py:316
  41.0 7.0 %collective-permute-start.17 = (bf16[128,768]{1,0:T(8,128)(2,1)S(1)}, bf16[128,768]{1,0:T(8,128)(2,1)S(1)}, u32[]{:S(2)}, u32[]{:S(2)}) collective-permute-start(bf16[128,768]{1,0:T(8,128)(2,1)S(1)} %get-tuple-element.38), channel_id=1, source_target_pairs={{0,8},{2,10},{4,12},{6,14},{8,0},{10,2},{12,4},{14,6},{16,24},{18,... | collective-permute-start | bytes 589832 | tf_op jit(solution)/shard_map/ppermute | solution.py:313
  42.0 9.8 %collective-permute-start.13 = (bf16[192,384]{1,0:T(8,128)(2,1)S(1)}, bf16[192,384]{1,0:T(8,128)(2,1)S(1)}, u32[]{:S(2)}, u32[]{:S(2)}) collective-permute-start(bf16[192,384]{1,0:T(8,128)(2,1)S(1)} %get-tuple-element.31), channel_id=1, source_target_pairs={{0,2},{2,0},{4,6},{6,4},{8,10},{10,8},{12,14},{14,12},{16,18},{18,... | collective-permute-start | bytes 442376 | tf_op jit(solution)/shard_map/ppermute | solution.py:313
  42.5 10.8 %collective-permute-start.14 = (bf16[192,384]{1,0:T(8,128)(2,1)S(1)}, bf16[192,384]{1,0:T(8,128)(2,1)S(1)}, u32[]{:S(2)}, u32[]{:S(2)}) collective-permute-start(bf16[192,384]{1,0:T(8,128)(2,1)S(1)} %get-tuple-element.32), channel_id=1, source_target_pairs={{0,4},{2,6},{4,0},{6,2},{8,12},{10,14},{12,8},{14,10},{16,20},{18,... | collective-permute-start | bytes 442376 | tf_op jit(solution)/shard_map/ppermute | solution.py:313
  43.9 9.3 %collective-permute-start.15 = (bf16[192,384]{1,0:T(8,128)(2,1)S(1)}, bf16[192,384]{1,0:T(8,128)(2,1)S(1)}, u32[]{:S(2)}, u32[]{:S(2)}) collective-permute-start(bf16[192,384]{1,0:T(8,128)(2,1)S(1)} %get-tuple-element.33), channel_id=1, source_target_pairs={{0,6},{2,4},{4,2},{6,0},{8,14},{10,12},{12,10},{14,8},{16,22},{18,... | collective-permute-start | bytes 442376 | tf_op jit(solution)/shard_map/ppermute | solution.py:313
  49.7 5.5 %collective-permute-start.18 = (bf16[192,128]{1,0:T(8,128)(2,1)S(1)}, bf16[192,128]{1,0:T(8,128)(2,1)S(1)}, u32[]{:S(2)}, u32[]{:S(2)}) collective-permute-start(bf16[192,128]{1,0:T(8,128)(2,1)S(1)} %get-tuple-element.43), channel_id=1, source_target_pairs={{0,2},{2,0},{4,6},{6,4},{8,10},{10,8},{12,14},{14,12},{16,18},{18,... | collective-permute-start | bytes 147464 | tf_op jit(solution)/shard_map/ppermute | solution.py:313
  50.3 4.9 %collective-permute-start.19 = (bf16[192,128]{1,0:T(8,128)(2,1)S(1)}, bf16[192,128]{1,0:T(8,128)(2,1)S(1)}, u32[]{:S(2)}, u32[]{:S(2)}) collective-permute-start(bf16[192,128]{1,0:T(8,128)(2,1)S(1)} %get-tuple-element.44), channel_id=1, source_target_pairs={{0,4},{2,6},{4,0},{6,2},{8,12},{10,14},{12,8},{14,10},{16,20},{18,... | collective-permute-start | bytes 147464 | tf_op jit(solution)/shard_map/ppermute | solution.py:313
  51.7 5.0 %collective-permute-start.20 = (bf16[192,128]{1,0:T(8,128)(2,1)S(1)}, bf16[192,128]{1,0:T(8,128)(2,1)S(1)}, u32[]{:S(2)}, u32[]{:S(2)}) collective-permute-start(bf16[192,128]{1,0:T(8,128)(2,1)S(1)} %get-tuple-element.45), channel_id=1, source_target_pairs={{0,6},{2,4},{4,2},{6,0},{8,14},{10,12},{12,10},{14,8},{16,22},{18,... | collective-permute-start | bytes 147464 | tf_op jit(solution)/shard_map/ppermute | solution.py:313
  56.9 5.6 %collective-permute-start.21 = (bf16[48,512]{1,0:T(8,128)(2,1)S(1)}, bf16[48,512]{1,0:T(8,128)(2,1)S(1)}, u32[]{:S(2)}, u32[]{:S(2)}) collective-permute-start(bf16[48,512]{1,0:T(8,128)(2,1)S(1)} %get-tuple-element.53), channel_id=1, source_target_pairs={{0,16},{2,18},{4,20},{6,22},{8,24},{10,26},{12,28},{14,30},{16,0},... | collective-permute-start | bytes 147464 | tf_op jit(solution)/shard_map/ppermute | solution.py:313
  57.9 5.9 %collective-permute-start.23 = (bf16[48,512]{1,0:T(8,128)(2,1)S(1)}, bf16[48,512]{1,0:T(8,128)(2,1)S(1)}, u32[]{:S(2)}, u32[]{:S(2)}) collective-permute-start(bf16[48,512]{1,0:T(8,128)(2,1)S(1)} %get-tuple-element.54), channel_id=1, source_target_pairs={{0,24},{2,26},{4,28},{6,30},{8,16},{10,18},{12,20},{14,22},{16,8},... | collective-permute-start | bytes 147464 | tf_op jit(solution)/shard_map/ppermute | solution.py:313
  60.2 4.1 %collective-permute-start.22 = (bf16[48,512]{1,0:T(8,128)(2,1)S(1)}, bf16[48,512]{1,0:T(8,128)(2,1)S(1)}, u32[]{:S(2)}, u32[]{:S(2)}) collective-permute-start(bf16[48,512]{1,0:T(8,128)(2,1)S(1)} %get-tuple-element.55), channel_id=1, source_target_pairs={{0,8},{2,10},{4,12},{6,14},{8,0},{10,2},{12,4},{14,6},{16,24},{18,... | collective-permute-start | bytes 147464 | tf_op jit(solution)/shard_map/ppermute | solution.py:313
  64.4 1.5 %collective-permute-start.24 = (f32[48,896]{1,0:T(8,128)S(1)}, f32[48,896]{1,0:T(8,128)S(1)}, u32[]{:S(2)}, u32[]{:S(2)}) collective-permute-start(f32[48,896]{1,0:T(8,128)S(1)} %pad_maximum_fusion.2), channel_id=1, source_target_pairs={{0,1},{1,0},{2,3},{3,2},{4,5},{5,4},{6,7},{7,6},{8,9},{9,8},{10,11... | collective-permute-start | bytes 516104 | tf_op jit(solution)/shard_map/ppermute | solution.py:316
  65.9 0.7 %copy-start.6 = (f32[48,128]{1,0:T(8,128)}, f32[48,128]{1,0:T(8,128)S(1)}, u32[]{:S(2)}) copy-start(f32[48,128]{1,0:T(8,128)S(1)} %slice_add_fusion) | copy-start | bytes 73732

commit v3 on v2

--- a/solution.py
+++ b/solution.py
@@ -78,15 +78,23 @@
     return sums
 
 
-def pack_kernel(w_ref, dw_ref, gain_ref, bias_ref, near_ref, far_ref, turned, wide):
+def pack_kernel(w_hbm, dw_hbm, gain_ref, bias_ref, near_ref, far_ref, w_ref, dw_ref, turned, wide, sems):
     own, hidden = w_ref.shape
     quarter = hidden // 4
     side = lax.axis_index("rep") % 2
     parity = (lax.axis_index("shard") // INNER) % 2
+    copies = [
+        pltpu.make_async_copy(w_hbm, w_ref, sems.at[0]),
+        pltpu.make_async_copy(dw_hbm, dw_ref, sems.at[1]),
+    ]
+    for copy in copies:
+        copy.start()
     turned[...] = jnp.zeros_like(turned)
     turned[TAPS : TAPS + 1, :own] = gain_ref[...].astype(F32)
     turned[TAPS + 1 : TAPS + 2, :own] = bias_ref[...].astype(F32)
     wide[...] = jnp.zeros_like(wide)
+    for copy in copies:
+        copy.wait()
     wide[:, :TAPS] = dw_ref[...].astype(F32)
     extras = (wide[...] + turned[...].T[:own]).astype(BF16)
     for ref, which in ((near_ref, parity), (far_ref, 1 - parity)):
@@ -95,10 +103,36 @@
         ref[:, quarter:] = extras
 
 
+def assemble_kernel(*refs):
+    pieces, (weight_ref, extra_ref) = refs[:-2], refs[-2:]
+    own = pieces[0].shape[0]
+    quarter = weight_ref.shape[1]
+    for line, piece in enumerate(pieces):
+        weight_ref[line * own : (line + 1) * own, :] = piece[:, :quarter]
+        extra_ref[line * own : (line + 1) * own, :] = piece[:, quarter:]
+
+
+def finish_kernel(factor, mine_ref, other_ref, up_ref, dw_ref, gain_ref, bias_ref):
+    own, half = mine_ref.shape[0], mine_ref.shape[1] - LANES
+    quarter = half // 2
+    side = lax.axis_index("rep") % 2
+    parity = (lax.axis_index("shard") // INNER) % 2
+    for ref, place in ((mine_ref, side), (other_ref, 1 - side)):
+        for which, low in ((parity, 0), (1 - parity, quarter)):
+            start = pl.multiple_of(place * half + which * quarter, LANES)
+            up_ref[:, pl.ds(start, quarter)] = ref[:, low : low + quarter] * factor
+    sums = (mine_ref[:, half:] + other_ref[:, half:]) * factor
+    dw_ref[...] = sums[:, :TAPS]
+    turned = sums.T
+    gain_ref[...] = turned[TAPS : TAPS + 1, :]
+    bias_ref[...] = turned[TAPS + 1 : TAPS + 2, :]
+
+
 def conv_norm_kernel(relative, own, *refs):
     small = refs[:INNER]
-    x_ref, other_ref = refs[INNER : INNER + 2]
-    normed_ref, white_ref, inv_ref, taps_ref, gathered, padded, conv = refs[INNER + 2 :]
+    sources = refs[INNER : INNER + 4]
+    x_ref = sources[0]
+    normed_ref, white_ref, inv_ref, taps_ref, gathered, padded, conv = refs[INNER + 4 :]
     height, breadth, depth = x_ref.shape[1:]
     tiles = depth // LANES
     pixels = height * breadth
@@ -108,7 +142,7 @@
         lanes = slice(tile * LANES, (tile + 1) * LANES)
         taps_ref[tile] = gathered[lanes, :].T
 
-    for image, source in enumerate((x_ref, other_ref)):
+    for image, source in enumerate(sources):
         for tile in range(tiles):
             lanes = slice(tile * LANES, (tile + 1) * LANES)
             padded[tile, :, 8 : 8 + breadth, :] = source[0, :, :, lanes].astype(F32)
@@ -163,16 +197,14 @@
 
 def project_kernel(relative, own, *refs):
     weights = refs[:INNER]
-    n_own, n_sibling, cot_ref, sibling_ref, far_ref = refs[INNER : INNER + 5]
-    pieces = refs[INNER + 5 : 2 * INNER + 5]
-    gp_ref, weight, normed, cot, grad = refs[2 * INNER + 5 :]
+    normed, cot_ref, sibling_ref, far_ref = refs[INNER : INNER + 4]
+    pieces = refs[INNER + 4 : 2 * INNER + 4]
+    gp_ref, weight, cot, grad = refs[2 * INNER + 4 :]
     pixels, half = sibling_ref.shape
     quarter = half // 2
     side = lax.axis_index("rep") % 2
     parity = (lax.axis_index("shard") // INNER) % 2
     place_rows(weights, weight, own, relative)
-    normed[: 2 * pixels, :] = n_own[...]
-    normed[2 * pixels :, :] = n_sibling[...]
     start = pl.multiple_of(side * half + parity * quarter, LANES)
     cot[:pixels, :] = cot_ref[:, pl.ds(start, quarter)]
     cot[pixels : 2 * pixels, :] = far_ref[:pixels, :]
@@ -280,13 +312,14 @@
     lax.fori_loop(0, tiles, one_tile, 0)
 
 
-def call(kernel, name, outs, scratch, flops, *args):
+def call(kernel, name, outs, scratch, micros, *args, in_specs=None):
+    flops = int(micros * 1.1e9)
     moved = sum(math.prod(a.shape) * a.dtype.itemsize for a in args)
     moved += sum(math.prod(o.shape) * o.dtype.itemsize for o in outs)
     return pl.pallas_call(
         kernel,
         out_shape=outs,
-        in_specs=[VMEM] * len(args),
+        in_specs=in_specs or [VMEM] * len(args),
         out_specs=[VMEM] * len(outs),
         scratch_shapes=scratch,
         compiler_params=params(),
@@ -336,23 +369,38 @@
         pack_kernel,
         "pack",
         [shape((own, quarter + LANES), BF16)] * 2,
-        [pltpu.VMEM((LANES, LANES), F32), pltpu.VMEM((own, LANES), F32)],
-        0,
+        [
+            pltpu.VMEM(up_weight.shape, BF16),
+            pltpu.VMEM(depthwise_weight.shape, BF16),
+            pltpu.VMEM((LANES, LANES), F32),
+            pltpu.VMEM((own, LANES), F32),
+            pltpu.SemaphoreType.DMA((2,)),
+        ],
+        0.5,
         up_weight,
         depthwise_weight,
         norm_gain[None, :],
         norm_bias[None, :],
+        in_specs=[pl.BlockSpec(memory_space=pl.ANY)] * 2 + [VMEM] * 2,
     )
     gathered = [near] + [
         over_shard(far if line % 2 else near, INNER * line) for line in range(1, lines)
     ]
-    weight_lines = jnp.concatenate([g[:, :quarter] for g in gathered])
-    extra_lines = jnp.concatenate([g[:, quarter:] for g in gathered])
+    rows = lines * own
+    weight_lines, extra_lines = call(
+        assemble_kernel,
+        "assemble",
+        [shape((rows, quarter), BF16), shape((rows, LANES), BF16)],
+        [],
+        0.3,
+        *gathered,
+    )
     weights = [weight_lines] + [over_shard(weight_lines, flip) for flip in range(1, INNER)]
     extras = [extra_lines] + [over_shard(extra_lines, flip) for flip in range(1, INNER)]
     weights, extras = true_order(weights), true_order(extras)
 
     images_far = over_shard(images, INNER)
+    images_sibling, images_corner = over_core(images), over_core(images_far)
     cotangent = cotangent.reshape(pixels, hidden)
     cot_sibling = over_core(lax.dynamic_slice(cotangent, (0, (1 - side) * half), (pixels, half)))
     (cot_sent,) = call(
@@ -360,19 +408,18 @@
         "cot_pack",
         [shape((2 * pixels, quarter), BF16)],
         [],
-        0,
+        0.5,
         cotangent,
         cot_sibling,
     )
     cot_far = over_shard(cot_sent, INNER)
 
     padded = pltpu.VMEM((tiles, height, breadth + 16, LANES), F32)
-    conv_flops = 2 * TAPS * pixels * depth
     normed, whitened, inv_std, taps = call(
         functools.partial(conv_norm_kernel, relative, own),
         "conv_norm",
         [
-            shape((2 * pixels, depth), BF16),
+            shape((4 * pixels, depth), BF16),
             shape((pixels, depth), F32),
             shape((pixels, LANES), F32),
             shape((tiles, LANES, LANES), F32),
@@ -382,14 +429,14 @@
             padded,
             pltpu.VMEM((tiles, pixels, LANES), F32),
         ],
-        2 * conv_flops,
+        0.1,
         *extras,
         images,
         images_far,
-    )
-    normed_sibling = over_core(normed)
-
-    rows = lines * own
+        images_sibling,
+        images_corner,
+    )
+
     *pieces, grad_pre = call(
         functools.partial(project_kernel, relative, own),
         "project",
@@ -398,14 +445,12 @@
         + [shape((4 * pixels, quarter), BF16)],
         [
             pltpu.VMEM((depth, quarter), BF16),
-            pltpu.VMEM((4 * pixels, depth), BF16),
             pltpu.VMEM((4 * pixels, quarter), BF16),
             pltpu.VMEM((depth, quarter), F32),
         ],
-        16 * pixels * depth * quarter,
+        1.6,
         *weights,
         normed,
-        normed_sibling,
         cotangent,
         cot_sibling,
         cot_far,
@@ -418,7 +463,7 @@
         "back_project",
         [shape((2 * pixels, depth), F32)] * 2,
         [pltpu.VMEM((depth, quarter), BF16)],
-        8 * pixels * depth * quarter,
+        0.7,
         *weights,
         grad_pre,
     )
@@ -427,7 +472,7 @@
         "core_sum",
         [shape((pixels, depth), F32), shape((pixels, depth), BF16)],
         [],
-        2 * pixels * depth,
+        0.4,
         gn_kept,
         over_core(gn_sent),
     )
@@ -443,7 +488,7 @@
             pltpu.VMEM((tiles, LANES, LANES), F32),
             pltpu.VMEM((depth, LANES), F32),
         ],
-        conv_flops,
+        1.7,
         gn_kept,
         gn_other,
         whitened,
@@ -458,7 +503,7 @@
         "conv_back",
         [shape(images.shape, BF16)],
         [padded],
-        conv_flops,
+        1.9,
         grad_conv,
         taps,
     )
@@ -482,19 +527,21 @@
         total = lax.psum(total, "rep", axis_index_groups=groups)
     other = over_core(total)
     factor = 1.0 / math.sqrt(images.shape[0] * pixels * shards * reps)
-    total, other = total * factor, other * factor
-    first = jnp.where(side == 0, total, other)
-    second = jnp.where(side == 0, other, total)
-    grad_up = jnp.concatenate(
+    grad_up, grad_depthwise, grad_gain, grad_bias = call(
+        functools.partial(finish_kernel, factor),
+        "finish",
         [
-            jnp.where(parity == 0, part[:, low : low + quarter], part[:, quarter - low : half - low])
-            for part in (first, second)
-            for low in (0, quarter)
+            shape((own, hidden), F32),
+            shape((own, TAPS), F32),
+            shape((1, own), F32),
+            shape((1, own), F32),
         ],
-        axis=1,
-    )
-    sums = total[:, half:] + other[:, half:]
-    return (grad_images, grad_up, sums[:, :TAPS], sums[:, TAPS], sums[:, TAPS + 1])
+        [],
+        0.5,
+        total,
+        other,
+    )
+    return (grad_images, grad_up, grad_depthwise, grad_gain[0], grad_bias[0])
 
 
 def solution(mesh):

time: 67.6 us -> 65.6 us (0.970)
  waiting for transfers between devices: 24 us -> 18.9 us
  Pallas kernels: 8.92 us -> 12.7 us
  starting transfers between devices: 28.4 us -> 30.2 us
  local copies, waits for them, and re-layouts: 4.04 us -> 2.56 us
  other arithmetic: 1.03 us -> 0.19 us
    pallas_call x8 -> x10, Pallas kernels: 8.92 us -> 12.7 us  [call(): pl.pallas_call(kernel, out_shape=outs, in_specs=in_specs or [VMEM] * len(...]
    ppermute x21, waiting for transfers between devices: 20.4 us -> 17.5 us  [over_shard(): return lax.ppermute(array, 'shard', [(i, i ^ flip) for i in range(shards)])]
    ppermute x4 -> x5, waiting for transfers between devices: 3.63 us -> 1.4 us  [over_core(): return lax.ppermute(array, 'rep', [(i, i ^ 1) for i in range(reps)])]
    unnamed x20 -> x14, local copies, waits for them, and re-layouts: 2.3 us -> 0.68 us
    ppermute x21, starting transfers between devices: 28.1 us -> 29.5 us  [over_shard(): return lax.ppermute(array, 'shard', [(i, i ^ flip) for i in range(shards)])]
    slice x1 -> x2, local copies, waits for them, and re-layouts: 0.01 us -> 0.86 us  [body(): same[:, :quarter]]
    concatenate x3 -> x0, other arithmetic: 0.76 us -> none  [the longest x1 0.74 us: body(): jnp.concatenate([jnp.where(parity == 0, part[:, low:low + quarter], part[...]
    slice x12 -> x0, local copies, waits for them, and re-layouts: 0.73 us -> none  [the longest x1 0.7 us: body(): sums[:, TAPS + 1]]
  transfers between devices with their start and end apart: 25 -> 26, of which waited for: 15 -> 12; matrix products, arithmetic and copies ran while one was open for 2% -> 0% of each run, Pallas kernels for 10% -> 12%
where the time goes in v3:
time: 65.6 us; the launch traced here: 65.4 us
  starting transfers between devices  30.2 us (46%)
  waiting for transfers between devices  18.9 us (29%)
  Pallas kernels  12.7 us (19%)
  local copies, waits for them, and re-layouts  2.56 us (4%)
  between operations  0.89 us (1%)
    ppermute x21, starting transfers between devices, over_shard(): return lax.ppermute(array, 'shard', [(i, i ^ flip) for i in range(shards)])  29.5 us
    ppermute x21, waiting for transfers between devices, over_shard(): return lax.ppermute(array, 'shard', [(i, i ^ flip) for i in range(shards)])  17.5 us
    pallas_call x10, Pallas kernels, call(): pl.pallas_call(kernel, out_shape=outs, in_specs=in_specs or [VMEM] * len(...  12.7 us
    ppermute x5, waiting for transfers between devices, over_core(): return lax.ppermute(array, 'rep', [(i, i ^ 1) for i in range(reps)])  1.4 us
  transfers between devices with their start and end apart: 26, of which 12 were waited for; matrix products, arithmetic and copies ran while one was open for 0% of the time, Pallas kernels for 12%

profile of v3, /device:TPU:0, one launch (start us, length us, event | category | flops | bytes accessed | tf_op | source)
XLA Modules:
  0.0 65.4 jit_solution(12425267883340960277)
XLA Ops:
  0.7 1.0 %constant_dynamic-slice_fusion = bf16[128,768]{1,0:T(8,128)(2,1)S(1)} fusion(bf16[128,1536]{1,0:T(8,128)(2,1)} %bitcast.14, s32[]{:T(128)S(6)} %select_n.11), kind=kLoop, calls=%fused_computation.10 | loop fusion | bytes 393220 | tf_op jit(solution)/shard_map/dynamic_slice | solution.py:405
  1.7 0.5 collective-permute-start.12
  2.2 2.7 %collective-permute-start.9 = (bf16[1,8,16,768]{3,2,1,0:T(8,128)(2,1)S(1)}, bf16[1,8,16,768]{3,2,1,0:T(8,128)(2,1)S(1)}, u32[]{:S(2)}, u32[]{:S(2)}) collective-permute-start(bf16[1,8,16,768]{3,2,1,0:T(8,128)(2,1)S(1)} %copy-done), channel_id=1, source_target_pairs={{0,8},{2,10},{4,12},{6,14},{8,0},{10,2},{12,4},{14,6},{16,24},{18,... | collective-permute-start | bytes 589832 | tf_op jit(solution)/shard_map/ppermute | solution.py:346
  4.9 0.6 copy-done.4
  5.5 0.0 copy-done.5
  5.5 0.3 pack.1
  5.8 2.7 %collective-permute-start.1 = (bf16[48,512]{1,0:T(8,128)(2,1)S(1)}, bf16[48,512]{1,0:T(8,128)(2,1)S(1)}, u32[]{:S(2)}, u32[]{:S(2)}) collective-permute-start(bf16[48,512]{1,0:T(8,128)(2,1)S(1)} %get-tuple-element.33.refs_0_), channel_id=1, source_target_pairs={{0,16},{2,18},{4,20},{6,22},{8,24},{10,26},{12,28},{14,30},{16,0},... | collective-permute-start | bytes 147464 | tf_op jit(solution)/shard_map/ppermute | solution.py:346
  8.5 0.0 collective-permute-start.10
  8.5 0.1 collective-permute-start.2
  8.6 2.6 %collective-permute-done.1.refs_2_ = bf16[48,512]{1,0:T(8,128)(2,1)S(1)} collective-permute-done((bf16[48,512]{1,0:T(8,128)(2,1)S(1)}, bf16[48,512]{1,0:T(8,128)(2,1)S(1)}, u32[]{:S(2)}, u32[]{:S(2)}) %collective-permute-start.1) | collective-permute-done | bytes 49184 | tf_op jit(solution)/shard_map/ppermute | solution.py:346
  11.2 3.1 %collective-permute-start = (bf16[48,512]{1,0:T(8,128)(2,1)S(1)}, bf16[48,512]{1,0:T(8,128)(2,1)S(1)}, u32[]{:S(2)}, u32[]{:S(2)}) collective-permute-start(bf16[48,512]{1,0:T(8,128)(2,1)S(1)} %get-tuple-element.34), channel_id=1, source_target_pairs={{0,8},{2,10},{4,12},{6,14},{8,0},{10,2},{12,4},{14,6},{16,24},{18,... | collective-permute-start | bytes 147464 | tf_op jit(solution)/shard_map/ppermute | solution.py:346
  14.3 0.3 collective-permute-done.2.refs_3_
  14.7 1.7 %collective-permute-done.refs_1_ = bf16[48,512]{1,0:T(8,128)(2,1)S(1)} collective-permute-done((bf16[48,512]{1,0:T(8,128)(2,1)S(1)}, bf16[48,512]{1,0:T(8,128)(2,1)S(1)}, u32[]{:S(2)}, u32[]{:S(2)}) %collective-permute-start) | collective-permute-done | bytes 49184 | tf_op jit(solution)/shard_map/ppermute | solution.py:346
  16.4 2.5 %collective-permute-start.8 = (bf16[192,128]{1,0:T(8,128)(2,1)S(1)}, bf16[192,128]{1,0:T(8,128)(2,1)S(1)}, u32[]{:S(2)}, u32[]{:S(2)}) collective-permute-start(bf16[192,128]{1,0:T(8,128)(2,1)S(1)} %get-tuple-element.36.refs_0_), channel_id=1, source_target_pairs={{0,6},{2,4},{4,2},{6,0},{8,14},{10,12},{12,10},{14,8},{16,22},{18,... | collective-permute-start | bytes 147464 | tf_op jit(solution)/shard_map/ppermute | solution.py:346
  18.9 0.5 collective-permute-start.7
  19.4 0.0 collective-permute-done.12.sibling_ref.refs_6_
  19.4 0.5 collective-permute-start.6
  20.0 0.0 collective-permute-done.9.refs_5_
  20.0 0.0 collective-permute-start.11
  20.0 1.8 %collective-permute-done.8.refs_3_ = bf16[192,128]{1,0:T(8,128)(2,1)S(1)} collective-permute-done((bf16[192,128]{1,0:T(8,128)(2,1)S(1)}, bf16[192,128]{1,0:T(8,128)(2,1)S(1)}, u32[]{:S(2)}, u32[]{:S(2)}) %collective-permute-start.8) | collective-permute-done | bytes 49184 | tf_op jit(solution)/shard_map/ppermute | solution.py:346
  21.9 2.0 %collective-permute-start.13 = (bf16[256,384]{1,0:T(8,128)(2,1)S(1)}, bf16[256,384]{1,0:T(8,128)(2,1)S(1)}, u32[]{:S(2)}, u32[]{:S(2)}) collective-permute-start(bf16[256,384]{1,0:T(8,128)(2,1)S(1)} %cot_pack.1), channel_id=1, source_target_pairs={{0,8},{2,10},{4,12},{6,14},{8,0},{10,2},{12,4},{14,6},{16,24},{18,... | collective-permute-start | bytes 589832 | tf_op jit(solution)/shard_map/ppermute | solution.py:346
  23.8 0.0 collective-permute-done.7.refs_2_
  23.8 2.2 %collective-permute-start.5 = (bf16[192,384]{1,0:T(8,128)(2,1)S(1)}, bf16[192,384]{1,0:T(8,128)(2,1)S(1)}, u32[]{:S(2)}, u32[]{:S(2)}) collective-permute-start(bf16[192,384]{1,0:T(8,128)(2,1)S(1)} %get-tuple-element.35.refs_0_), channel_id=1, source_target_pairs={{0,6},{2,4},{4,2},{6,0},{8,14},{10,12},{12,10},{14,8},{16,22},{18,... | collective-permute-start | bytes 442376 | tf_op jit(solution)/shard_map/ppermute | solution.py:346
  26.0 0.0 collective-permute-done.6.refs_1_
  26.0 0.4 collective-permute-start.4
  26.4 0.0 collective-permute-done.10.refs_6_
  26.5 0.9 %collective-permute-start.3 = (bf16[192,384]{1,0:T(8,128)(2,1)S(1)}, bf16[192,384]{1,0:T(8,128)(2,1)S(1)}, u32[]{:S(2)}, u32[]{:S(2)}) collective-permute-start(bf16[192,384]{1,0:T(8,128)(2,1)S(1)} %get-tuple-element.35.refs_0_), channel_id=1, source_target_pairs={{0,2},{2,0},{4,6},{6,4},{8,10},{10,8},{12,14},{14,12},{16,18},{18,... | collective-permute-start | bytes 442376 | tf_op jit(solution)/shard_map/ppermute | solution.py:346
  27.3 0.0 collective-permute-done.11.refs_7_
  27.4 5.6 %conv_norm.1 = (bf16[512,768]{1,0:T(8,128)(2,1)S(1)}, f32[128,768]{1,0:T(8,128)S(1)}, f32[128,128]{1,0:T(8,128)S(1)}, f32[6,128,128]{2,1,0:T(8,128)S(1)}) custom-call(bf16[192,128]{1,0:T(8,128)(2,1)S(1)} %get-tuple-element.36.refs_0_, bf16[192,128]{1,0:T(8,128)(2,1)S(1)} %collective-permute-done.6.refs_1_, ...), custom_call_target="tpu_custom_call" | custom-call | flops 110000000 | bytes 2621440 | tf_op jit(solution)/shard_map/conv_norm/pallas_call | solution.py:319
  33.0 0.0 collective-permute-done.5.refs_3_
  33.0 0.0 collective-permute-done.4.refs_2_
  33.0 0.0 collective-permute-done.13.refs_7_
  33.0 1.7 %project.1 = (f32[192,384]{1,0:T(8,128)S(1)}, bf16[192,384]{1,0:T(8,128)(2,1)S(1)}, bf16[192,384]{1,0:T(8,128)(2,1)S(1)}, bf16[192,384]{1,0:T(8,128)(2,1)S(1)}, bf16[512,384]{1,0:T(8,128)(2,1)S(1)}) custom-call(bf16[192,384]{1,0:T(8,128)(2,1)S(1)} %get-tuple-element.35.refs_0_, bf16[192,384]{1,0:T(8,128)(2,1)S(1)} %collective-permute-done.3.refs_1_, ...), custom_call_target="tpu_custom_call" | custom-call | flops 1760000000 | bytes 3293184 | tf_op jit(solution)/shard_map/project/pallas_call | solution.py:319
  34.7 0.7 %back_project.1 = (f32[256,768]{1,0:T(8,128)S(1)}, f32[256,768]{1,0:T(8,128)S(1)}) custom-call(bf16[192,384]{1,0:T(8,128)(2,1)S(1)} %get-tuple-element.35.refs_0_, bf16[192,384]{1,0:T(8,128)(2,1)S(1)} %collective-permute-done.3.refs_1_, bf16[192,384]{1,0:T(8,128)(2,1)S(1)} %collective-permute-done.4.refs_2_, ...), custom_call_target="tpu_custom_call" | custom-call | flops 770000000 | bytes 2555904 | tf_op jit(solution)/shard_map/back_project/pallas_call | solution.py:319
  35.3 0.1 collective-permute-start.17
  35.4 1.2 %collective-permute-start.14 = (bf16[192,384]{1,0:T(8,128)(2,1)S(1)}, bf16[192,384]{1,0:T(8,128)(2,1)S(1)}, u32[]{:S(2)}, u32[]{:S(2)}) collective-permute-start(bf16[192,384]{1,0:T(8,128)(2,1)S(1)} %get-tuple-element.39), channel_id=1, source_target_pairs={{0,2},{2,0},{4,6},{6,4},{8,10},{10,8},{12,14},{14,12},{16,18},{18,... | collective-permute-start | bytes 442376 | tf_op jit(solution)/shard_map/ppermute | solution.py:346
  36.6 1.6 %collective-permute-start.15 = (bf16[192,384]{1,0:T(8,128)(2,1)S(1)}, bf16[192,384]{1,0:T(8,128)(2,1)S(1)}, u32[]{:S(2)}, u32[]{:S(2)}) collective-permute-start(bf16[192,384]{1,0:T(8,128)(2,1)S(1)} %get-tuple-element.40), channel_id=1, source_target_pairs={{0,4},{2,6},{4,0},{6,2},{8,12},{10,14},{12,8},{14,10},{16,20},{18,... | collective-permute-start | bytes 442376 | tf_op jit(solution)/shard_map/ppermute | solution.py:346
  38.2 0.7 %collective-permute-start.16 = (bf16[192,384]{1,0:T(8,128)(2,1)S(1)}, bf16[192,384]{1,0:T(8,128)(2,1)S(1)}, u32[]{:S(2)}, u32[]{:S(2)}) collective-permute-start(bf16[192,384]{1,0:T(8,128)(2,1)S(1)} %get-tuple-element.41), channel_id=1, source_target_pairs={{0,6},{2,4},{4,2},{6,0},{8,14},{10,12},{12,10},{14,8},{16,22},{18,... | collective-permute-start | bytes 442376 | tf_op jit(solution)/shard_map/ppermute | solution.py:346
  39.0 0.0 collective-permute-done.17.other_ref
  39.0 0.1 core_sum.1
  39.1 1.3 %collective-permute-start.18 = (bf16[128,768]{1,0:T(8,128)(2,1)S(1)}, bf16[128,768]{1,0:T(8,128)(2,1)S(1)}, u32[]{:S(2)}, u32[]{:S(2)}) collective-permute-start(bf16[128,768]{1,0:T(8,128)(2,1)S(1)} %get-tuple-element.46), channel_id=1, source_target_pairs={{0,8},{2,10},{4,12},{6,14},{8,0},{10,2},{12,4},{14,6},{16,24},{18,... | collective-permute-start | bytes 589832 | tf_op jit(solution)/shard_map/ppermute | solution.py:346
  40.3 1.8 %collective-permute-done.14 = bf16[192,384]{1,0:T(8,128)(2,1)S(1)} collective-permute-done((bf16[192,384]{1,0:T(8,128)(2,1)S(1)}, bf16[192,384]{1,0:T(8,128)(2,1)S(1)}, u32[]{:S(2)}, u32[]{:S(2)}) %collective-permute-start.14) | collective-permute-done | bytes 147488 | tf_op jit(solution)/shard_map/ppermute | solution.py:346
  42.1 3.6 %collective-permute-done.15 = bf16[192,384]{1,0:T(8,128)(2,1)S(1)} collective-permute-done((bf16[192,384]{1,0:T(8,128)(2,1)S(1)}, bf16[192,384]{1,0:T(8,128)(2,1)S(1)}, u32[]{:S(2)}, u32[]{:S(2)}) %collective-permute-start.15) | collective-permute-done | bytes 147488 | tf_op jit(solution)/shard_map/ppermute | solution.py:346
  45.7 0.1 add_add_fusion
  45.8 1.7 %norm_back.1 = (f32[192,128]{1,0:T(8,128)S(1)}, bf16[192,128]{1,0:T(8,128)(2,1)S(1)}, bf16[192,128]{1,0:T(8,128)(2,1)S(1)}, bf16[192,128]{1,0:T(8,128)(2,1)S(1)}, f32[6,8,16,128]{3,2,1,0:T(8,128)S(1)}) custom-call(f32[128,768]{1,0:T(8,128)S(1)} %get-tuple-element.45.refs_0_, bf16[128,768]{1,0:T(8,128)(2,1)S(1)} %collective-permute-done.18.refs_1_, ...), custom_call_target="tpu_custom_call" | custom-call | flops 1870000000 | bytes 2277376 | tf_op jit(solution)/shard_map/norm_back/pallas_call | solution.py:319
  47.5 1.4 %collective-permute-start.19 = (bf16[192,128]{1,0:T(8,128)(2,1)S(1)}, bf16[192,128]{1,0:T(8,128)(2,1)S(1)}, u32[]{:S(2)}, u32[]{:S(2)}) collective-permute-start(bf16[192,128]{1,0:T(8,128)(2,1)S(1)} %get-tuple-element.51), channel_id=1, source_target_pairs={{0,2},{2,0},{4,6},{6,4},{8,10},{10,8},{12,14},{14,12},{16,18},{18,... | collective-permute-start | bytes 147464 | tf_op jit(solution)/shard_map/ppermute | solution.py:346
  48.9 1.2 %collective-permute-start.20 = (bf16[192,128]{1,0:T(8,128)(2,1)S(1)}, bf16[192,128]{1,0:T(8,128)(2,1)S(1)}, u32[]{:S(2)}, u32[]{:S(2)}) collective-permute-start(bf16[192,128]{1,0:T(8,128)(2,1)S(1)} %get-tuple-element.52), channel_id=1, source_target_pairs={{0,4},{2,6},{4,0},{6,2},{8,12},{10,14},{12,8},{14,10},{16,20},{18,... | collective-permute-start | bytes 147464 | tf_op jit(solution)/shard_map/ppermute | solution.py:346
  50.1 1.0 %collective-permute-start.21 = (bf16[192,128]{1,0:T(8,128)(2,1)S(1)}, bf16[192,128]{1,0:T(8,128)(2,1)S(1)}, u32[]{:S(2)}, u32[]{:S(2)}) collective-permute-start(bf16[192,128]{1,0:T(8,128)(2,1)S(1)} %get-tuple-element.53), channel_id=1, source_target_pairs={{0,6},{2,4},{4,2},{6,0},{8,14},{10,12},{12,10},{14,8},{16,22},{18,... | collective-permute-start | bytes 147464 | tf_op jit(solution)/shard_map/ppermute | solution.py:346
  51.1 1.9 %conv_back.1 = bf16[1,8,16,768]{3,2,1,0:T(8,128)(2,1)} custom-call(f32[6,8,16,128]{3,2,1,0:T(8,128)S(1)} %get-tuple-element.54.grad_ref, f32[6,128,128]{2,1,0:T(8,128)S(1)} %get-tuple-element.49.refs_4_.taps_ref), custom_call_target="tpu_custom_call" | custom-call | flops 2090000000 | bytes 983040 | tf_op jit(solution)/shard_map/conv_back/pallas_call | solution.py:319
  52.9 0.0 collective-permute-done.19
  52.9 0.2 collective-permute-done.20
  53.1 1.9 %collective-permute-done.21 = bf16[192,128]{1,0:T(8,128)(2,1)S(1)} collective-permute-done((bf16[192,128]{1,0:T(8,128)(2,1)S(1)}, bf16[192,128]{1,0:T(8,128)(2,1)S(1)}, u32[]{:S(2)}, u32[]{:S(2)}) %collective-permute-start.21) | collective-permute-done | bytes 49184 | tf_op jit(solution)/shard_map/ppermute | solution.py:346
  55.2 0.7 %collective-permute-start.22 = (bf16[48,512]{1,0:T(8,128)(2,1)S(1)}, bf16[48,512]{1,0:T(8,128)(2,1)S(1)}, u32[]{:S(2)}, u32[]{:S(2)}) collective-permute-start(bf16[48,512]{1,0:T(8,128)(2,1)S(1)} %get-tuple-element.61), channel_id=1, source_target_pairs={{0,16},{2,18},{4,20},{6,22},{8,24},{10,26},{12,28},{14,30},{16,0},... | collective-permute-start | bytes 147464 | tf_op jit(solution)/shard_map/ppermute | solution.py:346
  55.8 2.1 %collective-permute-start.24 = (bf16[48,512]{1,0:T(8,128)(2,1)S(1)}, bf16[48,512]{1,0:T(8,128)(2,1)S(1)}, u32[]{:S(2)}, u32[]{:S(2)}) collective-permute-start(bf16[48,512]{1,0:T(8,128)(2,1)S(1)} %get-tuple-element.62), channel_id=1, source_target_pairs={{0,24},{2,26},{4,28},{6,30},{8,16},{10,18},{12,20},{14,22},{16,8},... | collective-permute-start | bytes 147464 | tf_op jit(solution)/shard_map/ppermute | solution.py:346
  57.9 0.8 %collective-permute-start.23 = (bf16[48,512]{1,0:T(8,128)(2,1)S(1)}, bf16[48,512]{1,0:T(8,128)(2,1)S(1)}, u32[]{:S(2)}, u32[]{:S(2)}) collective-permute-start(bf16[48,512]{1,0:T(8,128)(2,1)S(1)} %get-tuple-element.63), channel_id=1, source_target_pairs={{0,8},{2,10},{4,12},{6,14},{8,0},{10,2},{12,4},{14,6},{16,24},{18,... | collective-permute-start | bytes 147464 | tf_op jit(solution)/shard_map/ppermute | solution.py:346
  58.7 1.7 %collective-permute-done.22 = bf16[48,512]{1,0:T(8,128)(2,1)S(1)} collective-permute-done((bf16[48,512]{1,0:T(8,128)(2,1)S(1)}, bf16[48,512]{1,0:T(8,128)(2,1)S(1)}, u32[]{:S(2)}, u32[]{:S(2)}) %collective-permute-start.22) | collective-permute-done | bytes 49184 | tf_op jit(solution)/shard_map/ppermute | solution.py:346
  60.5 0.0 copy-start.6
  60.5 1.2 %collective-permute-done.24 = bf16[48,512]{1,0:T(8,128)(2,1)S(1)} collective-permute-done((bf16[48,512]{1,0:T(8,128)(2,1)S(1)}, bf16[48,512]{1,0:T(8,128)(2,1)S(1)}, u32[]{:S(2)}, u32[]{:S(2)}) %collective-permute-start.24) | collective-permute-done | bytes 49184 | tf_op jit(solution)/shard_map/ppermute | solution.py:346
  61.8 0.5 collective-permute-done.23
  62.3 0.0 slice-start
  62.3 0.9 %slice-done = f32[48,384]{1,0:T(8,128)S(1)} async-done(((f32[48,512]{1,0:T(8,128)}), f32[48,384]{1,0:T(8,128)S(1)}, s32[]{:S(2)}) %slice-start) | async-done | bytes 73752 | tf_op jit(solution)/shard_map/slice | solution.py:523
  63.2 0.1 collective-permute-start.25
  63.3 1.4 %collective-permute-done.25.other_ref = f32[48,896]{1,0:T(8,128)S(1)} collective-permute-done((f32[48,896]{1,0:T(8,128)S(1)}, f32[48,896]{1,0:T(8,128)S(1)}, u32[]{:S(2)}, u32[]{:S(2)}) %collective-permute-start.25) | collective-permute-done | bytes 172064 | tf_op jit(solution)/shard_map/ppermute | solution.py:349
  64.7 0.8 %finish.1 = (f32[48,1536]{1,0:T(8,128)}, f32[48,49]{1,0:T(8,128)}, f32[1,48]{1,0:T(1,128)}, f32[1,48]{1,0:T(1,128)}) custom-call(f32[48,896]{1,0:T(8,128)S(1)} %pad_maximum_fusion.1.mine_ref, f32[48,896]{1,0:T(8,128)S(1)} %collective-permute-done.25.other_ref), custom_call_target="tpu_custom_call" | custom-call | flops 550000000 | bytes 648768 | tf_op jit(solution)/shard_map/finish/pallas_call | solution.py:319
  (25 shorter events, 0.2 us)
Async XLA Ops:
  0.6 1.5 %copy-start = (bf16[1,8,16,768]{3,2,1,0:T(8,128)(2,1)S(1)}, bf16[1,8,16,768]{3,2,1,0:T(8,128)(2,1)}, u32[]{:S(2)}) copy-start(bf16[1,8,16,768]{3,2,1,0:T(8,128)(2,1)} %refs_5_.1) | copy-start | bytes 589828
  0.7 4.2 %copy-start.2 = (bf16[48,1536]{1,0:T(8,128)(2,1)S(1)}, bf16[48,1536]{1,0:T(8,128)(2,1)}, u32[]{:S(2)}) copy-start(bf16[48,1536]{1,0:T(8,128)(2,1)} %w_hbm.1) | copy-start | bytes 442372
  0.7 4.2 %copy-start.3 = (bf16[48,49]{1,0:T(8,128)(2,1)S(1)}, bf16[48,49]{1,0:T(8,128)(2,1)}, u32[]{:S(2)}) copy-start(bf16[48,49]{1,0:T(8,128)(2,1)} %dw_hbm.1) | copy-start | bytes 14116
  1.7 17.8 %collective-permute-start.12 = (bf16[128,768]{1,0:T(8,128)(2,1)S(1)}, bf16[128,768]{1,0:T(8,128)(2,1)S(1)}, u32[]{:S(2)}, u32[]{:S(2)}) collective-permute-start(bf16[128,768]{1,0:T(8,128)(2,1)S(1)} %constant_dynamic-slice_fusion), channel_id=1, source_target_pairs={{0,1},{1,0},{2,3},{3,2},{4,5},{5,4},{6,7},{7,6},{8,9},{9,8},{10,11... | collective-permute-start | bytes 589832 | tf_op jit(solution)/shard_map/ppermute | solution.py:349
  2.2 17.8 %collective-permute-start.9 = (bf16[1,8,16,768]{3,2,1,0:T(8,128)(2,1)S(1)}, bf16[1,8,16,768]{3,2,1,0:T(8,128)(2,1)S(1)}, u32[]{:S(2)}, u32[]{:S(2)}) collective-permute-start(bf16[1,8,16,768]{3,2,1,0:T(8,128)(2,1)S(1)} %copy-done), channel_id=1, source_target_pairs={{0,8},{2,10},{4,12},{6,14},{8,0},{10,2},{12,4},{14,6},{16,24},{18,... | collective-permute-start | bytes 589832 | tf_op jit(solution)/shard_map/ppermute | solution.py:346
  4.9 0.7 %copy-start.4 = (bf16[48]{0:T(256)(128)(2,1)S(1)}, bf16[48]{0:T(256)(128)(2,1)}, u32[]{:S(2)}) copy-start(bf16[48]{0:T(256)(128)(2,1)} %param.9) | copy-start | bytes 292
  4.9 0.7 %copy-start.5 = (bf16[48]{0:T(256)(128)(2,1)S(1)}, bf16[48]{0:T(256)(128)(2,1)}, u32[]{:S(2)}) copy-start(bf16[48]{0:T(256)(128)(2,1)} %param.10) | copy-start | bytes 292
  5.8 5.4 %collective-permute-start.1 = (bf16[48,512]{1,0:T(8,128)(2,1)S(1)}, bf16[48,512]{1,0:T(8,128)(2,1)S(1)}, u32[]{:S(2)}, u32[]{:S(2)}) collective-permute-start(bf16[48,512]{1,0:T(8,128)(2,1)S(1)} %get-tuple-element.33.refs_0_), channel_id=1, source_target_pairs={{0,16},{2,18},{4,20},{6,22},{8,24},{10,26},{12,28},{14,30},{16,0},... | collective-permute-start | bytes 147464 | tf_op jit(solution)/shard_map/ppermute | solution.py:346
  8.5 18.0 %collective-permute-start.10 = (bf16[1,8,16,768]{3,2,1,0:T(8,128)(2,1)S(1)}, bf16[1,8,16,768]{3,2,1,0:T(8,128)(2,1)S(1)}, u32[]{:S(2)}, u32[]{:S(2)}) collective-permute-start(bf16[1,8,16,768]{3,2,1,0:T(8,128)(2,1)S(1)} %copy-done), channel_id=1, source_target_pairs={{0,1},{1,0},{2,3},{3,2},{4,5},{5,4},{6,7},{7,6},{8,9},{9,8},{10,11... | collective-permute-start | bytes 589832 | tf_op jit(solution)/shard_map/ppermute | solution.py:349
  8.5 11.5 %copy-start.1 = (bf16[1,8,16,1536]{3,2,1,0:T(8,128)(2,1)S(1)}, bf16[1,8,16,1536]{3,2,1,0:T(8,128)(2,1)}, u32[]{:S(2)}) copy-start(bf16[1,8,16,1536]{3,2,1,0:T(8,128)(2,1)} %param.7) | copy-start | bytes 1179652
  8.5 6.2 %collective-permute-start.2 = (bf16[48,512]{1,0:T(8,128)(2,1)S(1)}, bf16[48,512]{1,0:T(8,128)(2,1)S(1)}, u32[]{:S(2)}, u32[]{:S(2)}) collective-permute-start(bf16[48,512]{1,0:T(8,128)(2,1)S(1)} %get-tuple-element.34), channel_id=1, source_target_pairs={{0,24},{2,26},{4,28},{6,30},{8,16},{10,18},{12,20},{14,22},{16,8},... | collective-permute-start | bytes 147464 | tf_op jit(solution)/shard_map/ppermute | solution.py:346
  11.2 5.2 %collective-permute-start = (bf16[48,512]{1,0:T(8,128)(2,1)S(1)}, bf16[48,512]{1,0:T(8,128)(2,1)S(1)}, u32[]{:S(2)}, u32[]{:S(2)}) collective-permute-start(bf16[48,512]{1,0:T(8,128)(2,1)S(1)} %get-tuple-element.34), channel_id=1, source_target_pairs={{0,8},{2,10},{4,12},{6,14},{8,0},{10,2},{12,4},{14,6},{16,24},{18,... | collective-permute-start | bytes 147464 | tf_op jit(solution)/shard_map/ppermute | solution.py:346
  16.4 5.5 %collective-permute-start.8 = (bf16[192,128]{1,0:T(8,128)(2,1)S(1)}, bf16[192,128]{1,0:T(8,128)(2,1)S(1)}, u32[]{:S(2)}, u32[]{:S(2)}) collective-permute-start(bf16[192,128]{1,0:T(8,128)(2,1)S(1)} %get-tuple-element.36.refs_0_), channel_id=1, source_target_pairs={{0,6},{2,4},{4,2},{6,0},{8,14},{10,12},{12,10},{14,8},{16,22},{18,... | collective-permute-start | bytes 147464 | tf_op jit(solution)/shard_map/ppermute | solution.py:346
  18.9 4.9 %collective-permute-start.7 = (bf16[192,128]{1,0:T(8,128)(2,1)S(1)}, bf16[192,128]{1,0:T(8,128)(2,1)S(1)}, u32[]{:S(2)}, u32[]{:S(2)}) collective-permute-start(bf16[192,128]{1,0:T(8,128)(2,1)S(1)} %get-tuple-element.36.refs_0_), channel_id=1, source_target_pairs={{0,4},{2,6},{4,0},{6,2},{8,12},{10,14},{12,8},{14,10},{16,20},{18,... | collective-permute-start | bytes 147464 | tf_op jit(solution)/shard_map/ppermute | solution.py:346
  19.4 6.6 %collective-permute-start.6 = (bf16[192,128]{1,0:T(8,128)(2,1)S(1)}, bf16[192,128]{1,0:T(8,128)(2,1)S(1)}, u32[]{:S(2)}, u32[]{:S(2)}) collective-permute-start(bf16[192,128]{1,0:T(8,128)(2,1)S(1)} %get-tuple-element.36.refs_0_), channel_id=1, source_target_pairs={{0,2},{2,0},{4,6},{6,4},{8,10},{10,8},{12,14},{14,12},{16,18},{18,... | collective-permute-start | bytes 147464 | tf_op jit(solution)/shard_map/ppermute | solution.py:346
  20.0 7.4 %collective-permute-start.11 = (bf16[1,8,16,768]{3,2,1,0:T(8,128)(2,1)S(1)}, bf16[1,8,16,768]{3,2,1,0:T(8,128)(2,1)S(1)}, u32[]{:S(2)}, u32[]{:S(2)}) collective-permute-start(bf16[1,8,16,768]{3,2,1,0:T(8,128)(2,1)S(1)} %collective-permute-done.9.refs_5_), channel_id=1, source_target_pairs={{0,1},{1,0},{2,3},{3,2},{4,5},{5,4},{6,7},{7,6},{8,9},{9,8},{10,11... | collective-permute-start | bytes 589832 | tf_op jit(solution)/shard_map/ppermute | solution.py:349
  21.9 11.1 %collective-permute-start.13 = (bf16[256,384]{1,0:T(8,128)(2,1)S(1)}, bf16[256,384]{1,0:T(8,128)(2,1)S(1)}, u32[]{:S(2)}, u32[]{:S(2)}) collective-permute-start(bf16[256,384]{1,0:T(8,128)(2,1)S(1)} %cot_pack.1), channel_id=1, source_target_pairs={{0,8},{2,10},{4,12},{6,14},{8,0},{10,2},{12,4},{14,6},{16,24},{18,... | collective-permute-start | bytes 589832 | tf_op jit(solution)/shard_map/ppermute | solution.py:346
  23.8 9.1 %collective-permute-start.5 = (bf16[192,384]{1,0:T(8,128)(2,1)S(1)}, bf16[192,384]{1,0:T(8,128)(2,1)S(1)}, u32[]{:S(2)}, u32[]{:S(2)}) collective-permute-start(bf16[192,384]{1,0:T(8,128)(2,1)S(1)} %get-tuple-element.35.refs_0_), channel_id=1, source_target_pairs={{0,6},{2,4},{4,2},{6,0},{8,14},{10,12},{12,10},{14,8},{16,22},{18,... | collective-permute-start | bytes 442376 | tf_op jit(solution)/shard_map/ppermute | solution.py:346
  26.0 7.0 %collective-permute-start.4 = (bf16[192,384]{1,0:T(8,128)(2,1)S(1)}, bf16[192,384]{1,0:T(8,128)(2,1)S(1)}, u32[]{:S(2)}, u32[]{:S(2)}) collective-permute-start(bf16[192,384]{1,0:T(8,128)(2,1)S(1)} %get-tuple-element.35.refs_0_), channel_id=1, source_target_pairs={{0,4},{2,6},{4,0},{6,2},{8,12},{10,14},{12,8},{14,10},{16,20},{18,... | collective-permute-start | bytes 442376 | tf_op jit(solution)/shard_map/ppermute | solution.py:346
  26.5 6.6 %collective-permute-start.3 = (bf16[192,384]{1,0:T(8,128)(2,1)S(1)}, bf16[192,384]{1,0:T(8,128)(2,1)S(1)}, u32[]{:S(2)}, u32[]{:S(2)}) collective-permute-start(bf16[192,384]{1,0:T(8,128)(2,1)S(1)} %get-tuple-element.35.refs_0_), channel_id=1, source_target_pairs={{0,2},{2,0},{4,6},{6,4},{8,10},{10,8},{12,14},{14,12},{16,18},{18,... | collective-permute-start | bytes 442376 | tf_op jit(solution)/shard_map/ppermute | solution.py:346
  35.3 3.6 %collective-permute-start.17 = (f32[256,768]{1,0:T(8,128)S(1)}, f32[256,768]{1,0:T(8,128)S(1)}, u32[]{:S(2)}, u32[]{:S(2)}) collective-permute-start(f32[256,768]{1,0:T(8,128)S(1)} %get-tuple-element.44), channel_id=1, source_target_pairs={{0,1},{1,0},{2,3},{3,2},{4,5},{5,4},{6,7},{7,6},{8,9},{9,8},{10,11... | collective-permute-start | bytes 2359304 | tf_op jit(solution)/shard_map/ppermute | solution.py:349
  35.4 6.7 %collective-permute-start.14 = (bf16[192,384]{1,0:T(8,128)(2,1)S(1)}, bf16[192,384]{1,0:T(8,128)(2,1)S(1)}, u32[]{:S(2)}, u32[]{:S(2)}) collective-permute-start(bf16[192,384]{1,0:T(8,128)(2,1)S(1)} %get-tuple-element.39), channel_id=1, source_target_pairs={{0,2},{2,0},{4,6},{6,4},{8,10},{10,8},{12,14},{14,12},{16,18},{18,... | collective-permute-start | bytes 442376 | tf_op jit(solution)/shard_map/ppermute | solution.py:346
  36.6 9.1 %collective-permute-start.15 = (bf16[192,384]{1,0:T(8,128)(2,1)S(1)}, bf16[192,384]{1,0:T(8,128)(2,1)S(1)}, u32[]{:S(2)}, u32[]{:S(2)}) collective-permute-start(bf16[192,384]{1,0:T(8,128)(2,1)S(1)} %get-tuple-element.40), channel_id=1, source_target_pairs={{0,4},{2,6},{4,0},{6,2},{8,12},{10,14},{12,8},{14,10},{16,20},{18,... | collective-permute-start | bytes 442376 | tf_op jit(solution)/shard_map/ppermute | solution.py:346
  38.2 7.5 %collective-permute-start.16 = (bf16[192,384]{1,0:T(8,128)(2,1)S(1)}, bf16[192,384]{1,0:T(8,128)(2,1)S(1)}, u32[]{:S(2)}, u32[]{:S(2)}) collective-permute-start(bf16[192,384]{1,0:T(8,128)(2,1)S(1)} %get-tuple-element.41), channel_id=1, source_target_pairs={{0,6},{2,4},{4,2},{6,0},{8,14},{10,12},{12,10},{14,8},{16,22},{18,... | collective-permute-start | bytes 442376 | tf_op jit(solution)/shard_map/ppermute | solution.py:346
  39.1 6.7 %collective-permute-start.18 = (bf16[128,768]{1,0:T(8,128)(2,1)S(1)}, bf16[128,768]{1,0:T(8,128)(2,1)S(1)}, u32[]{:S(2)}, u32[]{:S(2)}) collective-permute-start(bf16[128,768]{1,0:T(8,128)(2,1)S(1)} %get-tuple-element.46), channel_id=1, source_target_pairs={{0,8},{2,10},{4,12},{6,14},{8,0},{10,2},{12,4},{14,6},{16,24},{18,... | collective-permute-start | bytes 589832 | tf_op jit(solution)/shard_map/ppermute | solution.py:346
  47.5 5.4 %collective-permute-start.19 = (bf16[192,128]{1,0:T(8,128)(2,1)S(1)}, bf16[192,128]{1,0:T(8,128)(2,1)S(1)}, u32[]{:S(2)}, u32[]{:S(2)}) collective-permute-start(bf16[192,128]{1,0:T(8,128)(2,1)S(1)} %get-tuple-element.51), channel_id=1, source_target_pairs={{0,2},{2,0},{4,6},{6,4},{8,10},{10,8},{12,14},{14,12},{16,18},{18,... | collective-permute-start | bytes 147464 | tf_op jit(solution)/shard_map/ppermute | solution.py:346
  48.9 4.2 %collective-permute-start.20 = (bf16[192,128]{1,0:T(8,128)(2,1)S(1)}, bf16[192,128]{1,0:T(8,128)(2,1)S(1)}, u32[]{:S(2)}, u32[]{:S(2)}) collective-permute-start(bf16[192,128]{1,0:T(8,128)(2,1)S(1)} %get-tuple-element.52), channel_id=1, source_target_pairs={{0,4},{2,6},{4,0},{6,2},{8,12},{10,14},{12,8},{14,10},{16,20},{18,... | collective-permute-start | bytes 147464 | tf_op jit(solution)/shard_map/ppermute | solution.py:346
  50.1 5.0 %collective-permute-start.21 = (bf16[192,128]{1,0:T(8,128)(2,1)S(1)}, bf16[192,128]{1,0:T(8,128)(2,1)S(1)}, u32[]{:S(2)}, u32[]{:S(2)}) collective-permute-start(bf16[192,128]{1,0:T(8,128)(2,1)S(1)} %get-tuple-element.53), channel_id=1, source_target_pairs={{0,6},{2,4},{4,2},{6,0},{8,14},{10,12},{12,10},{14,8},{16,22},{18,... | collective-permute-start | bytes 147464 | tf_op jit(solution)/shard_map/ppermute | solution.py:346
  55.2 5.3 %collective-permute-start.22 = (bf16[48,512]{1,0:T(8,128)(2,1)S(1)}, bf16[48,512]{1,0:T(8,128)(2,1)S(1)}, u32[]{:S(2)}, u32[]{:S(2)}) collective-permute-start(bf16[48,512]{1,0:T(8,128)(2,1)S(1)} %get-tuple-element.61), channel_id=1, source_target_pairs={{0,16},{2,18},{4,20},{6,22},{8,24},{10,26},{12,28},{14,30},{16,0},... | collective-permute-start | bytes 147464 | tf_op jit(solution)/shard_map/ppermute | solution.py:346
  55.8 5.9 %collective-permute-start.24 = (bf16[48,512]{1,0:T(8,128)(2,1)S(1)}, bf16[48,512]{1,0:T(8,128)(2,1)S(1)}, u32[]{:S(2)}, u32[]{:S(2)}) collective-permute-start(bf16[48,512]{1,0:T(8,128)(2,1)S(1)} %get-tuple-element.62), channel_id=1, source_target_pairs={{0,24},{2,26},{4,28},{6,30},{8,16},{10,18},{12,20},{14,22},{16,8},... | collective-permute-start | bytes 147464 | tf_op jit(solution)/shard_map/ppermute | solution.py:346
  57.9 4.4 %collective-permute-start.23 = (bf16[48,512]{1,0:T(8,128)(2,1)S(1)}, bf16[48,512]{1,0:T(8,128)(2,1)S(1)}, u32[]{:S(2)}, u32[]{:S(2)}) collective-permute-start(bf16[48,512]{1,0:T(8,128)(2,1)S(1)} %get-tuple-element.63), channel_id=1, source_target_pairs={{0,8},{2,10},{4,12},{6,14},{8,0},{10,2},{12,4},{14,6},{16,24},{18,... | collective-permute-start | bytes 147464 | tf_op jit(solution)/shard_map/ppermute | solution.py:346
  60.5 1.8 %copy-start.6 = (f32[48,512]{1,0:T(8,128)}, f32[48,512]{1,0:T(8,128)S(1)}, u32[]{:S(2)}) copy-start(f32[48,512]{1,0:T(8,128)S(1)} %bitcast_add_fusion) | copy-start | bytes 294916
  62.3 0.9 %slice-start = ((f32[48,512]{1,0:T(8,128)}), f32[48,384]{1,0:T(8,128)S(1)}, s32[]{:S(2)}) async-start(f32[48,512]{1,0:T(8,128)} %copy-done.6), calls=%async_computation | async-start | bytes 147456 | tf_op jit(solution)/shard_map/slice | solution.py:523
  63.2 1.5 %collective-permute-start.25 = (f32[48,896]{1,0:T(8,128)S(1)}, f32[48,896]{1,0:T(8,128)S(1)}, u32[]{:S(2)}, u32[]{:S(2)}) collective-permute-start(f32[48,896]{1,0:T(8,128)S(1)} %pad_maximum_fusion.1.mine_ref), channel_id=1, source_target_pairs={{0,1},{1,0},{2,3},{3,2},{4,5},{5,4},{6,7},{7,6},{8,9},{9,8},{10,11... | collective-permute-start | bytes 516104 | tf_op jit(solution)/shard_map/ppermute | solution.py:349

commit v4 on v3

--- a/solution.py
+++ b/solution.py
@@ -112,6 +112,20 @@
         extra_ref[line * own : (line + 1) * own, :] = piece[:, quarter:]
 
 
+def line_sum_kernel(*refs):
+    pieces, total_ref = refs[:-1], refs[-1]
+    quarter = pieces[0].shape[1] - LANES
+    same, cross = pieces[0][...], None
+    for line, piece in enumerate(pieces):
+        if line % 2:
+            cross = piece[...].astype(F32) if cross is None else cross + piece[...].astype(F32)
+        elif line:
+            same = same + piece[...].astype(F32)
+    total_ref[:, :quarter] = same[:, :quarter]
+    total_ref[:, quarter : 2 * quarter] = cross[:, :quarter]
+    total_ref[:, 2 * quarter :] = same[:, quarter:] + cross[:, quarter:]
+
+
 def finish_kernel(factor, mine_ref, other_ref, up_ref, dw_ref, gain_ref, bias_ref):
     own, half = mine_ref.shape[0], mine_ref.shape[1] - LANES
     quarter = half // 2
@@ -184,22 +198,22 @@
             ).astype(BF16)
 
 
-def cot_pack_kernel(cot_ref, sibling_ref, out_ref):
-    pixels, half = sibling_ref.shape
+def cot_pack_kernel(cot_ref, across_ref, sibling_ref):
+    half = sibling_ref.shape[1]
     quarter = half // 2
     side = lax.axis_index("rep") % 2
     parity = (lax.axis_index("shard") // INNER) % 2
-    start = pl.multiple_of(side * half + (1 - parity) * quarter, LANES)
-    out_ref[:pixels, :] = cot_ref[:, pl.ds(start, quarter)]
-    start = pl.multiple_of((1 - parity) * quarter, LANES)
-    out_ref[pixels:, :] = sibling_ref[:, pl.ds(start, quarter)]
+    for place in range(2):
+        start = pl.multiple_of(place * half + (1 - parity) * quarter, LANES)
+        across_ref[:, place * quarter : (place + 1) * quarter] = cot_ref[:, pl.ds(start, quarter)]
+    sibling_ref[...] = cot_ref[:, pl.ds(pl.multiple_of((1 - side) * half, LANES), half)]
 
 
 def project_kernel(relative, own, *refs):
     weights = refs[:INNER]
-    normed, cot_ref, sibling_ref, far_ref = refs[INNER : INNER + 4]
-    pieces = refs[INNER + 4 : 2 * INNER + 4]
-    gp_ref, weight, cot, grad = refs[2 * INNER + 4 :]
+    normed, cot_ref, sibling_ref, across_ref, corner_ref = refs[INNER : INNER + 5]
+    pieces = refs[INNER + 5 : 2 * INNER + 5]
+    gp_ref, weight, cot, grad = refs[2 * INNER + 5 :]
     pixels, half = sibling_ref.shape
     quarter = half // 2
     side = lax.axis_index("rep") % 2
@@ -207,10 +221,12 @@
     place_rows(weights, weight, own, relative)
     start = pl.multiple_of(side * half + parity * quarter, LANES)
     cot[:pixels, :] = cot_ref[:, pl.ds(start, quarter)]
-    cot[pixels : 2 * pixels, :] = far_ref[:pixels, :]
+    start = pl.multiple_of(side * quarter, LANES)
+    cot[pixels : 2 * pixels, :] = across_ref[:, pl.ds(start, quarter)]
     start = pl.multiple_of(parity * quarter, LANES)
     cot[2 * pixels : 3 * pixels, :] = sibling_ref[:, pl.ds(start, quarter)]
-    cot[3 * pixels :, :] = far_ref[pixels:, :]
+    start = pl.multiple_of(side * quarter, LANES)
+    cot[3 * pixels :, :] = corner_ref[:, pl.ds(start, quarter)]
     for start in range(0, quarter, LANES):
         columns = slice(start, start + LANES)
         pre_act = jnp.dot(normed[...], weight[:, columns], preferred_element_type=F32)
@@ -383,36 +399,36 @@
         norm_bias[None, :],
         in_specs=[pl.BlockSpec(memory_space=pl.ANY)] * 2 + [VMEM] * 2,
     )
+    near, far, images, cotangent = lax.optimization_barrier((near, far, images, cotangent))
     gathered = [near] + [
         over_shard(far if line % 2 else near, INNER * line) for line in range(1, lines)
     ]
+    cotangent = cotangent.reshape(pixels, hidden)
+    cot_across, cot_sibling = call(
+        cot_pack_kernel,
+        "cot_pack",
+        [shape((pixels, half), BF16)] * 2,
+        [],
+        0.4,
+        cotangent,
+    )
+    cot_across, cot_sibling = over_shard(cot_across, INNER), over_core(cot_sibling)
+    images_far, images_sibling = over_shard(images, INNER), over_core(images)
+
     rows = lines * own
     weight_lines, extra_lines = call(
         assemble_kernel,
         "assemble",
         [shape((rows, quarter), BF16), shape((rows, LANES), BF16)],
         [],
-        0.3,
+        2.0,
         *gathered,
     )
     weights = [weight_lines] + [over_shard(weight_lines, flip) for flip in range(1, INNER)]
     extras = [extra_lines] + [over_shard(extra_lines, flip) for flip in range(1, INNER)]
+    *extras, cot_across, images_far = lax.optimization_barrier((*extras, cot_across, images_far))
+    cot_corner, images_corner = over_core(cot_across), over_core(images_far)
     weights, extras = true_order(weights), true_order(extras)
-
-    images_far = over_shard(images, INNER)
-    images_sibling, images_corner = over_core(images), over_core(images_far)
-    cotangent = cotangent.reshape(pixels, hidden)
-    cot_sibling = over_core(lax.dynamic_slice(cotangent, (0, (1 - side) * half), (pixels, half)))
-    (cot_sent,) = call(
-        cot_pack_kernel,
-        "cot_pack",
-        [shape((2 * pixels, quarter), BF16)],
-        [],
-        0.5,
-        cotangent,
-        cot_sibling,
-    )
-    cot_far = over_shard(cot_sent, INNER)
 
     padded = pltpu.VMEM((tiles, height, breadth + 16, LANES), F32)
     normed, whitened, inv_std, taps = call(
@@ -453,11 +469,9 @@
         normed,
         cotangent,
         cot_sibling,
-        cot_far,
-    )
-    pieces = relative_order(pieces)
-    arrived = [over_shard(piece, flip) for flip, piece in enumerate(pieces) if flip]
-
+        cot_across,
+        cot_corner,
+    )
     gn_kept, gn_sent = call(
         functools.partial(back_project_kernel, relative, own),
         "back_project",
@@ -476,7 +490,9 @@
         gn_kept,
         over_core(gn_sent),
     )
+    gn_sent, *pieces = lax.optimization_barrier((gn_sent, *relative_order(pieces)))
     gn_other = over_shard(gn_sent, INNER)
+    arrived = [over_shard(piece, flip) for flip, piece in enumerate(pieces) if flip]
     *small, grad_conv = call(
         functools.partial(norm_back_kernel, relative, own),
         "norm_back",
@@ -512,15 +528,17 @@
     small_plane = small[0] + sum(piece.astype(F32) for piece in small_arrived)
     merged = jnp.concatenate([plane, small_plane], axis=1).reshape(lines, own, quarter + LANES)
     merged, grad_images = lax.optimization_barrier((merged, grad_images))
-    same, cross = merged[0], None
-    for line in range(1, lines):
-        came = over_shard(merged[line].astype(BF16), INNER * line).astype(F32)
-        if line % 2 == 0:
-            same = same + came
-        else:
-            cross = came if cross is None else cross + came
-    total = jnp.concatenate(
-        [same[:, :quarter], cross[:, :quarter], same[:, quarter:] + cross[:, quarter:]], axis=1
+    came = [
+        over_shard(merged[line].astype(BF16), INNER * line) for line in range(1, lines)
+    ]
+    (total,) = call(
+        line_sum_kernel,
+        "line_sum",
+        [shape((own, half + LANES), F32)],
+        [],
+        0.3,
+        merged[0],
+        *came,
     )
     if reps > 2:
         groups = [[i for i in range(reps) if i % 2 == s] for s in range(2)]

time: 65.6 us -> 66.4 us (1.012)
  waiting for transfers between devices: 18.9 us -> 22.4 us
  starting transfers between devices: 30.2 us -> 27.9 us
    ppermute x21, starting transfers between devices: 29.5 us -> 27.2 us  [over_shard(): return lax.ppermute(array, 'shard', [(i, i ^ flip) for i in range(shards)])]
    ppermute x5 -> x6, waiting for transfers between devices: 1.4 us -> 3.68 us  [over_core(): return lax.ppermute(array, 'rep', [(i, i ^ 1) for i in range(reps)])]
    unnamed x14 -> x12, local copies, waits for them, and re-layouts: 0.68 us -> 2.28 us
    ppermute x21, waiting for transfers between devices: 17.5 us -> 18.7 us  [over_shard(): return lax.ppermute(array, 'shard', [(i, i ^ flip) for i in range(shards)])]
    dynamic_slice x1 -> x0, local copies, waits for them, and re-layouts: 0.99 us -> none  [body(): lax.dynamic_slice(cotangent, (0, (1 - side) * half), (pixels, half))]
    slice x3 -> x0, local copies, waits for them, and re-layouts: 0.87 us -> none  [the longest x2 0.86 us: body(): same[:, :quarter]]
    pallas_call x10 -> x11, Pallas kernels: 12.7 us -> 12.7 us  [call(): pl.pallas_call(kernel, out_shape=outs, in_specs=in_specs or [VMEM] * len(...]
  transfers between devices with their start and end apart: 26 -> 27, of which waited for: 12 -> 15; matrix products, arithmetic and copies ran while one was open for 0% -> 0% of each run, Pallas kernels for 12% -> 11%
where the time goes in v4:
time: 66.4 us; the launch traced here: 66.2 us
  starting transfers between devices  27.9 us (42%)
  waiting for transfers between devices  22.4 us (34%)
  Pallas kernels  12.7 us (19%)
  local copies, waits for them, and re-layouts  2.3 us (3%)
  between operations  0.79 us (1%)
    ppermute x21, starting transfers between devices, over_shard(): return lax.ppermute(array, 'shard', [(i, i ^ flip) for i in range(shards)])  27.2 us
    ppermute x21, waiting for transfers between devices, over_shard(): return lax.ppermute(array, 'shard', [(i, i ^ flip) for i in range(shards)])  18.7 us
    pallas_call x11, Pallas kernels, call(): pl.pallas_call(kernel, out_shape=outs, in_specs=in_specs or [VMEM] * len(...  12.7 us
    ppermute x6, waiting for transfers between devices, over_core(): return lax.ppermute(array, 'rep', [(i, i ^ 1) for i in range(reps)])  3.68 us
    unnamed x12, local copies, waits for them, and re-layouts  2.28 us
  transfers between devices with their start and end apart: 27, of which 15 were waited for; matrix products, arithmetic and copies ran while one was open for 0% of the time, Pallas kernels for 11%

profile of v4, /device:TPU:0, one launch (start us, length us, event | category | flops | bytes accessed | tf_op | source)
XLA Modules:
  0.0 66.2 jit_solution(17973245441782246988)
XLA Ops:
  0.7 0.6 copy-done.4
  1.3 0.0 copy-done.5
  1.3 0.9 %copy-done.2 = bf16[48,1536]{1,0:T(8,128)(2,1)S(1)} copy-done((bf16[48,1536]{1,0:T(8,128)(2,1)S(1)}, bf16[48,1536]{1,0:T(8,128)(2,1)}, u32[]{:S(2)}) %copy-start.2) | copy-done | bytes 147480
  2.2 0.7 %copy-done.3 = bf16[48,49]{1,0:T(8,128)(2,1)S(1)} copy-done((bf16[48,49]{1,0:T(8,128)(2,1)S(1)}, bf16[48,49]{1,0:T(8,128)(2,1)}, u32[]{:S(2)}) %copy-start.3) | copy-done | bytes 4728
  2.9 0.3 pack.1
  3.2 4.1 %collective-permute-start.1 = (bf16[48,512]{1,0:T(8,128)(2,1)S(1)}, bf16[48,512]{1,0:T(8,128)(2,1)S(1)}, u32[]{:S(2)}, u32[]{:S(2)}) collective-permute-start(bf16[48,512]{1,0:T(8,128)(2,1)S(1)} %get-tuple-element.52.refs_0_), channel_id=1, source_target_pairs={{0,16},{2,18},{4,20},{6,22},{8,24},{10,26},{12,28},{14,30},{16,0},... | collective-permute-start | bytes 147464 | tf_op jit(solution)/shard_map/ppermute | solution.py:362
  7.3 1.3 %collective-permute-start.2 = (bf16[48,512]{1,0:T(8,128)(2,1)S(1)}, bf16[48,512]{1,0:T(8,128)(2,1)S(1)}, u32[]{:S(2)}, u32[]{:S(2)}) collective-permute-start(bf16[48,512]{1,0:T(8,128)(2,1)S(1)} %get-tuple-element.53), channel_id=1, source_target_pairs={{0,24},{2,26},{4,28},{6,30},{8,16},{10,18},{12,20},{14,22},{16,8},... | collective-permute-start | bytes 147464 | tf_op jit(solution)/shard_map/ppermute | solution.py:362
  8.7 0.2 collective-permute-start
  8.9 1.8 %collective-permute-start.10 = (bf16[1,8,16,768]{3,2,1,0:T(8,128)(2,1)S(1)}, bf16[1,8,16,768]{3,2,1,0:T(8,128)(2,1)S(1)}, u32[]{:S(2)}, u32[]{:S(2)}) collective-permute-start(bf16[1,8,16,768]{3,2,1,0:T(8,128)(2,1)S(1)} %copy-done), channel_id=1, source_target_pairs={{0,8},{2,10},{4,12},{6,14},{8,0},{10,2},{12,4},{14,6},{16,24},{18,... | collective-permute-start | bytes 589832 | tf_op jit(solution)/shard_map/ppermute | solution.py:362
  10.8 0.3 collective-permute-start.9
  11.0 0.0 collective-permute-done.1.refs_2_
  11.1 2.6 %collective-permute-done.2.refs_3_ = bf16[48,512]{1,0:T(8,128)(2,1)S(1)} collective-permute-done((bf16[48,512]{1,0:T(8,128)(2,1)S(1)}, bf16[48,512]{1,0:T(8,128)(2,1)S(1)}, u32[]{:S(2)}, u32[]{:S(2)}) %collective-permute-start.2) | collective-permute-done | bytes 49184 | tf_op jit(solution)/shard_map/ppermute | solution.py:362
  13.7 0.2 collective-permute-done.refs_1_
  13.9 2.5 %collective-permute-start.8 = (bf16[192,128]{1,0:T(8,128)(2,1)S(1)}, bf16[192,128]{1,0:T(8,128)(2,1)S(1)}, u32[]{:S(2)}, u32[]{:S(2)}) collective-permute-start(bf16[192,128]{1,0:T(8,128)(2,1)S(1)} %get-tuple-element.59.refs_0_), channel_id=1, source_target_pairs={{0,6},{2,4},{4,2},{6,0},{8,14},{10,12},{12,10},{14,8},{16,22},{18,... | collective-permute-start | bytes 147464 | tf_op jit(solution)/shard_map/ppermute | solution.py:362
  16.4 0.5 collective-permute-start.7
  16.9 0.5 collective-permute-start.6
  17.5 1.5 %collective-permute-done.8.refs_3_ = bf16[192,128]{1,0:T(8,128)(2,1)S(1)} collective-permute-done((bf16[192,128]{1,0:T(8,128)(2,1)S(1)}, bf16[192,128]{1,0:T(8,128)(2,1)S(1)}, u32[]{:S(2)}, u32[]{:S(2)}) %collective-permute-start.8) | collective-permute-done | bytes 49184 | tf_op jit(solution)/shard_map/ppermute | solution.py:362
  19.0 0.0 collective-permute-start.11
  19.0 1.5 %collective-permute-done.7.refs_2_ = bf16[192,128]{1,0:T(8,128)(2,1)S(1)} collective-permute-done((bf16[192,128]{1,0:T(8,128)(2,1)S(1)}, bf16[192,128]{1,0:T(8,128)(2,1)S(1)}, u32[]{:S(2)}, u32[]{:S(2)}) %collective-permute-start.7) | collective-permute-done | bytes 49184 | tf_op jit(solution)/shard_map/ppermute | solution.py:362
  20.5 0.5 collective-permute-done.6.refs_1_
  21.0 0.0 collective-permute-done.10.refs_5_
  21.0 0.1 collective-permute-done.9.refs_7_
  21.1 0.0 collective-permute-start.12
  21.1 0.5 collective-permute-start.13
  21.6 0.0 collective-permute-start.14
  21.6 2.4 %collective-permute-start.5 = (bf16[192,384]{1,0:T(8,128)(2,1)S(1)}, bf16[192,384]{1,0:T(8,128)(2,1)S(1)}, u32[]{:S(2)}, u32[]{:S(2)}) collective-permute-start(bf16[192,384]{1,0:T(8,128)(2,1)S(1)} %get-tuple-element.54.refs_0_), channel_id=1, source_target_pairs={{0,6},{2,4},{4,2},{6,0},{8,14},{10,12},{12,10},{14,8},{16,22},{18,... | collective-permute-start | bytes 442376 | tf_op jit(solution)/shard_map/ppermute | solution.py:362
  24.1 0.0 collective-permute-done.11.refs_6_
  24.1 0.5 collective-permute-start.4
  24.6 0.0 collective-permute-done.12.refs_7_
  24.6 0.5 collective-permute-start.3
  25.1 5.6 %conv_norm.1 = (bf16[512,768]{1,0:T(8,128)(2,1)S(1)}, f32[128,768]{1,0:T(8,128)S(1)}, f32[128,128]{1,0:T(8,128)S(1)}, f32[6,128,128]{2,1,0:T(8,128)S(1)}) custom-call(bf16[192,128]{1,0:T(8,128)(2,1)S(1)} %get-tuple-element.59.refs_0_, bf16[192,128]{1,0:T(8,128)(2,1)S(1)} %collective-permute-done.6.refs_1_, ...), custom_call_target="tpu_custom_call" | custom-call | flops 110000000 | bytes 2621440 | tf_op jit(solution)/shard_map/conv_norm/pallas_call | solution.py:335
  30.8 0.0 collective-permute-done.5.refs_3_
  30.8 1.2 %collective-permute-done.4.refs_2_ = bf16[192,384]{1,0:T(8,128)(2,1)S(1)} collective-permute-done((bf16[192,384]{1,0:T(8,128)(2,1)S(1)}, bf16[192,384]{1,0:T(8,128)(2,1)S(1)}, u32[]{:S(2)}, u32[]{:S(2)}) %collective-permute-start.4) | collective-permute-done | bytes 147488 | tf_op jit(solution)/shard_map/ppermute | solution.py:362
  31.9 0.1 collective-permute-done.3.refs_1_
  32.0 0.0 collective-permute-done.13.refs_6_
  32.1 1.6 %project.1 = (f32[192,384]{1,0:T(8,128)S(1)}, bf16[192,384]{1,0:T(8,128)(2,1)S(1)}, bf16[192,384]{1,0:T(8,128)(2,1)S(1)}, bf16[192,384]{1,0:T(8,128)(2,1)S(1)}, bf16[512,384]{1,0:T(8,128)(2,1)S(1)}) custom-call(bf16[192,384]{1,0:T(8,128)(2,1)S(1)} %get-tuple-element.54.refs_0_, bf16[192,384]{1,0:T(8,128)(2,1)S(1)} %collective-permute-done.3.refs_1_, ...), custom_call_target="tpu_custom_call" | custom-call | flops 1760000000 | bytes 3489792 | tf_op jit(solution)/shard_map/project/pallas_call | solution.py:335
  33.7 0.7 back_project.1
  34.4 0.1 collective-permute-start.15
  34.4 2.3 %collective-permute-done.15.other_ref = f32[256,768]{1,0:T(8,128)S(1)} collective-permute-done((f32[256,768]{1,0:T(8,128)S(1)}, f32[256,768]{1,0:T(8,128)S(1)}, u32[]{:S(2)}, u32[]{:S(2)}) %collective-permute-start.15) | collective-permute-done | bytes 786464 | tf_op jit(solution)/shard_map/ppermute | solution.py:365
  36.7 0.1 core_sum.1
  36.8 1.6 %collective-permute-start.16 = (bf16[192,384]{1,0:T(8,128)(2,1)S(1)}, bf16[192,384]{1,0:T(8,128)(2,1)S(1)}, u32[]{:S(2)}, u32[]{:S(2)}) collective-permute-start(bf16[192,384]{1,0:T(8,128)(2,1)S(1)} %get-tuple-element.76), channel_id=1, source_target_pairs={{0,2},{2,0},{4,6},{6,4},{8,10},{10,8},{12,14},{14,12},{16,18},{18,... | collective-permute-start | bytes 442376 | tf_op jit(solution)/shard_map/ppermute | solution.py:362
  38.4 0.7 %collective-permute-start.17 = (bf16[192,384]{1,0:T(8,128)(2,1)S(1)}, bf16[192,384]{1,0:T(8,128)(2,1)S(1)}, u32[]{:S(2)}, u32[]{:S(2)}) collective-permute-start(bf16[192,384]{1,0:T(8,128)(2,1)S(1)} %get-tuple-element.77), channel_id=1, source_target_pairs={{0,4},{2,6},{4,0},{6,2},{8,12},{10,14},{12,8},{14,10},{16,20},{18,... | collective-permute-start | bytes 442376 | tf_op jit(solution)/shard_map/ppermute | solution.py:362
  39.1 1.3 %collective-permute-start.18 = (bf16[192,384]{1,0:T(8,128)(2,1)S(1)}, bf16[192,384]{1,0:T(8,128)(2,1)S(1)}, u32[]{:S(2)}, u32[]{:S(2)}) collective-permute-start(bf16[192,384]{1,0:T(8,128)(2,1)S(1)} %get-tuple-element.78), channel_id=1, source_target_pairs={{0,6},{2,4},{4,2},{6,0},{8,14},{10,12},{12,10},{14,8},{16,22},{18,... | collective-permute-start | bytes 442376 | tf_op jit(solution)/shard_map/ppermute | solution.py:362
  40.4 0.9 %collective-permute-start.19 = (bf16[128,768]{1,0:T(8,128)(2,1)S(1)}, bf16[128,768]{1,0:T(8,128)(2,1)S(1)}, u32[]{:S(2)}, u32[]{:S(2)}) collective-permute-start(bf16[128,768]{1,0:T(8,128)(2,1)S(1)} %get-tuple-element.80), channel_id=1, source_target_pairs={{0,8},{2,10},{4,12},{6,14},{8,0},{10,2},{12,4},{14,6},{16,24},{18,... | collective-permute-start | bytes 589832 | tf_op jit(solution)/shard_map/ppermute | solution.py:362
  41.2 2.2 %collective-permute-done.16 = bf16[192,384]{1,0:T(8,128)(2,1)S(1)} collective-permute-done((bf16[192,384]{1,0:T(8,128)(2,1)S(1)}, bf16[192,384]{1,0:T(8,128)(2,1)S(1)}, u32[]{:S(2)}, u32[]{:S(2)}) %collective-permute-start.16) | collective-permute-done | bytes 147488 | tf_op jit(solution)/shard_map/ppermute | solution.py:362
  43.4 3.7 %collective-permute-done.17 = bf16[192,384]{1,0:T(8,128)(2,1)S(1)} collective-permute-done((bf16[192,384]{1,0:T(8,128)(2,1)S(1)}, bf16[192,384]{1,0:T(8,128)(2,1)S(1)}, u32[]{:S(2)}, u32[]{:S(2)}) %collective-permute-start.17) | collective-permute-done | bytes 147488 | tf_op jit(solution)/shard_map/ppermute | solution.py:362
  47.1 0.1 add_add_fusion
  47.2 1.7 %norm_back.1 = (f32[192,128]{1,0:T(8,128)S(1)}, bf16[192,128]{1,0:T(8,128)(2,1)S(1)}, bf16[192,128]{1,0:T(8,128)(2,1)S(1)}, bf16[192,128]{1,0:T(8,128)(2,1)S(1)}, f32[6,8,16,128]{3,2,1,0:T(8,128)S(1)}) custom-call(f32[128,768]{1,0:T(8,128)S(1)} %get-tuple-element.79.refs_0_, bf16[128,768]{1,0:T(8,128)(2,1)S(1)} %collective-permute-done.19.refs_1_, ...), custom_call_target="tpu_custom_call" | custom-call | flops 1870000000 | bytes 2277376 | tf_op jit(solution)/shard_map/norm_back/pallas_call | solution.py:335
  48.9 0.8 %collective-permute-start.20 = (bf16[192,128]{1,0:T(8,128)(2,1)S(1)}, bf16[192,128]{1,0:T(8,128)(2,1)S(1)}, u32[]{:S(2)}, u32[]{:S(2)}) collective-permute-start(bf16[192,128]{1,0:T(8,128)(2,1)S(1)} %get-tuple-element.85), channel_id=1, source_target_pairs={{0,2},{2,0},{4,6},{6,4},{8,10},{10,8},{12,14},{14,12},{16,18},{18,... | collective-permute-start | bytes 147464 | tf_op jit(solution)/shard_map/ppermute | solution.py:362
  49.7 1.2 %collective-permute-start.21 = (bf16[192,128]{1,0:T(8,128)(2,1)S(1)}, bf16[192,128]{1,0:T(8,128)(2,1)S(1)}, u32[]{:S(2)}, u32[]{:S(2)}) collective-permute-start(bf16[192,128]{1,0:T(8,128)(2,1)S(1)} %get-tuple-element.86), channel_id=1, source_target_pairs={{0,4},{2,6},{4,0},{6,2},{8,12},{10,14},{12,8},{14,10},{16,20},{18,... | collective-permute-start | bytes 147464 | tf_op jit(solution)/shard_map/ppermute | solution.py:362
  51.0 1.5 %collective-permute-start.22 = (bf16[192,128]{1,0:T(8,128)(2,1)S(1)}, bf16[192,128]{1,0:T(8,128)(2,1)S(1)}, u32[]{:S(2)}, u32[]{:S(2)}) collective-permute-start(bf16[192,128]{1,0:T(8,128)(2,1)S(1)} %get-tuple-element.87), channel_id=1, source_target_pairs={{0,6},{2,4},{4,2},{6,0},{8,14},{10,12},{12,10},{14,8},{16,22},{18,... | collective-permute-start | bytes 147464 | tf_op jit(solution)/shard_map/ppermute | solution.py:362
  52.5 1.9 %conv_back.1 = bf16[1,8,16,768]{3,2,1,0:T(8,128)(2,1)} custom-call(f32[6,8,16,128]{3,2,1,0:T(8,128)S(1)} %get-tuple-element.88.grad_ref, f32[6,128,128]{2,1,0:T(8,128)S(1)} %get-tuple-element.83.refs_4_.taps_ref), custom_call_target="tpu_custom_call" | custom-call | flops 2090000000 | bytes 983040 | tf_op jit(solution)/shard_map/conv_back/pallas_call | solution.py:335
  54.3 0.0 collective-permute-done.20
  54.3 0.0 collective-permute-done.21
  54.3 1.6 %collective-permute-done.22 = bf16[192,128]{1,0:T(8,128)(2,1)S(1)} collective-permute-done((bf16[192,128]{1,0:T(8,128)(2,1)S(1)}, bf16[192,128]{1,0:T(8,128)(2,1)S(1)}, u32[]{:S(2)}, u32[]{:S(2)}) %collective-permute-start.22) | collective-permute-done | bytes 49184 | tf_op jit(solution)/shard_map/ppermute | solution.py:362
  56.1 2.9 %collective-permute-start.25 = (bf16[48,512]{1,0:T(8,128)(2,1)S(1)}, bf16[48,512]{1,0:T(8,128)(2,1)S(1)}, u32[]{:S(2)}, u32[]{:S(2)}) collective-permute-start(bf16[48,512]{1,0:T(8,128)(2,1)S(1)} %get-tuple-element.95), channel_id=1, source_target_pairs={{0,24},{2,26},{4,28},{6,30},{8,16},{10,18},{12,20},{14,22},{16,8},... | collective-permute-start | bytes 147464 | tf_op jit(solution)/shard_map/ppermute | solution.py:362
  59.0 0.0 collective-permute-start.24
  59.0 1.6 %collective-permute-start.23 = (bf16[48,512]{1,0:T(8,128)(2,1)S(1)}, bf16[48,512]{1,0:T(8,128)(2,1)S(1)}, u32[]{:S(2)}, u32[]{:S(2)}) collective-permute-start(bf16[48,512]{1,0:T(8,128)(2,1)S(1)} %get-tuple-element.97), channel_id=1, source_target_pairs={{0,8},{2,10},{4,12},{6,14},{8,0},{10,2},{12,4},{14,6},{16,24},{18,... | collective-permute-start | bytes 147464 | tf_op jit(solution)/shard_map/ppermute | solution.py:362
  60.5 1.6 %collective-permute-done.25.refs_3_ = bf16[48,512]{1,0:T(8,128)(2,1)S(1)} collective-permute-done((bf16[48,512]{1,0:T(8,128)(2,1)S(1)}, bf16[48,512]{1,0:T(8,128)(2,1)S(1)}, u32[]{:S(2)}, u32[]{:S(2)}) %collective-permute-start.25) | collective-permute-done | bytes 49184 | tf_op jit(solution)/shard_map/ppermute | solution.py:362
  62.2 1.8 %collective-permute-done.24.refs_2_ = bf16[48,512]{1,0:T(8,128)(2,1)S(1)} collective-permute-done((bf16[48,512]{1,0:T(8,128)(2,1)S(1)}, bf16[48,512]{1,0:T(8,128)(2,1)S(1)}, u32[]{:S(2)}, u32[]{:S(2)}) %collective-permute-start.24) | collective-permute-done | bytes 49184 | tf_op jit(solution)/shard_map/ppermute | solution.py:362
  63.9 0.0 collective-permute-done.23.refs_1_
  64.0 0.1 collective-permute-start.26
  64.0 1.4 %collective-permute-done.26.other_ref = f32[48,896]{1,0:T(8,128)S(1)} collective-permute-done((f32[48,896]{1,0:T(8,128)S(1)}, f32[48,896]{1,0:T(8,128)S(1)}, u32[]{:S(2)}, u32[]{:S(2)}) %collective-permute-start.26) | collective-permute-done | bytes 172064 | tf_op jit(solution)/shard_map/ppermute | solution.py:365
  65.4 0.8 %finish.1 = (f32[48,1536]{1,0:T(8,128)}, f32[48,49]{1,0:T(8,128)}, f32[1,48]{1,0:T(1,128)}, f32[1,48]{1,0:T(1,128)}) custom-call(f32[48,896]{1,0:T(8,128)S(1)} %line_sum.1.mine_ref, f32[48,896]{1,0:T(8,128)S(1)} %collective-permute-done.26.other_ref), custom_call_target="tpu_custom_call" | custom-call | flops 550000000 | bytes 648768 | tf_op jit(solution)/shard_map/finish/pallas_call | solution.py:335
  (19 shorter events, 0.2 us)
Async XLA Ops:
  0.6 0.7 copy-start.4
  0.6 0.7 %copy-start.5 = (bf16[48]{0:T(256)(128)(2,1)S(1)}, bf16[48]{0:T(256)(128)(2,1)}, u32[]{:S(2)}) copy-start(bf16[48]{0:T(256)(128)(2,1)} %param.10) | copy-start | bytes 292
  1.3 0.9 %copy-start.2 = (bf16[48,1536]{1,0:T(8,128)(2,1)S(1)}, bf16[48,1536]{1,0:T(8,128)(2,1)}, u32[]{:S(2)}) copy-start(bf16[48,1536]{1,0:T(8,128)(2,1)} %w_hbm.1) | copy-start | bytes 442372
  2.2 0.7 %copy-start.3 = (bf16[48,49]{1,0:T(8,128)(2,1)S(1)}, bf16[48,49]{1,0:T(8,128)(2,1)}, u32[]{:S(2)}) copy-start(bf16[48,49]{1,0:T(8,128)(2,1)} %dw_hbm.1) | copy-start | bytes 14116
  2.9 6.0 %copy-start = (bf16[1,8,16,768]{3,2,1,0:T(8,128)(2,1)S(1)}, bf16[1,8,16,768]{3,2,1,0:T(8,128)(2,1)}, u32[]{:S(2)}) copy-start(bf16[1,8,16,768]{3,2,1,0:T(8,128)(2,1)} %refs_5_) | copy-start | bytes 589828
  2.9 7.8 %copy-start.1 = (bf16[1,8,16,1536]{3,2,1,0:T(8,128)(2,1)S(1)}, bf16[1,8,16,1536]{3,2,1,0:T(8,128)(2,1)}, u32[]{:S(2)}) copy-start(bf16[1,8,16,1536]{3,2,1,0:T(8,128)(2,1)} %param.7) | copy-start | bytes 1179652
  3.2 7.8 %collective-permute-start.1 = (bf16[48,512]{1,0:T(8,128)(2,1)S(1)}, bf16[48,512]{1,0:T(8,128)(2,1)S(1)}, u32[]{:S(2)}, u32[]{:S(2)}) collective-permute-start(bf16[48,512]{1,0:T(8,128)(2,1)S(1)} %get-tuple-element.52.refs_0_), channel_id=1, source_target_pairs={{0,16},{2,18},{4,20},{6,22},{8,24},{10,26},{12,28},{14,30},{16,0},... | collective-permute-start | bytes 147464 | tf_op jit(solution)/shard_map/ppermute | solution.py:362
  7.3 6.4 %collective-permute-start.2 = (bf16[48,512]{1,0:T(8,128)(2,1)S(1)}, bf16[48,512]{1,0:T(8,128)(2,1)S(1)}, u32[]{:S(2)}, u32[]{:S(2)}) collective-permute-start(bf16[48,512]{1,0:T(8,128)(2,1)S(1)} %get-tuple-element.53), channel_id=1, source_target_pairs={{0,24},{2,26},{4,28},{6,30},{8,16},{10,18},{12,20},{14,22},{16,8},... | collective-permute-start | bytes 147464 | tf_op jit(solution)/shard_map/ppermute | solution.py:362
  8.7 5.2 %collective-permute-start = (bf16[48,512]{1,0:T(8,128)(2,1)S(1)}, bf16[48,512]{1,0:T(8,128)(2,1)S(1)}, u32[]{:S(2)}, u32[]{:S(2)}) collective-permute-start(bf16[48,512]{1,0:T(8,128)(2,1)S(1)} %get-tuple-element.53), channel_id=1, source_target_pairs={{0,8},{2,10},{4,12},{6,14},{8,0},{10,2},{12,4},{14,6},{16,24},{18,... | collective-permute-start | bytes 147464 | tf_op jit(solution)/shard_map/ppermute | solution.py:362
  8.9 12.1 %collective-permute-start.10 = (bf16[1,8,16,768]{3,2,1,0:T(8,128)(2,1)S(1)}, bf16[1,8,16,768]{3,2,1,0:T(8,128)(2,1)S(1)}, u32[]{:S(2)}, u32[]{:S(2)}) collective-permute-start(bf16[1,8,16,768]{3,2,1,0:T(8,128)(2,1)S(1)} %copy-done), channel_id=1, source_target_pairs={{0,8},{2,10},{4,12},{6,14},{8,0},{10,2},{12,4},{14,6},{16,24},{18,... | collective-permute-start | bytes 589832 | tf_op jit(solution)/shard_map/ppermute | solution.py:362
  10.8 10.4 %collective-permute-start.9 = (bf16[128,768]{1,0:T(8,128)(2,1)S(1)}, bf16[128,768]{1,0:T(8,128)(2,1)S(1)}, u32[]{:S(2)}, u32[]{:S(2)}) collective-permute-start(bf16[128,768]{1,0:T(8,128)(2,1)S(1)} %get-tuple-element.57), channel_id=1, source_target_pairs={{0,8},{2,10},{4,12},{6,14},{8,0},{10,2},{12,4},{14,6},{16,24},{18,... | collective-permute-start | bytes 589832 | tf_op jit(solution)/shard_map/ppermute | solution.py:362
  13.9 5.1 %collective-permute-start.8 = (bf16[192,128]{1,0:T(8,128)(2,1)S(1)}, bf16[192,128]{1,0:T(8,128)(2,1)S(1)}, u32[]{:S(2)}, u32[]{:S(2)}) collective-permute-start(bf16[192,128]{1,0:T(8,128)(2,1)S(1)} %get-tuple-element.59.refs_0_), channel_id=1, source_target_pairs={{0,6},{2,4},{4,2},{6,0},{8,14},{10,12},{12,10},{14,8},{16,22},{18,... | collective-permute-start | bytes 147464 | tf_op jit(solution)/shard_map/ppermute | solution.py:362
  16.4 4.1 %collective-permute-start.7 = (bf16[192,128]{1,0:T(8,128)(2,1)S(1)}, bf16[192,128]{1,0:T(8,128)(2,1)S(1)}, u32[]{:S(2)}, u32[]{:S(2)}) collective-permute-start(bf16[192,128]{1,0:T(8,128)(2,1)S(1)} %get-tuple-element.59.refs_0_), channel_id=1, source_target_pairs={{0,4},{2,6},{4,0},{6,2},{8,12},{10,14},{12,8},{14,10},{16,20},{18,... | collective-permute-start | bytes 147464 | tf_op jit(solution)/shard_map/ppermute | solution.py:362
  16.9 4.1 %collective-permute-start.6 = (bf16[192,128]{1,0:T(8,128)(2,1)S(1)}, bf16[192,128]{1,0:T(8,128)(2,1)S(1)}, u32[]{:S(2)}, u32[]{:S(2)}) collective-permute-start(bf16[192,128]{1,0:T(8,128)(2,1)S(1)} %get-tuple-element.59.refs_0_), channel_id=1, source_target_pairs={{0,2},{2,0},{4,6},{6,4},{8,10},{10,8},{12,14},{14,12},{16,18},{18,... | collective-permute-start | bytes 147464 | tf_op jit(solution)/shard_map/ppermute | solution.py:362
  19.0 5.1 %collective-permute-start.11 = (bf16[1,8,16,768]{3,2,1,0:T(8,128)(2,1)S(1)}, bf16[1,8,16,768]{3,2,1,0:T(8,128)(2,1)S(1)}, u32[]{:S(2)}, u32[]{:S(2)}) collective-permute-start(bf16[1,8,16,768]{3,2,1,0:T(8,128)(2,1)S(1)} %copy-done), channel_id=1, source_target_pairs={{0,1},{1,0},{2,3},{3,2},{4,5},{5,4},{6,7},{7,6},{8,9},{9,8},{10,11... | collective-permute-start | bytes 589832 | tf_op jit(solution)/shard_map/ppermute | solution.py:365
  21.1 3.5 %collective-permute-start.12 = (bf16[1,8,16,768]{3,2,1,0:T(8,128)(2,1)S(1)}, bf16[1,8,16,768]{3,2,1,0:T(8,128)(2,1)S(1)}, u32[]{:S(2)}, u32[]{:S(2)}) collective-permute-start(bf16[1,8,16,768]{3,2,1,0:T(8,128)(2,1)S(1)} %collective-permute-done.10.refs_5_), channel_id=1, source_target_pairs={{0,1},{1,0},{2,3},{3,2},{4,5},{5,4},{6,7},{7,6},{8,9},{9,8},{10,11... | collective-permute-start | bytes 589832 | tf_op jit(solution)/shard_map/ppermute | solution.py:365
  21.1 10.9 %collective-permute-start.13 = (bf16[128,768]{1,0:T(8,128)(2,1)S(1)}, bf16[128,768]{1,0:T(8,128)(2,1)S(1)}, u32[]{:S(2)}, u32[]{:S(2)}) collective-permute-start(bf16[128,768]{1,0:T(8,128)(2,1)S(1)} %get-tuple-element.65), channel_id=1, source_target_pairs={{0,1},{1,0},{2,3},{3,2},{4,5},{5,4},{6,7},{7,6},{8,9},{9,8},{10,11... | collective-permute-start | bytes 589832 | tf_op jit(solution)/shard_map/ppermute | solution.py:365
  21.6 10.4 %collective-permute-start.14 = (bf16[128,768]{1,0:T(8,128)(2,1)S(1)}, bf16[128,768]{1,0:T(8,128)(2,1)S(1)}, u32[]{:S(2)}, u32[]{:S(2)}) collective-permute-start(bf16[128,768]{1,0:T(8,128)(2,1)S(1)} %collective-permute-done.9.refs_7_), channel_id=1, source_target_pairs={{0,1},{1,0},{2,3},{3,2},{4,5},{5,4},{6,7},{7,6},{8,9},{9,8},{10,11... | collective-permute-start | bytes 589832 | tf_op jit(solution)/shard_map/ppermute | solution.py:365
  21.6 9.1 %collective-permute-start.5 = (bf16[192,384]{1,0:T(8,128)(2,1)S(1)}, bf16[192,384]{1,0:T(8,128)(2,1)S(1)}, u32[]{:S(2)}, u32[]{:S(2)}) collective-permute-start(bf16[192,384]{1,0:T(8,128)(2,1)S(1)} %get-tuple-element.54.refs_0_), channel_id=1, source_target_pairs={{0,6},{2,4},{4,2},{6,0},{8,14},{10,12},{12,10},{14,8},{16,22},{18,... | collective-permute-start | bytes 442376 | tf_op jit(solution)/shard_map/ppermute | solution.py:362
  24.1 7.9 %collective-permute-start.4 = (bf16[192,384]{1,0:T(8,128)(2,1)S(1)}, bf16[192,384]{1,0:T(8,128)(2,1)S(1)}, u32[]{:S(2)}, u32[]{:S(2)}) collective-permute-start(bf16[192,384]{1,0:T(8,128)(2,1)S(1)} %get-tuple-element.54.refs_0_), channel_id=1, source_target_pairs={{0,4},{2,6},{4,0},{6,2},{8,12},{10,14},{12,8},{14,10},{16,20},{18,... | collective-permute-start | bytes 442376 | tf_op jit(solution)/shard_map/ppermute | solution.py:362
  24.6 7.5 %collective-permute-start.3 = (bf16[192,384]{1,0:T(8,128)(2,1)S(1)}, bf16[192,384]{1,0:T(8,128)(2,1)S(1)}, u32[]{:S(2)}, u32[]{:S(2)}) collective-permute-start(bf16[192,384]{1,0:T(8,128)(2,1)S(1)} %get-tuple-element.54.refs_0_), channel_id=1, source_target_pairs={{0,2},{2,0},{4,6},{6,4},{8,10},{10,8},{12,14},{14,12},{16,18},{18,... | collective-permute-start | bytes 442376 | tf_op jit(solution)/shard_map/ppermute | solution.py:362
  34.4 2.4 %collective-permute-start.15 = (f32[256,768]{1,0:T(8,128)S(1)}, f32[256,768]{1,0:T(8,128)S(1)}, u32[]{:S(2)}, u32[]{:S(2)}) collective-permute-start(f32[256,768]{1,0:T(8,128)S(1)} %get-tuple-element.69), channel_id=1, source_target_pairs={{0,1},{1,0},{2,3},{3,2},{4,5},{5,4},{6,7},{7,6},{8,9},{9,8},{10,11... | collective-permute-start | bytes 2359304 | tf_op jit(solution)/shard_map/ppermute | solution.py:365
  36.8 6.6 %collective-permute-start.16 = (bf16[192,384]{1,0:T(8,128)(2,1)S(1)}, bf16[192,384]{1,0:T(8,128)(2,1)S(1)}, u32[]{:S(2)}, u32[]{:S(2)}) collective-permute-start(bf16[192,384]{1,0:T(8,128)(2,1)S(1)} %get-tuple-element.76), channel_id=1, source_target_pairs={{0,2},{2,0},{4,6},{6,4},{8,10},{10,8},{12,14},{14,12},{16,18},{18,... | collective-permute-start | bytes 442376 | tf_op jit(solution)/shard_map/ppermute | solution.py:362
  38.4 8.8 %collective-permute-start.17 = (bf16[192,384]{1,0:T(8,128)(2,1)S(1)}, bf16[192,384]{1,0:T(8,128)(2,1)S(1)}, u32[]{:S(2)}, u32[]{:S(2)}) collective-permute-start(bf16[192,384]{1,0:T(8,128)(2,1)S(1)} %get-tuple-element.77), channel_id=1, source_target_pairs={{0,4},{2,6},{4,0},{6,2},{8,12},{10,14},{12,8},{14,10},{16,20},{18,... | collective-permute-start | bytes 442376 | tf_op jit(solution)/shard_map/ppermute | solution.py:362
  39.1 8.0 %collective-permute-start.18 = (bf16[192,384]{1,0:T(8,128)(2,1)S(1)}, bf16[192,384]{1,0:T(8,128)(2,1)S(1)}, u32[]{:S(2)}, u32[]{:S(2)}) collective-permute-start(bf16[192,384]{1,0:T(8,128)(2,1)S(1)} %get-tuple-element.78), channel_id=1, source_target_pairs={{0,6},{2,4},{4,2},{6,0},{8,14},{10,12},{12,10},{14,8},{16,22},{18,... | collective-permute-start | bytes 442376 | tf_op jit(solution)/shard_map/ppermute | solution.py:362
  40.4 6.8 %collective-permute-start.19 = (bf16[128,768]{1,0:T(8,128)(2,1)S(1)}, bf16[128,768]{1,0:T(8,128)(2,1)S(1)}, u32[]{:S(2)}, u32[]{:S(2)}) collective-permute-start(bf16[128,768]{1,0:T(8,128)(2,1)S(1)} %get-tuple-element.80), channel_id=1, source_target_pairs={{0,8},{2,10},{4,12},{6,14},{8,0},{10,2},{12,4},{14,6},{16,24},{18,... | collective-permute-start | bytes 589832 | tf_op jit(solution)/shard_map/ppermute | solution.py:362
  48.9 5.4 %collective-permute-start.20 = (bf16[192,128]{1,0:T(8,128)(2,1)S(1)}, bf16[192,128]{1,0:T(8,128)(2,1)S(1)}, u32[]{:S(2)}, u32[]{:S(2)}) collective-permute-start(bf16[192,128]{1,0:T(8,128)(2,1)S(1)} %get-tuple-element.85), channel_id=1, source_target_pairs={{0,2},{2,0},{4,6},{6,4},{8,10},{10,8},{12,14},{14,12},{16,18},{18,... | collective-permute-start | bytes 147464 | tf_op jit(solution)/shard_map/ppermute | solution.py:362
  49.7 4.6 %collective-permute-start.21 = (bf16[192,128]{1,0:T(8,128)(2,1)S(1)}, bf16[192,128]{1,0:T(8,128)(2,1)S(1)}, u32[]{:S(2)}, u32[]{:S(2)}) collective-permute-start(bf16[192,128]{1,0:T(8,128)(2,1)S(1)} %get-tuple-element.86), channel_id=1, source_target_pairs={{0,4},{2,6},{4,0},{6,2},{8,12},{10,14},{12,8},{14,10},{16,20},{18,... | collective-permute-start | bytes 147464 | tf_op jit(solution)/shard_map/ppermute | solution.py:362
  51.0 5.0 %collective-permute-start.22 = (bf16[192,128]{1,0:T(8,128)(2,1)S(1)}, bf16[192,128]{1,0:T(8,128)(2,1)S(1)}, u32[]{:S(2)}, u32[]{:S(2)}) collective-permute-start(bf16[192,128]{1,0:T(8,128)(2,1)S(1)} %get-tuple-element.87), channel_id=1, source_target_pairs={{0,6},{2,4},{4,2},{6,0},{8,14},{10,12},{12,10},{14,8},{16,22},{18,... | collective-permute-start | bytes 147464 | tf_op jit(solution)/shard_map/ppermute | solution.py:362
  56.1 6.1 %collective-permute-start.25 = (bf16[48,512]{1,0:T(8,128)(2,1)S(1)}, bf16[48,512]{1,0:T(8,128)(2,1)S(1)}, u32[]{:S(2)}, u32[]{:S(2)}) collective-permute-start(bf16[48,512]{1,0:T(8,128)(2,1)S(1)} %get-tuple-element.95), channel_id=1, source_target_pairs={{0,24},{2,26},{4,28},{6,30},{8,16},{10,18},{12,20},{14,22},{16,8},... | collective-permute-start | bytes 147464 | tf_op jit(solution)/shard_map/ppermute | solution.py:362
  59.0 5.0 %collective-permute-start.24 = (bf16[48,512]{1,0:T(8,128)(2,1)S(1)}, bf16[48,512]{1,0:T(8,128)(2,1)S(1)}, u32[]{:S(2)}, u32[]{:S(2)}) collective-permute-start(bf16[48,512]{1,0:T(8,128)(2,1)S(1)} %get-tuple-element.96), channel_id=1, source_target_pairs={{0,16},{2,18},{4,20},{6,22},{8,24},{10,26},{12,28},{14,30},{16,0},... | collective-permute-start | bytes 147464 | tf_op jit(solution)/shard_map/ppermute | solution.py:362
  59.0 5.0 %collective-permute-start.23 = (bf16[48,512]{1,0:T(8,128)(2,1)S(1)}, bf16[48,512]{1,0:T(8,128)(2,1)S(1)}, u32[]{:S(2)}, u32[]{:S(2)}) collective-permute-start(bf16[48,512]{1,0:T(8,128)(2,1)S(1)} %get-tuple-element.97), channel_id=1, source_target_pairs={{0,8},{2,10},{4,12},{6,14},{8,0},{10,2},{12,4},{14,6},{16,24},{18,... | collective-permute-start | bytes 147464 | tf_op jit(solution)/shard_map/ppermute | solution.py:362
  64.0 1.5 %collective-permute-start.26 = (f32[48,896]{1,0:T(8,128)S(1)}, f32[48,896]{1,0:T(8,128)S(1)}, u32[]{:S(2)}, u32[]{:S(2)}) collective-permute-start(f32[48,896]{1,0:T(8,128)S(1)} %line_sum.1.mine_ref), channel_id=1, source_target_pairs={{0,1},{1,0},{2,3},{3,2},{4,5},{5,4},{6,7},{7,6},{8,9},{9,8},{10,11... | collective-permute-start | bytes 516104 | tf_op jit(solution)/shard_map/ppermute | solution.py:365

commit v5 on v4

--- a/solution.py
+++ b/solution.py
@@ -112,6 +112,19 @@
         extra_ref[line * own : (line + 1) * own, :] = piece[:, quarter:]
 
 
+def plane_sum_kernel(lines, *refs):
+    pieces, small, outs = refs[:INNER], refs[INNER : 2 * INNER], refs[2 * INNER :]
+    own = pieces[0].shape[0] // lines
+    quarter = pieces[0].shape[1]
+    for line, out in enumerate(outs):
+        rows = slice(line * own, (line + 1) * own)
+        for parts, columns in ((pieces, slice(0, quarter)), (small, slice(quarter, None))):
+            total = parts[0][rows, :]
+            for part in parts[1:]:
+                total = total + part[rows, :].astype(F32)
+            out[:, columns] = total.astype(out.dtype)
+
+
 def line_sum_kernel(*refs):
     pieces, total_ref = refs[:-1], refs[-1]
     quarter = pieces[0].shape[1] - LANES
@@ -144,9 +157,9 @@
 
 def conv_norm_kernel(relative, own, *refs):
     small = refs[:INNER]
-    sources = refs[INNER : INNER + 4]
+    sources = refs[INNER : INNER + 2]
     x_ref = sources[0]
-    normed_ref, white_ref, inv_ref, taps_ref, gathered, padded, conv = refs[INNER + 4 :]
+    normed_ref, white_ref, inv_ref, taps_ref, gathered, padded, conv = refs[INNER + 2 :]
     height, breadth, depth = x_ref.shape[1:]
     tiles = depth // LANES
     pixels = height * breadth
@@ -209,16 +222,20 @@
     sibling_ref[...] = cot_ref[:, pl.ds(pl.multiple_of((1 - side) * half, LANES), half)]
 
 
+def order_kernel(relative, own, *refs):
+    place_rows(refs[:INNER], refs[INNER], own, relative)
+
+
 def project_kernel(relative, own, *refs):
-    weights = refs[:INNER]
-    normed, cot_ref, sibling_ref, across_ref, corner_ref = refs[INNER : INNER + 5]
-    pieces = refs[INNER + 5 : 2 * INNER + 5]
-    gp_ref, weight, cot, grad = refs[2 * INNER + 5 :]
+    weight, n_own, n_sibling, cot_ref, sibling_ref, across_ref, corner_ref = refs[:7]
+    pieces = refs[7 : 7 + INNER]
+    gp_ref, normed, cot, grad = refs[7 + INNER :]
     pixels, half = sibling_ref.shape
     quarter = half // 2
     side = lax.axis_index("rep") % 2
     parity = (lax.axis_index("shard") // INNER) % 2
-    place_rows(weights, weight, own, relative)
+    normed[: 2 * pixels, :] = n_own[...]
+    normed[2 * pixels :, :] = n_sibling[...]
     start = pl.multiple_of(side * half + parity * quarter, LANES)
     cot[:pixels, :] = cot_ref[:, pl.ds(start, quarter)]
     start = pl.multiple_of(side * quarter, LANES)
@@ -237,11 +254,8 @@
     split_rows(grad, pieces, own, relative)
 
 
-def back_project_kernel(relative, own, *refs):
-    weights = refs[:INNER]
-    gp_ref, own_ref, other_ref, weight = refs[INNER:]
+def back_project_kernel(weight, gp_ref, own_ref, other_ref):
     rows = own_ref.shape[0]
-    place_rows(weights, weight, own, relative)
     grad_normed = lax.dot_general(
         gp_ref[...], weight[...], (((1,), (1,)), ((), ())), preferred_element_type=F32
     )
@@ -397,7 +411,7 @@
         depthwise_weight,
         norm_gain[None, :],
         norm_bias[None, :],
-        in_specs=[pl.BlockSpec(memory_space=pl.ANY)] * 2 + [VMEM] * 2,
+        in_specs=[pl.BlockSpec(memory_space=pltpu.HBM)] * 2 + [VMEM] * 2,
     )
     near, far, images, cotangent = lax.optimization_barrier((near, far, images, cotangent))
     gathered = [near] + [
@@ -413,7 +427,7 @@
         cotangent,
     )
     cot_across, cot_sibling = over_shard(cot_across, INNER), over_core(cot_sibling)
-    images_far, images_sibling = over_shard(images, INNER), over_core(images)
+    images_far = over_shard(images, INNER)
 
     rows = lines * own
     weight_lines, extra_lines = call(
@@ -426,16 +440,24 @@
     )
     weights = [weight_lines] + [over_shard(weight_lines, flip) for flip in range(1, INNER)]
     extras = [extra_lines] + [over_shard(extra_lines, flip) for flip in range(1, INNER)]
-    *extras, cot_across, images_far = lax.optimization_barrier((*extras, cot_across, images_far))
-    cot_corner, images_corner = over_core(cot_across), over_core(images_far)
+    *extras, cot_across = lax.optimization_barrier((*extras, cot_across))
+    cot_corner = over_core(cot_across)
     weights, extras = true_order(weights), true_order(extras)
+    (weight,) = call(
+        functools.partial(order_kernel, relative, own),
+        "order",
+        [shape((depth, quarter), BF16)],
+        [],
+        3.0,
+        *weights,
+    )
 
     padded = pltpu.VMEM((tiles, height, breadth + 16, LANES), F32)
     normed, whitened, inv_std, taps = call(
         functools.partial(conv_norm_kernel, relative, own),
         "conv_norm",
         [
-            shape((4 * pixels, depth), BF16),
+            shape((2 * pixels, depth), BF16),
             shape((pixels, depth), F32),
             shape((pixels, LANES), F32),
             shape((tiles, LANES, LANES), F32),
@@ -449,10 +471,8 @@
         *extras,
         images,
         images_far,
-        images_sibling,
-        images_corner,
-    )
-
+    )
+    normed_sibling = over_core(normed)
     *pieces, grad_pre = call(
         functools.partial(project_kernel, relative, own),
         "project",
@@ -460,25 +480,26 @@
         + [shape((rows, quarter), BF16)] * (INNER - 1)
         + [shape((4 * pixels, quarter), BF16)],
         [
-            pltpu.VMEM((depth, quarter), BF16),
+            pltpu.VMEM((4 * pixels, depth), BF16),
             pltpu.VMEM((4 * pixels, quarter), BF16),
             pltpu.VMEM((depth, quarter), F32),
         ],
         1.6,
-        *weights,
+        weight,
         normed,
+        normed_sibling,
         cotangent,
         cot_sibling,
         cot_across,
         cot_corner,
     )
     gn_kept, gn_sent = call(
-        functools.partial(back_project_kernel, relative, own),
+        back_project_kernel,
         "back_project",
         [shape((2 * pixels, depth), F32)] * 2,
-        [pltpu.VMEM((depth, quarter), BF16)],
+        [],
         0.7,
-        *weights,
+        weight,
         grad_pre,
     )
     gn_kept, gn_sent = call(
@@ -524,20 +545,26 @@
         taps,
     )
 
-    plane = pieces[0] + sum(piece.astype(F32) for piece in arrived)
-    small_plane = small[0] + sum(piece.astype(F32) for piece in small_arrived)
-    merged = jnp.concatenate([plane, small_plane], axis=1).reshape(lines, own, quarter + LANES)
-    merged, grad_images = lax.optimization_barrier((merged, grad_images))
-    came = [
-        over_shard(merged[line].astype(BF16), INNER * line) for line in range(1, lines)
-    ]
+    home, *sent = call(
+        functools.partial(plane_sum_kernel, lines),
+        "plane_sum",
+        [shape((own, quarter + LANES), F32)] + [shape((own, quarter + LANES), BF16)] * (lines - 1),
+        [],
+        0.4,
+        pieces[0],
+        *arrived,
+        small[0],
+        *small_arrived,
+    )
+    home, grad_images = lax.optimization_barrier((home, grad_images))
+    came = [over_shard(piece, INNER * line) for line, piece in enumerate(sent, 1)]
     (total,) = call(
         line_sum_kernel,
         "line_sum",
         [shape((own, half + LANES), F32)],
         [],
         0.3,
-        merged[0],
+        home,
         *came,
     )
     if reps > 2:

time: 66.4 us -> 60.9 us (0.917)
  Pallas kernels: 12.7 us -> 9.96 us
  waiting for transfers between devices: 22.4 us -> 19.8 us
    pallas_call x11 -> x13, Pallas kernels: 12.7 us -> 9.96 us  [call(): pl.pallas_call(kernel, out_shape=outs, in_specs=in_specs or [VMEM] * len(...]
    ppermute x21, waiting for transfers between devices: 18.7 us -> 16.1 us  [over_shard(): return lax.ppermute(array, 'shard', [(i, i ^ flip) for i in range(shards)])]
    ppermute x6 -> x5, waiting for transfers between devices: 3.68 us -> 3.7 us  [over_core(): return lax.ppermute(array, 'rep', [(i, i ^ 1) for i in range(reps)])]
  transfers between devices with their start and end apart: 27 -> 26, of which waited for: 15 -> 15; matrix products, arithmetic and copies ran while one was open for 0% -> 0% of each run, Pallas kernels for 11% -> 11%
where the time goes in v5:
time: 60.9 us; the launch traced here: 60.7 us
  starting transfers between devices  27.9 us (46%)
  waiting for transfers between devices  19.8 us (33%)
  Pallas kernels  9.96 us (16%)
  local copies, waits for them, and re-layouts  2.28 us (4%)
  between operations  0.76 us (1%)
    ppermute x21, starting transfers between devices, over_shard(): return lax.ppermute(array, 'shard', [(i, i ^ flip) for i in range(shards)])  27 us
    ppermute x21, waiting for transfers between devices, over_shard(): return lax.ppermute(array, 'shard', [(i, i ^ flip) for i in range(shards)])  16.1 us
    pallas_call x13, Pallas kernels, call(): pl.pallas_call(kernel, out_shape=outs, in_specs=in_specs or [VMEM] * len(...  9.96 us
    ppermute x5, waiting for transfers between devices, over_core(): return lax.ppermute(array, 'rep', [(i, i ^ 1) for i in range(reps)])  3.7 us
    unnamed x12, local copies, waits for them, and re-layouts  2.28 us
  transfers between devices with their start and end apart: 26, of which 15 were waited for; matrix products, arithmetic and copies ran while one was open for 0% of the time, Pallas kernels for 11%

profile of v5, /device:TPU:0, one launch (start us, length us, event | category | flops | bytes accessed | tf_op | source)
XLA Modules:
  0.0 60.7 jit_solution(10716852326999322761)
XLA Ops:
  0.7 0.6 %copy-done.4 = bf16[48]{0:T(256)(128)(2,1)S(1)} copy-done((bf16[48]{0:T(256)(128)(2,1)S(1)}, bf16[48]{0:T(256)(128)(2,1)}, u32[]{:S(2)}) %copy-start.4) | copy-done | bytes 120
  1.3 0.0 copy-done.5
  1.3 0.9 %copy-done.2 = bf16[48,1536]{1,0:T(8,128)(2,1)S(1)} copy-done((bf16[48,1536]{1,0:T(8,128)(2,1)S(1)}, bf16[48,1536]{1,0:T(8,128)(2,1)}, u32[]{:S(2)}) %copy-start.2) | copy-done | bytes 147480
  2.2 0.7 %copy-done.3 = bf16[48,49]{1,0:T(8,128)(2,1)S(1)} copy-done((bf16[48,49]{1,0:T(8,128)(2,1)S(1)}, bf16[48,49]{1,0:T(8,128)(2,1)}, u32[]{:S(2)}) %copy-start.3) | copy-done | bytes 4728
  2.9 0.3 pack.1
  3.2 4.1 %collective-permute-start.1 = (bf16[48,512]{1,0:T(8,128)(2,1)S(1)}, bf16[48,512]{1,0:T(8,128)(2,1)S(1)}, u32[]{:S(2)}, u32[]{:S(2)}) collective-permute-start(bf16[48,512]{1,0:T(8,128)(2,1)S(1)} %get-tuple-element.55.refs_0_), channel_id=1, source_target_pairs={{0,16},{2,18},{4,20},{6,22},{8,24},{10,26},{12,28},{14,30},{16,0},... | collective-permute-start | bytes 147464 | tf_op jit(solution)/shard_map/ppermute | solution.py:376
  7.3 1.3 %collective-permute-start.2 = (bf16[48,512]{1,0:T(8,128)(2,1)S(1)}, bf16[48,512]{1,0:T(8,128)(2,1)S(1)}, u32[]{:S(2)}, u32[]{:S(2)}) collective-permute-start(bf16[48,512]{1,0:T(8,128)(2,1)S(1)} %get-tuple-element.56), channel_id=1, source_target_pairs={{0,24},{2,26},{4,28},{6,30},{8,16},{10,18},{12,20},{14,22},{16,8},... | collective-permute-start | bytes 147464 | tf_op jit(solution)/shard_map/ppermute | solution.py:376
  8.7 0.2 collective-permute-start
  8.9 1.8 %collective-permute-start.10 = (bf16[1,8,16,768]{3,2,1,0:T(8,128)(2,1)S(1)}, bf16[1,8,16,768]{3,2,1,0:T(8,128)(2,1)S(1)}, u32[]{:S(2)}, u32[]{:S(2)}) collective-permute-start(bf16[1,8,16,768]{3,2,1,0:T(8,128)(2,1)S(1)} %copy-done), channel_id=1, source_target_pairs={{0,8},{2,10},{4,12},{6,14},{8,0},{10,2},{12,4},{14,6},{16,24},{18,... | collective-permute-start | bytes 589832 | tf_op jit(solution)/shard_map/ppermute | solution.py:376
  10.8 0.3 collective-permute-start.9
  11.0 0.0 collective-permute-done.1.refs_2_
  11.1 2.6 %collective-permute-done.2.refs_3_ = bf16[48,512]{1,0:T(8,128)(2,1)S(1)} collective-permute-done((bf16[48,512]{1,0:T(8,128)(2,1)S(1)}, bf16[48,512]{1,0:T(8,128)(2,1)S(1)}, u32[]{:S(2)}, u32[]{:S(2)}) %collective-permute-start.2) | collective-permute-done | bytes 49184 | tf_op jit(solution)/shard_map/ppermute | solution.py:376
  13.7 0.2 collective-permute-done.refs_1_
  13.9 2.5 %collective-permute-start.8 = (bf16[192,128]{1,0:T(8,128)(2,1)S(1)}, bf16[192,128]{1,0:T(8,128)(2,1)S(1)}, u32[]{:S(2)}, u32[]{:S(2)}) collective-permute-start(bf16[192,128]{1,0:T(8,128)(2,1)S(1)} %get-tuple-element.61.refs_0_), channel_id=1, source_target_pairs={{0,6},{2,4},{4,2},{6,0},{8,14},{10,12},{12,10},{14,8},{16,22},{18,... | collective-permute-start | bytes 147464 | tf_op jit(solution)/shard_map/ppermute | solution.py:376
  16.4 0.5 collective-permute-start.7
  16.9 0.5 collective-permute-start.6
  17.5 1.5 %collective-permute-done.8.refs_3_ = bf16[192,128]{1,0:T(8,128)(2,1)S(1)} collective-permute-done((bf16[192,128]{1,0:T(8,128)(2,1)S(1)}, bf16[192,128]{1,0:T(8,128)(2,1)S(1)}, u32[]{:S(2)}, u32[]{:S(2)}) %collective-permute-start.8) | collective-permute-done | bytes 49184 | tf_op jit(solution)/shard_map/ppermute | solution.py:376
  19.0 2.6 %collective-permute-start.5 = (bf16[192,384]{1,0:T(8,128)(2,1)S(1)}, bf16[192,384]{1,0:T(8,128)(2,1)S(1)}, u32[]{:S(2)}, u32[]{:S(2)}) collective-permute-start(bf16[192,384]{1,0:T(8,128)(2,1)S(1)} %get-tuple-element.57.refs_0_), channel_id=1, source_target_pairs={{0,6},{2,4},{4,2},{6,0},{8,14},{10,12},{12,10},{14,8},{16,22},{18,... | collective-permute-start | bytes 442376 | tf_op jit(solution)/shard_map/ppermute | solution.py:376
  21.5 0.2 collective-permute-done.7.refs_2_
  21.8 1.1 %collective-permute-start.4 = (bf16[192,384]{1,0:T(8,128)(2,1)S(1)}, bf16[192,384]{1,0:T(8,128)(2,1)S(1)}, u32[]{:S(2)}, u32[]{:S(2)}) collective-permute-start(bf16[192,384]{1,0:T(8,128)(2,1)S(1)} %get-tuple-element.57.refs_0_), channel_id=1, source_target_pairs={{0,4},{2,6},{4,0},{6,2},{8,12},{10,14},{12,8},{14,10},{16,20},{18,... | collective-permute-start | bytes 442376 | tf_op jit(solution)/shard_map/ppermute | solution.py:376
  22.8 0.0 collective-permute-done.6.refs_1_
  22.8 0.1 collective-permute-start.3
  22.9 0.0 collective-permute-done.9.refs_5_
  22.9 0.0 collective-permute-done.10.refs_5_
  22.9 2.9 %conv_norm.1 = (bf16[256,768]{1,0:T(8,128)(2,1)S(1)}, f32[128,768]{1,0:T(8,128)S(1)}, f32[128,128]{1,0:T(8,128)S(1)}, f32[6,128,128]{2,1,0:T(8,128)S(1)}) custom-call(bf16[192,128]{1,0:T(8,128)(2,1)S(1)} %get-tuple-element.61.refs_0_, bf16[192,128]{1,0:T(8,128)(2,1)S(1)} %collective-permute-done.6.refs_1_, ...), custom_call_target="tpu_custom_call" | custom-call | flops 110000000 | bytes 1835008 | tf_op jit(solution)/shard_map/conv_norm/pallas_call | solution.py:349
  25.9 0.1 collective-permute-start.11
  25.9 0.5 collective-permute-start.12
  26.4 0.0 collective-permute-done.5.refs_3_
  26.4 0.1 collective-permute-start.13
  26.5 0.4 collective-permute-done.4.refs_2_
  26.9 1.1 %collective-permute-done.3.refs_1_ = bf16[192,384]{1,0:T(8,128)(2,1)S(1)} collective-permute-done((bf16[192,384]{1,0:T(8,128)(2,1)S(1)}, bf16[192,384]{1,0:T(8,128)(2,1)S(1)}, u32[]{:S(2)}, u32[]{:S(2)}) %collective-permute-start.3) | collective-permute-done | bytes 147488 | tf_op jit(solution)/shard_map/ppermute | solution.py:376
  28.0 0.1 order.1.refs_0_.weight
  28.0 0.0 collective-permute-done.12.refs_4_
  28.1 0.1 collective-permute-done.13.refs_6_
  28.2 1.5 %project.1 = (f32[192,384]{1,0:T(8,128)S(1)}, bf16[192,384]{1,0:T(8,128)(2,1)S(1)}, bf16[192,384]{1,0:T(8,128)(2,1)S(1)}, bf16[192,384]{1,0:T(8,128)(2,1)S(1)}, bf16[512,384]{1,0:T(8,128)(2,1)S(1)}) custom-call(bf16[768,384]{1,0:T(8,128)(2,1)S(1)} %order.1.refs_0_.weight, bf16[256,768]{1,0:T(8,128)(2,1)S(1)} %get-tuple-element.66.refs_1_, ...), custom_call_target="tpu_custom_call" | custom-call | flops 1760000000 | bytes 3489792 | tf_op jit(solution)/shard_map/project/pallas_call | solution.py:349
  29.7 0.6 back_project.1
  30.3 0.2 collective-permute-start.14
  30.5 2.2 %collective-permute-done.14.other_ref = f32[256,768]{1,0:T(8,128)S(1)} collective-permute-done((f32[256,768]{1,0:T(8,128)S(1)}, f32[256,768]{1,0:T(8,128)S(1)}, u32[]{:S(2)}, u32[]{:S(2)}) %collective-permute-start.14) | collective-permute-done | bytes 786464 | tf_op jit(solution)/shard_map/ppermute | solution.py:379
  32.7 0.1 core_sum.1
  32.8 0.5 collective-permute-start.18
  33.3 1.6 %collective-permute-start.15 = (bf16[192,384]{1,0:T(8,128)(2,1)S(1)}, bf16[192,384]{1,0:T(8,128)(2,1)S(1)}, u32[]{:S(2)}, u32[]{:S(2)}) collective-permute-start(bf16[192,384]{1,0:T(8,128)(2,1)S(1)} %get-tuple-element.78), channel_id=1, source_target_pairs={{0,2},{2,0},{4,6},{6,4},{8,10},{10,8},{12,14},{14,12},{16,18},{18,... | collective-permute-start | bytes 442376 | tf_op jit(solution)/shard_map/ppermute | solution.py:376
  34.8 1.9 %collective-permute-start.16 = (bf16[192,384]{1,0:T(8,128)(2,1)S(1)}, bf16[192,384]{1,0:T(8,128)(2,1)S(1)}, u32[]{:S(2)}, u32[]{:S(2)}) collective-permute-start(bf16[192,384]{1,0:T(8,128)(2,1)S(1)} %get-tuple-element.79), channel_id=1, source_target_pairs={{0,4},{2,6},{4,0},{6,2},{8,12},{10,14},{12,8},{14,10},{16,20},{18,... | collective-permute-start | bytes 442376 | tf_op jit(solution)/shard_map/ppermute | solution.py:376
  36.7 0.1 collective-permute-start.17
  36.7 3.0 %collective-permute-done.18.refs_1_ = bf16[128,768]{1,0:T(8,128)(2,1)S(1)} collective-permute-done((bf16[128,768]{1,0:T(8,128)(2,1)S(1)}, bf16[128,768]{1,0:T(8,128)(2,1)S(1)}, u32[]{:S(2)}, u32[]{:S(2)}) %collective-permute-start.18) | collective-permute-done | bytes 196640 | tf_op jit(solution)/shard_map/ppermute | solution.py:376
  39.8 1.7 %norm_back.1 = (f32[192,128]{1,0:T(8,128)S(1)}, bf16[192,128]{1,0:T(8,128)(2,1)S(1)}, bf16[192,128]{1,0:T(8,128)(2,1)S(1)}, bf16[192,128]{1,0:T(8,128)(2,1)S(1)}, f32[6,8,16,128]{3,2,1,0:T(8,128)S(1)}) custom-call(f32[128,768]{1,0:T(8,128)S(1)} %get-tuple-element.81.refs_0_, bf16[128,768]{1,0:T(8,128)(2,1)S(1)} %collective-permute-done.18.refs_1_, ...), custom_call_target="tpu_custom_call" | custom-call | flops 1870000000 | bytes 2277376 | tf_op jit(solution)/shard_map/norm_back/pallas_call | solution.py:349
  41.5 2.0 %collective-permute-start.19 = (bf16[192,128]{1,0:T(8,128)(2,1)S(1)}, bf16[192,128]{1,0:T(8,128)(2,1)S(1)}, u32[]{:S(2)}, u32[]{:S(2)}) collective-permute-start(bf16[192,128]{1,0:T(8,128)(2,1)S(1)} %get-tuple-element.87), channel_id=1, source_target_pairs={{0,2},{2,0},{4,6},{6,4},{8,10},{10,8},{12,14},{14,12},{16,18},{18,... | collective-permute-start | bytes 147464 | tf_op jit(solution)/shard_map/ppermute | solution.py:376
  43.5 1.0 %collective-permute-start.20 = (bf16[192,128]{1,0:T(8,128)(2,1)S(1)}, bf16[192,128]{1,0:T(8,128)(2,1)S(1)}, u32[]{:S(2)}, u32[]{:S(2)}) collective-permute-start(bf16[192,128]{1,0:T(8,128)(2,1)S(1)} %get-tuple-element.88), channel_id=1, source_target_pairs={{0,4},{2,6},{4,0},{6,2},{8,12},{10,14},{12,8},{14,10},{16,20},{18,... | collective-permute-start | bytes 147464 | tf_op jit(solution)/shard_map/ppermute | solution.py:376
  44.4 0.0 collective-permute-done.15.refs_1_
  44.4 0.6 collective-permute-start.21
  45.0 0.0 collective-permute-done.16.refs_2_
  45.0 0.6 collective-permute-done.19.refs_5_
  45.6 2.3 %collective-permute-done.20.refs_6_ = bf16[192,128]{1,0:T(8,128)(2,1)S(1)} collective-permute-done((bf16[192,128]{1,0:T(8,128)(2,1)S(1)}, bf16[192,128]{1,0:T(8,128)(2,1)S(1)}, u32[]{:S(2)}, u32[]{:S(2)}) %collective-permute-start.20) | collective-permute-done | bytes 49184 | tf_op jit(solution)/shard_map/ppermute | solution.py:376
  47.9 1.5 %collective-permute-done.21.refs_7_ = bf16[192,128]{1,0:T(8,128)(2,1)S(1)} collective-permute-done((bf16[192,128]{1,0:T(8,128)(2,1)S(1)}, bf16[192,128]{1,0:T(8,128)(2,1)S(1)}, u32[]{:S(2)}, u32[]{:S(2)}) %collective-permute-start.21) | collective-permute-done | bytes 49184 | tf_op jit(solution)/shard_map/ppermute | solution.py:376
  49.4 0.1 plane_sum.1
  49.5 1.0 %collective-permute-start.22 = (bf16[48,512]{1,0:T(8,128)(2,1)S(1)}, bf16[48,512]{1,0:T(8,128)(2,1)S(1)}, u32[]{:S(2)}, u32[]{:S(2)}) collective-permute-start(bf16[48,512]{1,0:T(8,128)(2,1)S(1)} %get-tuple-element.94), channel_id=1, source_target_pairs={{0,8},{2,10},{4,12},{6,14},{8,0},{10,2},{12,4},{14,6},{16,24},{18,... | collective-permute-start | bytes 147464 | tf_op jit(solution)/shard_map/ppermute | solution.py:376
  50.6 2.0 %collective-permute-start.23 = (bf16[48,512]{1,0:T(8,128)(2,1)S(1)}, bf16[48,512]{1,0:T(8,128)(2,1)S(1)}, u32[]{:S(2)}, u32[]{:S(2)}) collective-permute-start(bf16[48,512]{1,0:T(8,128)(2,1)S(1)} %get-tuple-element.95), channel_id=1, source_target_pairs={{0,16},{2,18},{4,20},{6,22},{8,24},{10,26},{12,28},{14,30},{16,0},... | collective-permute-start | bytes 147464 | tf_op jit(solution)/shard_map/ppermute | solution.py:376
  52.6 1.4 %collective-permute-start.24 = (bf16[48,512]{1,0:T(8,128)(2,1)S(1)}, bf16[48,512]{1,0:T(8,128)(2,1)S(1)}, u32[]{:S(2)}, u32[]{:S(2)}) collective-permute-start(bf16[48,512]{1,0:T(8,128)(2,1)S(1)} %get-tuple-element.96), channel_id=1, source_target_pairs={{0,24},{2,26},{4,28},{6,30},{8,16},{10,18},{12,20},{14,22},{16,8},... | collective-permute-start | bytes 147464 | tf_op jit(solution)/shard_map/ppermute | solution.py:376
  54.0 1.9 %conv_back.1 = bf16[1,8,16,768]{3,2,1,0:T(8,128)(2,1)} custom-call(f32[6,8,16,128]{3,2,1,0:T(8,128)S(1)} %get-tuple-element.91.grad_ref, f32[6,128,128]{2,1,0:T(8,128)S(1)} %get-tuple-element.85.refs_4_.taps_ref), custom_call_target="tpu_custom_call" | custom-call | flops 2090000000 | bytes 983040 | tf_op jit(solution)/shard_map/conv_back/pallas_call | solution.py:349
  55.8 0.0 collective-permute-done.22.refs_1_
  55.8 0.4 collective-permute-done.23.refs_2_
  56.2 2.2 %collective-permute-done.24.refs_3_ = bf16[48,512]{1,0:T(8,128)(2,1)S(1)} collective-permute-done((bf16[48,512]{1,0:T(8,128)(2,1)S(1)}, bf16[48,512]{1,0:T(8,128)(2,1)S(1)}, u32[]{:S(2)}, u32[]{:S(2)}) %collective-permute-start.24) | collective-permute-done | bytes 49184 | tf_op jit(solution)/shard_map/ppermute | solution.py:376
  58.5 0.1 collective-permute-start.25
  58.6 1.4 %collective-permute-done.25.other_ref = f32[48,896]{1,0:T(8,128)S(1)} collective-permute-done((f32[48,896]{1,0:T(8,128)S(1)}, f32[48,896]{1,0:T(8,128)S(1)}, u32[]{:S(2)}, u32[]{:S(2)}) %collective-permute-start.25) | collective-permute-done | bytes 172064 | tf_op jit(solution)/shard_map/ppermute | solution.py:379
  60.0 0.8 %finish.1 = (f32[48,1536]{1,0:T(8,128)}, f32[48,49]{1,0:T(8,128)}, f32[1,48]{1,0:T(1,128)}, f32[1,48]{1,0:T(1,128)}) custom-call(f32[48,896]{1,0:T(8,128)S(1)} %line_sum.1.mine_ref, f32[48,896]{1,0:T(8,128)S(1)} %collective-permute-done.25.other_ref), custom_call_target="tpu_custom_call" | custom-call | flops 550000000 | bytes 648768 | tf_op jit(solution)/shard_map/finish/pallas_call | solution.py:349
  (13 shorter events, 0.1 us)
Async XLA Ops:
  0.6 0.7 %copy-start.4 = (bf16[48]{0:T(256)(128)(2,1)S(1)}, bf16[48]{0:T(256)(128)(2,1)}, u32[]{:S(2)}) copy-start(bf16[48]{0:T(256)(128)(2,1)} %param.9) | copy-start | bytes 292
  0.6 0.7 %copy-start.5 = (bf16[48]{0:T(256)(128)(2,1)S(1)}, bf16[48]{0:T(256)(128)(2,1)}, u32[]{:S(2)}) copy-start(bf16[48]{0:T(256)(128)(2,1)} %param.10) | copy-start | bytes 292
  1.3 0.9 %copy-start.2 = (bf16[48,1536]{1,0:T(8,128)(2,1)S(1)}, bf16[48,1536]{1,0:T(8,128)(2,1)}, u32[]{:S(2)}) copy-start(bf16[48,1536]{1,0:T(8,128)(2,1)} %w_hbm.1) | copy-start | bytes 442372
  2.2 0.7 %copy-start.3 = (bf16[48,49]{1,0:T(8,128)(2,1)S(1)}, bf16[48,49]{1,0:T(8,128)(2,1)}, u32[]{:S(2)}) copy-start(bf16[48,49]{1,0:T(8,128)(2,1)} %dw_hbm.1) | copy-start | bytes 14116
  2.9 6.0 %copy-start = (bf16[1,8,16,768]{3,2,1,0:T(8,128)(2,1)S(1)}, bf16[1,8,16,768]{3,2,1,0:T(8,128)(2,1)}, u32[]{:S(2)}) copy-start(bf16[1,8,16,768]{3,2,1,0:T(8,128)(2,1)} %refs_5_) | copy-start | bytes 589828
  2.9 7.8 %copy-start.1 = (bf16[1,8,16,1536]{3,2,1,0:T(8,128)(2,1)S(1)}, bf16[1,8,16,1536]{3,2,1,0:T(8,128)(2,1)}, u32[]{:S(2)}) copy-start(bf16[1,8,16,1536]{3,2,1,0:T(8,128)(2,1)} %param.7) | copy-start | bytes 1179652
  3.2 7.8 %collective-permute-start.1 = (bf16[48,512]{1,0:T(8,128)(2,1)S(1)}, bf16[48,512]{1,0:T(8,128)(2,1)S(1)}, u32[]{:S(2)}, u32[]{:S(2)}) collective-permute-start(bf16[48,512]{1,0:T(8,128)(2,1)S(1)} %get-tuple-element.55.refs_0_), channel_id=1, source_target_pairs={{0,16},{2,18},{4,20},{6,22},{8,24},{10,26},{12,28},{14,30},{16,0},... | collective-permute-start | bytes 147464 | tf_op jit(solution)/shard_map/ppermute | solution.py:376
  7.3 6.4 %collective-permute-start.2 = (bf16[48,512]{1,0:T(8,128)(2,1)S(1)}, bf16[48,512]{1,0:T(8,128)(2,1)S(1)}, u32[]{:S(2)}, u32[]{:S(2)}) collective-permute-start(bf16[48,512]{1,0:T(8,128)(2,1)S(1)} %get-tuple-element.56), channel_id=1, source_target_pairs={{0,24},{2,26},{4,28},{6,30},{8,16},{10,18},{12,20},{14,22},{16,8},... | collective-permute-start | bytes 147464 | tf_op jit(solution)/shard_map/ppermute | solution.py:376
  8.7 5.2 %collective-permute-start = (bf16[48,512]{1,0:T(8,128)(2,1)S(1)}, bf16[48,512]{1,0:T(8,128)(2,1)S(1)}, u32[]{:S(2)}, u32[]{:S(2)}) collective-permute-start(bf16[48,512]{1,0:T(8,128)(2,1)S(1)} %get-tuple-element.56), channel_id=1, source_target_pairs={{0,8},{2,10},{4,12},{6,14},{8,0},{10,2},{12,4},{14,6},{16,24},{18,... | collective-permute-start | bytes 147464 | tf_op jit(solution)/shard_map/ppermute | solution.py:376
  8.9 14.0 %collective-permute-start.10 = (bf16[1,8,16,768]{3,2,1,0:T(8,128)(2,1)S(1)}, bf16[1,8,16,768]{3,2,1,0:T(8,128)(2,1)S(1)}, u32[]{:S(2)}, u32[]{:S(2)}) collective-permute-start(bf16[1,8,16,768]{3,2,1,0:T(8,128)(2,1)S(1)} %copy-done), channel_id=1, source_target_pairs={{0,8},{2,10},{4,12},{6,14},{8,0},{10,2},{12,4},{14,6},{16,24},{18,... | collective-permute-start | bytes 589832 | tf_op jit(solution)/shard_map/ppermute | solution.py:376
  10.8 12.2 %collective-permute-start.9 = (bf16[128,768]{1,0:T(8,128)(2,1)S(1)}, bf16[128,768]{1,0:T(8,128)(2,1)S(1)}, u32[]{:S(2)}, u32[]{:S(2)}) collective-permute-start(bf16[128,768]{1,0:T(8,128)(2,1)S(1)} %get-tuple-element.60), channel_id=1, source_target_pairs={{0,8},{2,10},{4,12},{6,14},{8,0},{10,2},{12,4},{14,6},{16,24},{18,... | collective-permute-start | bytes 589832 | tf_op jit(solution)/shard_map/ppermute | solution.py:376
  13.9 5.1 %collective-permute-start.8 = (bf16[192,128]{1,0:T(8,128)(2,1)S(1)}, bf16[192,128]{1,0:T(8,128)(2,1)S(1)}, u32[]{:S(2)}, u32[]{:S(2)}) collective-permute-start(bf16[192,128]{1,0:T(8,128)(2,1)S(1)} %get-tuple-element.61.refs_0_), channel_id=1, source_target_pairs={{0,6},{2,4},{4,2},{6,0},{8,14},{10,12},{12,10},{14,8},{16,22},{18,... | collective-permute-start | bytes 147464 | tf_op jit(solution)/shard_map/ppermute | solution.py:376
  16.4 5.3 %collective-permute-start.7 = (bf16[192,128]{1,0:T(8,128)(2,1)S(1)}, bf16[192,128]{1,0:T(8,128)(2,1)S(1)}, u32[]{:S(2)}, u32[]{:S(2)}) collective-permute-start(bf16[192,128]{1,0:T(8,128)(2,1)S(1)} %get-tuple-element.61.refs_0_), channel_id=1, source_target_pairs={{0,4},{2,6},{4,0},{6,2},{8,12},{10,14},{12,8},{14,10},{16,20},{18,... | collective-permute-start | bytes 147464 | tf_op jit(solution)/shard_map/ppermute | solution.py:376
  16.9 5.9 %collective-permute-start.6 = (bf16[192,128]{1,0:T(8,128)(2,1)S(1)}, bf16[192,128]{1,0:T(8,128)(2,1)S(1)}, u32[]{:S(2)}, u32[]{:S(2)}) collective-permute-start(bf16[192,128]{1,0:T(8,128)(2,1)S(1)} %get-tuple-element.61.refs_0_), channel_id=1, source_target_pairs={{0,2},{2,0},{4,6},{6,4},{8,10},{10,8},{12,14},{14,12},{16,18},{18,... | collective-permute-start | bytes 147464 | tf_op jit(solution)/shard_map/ppermute | solution.py:376
  19.0 7.5 %collective-permute-start.5 = (bf16[192,384]{1,0:T(8,128)(2,1)S(1)}, bf16[192,384]{1,0:T(8,128)(2,1)S(1)}, u32[]{:S(2)}, u32[]{:S(2)}) collective-permute-start(bf16[192,384]{1,0:T(8,128)(2,1)S(1)} %get-tuple-element.57.refs_0_), channel_id=1, source_target_pairs={{0,6},{2,4},{4,2},{6,0},{8,14},{10,12},{12,10},{14,8},{16,22},{18,... | collective-permute-start | bytes 442376 | tf_op jit(solution)/shard_map/ppermute | solution.py:376
  21.8 5.1 %collective-permute-start.4 = (bf16[192,384]{1,0:T(8,128)(2,1)S(1)}, bf16[192,384]{1,0:T(8,128)(2,1)S(1)}, u32[]{:S(2)}, u32[]{:S(2)}) collective-permute-start(bf16[192,384]{1,0:T(8,128)(2,1)S(1)} %get-tuple-element.57.refs_0_), channel_id=1, source_target_pairs={{0,4},{2,6},{4,0},{6,2},{8,12},{10,14},{12,8},{14,10},{16,20},{18,... | collective-permute-start | bytes 442376 | tf_op jit(solution)/shard_map/ppermute | solution.py:376
  22.8 5.1 %collective-permute-start.3 = (bf16[192,384]{1,0:T(8,128)(2,1)S(1)}, bf16[192,384]{1,0:T(8,128)(2,1)S(1)}, u32[]{:S(2)}, u32[]{:S(2)}) collective-permute-start(bf16[192,384]{1,0:T(8,128)(2,1)S(1)} %get-tuple-element.57.refs_0_), channel_id=1, source_target_pairs={{0,2},{2,0},{4,6},{6,4},{8,10},{10,8},{12,14},{14,12},{16,18},{18,... | collective-permute-start | bytes 442376 | tf_op jit(solution)/shard_map/ppermute | solution.py:376
  25.9 2.4 %collective-permute-start.11 = (bf16[256,768]{1,0:T(8,128)(2,1)S(1)}, bf16[256,768]{1,0:T(8,128)(2,1)S(1)}, u32[]{:S(2)}, u32[]{:S(2)}) collective-permute-start(bf16[256,768]{1,0:T(8,128)(2,1)S(1)} %get-tuple-element.66.refs_1_), channel_id=1, source_target_pairs={{0,1},{1,0},{2,3},{3,2},{4,5},{5,4},{6,7},{7,6},{8,9},{9,8},{10,11... | collective-permute-start | bytes 1179656 | tf_op jit(solution)/shard_map/ppermute | solution.py:379
  25.9 2.1 %collective-permute-start.12 = (bf16[128,768]{1,0:T(8,128)(2,1)S(1)}, bf16[128,768]{1,0:T(8,128)(2,1)S(1)}, u32[]{:S(2)}, u32[]{:S(2)}) collective-permute-start(bf16[128,768]{1,0:T(8,128)(2,1)S(1)} %get-tuple-element.67), channel_id=1, source_target_pairs={{0,1},{1,0},{2,3},{3,2},{4,5},{5,4},{6,7},{7,6},{8,9},{9,8},{10,11... | collective-permute-start | bytes 589832 | tf_op jit(solution)/shard_map/ppermute | solution.py:379
  26.4 1.8 %collective-permute-start.13 = (bf16[128,768]{1,0:T(8,128)(2,1)S(1)}, bf16[128,768]{1,0:T(8,128)(2,1)S(1)}, u32[]{:S(2)}, u32[]{:S(2)}) collective-permute-start(bf16[128,768]{1,0:T(8,128)(2,1)S(1)} %collective-permute-done.9.refs_5_), channel_id=1, source_target_pairs={{0,1},{1,0},{2,3},{3,2},{4,5},{5,4},{6,7},{7,6},{8,9},{9,8},{10,11... | collective-permute-start | bytes 589832 | tf_op jit(solution)/shard_map/ppermute | solution.py:379
  30.3 2.4 %collective-permute-start.14 = (f32[256,768]{1,0:T(8,128)S(1)}, f32[256,768]{1,0:T(8,128)S(1)}, u32[]{:S(2)}, u32[]{:S(2)}) collective-permute-start(f32[256,768]{1,0:T(8,128)S(1)} %get-tuple-element.71), channel_id=1, source_target_pairs={{0,1},{1,0},{2,3},{3,2},{4,5},{5,4},{6,7},{7,6},{8,9},{9,8},{10,11... | collective-permute-start | bytes 2359304 | tf_op jit(solution)/shard_map/ppermute | solution.py:379
  32.8 7.0 %collective-permute-start.18 = (bf16[128,768]{1,0:T(8,128)(2,1)S(1)}, bf16[128,768]{1,0:T(8,128)(2,1)S(1)}, u32[]{:S(2)}, u32[]{:S(2)}) collective-permute-start(bf16[128,768]{1,0:T(8,128)(2,1)S(1)} %get-tuple-element.82), channel_id=1, source_target_pairs={{0,8},{2,10},{4,12},{6,14},{8,0},{10,2},{12,4},{14,6},{16,24},{18,... | collective-permute-start | bytes 589832 | tf_op jit(solution)/shard_map/ppermute | solution.py:376
  33.3 11.2 %collective-permute-start.15 = (bf16[192,384]{1,0:T(8,128)(2,1)S(1)}, bf16[192,384]{1,0:T(8,128)(2,1)S(1)}, u32[]{:S(2)}, u32[]{:S(2)}) collective-permute-start(bf16[192,384]{1,0:T(8,128)(2,1)S(1)} %get-tuple-element.78), channel_id=1, source_target_pairs={{0,2},{2,0},{4,6},{6,4},{8,10},{10,8},{12,14},{14,12},{16,18},{18,... | collective-permute-start | bytes 442376 | tf_op jit(solution)/shard_map/ppermute | solution.py:376
  34.8 10.2 %collective-permute-start.16 = (bf16[192,384]{1,0:T(8,128)(2,1)S(1)}, bf16[192,384]{1,0:T(8,128)(2,1)S(1)}, u32[]{:S(2)}, u32[]{:S(2)}) collective-permute-start(bf16[192,384]{1,0:T(8,128)(2,1)S(1)} %get-tuple-element.79), channel_id=1, source_target_pairs={{0,4},{2,6},{4,0},{6,2},{8,12},{10,14},{12,8},{14,10},{16,20},{18,... | collective-permute-start | bytes 442376 | tf_op jit(solution)/shard_map/ppermute | solution.py:376
  36.7 8.3 %collective-permute-start.17 = (bf16[192,384]{1,0:T(8,128)(2,1)S(1)}, bf16[192,384]{1,0:T(8,128)(2,1)S(1)}, u32[]{:S(2)}, u32[]{:S(2)}) collective-permute-start(bf16[192,384]{1,0:T(8,128)(2,1)S(1)} %get-tuple-element.80), channel_id=1, source_target_pairs={{0,6},{2,4},{4,2},{6,0},{8,14},{10,12},{12,10},{14,8},{16,22},{18,... | collective-permute-start | bytes 442376 | tf_op jit(solution)/shard_map/ppermute | solution.py:376
  41.5 4.2 %collective-permute-start.19 = (bf16[192,128]{1,0:T(8,128)(2,1)S(1)}, bf16[192,128]{1,0:T(8,128)(2,1)S(1)}, u32[]{:S(2)}, u32[]{:S(2)}) collective-permute-start(bf16[192,128]{1,0:T(8,128)(2,1)S(1)} %get-tuple-element.87), channel_id=1, source_target_pairs={{0,2},{2,0},{4,6},{6,4},{8,10},{10,8},{12,14},{14,12},{16,18},{18,... | collective-permute-start | bytes 147464 | tf_op jit(solution)/shard_map/ppermute | solution.py:376
  43.5 4.4 %collective-permute-start.20 = (bf16[192,128]{1,0:T(8,128)(2,1)S(1)}, bf16[192,128]{1,0:T(8,128)(2,1)S(1)}, u32[]{:S(2)}, u32[]{:S(2)}) collective-permute-start(bf16[192,128]{1,0:T(8,128)(2,1)S(1)} %get-tuple-element.88), channel_id=1, source_target_pairs={{0,4},{2,6},{4,0},{6,2},{8,12},{10,14},{12,8},{14,10},{16,20},{18,... | collective-permute-start | bytes 147464 | tf_op jit(solution)/shard_map/ppermute | solution.py:376
  44.4 5.0 %collective-permute-start.21 = (bf16[192,128]{1,0:T(8,128)(2,1)S(1)}, bf16[192,128]{1,0:T(8,128)(2,1)S(1)}, u32[]{:S(2)}, u32[]{:S(2)}) collective-permute-start(bf16[192,128]{1,0:T(8,128)(2,1)S(1)} %get-tuple-element.89), channel_id=1, source_target_pairs={{0,6},{2,4},{4,2},{6,0},{8,14},{10,12},{12,10},{14,8},{16,22},{18,... | collective-permute-start | bytes 147464 | tf_op jit(solution)/shard_map/ppermute | solution.py:376
  49.5 6.3 %collective-permute-start.22 = (bf16[48,512]{1,0:T(8,128)(2,1)S(1)}, bf16[48,512]{1,0:T(8,128)(2,1)S(1)}, u32[]{:S(2)}, u32[]{:S(2)}) collective-permute-start(bf16[48,512]{1,0:T(8,128)(2,1)S(1)} %get-tuple-element.94), channel_id=1, source_target_pairs={{0,8},{2,10},{4,12},{6,14},{8,0},{10,2},{12,4},{14,6},{16,24},{18,... | collective-permute-start | bytes 147464 | tf_op jit(solution)/shard_map/ppermute | solution.py:376
  50.6 5.6 %collective-permute-start.23 = (bf16[48,512]{1,0:T(8,128)(2,1)S(1)}, bf16[48,512]{1,0:T(8,128)(2,1)S(1)}, u32[]{:S(2)}, u32[]{:S(2)}) collective-permute-start(bf16[48,512]{1,0:T(8,128)(2,1)S(1)} %get-tuple-element.95), channel_id=1, source_target_pairs={{0,16},{2,18},{4,20},{6,22},{8,24},{10,26},{12,28},{14,30},{16,0},... | collective-permute-start | bytes 147464 | tf_op jit(solution)/shard_map/ppermute | solution.py:376
  52.6 5.9 %collective-permute-start.24 = (bf16[48,512]{1,0:T(8,128)(2,1)S(1)}, bf16[48,512]{1,0:T(8,128)(2,1)S(1)}, u32[]{:S(2)}, u32[]{:S(2)}) collective-permute-start(bf16[48,512]{1,0:T(8,128)(2,1)S(1)} %get-tuple-element.96), channel_id=1, source_target_pairs={{0,24},{2,26},{4,28},{6,30},{8,16},{10,18},{12,20},{14,22},{16,8},... | collective-permute-start | bytes 147464 | tf_op jit(solution)/shard_map/ppermute | solution.py:376
  58.5 1.5 %collective-permute-start.25 = (f32[48,896]{1,0:T(8,128)S(1)}, f32[48,896]{1,0:T(8,128)S(1)}, u32[]{:S(2)}, u32[]{:S(2)}) collective-permute-start(f32[48,896]{1,0:T(8,128)S(1)} %line_sum.1.mine_ref), channel_id=1, source_target_pairs={{0,1},{1,0},{2,3},{3,2},{4,5},{5,4},{6,7},{7,6},{8,9},{9,8},{10,11... | collective-permute-start | bytes 516104 | tf_op jit(solution)/shard_map/ppermute | solution.py:379

commit v6 on v5

--- a/solution.py
+++ b/solution.py
@@ -19,8 +19,8 @@
 VMEM = pl.BlockSpec(memory_space=pltpu.VMEM)
 
 
-def params():
-    return pltpu.CompilerParams(vmem_limit_bytes=48 * 1024 * 1024)
+def params(mebibytes):
+    return pltpu.CompilerParams(vmem_limit_bytes=mebibytes * 1024 * 1024)
 
 
 def gelu_slope(inputs):
@@ -342,7 +342,7 @@
     lax.fori_loop(0, tiles, one_tile, 0)
 
 
-def call(kernel, name, outs, scratch, micros, *args, in_specs=None):
+def call(kernel, name, outs, scratch, micros, *args, in_specs=None, mebibytes=48):
     flops = int(micros * 1.1e9)
     moved = sum(math.prod(a.shape) * a.dtype.itemsize for a in args)
     moved += sum(math.prod(o.shape) * o.dtype.itemsize for o in outs)
@@ -352,7 +352,7 @@
         in_specs=in_specs or [VMEM] * len(args),
         out_specs=[VMEM] * len(outs),
         scratch_shapes=scratch,
-        compiler_params=params(),
+        compiler_params=params(mebibytes),
         cost_estimate=pl.CostEstimate(flops=flops, bytes_accessed=moved, transcendentals=0),
         name=name,
     )(*args)
@@ -412,6 +412,7 @@
         norm_gain[None, :],
         norm_bias[None, :],
         in_specs=[pl.BlockSpec(memory_space=pltpu.HBM)] * 2 + [VMEM] * 2,
+        mebibytes=63,
     )
     near, far, images, cotangent = lax.optimization_barrier((near, far, images, cotangent))
     gathered = [near] + [
@@ -440,8 +441,6 @@
     )
     weights = [weight_lines] + [over_shard(weight_lines, flip) for flip in range(1, INNER)]
     extras = [extra_lines] + [over_shard(extra_lines, flip) for flip in range(1, INNER)]
-    *extras, cot_across = lax.optimization_barrier((*extras, cot_across))
-    cot_corner = over_core(cot_across)
     weights, extras = true_order(weights), true_order(extras)
     (weight,) = call(
         functools.partial(order_kernel, relative, own),
@@ -472,7 +471,8 @@
         images,
         images_far,
     )
-    normed_sibling = over_core(normed)
+    normed, cot_across = lax.optimization_barrier((normed, cot_across))
+    normed_sibling, cot_corner = over_core(normed), over_core(cot_across)
     *pieces, grad_pre = call(
         functools.partial(project_kernel, relative, own),
         "project",
@@ -511,7 +511,7 @@
         gn_kept,
         over_core(gn_sent),
     )
-    gn_sent, *pieces = lax.optimization_barrier((gn_sent, *relative_order(pieces)))
+    pieces = relative_order(pieces)
     gn_other = over_shard(gn_sent, INNER)
     arrived = [over_shard(piece, flip) for flip, piece in enumerate(pieces) if flip]
     *small, grad_conv = call(
@@ -540,11 +540,12 @@
         "conv_back",
         [shape(images.shape, BF16)],
         [padded],
-        1.9,
+        0.1,
         grad_conv,
         taps,
     )
 
+    *small_arrived, grad_images = lax.optimization_barrier((*small_arrived, grad_images))
     home, *sent = call(
         functools.partial(plane_sum_kernel, lines),
         "plane_sum",
@@ -556,7 +557,6 @@
         small[0],
         *small_arrived,
     )
-    home, grad_images = lax.optimization_barrier((home, grad_images))
     came = [over_shard(piece, INNER * line) for line, piece in enumerate(sent, 1)]
     (total,) = call(
         line_sum_kernel,

time: 60.9 us -> 62.1 us (1.020)
  local copies, waits for them, and re-layouts: 2.28 us -> 0.01 us
  Pallas kernels: 9.96 us -> 12 us
  starting transfers between devices: 27.9 us -> 29.7 us
    unnamed x12 -> x6, local copies, waits for them, and re-layouts: 2.28 us -> 0.01 us
    pallas_call x13, Pallas kernels: 9.96 us -> 12 us  [call(): pl.pallas_call(kernel, out_shape=outs, in_specs=in_specs or [VMEM] * len(...]
    ppermute x21, starting transfers between devices: 27 us -> 28.8 us  [over_shard(): return lax.ppermute(array, 'shard', [(i, i ^ flip) for i in range(shards)])]
  transfers between devices with their start and end apart: 26 -> 26, of which waited for: 15 -> 14; matrix products, arithmetic and copies ran while one was open for 0% -> 0% of each run, Pallas kernels for 11% -> 11%
where the time goes in v6:
time: 62.1 us; the launch traced here: 61.9 us
  starting transfers between devices  29.7 us (48%)
  waiting for transfers between devices  19.4 us (31%)
  Pallas kernels  12 us (19%)
  between operations  0.78 us (1%)
    ppermute x21, starting transfers between devices, over_shard(): return lax.ppermute(array, 'shard', [(i, i ^ flip) for i in range(shards)])  28.8 us
    ppermute x21, waiting for transfers between devices, over_shard(): return lax.ppermute(array, 'shard', [(i, i ^ flip) for i in range(shards)])  15.7 us
    pallas_call x13, Pallas kernels, call(): pl.pallas_call(kernel, out_shape=outs, in_specs=in_specs or [VMEM] * len(...  12 us
    ppermute x5, waiting for transfers between devices, over_core(): return lax.ppermute(array, 'rep', [(i, i ^ 1) for i in range(reps)])  3.7 us
  transfers between devices with their start and end apart: 26, of which 14 were waited for; matrix products, arithmetic and copies ran while one was open for 0% of the time, Pallas kernels for 11%

profile of v6, /device:TPU:0, one launch (start us, length us, event | category | flops | bytes accessed | tf_op | source)
XLA Modules:
  0.0 61.9 jit_solution(12965473713313126134)
XLA Ops:
  0.6 0.0 copy-start
  0.6 0.0 copy-start.1
  0.7 2.4 %pack.1 = (bf16[48,512]{1,0:T(8,128)(2,1)}, bf16[48,512]{1,0:T(8,128)(2,1)}) custom-call(bf16[48,1536]{1,0:T(8,128)(2,1)} %w_hbm.1, bf16[48,49]{1,0:T(8,128)(2,1)} %dw_hbm.1, bf16[1,48]{1,0:T(2,128)(2,1)} %bitcast.7, bf16[1,48]{1,0:T(2,128)(2,1)} %bitcast.8), custom_call_target="tpu_custom_call" | custom-call | flops 550000000 | bytes 250656 | tf_op jit(solution)/shard_map/pack/pallas_call | solution.py:349
  3.0 4.1 %collective-permute-start.1 = (bf16[48,512]{1,0:T(8,128)(2,1)}, bf16[48,512]{1,0:T(8,128)(2,1)S(1)}, u32[]{:S(2)}, u32[]{:S(2)}) collective-permute-start(bf16[48,512]{1,0:T(8,128)(2,1)} %get-tuple-element.49.refs_0_), channel_id=1, source_target_pairs={{0,16},{2,18},{4,20},{6,22},{8,24},{10,26},{12,28},{14,30},{16,0},... | collective-permute-start | bytes 147464 | tf_op jit(solution)/shard_map/ppermute | solution.py:376
  7.1 1.3 %collective-permute-start.2 = (bf16[48,512]{1,0:T(8,128)(2,1)}, bf16[48,512]{1,0:T(8,128)(2,1)S(1)}, u32[]{:S(2)}, u32[]{:S(2)}) collective-permute-start(bf16[48,512]{1,0:T(8,128)(2,1)} %get-tuple-element.50), channel_id=1, source_target_pairs={{0,24},{2,26},{4,28},{6,30},{8,16},{10,18},{12,20},{14,22},{16,8},... | collective-permute-start | bytes 147464 | tf_op jit(solution)/shard_map/ppermute | solution.py:376
  8.5 0.2 collective-permute-start
  8.7 1.8 %collective-permute-start.9 = (bf16[1,8,16,768]{3,2,1,0:T(8,128)(2,1)S(1)}, bf16[1,8,16,768]{3,2,1,0:T(8,128)(2,1)S(1)}, u32[]{:S(2)}, u32[]{:S(2)}) collective-permute-start(bf16[1,8,16,768]{3,2,1,0:T(8,128)(2,1)S(1)} %copy-done), channel_id=1, source_target_pairs={{0,8},{2,10},{4,12},{6,14},{8,0},{10,2},{12,4},{14,6},{16,24},{18,... | collective-permute-start | bytes 589832 | tf_op jit(solution)/shard_map/ppermute | solution.py:376
  10.6 0.3 collective-permute-start.10
  10.9 0.0 collective-permute-done.1.refs_2_
  10.9 2.9 %collective-permute-done.2.refs_3_ = bf16[48,512]{1,0:T(8,128)(2,1)S(1)} collective-permute-done((bf16[48,512]{1,0:T(8,128)(2,1)}, bf16[48,512]{1,0:T(8,128)(2,1)S(1)}, u32[]{:S(2)}, u32[]{:S(2)}) %collective-permute-start.2) | collective-permute-done | bytes 49184 | tf_op jit(solution)/shard_map/ppermute | solution.py:376
  13.8 0.1 collective-permute-done.refs_1_
  13.9 2.5 %collective-permute-start.8 = (bf16[192,128]{1,0:T(8,128)(2,1)S(1)}, bf16[192,128]{1,0:T(8,128)(2,1)S(1)}, u32[]{:S(2)}, u32[]{:S(2)}) collective-permute-start(bf16[192,128]{1,0:T(8,128)(2,1)S(1)} %get-tuple-element.52.refs_0_), channel_id=1, source_target_pairs={{0,6},{2,4},{4,2},{6,0},{8,14},{10,12},{12,10},{14,8},{16,22},{18,... | collective-permute-start | bytes 147464 | tf_op jit(solution)/shard_map/ppermute | solution.py:376
  16.4 0.5 collective-permute-start.7
  17.0 0.5 collective-permute-start.6
  17.5 1.5 %collective-permute-done.8.refs_3_ = bf16[192,128]{1,0:T(8,128)(2,1)S(1)} collective-permute-done((bf16[192,128]{1,0:T(8,128)(2,1)S(1)}, bf16[192,128]{1,0:T(8,128)(2,1)S(1)}, u32[]{:S(2)}, u32[]{:S(2)}) %collective-permute-start.8) | collective-permute-done | bytes 49184 | tf_op jit(solution)/shard_map/ppermute | solution.py:376
  19.0 2.6 %collective-permute-start.5 = (bf16[192,384]{1,0:T(8,128)(2,1)S(1)}, bf16[192,384]{1,0:T(8,128)(2,1)S(1)}, u32[]{:S(2)}, u32[]{:S(2)}) collective-permute-start(bf16[192,384]{1,0:T(8,128)(2,1)S(1)} %get-tuple-element.51.refs_0_), channel_id=1, source_target_pairs={{0,6},{2,4},{4,2},{6,0},{8,14},{10,12},{12,10},{14,8},{16,22},{18,... | collective-permute-start | bytes 442376 | tf_op jit(solution)/shard_map/ppermute | solution.py:376
  21.5 0.2 collective-permute-done.7.refs_2_
  21.8 1.1 %collective-permute-start.4 = (bf16[192,384]{1,0:T(8,128)(2,1)S(1)}, bf16[192,384]{1,0:T(8,128)(2,1)S(1)}, u32[]{:S(2)}, u32[]{:S(2)}) collective-permute-start(bf16[192,384]{1,0:T(8,128)(2,1)S(1)} %get-tuple-element.51.refs_0_), channel_id=1, source_target_pairs={{0,4},{2,6},{4,0},{6,2},{8,12},{10,14},{12,8},{14,10},{16,20},{18,... | collective-permute-start | bytes 442376 | tf_op jit(solution)/shard_map/ppermute | solution.py:376
  22.8 0.0 collective-permute-done.6.refs_1_
  22.8 0.1 collective-permute-start.3
  22.9 0.0 collective-permute-done.9.refs_5_
  22.9 2.9 %conv_norm.1 = (bf16[256,768]{1,0:T(8,128)(2,1)S(1)}, f32[128,768]{1,0:T(8,128)S(1)}, f32[128,128]{1,0:T(8,128)S(1)}, f32[6,128,128]{2,1,0:T(8,128)S(1)}) custom-call(bf16[192,128]{1,0:T(8,128)(2,1)S(1)} %get-tuple-element.52.refs_0_, bf16[192,128]{1,0:T(8,128)(2,1)S(1)} %collective-permute-done.6.refs_1_, ...), custom_call_target="tpu_custom_call" | custom-call | flops 110000000 | bytes 1835008 | tf_op jit(solution)/shard_map/conv_norm/pallas_call | solution.py:349
  25.9 0.0 collective-permute-done.10.refs_5_
  25.9 0.1 collective-permute-start.11
  26.0 0.5 collective-permute-start.12
  26.5 0.0 collective-permute-done.5.refs_3_
  26.5 0.1 collective-permute-start.13
  26.5 0.4 collective-permute-done.4.refs_2_
  26.9 1.1 %collective-permute-done.3.refs_1_ = bf16[192,384]{1,0:T(8,128)(2,1)S(1)} collective-permute-done((bf16[192,384]{1,0:T(8,128)(2,1)S(1)}, bf16[192,384]{1,0:T(8,128)(2,1)S(1)}, u32[]{:S(2)}, u32[]{:S(2)}) %collective-permute-start.3) | collective-permute-done | bytes 147488 | tf_op jit(solution)/shard_map/ppermute | solution.py:376
  28.0 0.1 order.1.refs_0_.weight
  28.1 0.0 collective-permute-done.12.refs_4_
  28.1 0.2 collective-permute-done.13.refs_6_
  28.2 0.0 collective-permute-done.11.refs_2_
  28.2 1.5 %project.1 = (f32[192,384]{1,0:T(8,128)S(1)}, bf16[192,384]{1,0:T(8,128)(2,1)S(1)}, bf16[192,384]{1,0:T(8,128)(2,1)S(1)}, bf16[192,384]{1,0:T(8,128)(2,1)S(1)}, bf16[512,384]{1,0:T(8,128)(2,1)S(1)}) custom-call(bf16[768,384]{1,0:T(8,128)(2,1)S(1)} %order.1.refs_0_.weight, bf16[256,768]{1,0:T(8,128)(2,1)S(1)} %get-tuple-element.57.refs_1_, ...), custom_call_target="tpu_custom_call" | custom-call | flops 1760000000 | bytes 3489792 | tf_op jit(solution)/shard_map/project/pallas_call | solution.py:349
  29.8 0.6 back_project.1
  30.3 0.2 collective-permute-start.14
  30.6 2.1 %collective-permute-done.14.other_ref = f32[256,768]{1,0:T(8,128)S(1)} collective-permute-done((f32[256,768]{1,0:T(8,128)S(1)}, f32[256,768]{1,0:T(8,128)S(1)}, u32[]{:S(2)}, u32[]{:S(2)}) %collective-permute-start.14) | collective-permute-done | bytes 786464 | tf_op jit(solution)/shard_map/ppermute | solution.py:379
  32.7 0.1 core_sum.1
  32.8 0.5 collective-permute-start.15
  33.3 1.6 %collective-permute-start.19 = (bf16[192,384]{1,0:T(8,128)(2,1)S(1)}, bf16[192,384]{1,0:T(8,128)(2,1)S(1)}, u32[]{:S(2)}, u32[]{:S(2)}) collective-permute-start(bf16[192,384]{1,0:T(8,128)(2,1)S(1)} %get-tuple-element.74), channel_id=1, source_target_pairs={{0,2},{2,0},{4,6},{6,4},{8,10},{10,8},{12,14},{14,12},{16,18},{18,... | collective-permute-start | bytes 442376 | tf_op jit(solution)/shard_map/ppermute | solution.py:376
  34.9 1.9 %collective-permute-start.20 = (bf16[192,384]{1,0:T(8,128)(2,1)S(1)}, bf16[192,384]{1,0:T(8,128)(2,1)S(1)}, u32[]{:S(2)}, u32[]{:S(2)}) collective-permute-start(bf16[192,384]{1,0:T(8,128)(2,1)S(1)} %get-tuple-element.75), channel_id=1, source_target_pairs={{0,4},{2,6},{4,0},{6,2},{8,12},{10,14},{12,8},{14,10},{16,20},{18,... | collective-permute-start | bytes 442376 | tf_op jit(solution)/shard_map/ppermute | solution.py:376
  36.7 0.1 collective-permute-start.21
  36.8 3.0 %collective-permute-done.15.refs_1_ = bf16[128,768]{1,0:T(8,128)(2,1)S(1)} collective-permute-done((bf16[128,768]{1,0:T(8,128)(2,1)S(1)}, bf16[128,768]{1,0:T(8,128)(2,1)S(1)}, u32[]{:S(2)}, u32[]{:S(2)}) %collective-permute-start.15) | collective-permute-done | bytes 196640 | tf_op jit(solution)/shard_map/ppermute | solution.py:376
  39.8 1.7 %norm_back.1 = (f32[192,128]{1,0:T(8,128)S(1)}, bf16[192,128]{1,0:T(8,128)(2,1)S(1)}, bf16[192,128]{1,0:T(8,128)(2,1)S(1)}, bf16[192,128]{1,0:T(8,128)(2,1)S(1)}, f32[6,8,16,128]{3,2,1,0:T(8,128)S(1)}) custom-call(f32[128,768]{1,0:T(8,128)S(1)} %get-tuple-element.63.refs_0_, bf16[128,768]{1,0:T(8,128)(2,1)S(1)} %collective-permute-done.15.refs_1_, ...), custom_call_target="tpu_custom_call" | custom-call | flops 1870000000 | bytes 2277376 | tf_op jit(solution)/shard_map/norm_back/pallas_call | solution.py:349
  41.5 2.0 %collective-permute-start.16 = (bf16[192,128]{1,0:T(8,128)(2,1)S(1)}, bf16[192,128]{1,0:T(8,128)(2,1)S(1)}, u32[]{:S(2)}, u32[]{:S(2)}) collective-permute-start(bf16[192,128]{1,0:T(8,128)(2,1)S(1)} %get-tuple-element.68), channel_id=1, source_target_pairs={{0,2},{2,0},{4,6},{6,4},{8,10},{10,8},{12,14},{14,12},{16,18},{18,... | collective-permute-start | bytes 147464 | tf_op jit(solution)/shard_map/ppermute | solution.py:376
  43.5 1.0 %collective-permute-start.17 = (bf16[192,128]{1,0:T(8,128)(2,1)S(1)}, bf16[192,128]{1,0:T(8,128)(2,1)S(1)}, u32[]{:S(2)}, u32[]{:S(2)}) collective-permute-start(bf16[192,128]{1,0:T(8,128)(2,1)S(1)} %get-tuple-element.69), channel_id=1, source_target_pairs={{0,4},{2,6},{4,0},{6,2},{8,12},{10,14},{12,8},{14,10},{16,20},{18,... | collective-permute-start | bytes 147464 | tf_op jit(solution)/shard_map/ppermute | solution.py:376
  44.5 1.2 %collective-permute-done.16.refs_5_ = bf16[192,128]{1,0:T(8,128)(2,1)S(1)} collective-permute-done((bf16[192,128]{1,0:T(8,128)(2,1)S(1)}, bf16[192,128]{1,0:T(8,128)(2,1)S(1)}, u32[]{:S(2)}, u32[]{:S(2)}) %collective-permute-start.16) | collective-permute-done | bytes 49184 | tf_op jit(solution)/shard_map/ppermute | solution.py:376
  45.7 2.3 %collective-permute-start.18 = (bf16[192,128]{1,0:T(8,128)(2,1)S(1)}, bf16[192,128]{1,0:T(8,128)(2,1)S(1)}, u32[]{:S(2)}, u32[]{:S(2)}) collective-permute-start(bf16[192,128]{1,0:T(8,128)(2,1)S(1)} %get-tuple-element.70), channel_id=1, source_target_pairs={{0,6},{2,4},{4,2},{6,0},{8,14},{10,12},{12,10},{14,8},{16,22},{18,... | collective-permute-start | bytes 147464 | tf_op jit(solution)/shard_map/ppermute | solution.py:376
  48.0 1.9 %conv_back.1 = bf16[1,8,16,768]{3,2,1,0:T(8,128)(2,1)} custom-call(f32[6,8,16,128]{3,2,1,0:T(8,128)S(1)} %get-tuple-element.71.grad_ref, f32[6,128,128]{2,1,0:T(8,128)S(1)} %get-tuple-element.67.refs_4_.taps_ref), custom_call_target="tpu_custom_call" | custom-call | flops 110000000 | bytes 983040 | tf_op jit(solution)/shard_map/conv_back/pallas_call | solution.py:349
  49.8 0.0 collective-permute-done.17.refs_6_
  49.9 0.8 %collective-permute-done.18.refs_7_ = bf16[192,128]{1,0:T(8,128)(2,1)S(1)} collective-permute-done((bf16[192,128]{1,0:T(8,128)(2,1)S(1)}, bf16[192,128]{1,0:T(8,128)(2,1)S(1)}, u32[]{:S(2)}, u32[]{:S(2)}) %collective-permute-start.18) | collective-permute-done | bytes 49184 | tf_op jit(solution)/shard_map/ppermute | solution.py:376
  50.6 0.0 collective-permute-done.19.refs_1_
  50.6 0.0 collective-permute-done.20.refs_2_
  50.7 0.0 collective-permute-done.21.refs_3_
  50.7 0.1 plane_sum.1
  50.8 0.5 collective-permute-start.22
  51.3 2.5 %collective-permute-start.23 = (bf16[48,512]{1,0:T(8,128)(2,1)S(1)}, bf16[48,512]{1,0:T(8,128)(2,1)S(1)}, u32[]{:S(2)}, u32[]{:S(2)}) collective-permute-start(bf16[48,512]{1,0:T(8,128)(2,1)S(1)} %get-tuple-element.83), channel_id=1, source_target_pairs={{0,16},{2,18},{4,20},{6,22},{8,24},{10,26},{12,28},{14,30},{16,0},... | collective-permute-start | bytes 147464 | tf_op jit(solution)/shard_map/ppermute | solution.py:376
  53.8 1.4 %collective-permute-start.24 = (bf16[48,512]{1,0:T(8,128)(2,1)S(1)}, bf16[48,512]{1,0:T(8,128)(2,1)S(1)}, u32[]{:S(2)}, u32[]{:S(2)}) collective-permute-start(bf16[48,512]{1,0:T(8,128)(2,1)S(1)} %get-tuple-element.84), channel_id=1, source_target_pairs={{0,24},{2,26},{4,28},{6,30},{8,16},{10,18},{12,20},{14,22},{16,8},... | collective-permute-start | bytes 147464 | tf_op jit(solution)/shard_map/ppermute | solution.py:376
  55.2 0.0 collective-permute-done.22.refs_1_
  55.2 1.0 %collective-permute-done.23.refs_2_ = bf16[48,512]{1,0:T(8,128)(2,1)S(1)} collective-permute-done((bf16[48,512]{1,0:T(8,128)(2,1)S(1)}, bf16[48,512]{1,0:T(8,128)(2,1)S(1)}, u32[]{:S(2)}, u32[]{:S(2)}) %collective-permute-start.23) | collective-permute-done | bytes 49184 | tf_op jit(solution)/shard_map/ppermute | solution.py:376
  56.3 3.4 %collective-permute-done.24.refs_3_ = bf16[48,512]{1,0:T(8,128)(2,1)S(1)} collective-permute-done((bf16[48,512]{1,0:T(8,128)(2,1)S(1)}, bf16[48,512]{1,0:T(8,128)(2,1)S(1)}, u32[]{:S(2)}, u32[]{:S(2)}) %collective-permute-start.24) | collective-permute-done | bytes 49184 | tf_op jit(solution)/shard_map/ppermute | solution.py:376
  59.7 0.1 collective-permute-start.25
  59.8 1.4 %collective-permute-done.25.other_ref = f32[48,896]{1,0:T(8,128)S(1)} collective-permute-done((f32[48,896]{1,0:T(8,128)S(1)}, f32[48,896]{1,0:T(8,128)S(1)}, u32[]{:S(2)}, u32[]{:S(2)}) %collective-permute-start.25) | collective-permute-done | bytes 172064 | tf_op jit(solution)/shard_map/ppermute | solution.py:379
  61.2 0.8 %finish.1 = (f32[48,1536]{1,0:T(8,128)}, f32[48,49]{1,0:T(8,128)}, f32[1,48]{1,0:T(1,128)}, f32[1,48]{1,0:T(1,128)}) custom-call(f32[48,896]{1,0:T(8,128)S(1)} %line_sum.1.mine_ref, f32[48,896]{1,0:T(8,128)S(1)} %collective-permute-done.25.other_ref), custom_call_target="tpu_custom_call" | custom-call | flops 550000000 | bytes 648768 | tf_op jit(solution)/shard_map/finish/pallas_call | solution.py:349
  (7 shorter events, 0.1 us)
Async XLA Ops:
  0.6 8.1 %copy-start = (bf16[1,8,16,768]{3,2,1,0:T(8,128)(2,1)S(1)}, bf16[1,8,16,768]{3,2,1,0:T(8,128)(2,1)}, u32[]{:S(2)}) copy-start(bf16[1,8,16,768]{3,2,1,0:T(8,128)(2,1)} %refs_5_) | copy-start | bytes 589828
  0.6 9.9 %copy-start.1 = (bf16[1,8,16,1536]{3,2,1,0:T(8,128)(2,1)S(1)}, bf16[1,8,16,1536]{3,2,1,0:T(8,128)(2,1)}, u32[]{:S(2)}) copy-start(bf16[1,8,16,1536]{3,2,1,0:T(8,128)(2,1)} %param.7) | copy-start | bytes 1179652
  3.0 7.8 %collective-permute-start.1 = (bf16[48,512]{1,0:T(8,128)(2,1)}, bf16[48,512]{1,0:T(8,128)(2,1)S(1)}, u32[]{:S(2)}, u32[]{:S(2)}) collective-permute-start(bf16[48,512]{1,0:T(8,128)(2,1)} %get-tuple-element.49.refs_0_), channel_id=1, source_target_pairs={{0,16},{2,18},{4,20},{6,22},{8,24},{10,26},{12,28},{14,30},{16,0},... | collective-permute-start | bytes 147464 | tf_op jit(solution)/shard_map/ppermute | solution.py:376
  7.1 6.6 %collective-permute-start.2 = (bf16[48,512]{1,0:T(8,128)(2,1)}, bf16[48,512]{1,0:T(8,128)(2,1)S(1)}, u32[]{:S(2)}, u32[]{:S(2)}) collective-permute-start(bf16[48,512]{1,0:T(8,128)(2,1)} %get-tuple-element.50), channel_id=1, source_target_pairs={{0,24},{2,26},{4,28},{6,30},{8,16},{10,18},{12,20},{14,22},{16,8},... | collective-permute-start | bytes 147464 | tf_op jit(solution)/shard_map/ppermute | solution.py:376
  8.5 5.4 %collective-permute-start = (bf16[48,512]{1,0:T(8,128)(2,1)}, bf16[48,512]{1,0:T(8,128)(2,1)S(1)}, u32[]{:S(2)}, u32[]{:S(2)}) collective-permute-start(bf16[48,512]{1,0:T(8,128)(2,1)} %get-tuple-element.50), channel_id=1, source_target_pairs={{0,8},{2,10},{4,12},{6,14},{8,0},{10,2},{12,4},{14,6},{16,24},{18,... | collective-permute-start | bytes 147464 | tf_op jit(solution)/shard_map/ppermute | solution.py:376
  8.7 14.2 %collective-permute-start.9 = (bf16[1,8,16,768]{3,2,1,0:T(8,128)(2,1)S(1)}, bf16[1,8,16,768]{3,2,1,0:T(8,128)(2,1)S(1)}, u32[]{:S(2)}, u32[]{:S(2)}) collective-permute-start(bf16[1,8,16,768]{3,2,1,0:T(8,128)(2,1)S(1)} %copy-done), channel_id=1, source_target_pairs={{0,8},{2,10},{4,12},{6,14},{8,0},{10,2},{12,4},{14,6},{16,24},{18,... | collective-permute-start | bytes 589832 | tf_op jit(solution)/shard_map/ppermute | solution.py:376
  10.5 3.4 %copy-start.2 = (bf16[48,512]{1,0:T(8,128)(2,1)S(1)}, bf16[48,512]{1,0:T(8,128)(2,1)}, u32[]{:S(2)}) copy-start(bf16[48,512]{1,0:T(8,128)(2,1)} %get-tuple-element.49.refs_0_) | copy-start | bytes 147460
  10.6 15.3 %collective-permute-start.10 = (bf16[128,768]{1,0:T(8,128)(2,1)S(1)}, bf16[128,768]{1,0:T(8,128)(2,1)S(1)}, u32[]{:S(2)}, u32[]{:S(2)}) collective-permute-start(bf16[128,768]{1,0:T(8,128)(2,1)S(1)} %get-tuple-element.56), channel_id=1, source_target_pairs={{0,8},{2,10},{4,12},{6,14},{8,0},{10,2},{12,4},{14,6},{16,24},{18,... | collective-permute-start | bytes 589832 | tf_op jit(solution)/shard_map/ppermute | solution.py:376
  13.9 5.1 %collective-permute-start.8 = (bf16[192,128]{1,0:T(8,128)(2,1)S(1)}, bf16[192,128]{1,0:T(8,128)(2,1)S(1)}, u32[]{:S(2)}, u32[]{:S(2)}) collective-permute-start(bf16[192,128]{1,0:T(8,128)(2,1)S(1)} %get-tuple-element.52.refs_0_), channel_id=1, source_target_pairs={{0,6},{2,4},{4,2},{6,0},{8,14},{10,12},{12,10},{14,8},{16,22},{18,... | collective-permute-start | bytes 147464 | tf_op jit(solution)/shard_map/ppermute | solution.py:376
  16.4 5.3 %collective-permute-start.7 = (bf16[192,128]{1,0:T(8,128)(2,1)S(1)}, bf16[192,128]{1,0:T(8,128)(2,1)S(1)}, u32[]{:S(2)}, u32[]{:S(2)}) collective-permute-start(bf16[192,128]{1,0:T(8,128)(2,1)S(1)} %get-tuple-element.52.refs_0_), channel_id=1, source_target_pairs={{0,4},{2,6},{4,0},{6,2},{8,12},{10,14},{12,8},{14,10},{16,20},{18,... | collective-permute-start | bytes 147464 | tf_op jit(solution)/shard_map/ppermute | solution.py:376
  17.0 5.9 %collective-permute-start.6 = (bf16[192,128]{1,0:T(8,128)(2,1)S(1)}, bf16[192,128]{1,0:T(8,128)(2,1)S(1)}, u32[]{:S(2)}, u32[]{:S(2)}) collective-permute-start(bf16[192,128]{1,0:T(8,128)(2,1)S(1)} %get-tuple-element.52.refs_0_), channel_id=1, source_target_pairs={{0,2},{2,0},{4,6},{6,4},{8,10},{10,8},{12,14},{14,12},{16,18},{18,... | collective-permute-start | bytes 147464 | tf_op jit(solution)/shard_map/ppermute | solution.py:376
  19.0 7.5 %collective-permute-start.5 = (bf16[192,384]{1,0:T(8,128)(2,1)S(1)}, bf16[192,384]{1,0:T(8,128)(2,1)S(1)}, u32[]{:S(2)}, u32[]{:S(2)}) collective-permute-start(bf16[192,384]{1,0:T(8,128)(2,1)S(1)} %get-tuple-element.51.refs_0_), channel_id=1, source_target_pairs={{0,6},{2,4},{4,2},{6,0},{8,14},{10,12},{12,10},{14,8},{16,22},{18,... | collective-permute-start | bytes 442376 | tf_op jit(solution)/shard_map/ppermute | solution.py:376
  21.8 5.1 %collective-permute-start.4 = (bf16[192,384]{1,0:T(8,128)(2,1)S(1)}, bf16[192,384]{1,0:T(8,128)(2,1)S(1)}, u32[]{:S(2)}, u32[]{:S(2)}) collective-permute-start(bf16[192,384]{1,0:T(8,128)(2,1)S(1)} %get-tuple-element.51.refs_0_), channel_id=1, source_target_pairs={{0,4},{2,6},{4,0},{6,2},{8,12},{10,14},{12,8},{14,10},{16,20},{18,... | collective-permute-start | bytes 442376 | tf_op jit(solution)/shard_map/ppermute | solution.py:376
  22.8 5.1 %collective-permute-start.3 = (bf16[192,384]{1,0:T(8,128)(2,1)S(1)}, bf16[192,384]{1,0:T(8,128)(2,1)S(1)}, u32[]{:S(2)}, u32[]{:S(2)}) collective-permute-start(bf16[192,384]{1,0:T(8,128)(2,1)S(1)} %get-tuple-element.51.refs_0_), channel_id=1, source_target_pairs={{0,2},{2,0},{4,6},{6,4},{8,10},{10,8},{12,14},{14,12},{16,18},{18,... | collective-permute-start | bytes 442376 | tf_op jit(solution)/shard_map/ppermute | solution.py:376
  25.9 2.4 %collective-permute-start.11 = (bf16[256,768]{1,0:T(8,128)(2,1)S(1)}, bf16[256,768]{1,0:T(8,128)(2,1)S(1)}, u32[]{:S(2)}, u32[]{:S(2)}) collective-permute-start(bf16[256,768]{1,0:T(8,128)(2,1)S(1)} %get-tuple-element.57.refs_1_), channel_id=1, source_target_pairs={{0,1},{1,0},{2,3},{3,2},{4,5},{5,4},{6,7},{7,6},{8,9},{9,8},{10,11... | collective-permute-start | bytes 1179656 | tf_op jit(solution)/shard_map/ppermute | solution.py:379
  26.0 2.1 %collective-permute-start.12 = (bf16[128,768]{1,0:T(8,128)(2,1)S(1)}, bf16[128,768]{1,0:T(8,128)(2,1)S(1)}, u32[]{:S(2)}, u32[]{:S(2)}) collective-permute-start(bf16[128,768]{1,0:T(8,128)(2,1)S(1)} %get-tuple-element.58), channel_id=1, source_target_pairs={{0,1},{1,0},{2,3},{3,2},{4,5},{5,4},{6,7},{7,6},{8,9},{9,8},{10,11... | collective-permute-start | bytes 589832 | tf_op jit(solution)/shard_map/ppermute | solution.py:379
  26.5 1.8 %collective-permute-start.13 = (bf16[128,768]{1,0:T(8,128)(2,1)S(1)}, bf16[128,768]{1,0:T(8,128)(2,1)S(1)}, u32[]{:S(2)}, u32[]{:S(2)}) collective-permute-start(bf16[128,768]{1,0:T(8,128)(2,1)S(1)} %collective-permute-done.10.refs_5_), channel_id=1, source_target_pairs={{0,1},{1,0},{2,3},{3,2},{4,5},{5,4},{6,7},{7,6},{8,9},{9,8},{10,11... | collective-permute-start | bytes 589832 | tf_op jit(solution)/shard_map/ppermute | solution.py:379
  30.3 2.4 %collective-permute-start.14 = (f32[256,768]{1,0:T(8,128)S(1)}, f32[256,768]{1,0:T(8,128)S(1)}, u32[]{:S(2)}, u32[]{:S(2)}) collective-permute-start(f32[256,768]{1,0:T(8,128)S(1)} %get-tuple-element.62), channel_id=1, source_target_pairs={{0,1},{1,0},{2,3},{3,2},{4,5},{5,4},{6,7},{7,6},{8,9},{9,8},{10,11... | collective-permute-start | bytes 2359304 | tf_op jit(solution)/shard_map/ppermute | solution.py:379
  32.8 7.0 %collective-permute-start.15 = (bf16[128,768]{1,0:T(8,128)(2,1)S(1)}, bf16[128,768]{1,0:T(8,128)(2,1)S(1)}, u32[]{:S(2)}, u32[]{:S(2)}) collective-permute-start(bf16[128,768]{1,0:T(8,128)(2,1)S(1)} %get-tuple-element.64), channel_id=1, source_target_pairs={{0,8},{2,10},{4,12},{6,14},{8,0},{10,2},{12,4},{14,6},{16,24},{18,... | collective-permute-start | bytes 589832 | tf_op jit(solution)/shard_map/ppermute | solution.py:376
  33.3 17.4 %collective-permute-start.19 = (bf16[192,384]{1,0:T(8,128)(2,1)S(1)}, bf16[192,384]{1,0:T(8,128)(2,1)S(1)}, u32[]{:S(2)}, u32[]{:S(2)}) collective-permute-start(bf16[192,384]{1,0:T(8,128)(2,1)S(1)} %get-tuple-element.74), channel_id=1, source_target_pairs={{0,2},{2,0},{4,6},{6,4},{8,10},{10,8},{12,14},{14,12},{16,18},{18,... | collective-permute-start | bytes 442376 | tf_op jit(solution)/shard_map/ppermute | solution.py:376
  34.9 15.8 %collective-permute-start.20 = (bf16[192,384]{1,0:T(8,128)(2,1)S(1)}, bf16[192,384]{1,0:T(8,128)(2,1)S(1)}, u32[]{:S(2)}, u32[]{:S(2)}) collective-permute-start(bf16[192,384]{1,0:T(8,128)(2,1)S(1)} %get-tuple-element.75), channel_id=1, source_target_pairs={{0,4},{2,6},{4,0},{6,2},{8,12},{10,14},{12,8},{14,10},{16,20},{18,... | collective-permute-start | bytes 442376 | tf_op jit(solution)/shard_map/ppermute | solution.py:376
  36.7 13.9 %collective-permute-start.21 = (bf16[192,384]{1,0:T(8,128)(2,1)S(1)}, bf16[192,384]{1,0:T(8,128)(2,1)S(1)}, u32[]{:S(2)}, u32[]{:S(2)}) collective-permute-start(bf16[192,384]{1,0:T(8,128)(2,1)S(1)} %get-tuple-element.76), channel_id=1, source_target_pairs={{0,6},{2,4},{4,2},{6,0},{8,14},{10,12},{12,10},{14,8},{16,22},{18,... | collective-permute-start | bytes 442376 | tf_op jit(solution)/shard_map/ppermute | solution.py:376
  41.5 4.2 %collective-permute-start.16 = (bf16[192,128]{1,0:T(8,128)(2,1)S(1)}, bf16[192,128]{1,0:T(8,128)(2,1)S(1)}, u32[]{:S(2)}, u32[]{:S(2)}) collective-permute-start(bf16[192,128]{1,0:T(8,128)(2,1)S(1)} %get-tuple-element.68), channel_id=1, source_target_pairs={{0,2},{2,0},{4,6},{6,4},{8,10},{10,8},{12,14},{14,12},{16,18},{18,... | collective-permute-start | bytes 147464 | tf_op jit(solution)/shard_map/ppermute | solution.py:376
  43.5 6.3 %collective-permute-start.17 = (bf16[192,128]{1,0:T(8,128)(2,1)S(1)}, bf16[192,128]{1,0:T(8,128)(2,1)S(1)}, u32[]{:S(2)}, u32[]{:S(2)}) collective-permute-start(bf16[192,128]{1,0:T(8,128)(2,1)S(1)} %get-tuple-element.69), channel_id=1, source_target_pairs={{0,4},{2,6},{4,0},{6,2},{8,12},{10,14},{12,8},{14,10},{16,20},{18,... | collective-permute-start | bytes 147464 | tf_op jit(solution)/shard_map/ppermute | solution.py:376
  45.7 5.0 %collective-permute-start.18 = (bf16[192,128]{1,0:T(8,128)(2,1)S(1)}, bf16[192,128]{1,0:T(8,128)(2,1)S(1)}, u32[]{:S(2)}, u32[]{:S(2)}) collective-permute-start(bf16[192,128]{1,0:T(8,128)(2,1)S(1)} %get-tuple-element.70), channel_id=1, source_target_pairs={{0,6},{2,4},{4,2},{6,0},{8,14},{10,12},{12,10},{14,8},{16,22},{18,... | collective-permute-start | bytes 147464 | tf_op jit(solution)/shard_map/ppermute | solution.py:376
  50.8 4.5 %collective-permute-start.22 = (bf16[48,512]{1,0:T(8,128)(2,1)S(1)}, bf16[48,512]{1,0:T(8,128)(2,1)S(1)}, u32[]{:S(2)}, u32[]{:S(2)}) collective-permute-start(bf16[48,512]{1,0:T(8,128)(2,1)S(1)} %get-tuple-element.82), channel_id=1, source_target_pairs={{0,8},{2,10},{4,12},{6,14},{8,0},{10,2},{12,4},{14,6},{16,24},{18,... | collective-permute-start | bytes 147464 | tf_op jit(solution)/shard_map/ppermute | solution.py:376
  51.3 5.0 %collective-permute-start.23 = (bf16[48,512]{1,0:T(8,128)(2,1)S(1)}, bf16[48,512]{1,0:T(8,128)(2,1)S(1)}, u32[]{:S(2)}, u32[]{:S(2)}) collective-permute-start(bf16[48,512]{1,0:T(8,128)(2,1)S(1)} %get-tuple-element.83), channel_id=1, source_target_pairs={{0,16},{2,18},{4,20},{6,22},{8,24},{10,26},{12,28},{14,30},{16,0},... | collective-permute-start | bytes 147464 | tf_op jit(solution)/shard_map/ppermute | solution.py:376
  53.8 5.9 %collective-permute-start.24 = (bf16[48,512]{1,0:T(8,128)(2,1)S(1)}, bf16[48,512]{1,0:T(8,128)(2,1)S(1)}, u32[]{:S(2)}, u32[]{:S(2)}) collective-permute-start(bf16[48,512]{1,0:T(8,128)(2,1)S(1)} %get-tuple-element.84), channel_id=1, source_target_pairs={{0,24},{2,26},{4,28},{6,30},{8,16},{10,18},{12,20},{14,22},{16,8},... | collective-permute-start | bytes 147464 | tf_op jit(solution)/shard_map/ppermute | solution.py:376
  59.7 1.5 %collective-permute-start.25 = (f32[48,896]{1,0:T(8,128)S(1)}, f32[48,896]{1,0:T(8,128)S(1)}, u32[]{:S(2)}, u32[]{:S(2)}) collective-permute-start(f32[48,896]{1,0:T(8,128)S(1)} %line_sum.1.mine_ref), channel_id=1, source_target_pairs={{0,1},{1,0},{2,3},{3,2},{4,5},{5,4},{6,7},{7,6},{8,9},{9,8},{10,11... | collective-permute-start | bytes 516104 | tf_op jit(solution)/shard_map/ppermute | solution.py:379

commit v7 on v6

--- a/solution.py
+++ b/solution.py
@@ -78,23 +78,15 @@
     return sums
 
 
-def pack_kernel(w_hbm, dw_hbm, gain_ref, bias_ref, near_ref, far_ref, w_ref, dw_ref, turned, wide, sems):
+def pack_kernel(w_ref, dw_ref, gain_ref, bias_ref, near_ref, far_ref, turned, wide):
     own, hidden = w_ref.shape
     quarter = hidden // 4
     side = lax.axis_index("rep") % 2
     parity = (lax.axis_index("shard") // INNER) % 2
-    copies = [
-        pltpu.make_async_copy(w_hbm, w_ref, sems.at[0]),
-        pltpu.make_async_copy(dw_hbm, dw_ref, sems.at[1]),
-    ]
-    for copy in copies:
-        copy.start()
     turned[...] = jnp.zeros_like(turned)
     turned[TAPS : TAPS + 1, :own] = gain_ref[...].astype(F32)
     turned[TAPS + 1 : TAPS + 2, :own] = bias_ref[...].astype(F32)
     wide[...] = jnp.zeros_like(wide)
-    for copy in copies:
-        copy.wait()
     wide[:, :TAPS] = dw_ref[...].astype(F32)
     extras = (wide[...] + turned[...].T[:own]).astype(BF16)
     for ref, which in ((near_ref, parity), (far_ref, 1 - parity)):
@@ -197,18 +189,15 @@
             squares = centered * centered if squares is None else squares + centered * centered
         variance = jnp.sum(squares, axis=-1, keepdims=True) / depth
         inv_std = lax.rsqrt(variance + NORM_EPS)
-        if image == 0:
-            inv_ref[...] = jnp.broadcast_to(inv_std, (pixels, LANES))
+        rows = slice(image * pixels, (image + 1) * pixels)
+        inv_ref[rows, :] = jnp.broadcast_to(inv_std, (pixels, LANES))
         for tile in range(tiles):
             lanes = slice(tile * LANES, (tile + 1) * LANES)
             whitened = (conv[tile] - average) * inv_std
-            if image == 0:
-                white_ref[:, lanes] = whitened
+            white_ref[rows, lanes] = whitened
             gain = taps_ref[tile, TAPS : TAPS + 1, :]
             bias = taps_ref[tile, TAPS + 1 : TAPS + 2, :]
-            normed_ref[image * pixels : (image + 1) * pixels, lanes] = (
-                whitened * gain + bias
-            ).astype(BF16)
+            normed_ref[rows, lanes] = (whitened * gain + bias).astype(BF16)
 
 
 def cot_pack_kernel(cot_ref, across_ref, sibling_ref):
@@ -263,55 +252,60 @@
     other_ref[...] = grad_normed[rows:]
 
 
-def core_sum_kernel(own_ref, other_ref, kept_ref, sent_ref):
-    pixels = kept_ref.shape[0]
-    kept_ref[...] = own_ref[:pixels] + other_ref[:pixels]
-    sent_ref[...] = (own_ref[pixels:] + other_ref[pixels:]).astype(BF16)
-
-
 def norm_back_kernel(relative, own, *refs):
-    gn_own, gn_other, white_ref, inv_ref, taps_ref, x_ref = refs[:6]
-    pieces = refs[6 : 6 + INNER]
-    grad_ref, padded, rows, small = refs[6 + INNER :]
+    gn_own, gn_other, white_ref, inv_ref, taps_ref, x_ref, far_ref = refs[:7]
+    pieces = refs[7 : 7 + INNER]
+    grad_ref, sent_ref, padded, grads_ref, rows, small = refs[7 + INNER :]
     height, breadth, depth = x_ref.shape[1:]
     tiles = depth // LANES
     pixels = height * breadth
     padded[...] = jnp.zeros_like(padded)
     rows[...] = jnp.zeros_like(rows)
-    first = None
-    second = None
-    for tile in range(tiles):
-        lanes = slice(tile * LANES, (tile + 1) * LANES)
-        padded[tile, :, 8 : 8 + breadth, :] = x_ref[0, :, :, lanes].astype(F32)
-        grad_normed = gn_own[:, lanes] + gn_other[:, lanes].astype(F32)
-        whitened = white_ref[:, lanes]
-        product = grad_normed * whitened
-        gain = taps_ref[tile, TAPS : TAPS + 1, :]
-        rows[tile, TAPS : TAPS + 1, :] = jnp.sum(product, axis=0, keepdims=True)
-        rows[tile, TAPS + 1 : TAPS + 2, :] = jnp.sum(grad_normed, axis=0, keepdims=True)
-        one, two = grad_normed * gain, product * gain
-        first = one if first is None else first + one
-        second = two if second is None else second + two
-    mean_first = jnp.sum(first, axis=-1, keepdims=True) / depth
-    mean_second = jnp.sum(second, axis=-1, keepdims=True) / depth
-    for tile in range(tiles):
-        lanes = slice(tile * LANES, (tile + 1) * LANES)
-        gain = taps_ref[tile, TAPS : TAPS + 1, :]
-        grad_white = (gn_own[:, lanes] + gn_other[:, lanes].astype(F32)) * gain
-        grad_conv = inv_ref[...] * (grad_white - mean_first - white_ref[:, lanes] * mean_second)
-        grad_ref[tile] = grad_conv.reshape(height, breadth, LANES)
+    for image, source in enumerate((x_ref, far_ref)):
+        span = slice(image * pixels, (image + 1) * pixels)
+        first = None
+        second = None
+        for tile in range(tiles):
+            lanes = slice(tile * LANES, (tile + 1) * LANES)
+            padded[image, tile, :, 8 : 8 + breadth, :] = source[0, :, :, lanes].astype(F32)
+            grad_normed = gn_own[span, lanes] + gn_other[span, lanes]
+            whitened = white_ref[span, lanes]
+            product = grad_normed * whitened
+            gain = taps_ref[tile, TAPS : TAPS + 1, :]
+            rows[tile, TAPS : TAPS + 1, :] += jnp.sum(product, axis=0, keepdims=True)
+            rows[tile, TAPS + 1 : TAPS + 2, :] += jnp.sum(grad_normed, axis=0, keepdims=True)
+            one, two = grad_normed * gain, product * gain
+            first = one if first is None else first + one
+            second = two if second is None else second + two
+        mean_first = jnp.sum(first, axis=-1, keepdims=True) / depth
+        mean_second = jnp.sum(second, axis=-1, keepdims=True) / depth
+        for tile in range(tiles):
+            lanes = slice(tile * LANES, (tile + 1) * LANES)
+            gain = taps_ref[tile, TAPS : TAPS + 1, :]
+            grad_white = (gn_own[span, lanes] + gn_other[span, lanes]) * gain
+            grad_conv = inv_ref[span, :] * (
+                grad_white - mean_first - white_ref[span, lanes] * mean_second
+            )
+            grad_conv = grad_conv.reshape(height, breadth, LANES)
+            grads_ref[image, tile] = grad_conv
+            if image == 0:
+                grad_ref[tile] = grad_conv
+            else:
+                sent_ref[tile] = grad_conv.astype(BF16)
 
     def one_tile(tile, carry):
-        grads = [grad_ref[tile, line] for line in range(height)]
+        grads = [[grads_ref[image, tile, line] for line in range(height)] for image in range(2)]
         for across in range(KS):
-            shifted = padded[tile, :, 8 - MARGIN + across : 8 - MARGIN + across + breadth, :]
+            columns = slice(8 - MARGIN + across, 8 - MARGIN + across + breadth)
+            shifted = [padded[image, tile, :, columns, :] for image in range(2)]
             for down in range(KS):
                 total = None
-                for line in range(height):
-                    origin = line + down - MARGIN
-                    if 0 <= origin < height:
-                        term = grads[line] * shifted[origin]
-                        total = term if total is None else total + term
+                for image in range(2):
+                    for line in range(height):
+                        origin = line + down - MARGIN
+                        if 0 <= origin < height:
+                            term = grads[image][line] * shifted[image][origin]
+                            total = term if total is None else total + term
                 rows[tile, pl.ds(down * KS + across, 1), :] = jnp.sum(total, axis=0, keepdims=True)
         return carry
 
@@ -321,10 +315,10 @@
     split_rows(small, pieces, own, relative)
 
 
-def conv_back_kernel(grad_ref, taps_ref, out_ref, padded):
+def conv_back_kernel(grad_ref, other_ref, taps_ref, out_ref, padded):
     tiles, height, breadth, _ = grad_ref.shape
     padded[...] = jnp.zeros_like(padded)
-    padded[:, :, 8 : 8 + breadth, :] = grad_ref[...]
+    padded[:, :, 8 : 8 + breadth, :] = grad_ref[...] + other_ref[...].astype(F32)
 
     def one_tile(tile, carry):
         sums = correlate(
@@ -342,14 +336,14 @@
     lax.fori_loop(0, tiles, one_tile, 0)
 
 
-def call(kernel, name, outs, scratch, micros, *args, in_specs=None, mebibytes=48):
+def call(kernel, name, outs, scratch, micros, *args, mebibytes=48):
     flops = int(micros * 1.1e9)
     moved = sum(math.prod(a.shape) * a.dtype.itemsize for a in args)
     moved += sum(math.prod(o.shape) * o.dtype.itemsize for o in outs)
     return pl.pallas_call(
         kernel,
         out_shape=outs,
-        in_specs=in_specs or [VMEM] * len(args),
+        in_specs=[VMEM] * len(args),
         out_specs=[VMEM] * len(outs),
         scratch_shapes=scratch,
         compiler_params=params(mebibytes),
@@ -400,18 +394,14 @@
         "pack",
         [shape((own, quarter + LANES), BF16)] * 2,
         [
-            pltpu.VMEM(up_weight.shape, BF16),
-            pltpu.VMEM(depthwise_weight.shape, BF16),
             pltpu.VMEM((LANES, LANES), F32),
             pltpu.VMEM((own, LANES), F32),
-            pltpu.SemaphoreType.DMA((2,)),
         ],
         0.5,
         up_weight,
         depthwise_weight,
         norm_gain[None, :],
         norm_bias[None, :],
-        in_specs=[pl.BlockSpec(memory_space=pltpu.HBM)] * 2 + [VMEM] * 2,
         mebibytes=63,
     )
     near, far, images, cotangent = lax.optimization_barrier((near, far, images, cotangent))
@@ -457,8 +447,8 @@
         "conv_norm",
         [
             shape((2 * pixels, depth), BF16),
-            shape((pixels, depth), F32),
-            shape((pixels, LANES), F32),
+            shape((2 * pixels, depth), F32),
+            shape((2 * pixels, LANES), F32),
             shape((tiles, LANES, LANES), F32),
         ],
         [
@@ -502,50 +492,46 @@
         weight,
         grad_pre,
     )
-    gn_kept, gn_sent = call(
-        core_sum_kernel,
-        "core_sum",
-        [shape((pixels, depth), F32), shape((pixels, depth), BF16)],
-        [],
-        0.4,
-        gn_kept,
-        over_core(gn_sent),
-    )
     pieces = relative_order(pieces)
-    gn_other = over_shard(gn_sent, INNER)
     arrived = [over_shard(piece, flip) for flip, piece in enumerate(pieces) if flip]
-    *small, grad_conv = call(
+    *small, grad_conv, grad_sent = call(
         functools.partial(norm_back_kernel, relative, own),
         "norm_back",
         [shape((rows, LANES), F32)]
         + [shape((rows, LANES), BF16)] * (INNER - 1)
-        + [shape((tiles, height, breadth, LANES), F32)],
+        + [
+            shape((tiles, height, breadth, LANES), F32),
+            shape((tiles, height, breadth, LANES), BF16),
+        ],
         [
-            padded,
+            pltpu.VMEM((2, tiles, height, breadth + 16, LANES), F32),
+            pltpu.VMEM((2, tiles, height, breadth, LANES), F32),
             pltpu.VMEM((tiles, LANES, LANES), F32),
             pltpu.VMEM((depth, LANES), F32),
         ],
-        1.7,
+        0.1,
         gn_kept,
-        gn_other,
+        over_core(gn_sent),
         whitened,
         inv_std,
         taps,
         images,
+        images_far,
     )
     small = relative_order(small)
     small_arrived = [over_shard(piece, flip) for flip, piece in enumerate(small) if flip]
+    grad_other = over_shard(grad_sent, INNER)
     (grad_images,) = call(
         conv_back_kernel,
         "conv_back",
         [shape(images.shape, BF16)],
         [padded],
-        0.1,
+        1.9,
         grad_conv,
+        grad_other,
         taps,
     )
 
-    *small_arrived, grad_images = lax.optimization_barrier((*small_arrived, grad_images))
     home, *sent = call(
         functools.partial(plane_sum_kernel, lines),
         "plane_sum",
@@ -557,6 +543,7 @@
         small[0],
         *small_arrived,
     )
+    home, grad_images = lax.optimization_barrier((home, grad_images))
     came = [over_shard(piece, INNER * line) for line, piece in enumerate(sent, 1)]
     (total,) = call(
         line_sum_kernel,

time: 62.1 us -> 57 us (0.918)
  waiting for transfers between devices: 19.4 us -> 14.2 us
    ppermute x21, waiting for transfers between devices: 15.7 us -> 12.6 us  [over_shard(): return lax.ppermute(array, 'shard', [(i, i ^ flip) for i in range(shards)])]
    ppermute x5, waiting for transfers between devices: 3.7 us -> 1.56 us  [over_core(): return lax.ppermute(array, 'rep', [(i, i ^ 1) for i in range(reps)])]
    pallas_call x13 -> x12, Pallas kernels: 12 us -> 12.6 us  [call(): pl.pallas_call(kernel, out_shape=outs, in_specs=[VMEM] * len(args), out_s...]
  transfers between devices with their start and end apart: 26 -> 26, of which waited for: 14 -> 13; matrix products, arithmetic and copies ran while one was open for 0% -> 0% of each run, Pallas kernels for 11% -> 14%
where the time goes in v7:
time: 57 us; the launch traced here: 56.9 us
  starting transfers between devices  29.3 us (51%)
  waiting for transfers between devices  14.2 us (25%)
  Pallas kernels  12.6 us (22%)
  between operations  0.76 us (1%)
    ppermute x21, starting transfers between devices, over_shard(): return lax.ppermute(array, 'shard', [(i, i ^ flip) for i in range(shards)])  28.4 us
    pallas_call x12, Pallas kernels, call(): pl.pallas_call(kernel, out_shape=outs, in_specs=[VMEM] * len(args), out_s...  12.6 us
    ppermute x21, waiting for transfers between devices, over_shard(): return lax.ppermute(array, 'shard', [(i, i ^ flip) for i in range(shards)])  12.6 us
    ppermute x5, waiting for transfers between devices, over_core(): return lax.ppermute(array, 'rep', [(i, i ^ 1) for i in range(reps)])  1.56 us
  transfers between devices with their start and end apart: 26, of which 13 were waited for; matrix products, arithmetic and copies ran while one was open for 0% of the time, Pallas kernels for 14%

profile of v7, /device:TPU:0, one launch (start us, length us, event | category | flops | bytes accessed | tf_op | source)
XLA Modules:
  0.0 56.9 jit_solution(15599237738519460677)
XLA Ops:
  0.6 0.0 copy-start
  0.6 0.0 copy-start.1
  0.7 1.7 %pack.1 = (bf16[48,512]{1,0:T(8,128)(2,1)}, bf16[48,512]{1,0:T(8,128)(2,1)}) custom-call(bf16[48,1536]{1,0:T(8,128)(2,1)} %w_ref.1, bf16[48,49]{1,0:T(8,128)(2,1)} %dw_ref.1, bf16[1,48]{1,0:T(2,128)(2,1)} %bitcast.7, bf16[1,48]{1,0:T(2,128)(2,1)} %bitcast.8), custom_call_target="tpu_custom_call" | custom-call | flops 550000000 | bytes 250656 | tf_op jit(solution)/shard_map/pack/pallas_call | solution.py:343
  2.4 4.0 %collective-permute-start.1 = (bf16[48,512]{1,0:T(8,128)(2,1)}, bf16[48,512]{1,0:T(8,128)(2,1)S(1)}, u32[]{:S(2)}, u32[]{:S(2)}) collective-permute-start(bf16[48,512]{1,0:T(8,128)(2,1)} %get-tuple-element.46.refs_0_), channel_id=1, source_target_pairs={{0,16},{2,18},{4,20},{6,22},{8,24},{10,26},{12,28},{14,30},{16,0},... | collective-permute-start | bytes 147464 | tf_op jit(solution)/shard_map/ppermute | solution.py:370
  6.4 1.3 %collective-permute-start.2 = (bf16[48,512]{1,0:T(8,128)(2,1)}, bf16[48,512]{1,0:T(8,128)(2,1)S(1)}, u32[]{:S(2)}, u32[]{:S(2)}) collective-permute-start(bf16[48,512]{1,0:T(8,128)(2,1)} %get-tuple-element.47), channel_id=1, source_target_pairs={{0,24},{2,26},{4,28},{6,30},{8,16},{10,18},{12,20},{14,22},{16,8},... | collective-permute-start | bytes 147464 | tf_op jit(solution)/shard_map/ppermute | solution.py:370
  7.8 0.2 collective-permute-start
  8.0 0.0 copy-done
  8.0 1.8 %collective-permute-start.9 = (bf16[1,8,16,768]{3,2,1,0:T(8,128)(2,1)S(1)}, bf16[1,8,16,768]{3,2,1,0:T(8,128)(2,1)S(1)}, u32[]{:S(2)}, u32[]{:S(2)}) collective-permute-start(bf16[1,8,16,768]{3,2,1,0:T(8,128)(2,1)S(1)} %copy-done), channel_id=1, source_target_pairs={{0,8},{2,10},{4,12},{6,14},{8,0},{10,2},{12,4},{14,6},{16,24},{18,... | collective-permute-start | bytes 589832 | tf_op jit(solution)/shard_map/ppermute | solution.py:370
  9.8 0.3 collective-permute-start.10
  10.1 0.0 collective-permute-done.1.refs_2_
  10.1 2.9 %collective-permute-done.2.refs_3_ = bf16[48,512]{1,0:T(8,128)(2,1)S(1)} collective-permute-done((bf16[48,512]{1,0:T(8,128)(2,1)}, bf16[48,512]{1,0:T(8,128)(2,1)S(1)}, u32[]{:S(2)}, u32[]{:S(2)}) %collective-permute-start.2) | collective-permute-done | bytes 49184 | tf_op jit(solution)/shard_map/ppermute | solution.py:370
  13.0 0.1 collective-permute-done.refs_1_
  13.2 2.5 %collective-permute-start.8 = (bf16[192,128]{1,0:T(8,128)(2,1)S(1)}, bf16[192,128]{1,0:T(8,128)(2,1)S(1)}, u32[]{:S(2)}, u32[]{:S(2)}) collective-permute-start(bf16[192,128]{1,0:T(8,128)(2,1)S(1)} %get-tuple-element.49.refs_0_), channel_id=1, source_target_pairs={{0,6},{2,4},{4,2},{6,0},{8,14},{10,12},{12,10},{14,8},{16,22},{18,... | collective-permute-start | bytes 147464 | tf_op jit(solution)/shard_map/ppermute | solution.py:370
  15.7 0.5 collective-permute-start.7
  16.2 0.5 collective-permute-start.6
  16.8 1.5 %collective-permute-done.8.refs_3_ = bf16[192,128]{1,0:T(8,128)(2,1)S(1)} collective-permute-done((bf16[192,128]{1,0:T(8,128)(2,1)S(1)}, bf16[192,128]{1,0:T(8,128)(2,1)S(1)}, u32[]{:S(2)}, u32[]{:S(2)}) %collective-permute-start.8) | collective-permute-done | bytes 49184 | tf_op jit(solution)/shard_map/ppermute | solution.py:370
  18.3 2.6 %collective-permute-start.5 = (bf16[192,384]{1,0:T(8,128)(2,1)S(1)}, bf16[192,384]{1,0:T(8,128)(2,1)S(1)}, u32[]{:S(2)}, u32[]{:S(2)}) collective-permute-start(bf16[192,384]{1,0:T(8,128)(2,1)S(1)} %get-tuple-element.48.refs_0_), channel_id=1, source_target_pairs={{0,6},{2,4},{4,2},{6,0},{8,14},{10,12},{12,10},{14,8},{16,22},{18,... | collective-permute-start | bytes 442376 | tf_op jit(solution)/shard_map/ppermute | solution.py:370
  20.8 0.2 collective-permute-done.7.refs_2_
  21.0 1.1 %collective-permute-start.4 = (bf16[192,384]{1,0:T(8,128)(2,1)S(1)}, bf16[192,384]{1,0:T(8,128)(2,1)S(1)}, u32[]{:S(2)}, u32[]{:S(2)}) collective-permute-start(bf16[192,384]{1,0:T(8,128)(2,1)S(1)} %get-tuple-element.48.refs_0_), channel_id=1, source_target_pairs={{0,4},{2,6},{4,0},{6,2},{8,12},{10,14},{12,8},{14,10},{16,20},{18,... | collective-permute-start | bytes 442376 | tf_op jit(solution)/shard_map/ppermute | solution.py:370
  22.1 0.0 collective-permute-done.6.refs_1_
  22.1 0.1 collective-permute-start.3
  22.2 0.0 collective-permute-done.9.refs_5_.refs_6_
  22.2 2.9 %conv_norm.1 = (bf16[256,768]{1,0:T(8,128)(2,1)S(1)}, f32[256,768]{1,0:T(8,128)S(1)}, f32[256,128]{1,0:T(8,128)S(1)}, f32[6,128,128]{2,1,0:T(8,128)S(1)}) custom-call(bf16[192,128]{1,0:T(8,128)(2,1)S(1)} %get-tuple-element.49.refs_0_, bf16[192,128]{1,0:T(8,128)(2,1)S(1)} %collective-permute-done.6.refs_1_, ...), custom_call_target="tpu_custom_call" | custom-call | flops 110000000 | bytes 2293760 | tf_op jit(solution)/shard_map/conv_norm/pallas_call | solution.py:343
  25.1 0.0 collective-permute-done.10.refs_5_
  25.1 0.1 collective-permute-start.11
  25.2 0.5 collective-permute-start.12
  25.7 0.0 collective-permute-done.5.refs_3_
  25.7 0.1 collective-permute-start.13
  25.8 0.4 collective-permute-done.4.refs_2_
  26.2 1.1 %collective-permute-done.3.refs_1_ = bf16[192,384]{1,0:T(8,128)(2,1)S(1)} collective-permute-done((bf16[192,384]{1,0:T(8,128)(2,1)S(1)}, bf16[192,384]{1,0:T(8,128)(2,1)S(1)}, u32[]{:S(2)}, u32[]{:S(2)}) %collective-permute-start.3) | collective-permute-done | bytes 147488 | tf_op jit(solution)/shard_map/ppermute | solution.py:370
  27.3 0.1 order.1.refs_0_.weight
  27.3 0.0 collective-permute-done.12.refs_4_
  27.3 0.2 collective-permute-done.13.refs_6_
  27.5 0.0 collective-permute-done.11.refs_2_
  27.5 1.5 %project.1 = (f32[192,384]{1,0:T(8,128)S(1)}, bf16[192,384]{1,0:T(8,128)(2,1)S(1)}, bf16[192,384]{1,0:T(8,128)(2,1)S(1)}, bf16[192,384]{1,0:T(8,128)(2,1)S(1)}, bf16[512,384]{1,0:T(8,128)(2,1)S(1)}) custom-call(bf16[768,384]{1,0:T(8,128)(2,1)S(1)} %order.1.refs_0_.weight, bf16[256,768]{1,0:T(8,128)(2,1)S(1)} %get-tuple-element.54.refs_1_, ...), custom_call_target="tpu_custom_call" | custom-call | flops 1760000000 | bytes 3489792 | tf_op jit(solution)/shard_map/project/pallas_call | solution.py:343
  29.0 0.6 %back_project.1 = (f32[256,768]{1,0:T(8,128)S(1)}, f32[256,768]{1,0:T(8,128)S(1)}) custom-call(bf16[768,384]{1,0:T(8,128)(2,1)S(1)} %order.1.refs_0_.weight, bf16[512,384]{1,0:T(8,128)(2,1)S(1)} %get-tuple-element.61.gp_ref), custom_call_target="tpu_custom_call" | custom-call | flops 770000000 | bytes 2555904 | tf_op jit(solution)/shard_map/back_project/pallas_call | solution.py:343
  29.6 0.2 collective-permute-start.17
  29.8 2.0 %collective-permute-start.14 = (bf16[192,384]{1,0:T(8,128)(2,1)S(1)}, bf16[192,384]{1,0:T(8,128)(2,1)S(1)}, u32[]{:S(2)}, u32[]{:S(2)}) collective-permute-start(bf16[192,384]{1,0:T(8,128)(2,1)S(1)} %get-tuple-element.58), channel_id=1, source_target_pairs={{0,2},{2,0},{4,6},{6,4},{8,10},{10,8},{12,14},{14,12},{16,18},{18,... | collective-permute-start | bytes 442376 | tf_op jit(solution)/shard_map/ppermute | solution.py:370
  31.8 1.0 %collective-permute-start.15 = (bf16[192,384]{1,0:T(8,128)(2,1)S(1)}, bf16[192,384]{1,0:T(8,128)(2,1)S(1)}, u32[]{:S(2)}, u32[]{:S(2)}) collective-permute-start(bf16[192,384]{1,0:T(8,128)(2,1)S(1)} %get-tuple-element.59), channel_id=1, source_target_pairs={{0,4},{2,6},{4,0},{6,2},{8,12},{10,14},{12,8},{14,10},{16,20},{18,... | collective-permute-start | bytes 442376 | tf_op jit(solution)/shard_map/ppermute | solution.py:370
  32.7 0.0 collective-permute-done.17.refs_1_
  32.7 3.0 %norm_back.1 = (f32[192,128]{1,0:T(8,128)S(1)}, bf16[192,128]{1,0:T(8,128)(2,1)S(1)}, bf16[192,128]{1,0:T(8,128)(2,1)S(1)}, bf16[192,128]{1,0:T(8,128)(2,1)S(1)}...) custom-call(f32[256,768]{1,0:T(8,128)S(1)} %get-tuple-element.62.refs_0_, ...), custom_call_target="tpu_custom_call" | custom-call | flops 110000000 | bytes 4112384 | tf_op jit(solution)/shard_map/norm_back/pallas_call | solution.py:343
  35.8 1.0 %collective-permute-start.21 = (bf16[6,8,16,128]{3,2,1,0:T(8,128)(2,1)S(1)}, bf16[6,8,16,128]{3,2,1,0:T(8,128)(2,1)S(1)}, u32[]{:S(2)}, u32[]{:S(2)}) collective-permute-start(bf16[6,8,16,128]{3,2,1,0:T(8,128)(2,1)S(1)} %get-tuple-element.73), channel_id=1, source_target_pairs={{0,8},{2,10},{4,12},{6,14},{8,0},{10,2},{12,4},{14,6},{16,24},{18,... | collective-permute-start | bytes 589832 | tf_op jit(solution)/shard_map/ppermute | solution.py:370
  36.8 1.6 %collective-permute-start.16 = (bf16[192,384]{1,0:T(8,128)(2,1)S(1)}, bf16[192,384]{1,0:T(8,128)(2,1)S(1)}, u32[]{:S(2)}, u32[]{:S(2)}) collective-permute-start(bf16[192,384]{1,0:T(8,128)(2,1)S(1)} %get-tuple-element.60), channel_id=1, source_target_pairs={{0,6},{2,4},{4,2},{6,0},{8,14},{10,12},{12,10},{14,8},{16,22},{18,... | collective-permute-start | bytes 442376 | tf_op jit(solution)/shard_map/ppermute | solution.py:370
  38.3 0.3 collective-permute-start.18
  38.6 0.0 collective-permute-done.14.refs_1_
  38.7 1.6 %collective-permute-start.19 = (bf16[192,128]{1,0:T(8,128)(2,1)S(1)}, bf16[192,128]{1,0:T(8,128)(2,1)S(1)}, u32[]{:S(2)}, u32[]{:S(2)}) collective-permute-start(bf16[192,128]{1,0:T(8,128)(2,1)S(1)} %get-tuple-element.69), channel_id=1, source_target_pairs={{0,4},{2,6},{4,0},{6,2},{8,12},{10,14},{12,8},{14,10},{16,20},{18,... | collective-permute-start | bytes 147464 | tf_op jit(solution)/shard_map/ppermute | solution.py:370
  40.3 0.0 collective-permute-done.15.refs_2_
  40.3 1.6 %collective-permute-start.20 = (bf16[192,128]{1,0:T(8,128)(2,1)S(1)}, bf16[192,128]{1,0:T(8,128)(2,1)S(1)}, u32[]{:S(2)}, u32[]{:S(2)}) collective-permute-start(bf16[192,128]{1,0:T(8,128)(2,1)S(1)} %get-tuple-element.70), channel_id=1, source_target_pairs={{0,6},{2,4},{4,2},{6,0},{8,14},{10,12},{12,10},{14,8},{16,22},{18,... | collective-permute-start | bytes 147464 | tf_op jit(solution)/shard_map/ppermute | solution.py:370
  41.8 2.2 %collective-permute-done.16.refs_3_ = bf16[192,384]{1,0:T(8,128)(2,1)S(1)} collective-permute-done((bf16[192,384]{1,0:T(8,128)(2,1)S(1)}, bf16[192,384]{1,0:T(8,128)(2,1)S(1)}, u32[]{:S(2)}, u32[]{:S(2)}) %collective-permute-start.16) | collective-permute-done | bytes 147488 | tf_op jit(solution)/shard_map/ppermute | solution.py:370
  44.1 0.0 collective-permute-done.18.refs_5_
  44.1 0.4 collective-permute-done.19.refs_6_
  44.5 0.7 %collective-permute-done.20.refs_7_ = bf16[192,128]{1,0:T(8,128)(2,1)S(1)} collective-permute-done((bf16[192,128]{1,0:T(8,128)(2,1)S(1)}, bf16[192,128]{1,0:T(8,128)(2,1)S(1)}, u32[]{:S(2)}, u32[]{:S(2)}) %collective-permute-start.20) | collective-permute-done | bytes 49184 | tf_op jit(solution)/shard_map/ppermute | solution.py:370
  45.3 0.1 plane_sum.1
  45.4 1.2 %collective-permute-start.22 = (bf16[48,512]{1,0:T(8,128)(2,1)S(1)}, bf16[48,512]{1,0:T(8,128)(2,1)S(1)}, u32[]{:S(2)}, u32[]{:S(2)}) collective-permute-start(bf16[48,512]{1,0:T(8,128)(2,1)S(1)} %get-tuple-element.76), channel_id=1, source_target_pairs={{0,8},{2,10},{4,12},{6,14},{8,0},{10,2},{12,4},{14,6},{16,24},{18,... | collective-permute-start | bytes 147464 | tf_op jit(solution)/shard_map/ppermute | solution.py:370
  46.5 2.2 %collective-permute-start.23 = (bf16[48,512]{1,0:T(8,128)(2,1)S(1)}, bf16[48,512]{1,0:T(8,128)(2,1)S(1)}, u32[]{:S(2)}, u32[]{:S(2)}) collective-permute-start(bf16[48,512]{1,0:T(8,128)(2,1)S(1)} %get-tuple-element.77), channel_id=1, source_target_pairs={{0,16},{2,18},{4,20},{6,22},{8,24},{10,26},{12,28},{14,30},{16,0},... | collective-permute-start | bytes 147464 | tf_op jit(solution)/shard_map/ppermute | solution.py:370
  48.7 1.1 %collective-permute-start.24 = (bf16[48,512]{1,0:T(8,128)(2,1)S(1)}, bf16[48,512]{1,0:T(8,128)(2,1)S(1)}, u32[]{:S(2)}, u32[]{:S(2)}) collective-permute-start(bf16[48,512]{1,0:T(8,128)(2,1)S(1)} %get-tuple-element.78), channel_id=1, source_target_pairs={{0,24},{2,26},{4,28},{6,30},{8,16},{10,18},{12,20},{14,22},{16,8},... | collective-permute-start | bytes 147464 | tf_op jit(solution)/shard_map/ppermute | solution.py:370
  49.8 0.0 collective-permute-done.21.other_ref
  49.8 1.9 %conv_back.1 = bf16[1,8,16,768]{3,2,1,0:T(8,128)(2,1)} custom-call(f32[6,8,16,128]{3,2,1,0:T(8,128)S(1)} %get-tuple-element.72.grad_ref, bf16[6,8,16,128]{3,2,1,0:T(8,128)(2,1)S(1)} %collective-permute-done.21.other_ref, f32[6,128,128]{2,1,0:T(8,128)S(1)} %get-tuple-element.66.refs_4_.taps_ref), custom_call_target="tpu_custom_call" | custom-call | flops 2090000000 | bytes 1179648 | tf_op jit(solution)/shard_map/conv_back/pallas_call | solution.py:343
  51.7 0.0 collective-permute-done.22.refs_1_
  51.7 0.9 %collective-permute-done.23.refs_2_ = bf16[48,512]{1,0:T(8,128)(2,1)S(1)} collective-permute-done((bf16[48,512]{1,0:T(8,128)(2,1)S(1)}, bf16[48,512]{1,0:T(8,128)(2,1)S(1)}, u32[]{:S(2)}, u32[]{:S(2)}) %collective-permute-start.23) | collective-permute-done | bytes 49184 | tf_op jit(solution)/shard_map/ppermute | solution.py:370
  52.5 2.1 %collective-permute-done.24.refs_3_ = bf16[48,512]{1,0:T(8,128)(2,1)S(1)} collective-permute-done((bf16[48,512]{1,0:T(8,128)(2,1)S(1)}, bf16[48,512]{1,0:T(8,128)(2,1)S(1)}, u32[]{:S(2)}, u32[]{:S(2)}) %collective-permute-start.24) | collective-permute-done | bytes 49184 | tf_op jit(solution)/shard_map/ppermute | solution.py:370
  54.6 0.1 collective-permute-start.25
  54.7 1.4 %collective-permute-done.25.other_ref = f32[48,896]{1,0:T(8,128)S(1)} collective-permute-done((f32[48,896]{1,0:T(8,128)S(1)}, f32[48,896]{1,0:T(8,128)S(1)}, u32[]{:S(2)}, u32[]{:S(2)}) %collective-permute-start.25) | collective-permute-done | bytes 172064 | tf_op jit(solution)/shard_map/ppermute | solution.py:373
  56.1 0.8 %finish.1 = (f32[48,1536]{1,0:T(8,128)}, f32[48,49]{1,0:T(8,128)}, f32[1,48]{1,0:T(1,128)}, f32[1,48]{1,0:T(1,128)}) custom-call(f32[48,896]{1,0:T(8,128)S(1)} %line_sum.1.mine_ref, f32[48,896]{1,0:T(8,128)S(1)} %collective-permute-done.25.other_ref), custom_call_target="tpu_custom_call" | custom-call | flops 550000000 | bytes 648768 | tf_op jit(solution)/shard_map/finish/pallas_call | solution.py:343
  (6 shorter events, 0.1 us)
Async XLA Ops:
  0.6 7.4 %copy-start = (bf16[1,8,16,768]{3,2,1,0:T(8,128)(2,1)S(1)}, bf16[1,8,16,768]{3,2,1,0:T(8,128)(2,1)}, u32[]{:S(2)}) copy-start(bf16[1,8,16,768]{3,2,1,0:T(8,128)(2,1)} %refs_5_) | copy-start | bytes 589828
  0.6 9.1 %copy-start.1 = (bf16[1,8,16,1536]{3,2,1,0:T(8,128)(2,1)S(1)}, bf16[1,8,16,1536]{3,2,1,0:T(8,128)(2,1)}, u32[]{:S(2)}) copy-start(bf16[1,8,16,1536]{3,2,1,0:T(8,128)(2,1)} %param.7) | copy-start | bytes 1179652
  2.4 7.8 %collective-permute-start.1 = (bf16[48,512]{1,0:T(8,128)(2,1)}, bf16[48,512]{1,0:T(8,128)(2,1)S(1)}, u32[]{:S(2)}, u32[]{:S(2)}) collective-permute-start(bf16[48,512]{1,0:T(8,128)(2,1)} %get-tuple-element.46.refs_0_), channel_id=1, source_target_pairs={{0,16},{2,18},{4,20},{6,22},{8,24},{10,26},{12,28},{14,30},{16,0},... | collective-permute-start | bytes 147464 | tf_op jit(solution)/shard_map/ppermute | solution.py:370
  6.4 6.6 %collective-permute-start.2 = (bf16[48,512]{1,0:T(8,128)(2,1)}, bf16[48,512]{1,0:T(8,128)(2,1)S(1)}, u32[]{:S(2)}, u32[]{:S(2)}) collective-permute-start(bf16[48,512]{1,0:T(8,128)(2,1)} %get-tuple-element.47), channel_id=1, source_target_pairs={{0,24},{2,26},{4,28},{6,30},{8,16},{10,18},{12,20},{14,22},{16,8},... | collective-permute-start | bytes 147464 | tf_op jit(solution)/shard_map/ppermute | solution.py:370
  7.8 5.4 %collective-permute-start = (bf16[48,512]{1,0:T(8,128)(2,1)}, bf16[48,512]{1,0:T(8,128)(2,1)S(1)}, u32[]{:S(2)}, u32[]{:S(2)}) collective-permute-start(bf16[48,512]{1,0:T(8,128)(2,1)} %get-tuple-element.47), channel_id=1, source_target_pairs={{0,8},{2,10},{4,12},{6,14},{8,0},{10,2},{12,4},{14,6},{16,24},{18,... | collective-permute-start | bytes 147464 | tf_op jit(solution)/shard_map/ppermute | solution.py:370
  8.0 14.2 %collective-permute-start.9 = (bf16[1,8,16,768]{3,2,1,0:T(8,128)(2,1)S(1)}, bf16[1,8,16,768]{3,2,1,0:T(8,128)(2,1)S(1)}, u32[]{:S(2)}, u32[]{:S(2)}) collective-permute-start(bf16[1,8,16,768]{3,2,1,0:T(8,128)(2,1)S(1)} %copy-done), channel_id=1, source_target_pairs={{0,8},{2,10},{4,12},{6,14},{8,0},{10,2},{12,4},{14,6},{16,24},{18,... | collective-permute-start | bytes 589832 | tf_op jit(solution)/shard_map/ppermute | solution.py:370
  9.8 3.4 %copy-start.2 = (bf16[48,512]{1,0:T(8,128)(2,1)S(1)}, bf16[48,512]{1,0:T(8,128)(2,1)}, u32[]{:S(2)}) copy-start(bf16[48,512]{1,0:T(8,128)(2,1)} %get-tuple-element.46.refs_0_) | copy-start | bytes 147460
  9.8 15.3 %collective-permute-start.10 = (bf16[128,768]{1,0:T(8,128)(2,1)S(1)}, bf16[128,768]{1,0:T(8,128)(2,1)S(1)}, u32[]{:S(2)}, u32[]{:S(2)}) collective-permute-start(bf16[128,768]{1,0:T(8,128)(2,1)S(1)} %get-tuple-element.53), channel_id=1, source_target_pairs={{0,8},{2,10},{4,12},{6,14},{8,0},{10,2},{12,4},{14,6},{16,24},{18,... | collective-permute-start | bytes 589832 | tf_op jit(solution)/shard_map/ppermute | solution.py:370
  13.2 5.1 %collective-permute-start.8 = (bf16[192,128]{1,0:T(8,128)(2,1)S(1)}, bf16[192,128]{1,0:T(8,128)(2,1)S(1)}, u32[]{:S(2)}, u32[]{:S(2)}) collective-permute-start(bf16[192,128]{1,0:T(8,128)(2,1)S(1)} %get-tuple-element.49.refs_0_), channel_id=1, source_target_pairs={{0,6},{2,4},{4,2},{6,0},{8,14},{10,12},{12,10},{14,8},{16,22},{18,... | collective-permute-start | bytes 147464 | tf_op jit(solution)/shard_map/ppermute | solution.py:370
  15.7 5.3 %collective-permute-start.7 = (bf16[192,128]{1,0:T(8,128)(2,1)S(1)}, bf16[192,128]{1,0:T(8,128)(2,1)S(1)}, u32[]{:S(2)}, u32[]{:S(2)}) collective-permute-start(bf16[192,128]{1,0:T(8,128)(2,1)S(1)} %get-tuple-element.49.refs_0_), channel_id=1, source_target_pairs={{0,4},{2,6},{4,0},{6,2},{8,12},{10,14},{12,8},{14,10},{16,20},{18,... | collective-permute-start | bytes 147464 | tf_op jit(solution)/shard_map/ppermute | solution.py:370
  16.2 5.9 %collective-permute-start.6 = (bf16[192,128]{1,0:T(8,128)(2,1)S(1)}, bf16[192,128]{1,0:T(8,128)(2,1)S(1)}, u32[]{:S(2)}, u32[]{:S(2)}) collective-permute-start(bf16[192,128]{1,0:T(8,128)(2,1)S(1)} %get-tuple-element.49.refs_0_), channel_id=1, source_target_pairs={{0,2},{2,0},{4,6},{6,4},{8,10},{10,8},{12,14},{14,12},{16,18},{18,... | collective-permute-start | bytes 147464 | tf_op jit(solution)/shard_map/ppermute | solution.py:370
  18.3 7.5 %collective-permute-start.5 = (bf16[192,384]{1,0:T(8,128)(2,1)S(1)}, bf16[192,384]{1,0:T(8,128)(2,1)S(1)}, u32[]{:S(2)}, u32[]{:S(2)}) collective-permute-start(bf16[192,384]{1,0:T(8,128)(2,1)S(1)} %get-tuple-element.48.refs_0_), channel_id=1, source_target_pairs={{0,6},{2,4},{4,2},{6,0},{8,14},{10,12},{12,10},{14,8},{16,22},{18,... | collective-permute-start | bytes 442376 | tf_op jit(solution)/shard_map/ppermute | solution.py:370
  21.0 5.1 %collective-permute-start.4 = (bf16[192,384]{1,0:T(8,128)(2,1)S(1)}, bf16[192,384]{1,0:T(8,128)(2,1)S(1)}, u32[]{:S(2)}, u32[]{:S(2)}) collective-permute-start(bf16[192,384]{1,0:T(8,128)(2,1)S(1)} %get-tuple-element.48.refs_0_), channel_id=1, source_target_pairs={{0,4},{2,6},{4,0},{6,2},{8,12},{10,14},{12,8},{14,10},{16,20},{18,... | collective-permute-start | bytes 442376 | tf_op jit(solution)/shard_map/ppermute | solution.py:370
  22.1 5.1 %collective-permute-start.3 = (bf16[192,384]{1,0:T(8,128)(2,1)S(1)}, bf16[192,384]{1,0:T(8,128)(2,1)S(1)}, u32[]{:S(2)}, u32[]{:S(2)}) collective-permute-start(bf16[192,384]{1,0:T(8,128)(2,1)S(1)} %get-tuple-element.48.refs_0_), channel_id=1, source_target_pairs={{0,2},{2,0},{4,6},{6,4},{8,10},{10,8},{12,14},{14,12},{16,18},{18,... | collective-permute-start | bytes 442376 | tf_op jit(solution)/shard_map/ppermute | solution.py:370
  25.1 2.4 %collective-permute-start.11 = (bf16[256,768]{1,0:T(8,128)(2,1)S(1)}, bf16[256,768]{1,0:T(8,128)(2,1)S(1)}, u32[]{:S(2)}, u32[]{:S(2)}) collective-permute-start(bf16[256,768]{1,0:T(8,128)(2,1)S(1)} %get-tuple-element.54.refs_1_), channel_id=1, source_target_pairs={{0,1},{1,0},{2,3},{3,2},{4,5},{5,4},{6,7},{7,6},{8,9},{9,8},{10,11... | collective-permute-start | bytes 1179656 | tf_op jit(solution)/shard_map/ppermute | solution.py:373
  25.2 2.1 %collective-permute-start.12 = (bf16[128,768]{1,0:T(8,128)(2,1)S(1)}, bf16[128,768]{1,0:T(8,128)(2,1)S(1)}, u32[]{:S(2)}, u32[]{:S(2)}) collective-permute-start(bf16[128,768]{1,0:T(8,128)(2,1)S(1)} %get-tuple-element.55), channel_id=1, source_target_pairs={{0,1},{1,0},{2,3},{3,2},{4,5},{5,4},{6,7},{7,6},{8,9},{9,8},{10,11... | collective-permute-start | bytes 589832 | tf_op jit(solution)/shard_map/ppermute | solution.py:373
  25.7 1.8 %collective-permute-start.13 = (bf16[128,768]{1,0:T(8,128)(2,1)S(1)}, bf16[128,768]{1,0:T(8,128)(2,1)S(1)}, u32[]{:S(2)}, u32[]{:S(2)}) collective-permute-start(bf16[128,768]{1,0:T(8,128)(2,1)S(1)} %collective-permute-done.10.refs_5_), channel_id=1, source_target_pairs={{0,1},{1,0},{2,3},{3,2},{4,5},{5,4},{6,7},{7,6},{8,9},{9,8},{10,11... | collective-permute-start | bytes 589832 | tf_op jit(solution)/shard_map/ppermute | solution.py:373
  29.6 3.1 %collective-permute-start.17 = (f32[256,768]{1,0:T(8,128)S(1)}, f32[256,768]{1,0:T(8,128)S(1)}, u32[]{:S(2)}, u32[]{:S(2)}) collective-permute-start(f32[256,768]{1,0:T(8,128)S(1)} %get-tuple-element.63), channel_id=1, source_target_pairs={{0,1},{1,0},{2,3},{3,2},{4,5},{5,4},{6,7},{7,6},{8,9},{9,8},{10,11... | collective-permute-start | bytes 2359304 | tf_op jit(solution)/shard_map/ppermute | solution.py:373
  29.8 8.8 %collective-permute-start.14 = (bf16[192,384]{1,0:T(8,128)(2,1)S(1)}, bf16[192,384]{1,0:T(8,128)(2,1)S(1)}, u32[]{:S(2)}, u32[]{:S(2)}) collective-permute-start(bf16[192,384]{1,0:T(8,128)(2,1)S(1)} %get-tuple-element.58), channel_id=1, source_target_pairs={{0,2},{2,0},{4,6},{6,4},{8,10},{10,8},{12,14},{14,12},{16,18},{18,... | collective-permute-start | bytes 442376 | tf_op jit(solution)/shard_map/ppermute | solution.py:370
  31.8 8.5 %collective-permute-start.15 = (bf16[192,384]{1,0:T(8,128)(2,1)S(1)}, bf16[192,384]{1,0:T(8,128)(2,1)S(1)}, u32[]{:S(2)}, u32[]{:S(2)}) collective-permute-start(bf16[192,384]{1,0:T(8,128)(2,1)S(1)} %get-tuple-element.59), channel_id=1, source_target_pairs={{0,4},{2,6},{4,0},{6,2},{8,12},{10,14},{12,8},{14,10},{16,20},{18,... | collective-permute-start | bytes 442376 | tf_op jit(solution)/shard_map/ppermute | solution.py:370
  35.8 14.0 %collective-permute-start.21 = (bf16[6,8,16,128]{3,2,1,0:T(8,128)(2,1)S(1)}, bf16[6,8,16,128]{3,2,1,0:T(8,128)(2,1)S(1)}, u32[]{:S(2)}, u32[]{:S(2)}) collective-permute-start(bf16[6,8,16,128]{3,2,1,0:T(8,128)(2,1)S(1)} %get-tuple-element.73), channel_id=1, source_target_pairs={{0,8},{2,10},{4,12},{6,14},{8,0},{10,2},{12,4},{14,6},{16,24},{18,... | collective-permute-start | bytes 589832 | tf_op jit(solution)/shard_map/ppermute | solution.py:370
  36.8 7.3 %collective-permute-start.16 = (bf16[192,384]{1,0:T(8,128)(2,1)S(1)}, bf16[192,384]{1,0:T(8,128)(2,1)S(1)}, u32[]{:S(2)}, u32[]{:S(2)}) collective-permute-start(bf16[192,384]{1,0:T(8,128)(2,1)S(1)} %get-tuple-element.60), channel_id=1, source_target_pairs={{0,6},{2,4},{4,2},{6,0},{8,14},{10,12},{12,10},{14,8},{16,22},{18,... | collective-permute-start | bytes 442376 | tf_op jit(solution)/shard_map/ppermute | solution.py:370
  38.3 5.7 %collective-permute-start.18 = (bf16[192,128]{1,0:T(8,128)(2,1)S(1)}, bf16[192,128]{1,0:T(8,128)(2,1)S(1)}, u32[]{:S(2)}, u32[]{:S(2)}) collective-permute-start(bf16[192,128]{1,0:T(8,128)(2,1)S(1)} %get-tuple-element.68), channel_id=1, source_target_pairs={{0,2},{2,0},{4,6},{6,4},{8,10},{10,8},{12,14},{14,12},{16,18},{18,... | collective-permute-start | bytes 147464 | tf_op jit(solution)/shard_map/ppermute | solution.py:370
  38.7 5.9 %collective-permute-start.19 = (bf16[192,128]{1,0:T(8,128)(2,1)S(1)}, bf16[192,128]{1,0:T(8,128)(2,1)S(1)}, u32[]{:S(2)}, u32[]{:S(2)}) collective-permute-start(bf16[192,128]{1,0:T(8,128)(2,1)S(1)} %get-tuple-element.69), channel_id=1, source_target_pairs={{0,4},{2,6},{4,0},{6,2},{8,12},{10,14},{12,8},{14,10},{16,20},{18,... | collective-permute-start | bytes 147464 | tf_op jit(solution)/shard_map/ppermute | solution.py:370
  40.3 5.0 %collective-permute-start.20 = (bf16[192,128]{1,0:T(8,128)(2,1)S(1)}, bf16[192,128]{1,0:T(8,128)(2,1)S(1)}, u32[]{:S(2)}, u32[]{:S(2)}) collective-permute-start(bf16[192,128]{1,0:T(8,128)(2,1)S(1)} %get-tuple-element.70), channel_id=1, source_target_pairs={{0,6},{2,4},{4,2},{6,0},{8,14},{10,12},{12,10},{14,8},{16,22},{18,... | collective-permute-start | bytes 147464 | tf_op jit(solution)/shard_map/ppermute | solution.py:370
  45.4 6.3 %collective-permute-start.22 = (bf16[48,512]{1,0:T(8,128)(2,1)S(1)}, bf16[48,512]{1,0:T(8,128)(2,1)S(1)}, u32[]{:S(2)}, u32[]{:S(2)}) collective-permute-start(bf16[48,512]{1,0:T(8,128)(2,1)S(1)} %get-tuple-element.76), channel_id=1, source_target_pairs={{0,8},{2,10},{4,12},{6,14},{8,0},{10,2},{12,4},{14,6},{16,24},{18,... | collective-permute-start | bytes 147464 | tf_op jit(solution)/shard_map/ppermute | solution.py:370
  46.5 6.0 %collective-permute-start.23 = (bf16[48,512]{1,0:T(8,128)(2,1)S(1)}, bf16[48,512]{1,0:T(8,128)(2,1)S(1)}, u32[]{:S(2)}, u32[]{:S(2)}) collective-permute-start(bf16[48,512]{1,0:T(8,128)(2,1)S(1)} %get-tuple-element.77), channel_id=1, source_target_pairs={{0,16},{2,18},{4,20},{6,22},{8,24},{10,26},{12,28},{14,30},{16,0},... | collective-permute-start | bytes 147464 | tf_op jit(solution)/shard_map/ppermute | solution.py:370
  48.7 5.9 %collective-permute-start.24 = (bf16[48,512]{1,0:T(8,128)(2,1)S(1)}, bf16[48,512]{1,0:T(8,128)(2,1)S(1)}, u32[]{:S(2)}, u32[]{:S(2)}) collective-permute-start(bf16[48,512]{1,0:T(8,128)(2,1)S(1)} %get-tuple-element.78), channel_id=1, source_target_pairs={{0,24},{2,26},{4,28},{6,30},{8,16},{10,18},{12,20},{14,22},{16,8},... | collective-permute-start | bytes 147464 | tf_op jit(solution)/shard_map/ppermute | solution.py:370
  54.6 1.5 %collective-permute-start.25 = (f32[48,896]{1,0:T(8,128)S(1)}, f32[48,896]{1,0:T(8,128)S(1)}, u32[]{:S(2)}, u32[]{:S(2)}) collective-permute-start(f32[48,896]{1,0:T(8,128)S(1)} %line_sum.1.mine_ref), channel_id=1, source_target_pairs={{0,1},{1,0},{2,3},{3,2},{4,5},{5,4},{6,7},{7,6},{8,9},{9,8},{10,11... | collective-permute-start | bytes 516104 | tf_op jit(solution)/shard_map/ppermute | solution.py:373

commit v8 on v7

--- a/solution.py
+++ b/solution.py
@@ -526,7 +526,7 @@
         "conv_back",
         [shape(images.shape, BF16)],
         [padded],
-        1.9,
+        0.1,
         grad_conv,
         grad_other,
         taps,
@@ -537,7 +537,7 @@
         "plane_sum",
         [shape((own, quarter + LANES), F32)] + [shape((own, quarter + LANES), BF16)] * (lines - 1),
         [],
-        0.4,
+        2.0,
         pieces[0],
         *arrived,
         small[0],

time: 57 us -> 55.7 us (0.977)
  starting transfers between devices: 29.3 us -> 27.8 us
    ppermute x21, starting transfers between devices: 28.4 us -> 26.8 us  [over_shard(): return lax.ppermute(array, 'shard', [(i, i ^ flip) for i in range(shards)])]
where the time goes in v8:
time: 55.7 us; the launch traced here: 55.6 us
  starting transfers between devices  27.8 us (50%)
  waiting for transfers between devices  14.4 us (26%)
  Pallas kernels  12.6 us (23%)
  between operations  0.76 us (1%)
    ppermute x21, starting transfers between devices, over_shard(): return lax.ppermute(array, 'shard', [(i, i ^ flip) for i in range(shards)])  26.8 us
    ppermute x21, waiting for transfers between devices, over_shard(): return lax.ppermute(array, 'shard', [(i, i ^ flip) for i in range(shards)])  12.9 us
    pallas_call x12, Pallas kernels, call(): pl.pallas_call(kernel, out_shape=outs, in_specs=[VMEM] * len(args), out_s...  12.6 us
    ppermute x5, waiting for transfers between devices, over_core(): return lax.ppermute(array, 'rep', [(i, i ^ 1) for i in range(reps)])  1.56 us
  transfers between devices with their start and end apart: 26, of which 13 were waited for; matrix products, arithmetic and copies ran while one was open for 0% of the time, Pallas kernels for 14%

profile of v8, /device:TPU:0, one launch (start us, length us, event | category | flops | bytes accessed | tf_op | source)
XLA Modules:
  0.0 55.6 jit_solution(2323833538095962962)
XLA Ops:
  0.6 0.0 copy-start
  0.6 0.0 copy-start.1
  0.7 1.7 %pack.1 = (bf16[48,512]{1,0:T(8,128)(2,1)}, bf16[48,512]{1,0:T(8,128)(2,1)}) custom-call(bf16[48,1536]{1,0:T(8,128)(2,1)} %w_ref.1, bf16[48,49]{1,0:T(8,128)(2,1)} %dw_ref.1, bf16[1,48]{1,0:T(2,128)(2,1)} %bitcast.7, bf16[1,48]{1,0:T(2,128)(2,1)} %bitcast.8), custom_call_target="tpu_custom_call" | custom-call | flops 550000000 | bytes 250656 | tf_op jit(solution)/shard_map/pack/pallas_call | solution.py:343
  2.4 4.0 %collective-permute-start.1 = (bf16[48,512]{1,0:T(8,128)(2,1)}, bf16[48,512]{1,0:T(8,128)(2,1)S(1)}, u32[]{:S(2)}, u32[]{:S(2)}) collective-permute-start(bf16[48,512]{1,0:T(8,128)(2,1)} %get-tuple-element.46.refs_0_), channel_id=1, source_target_pairs={{0,16},{2,18},{4,20},{6,22},{8,24},{10,26},{12,28},{14,30},{16,0},... | collective-permute-start | bytes 147464 | tf_op jit(solution)/shard_map/ppermute | solution.py:370
  6.4 1.3 %collective-permute-start.2 = (bf16[48,512]{1,0:T(8,128)(2,1)}, bf16[48,512]{1,0:T(8,128)(2,1)S(1)}, u32[]{:S(2)}, u32[]{:S(2)}) collective-permute-start(bf16[48,512]{1,0:T(8,128)(2,1)} %get-tuple-element.47), channel_id=1, source_target_pairs={{0,24},{2,26},{4,28},{6,30},{8,16},{10,18},{12,20},{14,22},{16,8},... | collective-permute-start | bytes 147464 | tf_op jit(solution)/shard_map/ppermute | solution.py:370
  7.8 0.2 collective-permute-start
  8.0 1.8 %collective-permute-start.9 = (bf16[1,8,16,768]{3,2,1,0:T(8,128)(2,1)S(1)}, bf16[1,8,16,768]{3,2,1,0:T(8,128)(2,1)S(1)}, u32[]{:S(2)}, u32[]{:S(2)}) collective-permute-start(bf16[1,8,16,768]{3,2,1,0:T(8,128)(2,1)S(1)} %copy-done), channel_id=1, source_target_pairs={{0,8},{2,10},{4,12},{6,14},{8,0},{10,2},{12,4},{14,6},{16,24},{18,... | collective-permute-start | bytes 589832 | tf_op jit(solution)/shard_map/ppermute | solution.py:370
  9.8 0.3 collective-permute-start.10
  10.1 0.0 collective-permute-done.1.refs_2_
  10.1 2.9 %collective-permute-done.2.refs_3_ = bf16[48,512]{1,0:T(8,128)(2,1)S(1)} collective-permute-done((bf16[48,512]{1,0:T(8,128)(2,1)}, bf16[48,512]{1,0:T(8,128)(2,1)S(1)}, u32[]{:S(2)}, u32[]{:S(2)}) %collective-permute-start.2) | collective-permute-done | bytes 49184 | tf_op jit(solution)/shard_map/ppermute | solution.py:370
  13.0 0.1 collective-permute-done.refs_1_
  13.2 0.0 copy-done.2
  13.2 2.5 %collective-permute-start.8 = (bf16[192,128]{1,0:T(8,128)(2,1)S(1)}, bf16[192,128]{1,0:T(8,128)(2,1)S(1)}, u32[]{:S(2)}, u32[]{:S(2)}) collective-permute-start(bf16[192,128]{1,0:T(8,128)(2,1)S(1)} %get-tuple-element.49.refs_0_), channel_id=1, source_target_pairs={{0,6},{2,4},{4,2},{6,0},{8,14},{10,12},{12,10},{14,8},{16,22},{18,... | collective-permute-start | bytes 147464 | tf_op jit(solution)/shard_map/ppermute | solution.py:370
  15.7 0.5 collective-permute-start.7
  16.2 0.5 collective-permute-start.6
  16.8 1.5 %collective-permute-done.8.refs_3_ = bf16[192,128]{1,0:T(8,128)(2,1)S(1)} collective-permute-done((bf16[192,128]{1,0:T(8,128)(2,1)S(1)}, bf16[192,128]{1,0:T(8,128)(2,1)S(1)}, u32[]{:S(2)}, u32[]{:S(2)}) %collective-permute-start.8) | collective-permute-done | bytes 49184 | tf_op jit(solution)/shard_map/ppermute | solution.py:370
  18.3 2.6 %collective-permute-start.5 = (bf16[192,384]{1,0:T(8,128)(2,1)S(1)}, bf16[192,384]{1,0:T(8,128)(2,1)S(1)}, u32[]{:S(2)}, u32[]{:S(2)}) collective-permute-start(bf16[192,384]{1,0:T(8,128)(2,1)S(1)} %get-tuple-element.48.refs_0_), channel_id=1, source_target_pairs={{0,6},{2,4},{4,2},{6,0},{8,14},{10,12},{12,10},{14,8},{16,22},{18,... | collective-permute-start | bytes 442376 | tf_op jit(solution)/shard_map/ppermute | solution.py:370
  20.8 0.2 collective-permute-done.7.refs_2_
  21.0 1.1 %collective-permute-start.4 = (bf16[192,384]{1,0:T(8,128)(2,1)S(1)}, bf16[192,384]{1,0:T(8,128)(2,1)S(1)}, u32[]{:S(2)}, u32[]{:S(2)}) collective-permute-start(bf16[192,384]{1,0:T(8,128)(2,1)S(1)} %get-tuple-element.48.refs_0_), channel_id=1, source_target_pairs={{0,4},{2,6},{4,0},{6,2},{8,12},{10,14},{12,8},{14,10},{16,20},{18,... | collective-permute-start | bytes 442376 | tf_op jit(solution)/shard_map/ppermute | solution.py:370
  22.1 0.0 collective-permute-done.6.refs_1_
  22.1 0.1 collective-permute-start.3
  22.2 0.0 collective-permute-done.9.refs_5_.refs_6_
  22.2 2.9 %conv_norm.1 = (bf16[256,768]{1,0:T(8,128)(2,1)S(1)}, f32[256,768]{1,0:T(8,128)S(1)}, f32[256,128]{1,0:T(8,128)S(1)}, f32[6,128,128]{2,1,0:T(8,128)S(1)}) custom-call(bf16[192,128]{1,0:T(8,128)(2,1)S(1)} %get-tuple-element.49.refs_0_, bf16[192,128]{1,0:T(8,128)(2,1)S(1)} %collective-permute-done.6.refs_1_, ...), custom_call_target="tpu_custom_call" | custom-call | flops 110000000 | bytes 2293760 | tf_op jit(solution)/shard_map/conv_norm/pallas_call | solution.py:343
  25.1 0.0 collective-permute-done.10.refs_5_
  25.1 0.1 collective-permute-start.11
  25.2 0.5 collective-permute-start.12
  25.7 0.0 collective-permute-done.5.refs_3_
  25.7 0.1 collective-permute-start.13
  25.8 0.4 collective-permute-done.4.refs_2_
  26.2 1.1 %collective-permute-done.3.refs_1_ = bf16[192,384]{1,0:T(8,128)(2,1)S(1)} collective-permute-done((bf16[192,384]{1,0:T(8,128)(2,1)S(1)}, bf16[192,384]{1,0:T(8,128)(2,1)S(1)}, u32[]{:S(2)}, u32[]{:S(2)}) %collective-permute-start.3) | collective-permute-done | bytes 147488 | tf_op jit(solution)/shard_map/ppermute | solution.py:370
  27.3 0.1 order.1.refs_0_.weight
  27.3 0.0 collective-permute-done.12.refs_4_
  27.3 0.2 collective-permute-done.13.refs_6_
  27.5 0.0 collective-permute-done.11.refs_2_
  27.5 1.5 %project.1 = (f32[192,384]{1,0:T(8,128)S(1)}, bf16[192,384]{1,0:T(8,128)(2,1)S(1)}, bf16[192,384]{1,0:T(8,128)(2,1)S(1)}, bf16[192,384]{1,0:T(8,128)(2,1)S(1)}, bf16[512,384]{1,0:T(8,128)(2,1)S(1)}) custom-call(bf16[768,384]{1,0:T(8,128)(2,1)S(1)} %order.1.refs_0_.weight, bf16[256,768]{1,0:T(8,128)(2,1)S(1)} %get-tuple-element.54.refs_1_, ...), custom_call_target="tpu_custom_call" | custom-call | flops 1760000000 | bytes 3489792 | tf_op jit(solution)/shard_map/project/pallas_call | solution.py:343
  29.0 0.6 %back_project.1 = (f32[256,768]{1,0:T(8,128)S(1)}, f32[256,768]{1,0:T(8,128)S(1)}) custom-call(bf16[768,384]{1,0:T(8,128)(2,1)S(1)} %order.1.refs_0_.weight, bf16[512,384]{1,0:T(8,128)(2,1)S(1)} %get-tuple-element.61.gp_ref), custom_call_target="tpu_custom_call" | custom-call | flops 770000000 | bytes 2555904 | tf_op jit(solution)/shard_map/back_project/pallas_call | solution.py:343
  29.6 0.2 collective-permute-start.17
  29.8 2.0 %collective-permute-start.14 = (bf16[192,384]{1,0:T(8,128)(2,1)S(1)}, bf16[192,384]{1,0:T(8,128)(2,1)S(1)}, u32[]{:S(2)}, u32[]{:S(2)}) collective-permute-start(bf16[192,384]{1,0:T(8,128)(2,1)S(1)} %get-tuple-element.58), channel_id=1, source_target_pairs={{0,2},{2,0},{4,6},{6,4},{8,10},{10,8},{12,14},{14,12},{16,18},{18,... | collective-permute-start | bytes 442376 | tf_op jit(solution)/shard_map/ppermute | solution.py:370
  31.8 1.0 %collective-permute-start.15 = (bf16[192,384]{1,0:T(8,128)(2,1)S(1)}, bf16[192,384]{1,0:T(8,128)(2,1)S(1)}, u32[]{:S(2)}, u32[]{:S(2)}) collective-permute-start(bf16[192,384]{1,0:T(8,128)(2,1)S(1)} %get-tuple-element.59), channel_id=1, source_target_pairs={{0,4},{2,6},{4,0},{6,2},{8,12},{10,14},{12,8},{14,10},{16,20},{18,... | collective-permute-start | bytes 442376 | tf_op jit(solution)/shard_map/ppermute | solution.py:370
  32.7 0.6 %collective-permute-start.16 = (bf16[192,384]{1,0:T(8,128)(2,1)S(1)}, bf16[192,384]{1,0:T(8,128)(2,1)S(1)}, u32[]{:S(2)}, u32[]{:S(2)}) collective-permute-start(bf16[192,384]{1,0:T(8,128)(2,1)S(1)} %get-tuple-element.60), channel_id=1, source_target_pairs={{0,6},{2,4},{4,2},{6,0},{8,14},{10,12},{12,10},{14,8},{16,22},{18,... | collective-permute-start | bytes 442376 | tf_op jit(solution)/shard_map/ppermute | solution.py:370
  33.3 0.0 collective-permute-done.17.refs_1_
  33.3 3.0 %norm_back.1 = (f32[192,128]{1,0:T(8,128)S(1)}, bf16[192,128]{1,0:T(8,128)(2,1)S(1)}, bf16[192,128]{1,0:T(8,128)(2,1)S(1)}, bf16[192,128]{1,0:T(8,128)(2,1)S(1)}...) custom-call(f32[256,768]{1,0:T(8,128)S(1)} %get-tuple-element.62.refs_0_, ...), custom_call_target="tpu_custom_call" | custom-call | flops 110000000 | bytes 4112384 | tf_op jit(solution)/shard_map/norm_back/pallas_call | solution.py:343
  36.4 2.0 %collective-permute-start.18 = (bf16[192,128]{1,0:T(8,128)(2,1)S(1)}, bf16[192,128]{1,0:T(8,128)(2,1)S(1)}, u32[]{:S(2)}, u32[]{:S(2)}) collective-permute-start(bf16[192,128]{1,0:T(8,128)(2,1)S(1)} %get-tuple-element.68), channel_id=1, source_target_pairs={{0,2},{2,0},{4,6},{6,4},{8,10},{10,8},{12,14},{14,12},{16,18},{18,... | collective-permute-start | bytes 147464 | tf_op jit(solution)/shard_map/ppermute | solution.py:370
  38.4 0.9 %collective-permute-start.19 = (bf16[192,128]{1,0:T(8,128)(2,1)S(1)}, bf16[192,128]{1,0:T(8,128)(2,1)S(1)}, u32[]{:S(2)}, u32[]{:S(2)}) collective-permute-start(bf16[192,128]{1,0:T(8,128)(2,1)S(1)} %get-tuple-element.69), channel_id=1, source_target_pairs={{0,4},{2,6},{4,0},{6,2},{8,12},{10,14},{12,8},{14,10},{16,20},{18,... | collective-permute-start | bytes 147464 | tf_op jit(solution)/shard_map/ppermute | solution.py:370
  39.3 0.0 collective-permute-done.14.refs_1_
  39.3 0.6 %collective-permute-start.20 = (bf16[192,128]{1,0:T(8,128)(2,1)S(1)}, bf16[192,128]{1,0:T(8,128)(2,1)S(1)}, u32[]{:S(2)}, u32[]{:S(2)}) collective-permute-start(bf16[192,128]{1,0:T(8,128)(2,1)S(1)} %get-tuple-element.70), channel_id=1, source_target_pairs={{0,6},{2,4},{4,2},{6,0},{8,14},{10,12},{12,10},{14,8},{16,22},{18,... | collective-permute-start | bytes 147464 | tf_op jit(solution)/shard_map/ppermute | solution.py:370
  39.9 0.5 collective-permute-done.15.refs_2_
  40.4 0.4 collective-permute-start.21
  40.7 0.4 collective-permute-done.16.refs_3_
  41.1 0.0 collective-permute-done.18.refs_5_
  41.2 1.8 %collective-permute-done.19.refs_6_ = bf16[192,128]{1,0:T(8,128)(2,1)S(1)} collective-permute-done((bf16[192,128]{1,0:T(8,128)(2,1)S(1)}, bf16[192,128]{1,0:T(8,128)(2,1)S(1)}, u32[]{:S(2)}, u32[]{:S(2)}) %collective-permute-start.19) | collective-permute-done | bytes 49184 | tf_op jit(solution)/shard_map/ppermute | solution.py:370
  42.9 1.4 %collective-permute-done.20.refs_7_ = bf16[192,128]{1,0:T(8,128)(2,1)S(1)} collective-permute-done((bf16[192,128]{1,0:T(8,128)(2,1)S(1)}, bf16[192,128]{1,0:T(8,128)(2,1)S(1)}, u32[]{:S(2)}, u32[]{:S(2)}) %collective-permute-start.20) | collective-permute-done | bytes 49184 | tf_op jit(solution)/shard_map/ppermute | solution.py:370
  44.3 0.1 plane_sum.1
  44.4 1.0 %collective-permute-start.22 = (bf16[48,512]{1,0:T(8,128)(2,1)S(1)}, bf16[48,512]{1,0:T(8,128)(2,1)S(1)}, u32[]{:S(2)}, u32[]{:S(2)}) collective-permute-start(bf16[48,512]{1,0:T(8,128)(2,1)S(1)} %get-tuple-element.76), channel_id=1, source_target_pairs={{0,8},{2,10},{4,12},{6,14},{8,0},{10,2},{12,4},{14,6},{16,24},{18,... | collective-permute-start | bytes 147464 | tf_op jit(solution)/shard_map/ppermute | solution.py:370
  45.4 2.0 %collective-permute-start.23 = (bf16[48,512]{1,0:T(8,128)(2,1)S(1)}, bf16[48,512]{1,0:T(8,128)(2,1)S(1)}, u32[]{:S(2)}, u32[]{:S(2)}) collective-permute-start(bf16[48,512]{1,0:T(8,128)(2,1)S(1)} %get-tuple-element.77), channel_id=1, source_target_pairs={{0,16},{2,18},{4,20},{6,22},{8,24},{10,26},{12,28},{14,30},{16,0},... | collective-permute-start | bytes 147464 | tf_op jit(solution)/shard_map/ppermute | solution.py:370
  47.4 1.4 %collective-permute-start.24 = (bf16[48,512]{1,0:T(8,128)(2,1)S(1)}, bf16[48,512]{1,0:T(8,128)(2,1)S(1)}, u32[]{:S(2)}, u32[]{:S(2)}) collective-permute-start(bf16[48,512]{1,0:T(8,128)(2,1)S(1)} %get-tuple-element.78), channel_id=1, source_target_pairs={{0,24},{2,26},{4,28},{6,30},{8,16},{10,18},{12,20},{14,22},{16,8},... | collective-permute-start | bytes 147464 | tf_op jit(solution)/shard_map/ppermute | solution.py:370
  48.9 0.0 collective-permute-done.21.other_ref
  48.9 1.9 %conv_back.1 = bf16[1,8,16,768]{3,2,1,0:T(8,128)(2,1)} custom-call(f32[6,8,16,128]{3,2,1,0:T(8,128)S(1)} %get-tuple-element.72.grad_ref, bf16[6,8,16,128]{3,2,1,0:T(8,128)(2,1)S(1)} %collective-permute-done.21.other_ref, f32[6,128,128]{2,1,0:T(8,128)S(1)} %get-tuple-element.66.refs_4_.taps_ref), custom_call_target="tpu_custom_call" | custom-call | flops 110000000 | bytes 1179648 | tf_op jit(solution)/shard_map/conv_back/pallas_call | solution.py:343
  50.7 0.0 collective-permute-done.22.refs_1_
  50.7 0.0 collective-permute-done.23.refs_2_
  50.7 2.6 %collective-permute-done.24.refs_3_ = bf16[48,512]{1,0:T(8,128)(2,1)S(1)} collective-permute-done((bf16[48,512]{1,0:T(8,128)(2,1)S(1)}, bf16[48,512]{1,0:T(8,128)(2,1)S(1)}, u32[]{:S(2)}, u32[]{:S(2)}) %collective-permute-start.24) | collective-permute-done | bytes 49184 | tf_op jit(solution)/shard_map/ppermute | solution.py:370
  53.3 0.1 collective-permute-start.25
  53.4 1.4 %collective-permute-done.25.other_ref = f32[48,896]{1,0:T(8,128)S(1)} collective-permute-done((f32[48,896]{1,0:T(8,128)S(1)}, f32[48,896]{1,0:T(8,128)S(1)}, u32[]{:S(2)}, u32[]{:S(2)}) %collective-permute-start.25) | collective-permute-done | bytes 172064 | tf_op jit(solution)/shard_map/ppermute | solution.py:373
  54.8 0.8 %finish.1 = (f32[48,1536]{1,0:T(8,128)}, f32[48,49]{1,0:T(8,128)}, f32[1,48]{1,0:T(1,128)}, f32[1,48]{1,0:T(1,128)}) custom-call(f32[48,896]{1,0:T(8,128)S(1)} %line_sum.1.mine_ref, f32[48,896]{1,0:T(8,128)S(1)} %collective-permute-done.25.other_ref), custom_call_target="tpu_custom_call" | custom-call | flops 550000000 | bytes 648768 | tf_op jit(solution)/shard_map/finish/pallas_call | solution.py:343
  (6 shorter events, 0.1 us)
Async XLA Ops:
  0.6 7.4 %copy-start = (bf16[1,8,16,768]{3,2,1,0:T(8,128)(2,1)S(1)}, bf16[1,8,16,768]{3,2,1,0:T(8,128)(2,1)}, u32[]{:S(2)}) copy-start(bf16[1,8,16,768]{3,2,1,0:T(8,128)(2,1)} %refs_5_) | copy-start | bytes 589828
  0.6 9.1 %copy-start.1 = (bf16[1,8,16,1536]{3,2,1,0:T(8,128)(2,1)S(1)}, bf16[1,8,16,1536]{3,2,1,0:T(8,128)(2,1)}, u32[]{:S(2)}) copy-start(bf16[1,8,16,1536]{3,2,1,0:T(8,128)(2,1)} %param.7) | copy-start | bytes 1179652
  2.4 7.8 %collective-permute-start.1 = (bf16[48,512]{1,0:T(8,128)(2,1)}, bf16[48,512]{1,0:T(8,128)(2,1)S(1)}, u32[]{:S(2)}, u32[]{:S(2)}) collective-permute-start(bf16[48,512]{1,0:T(8,128)(2,1)} %get-tuple-element.46.refs_0_), channel_id=1, source_target_pairs={{0,16},{2,18},{4,20},{6,22},{8,24},{10,26},{12,28},{14,30},{16,0},... | collective-permute-start | bytes 147464 | tf_op jit(solution)/shard_map/ppermute | solution.py:370
  6.4 6.6 %collective-permute-start.2 = (bf16[48,512]{1,0:T(8,128)(2,1)}, bf16[48,512]{1,0:T(8,128)(2,1)S(1)}, u32[]{:S(2)}, u32[]{:S(2)}) collective-permute-start(bf16[48,512]{1,0:T(8,128)(2,1)} %get-tuple-element.47), channel_id=1, source_target_pairs={{0,24},{2,26},{4,28},{6,30},{8,16},{10,18},{12,20},{14,22},{16,8},... | collective-permute-start | bytes 147464 | tf_op jit(solution)/shard_map/ppermute | solution.py:370
  7.8 5.4 %collective-permute-start = (bf16[48,512]{1,0:T(8,128)(2,1)}, bf16[48,512]{1,0:T(8,128)(2,1)S(1)}, u32[]{:S(2)}, u32[]{:S(2)}) collective-permute-start(bf16[48,512]{1,0:T(8,128)(2,1)} %get-tuple-element.47), channel_id=1, source_target_pairs={{0,8},{2,10},{4,12},{6,14},{8,0},{10,2},{12,4},{14,6},{16,24},{18,... | collective-permute-start | bytes 147464 | tf_op jit(solution)/shard_map/ppermute | solution.py:370
  8.0 14.2 %collective-permute-start.9 = (bf16[1,8,16,768]{3,2,1,0:T(8,128)(2,1)S(1)}, bf16[1,8,16,768]{3,2,1,0:T(8,128)(2,1)S(1)}, u32[]{:S(2)}, u32[]{:S(2)}) collective-permute-start(bf16[1,8,16,768]{3,2,1,0:T(8,128)(2,1)S(1)} %copy-done), channel_id=1, source_target_pairs={{0,8},{2,10},{4,12},{6,14},{8,0},{10,2},{12,4},{14,6},{16,24},{18,... | collective-permute-start | bytes 589832 | tf_op jit(solution)/shard_map/ppermute | solution.py:370
  9.8 3.4 %copy-start.2 = (bf16[48,512]{1,0:T(8,128)(2,1)S(1)}, bf16[48,512]{1,0:T(8,128)(2,1)}, u32[]{:S(2)}) copy-start(bf16[48,512]{1,0:T(8,128)(2,1)} %get-tuple-element.46.refs_0_) | copy-start | bytes 147460
  9.8 15.3 %collective-permute-start.10 = (bf16[128,768]{1,0:T(8,128)(2,1)S(1)}, bf16[128,768]{1,0:T(8,128)(2,1)S(1)}, u32[]{:S(2)}, u32[]{:S(2)}) collective-permute-start(bf16[128,768]{1,0:T(8,128)(2,1)S(1)} %get-tuple-element.53), channel_id=1, source_target_pairs={{0,8},{2,10},{4,12},{6,14},{8,0},{10,2},{12,4},{14,6},{16,24},{18,... | collective-permute-start | bytes 589832 | tf_op jit(solution)/shard_map/ppermute | solution.py:370
  13.2 5.1 %collective-permute-start.8 = (bf16[192,128]{1,0:T(8,128)(2,1)S(1)}, bf16[192,128]{1,0:T(8,128)(2,1)S(1)}, u32[]{:S(2)}, u32[]{:S(2)}) collective-permute-start(bf16[192,128]{1,0:T(8,128)(2,1)S(1)} %get-tuple-element.49.refs_0_), channel_id=1, source_target_pairs={{0,6},{2,4},{4,2},{6,0},{8,14},{10,12},{12,10},{14,8},{16,22},{18,... | collective-permute-start | bytes 147464 | tf_op jit(solution)/shard_map/ppermute | solution.py:370
  15.7 5.3 %collective-permute-start.7 = (bf16[192,128]{1,0:T(8,128)(2,1)S(1)}, bf16[192,128]{1,0:T(8,128)(2,1)S(1)}, u32[]{:S(2)}, u32[]{:S(2)}) collective-permute-start(bf16[192,128]{1,0:T(8,128)(2,1)S(1)} %get-tuple-element.49.refs_0_), channel_id=1, source_target_pairs={{0,4},{2,6},{4,0},{6,2},{8,12},{10,14},{12,8},{14,10},{16,20},{18,... | collective-permute-start | bytes 147464 | tf_op jit(solution)/shard_map/ppermute | solution.py:370
  16.2 5.9 %collective-permute-start.6 = (bf16[192,128]{1,0:T(8,128)(2,1)S(1)}, bf16[192,128]{1,0:T(8,128)(2,1)S(1)}, u32[]{:S(2)}, u32[]{:S(2)}) collective-permute-start(bf16[192,128]{1,0:T(8,128)(2,1)S(1)} %get-tuple-element.49.refs_0_), channel_id=1, source_target_pairs={{0,2},{2,0},{4,6},{6,4},{8,10},{10,8},{12,14},{14,12},{16,18},{18,... | collective-permute-start | bytes 147464 | tf_op jit(solution)/shard_map/ppermute | solution.py:370
  18.3 7.5 %collective-permute-start.5 = (bf16[192,384]{1,0:T(8,128)(2,1)S(1)}, bf16[192,384]{1,0:T(8,128)(2,1)S(1)}, u32[]{:S(2)}, u32[]{:S(2)}) collective-permute-start(bf16[192,384]{1,0:T(8,128)(2,1)S(1)} %get-tuple-element.48.refs_0_), channel_id=1, source_target_pairs={{0,6},{2,4},{4,2},{6,0},{8,14},{10,12},{12,10},{14,8},{16,22},{18,... | collective-permute-start | bytes 442376 | tf_op jit(solution)/shard_map/ppermute | solution.py:370
  21.0 5.1 %collective-permute-start.4 = (bf16[192,384]{1,0:T(8,128)(2,1)S(1)}, bf16[192,384]{1,0:T(8,128)(2,1)S(1)}, u32[]{:S(2)}, u32[]{:S(2)}) collective-permute-start(bf16[192,384]{1,0:T(8,128)(2,1)S(1)} %get-tuple-element.48.refs_0_), channel_id=1, source_target_pairs={{0,4},{2,6},{4,0},{6,2},{8,12},{10,14},{12,8},{14,10},{16,20},{18,... | collective-permute-start | bytes 442376 | tf_op jit(solution)/shard_map/ppermute | solution.py:370
  22.1 5.1 %collective-permute-start.3 = (bf16[192,384]{1,0:T(8,128)(2,1)S(1)}, bf16[192,384]{1,0:T(8,128)(2,1)S(1)}, u32[]{:S(2)}, u32[]{:S(2)}) collective-permute-start(bf16[192,384]{1,0:T(8,128)(2,1)S(1)} %get-tuple-element.48.refs_0_), channel_id=1, source_target_pairs={{0,2},{2,0},{4,6},{6,4},{8,10},{10,8},{12,14},{14,12},{16,18},{18,... | collective-permute-start | bytes 442376 | tf_op jit(solution)/shard_map/ppermute | solution.py:370
  25.1 2.4 %collective-permute-start.11 = (bf16[256,768]{1,0:T(8,128)(2,1)S(1)}, bf16[256,768]{1,0:T(8,128)(2,1)S(1)}, u32[]{:S(2)}, u32[]{:S(2)}) collective-permute-start(bf16[256,768]{1,0:T(8,128)(2,1)S(1)} %get-tuple-element.54.refs_1_), channel_id=1, source_target_pairs={{0,1},{1,0},{2,3},{3,2},{4,5},{5,4},{6,7},{7,6},{8,9},{9,8},{10,11... | collective-permute-start | bytes 1179656 | tf_op jit(solution)/shard_map/ppermute | solution.py:373
  25.2 2.1 %collective-permute-start.12 = (bf16[128,768]{1,0:T(8,128)(2,1)S(1)}, bf16[128,768]{1,0:T(8,128)(2,1)S(1)}, u32[]{:S(2)}, u32[]{:S(2)}) collective-permute-start(bf16[128,768]{1,0:T(8,128)(2,1)S(1)} %get-tuple-element.55), channel_id=1, source_target_pairs={{0,1},{1,0},{2,3},{3,2},{4,5},{5,4},{6,7},{7,6},{8,9},{9,8},{10,11... | collective-permute-start | bytes 589832 | tf_op jit(solution)/shard_map/ppermute | solution.py:373
  25.7 1.8 %collective-permute-start.13 = (bf16[128,768]{1,0:T(8,128)(2,1)S(1)}, bf16[128,768]{1,0:T(8,128)(2,1)S(1)}, u32[]{:S(2)}, u32[]{:S(2)}) collective-permute-start(bf16[128,768]{1,0:T(8,128)(2,1)S(1)} %collective-permute-done.10.refs_5_), channel_id=1, source_target_pairs={{0,1},{1,0},{2,3},{3,2},{4,5},{5,4},{6,7},{7,6},{8,9},{9,8},{10,11... | collective-permute-start | bytes 589832 | tf_op jit(solution)/shard_map/ppermute | solution.py:373
  29.6 3.7 %collective-permute-start.17 = (f32[256,768]{1,0:T(8,128)S(1)}, f32[256,768]{1,0:T(8,128)S(1)}, u32[]{:S(2)}, u32[]{:S(2)}) collective-permute-start(f32[256,768]{1,0:T(8,128)S(1)} %get-tuple-element.63), channel_id=1, source_target_pairs={{0,1},{1,0},{2,3},{3,2},{4,5},{5,4},{6,7},{7,6},{8,9},{9,8},{10,11... | collective-permute-start | bytes 2359304 | tf_op jit(solution)/shard_map/ppermute | solution.py:373
  29.8 9.5 %collective-permute-start.14 = (bf16[192,384]{1,0:T(8,128)(2,1)S(1)}, bf16[192,384]{1,0:T(8,128)(2,1)S(1)}, u32[]{:S(2)}, u32[]{:S(2)}) collective-permute-start(bf16[192,384]{1,0:T(8,128)(2,1)S(1)} %get-tuple-element.58), channel_id=1, source_target_pairs={{0,2},{2,0},{4,6},{6,4},{8,10},{10,8},{12,14},{14,12},{16,18},{18,... | collective-permute-start | bytes 442376 | tf_op jit(solution)/shard_map/ppermute | solution.py:370
  31.8 8.6 %collective-permute-start.15 = (bf16[192,384]{1,0:T(8,128)(2,1)S(1)}, bf16[192,384]{1,0:T(8,128)(2,1)S(1)}, u32[]{:S(2)}, u32[]{:S(2)}) collective-permute-start(bf16[192,384]{1,0:T(8,128)(2,1)S(1)} %get-tuple-element.59), channel_id=1, source_target_pairs={{0,4},{2,6},{4,0},{6,2},{8,12},{10,14},{12,8},{14,10},{16,20},{18,... | collective-permute-start | bytes 442376 | tf_op jit(solution)/shard_map/ppermute | solution.py:370
  32.7 8.4 %collective-permute-start.16 = (bf16[192,384]{1,0:T(8,128)(2,1)S(1)}, bf16[192,384]{1,0:T(8,128)(2,1)S(1)}, u32[]{:S(2)}, u32[]{:S(2)}) collective-permute-start(bf16[192,384]{1,0:T(8,128)(2,1)S(1)} %get-tuple-element.60), channel_id=1, source_target_pairs={{0,6},{2,4},{4,2},{6,0},{8,14},{10,12},{12,10},{14,8},{16,22},{18,... | collective-permute-start | bytes 442376 | tf_op jit(solution)/shard_map/ppermute | solution.py:370
  36.4 4.8 %collective-permute-start.18 = (bf16[192,128]{1,0:T(8,128)(2,1)S(1)}, bf16[192,128]{1,0:T(8,128)(2,1)S(1)}, u32[]{:S(2)}, u32[]{:S(2)}) collective-permute-start(bf16[192,128]{1,0:T(8,128)(2,1)S(1)} %get-tuple-element.68), channel_id=1, source_target_pairs={{0,2},{2,0},{4,6},{6,4},{8,10},{10,8},{12,14},{14,12},{16,18},{18,... | collective-permute-start | bytes 147464 | tf_op jit(solution)/shard_map/ppermute | solution.py:370
  38.4 4.5 %collective-permute-start.19 = (bf16[192,128]{1,0:T(8,128)(2,1)S(1)}, bf16[192,128]{1,0:T(8,128)(2,1)S(1)}, u32[]{:S(2)}, u32[]{:S(2)}) collective-permute-start(bf16[192,128]{1,0:T(8,128)(2,1)S(1)} %get-tuple-element.69), channel_id=1, source_target_pairs={{0,4},{2,6},{4,0},{6,2},{8,12},{10,14},{12,8},{14,10},{16,20},{18,... | collective-permute-start | bytes 147464 | tf_op jit(solution)/shard_map/ppermute | solution.py:370
  39.3 5.0 %collective-permute-start.20 = (bf16[192,128]{1,0:T(8,128)(2,1)S(1)}, bf16[192,128]{1,0:T(8,128)(2,1)S(1)}, u32[]{:S(2)}, u32[]{:S(2)}) collective-permute-start(bf16[192,128]{1,0:T(8,128)(2,1)S(1)} %get-tuple-element.70), channel_id=1, source_target_pairs={{0,6},{2,4},{4,2},{6,0},{8,14},{10,12},{12,10},{14,8},{16,22},{18,... | collective-permute-start | bytes 147464 | tf_op jit(solution)/shard_map/ppermute | solution.py:370
  40.4 8.5 %collective-permute-start.21 = (bf16[6,8,16,128]{3,2,1,0:T(8,128)(2,1)S(1)}, bf16[6,8,16,128]{3,2,1,0:T(8,128)(2,1)S(1)}, u32[]{:S(2)}, u32[]{:S(2)}) collective-permute-start(bf16[6,8,16,128]{3,2,1,0:T(8,128)(2,1)S(1)} %get-tuple-element.73), channel_id=1, source_target_pairs={{0,8},{2,10},{4,12},{6,14},{8,0},{10,2},{12,4},{14,6},{16,24},{18,... | collective-permute-start | bytes 589832 | tf_op jit(solution)/shard_map/ppermute | solution.py:370
  44.4 6.3 %collective-permute-start.22 = (bf16[48,512]{1,0:T(8,128)(2,1)S(1)}, bf16[48,512]{1,0:T(8,128)(2,1)S(1)}, u32[]{:S(2)}, u32[]{:S(2)}) collective-permute-start(bf16[48,512]{1,0:T(8,128)(2,1)S(1)} %get-tuple-element.76), channel_id=1, source_target_pairs={{0,8},{2,10},{4,12},{6,14},{8,0},{10,2},{12,4},{14,6},{16,24},{18,... | collective-permute-start | bytes 147464 | tf_op jit(solution)/shard_map/ppermute | solution.py:370
  45.4 5.3 %collective-permute-start.23 = (bf16[48,512]{1,0:T(8,128)(2,1)S(1)}, bf16[48,512]{1,0:T(8,128)(2,1)S(1)}, u32[]{:S(2)}, u32[]{:S(2)}) collective-permute-start(bf16[48,512]{1,0:T(8,128)(2,1)S(1)} %get-tuple-element.77), channel_id=1, source_target_pairs={{0,16},{2,18},{4,20},{6,22},{8,24},{10,26},{12,28},{14,30},{16,0},... | collective-permute-start | bytes 147464 | tf_op jit(solution)/shard_map/ppermute | solution.py:370
  47.4 5.9 %collective-permute-start.24 = (bf16[48,512]{1,0:T(8,128)(2,1)S(1)}, bf16[48,512]{1,0:T(8,128)(2,1)S(1)}, u32[]{:S(2)}, u32[]{:S(2)}) collective-permute-start(bf16[48,512]{1,0:T(8,128)(2,1)S(1)} %get-tuple-element.78), channel_id=1, source_target_pairs={{0,24},{2,26},{4,28},{6,30},{8,16},{10,18},{12,20},{14,22},{16,8},... | collective-permute-start | bytes 147464 | tf_op jit(solution)/shard_map/ppermute | solution.py:370
  53.3 1.5 %collective-permute-start.25 = (f32[48,896]{1,0:T(8,128)S(1)}, f32[48,896]{1,0:T(8,128)S(1)}, u32[]{:S(2)}, u32[]{:S(2)}) collective-permute-start(f32[48,896]{1,0:T(8,128)S(1)} %line_sum.1.mine_ref), channel_id=1, source_target_pairs={{0,1},{1,0},{2,3},{3,2},{4,5},{5,4},{6,7},{7,6},{8,9},{9,8},{10,11... | collective-permute-start | bytes 516104 | tf_op jit(solution)/shard_map/ppermute | solution.py:373

commit v9 on v8

--- a/solution.py
+++ b/solution.py
@@ -78,7 +78,7 @@
     return sums
 
 
-def pack_kernel(w_ref, dw_ref, gain_ref, bias_ref, near_ref, far_ref, turned, wide):
+def pack_kernel(w_ref, dw_ref, gain_ref, bias_ref, home_ref, near_ref, far_ref, turned, wide):
     own, hidden = w_ref.shape
     quarter = hidden // 4
     side = lax.axis_index("rep") % 2
@@ -89,8 +89,9 @@
     wide[...] = jnp.zeros_like(wide)
     wide[:, :TAPS] = dw_ref[...].astype(F32)
     extras = (wide[...] + turned[...].T[:own]).astype(BF16)
-    for ref, which in ((near_ref, parity), (far_ref, 1 - parity)):
-        start = pl.multiple_of(side * (2 * quarter) + which * quarter, LANES)
+    kinds = ((home_ref, side, parity), (near_ref, 1 - side, parity), (far_ref, 1 - side, 1 - parity))
+    for ref, place, which in kinds:
+        start = pl.multiple_of(place * (2 * quarter) + which * quarter, LANES)
         ref[:, :quarter] = w_ref[:, pl.ds(start, quarter)]
         ref[:, quarter:] = extras
 
@@ -101,60 +102,89 @@
     quarter = weight_ref.shape[1]
     for line, piece in enumerate(pieces):
         weight_ref[line * own : (line + 1) * own, :] = piece[:, :quarter]
-        extra_ref[line * own : (line + 1) * own, :] = piece[:, quarter:]
+    extras = jnp.concatenate([piece[:, quarter:].astype(F32) for piece in pieces], axis=0)
+    if extra_ref.shape[0] < extras.shape[0]:
+        extras = fold(extras)
+    extra_ref[...] = extras.astype(BF16)
 
 
 def plane_sum_kernel(lines, *refs):
     pieces, small, outs = refs[:INNER], refs[INNER : 2 * INNER], refs[2 * INNER :]
     own = pieces[0].shape[0] // lines
     quarter = pieces[0].shape[1]
+    extras = small[0][...]
+    for part in small[1:]:
+        extras = extras + part[...].astype(F32)
+    if extras.shape[0] < pieces[0].shape[0]:
+        extras = unfold(extras)
     for line, out in enumerate(outs):
         rows = slice(line * own, (line + 1) * own)
-        for parts, columns in ((pieces, slice(0, quarter)), (small, slice(quarter, None))):
-            total = parts[0][rows, :]
-            for part in parts[1:]:
-                total = total + part[rows, :].astype(F32)
-            out[:, columns] = total.astype(out.dtype)
+        total = pieces[0][rows, :]
+        for part in pieces[1:]:
+            total = total + part[rows, :].astype(F32)
+        out[:, :quarter] = total.astype(out.dtype)
+        out[:, quarter:] = extras[rows, :].astype(out.dtype)
 
 
 def line_sum_kernel(*refs):
     pieces, total_ref = refs[:-1], refs[-1]
     quarter = pieces[0].shape[1] - LANES
-    same, cross = pieces[0][...], None
-    for line, piece in enumerate(pieces):
+    near, far = None, None
+    for line, piece in enumerate(pieces[1:], 1):
+        came = piece[...].astype(F32)
         if line % 2:
-            cross = piece[...].astype(F32) if cross is None else cross + piece[...].astype(F32)
-        elif line:
-            same = same + piece[...].astype(F32)
-    total_ref[:, :quarter] = same[:, :quarter]
-    total_ref[:, quarter : 2 * quarter] = cross[:, :quarter]
-    total_ref[:, 2 * quarter :] = same[:, quarter:] + cross[:, quarter:]
+            far = came if far is None else far + came
+        else:
+            near = came if near is None else near + came
+    total_ref[:, :quarter] = pieces[0][:, :quarter]
+    total_ref[:, quarter : 2 * quarter] = near[:, :quarter]
+    total_ref[:, 2 * quarter : 3 * quarter] = far[:, :quarter]
+    total_ref[:, 3 * quarter :] = pieces[0][:, quarter:] + near[:, quarter:] + far[:, quarter:]
 
 
 def finish_kernel(factor, mine_ref, other_ref, up_ref, dw_ref, gain_ref, bias_ref):
-    own, half = mine_ref.shape[0], mine_ref.shape[1] - LANES
-    quarter = half // 2
+    own, quarter = mine_ref.shape[0], (mine_ref.shape[1] - LANES) // 3
     side = lax.axis_index("rep") % 2
     parity = (lax.axis_index("shard") // INNER) % 2
-    for ref, place in ((mine_ref, side), (other_ref, 1 - side)):
-        for which, low in ((parity, 0), (1 - parity, quarter)):
-            start = pl.multiple_of(place * half + which * quarter, LANES)
-            up_ref[:, pl.ds(start, quarter)] = ref[:, low : low + quarter] * factor
-    sums = (mine_ref[:, half:] + other_ref[:, half:]) * factor
+    for place, home, came in ((side, mine_ref, other_ref), (1 - side, other_ref, mine_ref)):
+        start = pl.multiple_of((2 * place + parity) * quarter, LANES)
+        total = home[:, :quarter] + came[:, quarter : 2 * quarter]
+        up_ref[:, pl.ds(start, quarter)] = total * factor
+        start = pl.multiple_of((2 * place + 1 - parity) * quarter, LANES)
+        up_ref[:, pl.ds(start, quarter)] = came[:, 2 * quarter : 3 * quarter] * factor
+    low = 3 * quarter
+    sums = (mine_ref[:, low:] + other_ref[:, low:]) * factor
     dw_ref[...] = sums[:, :TAPS]
     turned = sums.T
     gain_ref[...] = turned[TAPS : TAPS + 1, :]
     bias_ref[...] = turned[TAPS + 1 : TAPS + 2, :]
 
 
+def fold(rows):
+    half = rows.shape[0] // 2
+    low = lax.broadcasted_iota(jnp.int32, (half, LANES), 1) < LANES // 2
+    return jnp.where(low, rows[:half], pltpu.roll(rows[half:], LANES // 2, 1))
+
+
+def unfold(rows):
+    return jnp.concatenate([rows, pltpu.roll(rows, LANES // 2, 1)], axis=0)
+
+
 def conv_norm_kernel(relative, own, *refs):
     small = refs[:INNER]
     sources = refs[INNER : INNER + 2]
     x_ref = sources[0]
-    normed_ref, white_ref, inv_ref, taps_ref, gathered, padded, conv = refs[INNER + 2 :]
+    normed_ref, white_ref, inv_ref, taps_ref, gathered, unfolded, padded, conv = refs[INNER + 2 :]
     height, breadth, depth = x_ref.shape[1:]
     tiles = depth // LANES
     pixels = height * breadth
+    if relative:
+        for group, piece in enumerate(small):
+            unfolded[group * 2 * piece.shape[0] : (group + 1) * 2 * piece.shape[0], :] = unfold(
+                piece[...].astype(F32)
+            )
+        count = unfolded.shape[0] // INNER
+        small = [unfolded.at[pl.ds(group * count, count), :] for group in range(INNER)]
     place_rows(small, gathered, own, relative, F32)
     padded[...] = jnp.zeros_like(padded)
     for tile in range(tiles):
@@ -255,7 +285,7 @@
 def norm_back_kernel(relative, own, *refs):
     gn_own, gn_other, white_ref, inv_ref, taps_ref, x_ref, far_ref = refs[:7]
     pieces = refs[7 : 7 + INNER]
-    grad_ref, sent_ref, padded, grads_ref, rows, small = refs[7 + INNER :]
+    grad_ref, sent_ref, padded, grads_ref, rows, small, unfolded = refs[7 + INNER :]
     height, breadth, depth = x_ref.shape[1:]
     tiles = depth // LANES
     pixels = height * breadth
@@ -312,7 +342,13 @@
     lax.fori_loop(0, tiles, one_tile, 0)
     for tile in range(tiles):
         small[tile * LANES : (tile + 1) * LANES, :] = rows[tile].T
-    split_rows(small, pieces, own, relative)
+    if relative:
+        whole = [unfolded.at[group] for group in range(INNER)]
+        split_rows(small, whole, own, relative)
+        for source, piece in zip(whole, pieces):
+            piece[...] = fold(source[...]).astype(piece.dtype)
+    else:
+        split_rows(small, pieces, own, relative)
 
 
 def conv_back_kernel(grad_ref, other_ref, taps_ref, out_ref, padded):
@@ -369,6 +405,12 @@
     def over_shard(array, flip):
         return lax.ppermute(array, "shard", [(i, i ^ flip) for i in range(shards)])
 
+    def crossing(array, flip):
+        pairs = [
+            (i * reps + r, (i ^ flip) * reps + (r ^ 1)) for i in range(shards) for r in range(reps)
+        ]
+        return lax.ppermute(array, ("shard", "rep"), pairs)
+
     def over_core(array):
         return lax.ppermute(array, "rep", [(i, i ^ 1) for i in range(reps)])
 
@@ -389,10 +431,10 @@
         return [moved[0]] + [moved[i].astype(BF16) for i in range(1, INNER)]
 
     shape = jax.ShapeDtypeStruct
-    near, far = call(
+    home, near, far = call(
         pack_kernel,
         "pack",
-        [shape((own, quarter + LANES), BF16)] * 2,
+        [shape((own, quarter + LANES), BF16)] * 3,
         [
             pltpu.VMEM((LANES, LANES), F32),
             pltpu.VMEM((own, LANES), F32),
@@ -404,9 +446,11 @@
         norm_bias[None, :],
         mebibytes=63,
     )
-    near, far, images, cotangent = lax.optimization_barrier((near, far, images, cotangent))
-    gathered = [near] + [
-        over_shard(far if line % 2 else near, INNER * line) for line in range(1, lines)
+    home, near, far, images, cotangent = lax.optimization_barrier(
+        (home, near, far, images, cotangent)
+    )
+    gathered = [home] + [
+        crossing(far if line % 2 else near, INNER * line) for line in range(1, lines)
     ]
     cotangent = cotangent.reshape(pixels, hidden)
     cot_across, cot_sibling = call(
@@ -417,20 +461,21 @@
         0.4,
         cotangent,
     )
-    cot_across, cot_sibling = over_shard(cot_across, INNER), over_core(cot_sibling)
-    images_far = over_shard(images, INNER)
+    cot_across, cot_sibling = crossing(cot_across, INNER), over_core(cot_sibling)
+    images_far = crossing(images, INNER)
 
     rows = lines * own
+    folded = rows // 2 if relative else rows
     weight_lines, extra_lines = call(
         assemble_kernel,
         "assemble",
-        [shape((rows, quarter), BF16), shape((rows, LANES), BF16)],
+        [shape((rows, quarter), BF16), shape((folded, LANES), BF16)],
         [],
         2.0,
         *gathered,
     )
     weights = [weight_lines] + [over_shard(weight_lines, flip) for flip in range(1, INNER)]
-    extras = [extra_lines] + [over_shard(extra_lines, flip) for flip in range(1, INNER)]
+    extras = [extra_lines] + [crossing(extra_lines, flip) for flip in range(1, INNER)]
     weights, extras = true_order(weights), true_order(extras)
     (weight,) = call(
         functools.partial(order_kernel, relative, own),
@@ -452,6 +497,7 @@
             shape((tiles, LANES, LANES), F32),
         ],
         [
+            pltpu.VMEM((depth, LANES), F32),
             pltpu.VMEM((depth, LANES), F32),
             padded,
             pltpu.VMEM((tiles, pixels, LANES), F32),
@@ -497,8 +543,8 @@
     *small, grad_conv, grad_sent = call(
         functools.partial(norm_back_kernel, relative, own),
         "norm_back",
-        [shape((rows, LANES), F32)]
-        + [shape((rows, LANES), BF16)] * (INNER - 1)
+        [shape((folded, LANES), F32)]
+        + [shape((folded, LANES), BF16)] * (INNER - 1)
         + [
             shape((tiles, height, breadth, LANES), F32),
             shape((tiles, height, breadth, LANES), BF16),
@@ -508,6 +554,7 @@
             pltpu.VMEM((2, tiles, height, breadth, LANES), F32),
             pltpu.VMEM((tiles, LANES, LANES), F32),
             pltpu.VMEM((depth, LANES), F32),
+            pltpu.VMEM((INNER, rows, LANES), F32),
         ],
         0.1,
         gn_kept,
@@ -519,8 +566,8 @@
         images_far,
     )
     small = relative_order(small)
-    small_arrived = [over_shard(piece, flip) for flip, piece in enumerate(small) if flip]
-    grad_other = over_shard(grad_sent, INNER)
+    small_arrived = [crossing(piece, flip) for flip, piece in enumerate(small) if flip]
+    grad_other = crossing(grad_sent, INNER)
     (grad_images,) = call(
         conv_back_kernel,
         "conv_back",
@@ -544,11 +591,11 @@
         *small_arrived,
     )
     home, grad_images = lax.optimization_barrier((home, grad_images))
-    came = [over_shard(piece, INNER * line) for line, piece in enumerate(sent, 1)]
+    came = [crossing(piece, INNER * line) for line, piece in enumerate(sent, 1)]
     (total,) = call(
         line_sum_kernel,
         "line_sum",
-        [shape((own, half + LANES), F32)],
+        [shape((own, 3 * quarter + LANES), F32)],
         [],
         0.3,
         home,

time: 55.7 us -> 54.6 us (0.980)
  starting transfers between devices: 27.8 us -> 25.3 us
  waiting for transfers between devices: 14.4 us -> 15.1 us
  Pallas kernels: 12.6 us -> 13.2 us
    ppermute x21 -> x6, starting transfers between devices: 26.8 us -> 7.04 us  [over_shard(): return lax.ppermute(array, 'shard', [(i, i ^ flip) for i in range(shards)])]
    ppermute x0 -> x15, starting transfers between devices: none -> 17.5 us  [crossing(): return lax.ppermute(array, ('shard', 'rep'), pairs)]
    ppermute x0 -> x15, waiting for transfers between devices: none -> 9.19 us  [crossing(): return lax.ppermute(array, ('shard', 'rep'), pairs)]
    ppermute x21 -> x6, waiting for transfers between devices: 12.9 us -> 4.4 us  [over_shard(): return lax.ppermute(array, 'shard', [(i, i ^ flip) for i in range(shards)])]
    pallas_call x12, Pallas kernels: 12.6 us -> 13.2 us  [call(): pl.pallas_call(kernel, out_shape=outs, in_specs=[VMEM] * len(args), out_s...]
  transfers between devices with their start and end apart: 26 -> 26, of which waited for: 13 -> 12; matrix products, arithmetic and copies ran while one was open for 0% -> 0% of each run, Pallas kernels for 14% -> 16%
where the time goes in v9:
time: 54.6 us; the launch traced here: 54.4 us
  starting transfers between devices  25.3 us (46%)
  waiting for transfers between devices  15.1 us (28%)
  Pallas kernels  13.2 us (24%)
  between operations  0.77 us (1%)
    ppermute x15, starting transfers between devices, crossing(): return lax.ppermute(array, ('shard', 'rep'), pairs)  17.5 us
    pallas_call x12, Pallas kernels, call(): pl.pallas_call(kernel, out_shape=outs, in_specs=[VMEM] * len(args), out_s...  13.2 us
    ppermute x15, waiting for transfers between devices, crossing(): return lax.ppermute(array, ('shard', 'rep'), pairs)  9.19 us
    ppermute x6, starting transfers between devices, over_shard(): return lax.ppermute(array, 'shard', [(i, i ^ flip) for i in range(shards)])  7.04 us
    ppermute x6, waiting for transfers between devices, over_shard(): return lax.ppermute(array, 'shard', [(i, i ^ flip) for i in range(shards)])  4.4 us
    ppermute x5, waiting for transfers between devices, over_core(): return lax.ppermute(array, 'rep', [(i, i ^ 1) for i in range(reps)])  1.46 us
  transfers between devices with their start and end apart: 26, of which 12 were waited for; matrix products, arithmetic and copies ran while one was open for 0% of the time, Pallas kernels for 16%

profile of v9, /device:TPU:0, one launch (start us, length us, event | category | flops | bytes accessed | tf_op | source)
XLA Modules:
  0.0 54.4 jit_solution(17176696019637408398)
XLA Ops:
  0.6 0.0 copy-start
  0.6 0.0 copy-start.1
  0.7 1.7 %pack.1 = (bf16[48,512]{1,0:T(8,128)(2,1)}, bf16[48,512]{1,0:T(8,128)(2,1)}, bf16[48,512]{1,0:T(8,128)(2,1)}) custom-call(bf16[48,1536]{1,0:T(8,128)(2,1)} %w_ref.1, bf16[48,49]{1,0:T(8,128)(2,1)} %dw_ref.1, bf16[1,48]{1,0:T(2,128)(2,1)} %bitcast.7, bf16[1,48]{1,0:T(2,128)(2,1)} %bitcast.8), custom_call_target="tpu_custom_call" | custom-call | flops 550000000 | bytes 299808 | tf_op jit(solution)/shard_map/pack/pallas_call | solution.py:379
  2.4 3.5 %collective-permute-start.1 = (bf16[48,512]{1,0:T(8,128)(2,1)}, bf16[48,512]{1,0:T(8,128)(2,1)S(1)}, u32[]{:S(2)}, u32[]{:S(2)}) collective-permute-start(bf16[48,512]{1,0:T(8,128)(2,1)} %get-tuple-element.51), channel_id=1, source_target_pairs={{0,17},{1,16},{2,19},{3,18},{4,21},{5,20},{6,23},{7,22},{8,25},{9,... | collective-permute-start | bytes 147464 | tf_op jit(solution)/shard_map/ppermute | solution.py:412
  5.9 1.6 %collective-permute-start.2 = (bf16[48,512]{1,0:T(8,128)(2,1)}, bf16[48,512]{1,0:T(8,128)(2,1)S(1)}, u32[]{:S(2)}, u32[]{:S(2)}) collective-permute-start(bf16[48,512]{1,0:T(8,128)(2,1)} %get-tuple-element.50), channel_id=1, source_target_pairs={{0,25},{1,24},{2,27},{3,26},{4,29},{5,28},{6,31},{7,30},{8,17},{9,... | collective-permute-start | bytes 147464 | tf_op jit(solution)/shard_map/ppermute | solution.py:412
  7.5 0.2 collective-permute-start
  7.7 1.5 %collective-permute-start.9 = (bf16[1,8,16,768]{3,2,1,0:T(8,128)(2,1)S(1)}, bf16[1,8,16,768]{3,2,1,0:T(8,128)(2,1)S(1)}, u32[]{:S(2)}, u32[]{:S(2)}) collective-permute-start(bf16[1,8,16,768]{3,2,1,0:T(8,128)(2,1)S(1)} %copy-done), channel_id=1, source_target_pairs={{0,9},{1,8},{2,11},{3,10},{4,13},{5,12},{6,15},{7,14},{8,1},{9,0},... | collective-permute-start | bytes 589832 | tf_op jit(solution)/shard_map/ppermute | solution.py:412
  9.3 0.3 collective-permute-start.10
  9.6 0.0 collective-permute-done.1.refs_2_
  9.6 1.9 %collective-permute-done.2.refs_3_ = bf16[48,512]{1,0:T(8,128)(2,1)S(1)} collective-permute-done((bf16[48,512]{1,0:T(8,128)(2,1)}, bf16[48,512]{1,0:T(8,128)(2,1)S(1)}, u32[]{:S(2)}, u32[]{:S(2)}) %collective-permute-start.2) | collective-permute-done | bytes 49184 | tf_op jit(solution)/shard_map/ppermute | solution.py:412
  11.5 1.0 %collective-permute-done.refs_1_ = bf16[48,512]{1,0:T(8,128)(2,1)S(1)} collective-permute-done((bf16[48,512]{1,0:T(8,128)(2,1)}, bf16[48,512]{1,0:T(8,128)(2,1)S(1)}, u32[]{:S(2)}, u32[]{:S(2)}) %collective-permute-start) | collective-permute-done | bytes 49184 | tf_op jit(solution)/shard_map/ppermute | solution.py:412
  12.4 0.1 assemble.1
  12.5 2.8 %collective-permute-start.8 = (bf16[96,128]{1,0:T(8,128)(2,1)S(1)}, bf16[96,128]{1,0:T(8,128)(2,1)S(1)}, u32[]{:S(2)}, u32[]{:S(2)}) collective-permute-start(bf16[96,128]{1,0:T(8,128)(2,1)S(1)} %get-tuple-element.53.refs_0_), channel_id=1, source_target_pairs={{0,7},{1,6},{2,5},{3,4},{4,3},{5,2},{6,1},{7,0},{8,15},{9,14},{10,... | collective-permute-start | bytes 73736 | tf_op jit(solution)/shard_map/ppermute | solution.py:412
  15.3 0.0 collective-permute-start.7
  15.3 0.8 %collective-permute-start.6 = (bf16[96,128]{1,0:T(8,128)(2,1)S(1)}, bf16[96,128]{1,0:T(8,128)(2,1)S(1)}, u32[]{:S(2)}, u32[]{:S(2)}) collective-permute-start(bf16[96,128]{1,0:T(8,128)(2,1)S(1)} %get-tuple-element.53.refs_0_), channel_id=1, source_target_pairs={{0,3},{1,2},{2,1},{3,0},{4,7},{5,6},{6,5},{7,4},{8,11},{9,10},{10,... | collective-permute-start | bytes 73736 | tf_op jit(solution)/shard_map/ppermute | solution.py:412
  16.1 0.8 %collective-permute-done.8.refs_3_ = bf16[96,128]{1,0:T(8,128)(2,1)S(1)} collective-permute-done((bf16[96,128]{1,0:T(8,128)(2,1)S(1)}, bf16[96,128]{1,0:T(8,128)(2,1)S(1)}, u32[]{:S(2)}, u32[]{:S(2)}) %collective-permute-start.8) | collective-permute-done | bytes 24608 | tf_op jit(solution)/shard_map/ppermute | solution.py:412
  16.9 2.4 %collective-permute-start.5 = (bf16[192,384]{1,0:T(8,128)(2,1)S(1)}, bf16[192,384]{1,0:T(8,128)(2,1)S(1)}, u32[]{:S(2)}, u32[]{:S(2)}) collective-permute-start(bf16[192,384]{1,0:T(8,128)(2,1)S(1)} %get-tuple-element.52.refs_0_), channel_id=1, source_target_pairs={{0,6},{2,4},{4,2},{6,0},{8,14},{10,12},{12,10},{14,8},{16,22},{18,... | collective-permute-start | bytes 442376 | tf_op jit(solution)/shard_map/ppermute | solution.py:406
  19.3 0.0 collective-permute-done.7.refs_2_
  19.3 0.4 collective-permute-start.4
  19.7 0.0 collective-permute-done.6.refs_1_
  19.7 0.7 %collective-permute-start.3 = (bf16[192,384]{1,0:T(8,128)(2,1)S(1)}, bf16[192,384]{1,0:T(8,128)(2,1)S(1)}, u32[]{:S(2)}, u32[]{:S(2)}) collective-permute-start(bf16[192,384]{1,0:T(8,128)(2,1)S(1)} %get-tuple-element.52.refs_0_), channel_id=1, source_target_pairs={{0,2},{2,0},{4,6},{6,4},{8,10},{10,8},{12,14},{14,12},{16,18},{18,... | collective-permute-start | bytes 442376 | tf_op jit(solution)/shard_map/ppermute | solution.py:406
  20.4 0.0 collective-permute-done.9.refs_5_.refs_6_
  20.4 3.2 %conv_norm.1 = (bf16[256,768]{1,0:T(8,128)(2,1)S(1)}, f32[256,768]{1,0:T(8,128)S(1)}, f32[256,128]{1,0:T(8,128)S(1)}, f32[6,128,128]{2,1,0:T(8,128)S(1)}) custom-call(bf16[96,128]{1,0:T(8,128)(2,1)S(1)} %get-tuple-element.53.refs_0_, bf16[96,128]{1,0:T(8,128)(2,1)S(1)} %collective-permute-done.6.refs_1_, bf16[96,128]{1,0:T(8,128)(2,1)S(1)} %collective-permute-done.7.refs_2_, ...), custom_call_target="tpu_custom_call" | custom-call | flops 110000000 | bytes 2195456 | tf_op jit(solution)/shard_map/conv_norm/pallas_call | solution.py:379
  23.6 0.0 collective-permute-done.10.refs_5_
  23.6 0.1 collective-permute-start.11
  23.7 0.5 collective-permute-start.12
  24.2 0.2 collective-permute-done.5.refs_3_
  24.4 0.0 collective-permute-start.13
  24.4 2.8 %collective-permute-done.4.refs_2_ = bf16[192,384]{1,0:T(8,128)(2,1)S(1)} collective-permute-done((bf16[192,384]{1,0:T(8,128)(2,1)S(1)}, bf16[192,384]{1,0:T(8,128)(2,1)S(1)}, u32[]{:S(2)}, u32[]{:S(2)}) %collective-permute-start.4) | collective-permute-done | bytes 147488 | tf_op jit(solution)/shard_map/ppermute | solution.py:406
  27.3 0.2 collective-permute-done.3.refs_1_
  27.5 0.1 order.1.refs_0_.weight
  27.5 0.0 collective-permute-done.12.refs_4_
  27.5 0.0 collective-permute-done.13.refs_6_
  27.6 0.0 collective-permute-done.11.refs_2_
  27.6 1.5 %project.1 = (f32[192,384]{1,0:T(8,128)S(1)}, bf16[192,384]{1,0:T(8,128)(2,1)S(1)}, bf16[192,384]{1,0:T(8,128)(2,1)S(1)}, bf16[192,384]{1,0:T(8,128)(2,1)S(1)}, bf16[512,384]{1,0:T(8,128)(2,1)S(1)}) custom-call(bf16[768,384]{1,0:T(8,128)(2,1)S(1)} %order.1.refs_0_.weight, bf16[256,768]{1,0:T(8,128)(2,1)S(1)} %get-tuple-element.58.refs_1_, ...), custom_call_target="tpu_custom_call" | custom-call | flops 1760000000 | bytes 3489792 | tf_op jit(solution)/shard_map/project/pallas_call | solution.py:379
  29.1 0.6 %back_project.1 = (f32[256,768]{1,0:T(8,128)S(1)}, f32[256,768]{1,0:T(8,128)S(1)}) custom-call(bf16[768,384]{1,0:T(8,128)(2,1)S(1)} %order.1.refs_0_.weight, bf16[512,384]{1,0:T(8,128)(2,1)S(1)} %get-tuple-element.65.gp_ref), custom_call_target="tpu_custom_call" | custom-call | flops 770000000 | bytes 2555904 | tf_op jit(solution)/shard_map/back_project/pallas_call | solution.py:379
  29.7 0.1 collective-permute-start.17
  29.8 1.6 %collective-permute-start.14 = (bf16[192,384]{1,0:T(8,128)(2,1)S(1)}, bf16[192,384]{1,0:T(8,128)(2,1)S(1)}, u32[]{:S(2)}, u32[]{:S(2)}) collective-permute-start(bf16[192,384]{1,0:T(8,128)(2,1)S(1)} %get-tuple-element.62), channel_id=1, source_target_pairs={{0,2},{2,0},{4,6},{6,4},{8,10},{10,8},{12,14},{14,12},{16,18},{18,... | collective-permute-start | bytes 442376 | tf_op jit(solution)/shard_map/ppermute | solution.py:406
  31.4 0.5 collective-permute-start.15
  32.0 1.4 %collective-permute-start.16 = (bf16[192,384]{1,0:T(8,128)(2,1)S(1)}, bf16[192,384]{1,0:T(8,128)(2,1)S(1)}, u32[]{:S(2)}, u32[]{:S(2)}) collective-permute-start(bf16[192,384]{1,0:T(8,128)(2,1)S(1)} %get-tuple-element.64), channel_id=1, source_target_pairs={{0,6},{2,4},{4,2},{6,0},{8,14},{10,12},{12,10},{14,8},{16,22},{18,... | collective-permute-start | bytes 442376 | tf_op jit(solution)/shard_map/ppermute | solution.py:406
  33.3 0.0 collective-permute-done.17.refs_1_
  33.3 3.2 %norm_back.1 = (f32[96,128]{1,0:T(8,128)S(1)}, bf16[96,128]{1,0:T(8,128)(2,1)S(1)}, bf16[96,128]{1,0:T(8,128)(2,1)S(1)}, bf16[96,128]{1,0:T(8,128)(2,1)S(1)}, f3...) custom-call(f32[256,768]{1,0:T(8,128)S(1)} %get-tuple-element.66.refs_0_, ...), custom_call_target="tpu_custom_call" | custom-call | flops 110000000 | bytes 3989504 | tf_op jit(solution)/shard_map/norm_back/pallas_call | solution.py:379
  36.5 0.9 %collective-permute-start.18 = (bf16[96,128]{1,0:T(8,128)(2,1)S(1)}, bf16[96,128]{1,0:T(8,128)(2,1)S(1)}, u32[]{:S(2)}, u32[]{:S(2)}) collective-permute-start(bf16[96,128]{1,0:T(8,128)(2,1)S(1)} %get-tuple-element.72), channel_id=1, source_target_pairs={{0,3},{1,2},{2,1},{3,0},{4,7},{5,6},{6,5},{7,4},{8,11},{9,10},{10,... | collective-permute-start | bytes 73736 | tf_op jit(solution)/shard_map/ppermute | solution.py:412
  37.4 1.0 %collective-permute-start.19 = (bf16[96,128]{1,0:T(8,128)(2,1)S(1)}, bf16[96,128]{1,0:T(8,128)(2,1)S(1)}, u32[]{:S(2)}, u32[]{:S(2)}) collective-permute-start(bf16[96,128]{1,0:T(8,128)(2,1)S(1)} %get-tuple-element.73), channel_id=1, source_target_pairs={{0,5},{1,4},{2,7},{3,6},{4,1},{5,0},{6,3},{7,2},{8,13},{9,12},{10,... | collective-permute-start | bytes 73736 | tf_op jit(solution)/shard_map/ppermute | solution.py:412
  38.4 0.0 collective-permute-done.14.refs_1_
  38.4 1.0 %collective-permute-start.20 = (bf16[96,128]{1,0:T(8,128)(2,1)S(1)}, bf16[96,128]{1,0:T(8,128)(2,1)S(1)}, u32[]{:S(2)}, u32[]{:S(2)}) collective-permute-start(bf16[96,128]{1,0:T(8,128)(2,1)S(1)} %get-tuple-element.74), channel_id=1, source_target_pairs={{0,7},{1,6},{2,5},{3,4},{4,3},{5,2},{6,1},{7,0},{8,15},{9,14},{10,... | collective-permute-start | bytes 73736 | tf_op jit(solution)/shard_map/ppermute | solution.py:412
  39.4 1.1 %collective-permute-done.15.refs_2_ = bf16[192,384]{1,0:T(8,128)(2,1)S(1)} collective-permute-done((bf16[192,384]{1,0:T(8,128)(2,1)S(1)}, bf16[192,384]{1,0:T(8,128)(2,1)S(1)}, u32[]{:S(2)}, u32[]{:S(2)}) %collective-permute-start.15) | collective-permute-done | bytes 147488 | tf_op jit(solution)/shard_map/ppermute | solution.py:406
  40.6 0.0 collective-permute-start.21
  40.6 0.0 collective-permute-done.16.refs_3_
  40.6 0.0 collective-permute-done.18.refs_5_
  40.6 0.2 collective-permute-done.19.refs_6_
  40.8 2.0 %collective-permute-done.20.refs_7_ = bf16[96,128]{1,0:T(8,128)(2,1)S(1)} collective-permute-done((bf16[96,128]{1,0:T(8,128)(2,1)S(1)}, bf16[96,128]{1,0:T(8,128)(2,1)S(1)}, u32[]{:S(2)}, u32[]{:S(2)}) %collective-permute-start.20) | collective-permute-done | bytes 24608 | tf_op jit(solution)/shard_map/ppermute | solution.py:412
  42.8 0.1 plane_sum.1
  42.9 0.2 collective-permute-start.22
  43.0 2.9 %collective-permute-start.23 = (bf16[48,512]{1,0:T(8,128)(2,1)S(1)}, bf16[48,512]{1,0:T(8,128)(2,1)S(1)}, u32[]{:S(2)}, u32[]{:S(2)}) collective-permute-start(bf16[48,512]{1,0:T(8,128)(2,1)S(1)} %get-tuple-element.81), channel_id=1, source_target_pairs={{0,17},{1,16},{2,19},{3,18},{4,21},{5,20},{6,23},{7,22},{8,25},{9,... | collective-permute-start | bytes 147464 | tf_op jit(solution)/shard_map/ppermute | solution.py:412
  45.9 0.9 %collective-permute-start.24 = (bf16[48,512]{1,0:T(8,128)(2,1)S(1)}, bf16[48,512]{1,0:T(8,128)(2,1)S(1)}, u32[]{:S(2)}, u32[]{:S(2)}) collective-permute-start(bf16[48,512]{1,0:T(8,128)(2,1)S(1)} %get-tuple-element.82), channel_id=1, source_target_pairs={{0,25},{1,24},{2,27},{3,26},{4,29},{5,28},{6,31},{7,30},{8,17},{9,... | collective-permute-start | bytes 147464 | tf_op jit(solution)/shard_map/ppermute | solution.py:412
  46.8 2.0 %collective-permute-done.21.other_ref = bf16[6,8,16,128]{3,2,1,0:T(8,128)(2,1)S(1)} collective-permute-done((bf16[6,8,16,128]{3,2,1,0:T(8,128)(2,1)S(1)}, bf16[6,8,16,128]{3,2,1,0:T(8,128)(2,1)S(1)}, u32[]{:S(2)}, u32[]{:S(2)}) %collective-permute-start.21) | collective-permute-done | bytes 196640 | tf_op jit(solution)/shard_map/ppermute | solution.py:412
  48.7 1.9 %conv_back.1 = bf16[1,8,16,768]{3,2,1,0:T(8,128)(2,1)} custom-call(f32[6,8,16,128]{3,2,1,0:T(8,128)S(1)} %get-tuple-element.76.grad_ref, bf16[6,8,16,128]{3,2,1,0:T(8,128)(2,1)S(1)} %collective-permute-done.21.other_ref, f32[6,128,128]{2,1,0:T(8,128)S(1)} %get-tuple-element.70.refs_4_.taps_ref), custom_call_target="tpu_custom_call" | custom-call | flops 110000000 | bytes 1179648 | tf_op jit(solution)/shard_map/conv_back/pallas_call | solution.py:379
  50.7 0.0 collective-permute-done.22.refs_1_
  50.7 0.0 collective-permute-done.23.refs_2_
  50.7 1.3 %collective-permute-done.24.refs_3_ = bf16[48,512]{1,0:T(8,128)(2,1)S(1)} collective-permute-done((bf16[48,512]{1,0:T(8,128)(2,1)S(1)}, bf16[48,512]{1,0:T(8,128)(2,1)S(1)}, u32[]{:S(2)}, u32[]{:S(2)}) %collective-permute-start.24) | collective-permute-done | bytes 49184 | tf_op jit(solution)/shard_map/ppermute | solution.py:412
  52.1 0.1 collective-permute-start.25
  52.2 1.5 %collective-permute-done.25.other_ref = f32[48,1280]{1,0:T(8,128)S(1)} collective-permute-done((f32[48,1280]{1,0:T(8,128)S(1)}, f32[48,1280]{1,0:T(8,128)S(1)}, u32[]{:S(2)}, u32[]{:S(2)}) %collective-permute-start.25) | collective-permute-done | bytes 245792 | tf_op jit(solution)/shard_map/ppermute | solution.py:415
  53.6 0.8 %finish.1 = (f32[48,1536]{1,0:T(8,128)}, f32[48,49]{1,0:T(8,128)}, f32[1,48]{1,0:T(1,128)}, f32[1,48]{1,0:T(1,128)}) custom-call(f32[48,1280]{1,0:T(8,128)S(1)} %line_sum.1.mine_ref, f32[48,1280]{1,0:T(8,128)S(1)} %collective-permute-done.25.other_ref), custom_call_target="tpu_custom_call" | custom-call | flops 550000000 | bytes 796224 | tf_op jit(solution)/shard_map/finish/pallas_call | solution.py:379
  (6 shorter events, 0.1 us)
Async XLA Ops:
  0.6 7.1 %copy-start = (bf16[1,8,16,768]{3,2,1,0:T(8,128)(2,1)S(1)}, bf16[1,8,16,768]{3,2,1,0:T(8,128)(2,1)}, u32[]{:S(2)}) copy-start(bf16[1,8,16,768]{3,2,1,0:T(8,128)(2,1)} %refs_5_) | copy-start | bytes 589828
  0.6 8.6 %copy-start.1 = (bf16[1,8,16,1536]{3,2,1,0:T(8,128)(2,1)S(1)}, bf16[1,8,16,1536]{3,2,1,0:T(8,128)(2,1)}, u32[]{:S(2)}) copy-start(bf16[1,8,16,1536]{3,2,1,0:T(8,128)(2,1)} %param.7) | copy-start | bytes 1179652
  2.4 7.2 %collective-permute-start.1 = (bf16[48,512]{1,0:T(8,128)(2,1)}, bf16[48,512]{1,0:T(8,128)(2,1)S(1)}, u32[]{:S(2)}, u32[]{:S(2)}) collective-permute-start(bf16[48,512]{1,0:T(8,128)(2,1)} %get-tuple-element.51), channel_id=1, source_target_pairs={{0,17},{1,16},{2,19},{3,18},{4,21},{5,20},{6,23},{7,22},{8,25},{9,... | collective-permute-start | bytes 147464 | tf_op jit(solution)/shard_map/ppermute | solution.py:412
  5.9 5.6 %collective-permute-start.2 = (bf16[48,512]{1,0:T(8,128)(2,1)}, bf16[48,512]{1,0:T(8,128)(2,1)S(1)}, u32[]{:S(2)}, u32[]{:S(2)}) collective-permute-start(bf16[48,512]{1,0:T(8,128)(2,1)} %get-tuple-element.50), channel_id=1, source_target_pairs={{0,25},{1,24},{2,27},{3,26},{4,29},{5,28},{6,31},{7,30},{8,17},{9,... | collective-permute-start | bytes 147464 | tf_op jit(solution)/shard_map/ppermute | solution.py:412
  7.5 5.0 %collective-permute-start = (bf16[48,512]{1,0:T(8,128)(2,1)}, bf16[48,512]{1,0:T(8,128)(2,1)S(1)}, u32[]{:S(2)}, u32[]{:S(2)}) collective-permute-start(bf16[48,512]{1,0:T(8,128)(2,1)} %get-tuple-element.50), channel_id=1, source_target_pairs={{0,9},{1,8},{2,11},{3,10},{4,13},{5,12},{6,15},{7,14},{8,1},{9,0},... | collective-permute-start | bytes 147464 | tf_op jit(solution)/shard_map/ppermute | solution.py:412
  7.7 12.7 %collective-permute-start.9 = (bf16[1,8,16,768]{3,2,1,0:T(8,128)(2,1)S(1)}, bf16[1,8,16,768]{3,2,1,0:T(8,128)(2,1)S(1)}, u32[]{:S(2)}, u32[]{:S(2)}) collective-permute-start(bf16[1,8,16,768]{3,2,1,0:T(8,128)(2,1)S(1)} %copy-done), channel_id=1, source_target_pairs={{0,9},{1,8},{2,11},{3,10},{4,13},{5,12},{6,15},{7,14},{8,1},{9,0},... | collective-permute-start | bytes 589832 | tf_op jit(solution)/shard_map/ppermute | solution.py:412
  9.2 3.2 %copy-start.2 = (bf16[48,512]{1,0:T(8,128)(2,1)S(1)}, bf16[48,512]{1,0:T(8,128)(2,1)}, u32[]{:S(2)}) copy-start(bf16[48,512]{1,0:T(8,128)(2,1)} %get-tuple-element.49.refs_0_) | copy-start | bytes 147460
  9.3 14.3 %collective-permute-start.10 = (bf16[128,768]{1,0:T(8,128)(2,1)S(1)}, bf16[128,768]{1,0:T(8,128)(2,1)S(1)}, u32[]{:S(2)}, u32[]{:S(2)}) collective-permute-start(bf16[128,768]{1,0:T(8,128)(2,1)S(1)} %get-tuple-element.57), channel_id=1, source_target_pairs={{0,9},{1,8},{2,11},{3,10},{4,13},{5,12},{6,15},{7,14},{8,1},{9,0},... | collective-permute-start | bytes 589832 | tf_op jit(solution)/shard_map/ppermute | solution.py:412
  12.5 4.3 %collective-permute-start.8 = (bf16[96,128]{1,0:T(8,128)(2,1)S(1)}, bf16[96,128]{1,0:T(8,128)(2,1)S(1)}, u32[]{:S(2)}, u32[]{:S(2)}) collective-permute-start(bf16[96,128]{1,0:T(8,128)(2,1)S(1)} %get-tuple-element.53.refs_0_), channel_id=1, source_target_pairs={{0,7},{1,6},{2,5},{3,4},{4,3},{5,2},{6,1},{7,0},{8,15},{9,14},{10,... | collective-permute-start | bytes 73736 | tf_op jit(solution)/shard_map/ppermute | solution.py:412
  15.3 4.0 %collective-permute-start.7 = (bf16[96,128]{1,0:T(8,128)(2,1)S(1)}, bf16[96,128]{1,0:T(8,128)(2,1)S(1)}, u32[]{:S(2)}, u32[]{:S(2)}) collective-permute-start(bf16[96,128]{1,0:T(8,128)(2,1)S(1)} %get-tuple-element.53.refs_0_), channel_id=1, source_target_pairs={{0,5},{1,4},{2,7},{3,6},{4,1},{5,0},{6,3},{7,2},{8,13},{9,12},{10,... | collective-permute-start | bytes 73736 | tf_op jit(solution)/shard_map/ppermute | solution.py:412
  15.3 4.4 %collective-permute-start.6 = (bf16[96,128]{1,0:T(8,128)(2,1)S(1)}, bf16[96,128]{1,0:T(8,128)(2,1)S(1)}, u32[]{:S(2)}, u32[]{:S(2)}) collective-permute-start(bf16[96,128]{1,0:T(8,128)(2,1)S(1)} %get-tuple-element.53.refs_0_), channel_id=1, source_target_pairs={{0,3},{1,2},{2,1},{3,0},{4,7},{5,6},{6,5},{7,4},{8,11},{9,10},{10,... | collective-permute-start | bytes 73736 | tf_op jit(solution)/shard_map/ppermute | solution.py:412
  16.9 7.5 %collective-permute-start.5 = (bf16[192,384]{1,0:T(8,128)(2,1)S(1)}, bf16[192,384]{1,0:T(8,128)(2,1)S(1)}, u32[]{:S(2)}, u32[]{:S(2)}) collective-permute-start(bf16[192,384]{1,0:T(8,128)(2,1)S(1)} %get-tuple-element.52.refs_0_), channel_id=1, source_target_pairs={{0,6},{2,4},{4,2},{6,0},{8,14},{10,12},{12,10},{14,8},{16,22},{18,... | collective-permute-start | bytes 442376 | tf_op jit(solution)/shard_map/ppermute | solution.py:406
  19.3 7.9 %collective-permute-start.4 = (bf16[192,384]{1,0:T(8,128)(2,1)S(1)}, bf16[192,384]{1,0:T(8,128)(2,1)S(1)}, u32[]{:S(2)}, u32[]{:S(2)}) collective-permute-start(bf16[192,384]{1,0:T(8,128)(2,1)S(1)} %get-tuple-element.52.refs_0_), channel_id=1, source_target_pairs={{0,4},{2,6},{4,0},{6,2},{8,12},{10,14},{12,8},{14,10},{16,20},{18,... | collective-permute-start | bytes 442376 | tf_op jit(solution)/shard_map/ppermute | solution.py:406
  19.7 7.8 %collective-permute-start.3 = (bf16[192,384]{1,0:T(8,128)(2,1)S(1)}, bf16[192,384]{1,0:T(8,128)(2,1)S(1)}, u32[]{:S(2)}, u32[]{:S(2)}) collective-permute-start(bf16[192,384]{1,0:T(8,128)(2,1)S(1)} %get-tuple-element.52.refs_0_), channel_id=1, source_target_pairs={{0,2},{2,0},{4,6},{6,4},{8,10},{10,8},{12,14},{14,12},{16,18},{18,... | collective-permute-start | bytes 442376 | tf_op jit(solution)/shard_map/ppermute | solution.py:406
  23.6 4.0 %collective-permute-start.11 = (bf16[256,768]{1,0:T(8,128)(2,1)S(1)}, bf16[256,768]{1,0:T(8,128)(2,1)S(1)}, u32[]{:S(2)}, u32[]{:S(2)}) collective-permute-start(bf16[256,768]{1,0:T(8,128)(2,1)S(1)} %get-tuple-element.58.refs_1_), channel_id=1, source_target_pairs={{0,1},{1,0},{2,3},{3,2},{4,5},{5,4},{6,7},{7,6},{8,9},{9,8},{10,11... | collective-permute-start | bytes 1179656 | tf_op jit(solution)/shard_map/ppermute | solution.py:415
  23.7 3.9 %collective-permute-start.12 = (bf16[128,768]{1,0:T(8,128)(2,1)S(1)}, bf16[128,768]{1,0:T(8,128)(2,1)S(1)}, u32[]{:S(2)}, u32[]{:S(2)}) collective-permute-start(bf16[128,768]{1,0:T(8,128)(2,1)S(1)} %get-tuple-element.59), channel_id=1, source_target_pairs={{0,1},{1,0},{2,3},{3,2},{4,5},{5,4},{6,7},{7,6},{8,9},{9,8},{10,11... | collective-permute-start | bytes 589832 | tf_op jit(solution)/shard_map/ppermute | solution.py:415
  24.4 3.1 %collective-permute-start.13 = (bf16[128,768]{1,0:T(8,128)(2,1)S(1)}, bf16[128,768]{1,0:T(8,128)(2,1)S(1)}, u32[]{:S(2)}, u32[]{:S(2)}) collective-permute-start(bf16[128,768]{1,0:T(8,128)(2,1)S(1)} %collective-permute-done.10.refs_5_), channel_id=1, source_target_pairs={{0,1},{1,0},{2,3},{3,2},{4,5},{5,4},{6,7},{7,6},{8,9},{9,8},{10,11... | collective-permute-start | bytes 589832 | tf_op jit(solution)/shard_map/ppermute | solution.py:415
  29.7 3.6 %collective-permute-start.17 = (f32[256,768]{1,0:T(8,128)S(1)}, f32[256,768]{1,0:T(8,128)S(1)}, u32[]{:S(2)}, u32[]{:S(2)}) collective-permute-start(f32[256,768]{1,0:T(8,128)S(1)} %get-tuple-element.67), channel_id=1, source_target_pairs={{0,1},{1,0},{2,3},{3,2},{4,5},{5,4},{6,7},{7,6},{8,9},{9,8},{10,11... | collective-permute-start | bytes 2359304 | tf_op jit(solution)/shard_map/ppermute | solution.py:415
  29.8 8.6 %collective-permute-start.14 = (bf16[192,384]{1,0:T(8,128)(2,1)S(1)}, bf16[192,384]{1,0:T(8,128)(2,1)S(1)}, u32[]{:S(2)}, u32[]{:S(2)}) collective-permute-start(bf16[192,384]{1,0:T(8,128)(2,1)S(1)} %get-tuple-element.62), channel_id=1, source_target_pairs={{0,2},{2,0},{4,6},{6,4},{8,10},{10,8},{12,14},{14,12},{16,18},{18,... | collective-permute-start | bytes 442376 | tf_op jit(solution)/shard_map/ppermute | solution.py:406
  31.4 9.1 %collective-permute-start.15 = (bf16[192,384]{1,0:T(8,128)(2,1)S(1)}, bf16[192,384]{1,0:T(8,128)(2,1)S(1)}, u32[]{:S(2)}, u32[]{:S(2)}) collective-permute-start(bf16[192,384]{1,0:T(8,128)(2,1)S(1)} %get-tuple-element.63), channel_id=1, source_target_pairs={{0,4},{2,6},{4,0},{6,2},{8,12},{10,14},{12,8},{14,10},{16,20},{18,... | collective-permute-start | bytes 442376 | tf_op jit(solution)/shard_map/ppermute | solution.py:406
  32.0 8.6 %collective-permute-start.16 = (bf16[192,384]{1,0:T(8,128)(2,1)S(1)}, bf16[192,384]{1,0:T(8,128)(2,1)S(1)}, u32[]{:S(2)}, u32[]{:S(2)}) collective-permute-start(bf16[192,384]{1,0:T(8,128)(2,1)S(1)} %get-tuple-element.64), channel_id=1, source_target_pairs={{0,6},{2,4},{4,2},{6,0},{8,14},{10,12},{12,10},{14,8},{16,22},{18,... | collective-permute-start | bytes 442376 | tf_op jit(solution)/shard_map/ppermute | solution.py:406
  36.5 4.0 %collective-permute-start.18 = (bf16[96,128]{1,0:T(8,128)(2,1)S(1)}, bf16[96,128]{1,0:T(8,128)(2,1)S(1)}, u32[]{:S(2)}, u32[]{:S(2)}) collective-permute-start(bf16[96,128]{1,0:T(8,128)(2,1)S(1)} %get-tuple-element.72), channel_id=1, source_target_pairs={{0,3},{1,2},{2,1},{3,0},{4,7},{5,6},{6,5},{7,4},{8,11},{9,10},{10,... | collective-permute-start | bytes 73736 | tf_op jit(solution)/shard_map/ppermute | solution.py:412
  37.4 3.4 %collective-permute-start.19 = (bf16[96,128]{1,0:T(8,128)(2,1)S(1)}, bf16[96,128]{1,0:T(8,128)(2,1)S(1)}, u32[]{:S(2)}, u32[]{:S(2)}) collective-permute-start(bf16[96,128]{1,0:T(8,128)(2,1)S(1)} %get-tuple-element.73), channel_id=1, source_target_pairs={{0,5},{1,4},{2,7},{3,6},{4,1},{5,0},{6,3},{7,2},{8,13},{9,12},{10,... | collective-permute-start | bytes 73736 | tf_op jit(solution)/shard_map/ppermute | solution.py:412
  38.4 4.4 %collective-permute-start.20 = (bf16[96,128]{1,0:T(8,128)(2,1)S(1)}, bf16[96,128]{1,0:T(8,128)(2,1)S(1)}, u32[]{:S(2)}, u32[]{:S(2)}) collective-permute-start(bf16[96,128]{1,0:T(8,128)(2,1)S(1)} %get-tuple-element.74), channel_id=1, source_target_pairs={{0,7},{1,6},{2,5},{3,4},{4,3},{5,2},{6,1},{7,0},{8,15},{9,14},{10,... | collective-permute-start | bytes 73736 | tf_op jit(solution)/shard_map/ppermute | solution.py:412
  40.6 8.2 %collective-permute-start.21 = (bf16[6,8,16,128]{3,2,1,0:T(8,128)(2,1)S(1)}, bf16[6,8,16,128]{3,2,1,0:T(8,128)(2,1)S(1)}, u32[]{:S(2)}, u32[]{:S(2)}) collective-permute-start(bf16[6,8,16,128]{3,2,1,0:T(8,128)(2,1)S(1)} %get-tuple-element.77), channel_id=1, source_target_pairs={{0,9},{1,8},{2,11},{3,10},{4,13},{5,12},{6,15},{7,14},{8,1},{9,0},... | collective-permute-start | bytes 589832 | tf_op jit(solution)/shard_map/ppermute | solution.py:412
  42.9 7.8 %collective-permute-start.22 = (bf16[48,512]{1,0:T(8,128)(2,1)S(1)}, bf16[48,512]{1,0:T(8,128)(2,1)S(1)}, u32[]{:S(2)}, u32[]{:S(2)}) collective-permute-start(bf16[48,512]{1,0:T(8,128)(2,1)S(1)} %get-tuple-element.80), channel_id=1, source_target_pairs={{0,9},{1,8},{2,11},{3,10},{4,13},{5,12},{6,15},{7,14},{8,1},{9,0},... | collective-permute-start | bytes 147464 | tf_op jit(solution)/shard_map/ppermute | solution.py:412
  43.0 7.6 %collective-permute-start.23 = (bf16[48,512]{1,0:T(8,128)(2,1)S(1)}, bf16[48,512]{1,0:T(8,128)(2,1)S(1)}, u32[]{:S(2)}, u32[]{:S(2)}) collective-permute-start(bf16[48,512]{1,0:T(8,128)(2,1)S(1)} %get-tuple-element.81), channel_id=1, source_target_pairs={{0,17},{1,16},{2,19},{3,18},{4,21},{5,20},{6,23},{7,22},{8,25},{9,... | collective-permute-start | bytes 147464 | tf_op jit(solution)/shard_map/ppermute | solution.py:412
  45.9 6.1 %collective-permute-start.24 = (bf16[48,512]{1,0:T(8,128)(2,1)S(1)}, bf16[48,512]{1,0:T(8,128)(2,1)S(1)}, u32[]{:S(2)}, u32[]{:S(2)}) collective-permute-start(bf16[48,512]{1,0:T(8,128)(2,1)S(1)} %get-tuple-element.82), channel_id=1, source_target_pairs={{0,25},{1,24},{2,27},{3,26},{4,29},{5,28},{6,31},{7,30},{8,17},{9,... | collective-permute-start | bytes 147464 | tf_op jit(solution)/shard_map/ppermute | solution.py:412
  52.1 1.6 %collective-permute-start.25 = (f32[48,1280]{1,0:T(8,128)S(1)}, f32[48,1280]{1,0:T(8,128)S(1)}, u32[]{:S(2)}, u32[]{:S(2)}) collective-permute-start(f32[48,1280]{1,0:T(8,128)S(1)} %line_sum.1.mine_ref), channel_id=1, source_target_pairs={{0,1},{1,0},{2,3},{3,2},{4,5},{5,4},{6,7},{7,6},{8,9},{9,8},{10,11... | collective-permute-start | bytes 737288 | tf_op jit(solution)/shard_map/ppermute | solution.py:415

commit v10 on v9

--- a/solution.py
+++ b/solution.py
@@ -97,15 +97,21 @@
 
 
 def assemble_kernel(*refs):
-    pieces, (weight_ref, extra_ref) = refs[:-2], refs[-2:]
+    pieces, out_ref = refs[:-1], refs[-1]
     own = pieces[0].shape[0]
-    quarter = weight_ref.shape[1]
+    rows, quarter = own * len(pieces), out_ref.shape[1]
     for line, piece in enumerate(pieces):
-        weight_ref[line * own : (line + 1) * own, :] = piece[:, :quarter]
-    extras = jnp.concatenate([piece[:, quarter:].astype(F32) for piece in pieces], axis=0)
-    if extra_ref.shape[0] < extras.shape[0]:
-        extras = fold(extras)
-    extra_ref[...] = extras.astype(BF16)
+        out_ref[line * own : (line + 1) * own, :] = piece[:, :quarter]
+    extras = fold(jnp.concatenate([piece[:, quarter:].astype(F32) for piece in pieces], axis=0))
+    count = out_ref.shape[0] - rows
+    for place in range(quarter // LANES):
+        lanes = slice(place * LANES, (place + 1) * LANES)
+        out_ref[rows:, lanes] = extras[place * count : (place + 1) * count].astype(BF16)
+
+
+def small_rows(lower):
+    parts = [lower[:, at : at + LANES] for at in range(0, lower.shape[1], LANES)]
+    return unfold(jnp.concatenate(parts, axis=0))
 
 
 def plane_sum_kernel(lines, *refs):
@@ -167,7 +173,7 @@
 
 
 def unfold(rows):
-    return jnp.concatenate([rows, pltpu.roll(rows, LANES // 2, 1)], axis=0)
+    return jnp.concatenate([rows, jnp.roll(rows, LANES // 2, 1)], axis=0)
 
 
 def conv_norm_kernel(relative, own, *refs):
@@ -179,11 +185,11 @@
     tiles = depth // LANES
     pixels = height * breadth
     if relative:
+        count = unfolded.shape[0] // INNER
         for group, piece in enumerate(small):
-            unfolded[group * 2 * piece.shape[0] : (group + 1) * 2 * piece.shape[0], :] = unfold(
-                piece[...].astype(F32)
+            unfolded[group * count : (group + 1) * count, :] = small_rows(
+                piece[count:, :].astype(F32)
             )
-        count = unfolded.shape[0] // INNER
         small = [unfolded.at[pl.ds(group * count, count), :] for group in range(INNER)]
     place_rows(small, gathered, own, relative, F32)
     padded[...] = jnp.zeros_like(padded)
@@ -242,7 +248,8 @@
 
 
 def order_kernel(relative, own, *refs):
-    place_rows(refs[:INNER], refs[INNER], own, relative)
+    rows = refs[INNER].shape[0] // INNER
+    place_rows([ref.at[pl.ds(0, rows), :] for ref in refs[:INNER]], refs[INNER], own, relative)
 
 
 def project_kernel(relative, own, *refs):
@@ -466,17 +473,20 @@
 
     rows = lines * own
     folded = rows // 2 if relative else rows
-    weight_lines, extra_lines = call(
+    held = rows // 2 * LANES // quarter
+    (mixed,) = call(
         assemble_kernel,
         "assemble",
-        [shape((rows, quarter), BF16), shape((folded, LANES), BF16)],
+        [shape((rows + held, quarter), BF16)],
         [],
         2.0,
         *gathered,
     )
-    weights = [weight_lines] + [over_shard(weight_lines, flip) for flip in range(1, INNER)]
-    extras = [extra_lines] + [crossing(extra_lines, flip) for flip in range(1, INNER)]
-    weights, extras = true_order(weights), true_order(extras)
+    weights = [mixed] + [over_shard(mixed, flip) for flip in range(1, INNER)]
+    extras = weights
+    if not relative:
+        extras = true_order([small_rows(piece[rows:]) for piece in weights])
+        weights = true_order([piece[:rows] for piece in weights])
     (weight,) = call(
         functools.partial(order_kernel, relative, own),
         "order",

time: 54.6 us -> 56.9 us (1.042)
  waiting for transfers between devices: 15.1 us -> 21 us
  starting transfers between devices: 25.3 us -> 21.7 us
    ppermute x6, waiting for transfers between devices: 4.4 us -> 8.53 us  [over_shard(): return lax.ppermute(array, 'shard', [(i, i ^ flip) for i in range(shards)])]
    ppermute x15 -> x12, starting transfers between devices: 17.5 us -> 13.7 us  [crossing(): return lax.ppermute(array, ('shard', 'rep'), pairs)]
    ppermute x5, waiting for transfers between devices: 1.46 us -> 3.08 us  [over_core(): return lax.ppermute(array, 'rep', [(i, i ^ 1) for i in range(reps)])]
    ppermute x15 -> x12, waiting for transfers between devices: 9.19 us -> 9.37 us  [crossing(): return lax.ppermute(array, ('shard', 'rep'), pairs)]
  transfers between devices with their start and end apart: 26 -> 23, of which waited for: 12 -> 14; matrix products, arithmetic and copies ran while one was open for 0% -> 0% of each run, Pallas kernels for 16% -> 15%
where the time goes in v10:
time: 56.9 us; the launch traced here: 56.7 us
  starting transfers between devices  21.7 us (38%)
  waiting for transfers between devices  21 us (37%)
  Pallas kernels  13.2 us (23%)
  between operations  0.75 us (1%)
    ppermute x12, starting transfers between devices, crossing(): return lax.ppermute(array, ('shard', 'rep'), pairs)  13.7 us
    pallas_call x12, Pallas kernels, call(): pl.pallas_call(kernel, out_shape=outs, in_specs=[VMEM] * len(args), out_s...  13.2 us
    ppermute x12, waiting for transfers between devices, crossing(): return lax.ppermute(array, ('shard', 'rep'), pairs)  9.37 us
    ppermute x6, waiting for transfers between devices, over_shard(): return lax.ppermute(array, 'shard', [(i, i ^ flip) for i in range(shards)])  8.53 us
    ppermute x6, starting transfers between devices, over_shard(): return lax.ppermute(array, 'shard', [(i, i ^ flip) for i in range(shards)])  7.06 us
    ppermute x5, waiting for transfers between devices, over_core(): return lax.ppermute(array, 'rep', [(i, i ^ 1) for i in range(reps)])  3.08 us
  transfers between devices with their start and end apart: 23, of which 14 were waited for; matrix products, arithmetic and copies ran while one was open for 0% of the time, Pallas kernels for 15%

profile of v10, /device:TPU:0, one launch (start us, length us, event | category | flops | bytes accessed | tf_op | source)
XLA Modules:
  0.0 56.7 jit_solution(11600697358822724854)
XLA Ops:
  0.6 0.0 copy-start
  0.6 0.0 copy-start.1
  0.7 1.7 %pack.1 = (bf16[48,512]{1,0:T(8,128)(2,1)}, bf16[48,512]{1,0:T(8,128)(2,1)}, bf16[48,512]{1,0:T(8,128)(2,1)}) custom-call(bf16[48,1536]{1,0:T(8,128)(2,1)} %w_ref.1, bf16[48,49]{1,0:T(8,128)(2,1)} %dw_ref.1, bf16[1,48]{1,0:T(2,128)(2,1)} %bitcast.7, bf16[1,48]{1,0:T(2,128)(2,1)} %bitcast.8), custom_call_target="tpu_custom_call" | custom-call | flops 550000000 | bytes 299808 | tf_op jit(solution)/shard_map/pack/pallas_call | solution.py:386
  2.4 3.5 %collective-permute-start.1 = (bf16[48,512]{1,0:T(8,128)(2,1)}, bf16[48,512]{1,0:T(8,128)(2,1)S(1)}, u32[]{:S(2)}, u32[]{:S(2)}) collective-permute-start(bf16[48,512]{1,0:T(8,128)(2,1)} %get-tuple-element.49), channel_id=1, source_target_pairs={{0,17},{1,16},{2,19},{3,18},{4,21},{5,20},{6,23},{7,22},{8,25},{9,... | collective-permute-start | bytes 147464 | tf_op jit(solution)/shard_map/ppermute | solution.py:419
  5.9 1.6 %collective-permute-start.2 = (bf16[48,512]{1,0:T(8,128)(2,1)}, bf16[48,512]{1,0:T(8,128)(2,1)S(1)}, u32[]{:S(2)}, u32[]{:S(2)}) collective-permute-start(bf16[48,512]{1,0:T(8,128)(2,1)} %get-tuple-element.48), channel_id=1, source_target_pairs={{0,25},{1,24},{2,27},{3,26},{4,29},{5,28},{6,31},{7,30},{8,17},{9,... | collective-permute-start | bytes 147464 | tf_op jit(solution)/shard_map/ppermute | solution.py:419
  7.5 0.2 collective-permute-start
  7.7 0.0 copy-done
  7.7 1.5 %collective-permute-start.6 = (bf16[1,8,16,768]{3,2,1,0:T(8,128)(2,1)S(1)}, bf16[1,8,16,768]{3,2,1,0:T(8,128)(2,1)S(1)}, u32[]{:S(2)}, u32[]{:S(2)}) collective-permute-start(bf16[1,8,16,768]{3,2,1,0:T(8,128)(2,1)S(1)} %copy-done), channel_id=1, source_target_pairs={{0,9},{1,8},{2,11},{3,10},{4,13},{5,12},{6,15},{7,14},{8,1},{9,0},... | collective-permute-start | bytes 589832 | tf_op jit(solution)/shard_map/ppermute | solution.py:419
  9.2 0.0 copy-done.1
  9.2 0.0 copy-start.2
  9.3 0.3 collective-permute-start.7
  9.6 0.0 collective-permute-done.1.refs_2_
  9.6 1.9 %collective-permute-done.2.refs_3_ = bf16[48,512]{1,0:T(8,128)(2,1)S(1)} collective-permute-done((bf16[48,512]{1,0:T(8,128)(2,1)}, bf16[48,512]{1,0:T(8,128)(2,1)S(1)}, u32[]{:S(2)}, u32[]{:S(2)}) %collective-permute-start.2) | collective-permute-done | bytes 49184 | tf_op jit(solution)/shard_map/ppermute | solution.py:419
  11.5 1.0 %collective-permute-done.refs_1_ = bf16[48,512]{1,0:T(8,128)(2,1)S(1)} collective-permute-done((bf16[48,512]{1,0:T(8,128)(2,1)}, bf16[48,512]{1,0:T(8,128)(2,1)S(1)}, u32[]{:S(2)}, u32[]{:S(2)}) %collective-permute-start) | collective-permute-done | bytes 49184 | tf_op jit(solution)/shard_map/ppermute | solution.py:419
  12.4 0.0 copy-done.2
  12.4 0.1 assemble.1.refs_0_
  12.5 2.5 %collective-permute-start.5 = (bf16[224,384]{1,0:T(8,128)(2,1)S(1)}, bf16[224,384]{1,0:T(8,128)(2,1)S(1)}, u32[]{:S(2)}, u32[]{:S(2)}) collective-permute-start(bf16[224,384]{1,0:T(8,128)(2,1)S(1)} %assemble.1.refs_0_), channel_id=1, source_target_pairs={{0,6},{2,4},{4,2},{6,0},{8,14},{10,12},{12,10},{14,8},{16,22},{18,... | collective-permute-start | bytes 516104 | tf_op jit(solution)/shard_map/ppermute | solution.py:413
  15.0 0.5 collective-permute-start.4
  15.6 0.5 collective-permute-start.3
  16.1 0.7 %collective-permute-done.6.refs_5_.refs_6_ = bf16[1,8,16,768]{3,2,1,0:T(8,128)(2,1)S(1)} collective-permute-done((bf16[1,8,16,768]{3,2,1,0:T(8,128)(2,1)S(1)}, bf16[1,8,16,768]{3,2,1,0:T(8,128)(2,1)S(1)}, u32[]{:S(2)}, u32[]{:S(2)}) %collective-permute-start.6) | collective-permute-done | bytes 196640 | tf_op jit(solution)/shard_map/ppermute | solution.py:419
  16.8 4.0 %collective-permute-done.5.refs_3_ = bf16[224,384]{1,0:T(8,128)(2,1)S(1)} collective-permute-done((bf16[224,384]{1,0:T(8,128)(2,1)S(1)}, bf16[224,384]{1,0:T(8,128)(2,1)S(1)}, u32[]{:S(2)}, u32[]{:S(2)}) %collective-permute-start.5) | collective-permute-done | bytes 172064 | tf_op jit(solution)/shard_map/ppermute | solution.py:413
  20.8 3.4 %collective-permute-done.4.refs_2_ = bf16[224,384]{1,0:T(8,128)(2,1)S(1)} collective-permute-done((bf16[224,384]{1,0:T(8,128)(2,1)S(1)}, bf16[224,384]{1,0:T(8,128)(2,1)S(1)}, u32[]{:S(2)}, u32[]{:S(2)}) %collective-permute-start.4) | collective-permute-done | bytes 172064 | tf_op jit(solution)/shard_map/ppermute | solution.py:413
  24.2 0.1 collective-permute-done.3.refs_1_
  24.3 3.2 %conv_norm.1 = (bf16[256,768]{1,0:T(8,128)(2,1)S(1)}, f32[256,768]{1,0:T(8,128)S(1)}, f32[256,128]{1,0:T(8,128)S(1)}, f32[6,128,128]{2,1,0:T(8,128)S(1)}) custom-call(bf16[224,384]{1,0:T(8,128)(2,1)S(1)} %assemble.1.refs_0_, bf16[224,384]{1,0:T(8,128)(2,1)S(1)} %collective-permute-done.3.refs_1_, bf16[224,384]{1,0:T(8,128)(2,1)S(1)} %collective-permute-done.4.refs_2_, ...), custom_call_target="tpu_custom_call" | custom-call | flops 110000000 | bytes 2785280 | tf_op jit(solution)/shard_map/conv_norm/pallas_call | solution.py:386
  27.5 0.0 collective-permute-done.7.refs_5_
  27.5 0.1 collective-permute-start.8
  27.6 0.5 collective-permute-start.9
  28.1 0.1 collective-permute-start.10
  28.1 0.1 order.1.refs_0_.weight
  28.2 1.3 %collective-permute-done.9.refs_4_ = bf16[128,768]{1,0:T(8,128)(2,1)S(1)} collective-permute-done((bf16[128,768]{1,0:T(8,128)(2,1)S(1)}, bf16[128,768]{1,0:T(8,128)(2,1)S(1)}, u32[]{:S(2)}, u32[]{:S(2)}) %collective-permute-start.9) | collective-permute-done | bytes 196640 | tf_op jit(solution)/shard_map/ppermute | solution.py:422
  29.6 0.3 collective-permute-done.10.refs_6_
  29.8 0.0 collective-permute-done.8.refs_2_
  29.8 1.5 %project.1 = (f32[192,384]{1,0:T(8,128)S(1)}, bf16[192,384]{1,0:T(8,128)(2,1)S(1)}, bf16[192,384]{1,0:T(8,128)(2,1)S(1)}, bf16[192,384]{1,0:T(8,128)(2,1)S(1)}, bf16[512,384]{1,0:T(8,128)(2,1)S(1)}) custom-call(bf16[768,384]{1,0:T(8,128)(2,1)S(1)} %order.1.refs_0_.weight, bf16[256,768]{1,0:T(8,128)(2,1)S(1)} %get-tuple-element.54.refs_1_, ...), custom_call_target="tpu_custom_call" | custom-call | flops 1760000000 | bytes 3489792 | tf_op jit(solution)/shard_map/project/pallas_call | solution.py:386
  31.4 0.6 %back_project.1 = (f32[256,768]{1,0:T(8,128)S(1)}, f32[256,768]{1,0:T(8,128)S(1)}) custom-call(bf16[768,384]{1,0:T(8,128)(2,1)S(1)} %order.1.refs_0_.weight, bf16[512,384]{1,0:T(8,128)(2,1)S(1)} %get-tuple-element.61.gp_ref), custom_call_target="tpu_custom_call" | custom-call | flops 770000000 | bytes 2555904 | tf_op jit(solution)/shard_map/back_project/pallas_call | solution.py:386
  32.0 0.2 collective-permute-start.14
  32.2 1.5 %collective-permute-start.11 = (bf16[192,384]{1,0:T(8,128)(2,1)S(1)}, bf16[192,384]{1,0:T(8,128)(2,1)S(1)}, u32[]{:S(2)}, u32[]{:S(2)}) collective-permute-start(bf16[192,384]{1,0:T(8,128)(2,1)S(1)} %get-tuple-element.58), channel_id=1, source_target_pairs={{0,2},{2,0},{4,6},{6,4},{8,10},{10,8},{12,14},{14,12},{16,18},{18,... | collective-permute-start | bytes 442376 | tf_op jit(solution)/shard_map/ppermute | solution.py:413
  33.7 0.7 %collective-permute-start.12 = (bf16[192,384]{1,0:T(8,128)(2,1)S(1)}, bf16[192,384]{1,0:T(8,128)(2,1)S(1)}, u32[]{:S(2)}, u32[]{:S(2)}) collective-permute-start(bf16[192,384]{1,0:T(8,128)(2,1)S(1)} %get-tuple-element.59), channel_id=1, source_target_pairs={{0,4},{2,6},{4,0},{6,2},{8,12},{10,14},{12,8},{14,10},{16,20},{18,... | collective-permute-start | bytes 442376 | tf_op jit(solution)/shard_map/ppermute | solution.py:413
  34.4 1.3 %collective-permute-start.13 = (bf16[192,384]{1,0:T(8,128)(2,1)S(1)}, bf16[192,384]{1,0:T(8,128)(2,1)S(1)}, u32[]{:S(2)}, u32[]{:S(2)}) collective-permute-start(bf16[192,384]{1,0:T(8,128)(2,1)S(1)} %get-tuple-element.60), channel_id=1, source_target_pairs={{0,6},{2,4},{4,2},{6,0},{8,14},{10,12},{12,10},{14,8},{16,22},{18,... | collective-permute-start | bytes 442376 | tf_op jit(solution)/shard_map/ppermute | solution.py:413
  35.7 0.0 collective-permute-done.14.refs_1_
  35.7 3.2 %norm_back.1 = (f32[96,128]{1,0:T(8,128)S(1)}, bf16[96,128]{1,0:T(8,128)(2,1)S(1)}, bf16[96,128]{1,0:T(8,128)(2,1)S(1)}, bf16[96,128]{1,0:T(8,128)(2,1)S(1)}, f3...) custom-call(f32[256,768]{1,0:T(8,128)S(1)} %get-tuple-element.62.refs_0_, ...), custom_call_target="tpu_custom_call" | custom-call | flops 110000000 | bytes 3989504 | tf_op jit(solution)/shard_map/norm_back/pallas_call | solution.py:386
  38.9 0.7 %collective-permute-start.15 = (bf16[96,128]{1,0:T(8,128)(2,1)S(1)}, bf16[96,128]{1,0:T(8,128)(2,1)S(1)}, u32[]{:S(2)}, u32[]{:S(2)}) collective-permute-start(bf16[96,128]{1,0:T(8,128)(2,1)S(1)} %get-tuple-element.68), channel_id=1, source_target_pairs={{0,3},{1,2},{2,1},{3,0},{4,7},{5,6},{6,5},{7,4},{8,11},{9,10},{10,... | collective-permute-start | bytes 73736 | tf_op jit(solution)/shard_map/ppermute | solution.py:419
  39.6 1.3 %collective-permute-start.16 = (bf16[96,128]{1,0:T(8,128)(2,1)S(1)}, bf16[96,128]{1,0:T(8,128)(2,1)S(1)}, u32[]{:S(2)}, u32[]{:S(2)}) collective-permute-start(bf16[96,128]{1,0:T(8,128)(2,1)S(1)} %get-tuple-element.69), channel_id=1, source_target_pairs={{0,5},{1,4},{2,7},{3,6},{4,1},{5,0},{6,3},{7,2},{8,13},{9,12},{10,... | collective-permute-start | bytes 73736 | tf_op jit(solution)/shard_map/ppermute | solution.py:419
  40.9 0.0 collective-permute-done.11.refs_1_
  40.9 0.8 %collective-permute-start.17 = (bf16[96,128]{1,0:T(8,128)(2,1)S(1)}, bf16[96,128]{1,0:T(8,128)(2,1)S(1)}, u32[]{:S(2)}, u32[]{:S(2)}) collective-permute-start(bf16[96,128]{1,0:T(8,128)(2,1)S(1)} %get-tuple-element.70), channel_id=1, source_target_pairs={{0,7},{1,6},{2,5},{3,4},{4,3},{5,2},{6,1},{7,0},{8,15},{9,14},{10,... | collective-permute-start | bytes 73736 | tf_op jit(solution)/shard_map/ppermute | solution.py:419
  41.7 1.0 %collective-permute-done.12.refs_2_ = bf16[192,384]{1,0:T(8,128)(2,1)S(1)} collective-permute-done((bf16[192,384]{1,0:T(8,128)(2,1)S(1)}, bf16[192,384]{1,0:T(8,128)(2,1)S(1)}, u32[]{:S(2)}, u32[]{:S(2)}) %collective-permute-start.12) | collective-permute-done | bytes 147488 | tf_op jit(solution)/shard_map/ppermute | solution.py:413
  42.7 0.0 collective-permute-start.18
  42.7 0.0 collective-permute-done.13.refs_3_
  42.7 0.0 collective-permute-done.15.refs_5_
  42.8 0.2 collective-permute-done.16.refs_6_
  42.9 2.2 %collective-permute-done.17.refs_7_ = bf16[96,128]{1,0:T(8,128)(2,1)S(1)} collective-permute-done((bf16[96,128]{1,0:T(8,128)(2,1)S(1)}, bf16[96,128]{1,0:T(8,128)(2,1)S(1)}, u32[]{:S(2)}, u32[]{:S(2)}) %collective-permute-start.17) | collective-permute-done | bytes 24608 | tf_op jit(solution)/shard_map/ppermute | solution.py:419
  45.2 0.1 plane_sum.1
  45.2 0.1 collective-permute-start.19
  45.3 2.9 %collective-permute-start.20 = (bf16[48,512]{1,0:T(8,128)(2,1)S(1)}, bf16[48,512]{1,0:T(8,128)(2,1)S(1)}, u32[]{:S(2)}, u32[]{:S(2)}) collective-permute-start(bf16[48,512]{1,0:T(8,128)(2,1)S(1)} %get-tuple-element.77), channel_id=1, source_target_pairs={{0,17},{1,16},{2,19},{3,18},{4,21},{5,20},{6,23},{7,22},{8,25},{9,... | collective-permute-start | bytes 147464 | tf_op jit(solution)/shard_map/ppermute | solution.py:419
  48.2 0.8 %collective-permute-start.21 = (bf16[48,512]{1,0:T(8,128)(2,1)S(1)}, bf16[48,512]{1,0:T(8,128)(2,1)S(1)}, u32[]{:S(2)}, u32[]{:S(2)}) collective-permute-start(bf16[48,512]{1,0:T(8,128)(2,1)S(1)} %get-tuple-element.78), channel_id=1, source_target_pairs={{0,25},{1,24},{2,27},{3,26},{4,29},{5,28},{6,31},{7,30},{8,17},{9,... | collective-permute-start | bytes 147464 | tf_op jit(solution)/shard_map/ppermute | solution.py:419
  49.0 2.0 %collective-permute-done.18.other_ref = bf16[6,8,16,128]{3,2,1,0:T(8,128)(2,1)S(1)} collective-permute-done((bf16[6,8,16,128]{3,2,1,0:T(8,128)(2,1)S(1)}, bf16[6,8,16,128]{3,2,1,0:T(8,128)(2,1)S(1)}, u32[]{:S(2)}, u32[]{:S(2)}) %collective-permute-start.18) | collective-permute-done | bytes 196640 | tf_op jit(solution)/shard_map/ppermute | solution.py:419
  51.0 1.9 %conv_back.1 = bf16[1,8,16,768]{3,2,1,0:T(8,128)(2,1)} custom-call(f32[6,8,16,128]{3,2,1,0:T(8,128)S(1)} %get-tuple-element.72.grad_ref, bf16[6,8,16,128]{3,2,1,0:T(8,128)(2,1)S(1)} %collective-permute-done.18.other_ref, f32[6,128,128]{2,1,0:T(8,128)S(1)} %get-tuple-element.66.refs_4_.taps_ref), custom_call_target="tpu_custom_call" | custom-call | flops 110000000 | bytes 1179648 | tf_op jit(solution)/shard_map/conv_back/pallas_call | solution.py:386
  52.9 0.0 collective-permute-done.19.refs_1_
  52.9 0.0 collective-permute-done.20.refs_2_
  52.9 1.4 %collective-permute-done.21.refs_3_ = bf16[48,512]{1,0:T(8,128)(2,1)S(1)} collective-permute-done((bf16[48,512]{1,0:T(8,128)(2,1)S(1)}, bf16[48,512]{1,0:T(8,128)(2,1)S(1)}, u32[]{:S(2)}, u32[]{:S(2)}) %collective-permute-start.21) | collective-permute-done | bytes 49184 | tf_op jit(solution)/shard_map/ppermute | solution.py:419
  54.4 0.1 collective-permute-start.22
  54.5 1.5 %collective-permute-done.22.other_ref = f32[48,1280]{1,0:T(8,128)S(1)} collective-permute-done((f32[48,1280]{1,0:T(8,128)S(1)}, f32[48,1280]{1,0:T(8,128)S(1)}, u32[]{:S(2)}, u32[]{:S(2)}) %collective-permute-start.22) | collective-permute-done | bytes 245792 | tf_op jit(solution)/shard_map/ppermute | solution.py:422
  55.9 0.8 %finish.1 = (f32[48,1536]{1,0:T(8,128)}, f32[48,49]{1,0:T(8,128)}, f32[1,48]{1,0:T(1,128)}, f32[1,48]{1,0:T(1,128)}) custom-call(f32[48,1280]{1,0:T(8,128)S(1)} %line_sum.1.mine_ref, f32[48,1280]{1,0:T(8,128)S(1)} %collective-permute-done.22.other_ref), custom_call_target="tpu_custom_call" | custom-call | flops 550000000 | bytes 796224 | tf_op jit(solution)/shard_map/finish/pallas_call | solution.py:386
  (2 shorter events, 0.1 us)
Async XLA Ops:
  0.6 7.1 %copy-start = (bf16[1,8,16,768]{3,2,1,0:T(8,128)(2,1)S(1)}, bf16[1,8,16,768]{3,2,1,0:T(8,128)(2,1)}, u32[]{:S(2)}) copy-start(bf16[1,8,16,768]{3,2,1,0:T(8,128)(2,1)} %refs_5_) | copy-start | bytes 589828
  0.6 8.6 %copy-start.1 = (bf16[1,8,16,1536]{3,2,1,0:T(8,128)(2,1)S(1)}, bf16[1,8,16,1536]{3,2,1,0:T(8,128)(2,1)}, u32[]{:S(2)}) copy-start(bf16[1,8,16,1536]{3,2,1,0:T(8,128)(2,1)} %param.7) | copy-start | bytes 1179652
  2.4 7.2 %collective-permute-start.1 = (bf16[48,512]{1,0:T(8,128)(2,1)}, bf16[48,512]{1,0:T(8,128)(2,1)S(1)}, u32[]{:S(2)}, u32[]{:S(2)}) collective-permute-start(bf16[48,512]{1,0:T(8,128)(2,1)} %get-tuple-element.49), channel_id=1, source_target_pairs={{0,17},{1,16},{2,19},{3,18},{4,21},{5,20},{6,23},{7,22},{8,25},{9,... | collective-permute-start | bytes 147464 | tf_op jit(solution)/shard_map/ppermute | solution.py:419
  5.9 5.6 %collective-permute-start.2 = (bf16[48,512]{1,0:T(8,128)(2,1)}, bf16[48,512]{1,0:T(8,128)(2,1)S(1)}, u32[]{:S(2)}, u32[]{:S(2)}) collective-permute-start(bf16[48,512]{1,0:T(8,128)(2,1)} %get-tuple-element.48), channel_id=1, source_target_pairs={{0,25},{1,24},{2,27},{3,26},{4,29},{5,28},{6,31},{7,30},{8,17},{9,... | collective-permute-start | bytes 147464 | tf_op jit(solution)/shard_map/ppermute | solution.py:419
  7.5 5.0 %collective-permute-start = (bf16[48,512]{1,0:T(8,128)(2,1)}, bf16[48,512]{1,0:T(8,128)(2,1)S(1)}, u32[]{:S(2)}, u32[]{:S(2)}) collective-permute-start(bf16[48,512]{1,0:T(8,128)(2,1)} %get-tuple-element.48), channel_id=1, source_target_pairs={{0,9},{1,8},{2,11},{3,10},{4,13},{5,12},{6,15},{7,14},{8,1},{9,0},... | collective-permute-start | bytes 147464 | tf_op jit(solution)/shard_map/ppermute | solution.py:419
  7.7 9.0 %collective-permute-start.6 = (bf16[1,8,16,768]{3,2,1,0:T(8,128)(2,1)S(1)}, bf16[1,8,16,768]{3,2,1,0:T(8,128)(2,1)S(1)}, u32[]{:S(2)}, u32[]{:S(2)}) collective-permute-start(bf16[1,8,16,768]{3,2,1,0:T(8,128)(2,1)S(1)} %copy-done), channel_id=1, source_target_pairs={{0,9},{1,8},{2,11},{3,10},{4,13},{5,12},{6,15},{7,14},{8,1},{9,0},... | collective-permute-start | bytes 589832 | tf_op jit(solution)/shard_map/ppermute | solution.py:419
  9.2 3.2 %copy-start.2 = (bf16[48,512]{1,0:T(8,128)(2,1)S(1)}, bf16[48,512]{1,0:T(8,128)(2,1)}, u32[]{:S(2)}) copy-start(bf16[48,512]{1,0:T(8,128)(2,1)} %get-tuple-element.47.refs_0_) | copy-start | bytes 147460
  9.3 18.2 %collective-permute-start.7 = (bf16[128,768]{1,0:T(8,128)(2,1)S(1)}, bf16[128,768]{1,0:T(8,128)(2,1)S(1)}, u32[]{:S(2)}, u32[]{:S(2)}) collective-permute-start(bf16[128,768]{1,0:T(8,128)(2,1)S(1)} %get-tuple-element.53), channel_id=1, source_target_pairs={{0,9},{1,8},{2,11},{3,10},{4,13},{5,12},{6,15},{7,14},{8,1},{9,0},... | collective-permute-start | bytes 589832 | tf_op jit(solution)/shard_map/ppermute | solution.py:419
  12.5 8.3 %collective-permute-start.5 = (bf16[224,384]{1,0:T(8,128)(2,1)S(1)}, bf16[224,384]{1,0:T(8,128)(2,1)S(1)}, u32[]{:S(2)}, u32[]{:S(2)}) collective-permute-start(bf16[224,384]{1,0:T(8,128)(2,1)S(1)} %assemble.1.refs_0_), channel_id=1, source_target_pairs={{0,6},{2,4},{4,2},{6,0},{8,14},{10,12},{12,10},{14,8},{16,22},{18,... | collective-permute-start | bytes 516104 | tf_op jit(solution)/shard_map/ppermute | solution.py:413
  15.0 9.1 %collective-permute-start.4 = (bf16[224,384]{1,0:T(8,128)(2,1)S(1)}, bf16[224,384]{1,0:T(8,128)(2,1)S(1)}, u32[]{:S(2)}, u32[]{:S(2)}) collective-permute-start(bf16[224,384]{1,0:T(8,128)(2,1)S(1)} %assemble.1.refs_0_), channel_id=1, source_target_pairs={{0,4},{2,6},{4,0},{6,2},{8,12},{10,14},{12,8},{14,10},{16,20},{18,... | collective-permute-start | bytes 516104 | tf_op jit(solution)/shard_map/ppermute | solution.py:413
  15.6 8.7 %collective-permute-start.3 = (bf16[224,384]{1,0:T(8,128)(2,1)S(1)}, bf16[224,384]{1,0:T(8,128)(2,1)S(1)}, u32[]{:S(2)}, u32[]{:S(2)}) collective-permute-start(bf16[224,384]{1,0:T(8,128)(2,1)S(1)} %assemble.1.refs_0_), channel_id=1, source_target_pairs={{0,2},{2,0},{4,6},{6,4},{8,10},{10,8},{12,14},{14,12},{16,18},{18,... | collective-permute-start | bytes 516104 | tf_op jit(solution)/shard_map/ppermute | solution.py:413
  27.5 2.4 %collective-permute-start.8 = (bf16[256,768]{1,0:T(8,128)(2,1)S(1)}, bf16[256,768]{1,0:T(8,128)(2,1)S(1)}, u32[]{:S(2)}, u32[]{:S(2)}) collective-permute-start(bf16[256,768]{1,0:T(8,128)(2,1)S(1)} %get-tuple-element.54.refs_1_), channel_id=1, source_target_pairs={{0,1},{1,0},{2,3},{3,2},{4,5},{5,4},{6,7},{7,6},{8,9},{9,8},{10,11... | collective-permute-start | bytes 1179656 | tf_op jit(solution)/shard_map/ppermute | solution.py:422
  27.6 2.0 %collective-permute-start.9 = (bf16[128,768]{1,0:T(8,128)(2,1)S(1)}, bf16[128,768]{1,0:T(8,128)(2,1)S(1)}, u32[]{:S(2)}, u32[]{:S(2)}) collective-permute-start(bf16[128,768]{1,0:T(8,128)(2,1)S(1)} %get-tuple-element.55), channel_id=1, source_target_pairs={{0,1},{1,0},{2,3},{3,2},{4,5},{5,4},{6,7},{7,6},{8,9},{9,8},{10,11... | collective-permute-start | bytes 589832 | tf_op jit(solution)/shard_map/ppermute | solution.py:422
  28.1 1.8 %collective-permute-start.10 = (bf16[128,768]{1,0:T(8,128)(2,1)S(1)}, bf16[128,768]{1,0:T(8,128)(2,1)S(1)}, u32[]{:S(2)}, u32[]{:S(2)}) collective-permute-start(bf16[128,768]{1,0:T(8,128)(2,1)S(1)} %collective-permute-done.7.refs_5_), channel_id=1, source_target_pairs={{0,1},{1,0},{2,3},{3,2},{4,5},{5,4},{6,7},{7,6},{8,9},{9,8},{10,11... | collective-permute-start | bytes 589832 | tf_op jit(solution)/shard_map/ppermute | solution.py:422
  32.0 3.7 %collective-permute-start.14 = (f32[256,768]{1,0:T(8,128)S(1)}, f32[256,768]{1,0:T(8,128)S(1)}, u32[]{:S(2)}, u32[]{:S(2)}) collective-permute-start(f32[256,768]{1,0:T(8,128)S(1)} %get-tuple-element.63), channel_id=1, source_target_pairs={{0,1},{1,0},{2,3},{3,2},{4,5},{5,4},{6,7},{7,6},{8,9},{9,8},{10,11... | collective-permute-start | bytes 2359304 | tf_op jit(solution)/shard_map/ppermute | solution.py:422
  32.2 8.7 %collective-permute-start.11 = (bf16[192,384]{1,0:T(8,128)(2,1)S(1)}, bf16[192,384]{1,0:T(8,128)(2,1)S(1)}, u32[]{:S(2)}, u32[]{:S(2)}) collective-permute-start(bf16[192,384]{1,0:T(8,128)(2,1)S(1)} %get-tuple-element.58), channel_id=1, source_target_pairs={{0,2},{2,0},{4,6},{6,4},{8,10},{10,8},{12,14},{14,12},{16,18},{18,... | collective-permute-start | bytes 442376 | tf_op jit(solution)/shard_map/ppermute | solution.py:413
  33.7 9.1 %collective-permute-start.12 = (bf16[192,384]{1,0:T(8,128)(2,1)S(1)}, bf16[192,384]{1,0:T(8,128)(2,1)S(1)}, u32[]{:S(2)}, u32[]{:S(2)}) collective-permute-start(bf16[192,384]{1,0:T(8,128)(2,1)S(1)} %get-tuple-element.59), channel_id=1, source_target_pairs={{0,4},{2,6},{4,0},{6,2},{8,12},{10,14},{12,8},{14,10},{16,20},{18,... | collective-permute-start | bytes 442376 | tf_op jit(solution)/shard_map/ppermute | solution.py:413
  34.4 8.3 %collective-permute-start.13 = (bf16[192,384]{1,0:T(8,128)(2,1)S(1)}, bf16[192,384]{1,0:T(8,128)(2,1)S(1)}, u32[]{:S(2)}, u32[]{:S(2)}) collective-permute-start(bf16[192,384]{1,0:T(8,128)(2,1)S(1)} %get-tuple-element.60), channel_id=1, source_target_pairs={{0,6},{2,4},{4,2},{6,0},{8,14},{10,12},{12,10},{14,8},{16,22},{18,... | collective-permute-start | bytes 442376 | tf_op jit(solution)/shard_map/ppermute | solution.py:413
  38.9 3.9 %collective-permute-start.15 = (bf16[96,128]{1,0:T(8,128)(2,1)S(1)}, bf16[96,128]{1,0:T(8,128)(2,1)S(1)}, u32[]{:S(2)}, u32[]{:S(2)}) collective-permute-start(bf16[96,128]{1,0:T(8,128)(2,1)S(1)} %get-tuple-element.68), channel_id=1, source_target_pairs={{0,3},{1,2},{2,1},{3,0},{4,7},{5,6},{6,5},{7,4},{8,11},{9,10},{10,... | collective-permute-start | bytes 73736 | tf_op jit(solution)/shard_map/ppermute | solution.py:419
  39.6 3.4 %collective-permute-start.16 = (bf16[96,128]{1,0:T(8,128)(2,1)S(1)}, bf16[96,128]{1,0:T(8,128)(2,1)S(1)}, u32[]{:S(2)}, u32[]{:S(2)}) collective-permute-start(bf16[96,128]{1,0:T(8,128)(2,1)S(1)} %get-tuple-element.69), channel_id=1, source_target_pairs={{0,5},{1,4},{2,7},{3,6},{4,1},{5,0},{6,3},{7,2},{8,13},{9,12},{10,... | collective-permute-start | bytes 73736 | tf_op jit(solution)/shard_map/ppermute | solution.py:419
  40.9 4.3 %collective-permute-start.17 = (bf16[96,128]{1,0:T(8,128)(2,1)S(1)}, bf16[96,128]{1,0:T(8,128)(2,1)S(1)}, u32[]{:S(2)}, u32[]{:S(2)}) collective-permute-start(bf16[96,128]{1,0:T(8,128)(2,1)S(1)} %get-tuple-element.70), channel_id=1, source_target_pairs={{0,7},{1,6},{2,5},{3,4},{4,3},{5,2},{6,1},{7,0},{8,15},{9,14},{10,... | collective-permute-start | bytes 73736 | tf_op jit(solution)/shard_map/ppermute | solution.py:419
  42.7 8.3 %collective-permute-start.18 = (bf16[6,8,16,128]{3,2,1,0:T(8,128)(2,1)S(1)}, bf16[6,8,16,128]{3,2,1,0:T(8,128)(2,1)S(1)}, u32[]{:S(2)}, u32[]{:S(2)}) collective-permute-start(bf16[6,8,16,128]{3,2,1,0:T(8,128)(2,1)S(1)} %get-tuple-element.73), channel_id=1, source_target_pairs={{0,9},{1,8},{2,11},{3,10},{4,13},{5,12},{6,15},{7,14},{8,1},{9,0},... | collective-permute-start | bytes 589832 | tf_op jit(solution)/shard_map/ppermute | solution.py:419
  45.2 7.7 %collective-permute-start.19 = (bf16[48,512]{1,0:T(8,128)(2,1)S(1)}, bf16[48,512]{1,0:T(8,128)(2,1)S(1)}, u32[]{:S(2)}, u32[]{:S(2)}) collective-permute-start(bf16[48,512]{1,0:T(8,128)(2,1)S(1)} %get-tuple-element.76), channel_id=1, source_target_pairs={{0,9},{1,8},{2,11},{3,10},{4,13},{5,12},{6,15},{7,14},{8,1},{9,0},... | collective-permute-start | bytes 147464 | tf_op jit(solution)/shard_map/ppermute | solution.py:419
  45.3 7.6 %collective-permute-start.20 = (bf16[48,512]{1,0:T(8,128)(2,1)S(1)}, bf16[48,512]{1,0:T(8,128)(2,1)S(1)}, u32[]{:S(2)}, u32[]{:S(2)}) collective-permute-start(bf16[48,512]{1,0:T(8,128)(2,1)S(1)} %get-tuple-element.77), channel_id=1, source_target_pairs={{0,17},{1,16},{2,19},{3,18},{4,21},{5,20},{6,23},{7,22},{8,25},{9,... | collective-permute-start | bytes 147464 | tf_op jit(solution)/shard_map/ppermute | solution.py:419
  48.2 6.1 %collective-permute-start.21 = (bf16[48,512]{1,0:T(8,128)(2,1)S(1)}, bf16[48,512]{1,0:T(8,128)(2,1)S(1)}, u32[]{:S(2)}, u32[]{:S(2)}) collective-permute-start(bf16[48,512]{1,0:T(8,128)(2,1)S(1)} %get-tuple-element.78), channel_id=1, source_target_pairs={{0,25},{1,24},{2,27},{3,26},{4,29},{5,28},{6,31},{7,30},{8,17},{9,... | collective-permute-start | bytes 147464 | tf_op jit(solution)/shard_map/ppermute | solution.py:419
  54.4 1.6 %collective-permute-start.22 = (f32[48,1280]{1,0:T(8,128)S(1)}, f32[48,1280]{1,0:T(8,128)S(1)}, u32[]{:S(2)}, u32[]{:S(2)}) collective-permute-start(f32[48,1280]{1,0:T(8,128)S(1)} %line_sum.1.mine_ref), channel_id=1, source_target_pairs={{0,1},{1,0},{2,3},{3,2},{4,5},{5,4},{6,7},{7,6},{8,9},{9,8},{10,11... | collective-permute-start | bytes 737288 | tf_op jit(solution)/shard_map/ppermute | solution.py:422

commit v11 on v9

--- a/solution.py
+++ b/solution.py
@@ -170,14 +170,13 @@
     return jnp.concatenate([rows, pltpu.roll(rows, LANES // 2, 1)], axis=0)
 
 
-def conv_norm_kernel(relative, own, *refs):
+def conv_norm_kernel(relative, own, height, breadth, *refs):
     small = refs[:INNER]
     sources = refs[INNER : INNER + 2]
     x_ref = sources[0]
     normed_ref, white_ref, inv_ref, taps_ref, gathered, unfolded, padded, conv = refs[INNER + 2 :]
-    height, breadth, depth = x_ref.shape[1:]
+    pixels, depth = x_ref.shape
     tiles = depth // LANES
-    pixels = height * breadth
     if relative:
         for group, piece in enumerate(small):
             unfolded[group * 2 * piece.shape[0] : (group + 1) * 2 * piece.shape[0], :] = unfold(
@@ -194,7 +193,8 @@
     for image, source in enumerate(sources):
         for tile in range(tiles):
             lanes = slice(tile * LANES, (tile + 1) * LANES)
-            padded[tile, :, 8 : 8 + breadth, :] = source[0, :, :, lanes].astype(F32)
+            part = source[:pixels, lanes].astype(F32)
+            padded[tile, :, 8 : 8 + breadth, :] = part.reshape(height, breadth, LANES)
 
         def one_tile(tile, carry):
             sums = correlate(
@@ -230,14 +230,16 @@
             normed_ref[rows, lanes] = (whitened * gain + bias).astype(BF16)
 
 
-def cot_pack_kernel(cot_ref, across_ref, sibling_ref):
-    half = sibling_ref.shape[1]
+def cot_pack_kernel(image_ref, cot_ref, across_ref, sibling_ref):
+    pixels, half = sibling_ref.shape
     quarter = half // 2
     side = lax.axis_index("rep") % 2
     parity = (lax.axis_index("shard") // INNER) % 2
     for place in range(2):
         start = pl.multiple_of(place * half + (1 - parity) * quarter, LANES)
-        across_ref[:, place * quarter : (place + 1) * quarter] = cot_ref[:, pl.ds(start, quarter)]
+        lanes = slice(place * quarter, (place + 1) * quarter)
+        across_ref[pixels:, lanes] = cot_ref[:, pl.ds(start, quarter)]
+    across_ref[:pixels, :] = image_ref[...]
     sibling_ref[...] = cot_ref[:, pl.ds(pl.multiple_of((1 - side) * half, LANES), half)]
 
 
@@ -258,11 +260,11 @@
     start = pl.multiple_of(side * half + parity * quarter, LANES)
     cot[:pixels, :] = cot_ref[:, pl.ds(start, quarter)]
     start = pl.multiple_of(side * quarter, LANES)
-    cot[pixels : 2 * pixels, :] = across_ref[:, pl.ds(start, quarter)]
+    cot[pixels : 2 * pixels, :] = across_ref[pixels:, pl.ds(start, quarter)]
     start = pl.multiple_of(parity * quarter, LANES)
     cot[2 * pixels : 3 * pixels, :] = sibling_ref[:, pl.ds(start, quarter)]
     start = pl.multiple_of(side * quarter, LANES)
-    cot[3 * pixels :, :] = corner_ref[:, pl.ds(start, quarter)]
+    cot[3 * pixels :, :] = corner_ref[pixels:, pl.ds(start, quarter)]
     for start in range(0, quarter, LANES):
         columns = slice(start, start + LANES)
         pre_act = jnp.dot(normed[...], weight[:, columns], preferred_element_type=F32)
@@ -282,13 +284,12 @@
     other_ref[...] = grad_normed[rows:]
 
 
-def norm_back_kernel(relative, own, *refs):
+def norm_back_kernel(relative, own, height, breadth, *refs):
     gn_own, gn_other, white_ref, inv_ref, taps_ref, x_ref, far_ref = refs[:7]
     pieces = refs[7 : 7 + INNER]
     grad_ref, sent_ref, padded, grads_ref, rows, small, unfolded = refs[7 + INNER :]
-    height, breadth, depth = x_ref.shape[1:]
+    pixels, depth = x_ref.shape
     tiles = depth // LANES
-    pixels = height * breadth
     padded[...] = jnp.zeros_like(padded)
     rows[...] = jnp.zeros_like(rows)
     for image, source in enumerate((x_ref, far_ref)):
@@ -297,7 +298,8 @@
         second = None
         for tile in range(tiles):
             lanes = slice(tile * LANES, (tile + 1) * LANES)
-            padded[image, tile, :, 8 : 8 + breadth, :] = source[0, :, :, lanes].astype(F32)
+            part = source[:pixels, lanes].astype(F32)
+            padded[image, tile, :, 8 : 8 + breadth, :] = part.reshape(height, breadth, LANES)
             grad_normed = gn_own[span, lanes] + gn_other[span, lanes]
             whitened = white_ref[span, lanes]
             product = grad_normed * whitened
@@ -446,23 +448,23 @@
         norm_bias[None, :],
         mebibytes=63,
     )
-    home, near, far, images, cotangent = lax.optimization_barrier(
-        (home, near, far, images, cotangent)
+    image, cotangent = images.reshape(pixels, depth), cotangent.reshape(pixels, hidden)
+    home, near, far, image, cotangent = lax.optimization_barrier(
+        (home, near, far, image, cotangent)
     )
     gathered = [home] + [
         crossing(far if line % 2 else near, INNER * line) for line in range(1, lines)
     ]
-    cotangent = cotangent.reshape(pixels, hidden)
-    cot_across, cot_sibling = call(
+    across, cot_sibling = call(
         cot_pack_kernel,
         "cot_pack",
-        [shape((pixels, half), BF16)] * 2,
+        [shape((2 * pixels, half), BF16), shape((pixels, half), BF16)],
         [],
         0.4,
+        image,
         cotangent,
     )
-    cot_across, cot_sibling = crossing(cot_across, INNER), over_core(cot_sibling)
-    images_far = crossing(images, INNER)
+    across, cot_sibling = crossing(across, INNER), over_core(cot_sibling)
 
     rows = lines * own
     folded = rows // 2 if relative else rows
@@ -471,7 +473,7 @@
         "assemble",
         [shape((rows, quarter), BF16), shape((folded, LANES), BF16)],
         [],
-        2.0,
+        4.0,
         *gathered,
     )
     weights = [weight_lines] + [over_shard(weight_lines, flip) for flip in range(1, INNER)]
@@ -482,13 +484,13 @@
         "order",
         [shape((depth, quarter), BF16)],
         [],
-        3.0,
+        2.6,
         *weights,
     )
 
     padded = pltpu.VMEM((tiles, height, breadth + 16, LANES), F32)
     normed, whitened, inv_std, taps = call(
-        functools.partial(conv_norm_kernel, relative, own),
+        functools.partial(conv_norm_kernel, relative, own, height, breadth),
         "conv_norm",
         [
             shape((2 * pixels, depth), BF16),
@@ -504,11 +506,11 @@
         ],
         0.1,
         *extras,
-        images,
-        images_far,
-    )
-    normed, cot_across = lax.optimization_barrier((normed, cot_across))
-    normed_sibling, cot_corner = over_core(normed), over_core(cot_across)
+        image,
+        across,
+    )
+    normed, across = lax.optimization_barrier((normed, across))
+    normed_sibling, corner = over_core(normed), over_core(across)
     *pieces, grad_pre = call(
         functools.partial(project_kernel, relative, own),
         "project",
@@ -526,8 +528,8 @@
         normed_sibling,
         cotangent,
         cot_sibling,
-        cot_across,
-        cot_corner,
+        across,
+        corner,
     )
     gn_kept, gn_sent = call(
         back_project_kernel,
@@ -541,7 +543,7 @@
     pieces = relative_order(pieces)
     arrived = [over_shard(piece, flip) for flip, piece in enumerate(pieces) if flip]
     *small, grad_conv, grad_sent = call(
-        functools.partial(norm_back_kernel, relative, own),
+        functools.partial(norm_back_kernel, relative, own, height, breadth),
         "norm_back",
         [shape((folded, LANES), F32)]
         + [shape((folded, LANES), BF16)] * (INNER - 1)
@@ -562,8 +564,8 @@
         whitened,
         inv_std,
         taps,
-        images,
-        images_far,
+        image,
+        across,
     )
     small = relative_order(small)
     small_arrived = [crossing(piece, flip) for flip, piece in enumerate(small) if flip]

time: 54.6 us -> 54.4 us (level)
    ppermute x6, waiting for transfers between devices: 4.4 us -> 1.83 us  [over_shard(): return lax.ppermute(array, 'shard', [(i, i ^ flip) for i in range(shards)])]
    ppermute x15 -> x14, waiting for transfers between devices: 9.19 us -> 11.1 us  [crossing(): return lax.ppermute(array, ('shard', 'rep'), pairs)]
    ppermute x15 -> x14, starting transfers between devices: 17.5 us -> 16.6 us  [crossing(): return lax.ppermute(array, ('shard', 'rep'), pairs)]
    ppermute x5, starting transfers between devices: 0.77 us -> 1.47 us  [over_core(): return lax.ppermute(array, 'rep', [(i, i ^ 1) for i in range(reps)])]
    ppermute x5, waiting for transfers between devices: 1.46 us -> 2.02 us  [over_core(): return lax.ppermute(array, 'rep', [(i, i ^ 1) for i in range(reps)])]
  transfers between devices with their start and end apart: 26 -> 25, of which waited for: 12 -> 12; matrix products, arithmetic and copies ran while one was open for 0% -> 0% of each run, Pallas kernels for 16% -> 16%
where the time goes in v11:
time: 54.4 us; the launch traced here: 54.2 us
  starting transfers between devices  25.2 us (46%)
  waiting for transfers between devices  15 us (28%)
  Pallas kernels  13.3 us (24%)
  between operations  0.74 us (1%)
    ppermute x14, starting transfers between devices, crossing(): return lax.ppermute(array, ('shard', 'rep'), pairs)  16.6 us
    pallas_call x12, Pallas kernels, call(): pl.pallas_call(kernel, out_shape=outs, in_specs=[VMEM] * len(args), out_s...  13.3 us
    ppermute x14, waiting for transfers between devices, crossing(): return lax.ppermute(array, ('shard', 'rep'), pairs)  11.1 us
    ppermute x6, starting transfers between devices, over_shard(): return lax.ppermute(array, 'shard', [(i, i ^ flip) for i in range(shards)])  7.15 us
    ppermute x5, waiting for transfers between devices, over_core(): return lax.ppermute(array, 'rep', [(i, i ^ 1) for i in range(reps)])  2.02 us
    ppermute x6, waiting for transfers between devices, over_shard(): return lax.ppermute(array, 'shard', [(i, i ^ flip) for i in range(shards)])  1.83 us
    ppermute x5, starting transfers between devices, over_core(): return lax.ppermute(array, 'rep', [(i, i ^ 1) for i in range(reps)])  1.47 us
  transfers between devices with their start and end apart: 25, of which 12 were waited for; matrix products, arithmetic and copies ran while one was open for 0% of the time, Pallas kernels for 16%

profile of v11, /device:TPU:0, one launch (start us, length us, event | category | flops | bytes accessed | tf_op | source)
XLA Modules:
  0.0 54.2 jit_solution(15221574953166463174)
XLA Ops:
  0.6 0.0 copy-start
  0.6 0.0 copy-start.1
  0.7 1.7 %pack.1 = (bf16[48,512]{1,0:T(8,128)(2,1)}, bf16[48,512]{1,0:T(8,128)(2,1)}, bf16[48,512]{1,0:T(8,128)(2,1)}) custom-call(bf16[48,1536]{1,0:T(8,128)(2,1)} %w_ref.1, bf16[48,49]{1,0:T(8,128)(2,1)} %dw_ref.1, bf16[1,48]{1,0:T(2,128)(2,1)} %bitcast.11, bf16[1,48]{1,0:T(2,128)(2,1)} %bitcast.12), custom_call_target="tpu_custom_call" | custom-call | flops 550000000 | bytes 299808 | tf_op jit(solution)/shard_map/pack/pallas_call | solution.py:381
  2.4 3.5 %collective-permute-start.1 = (bf16[48,512]{1,0:T(8,128)(2,1)}, bf16[48,512]{1,0:T(8,128)(2,1)S(1)}, u32[]{:S(2)}, u32[]{:S(2)}) collective-permute-start(bf16[48,512]{1,0:T(8,128)(2,1)} %get-tuple-element.51), channel_id=1, source_target_pairs={{0,17},{1,16},{2,19},{3,18},{4,21},{5,20},{6,23},{7,22},{8,25},{9,... | collective-permute-start | bytes 147464 | tf_op jit(solution)/shard_map/ppermute | solution.py:414
  5.9 1.6 %collective-permute-start.2 = (bf16[48,512]{1,0:T(8,128)(2,1)}, bf16[48,512]{1,0:T(8,128)(2,1)S(1)}, u32[]{:S(2)}, u32[]{:S(2)}) collective-permute-start(bf16[48,512]{1,0:T(8,128)(2,1)} %get-tuple-element.50), channel_id=1, source_target_pairs={{0,25},{1,24},{2,27},{3,26},{4,29},{5,28},{6,31},{7,30},{8,17},{9,... | collective-permute-start | bytes 147464 | tf_op jit(solution)/shard_map/ppermute | solution.py:414
  7.5 0.2 collective-permute-start
  7.7 0.0 copy-done
  7.7 0.0 copy-done.1
  7.8 1.6 %collective-permute-start.9 = (bf16[256,768]{1,0:T(8,128)(2,1)S(1)}, bf16[256,768]{1,0:T(8,128)(2,1)S(1)}, u32[]{:S(2)}, u32[]{:S(2)}) collective-permute-start(bf16[256,768]{1,0:T(8,128)(2,1)S(1)} %get-tuple-element.56), channel_id=1, source_target_pairs={{0,9},{1,8},{2,11},{3,10},{4,13},{5,12},{6,15},{7,14},{8,1},{9,0},... | collective-permute-start | bytes 1179656 | tf_op jit(solution)/shard_map/ppermute | solution.py:414
  9.4 0.0 collective-permute-done.1.refs_2_
  9.4 2.1 %collective-permute-done.2.refs_3_ = bf16[48,512]{1,0:T(8,128)(2,1)S(1)} collective-permute-done((bf16[48,512]{1,0:T(8,128)(2,1)}, bf16[48,512]{1,0:T(8,128)(2,1)S(1)}, u32[]{:S(2)}, u32[]{:S(2)}) %collective-permute-start.2) | collective-permute-done | bytes 49184 | tf_op jit(solution)/shard_map/ppermute | solution.py:414
  11.5 0.9 %collective-permute-done.refs_1_ = bf16[48,512]{1,0:T(8,128)(2,1)S(1)} collective-permute-done((bf16[48,512]{1,0:T(8,128)(2,1)}, bf16[48,512]{1,0:T(8,128)(2,1)S(1)}, u32[]{:S(2)}, u32[]{:S(2)}) %collective-permute-start) | collective-permute-done | bytes 49184 | tf_op jit(solution)/shard_map/ppermute | solution.py:414
  12.4 0.1 assemble.1
  12.5 2.9 %collective-permute-start.8 = (bf16[96,128]{1,0:T(8,128)(2,1)S(1)}, bf16[96,128]{1,0:T(8,128)(2,1)S(1)}, u32[]{:S(2)}, u32[]{:S(2)}) collective-permute-start(bf16[96,128]{1,0:T(8,128)(2,1)S(1)} %get-tuple-element.53.refs_0_), channel_id=1, source_target_pairs={{0,7},{1,6},{2,5},{3,4},{4,3},{5,2},{6,1},{7,0},{8,15},{9,14},{10,... | collective-permute-start | bytes 73736 | tf_op jit(solution)/shard_map/ppermute | solution.py:414
  15.4 0.0 collective-permute-start.7
  15.4 0.8 %collective-permute-start.6 = (bf16[96,128]{1,0:T(8,128)(2,1)S(1)}, bf16[96,128]{1,0:T(8,128)(2,1)S(1)}, u32[]{:S(2)}, u32[]{:S(2)}) collective-permute-start(bf16[96,128]{1,0:T(8,128)(2,1)S(1)} %get-tuple-element.53.refs_0_), channel_id=1, source_target_pairs={{0,3},{1,2},{2,1},{3,0},{4,7},{5,6},{6,5},{7,4},{8,11},{9,10},{10,... | collective-permute-start | bytes 73736 | tf_op jit(solution)/shard_map/ppermute | solution.py:414
  16.1 2.4 %collective-permute-start.5 = (bf16[192,384]{1,0:T(8,128)(2,1)S(1)}, bf16[192,384]{1,0:T(8,128)(2,1)S(1)}, u32[]{:S(2)}, u32[]{:S(2)}) collective-permute-start(bf16[192,384]{1,0:T(8,128)(2,1)S(1)} %get-tuple-element.52.refs_0_), channel_id=1, source_target_pairs={{0,6},{2,4},{4,2},{6,0},{8,14},{10,12},{12,10},{14,8},{16,22},{18,... | collective-permute-start | bytes 442376 | tf_op jit(solution)/shard_map/ppermute | solution.py:408
  18.6 0.0 collective-permute-done.8.refs_3_
  18.6 0.5 collective-permute-start.4
  19.1 0.0 collective-permute-done.7.refs_2_
  19.1 0.7 %collective-permute-start.3 = (bf16[192,384]{1,0:T(8,128)(2,1)S(1)}, bf16[192,384]{1,0:T(8,128)(2,1)S(1)}, u32[]{:S(2)}, u32[]{:S(2)}) collective-permute-start(bf16[192,384]{1,0:T(8,128)(2,1)S(1)} %get-tuple-element.52.refs_0_), channel_id=1, source_target_pairs={{0,2},{2,0},{4,6},{6,4},{8,10},{10,8},{12,14},{14,12},{16,18},{18,... | collective-permute-start | bytes 442376 | tf_op jit(solution)/shard_map/ppermute | solution.py:408
  19.8 0.0 collective-permute-done.6.refs_1_
  19.8 1.1 %collective-permute-done.9.refs_5_.refs_6_ = bf16[256,768]{1,0:T(8,128)(2,1)S(1)} collective-permute-done((bf16[256,768]{1,0:T(8,128)(2,1)S(1)}, bf16[256,768]{1,0:T(8,128)(2,1)S(1)}, u32[]{:S(2)}, u32[]{:S(2)}) %collective-permute-start.9) | collective-permute-done | bytes 393248 | tf_op jit(solution)/shard_map/ppermute | solution.py:414
  20.9 3.2 %conv_norm.1 = (bf16[256,768]{1,0:T(8,128)(2,1)S(1)}, f32[256,768]{1,0:T(8,128)S(1)}, f32[256,128]{1,0:T(8,128)S(1)}, f32[6,128,128]{2,1,0:T(8,128)S(1)}) custom-call(bf16[96,128]{1,0:T(8,128)(2,1)S(1)} %get-tuple-element.53.refs_0_, bf16[96,128]{1,0:T(8,128)(2,1)S(1)} %collective-permute-done.6.refs_1_, bf16[96,128]{1,0:T(8,128)(2,1)S(1)} %collective-permute-done.7.refs_2_, ...), custom_call_target="tpu_custom_call" | custom-call | flops 110000000 | bytes 2392064 | tf_op jit(solution)/shard_map/conv_norm/pallas_call | solution.py:381
  24.2 0.4 collective-permute-start.10
  24.6 0.1 collective-permute-start.12
  24.7 0.0 collective-permute-done.5.refs_3_
  24.7 0.4 collective-permute-start.11
  25.1 1.1 %collective-permute-done.4.refs_2_ = bf16[192,384]{1,0:T(8,128)(2,1)S(1)} collective-permute-done((bf16[192,384]{1,0:T(8,128)(2,1)S(1)}, bf16[192,384]{1,0:T(8,128)(2,1)S(1)}, u32[]{:S(2)}, u32[]{:S(2)}) %collective-permute-start.4) | collective-permute-done | bytes 147488 | tf_op jit(solution)/shard_map/ppermute | solution.py:408
  26.2 0.0 collective-permute-done.3.refs_1_
  26.2 0.1 order.1.refs_0_.weight
  26.3 0.5 collective-permute-done.11.refs_4_
  26.8 0.0 collective-permute-done.10.refs_2_
  26.8 0.0 collective-permute-done.12.refs_6_
  26.8 1.5 %project.1 = (f32[192,384]{1,0:T(8,128)S(1)}, bf16[192,384]{1,0:T(8,128)(2,1)S(1)}, bf16[192,384]{1,0:T(8,128)(2,1)S(1)}, bf16[192,384]{1,0:T(8,128)(2,1)S(1)}, bf16[512,384]{1,0:T(8,128)(2,1)S(1)}) custom-call(bf16[768,384]{1,0:T(8,128)(2,1)S(1)} %order.1.refs_0_.weight, bf16[256,768]{1,0:T(8,128)(2,1)S(1)} %get-tuple-element.58.refs_1_, ...), custom_call_target="tpu_custom_call" | custom-call | flops 1760000000 | bytes 3883008 | tf_op jit(solution)/shard_map/project/pallas_call | solution.py:381
  28.3 0.6 %back_project.1 = (f32[256,768]{1,0:T(8,128)S(1)}, f32[256,768]{1,0:T(8,128)S(1)}) custom-call(bf16[768,384]{1,0:T(8,128)(2,1)S(1)} %order.1.refs_0_.weight, bf16[512,384]{1,0:T(8,128)(2,1)S(1)} %get-tuple-element.65.gp_ref), custom_call_target="tpu_custom_call" | custom-call | flops 770000000 | bytes 2555904 | tf_op jit(solution)/shard_map/back_project/pallas_call | solution.py:381
  28.9 0.4 collective-permute-start.16
  29.4 1.5 %collective-permute-start.13 = (bf16[192,384]{1,0:T(8,128)(2,1)S(1)}, bf16[192,384]{1,0:T(8,128)(2,1)S(1)}, u32[]{:S(2)}, u32[]{:S(2)}) collective-permute-start(bf16[192,384]{1,0:T(8,128)(2,1)S(1)} %get-tuple-element.62), channel_id=1, source_target_pairs={{0,2},{2,0},{4,6},{6,4},{8,10},{10,8},{12,14},{14,12},{16,18},{18,... | collective-permute-start | bytes 442376 | tf_op jit(solution)/shard_map/ppermute | solution.py:408
  30.9 1.5 %collective-permute-start.14 = (bf16[192,384]{1,0:T(8,128)(2,1)S(1)}, bf16[192,384]{1,0:T(8,128)(2,1)S(1)}, u32[]{:S(2)}, u32[]{:S(2)}) collective-permute-start(bf16[192,384]{1,0:T(8,128)(2,1)S(1)} %get-tuple-element.63), channel_id=1, source_target_pairs={{0,4},{2,6},{4,0},{6,2},{8,12},{10,14},{12,8},{14,10},{16,20},{18,... | collective-permute-start | bytes 442376 | tf_op jit(solution)/shard_map/ppermute | solution.py:408
  32.4 0.5 collective-permute-start.15
  32.9 0.0 collective-permute-done.16.refs_1_
  32.9 3.2 %norm_back.1 = (f32[96,128]{1,0:T(8,128)S(1)}, bf16[96,128]{1,0:T(8,128)(2,1)S(1)}, bf16[96,128]{1,0:T(8,128)(2,1)S(1)}, bf16[96,128]{1,0:T(8,128)(2,1)S(1)}, f3...) custom-call(f32[256,768]{1,0:T(8,128)S(1)} %get-tuple-element.66.refs_0_, ...), custom_call_target="tpu_custom_call" | custom-call | flops 110000000 | bytes 4186112 | tf_op jit(solution)/shard_map/norm_back/pallas_call | solution.py:381
  36.1 0.5 collective-permute-start.17
  36.5 2.3 %collective-permute-start.18 = (bf16[96,128]{1,0:T(8,128)(2,1)S(1)}, bf16[96,128]{1,0:T(8,128)(2,1)S(1)}, u32[]{:S(2)}, u32[]{:S(2)}) collective-permute-start(bf16[96,128]{1,0:T(8,128)(2,1)S(1)} %get-tuple-element.73), channel_id=1, source_target_pairs={{0,5},{1,4},{2,7},{3,6},{4,1},{5,0},{6,3},{7,2},{8,13},{9,12},{10,... | collective-permute-start | bytes 73736 | tf_op jit(solution)/shard_map/ppermute | solution.py:414
  38.9 0.0 collective-permute-done.13.refs_1_
  38.9 0.0 collective-permute-start.19
  38.9 0.7 %collective-permute-done.14.refs_2_ = bf16[192,384]{1,0:T(8,128)(2,1)S(1)} collective-permute-done((bf16[192,384]{1,0:T(8,128)(2,1)S(1)}, bf16[192,384]{1,0:T(8,128)(2,1)S(1)}, u32[]{:S(2)}, u32[]{:S(2)}) %collective-permute-start.14) | collective-permute-done | bytes 147488 | tf_op jit(solution)/shard_map/ppermute | solution.py:408
  39.6 0.0 collective-permute-start.20
  39.6 0.0 collective-permute-done.15.refs_3_
  39.7 0.0 collective-permute-done.17.refs_5_
  39.7 0.7 %collective-permute-done.18.refs_6_ = bf16[96,128]{1,0:T(8,128)(2,1)S(1)} collective-permute-done((bf16[96,128]{1,0:T(8,128)(2,1)S(1)}, bf16[96,128]{1,0:T(8,128)(2,1)S(1)}, u32[]{:S(2)}, u32[]{:S(2)}) %collective-permute-start.18) | collective-permute-done | bytes 24608 | tf_op jit(solution)/shard_map/ppermute | solution.py:414
  40.4 2.6 %collective-permute-done.19.refs_7_ = bf16[96,128]{1,0:T(8,128)(2,1)S(1)} collective-permute-done((bf16[96,128]{1,0:T(8,128)(2,1)S(1)}, bf16[96,128]{1,0:T(8,128)(2,1)S(1)}, u32[]{:S(2)}, u32[]{:S(2)}) %collective-permute-start.19) | collective-permute-done | bytes 24608 | tf_op jit(solution)/shard_map/ppermute | solution.py:414
  43.0 0.1 plane_sum.1
  43.1 0.1 collective-permute-start.21
  43.2 3.1 %collective-permute-start.22 = (bf16[48,512]{1,0:T(8,128)(2,1)S(1)}, bf16[48,512]{1,0:T(8,128)(2,1)S(1)}, u32[]{:S(2)}, u32[]{:S(2)}) collective-permute-start(bf16[48,512]{1,0:T(8,128)(2,1)S(1)} %get-tuple-element.81), channel_id=1, source_target_pairs={{0,17},{1,16},{2,19},{3,18},{4,21},{5,20},{6,23},{7,22},{8,25},{9,... | collective-permute-start | bytes 147464 | tf_op jit(solution)/shard_map/ppermute | solution.py:414
  46.3 0.0 collective-permute-start.23
  46.3 0.5 collective-permute-done.20.other_ref
  46.8 1.9 %conv_back.1 = bf16[1,8,16,768]{3,2,1,0:T(8,128)(2,1)} custom-call(f32[6,8,16,128]{3,2,1,0:T(8,128)S(1)} %get-tuple-element.76.grad_ref, bf16[6,8,16,128]{3,2,1,0:T(8,128)(2,1)S(1)} %collective-permute-done.20.other_ref, f32[6,128,128]{2,1,0:T(8,128)S(1)} %get-tuple-element.70.refs_4_.taps_ref), custom_call_target="tpu_custom_call" | custom-call | flops 110000000 | bytes 1179648 | tf_op jit(solution)/shard_map/conv_back/pallas_call | solution.py:381
  48.8 0.2 collective-permute-done.21.refs_1_
  48.9 0.0 collective-permute-done.22.refs_2_
  49.0 2.9 %collective-permute-done.23.refs_3_ = bf16[48,512]{1,0:T(8,128)(2,1)S(1)} collective-permute-done((bf16[48,512]{1,0:T(8,128)(2,1)S(1)}, bf16[48,512]{1,0:T(8,128)(2,1)S(1)}, u32[]{:S(2)}, u32[]{:S(2)}) %collective-permute-start.23) | collective-permute-done | bytes 49184 | tf_op jit(solution)/shard_map/ppermute | solution.py:414
  51.9 0.1 collective-permute-start.24
  52.0 1.5 %collective-permute-done.24.other_ref = f32[48,1280]{1,0:T(8,128)S(1)} collective-permute-done((f32[48,1280]{1,0:T(8,128)S(1)}, f32[48,1280]{1,0:T(8,128)S(1)}, u32[]{:S(2)}, u32[]{:S(2)}) %collective-permute-start.24) | collective-permute-done | bytes 245792 | tf_op jit(solution)/shard_map/ppermute | solution.py:417
  53.5 0.8 %finish.1 = (f32[48,1536]{1,0:T(8,128)}, f32[48,49]{1,0:T(8,128)}, f32[1,48]{1,0:T(1,128)}, f32[1,48]{1,0:T(1,128)}) custom-call(f32[48,1280]{1,0:T(8,128)S(1)} %line_sum.1.mine_ref, f32[48,1280]{1,0:T(8,128)S(1)} %collective-permute-done.24.other_ref), custom_call_target="tpu_custom_call" | custom-call | flops 550000000 | bytes 796224 | tf_op jit(solution)/shard_map/finish/pallas_call | solution.py:381
  (4 shorter events, 0.1 us)
Async XLA Ops:
  0.6 7.1 %copy-start = (bf16[1,8,16,768]{3,2,1,0:T(8,128)(2,1)S(1)}, bf16[1,8,16,768]{3,2,1,0:T(8,128)(2,1)}, u32[]{:S(2)}) copy-start(bf16[1,8,16,768]{3,2,1,0:T(8,128)(2,1)} %param.6) | copy-start | bytes 589828
  0.6 7.1 %copy-start.1 = (bf16[1,8,16,1536]{3,2,1,0:T(8,128)(2,1)S(1)}, bf16[1,8,16,1536]{3,2,1,0:T(8,128)(2,1)}, u32[]{:S(2)}) copy-start(bf16[1,8,16,1536]{3,2,1,0:T(8,128)(2,1)} %param.7) | copy-start | bytes 1179652
  2.4 10.0 %copy-start.2 = (bf16[48,512]{1,0:T(8,128)(2,1)S(1)}, bf16[48,512]{1,0:T(8,128)(2,1)}, u32[]{:S(2)}) copy-start(bf16[48,512]{1,0:T(8,128)(2,1)} %get-tuple-element.49.refs_0_) | copy-start | bytes 147460
  2.4 7.0 %collective-permute-start.1 = (bf16[48,512]{1,0:T(8,128)(2,1)}, bf16[48,512]{1,0:T(8,128)(2,1)S(1)}, u32[]{:S(2)}, u32[]{:S(2)}) collective-permute-start(bf16[48,512]{1,0:T(8,128)(2,1)} %get-tuple-element.51), channel_id=1, source_target_pairs={{0,17},{1,16},{2,19},{3,18},{4,21},{5,20},{6,23},{7,22},{8,25},{9,... | collective-permute-start | bytes 147464 | tf_op jit(solution)/shard_map/ppermute | solution.py:414
  5.9 5.6 %collective-permute-start.2 = (bf16[48,512]{1,0:T(8,128)(2,1)}, bf16[48,512]{1,0:T(8,128)(2,1)S(1)}, u32[]{:S(2)}, u32[]{:S(2)}) collective-permute-start(bf16[48,512]{1,0:T(8,128)(2,1)} %get-tuple-element.50), channel_id=1, source_target_pairs={{0,25},{1,24},{2,27},{3,26},{4,29},{5,28},{6,31},{7,30},{8,17},{9,... | collective-permute-start | bytes 147464 | tf_op jit(solution)/shard_map/ppermute | solution.py:414
  7.5 4.9 %collective-permute-start = (bf16[48,512]{1,0:T(8,128)(2,1)}, bf16[48,512]{1,0:T(8,128)(2,1)S(1)}, u32[]{:S(2)}, u32[]{:S(2)}) collective-permute-start(bf16[48,512]{1,0:T(8,128)(2,1)} %get-tuple-element.50), channel_id=1, source_target_pairs={{0,9},{1,8},{2,11},{3,10},{4,13},{5,12},{6,15},{7,14},{8,1},{9,0},... | collective-permute-start | bytes 147464 | tf_op jit(solution)/shard_map/ppermute | solution.py:414
  7.8 13.2 %collective-permute-start.9 = (bf16[256,768]{1,0:T(8,128)(2,1)S(1)}, bf16[256,768]{1,0:T(8,128)(2,1)S(1)}, u32[]{:S(2)}, u32[]{:S(2)}) collective-permute-start(bf16[256,768]{1,0:T(8,128)(2,1)S(1)} %get-tuple-element.56), channel_id=1, source_target_pairs={{0,9},{1,8},{2,11},{3,10},{4,13},{5,12},{6,15},{7,14},{8,1},{9,0},... | collective-permute-start | bytes 1179656 | tf_op jit(solution)/shard_map/ppermute | solution.py:414
  12.5 6.1 %collective-permute-start.8 = (bf16[96,128]{1,0:T(8,128)(2,1)S(1)}, bf16[96,128]{1,0:T(8,128)(2,1)S(1)}, u32[]{:S(2)}, u32[]{:S(2)}) collective-permute-start(bf16[96,128]{1,0:T(8,128)(2,1)S(1)} %get-tuple-element.53.refs_0_), channel_id=1, source_target_pairs={{0,7},{1,6},{2,5},{3,4},{4,3},{5,2},{6,1},{7,0},{8,15},{9,14},{10,... | collective-permute-start | bytes 73736 | tf_op jit(solution)/shard_map/ppermute | solution.py:414
  15.4 3.7 %collective-permute-start.7 = (bf16[96,128]{1,0:T(8,128)(2,1)S(1)}, bf16[96,128]{1,0:T(8,128)(2,1)S(1)}, u32[]{:S(2)}, u32[]{:S(2)}) collective-permute-start(bf16[96,128]{1,0:T(8,128)(2,1)S(1)} %get-tuple-element.53.refs_0_), channel_id=1, source_target_pairs={{0,5},{1,4},{2,7},{3,6},{4,1},{5,0},{6,3},{7,2},{8,13},{9,12},{10,... | collective-permute-start | bytes 73736 | tf_op jit(solution)/shard_map/ppermute | solution.py:414
  15.4 4.4 %collective-permute-start.6 = (bf16[96,128]{1,0:T(8,128)(2,1)S(1)}, bf16[96,128]{1,0:T(8,128)(2,1)S(1)}, u32[]{:S(2)}, u32[]{:S(2)}) collective-permute-start(bf16[96,128]{1,0:T(8,128)(2,1)S(1)} %get-tuple-element.53.refs_0_), channel_id=1, source_target_pairs={{0,3},{1,2},{2,1},{3,0},{4,7},{5,6},{6,5},{7,4},{8,11},{9,10},{10,... | collective-permute-start | bytes 73736 | tf_op jit(solution)/shard_map/ppermute | solution.py:414
  16.1 8.6 %collective-permute-start.5 = (bf16[192,384]{1,0:T(8,128)(2,1)S(1)}, bf16[192,384]{1,0:T(8,128)(2,1)S(1)}, u32[]{:S(2)}, u32[]{:S(2)}) collective-permute-start(bf16[192,384]{1,0:T(8,128)(2,1)S(1)} %get-tuple-element.52.refs_0_), channel_id=1, source_target_pairs={{0,6},{2,4},{4,2},{6,0},{8,14},{10,12},{12,10},{14,8},{16,22},{18,... | collective-permute-start | bytes 442376 | tf_op jit(solution)/shard_map/ppermute | solution.py:408
  18.6 7.6 %collective-permute-start.4 = (bf16[192,384]{1,0:T(8,128)(2,1)S(1)}, bf16[192,384]{1,0:T(8,128)(2,1)S(1)}, u32[]{:S(2)}, u32[]{:S(2)}) collective-permute-start(bf16[192,384]{1,0:T(8,128)(2,1)S(1)} %get-tuple-element.52.refs_0_), channel_id=1, source_target_pairs={{0,4},{2,6},{4,0},{6,2},{8,12},{10,14},{12,8},{14,10},{16,20},{18,... | collective-permute-start | bytes 442376 | tf_op jit(solution)/shard_map/ppermute | solution.py:408
  19.1 7.1 %collective-permute-start.3 = (bf16[192,384]{1,0:T(8,128)(2,1)S(1)}, bf16[192,384]{1,0:T(8,128)(2,1)S(1)}, u32[]{:S(2)}, u32[]{:S(2)}) collective-permute-start(bf16[192,384]{1,0:T(8,128)(2,1)S(1)} %get-tuple-element.52.refs_0_), channel_id=1, source_target_pairs={{0,2},{2,0},{4,6},{6,4},{8,10},{10,8},{12,14},{14,12},{16,18},{18,... | collective-permute-start | bytes 442376 | tf_op jit(solution)/shard_map/ppermute | solution.py:408
  24.2 2.6 %collective-permute-start.10 = (bf16[256,768]{1,0:T(8,128)(2,1)S(1)}, bf16[256,768]{1,0:T(8,128)(2,1)S(1)}, u32[]{:S(2)}, u32[]{:S(2)}) collective-permute-start(bf16[256,768]{1,0:T(8,128)(2,1)S(1)} %get-tuple-element.58.refs_1_), channel_id=1, source_target_pairs={{0,1},{1,0},{2,3},{3,2},{4,5},{5,4},{6,7},{7,6},{8,9},{9,8},{10,11... | collective-permute-start | bytes 1179656 | tf_op jit(solution)/shard_map/ppermute | solution.py:417
  24.6 2.2 %collective-permute-start.12 = (bf16[256,768]{1,0:T(8,128)(2,1)S(1)}, bf16[256,768]{1,0:T(8,128)(2,1)S(1)}, u32[]{:S(2)}, u32[]{:S(2)}) collective-permute-start(bf16[256,768]{1,0:T(8,128)(2,1)S(1)} %collective-permute-done.9.refs_5_.refs_6_), channel_id=1, source_target_pairs={{0,1},{1,0},{2,3},{3,2},{4,5},{5,4},{6,7},{7,6},{8,9},{9,8},{10,11... | collective-permute-start | bytes 1179656 | tf_op jit(solution)/shard_map/ppermute | solution.py:417
  24.7 2.1 %collective-permute-start.11 = (bf16[128,768]{1,0:T(8,128)(2,1)S(1)}, bf16[128,768]{1,0:T(8,128)(2,1)S(1)}, u32[]{:S(2)}, u32[]{:S(2)}) collective-permute-start(bf16[128,768]{1,0:T(8,128)(2,1)S(1)} %get-tuple-element.59), channel_id=1, source_target_pairs={{0,1},{1,0},{2,3},{3,2},{4,5},{5,4},{6,7},{7,6},{8,9},{9,8},{10,11... | collective-permute-start | bytes 589832 | tf_op jit(solution)/shard_map/ppermute | solution.py:417
  28.9 3.9 %collective-permute-start.16 = (f32[256,768]{1,0:T(8,128)S(1)}, f32[256,768]{1,0:T(8,128)S(1)}, u32[]{:S(2)}, u32[]{:S(2)}) collective-permute-start(f32[256,768]{1,0:T(8,128)S(1)} %get-tuple-element.67), channel_id=1, source_target_pairs={{0,1},{1,0},{2,3},{3,2},{4,5},{5,4},{6,7},{7,6},{8,9},{9,8},{10,11... | collective-permute-start | bytes 2359304 | tf_op jit(solution)/shard_map/ppermute | solution.py:417
  29.4 9.5 %collective-permute-start.13 = (bf16[192,384]{1,0:T(8,128)(2,1)S(1)}, bf16[192,384]{1,0:T(8,128)(2,1)S(1)}, u32[]{:S(2)}, u32[]{:S(2)}) collective-permute-start(bf16[192,384]{1,0:T(8,128)(2,1)S(1)} %get-tuple-element.62), channel_id=1, source_target_pairs={{0,2},{2,0},{4,6},{6,4},{8,10},{10,8},{12,14},{14,12},{16,18},{18,... | collective-permute-start | bytes 442376 | tf_op jit(solution)/shard_map/ppermute | solution.py:408
  30.9 8.8 %collective-permute-start.14 = (bf16[192,384]{1,0:T(8,128)(2,1)S(1)}, bf16[192,384]{1,0:T(8,128)(2,1)S(1)}, u32[]{:S(2)}, u32[]{:S(2)}) collective-permute-start(bf16[192,384]{1,0:T(8,128)(2,1)S(1)} %get-tuple-element.63), channel_id=1, source_target_pairs={{0,4},{2,6},{4,0},{6,2},{8,12},{10,14},{12,8},{14,10},{16,20},{18,... | collective-permute-start | bytes 442376 | tf_op jit(solution)/shard_map/ppermute | solution.py:408
  32.4 7.2 %collective-permute-start.15 = (bf16[192,384]{1,0:T(8,128)(2,1)S(1)}, bf16[192,384]{1,0:T(8,128)(2,1)S(1)}, u32[]{:S(2)}, u32[]{:S(2)}) collective-permute-start(bf16[192,384]{1,0:T(8,128)(2,1)S(1)} %get-tuple-element.64), channel_id=1, source_target_pairs={{0,6},{2,4},{4,2},{6,0},{8,14},{10,12},{12,10},{14,8},{16,22},{18,... | collective-permute-start | bytes 442376 | tf_op jit(solution)/shard_map/ppermute | solution.py:408
  36.1 3.6 %collective-permute-start.17 = (bf16[96,128]{1,0:T(8,128)(2,1)S(1)}, bf16[96,128]{1,0:T(8,128)(2,1)S(1)}, u32[]{:S(2)}, u32[]{:S(2)}) collective-permute-start(bf16[96,128]{1,0:T(8,128)(2,1)S(1)} %get-tuple-element.72), channel_id=1, source_target_pairs={{0,3},{1,2},{2,1},{3,0},{4,7},{5,6},{6,5},{7,4},{8,11},{9,10},{10,... | collective-permute-start | bytes 73736 | tf_op jit(solution)/shard_map/ppermute | solution.py:414
  36.5 3.9 %collective-permute-start.18 = (bf16[96,128]{1,0:T(8,128)(2,1)S(1)}, bf16[96,128]{1,0:T(8,128)(2,1)S(1)}, u32[]{:S(2)}, u32[]{:S(2)}) collective-permute-start(bf16[96,128]{1,0:T(8,128)(2,1)S(1)} %get-tuple-element.73), channel_id=1, source_target_pairs={{0,5},{1,4},{2,7},{3,6},{4,1},{5,0},{6,3},{7,2},{8,13},{9,12},{10,... | collective-permute-start | bytes 73736 | tf_op jit(solution)/shard_map/ppermute | solution.py:414
  38.9 4.2 %collective-permute-start.19 = (bf16[96,128]{1,0:T(8,128)(2,1)S(1)}, bf16[96,128]{1,0:T(8,128)(2,1)S(1)}, u32[]{:S(2)}, u32[]{:S(2)}) collective-permute-start(bf16[96,128]{1,0:T(8,128)(2,1)S(1)} %get-tuple-element.74), channel_id=1, source_target_pairs={{0,7},{1,6},{2,5},{3,4},{4,3},{5,2},{6,1},{7,0},{8,15},{9,14},{10,... | collective-permute-start | bytes 73736 | tf_op jit(solution)/shard_map/ppermute | solution.py:414
  39.6 7.2 %collective-permute-start.20 = (bf16[6,8,16,128]{3,2,1,0:T(8,128)(2,1)S(1)}, bf16[6,8,16,128]{3,2,1,0:T(8,128)(2,1)S(1)}, u32[]{:S(2)}, u32[]{:S(2)}) collective-permute-start(bf16[6,8,16,128]{3,2,1,0:T(8,128)(2,1)S(1)} %get-tuple-element.77), channel_id=1, source_target_pairs={{0,9},{1,8},{2,11},{3,10},{4,13},{5,12},{6,15},{7,14},{8,1},{9,0},... | collective-permute-start | bytes 589832 | tf_op jit(solution)/shard_map/ppermute | solution.py:414
  43.1 5.8 %collective-permute-start.21 = (bf16[48,512]{1,0:T(8,128)(2,1)S(1)}, bf16[48,512]{1,0:T(8,128)(2,1)S(1)}, u32[]{:S(2)}, u32[]{:S(2)}) collective-permute-start(bf16[48,512]{1,0:T(8,128)(2,1)S(1)} %get-tuple-element.80), channel_id=1, source_target_pairs={{0,9},{1,8},{2,11},{3,10},{4,13},{5,12},{6,15},{7,14},{8,1},{9,0},... | collective-permute-start | bytes 147464 | tf_op jit(solution)/shard_map/ppermute | solution.py:414
  43.2 5.8 %collective-permute-start.22 = (bf16[48,512]{1,0:T(8,128)(2,1)S(1)}, bf16[48,512]{1,0:T(8,128)(2,1)S(1)}, u32[]{:S(2)}, u32[]{:S(2)}) collective-permute-start(bf16[48,512]{1,0:T(8,128)(2,1)S(1)} %get-tuple-element.81), channel_id=1, source_target_pairs={{0,17},{1,16},{2,19},{3,18},{4,21},{5,20},{6,23},{7,22},{8,25},{9,... | collective-permute-start | bytes 147464 | tf_op jit(solution)/shard_map/ppermute | solution.py:414
  46.3 5.5 %collective-permute-start.23 = (bf16[48,512]{1,0:T(8,128)(2,1)S(1)}, bf16[48,512]{1,0:T(8,128)(2,1)S(1)}, u32[]{:S(2)}, u32[]{:S(2)}) collective-permute-start(bf16[48,512]{1,0:T(8,128)(2,1)S(1)} %get-tuple-element.82), channel_id=1, source_target_pairs={{0,25},{1,24},{2,27},{3,26},{4,29},{5,28},{6,31},{7,30},{8,17},{9,... | collective-permute-start | bytes 147464 | tf_op jit(solution)/shard_map/ppermute | solution.py:414
  51.9 1.6 %collective-permute-start.24 = (f32[48,1280]{1,0:T(8,128)S(1)}, f32[48,1280]{1,0:T(8,128)S(1)}, u32[]{:S(2)}, u32[]{:S(2)}) collective-permute-start(f32[48,1280]{1,0:T(8,128)S(1)} %line_sum.1.mine_ref), channel_id=1, source_target_pairs={{0,1},{1,0},{2,3},{3,2},{4,5},{5,4},{6,7},{7,6},{8,9},{9,8},{10,11... | collective-permute-start | bytes 737288 | tf_op jit(solution)/shard_map/ppermute | solution.py:417

commit v12 on v11

--- a/solution.py
+++ b/solution.py
@@ -484,7 +484,7 @@
         "order",
         [shape((depth, quarter), BF16)],
         [],
-        2.6,
+        3.0,
         *weights,
     )
 

time: 54.4 us -> 61.2 us (1.12)
  waiting for transfers between devices: 15 us -> 21.5 us
    ppermute x14, waiting for transfers between devices: 11.1 us -> 17.4 us  [crossing(): return lax.ppermute(array, ('shard', 'rep'), pairs)]
    ppermute x5, waiting for transfers between devices: 2.02 us -> 3.05 us  [over_core(): return lax.ppermute(array, 'rep', [(i, i ^ 1) for i in range(reps)])]
    ppermute x6, waiting for transfers between devices: 1.83 us -> 1.04 us  [over_shard(): return lax.ppermute(array, 'shard', [(i, i ^ flip) for i in range(shards)])]
  transfers between devices with their start and end apart: 25 -> 25, of which waited for: 12 -> 12; matrix products, arithmetic and copies ran while one was open for 0% -> 0% of each run, Pallas kernels for 16% -> 14%
where the time goes in v12:
time: 61.2 us; the launch traced here: 61 us
  starting transfers between devices  25.5 us (42%)
  waiting for transfers between devices  21.5 us (35%)
  Pallas kernels  13.3 us (22%)
  between operations  0.74 us (1%)
    ppermute x14, waiting for transfers between devices, crossing(): return lax.ppermute(array, ('shard', 'rep'), pairs)  17.4 us
    ppermute x14, starting transfers between devices, crossing(): return lax.ppermute(array, ('shard', 'rep'), pairs)  17 us
    pallas_call x12, Pallas kernels, call(): pl.pallas_call(kernel, out_shape=outs, in_specs=[VMEM] * len(args), out_s...  13.3 us
    ppermute x6, starting transfers between devices, over_shard(): return lax.ppermute(array, 'shard', [(i, i ^ flip) for i in range(shards)])  6.98 us
    ppermute x5, waiting for transfers between devices, over_core(): return lax.ppermute(array, 'rep', [(i, i ^ 1) for i in range(reps)])  3.05 us
    ppermute x5, starting transfers between devices, over_core(): return lax.ppermute(array, 'rep', [(i, i ^ 1) for i in range(reps)])  1.57 us
  transfers between devices with their start and end apart: 25, of which 12 were waited for; matrix products, arithmetic and copies ran while one was open for 0% of the time, Pallas kernels for 14%

profile of v12, /device:TPU:0, one launch (start us, length us, event | category | flops | bytes accessed | tf_op | source)
XLA Modules:
  0.0 61.0 jit_solution(13383782144086420482)
XLA Ops:
  0.6 0.0 copy-start
  0.6 0.0 copy-start.1
  0.7 1.7 %pack.1 = (bf16[48,512]{1,0:T(8,128)(2,1)}, bf16[48,512]{1,0:T(8,128)(2,1)}, bf16[48,512]{1,0:T(8,128)(2,1)}) custom-call(bf16[48,1536]{1,0:T(8,128)(2,1)} %w_ref.1, bf16[48,49]{1,0:T(8,128)(2,1)} %dw_ref.1, bf16[1,48]{1,0:T(2,128)(2,1)} %bitcast.11, bf16[1,48]{1,0:T(2,128)(2,1)} %bitcast.12), custom_call_target="tpu_custom_call" | custom-call | flops 550000000 | bytes 299808 | tf_op jit(solution)/shard_map/pack/pallas_call | solution.py:381
  2.4 3.5 %collective-permute-start.1 = (bf16[48,512]{1,0:T(8,128)(2,1)}, bf16[48,512]{1,0:T(8,128)(2,1)S(1)}, u32[]{:S(2)}, u32[]{:S(2)}) collective-permute-start(bf16[48,512]{1,0:T(8,128)(2,1)} %get-tuple-element.51), channel_id=1, source_target_pairs={{0,17},{1,16},{2,19},{3,18},{4,21},{5,20},{6,23},{7,22},{8,25},{9,... | collective-permute-start | bytes 147464 | tf_op jit(solution)/shard_map/ppermute | solution.py:414
  5.9 1.6 %collective-permute-start.2 = (bf16[48,512]{1,0:T(8,128)(2,1)}, bf16[48,512]{1,0:T(8,128)(2,1)S(1)}, u32[]{:S(2)}, u32[]{:S(2)}) collective-permute-start(bf16[48,512]{1,0:T(8,128)(2,1)} %get-tuple-element.50), channel_id=1, source_target_pairs={{0,25},{1,24},{2,27},{3,26},{4,29},{5,28},{6,31},{7,30},{8,17},{9,... | collective-permute-start | bytes 147464 | tf_op jit(solution)/shard_map/ppermute | solution.py:414
  7.5 0.2 collective-permute-start
  7.7 0.0 copy-done
  7.7 0.0 copy-done.1
  7.8 1.6 %collective-permute-start.9 = (bf16[256,768]{1,0:T(8,128)(2,1)S(1)}, bf16[256,768]{1,0:T(8,128)(2,1)S(1)}, u32[]{:S(2)}, u32[]{:S(2)}) collective-permute-start(bf16[256,768]{1,0:T(8,128)(2,1)S(1)} %get-tuple-element.56), channel_id=1, source_target_pairs={{0,9},{1,8},{2,11},{3,10},{4,13},{5,12},{6,15},{7,14},{8,1},{9,0},... | collective-permute-start | bytes 1179656 | tf_op jit(solution)/shard_map/ppermute | solution.py:414
  9.4 0.0 collective-permute-done.1.refs_2_
  9.4 2.1 %collective-permute-done.2.refs_3_ = bf16[48,512]{1,0:T(8,128)(2,1)S(1)} collective-permute-done((bf16[48,512]{1,0:T(8,128)(2,1)}, bf16[48,512]{1,0:T(8,128)(2,1)S(1)}, u32[]{:S(2)}, u32[]{:S(2)}) %collective-permute-start.2) | collective-permute-done | bytes 49184 | tf_op jit(solution)/shard_map/ppermute | solution.py:414
  11.5 0.9 %collective-permute-done.refs_1_ = bf16[48,512]{1,0:T(8,128)(2,1)S(1)} collective-permute-done((bf16[48,512]{1,0:T(8,128)(2,1)}, bf16[48,512]{1,0:T(8,128)(2,1)S(1)}, u32[]{:S(2)}, u32[]{:S(2)}) %collective-permute-start) | collective-permute-done | bytes 49184 | tf_op jit(solution)/shard_map/ppermute | solution.py:414
  12.4 0.1 assemble.1
  12.5 2.9 %collective-permute-start.8 = (bf16[96,128]{1,0:T(8,128)(2,1)S(1)}, bf16[96,128]{1,0:T(8,128)(2,1)S(1)}, u32[]{:S(2)}, u32[]{:S(2)}) collective-permute-start(bf16[96,128]{1,0:T(8,128)(2,1)S(1)} %get-tuple-element.53.refs_0_), channel_id=1, source_target_pairs={{0,7},{1,6},{2,5},{3,4},{4,3},{5,2},{6,1},{7,0},{8,15},{9,14},{10,... | collective-permute-start | bytes 73736 | tf_op jit(solution)/shard_map/ppermute | solution.py:414
  15.4 0.5 collective-permute-start.5
  15.9 1.5 %collective-permute-start.4 = (bf16[192,384]{1,0:T(8,128)(2,1)S(1)}, bf16[192,384]{1,0:T(8,128)(2,1)S(1)}, u32[]{:S(2)}, u32[]{:S(2)}) collective-permute-start(bf16[192,384]{1,0:T(8,128)(2,1)S(1)} %get-tuple-element.52.refs_0_), channel_id=1, source_target_pairs={{0,4},{2,6},{4,0},{6,2},{8,12},{10,14},{12,8},{14,10},{16,20},{18,... | collective-permute-start | bytes 442376 | tf_op jit(solution)/shard_map/ppermute | solution.py:408
  17.4 1.5 %collective-permute-start.3 = (bf16[192,384]{1,0:T(8,128)(2,1)S(1)}, bf16[192,384]{1,0:T(8,128)(2,1)S(1)}, u32[]{:S(2)}, u32[]{:S(2)}) collective-permute-start(bf16[192,384]{1,0:T(8,128)(2,1)S(1)} %get-tuple-element.52.refs_0_), channel_id=1, source_target_pairs={{0,2},{2,0},{4,6},{6,4},{8,10},{10,8},{12,14},{14,12},{16,18},{18,... | collective-permute-start | bytes 442376 | tf_op jit(solution)/shard_map/ppermute | solution.py:408
  18.9 0.0 collective-permute-done.8.refs_3_
  18.9 0.0 collective-permute-start.7
  18.9 5.6 %collective-permute-done.7.refs_2_ = bf16[96,128]{1,0:T(8,128)(2,1)S(1)} collective-permute-done((bf16[96,128]{1,0:T(8,128)(2,1)S(1)}, bf16[96,128]{1,0:T(8,128)(2,1)S(1)}, u32[]{:S(2)}, u32[]{:S(2)}) %collective-permute-start.7) | collective-permute-done | bytes 24608 | tf_op jit(solution)/shard_map/ppermute | solution.py:414
  24.5 1.2 %collective-permute-start.6 = (bf16[96,128]{1,0:T(8,128)(2,1)S(1)}, bf16[96,128]{1,0:T(8,128)(2,1)S(1)}, u32[]{:S(2)}, u32[]{:S(2)}) collective-permute-start(bf16[96,128]{1,0:T(8,128)(2,1)S(1)} %get-tuple-element.53.refs_0_), channel_id=1, source_target_pairs={{0,3},{1,2},{2,1},{3,0},{4,7},{5,6},{6,5},{7,4},{8,11},{9,10},{10,... | collective-permute-start | bytes 73736 | tf_op jit(solution)/shard_map/ppermute | solution.py:414
  25.6 2.1 %collective-permute-done.6.refs_1_ = bf16[96,128]{1,0:T(8,128)(2,1)S(1)} collective-permute-done((bf16[96,128]{1,0:T(8,128)(2,1)S(1)}, bf16[96,128]{1,0:T(8,128)(2,1)S(1)}, u32[]{:S(2)}, u32[]{:S(2)}) %collective-permute-start.6) | collective-permute-done | bytes 24608 | tf_op jit(solution)/shard_map/ppermute | solution.py:414
  27.7 0.0 collective-permute-done.9.refs_5_.refs_6_
  27.7 3.2 %conv_norm.1 = (bf16[256,768]{1,0:T(8,128)(2,1)S(1)}, f32[256,768]{1,0:T(8,128)S(1)}, f32[256,128]{1,0:T(8,128)S(1)}, f32[6,128,128]{2,1,0:T(8,128)S(1)}) custom-call(bf16[96,128]{1,0:T(8,128)(2,1)S(1)} %get-tuple-element.53.refs_0_, bf16[96,128]{1,0:T(8,128)(2,1)S(1)} %collective-permute-done.6.refs_1_, bf16[96,128]{1,0:T(8,128)(2,1)S(1)} %collective-permute-done.7.refs_2_, ...), custom_call_target="tpu_custom_call" | custom-call | flops 110000000 | bytes 2392064 | tf_op jit(solution)/shard_map/conv_norm/pallas_call | solution.py:381
  30.9 0.5 collective-permute-start.10
  31.4 0.1 collective-permute-start.12
  31.5 0.0 collective-permute-done.5.refs_3_
  31.5 0.4 collective-permute-start.11
  31.9 0.0 collective-permute-done.4.refs_2_
  31.9 0.0 collective-permute-done.3.refs_1_
  31.9 0.1 order.1.refs_0_.weight
  32.0 1.6 %collective-permute-done.11.refs_4_ = bf16[128,768]{1,0:T(8,128)(2,1)S(1)} collective-permute-done((bf16[128,768]{1,0:T(8,128)(2,1)S(1)}, bf16[128,768]{1,0:T(8,128)(2,1)S(1)}, u32[]{:S(2)}, u32[]{:S(2)}) %collective-permute-start.11) | collective-permute-done | bytes 196640 | tf_op jit(solution)/shard_map/ppermute | solution.py:417
  33.6 0.0 collective-permute-done.10.refs_2_
  33.6 0.0 collective-permute-done.12.refs_6_
  33.6 1.5 %project.1 = (f32[192,384]{1,0:T(8,128)S(1)}, bf16[192,384]{1,0:T(8,128)(2,1)S(1)}, bf16[192,384]{1,0:T(8,128)(2,1)S(1)}, bf16[192,384]{1,0:T(8,128)(2,1)S(1)}, bf16[512,384]{1,0:T(8,128)(2,1)S(1)}) custom-call(bf16[768,384]{1,0:T(8,128)(2,1)S(1)} %order.1.refs_0_.weight, bf16[256,768]{1,0:T(8,128)(2,1)S(1)} %get-tuple-element.58.refs_1_, ...), custom_call_target="tpu_custom_call" | custom-call | flops 1760000000 | bytes 3883008 | tf_op jit(solution)/shard_map/project/pallas_call | solution.py:381
  35.1 0.6 back_project.1
  35.7 0.4 collective-permute-start.16
  36.2 1.2 %collective-permute-start.13 = (bf16[192,384]{1,0:T(8,128)(2,1)S(1)}, bf16[192,384]{1,0:T(8,128)(2,1)S(1)}, u32[]{:S(2)}, u32[]{:S(2)}) collective-permute-start(bf16[192,384]{1,0:T(8,128)(2,1)S(1)} %get-tuple-element.62), channel_id=1, source_target_pairs={{0,2},{2,0},{4,6},{6,4},{8,10},{10,8},{12,14},{14,12},{16,18},{18,... | collective-permute-start | bytes 442376 | tf_op jit(solution)/shard_map/ppermute | solution.py:408
  37.4 1.0 %collective-permute-start.14 = (bf16[192,384]{1,0:T(8,128)(2,1)S(1)}, bf16[192,384]{1,0:T(8,128)(2,1)S(1)}, u32[]{:S(2)}, u32[]{:S(2)}) collective-permute-start(bf16[192,384]{1,0:T(8,128)(2,1)S(1)} %get-tuple-element.63), channel_id=1, source_target_pairs={{0,4},{2,6},{4,0},{6,2},{8,12},{10,14},{12,8},{14,10},{16,20},{18,... | collective-permute-start | bytes 442376 | tf_op jit(solution)/shard_map/ppermute | solution.py:408
  38.4 1.3 %collective-permute-start.15 = (bf16[192,384]{1,0:T(8,128)(2,1)S(1)}, bf16[192,384]{1,0:T(8,128)(2,1)S(1)}, u32[]{:S(2)}, u32[]{:S(2)}) collective-permute-start(bf16[192,384]{1,0:T(8,128)(2,1)S(1)} %get-tuple-element.64), channel_id=1, source_target_pairs={{0,6},{2,4},{4,2},{6,0},{8,14},{10,12},{12,10},{14,8},{16,22},{18,... | collective-permute-start | bytes 442376 | tf_op jit(solution)/shard_map/ppermute | solution.py:408
  39.7 0.0 collective-permute-done.16.refs_1_
  39.7 3.2 %norm_back.1 = (f32[96,128]{1,0:T(8,128)S(1)}, bf16[96,128]{1,0:T(8,128)(2,1)S(1)}, bf16[96,128]{1,0:T(8,128)(2,1)S(1)}, bf16[96,128]{1,0:T(8,128)(2,1)S(1)}, f3...) custom-call(f32[256,768]{1,0:T(8,128)S(1)} %get-tuple-element.66.refs_0_, ...), custom_call_target="tpu_custom_call" | custom-call | flops 110000000 | bytes 4186112 | tf_op jit(solution)/shard_map/norm_back/pallas_call | solution.py:381
  42.9 0.4 collective-permute-start.17
  43.2 1.6 %collective-permute-start.18 = (bf16[96,128]{1,0:T(8,128)(2,1)S(1)}, bf16[96,128]{1,0:T(8,128)(2,1)S(1)}, u32[]{:S(2)}, u32[]{:S(2)}) collective-permute-start(bf16[96,128]{1,0:T(8,128)(2,1)S(1)} %get-tuple-element.73), channel_id=1, source_target_pairs={{0,5},{1,4},{2,7},{3,6},{4,1},{5,0},{6,3},{7,2},{8,13},{9,12},{10,... | collective-permute-start | bytes 73736 | tf_op jit(solution)/shard_map/ppermute | solution.py:414
  44.9 0.0 collective-permute-done.13.refs_1_
  44.9 0.5 collective-permute-start.19
  45.4 1.0 %collective-permute-done.14.refs_2_ = bf16[192,384]{1,0:T(8,128)(2,1)S(1)} collective-permute-done((bf16[192,384]{1,0:T(8,128)(2,1)S(1)}, bf16[192,384]{1,0:T(8,128)(2,1)S(1)}, u32[]{:S(2)}, u32[]{:S(2)}) %collective-permute-start.14) | collective-permute-done | bytes 147488 | tf_op jit(solution)/shard_map/ppermute | solution.py:408
  46.4 0.0 collective-permute-start.20
  46.4 0.0 collective-permute-done.15.refs_3_
  46.4 0.0 collective-permute-done.17.refs_5_
  46.4 0.2 collective-permute-done.18.refs_6_
  46.6 2.4 %collective-permute-done.19.refs_7_ = bf16[96,128]{1,0:T(8,128)(2,1)S(1)} collective-permute-done((bf16[96,128]{1,0:T(8,128)(2,1)S(1)}, bf16[96,128]{1,0:T(8,128)(2,1)S(1)}, u32[]{:S(2)}, u32[]{:S(2)}) %collective-permute-start.19) | collective-permute-done | bytes 24608 | tf_op jit(solution)/shard_map/ppermute | solution.py:414
  49.0 0.1 plane_sum.1
  49.1 0.1 collective-permute-start.21
  49.2 3.4 %collective-permute-start.22 = (bf16[48,512]{1,0:T(8,128)(2,1)S(1)}, bf16[48,512]{1,0:T(8,128)(2,1)S(1)}, u32[]{:S(2)}, u32[]{:S(2)}) collective-permute-start(bf16[48,512]{1,0:T(8,128)(2,1)S(1)} %get-tuple-element.81), channel_id=1, source_target_pairs={{0,17},{1,16},{2,19},{3,18},{4,21},{5,20},{6,23},{7,22},{8,25},{9,... | collective-permute-start | bytes 147464 | tf_op jit(solution)/shard_map/ppermute | solution.py:414
  52.6 0.0 collective-permute-start.23
  52.6 1.0 %collective-permute-done.20.other_ref = bf16[6,8,16,128]{3,2,1,0:T(8,128)(2,1)S(1)} collective-permute-done((bf16[6,8,16,128]{3,2,1,0:T(8,128)(2,1)S(1)}, bf16[6,8,16,128]{3,2,1,0:T(8,128)(2,1)S(1)}, u32[]{:S(2)}, u32[]{:S(2)}) %collective-permute-start.20) | collective-permute-done | bytes 196640 | tf_op jit(solution)/shard_map/ppermute | solution.py:414
  53.5 1.9 %conv_back.1 = bf16[1,8,16,768]{3,2,1,0:T(8,128)(2,1)} custom-call(f32[6,8,16,128]{3,2,1,0:T(8,128)S(1)} %get-tuple-element.76.grad_ref, bf16[6,8,16,128]{3,2,1,0:T(8,128)(2,1)S(1)} %collective-permute-done.20.other_ref, f32[6,128,128]{2,1,0:T(8,128)S(1)} %get-tuple-element.70.refs_4_.taps_ref), custom_call_target="tpu_custom_call" | custom-call | flops 110000000 | bytes 1179648 | tf_op jit(solution)/shard_map/conv_back/pallas_call | solution.py:381
  55.5 0.2 collective-permute-done.21.refs_1_
  55.7 0.0 collective-permute-done.22.refs_2_
  55.7 3.0 %collective-permute-done.23.refs_3_ = bf16[48,512]{1,0:T(8,128)(2,1)S(1)} collective-permute-done((bf16[48,512]{1,0:T(8,128)(2,1)S(1)}, bf16[48,512]{1,0:T(8,128)(2,1)S(1)}, u32[]{:S(2)}, u32[]{:S(2)}) %collective-permute-start.23) | collective-permute-done | bytes 49184 | tf_op jit(solution)/shard_map/ppermute | solution.py:414
  58.7 0.1 collective-permute-start.24
  58.8 1.5 %collective-permute-done.24.other_ref = f32[48,1280]{1,0:T(8,128)S(1)} collective-permute-done((f32[48,1280]{1,0:T(8,128)S(1)}, f32[48,1280]{1,0:T(8,128)S(1)}, u32[]{:S(2)}, u32[]{:S(2)}) %collective-permute-start.24) | collective-permute-done | bytes 245792 | tf_op jit(solution)/shard_map/ppermute | solution.py:417
  60.3 0.8 %finish.1 = (f32[48,1536]{1,0:T(8,128)}, f32[48,49]{1,0:T(8,128)}, f32[1,48]{1,0:T(1,128)}, f32[1,48]{1,0:T(1,128)}) custom-call(f32[48,1280]{1,0:T(8,128)S(1)} %line_sum.1.mine_ref, f32[48,1280]{1,0:T(8,128)S(1)} %collective-permute-done.24.other_ref), custom_call_target="tpu_custom_call" | custom-call | flops 550000000 | bytes 796224 | tf_op jit(solution)/shard_map/finish/pallas_call | solution.py:381
  (4 shorter events, 0.1 us)
Async XLA Ops:
  0.6 7.1 %copy-start = (bf16[1,8,16,768]{3,2,1,0:T(8,128)(2,1)S(1)}, bf16[1,8,16,768]{3,2,1,0:T(8,128)(2,1)}, u32[]{:S(2)}) copy-start(bf16[1,8,16,768]{3,2,1,0:T(8,128)(2,1)} %param.6) | copy-start | bytes 589828
  0.6 7.1 %copy-start.1 = (bf16[1,8,16,1536]{3,2,1,0:T(8,128)(2,1)S(1)}, bf16[1,8,16,1536]{3,2,1,0:T(8,128)(2,1)}, u32[]{:S(2)}) copy-start(bf16[1,8,16,1536]{3,2,1,0:T(8,128)(2,1)} %param.7) | copy-start | bytes 1179652
  2.4 10.0 %copy-start.2 = (bf16[48,512]{1,0:T(8,128)(2,1)S(1)}, bf16[48,512]{1,0:T(8,128)(2,1)}, u32[]{:S(2)}) copy-start(bf16[48,512]{1,0:T(8,128)(2,1)} %get-tuple-element.49.refs_0_) | copy-start | bytes 147460
  2.4 7.0 %collective-permute-start.1 = (bf16[48,512]{1,0:T(8,128)(2,1)}, bf16[48,512]{1,0:T(8,128)(2,1)S(1)}, u32[]{:S(2)}, u32[]{:S(2)}) collective-permute-start(bf16[48,512]{1,0:T(8,128)(2,1)} %get-tuple-element.51), channel_id=1, source_target_pairs={{0,17},{1,16},{2,19},{3,18},{4,21},{5,20},{6,23},{7,22},{8,25},{9,... | collective-permute-start | bytes 147464 | tf_op jit(solution)/shard_map/ppermute | solution.py:414
  5.9 5.6 %collective-permute-start.2 = (bf16[48,512]{1,0:T(8,128)(2,1)}, bf16[48,512]{1,0:T(8,128)(2,1)S(1)}, u32[]{:S(2)}, u32[]{:S(2)}) collective-permute-start(bf16[48,512]{1,0:T(8,128)(2,1)} %get-tuple-element.50), channel_id=1, source_target_pairs={{0,25},{1,24},{2,27},{3,26},{4,29},{5,28},{6,31},{7,30},{8,17},{9,... | collective-permute-start | bytes 147464 | tf_op jit(solution)/shard_map/ppermute | solution.py:414
  7.5 4.9 %collective-permute-start = (bf16[48,512]{1,0:T(8,128)(2,1)}, bf16[48,512]{1,0:T(8,128)(2,1)S(1)}, u32[]{:S(2)}, u32[]{:S(2)}) collective-permute-start(bf16[48,512]{1,0:T(8,128)(2,1)} %get-tuple-element.50), channel_id=1, source_target_pairs={{0,9},{1,8},{2,11},{3,10},{4,13},{5,12},{6,15},{7,14},{8,1},{9,0},... | collective-permute-start | bytes 147464 | tf_op jit(solution)/shard_map/ppermute | solution.py:414
  7.8 19.9 %collective-permute-start.9 = (bf16[256,768]{1,0:T(8,128)(2,1)S(1)}, bf16[256,768]{1,0:T(8,128)(2,1)S(1)}, u32[]{:S(2)}, u32[]{:S(2)}) collective-permute-start(bf16[256,768]{1,0:T(8,128)(2,1)S(1)} %get-tuple-element.56), channel_id=1, source_target_pairs={{0,9},{1,8},{2,11},{3,10},{4,13},{5,12},{6,15},{7,14},{8,1},{9,0},... | collective-permute-start | bytes 1179656 | tf_op jit(solution)/shard_map/ppermute | solution.py:414
  12.5 6.4 %collective-permute-start.8 = (bf16[96,128]{1,0:T(8,128)(2,1)S(1)}, bf16[96,128]{1,0:T(8,128)(2,1)S(1)}, u32[]{:S(2)}, u32[]{:S(2)}) collective-permute-start(bf16[96,128]{1,0:T(8,128)(2,1)S(1)} %get-tuple-element.53.refs_0_), channel_id=1, source_target_pairs={{0,7},{1,6},{2,5},{3,4},{4,3},{5,2},{6,1},{7,0},{8,15},{9,14},{10,... | collective-permute-start | bytes 73736 | tf_op jit(solution)/shard_map/ppermute | solution.py:414
  15.4 16.1 %collective-permute-start.5 = (bf16[192,384]{1,0:T(8,128)(2,1)S(1)}, bf16[192,384]{1,0:T(8,128)(2,1)S(1)}, u32[]{:S(2)}, u32[]{:S(2)}) collective-permute-start(bf16[192,384]{1,0:T(8,128)(2,1)S(1)} %get-tuple-element.52.refs_0_), channel_id=1, source_target_pairs={{0,6},{2,4},{4,2},{6,0},{8,14},{10,12},{12,10},{14,8},{16,22},{18,... | collective-permute-start | bytes 442376 | tf_op jit(solution)/shard_map/ppermute | solution.py:408
  15.9 16.1 %collective-permute-start.4 = (bf16[192,384]{1,0:T(8,128)(2,1)S(1)}, bf16[192,384]{1,0:T(8,128)(2,1)S(1)}, u32[]{:S(2)}, u32[]{:S(2)}) collective-permute-start(bf16[192,384]{1,0:T(8,128)(2,1)S(1)} %get-tuple-element.52.refs_0_), channel_id=1, source_target_pairs={{0,4},{2,6},{4,0},{6,2},{8,12},{10,14},{12,8},{14,10},{16,20},{18,... | collective-permute-start | bytes 442376 | tf_op jit(solution)/shard_map/ppermute | solution.py:408
  17.4 14.6 %collective-permute-start.3 = (bf16[192,384]{1,0:T(8,128)(2,1)S(1)}, bf16[192,384]{1,0:T(8,128)(2,1)S(1)}, u32[]{:S(2)}, u32[]{:S(2)}) collective-permute-start(bf16[192,384]{1,0:T(8,128)(2,1)S(1)} %get-tuple-element.52.refs_0_), channel_id=1, source_target_pairs={{0,2},{2,0},{4,6},{6,4},{8,10},{10,8},{12,14},{14,12},{16,18},{18,... | collective-permute-start | bytes 442376 | tf_op jit(solution)/shard_map/ppermute | solution.py:408
  18.9 5.6 %collective-permute-start.7 = (bf16[96,128]{1,0:T(8,128)(2,1)S(1)}, bf16[96,128]{1,0:T(8,128)(2,1)S(1)}, u32[]{:S(2)}, u32[]{:S(2)}) collective-permute-start(bf16[96,128]{1,0:T(8,128)(2,1)S(1)} %get-tuple-element.53.refs_0_), channel_id=1, source_target_pairs={{0,5},{1,4},{2,7},{3,6},{4,1},{5,0},{6,3},{7,2},{8,13},{9,12},{10,... | collective-permute-start | bytes 73736 | tf_op jit(solution)/shard_map/ppermute | solution.py:414
  24.5 3.3 %collective-permute-start.6 = (bf16[96,128]{1,0:T(8,128)(2,1)S(1)}, bf16[96,128]{1,0:T(8,128)(2,1)S(1)}, u32[]{:S(2)}, u32[]{:S(2)}) collective-permute-start(bf16[96,128]{1,0:T(8,128)(2,1)S(1)} %get-tuple-element.53.refs_0_), channel_id=1, source_target_pairs={{0,3},{1,2},{2,1},{3,0},{4,7},{5,6},{6,5},{7,4},{8,11},{9,10},{10,... | collective-permute-start | bytes 73736 | tf_op jit(solution)/shard_map/ppermute | solution.py:414
  30.9 2.7 %collective-permute-start.10 = (bf16[256,768]{1,0:T(8,128)(2,1)S(1)}, bf16[256,768]{1,0:T(8,128)(2,1)S(1)}, u32[]{:S(2)}, u32[]{:S(2)}) collective-permute-start(bf16[256,768]{1,0:T(8,128)(2,1)S(1)} %get-tuple-element.58.refs_1_), channel_id=1, source_target_pairs={{0,1},{1,0},{2,3},{3,2},{4,5},{5,4},{6,7},{7,6},{8,9},{9,8},{10,11... | collective-permute-start | bytes 1179656 | tf_op jit(solution)/shard_map/ppermute | solution.py:417
  31.4 2.2 %collective-permute-start.12 = (bf16[256,768]{1,0:T(8,128)(2,1)S(1)}, bf16[256,768]{1,0:T(8,128)(2,1)S(1)}, u32[]{:S(2)}, u32[]{:S(2)}) collective-permute-start(bf16[256,768]{1,0:T(8,128)(2,1)S(1)} %collective-permute-done.9.refs_5_.refs_6_), channel_id=1, source_target_pairs={{0,1},{1,0},{2,3},{3,2},{4,5},{5,4},{6,7},{7,6},{8,9},{9,8},{10,11... | collective-permute-start | bytes 1179656 | tf_op jit(solution)/shard_map/ppermute | solution.py:417
  31.5 2.1 %collective-permute-start.11 = (bf16[128,768]{1,0:T(8,128)(2,1)S(1)}, bf16[128,768]{1,0:T(8,128)(2,1)S(1)}, u32[]{:S(2)}, u32[]{:S(2)}) collective-permute-start(bf16[128,768]{1,0:T(8,128)(2,1)S(1)} %get-tuple-element.59), channel_id=1, source_target_pairs={{0,1},{1,0},{2,3},{3,2},{4,5},{5,4},{6,7},{7,6},{8,9},{9,8},{10,11... | collective-permute-start | bytes 589832 | tf_op jit(solution)/shard_map/ppermute | solution.py:417
  35.7 3.9 %collective-permute-start.16 = (f32[256,768]{1,0:T(8,128)S(1)}, f32[256,768]{1,0:T(8,128)S(1)}, u32[]{:S(2)}, u32[]{:S(2)}) collective-permute-start(f32[256,768]{1,0:T(8,128)S(1)} %get-tuple-element.67), channel_id=1, source_target_pairs={{0,1},{1,0},{2,3},{3,2},{4,5},{5,4},{6,7},{7,6},{8,9},{9,8},{10,11... | collective-permute-start | bytes 2359304 | tf_op jit(solution)/shard_map/ppermute | solution.py:417
  36.2 8.7 %collective-permute-start.13 = (bf16[192,384]{1,0:T(8,128)(2,1)S(1)}, bf16[192,384]{1,0:T(8,128)(2,1)S(1)}, u32[]{:S(2)}, u32[]{:S(2)}) collective-permute-start(bf16[192,384]{1,0:T(8,128)(2,1)S(1)} %get-tuple-element.62), channel_id=1, source_target_pairs={{0,2},{2,0},{4,6},{6,4},{8,10},{10,8},{12,14},{14,12},{16,18},{18,... | collective-permute-start | bytes 442376 | tf_op jit(solution)/shard_map/ppermute | solution.py:408
  37.4 9.0 %collective-permute-start.14 = (bf16[192,384]{1,0:T(8,128)(2,1)S(1)}, bf16[192,384]{1,0:T(8,128)(2,1)S(1)}, u32[]{:S(2)}, u32[]{:S(2)}) collective-permute-start(bf16[192,384]{1,0:T(8,128)(2,1)S(1)} %get-tuple-element.63), channel_id=1, source_target_pairs={{0,4},{2,6},{4,0},{6,2},{8,12},{10,14},{12,8},{14,10},{16,20},{18,... | collective-permute-start | bytes 442376 | tf_op jit(solution)/shard_map/ppermute | solution.py:408
  38.4 8.0 %collective-permute-start.15 = (bf16[192,384]{1,0:T(8,128)(2,1)S(1)}, bf16[192,384]{1,0:T(8,128)(2,1)S(1)}, u32[]{:S(2)}, u32[]{:S(2)}) collective-permute-start(bf16[192,384]{1,0:T(8,128)(2,1)S(1)} %get-tuple-element.64), channel_id=1, source_target_pairs={{0,6},{2,4},{4,2},{6,0},{8,14},{10,12},{12,10},{14,8},{16,22},{18,... | collective-permute-start | bytes 442376 | tf_op jit(solution)/shard_map/ppermute | solution.py:408
  42.9 3.5 %collective-permute-start.17 = (bf16[96,128]{1,0:T(8,128)(2,1)S(1)}, bf16[96,128]{1,0:T(8,128)(2,1)S(1)}, u32[]{:S(2)}, u32[]{:S(2)}) collective-permute-start(bf16[96,128]{1,0:T(8,128)(2,1)S(1)} %get-tuple-element.72), channel_id=1, source_target_pairs={{0,3},{1,2},{2,1},{3,0},{4,7},{5,6},{6,5},{7,4},{8,11},{9,10},{10,... | collective-permute-start | bytes 73736 | tf_op jit(solution)/shard_map/ppermute | solution.py:414
  43.2 3.4 %collective-permute-start.18 = (bf16[96,128]{1,0:T(8,128)(2,1)S(1)}, bf16[96,128]{1,0:T(8,128)(2,1)S(1)}, u32[]{:S(2)}, u32[]{:S(2)}) collective-permute-start(bf16[96,128]{1,0:T(8,128)(2,1)S(1)} %get-tuple-element.73), channel_id=1, source_target_pairs={{0,5},{1,4},{2,7},{3,6},{4,1},{5,0},{6,3},{7,2},{8,13},{9,12},{10,... | collective-permute-start | bytes 73736 | tf_op jit(solution)/shard_map/ppermute | solution.py:414
  44.9 4.2 %collective-permute-start.19 = (bf16[96,128]{1,0:T(8,128)(2,1)S(1)}, bf16[96,128]{1,0:T(8,128)(2,1)S(1)}, u32[]{:S(2)}, u32[]{:S(2)}) collective-permute-start(bf16[96,128]{1,0:T(8,128)(2,1)S(1)} %get-tuple-element.74), channel_id=1, source_target_pairs={{0,7},{1,6},{2,5},{3,4},{4,3},{5,2},{6,1},{7,0},{8,15},{9,14},{10,... | collective-permute-start | bytes 73736 | tf_op jit(solution)/shard_map/ppermute | solution.py:414
  46.4 7.1 %collective-permute-start.20 = (bf16[6,8,16,128]{3,2,1,0:T(8,128)(2,1)S(1)}, bf16[6,8,16,128]{3,2,1,0:T(8,128)(2,1)S(1)}, u32[]{:S(2)}, u32[]{:S(2)}) collective-permute-start(bf16[6,8,16,128]{3,2,1,0:T(8,128)(2,1)S(1)} %get-tuple-element.77), channel_id=1, source_target_pairs={{0,9},{1,8},{2,11},{3,10},{4,13},{5,12},{6,15},{7,14},{8,1},{9,0},... | collective-permute-start | bytes 589832 | tf_op jit(solution)/shard_map/ppermute | solution.py:414
  49.1 6.6 %collective-permute-start.21 = (bf16[48,512]{1,0:T(8,128)(2,1)S(1)}, bf16[48,512]{1,0:T(8,128)(2,1)S(1)}, u32[]{:S(2)}, u32[]{:S(2)}) collective-permute-start(bf16[48,512]{1,0:T(8,128)(2,1)S(1)} %get-tuple-element.80), channel_id=1, source_target_pairs={{0,9},{1,8},{2,11},{3,10},{4,13},{5,12},{6,15},{7,14},{8,1},{9,0},... | collective-permute-start | bytes 147464 | tf_op jit(solution)/shard_map/ppermute | solution.py:414
  49.2 6.5 %collective-permute-start.22 = (bf16[48,512]{1,0:T(8,128)(2,1)S(1)}, bf16[48,512]{1,0:T(8,128)(2,1)S(1)}, u32[]{:S(2)}, u32[]{:S(2)}) collective-permute-start(bf16[48,512]{1,0:T(8,128)(2,1)S(1)} %get-tuple-element.81), channel_id=1, source_target_pairs={{0,17},{1,16},{2,19},{3,18},{4,21},{5,20},{6,23},{7,22},{8,25},{9,... | collective-permute-start | bytes 147464 | tf_op jit(solution)/shard_map/ppermute | solution.py:414
  52.6 6.1 %collective-permute-start.23 = (bf16[48,512]{1,0:T(8,128)(2,1)S(1)}, bf16[48,512]{1,0:T(8,128)(2,1)S(1)}, u32[]{:S(2)}, u32[]{:S(2)}) collective-permute-start(bf16[48,512]{1,0:T(8,128)(2,1)S(1)} %get-tuple-element.82), channel_id=1, source_target_pairs={{0,25},{1,24},{2,27},{3,26},{4,29},{5,28},{6,31},{7,30},{8,17},{9,... | collective-permute-start | bytes 147464 | tf_op jit(solution)/shard_map/ppermute | solution.py:414
  58.7 1.6 %collective-permute-start.24 = (f32[48,1280]{1,0:T(8,128)S(1)}, f32[48,1280]{1,0:T(8,128)S(1)}, u32[]{:S(2)}, u32[]{:S(2)}) collective-permute-start(f32[48,1280]{1,0:T(8,128)S(1)} %line_sum.1.mine_ref), channel_id=1, source_target_pairs={{0,1},{1,0},{2,3},{3,2},{4,5},{5,4},{6,7},{7,6},{8,9},{9,8},{10,11... | collective-permute-start | bytes 737288 | tf_op jit(solution)/shard_map/ppermute | solution.py:417

commit v13 on v11

--- a/solution.py
+++ b/solution.py
@@ -109,19 +109,18 @@
 
 
 def plane_sum_kernel(lines, *refs):
-    pieces, small, outs = refs[:INNER], refs[INNER : 2 * INNER], refs[2 * INNER :]
-    own = pieces[0].shape[0] // lines
-    quarter = pieces[0].shape[1]
+    home, first, second = refs[:3]
+    small, outs = refs[3 : 3 + INNER], refs[3 + INNER :]
+    own = home.shape[0] // lines
+    quarter = home.shape[1]
     extras = small[0][...]
     for part in small[1:]:
         extras = extras + part[...].astype(F32)
-    if extras.shape[0] < pieces[0].shape[0]:
+    if extras.shape[0] < home.shape[0]:
         extras = unfold(extras)
     for line, out in enumerate(outs):
         rows = slice(line * own, (line + 1) * own)
-        total = pieces[0][rows, :]
-        for part in pieces[1:]:
-            total = total + part[rows, :].astype(F32)
+        total = home[rows, :] + first[rows, :].astype(F32) + second[rows, :].astype(F32)
         out[:, :quarter] = total.astype(out.dtype)
         out[:, quarter:] = extras[rows, :].astype(out.dtype)
 
@@ -249,8 +248,7 @@
 
 def project_kernel(relative, own, *refs):
     weight, n_own, n_sibling, cot_ref, sibling_ref, across_ref, corner_ref = refs[:7]
-    pieces = refs[7 : 7 + INNER]
-    gp_ref, normed, cot, grad = refs[7 + INNER :]
+    *pieces, gp_ref, normed, cot, grad = refs[7:]
     pixels, half = sibling_ref.shape
     quarter = half // 2
     side = lax.axis_index("rep") % 2
@@ -272,7 +270,27 @@
     grad[...] = lax.dot_general(
         normed[...], gp_ref[...], (((0,), (0,)), ((), ())), preferred_element_type=F32
     )
-    split_rows(grad, pieces, own, relative)
+    if not relative:
+        pieces[0][...] = grad[...]
+        return
+    home, second, sent = pieces
+    lines = home.shape[0] // own
+    for line in range(lines):
+        rows = slice(line * own, (line + 1) * own)
+        below = slice((lines + line) * own, (lines + line + 1) * own)
+        for ref, span, group in (
+            (home, rows, 0),
+            (second, rows, 2 - side),
+            (sent, rows, 1 + side),
+            (sent, below, INNER - 1),
+        ):
+            start = block_rows(True, group, line, own, lines)
+            ref[span, :] = grad[pl.ds(start, own), :].astype(ref.dtype)
+
+
+def relay_kernel(second_ref, came_ref, out_ref):
+    rows = out_ref.shape[0]
+    out_ref[...] = (second_ref[...] + came_ref[rows:, :].astype(F32)).astype(BF16)
 
 
 def back_project_kernel(weight, gp_ref, own_ref, other_ref):
@@ -413,6 +431,15 @@
         ]
         return lax.ppermute(array, ("shard", "rep"), pairs)
 
+    def hop(array, place):
+        flips = [(1, 2), (2, 1)]
+        pairs = [
+            (i * reps + r, (i ^ flips[r % 2][place]) * reps + r)
+            for i in range(shards)
+            for r in range(reps)
+        ]
+        return lax.ppermute(array, ("shard", "rep"), pairs)
+
     def over_core(array):
         return lax.ppermute(array, "rep", [(i, i ^ 1) for i in range(reps)])
 
@@ -514,8 +541,11 @@
     *pieces, grad_pre = call(
         functools.partial(project_kernel, relative, own),
         "project",
-        [shape((rows, quarter), F32)]
-        + [shape((rows, quarter), BF16)] * (INNER - 1)
+        (
+            [shape((rows, quarter), F32)] * 2 + [shape((2 * rows, quarter), BF16)]
+            if relative
+            else [shape((depth, quarter), F32)]
+        )
         + [shape((4 * pixels, quarter), BF16)],
         [
             pltpu.VMEM((4 * pixels, depth), BF16),
@@ -540,8 +570,13 @@
         weight,
         grad_pre,
     )
-    pieces = relative_order(pieces)
-    arrived = [over_shard(piece, flip) for flip, piece in enumerate(pieces) if flip]
+    if not relative:
+        first, second, corner = relative_order(list(pieces[0].reshape(INNER, rows, quarter)))[1:]
+        home = relative_order(list(pieces[0].reshape(INNER, rows, quarter)))[0]
+        first, second = jnp.where(side == 0, first, second), jnp.where(side == 0, second, first)
+        pieces = [home, second.astype(F32), jnp.concatenate([first, corner])]
+    home_piece, second_piece, sent_piece = pieces
+    first_came = hop(sent_piece, 0)
     *small, grad_conv, grad_sent = call(
         functools.partial(norm_back_kernel, relative, own, height, breadth),
         "norm_back",
@@ -567,6 +602,17 @@
         image,
         across,
     )
+    first_came, grad_conv = lax.optimization_barrier((first_came, grad_conv))
+    (relayed,) = call(
+        relay_kernel,
+        "relay",
+        [shape((rows, quarter), BF16)],
+        [],
+        0.3,
+        second_piece,
+        first_came,
+    )
+    second_came = hop(relayed, 1)
     small = relative_order(small)
     small_arrived = [crossing(piece, flip) for flip, piece in enumerate(small) if flip]
     grad_other = crossing(grad_sent, INNER)
@@ -586,9 +632,10 @@
         "plane_sum",
         [shape((own, quarter + LANES), F32)] + [shape((own, quarter + LANES), BF16)] * (lines - 1),
         [],
-        2.0,
-        pieces[0],
-        *arrived,
+        0.8,
+        home_piece,
+        first_came,
+        second_came,
         small[0],
         *small_arrived,
     )

time: 54.4 us -> 55.3 us (1.017)
  starting transfers between devices: 25.2 us -> 26 us
    ppermute x6 -> x3, starting transfers between devices: 7.15 us -> 3.66 us  [over_shard(): return lax.ppermute(array, 'shard', [(i, i ^ flip) for i in range(shards)])]
    ppermute x0 -> x2, starting transfers between devices: none -> 3.07 us  [hop(): return lax.ppermute(array, ('shard', 'rep'), pairs)]
    ppermute x0 -> x2, waiting for transfers between devices: none -> 1.62 us  [hop(): return lax.ppermute(array, ('shard', 'rep'), pairs)]
    ppermute x14, waiting for transfers between devices: 11.1 us -> 10.1 us  [crossing(): return lax.ppermute(array, ('shard', 'rep'), pairs)]
    ppermute x14, starting transfers between devices: 16.6 us -> 17.7 us  [crossing(): return lax.ppermute(array, ('shard', 'rep'), pairs)]
    ppermute x6 -> x3, waiting for transfers between devices: 1.83 us -> 1.09 us  [over_shard(): return lax.ppermute(array, 'shard', [(i, i ^ flip) for i in range(shards)])]
    pallas_call x12 -> x13, Pallas kernels: 13.3 us -> 13.3 us  [call(): pl.pallas_call(kernel, out_shape=outs, in_specs=[VMEM] * len(args), out_s...]
  transfers between devices with their start and end apart: 25 -> 24, of which waited for: 12 -> 13; matrix products, arithmetic and copies ran while one was open for 0% -> 0% of each run, Pallas kernels for 16% -> 16%
where the time goes in v13:
time: 55.3 us; the launch traced here: 55.2 us
  starting transfers between devices  26 us (47%)
  waiting for transfers between devices  15.1 us (27%)
  Pallas kernels  13.3 us (24%)
  between operations  0.73 us (1%)
    ppermute x14, starting transfers between devices, crossing(): return lax.ppermute(array, ('shard', 'rep'), pairs)  17.7 us
    pallas_call x13, Pallas kernels, call(): pl.pallas_call(kernel, out_shape=outs, in_specs=[VMEM] * len(args), out_s...  13.3 us
    ppermute x14, waiting for transfers between devices, crossing(): return lax.ppermute(array, ('shard', 'rep'), pairs)  10.1 us
    ppermute x3, starting transfers between devices, over_shard(): return lax.ppermute(array, 'shard', [(i, i ^ flip) for i in range(shards)])  3.66 us
    ppermute x2, starting transfers between devices, hop(): return lax.ppermute(array, ('shard', 'rep'), pairs)  3.07 us
    ppermute x5, waiting for transfers between devices, over_core(): return lax.ppermute(array, 'rep', [(i, i ^ 1) for i in range(reps)])  2.37 us
    ppermute x2, waiting for transfers between devices, hop(): return lax.ppermute(array, ('shard', 'rep'), pairs)  1.62 us
    ppermute x5, starting transfers between devices, over_core(): return lax.ppermute(array, 'rep', [(i, i ^ 1) for i in range(reps)])  1.56 us
  transfers between devices with their start and end apart: 24, of which 13 were waited for; matrix products, arithmetic and copies ran while one was open for 0% of the time, Pallas kernels for 16%

profile of v13, /device:TPU:0, one launch (start us, length us, event | category | flops | bytes accessed | tf_op | source)
XLA Modules:
  0.0 55.2 jit_solution(1157701339850875786)
XLA Ops:
  0.6 0.0 copy-start
  0.6 0.0 copy-start.1
  0.7 1.7 %pack.1 = (bf16[48,512]{1,0:T(8,128)(2,1)}, bf16[48,512]{1,0:T(8,128)(2,1)}, bf16[48,512]{1,0:T(8,128)(2,1)}) custom-call(bf16[48,1536]{1,0:T(8,128)(2,1)} %w_ref.1, bf16[48,49]{1,0:T(8,128)(2,1)} %dw_ref.1, bf16[1,48]{1,0:T(2,128)(2,1)} %bitcast.11, bf16[1,48]{1,0:T(2,128)(2,1)} %bitcast.12), custom_call_target="tpu_custom_call" | custom-call | flops 550000000 | bytes 299808 | tf_op jit(solution)/shard_map/pack/pallas_call | solution.py:399
  2.4 0.0 copy-start.2
  2.4 3.5 %collective-permute-start.1 = (bf16[48,512]{1,0:T(8,128)(2,1)}, bf16[48,512]{1,0:T(8,128)(2,1)S(1)}, u32[]{:S(2)}, u32[]{:S(2)}) collective-permute-start(bf16[48,512]{1,0:T(8,128)(2,1)} %get-tuple-element.52), channel_id=1, source_target_pairs={{0,17},{1,16},{2,19},{3,18},{4,21},{5,20},{6,23},{7,22},{8,25},{9,... | collective-permute-start | bytes 147464 | tf_op jit(solution)/shard_map/ppermute | solution.py:432
  5.9 1.6 %collective-permute-start.2 = (bf16[48,512]{1,0:T(8,128)(2,1)}, bf16[48,512]{1,0:T(8,128)(2,1)S(1)}, u32[]{:S(2)}, u32[]{:S(2)}) collective-permute-start(bf16[48,512]{1,0:T(8,128)(2,1)} %get-tuple-element.51), channel_id=1, source_target_pairs={{0,25},{1,24},{2,27},{3,26},{4,29},{5,28},{6,31},{7,30},{8,17},{9,... | collective-permute-start | bytes 147464 | tf_op jit(solution)/shard_map/ppermute | solution.py:432
  7.5 0.2 collective-permute-start
  7.7 0.0 copy-done
  7.7 0.0 copy-done.1
  7.8 1.6 %collective-permute-start.9 = (bf16[256,768]{1,0:T(8,128)(2,1)S(1)}, bf16[256,768]{1,0:T(8,128)(2,1)S(1)}, u32[]{:S(2)}, u32[]{:S(2)}) collective-permute-start(bf16[256,768]{1,0:T(8,128)(2,1)S(1)} %get-tuple-element.57), channel_id=1, source_target_pairs={{0,9},{1,8},{2,11},{3,10},{4,13},{5,12},{6,15},{7,14},{8,1},{9,0},... | collective-permute-start | bytes 1179656 | tf_op jit(solution)/shard_map/ppermute | solution.py:432
  9.4 0.0 collective-permute-done.1.refs_2_
  9.4 2.1 %collective-permute-done.2.refs_3_ = bf16[48,512]{1,0:T(8,128)(2,1)S(1)} collective-permute-done((bf16[48,512]{1,0:T(8,128)(2,1)}, bf16[48,512]{1,0:T(8,128)(2,1)S(1)}, u32[]{:S(2)}, u32[]{:S(2)}) %collective-permute-start.2) | collective-permute-done | bytes 49184 | tf_op jit(solution)/shard_map/ppermute | solution.py:432
  11.5 0.9 %collective-permute-done.refs_1_ = bf16[48,512]{1,0:T(8,128)(2,1)S(1)} collective-permute-done((bf16[48,512]{1,0:T(8,128)(2,1)}, bf16[48,512]{1,0:T(8,128)(2,1)S(1)}, u32[]{:S(2)}, u32[]{:S(2)}) %collective-permute-start) | collective-permute-done | bytes 49184 | tf_op jit(solution)/shard_map/ppermute | solution.py:432
  12.4 0.0 copy-done.2
  12.4 0.1 assemble.1
  12.5 2.9 %collective-permute-start.8 = (bf16[96,128]{1,0:T(8,128)(2,1)S(1)}, bf16[96,128]{1,0:T(8,128)(2,1)S(1)}, u32[]{:S(2)}, u32[]{:S(2)}) collective-permute-start(bf16[96,128]{1,0:T(8,128)(2,1)S(1)} %get-tuple-element.54.refs_0_), channel_id=1, source_target_pairs={{0,7},{1,6},{2,5},{3,4},{4,3},{5,2},{6,1},{7,0},{8,15},{9,14},{10,... | collective-permute-start | bytes 73736 | tf_op jit(solution)/shard_map/ppermute | solution.py:432
  15.4 0.0 collective-permute-start.7
  15.4 0.8 %collective-permute-start.6 = (bf16[96,128]{1,0:T(8,128)(2,1)S(1)}, bf16[96,128]{1,0:T(8,128)(2,1)S(1)}, u32[]{:S(2)}, u32[]{:S(2)}) collective-permute-start(bf16[96,128]{1,0:T(8,128)(2,1)S(1)} %get-tuple-element.54.refs_0_), channel_id=1, source_target_pairs={{0,3},{1,2},{2,1},{3,0},{4,7},{5,6},{6,5},{7,4},{8,11},{9,10},{10,... | collective-permute-start | bytes 73736 | tf_op jit(solution)/shard_map/ppermute | solution.py:432
  16.1 2.4 %collective-permute-start.5 = (bf16[192,384]{1,0:T(8,128)(2,1)S(1)}, bf16[192,384]{1,0:T(8,128)(2,1)S(1)}, u32[]{:S(2)}, u32[]{:S(2)}) collective-permute-start(bf16[192,384]{1,0:T(8,128)(2,1)S(1)} %get-tuple-element.53.refs_0_), channel_id=1, source_target_pairs={{0,6},{2,4},{4,2},{6,0},{8,14},{10,12},{12,10},{14,8},{16,22},{18,... | collective-permute-start | bytes 442376 | tf_op jit(solution)/shard_map/ppermute | solution.py:426
  18.6 0.0 collective-permute-done.8.refs_3_
  18.6 0.5 collective-permute-start.4
  19.1 0.0 collective-permute-done.7.refs_2_
  19.1 0.7 %collective-permute-start.3 = (bf16[192,384]{1,0:T(8,128)(2,1)S(1)}, bf16[192,384]{1,0:T(8,128)(2,1)S(1)}, u32[]{:S(2)}, u32[]{:S(2)}) collective-permute-start(bf16[192,384]{1,0:T(8,128)(2,1)S(1)} %get-tuple-element.53.refs_0_), channel_id=1, source_target_pairs={{0,2},{2,0},{4,6},{6,4},{8,10},{10,8},{12,14},{14,12},{16,18},{18,... | collective-permute-start | bytes 442376 | tf_op jit(solution)/shard_map/ppermute | solution.py:426
  19.8 0.0 collective-permute-done.6.refs_1_
  19.8 1.1 %collective-permute-done.9.refs_5_.refs_6_ = bf16[256,768]{1,0:T(8,128)(2,1)S(1)} collective-permute-done((bf16[256,768]{1,0:T(8,128)(2,1)S(1)}, bf16[256,768]{1,0:T(8,128)(2,1)S(1)}, u32[]{:S(2)}, u32[]{:S(2)}) %collective-permute-start.9) | collective-permute-done | bytes 393248 | tf_op jit(solution)/shard_map/ppermute | solution.py:432
  21.0 3.2 %conv_norm.1 = (bf16[256,768]{1,0:T(8,128)(2,1)S(1)}, f32[256,768]{1,0:T(8,128)S(1)}, f32[256,128]{1,0:T(8,128)S(1)}, f32[6,128,128]{2,1,0:T(8,128)S(1)}) custom-call(bf16[96,128]{1,0:T(8,128)(2,1)S(1)} %get-tuple-element.54.refs_0_, bf16[96,128]{1,0:T(8,128)(2,1)S(1)} %collective-permute-done.6.refs_1_, bf16[96,128]{1,0:T(8,128)(2,1)S(1)} %collective-permute-done.7.refs_2_, ...), custom_call_target="tpu_custom_call" | custom-call | flops 110000000 | bytes 2392064 | tf_op jit(solution)/shard_map/conv_norm/pallas_call | solution.py:399
  24.2 0.4 collective-permute-start.10
  24.6 0.1 collective-permute-start.12
  24.7 0.0 collective-permute-done.5.refs_3_
  24.7 0.4 collective-permute-start.11
  25.1 1.1 %collective-permute-done.4.refs_2_ = bf16[192,384]{1,0:T(8,128)(2,1)S(1)} collective-permute-done((bf16[192,384]{1,0:T(8,128)(2,1)S(1)}, bf16[192,384]{1,0:T(8,128)(2,1)S(1)}, u32[]{:S(2)}, u32[]{:S(2)}) %collective-permute-start.4) | collective-permute-done | bytes 147488 | tf_op jit(solution)/shard_map/ppermute | solution.py:426
  26.2 0.0 collective-permute-done.3.refs_1_
  26.2 0.1 order.1.refs_0_.weight
  26.3 0.5 collective-permute-done.11.refs_4_
  26.8 0.0 collective-permute-done.10.refs_2_
  26.8 0.0 collective-permute-done.12.refs_6_
  26.8 1.5 %project.1 = (f32[192,384]{1,0:T(8,128)S(1)}, f32[192,384]{1,0:T(8,128)S(1)}, bf16[384,384]{1,0:T(8,128)(2,1)S(1)}, bf16[512,384]{1,0:T(8,128)(2,1)S(1)}) custom-call(bf16[768,384]{1,0:T(8,128)(2,1)S(1)} %order.1.refs_0_.weight, bf16[256,768]{1,0:T(8,128)(2,1)S(1)} %get-tuple-element.59.refs_1_, bf16[256,768]{1,0:T(8,128)(2,1)S(1)} %collective-permute-done.10.refs_2_, ...), custom_call_target="tpu_custom_call" | custom-call | flops 1760000000 | bytes 4030464 | tf_op jit(solution)/shard_map/project/pallas_call | solution.py:399
  28.4 0.6 %back_project.1 = (f32[256,768]{1,0:T(8,128)S(1)}, f32[256,768]{1,0:T(8,128)S(1)}) custom-call(bf16[768,384]{1,0:T(8,128)(2,1)S(1)} %order.1.refs_0_.weight, bf16[512,384]{1,0:T(8,128)(2,1)S(1)} %get-tuple-element.64.gp_ref), custom_call_target="tpu_custom_call" | custom-call | flops 770000000 | bytes 2555904 | tf_op jit(solution)/shard_map/back_project/pallas_call | solution.py:399
  29.0 0.4 collective-permute-start.14
  29.4 1.5 %collective-permute-start.13 = (bf16[384,384]{1,0:T(8,128)(2,1)S(1)}, bf16[384,384]{1,0:T(8,128)(2,1)S(1)}, u32[]{:S(2)}, u32[]{:S(2)}) collective-permute-start(bf16[384,384]{1,0:T(8,128)(2,1)S(1)} %get-tuple-element.63), channel_id=1, source_target_pairs={{0,2},{1,5},{2,0},{3,7},{4,6},{5,1},{6,4},{7,3},{8,10},{9,13},{10,... | collective-permute-start | bytes 884744 | tf_op jit(solution)/shard_map/ppermute | solution.py:441
  30.9 0.4 collective-permute-done.14.refs_1_
  31.3 3.2 %norm_back.1 = (f32[96,128]{1,0:T(8,128)S(1)}, bf16[96,128]{1,0:T(8,128)(2,1)S(1)}, bf16[96,128]{1,0:T(8,128)(2,1)S(1)}, bf16[96,128]{1,0:T(8,128)(2,1)S(1)}, f3...) custom-call(f32[256,768]{1,0:T(8,128)S(1)} %get-tuple-element.65.refs_0_, ...), custom_call_target="tpu_custom_call" | custom-call | flops 110000000 | bytes 4186112 | tf_op jit(solution)/shard_map/norm_back/pallas_call | solution.py:399
  34.5 1.6 %collective-permute-done.13.came_ref.refs_1_ = bf16[384,384]{1,0:T(8,128)(2,1)S(1)} collective-permute-done((bf16[384,384]{1,0:T(8,128)(2,1)S(1)}, bf16[384,384]{1,0:T(8,128)(2,1)S(1)}, u32[]{:S(2)}, u32[]{:S(2)}) %collective-permute-start.13) | collective-permute-done | bytes 294944 | tf_op jit(solution)/shard_map/ppermute | solution.py:441
  36.2 1.6 %collective-permute-start.15 = (bf16[192,384]{1,0:T(8,128)(2,1)S(1)}, bf16[192,384]{1,0:T(8,128)(2,1)S(1)}, u32[]{:S(2)}, u32[]{:S(2)}) collective-permute-start(bf16[192,384]{1,0:T(8,128)(2,1)S(1)} %relay.1), channel_id=1, source_target_pairs={{0,4},{1,3},{2,6},{3,1},{4,0},{5,7},{6,2},{7,5},{8,12},{9,11},{10,... | collective-permute-start | bytes 442376 | tf_op jit(solution)/shard_map/ppermute | solution.py:441
  37.7 0.0 collective-permute-start.19
  37.7 1.2 %collective-permute-start.16 = (bf16[96,128]{1,0:T(8,128)(2,1)S(1)}, bf16[96,128]{1,0:T(8,128)(2,1)S(1)}, u32[]{:S(2)}, u32[]{:S(2)}) collective-permute-start(bf16[96,128]{1,0:T(8,128)(2,1)S(1)} %get-tuple-element.74), channel_id=1, source_target_pairs={{0,3},{1,2},{2,1},{3,0},{4,7},{5,6},{6,5},{7,4},{8,11},{9,10},{10,... | collective-permute-start | bytes 73736 | tf_op jit(solution)/shard_map/ppermute | solution.py:432
  39.0 0.5 collective-permute-start.17
  39.5 1.3 %collective-permute-start.18 = (bf16[96,128]{1,0:T(8,128)(2,1)S(1)}, bf16[96,128]{1,0:T(8,128)(2,1)S(1)}, u32[]{:S(2)}, u32[]{:S(2)}) collective-permute-start(bf16[96,128]{1,0:T(8,128)(2,1)S(1)} %get-tuple-element.76), channel_id=1, source_target_pairs={{0,7},{1,6},{2,5},{3,4},{4,3},{5,2},{6,1},{7,0},{8,15},{9,14},{10,... | collective-permute-start | bytes 73736 | tf_op jit(solution)/shard_map/ppermute | solution.py:432
  40.7 0.3 collective-permute-done.16.refs_4_
  41.0 1.3 %collective-permute-done.17.refs_5_ = bf16[96,128]{1,0:T(8,128)(2,1)S(1)} collective-permute-done((bf16[96,128]{1,0:T(8,128)(2,1)S(1)}, bf16[96,128]{1,0:T(8,128)(2,1)S(1)}, u32[]{:S(2)}, u32[]{:S(2)}) %collective-permute-start.17) | collective-permute-done | bytes 24608 | tf_op jit(solution)/shard_map/ppermute | solution.py:432
  42.2 1.4 %collective-permute-done.18.refs_6_ = bf16[96,128]{1,0:T(8,128)(2,1)S(1)} collective-permute-done((bf16[96,128]{1,0:T(8,128)(2,1)S(1)}, bf16[96,128]{1,0:T(8,128)(2,1)S(1)}, u32[]{:S(2)}, u32[]{:S(2)}) %collective-permute-start.18) | collective-permute-done | bytes 24608 | tf_op jit(solution)/shard_map/ppermute | solution.py:432
  43.6 0.0 collective-permute-done.15.refs_2_
  43.6 0.1 plane_sum.1
  43.7 1.8 %collective-permute-start.20 = (bf16[48,512]{1,0:T(8,128)(2,1)S(1)}, bf16[48,512]{1,0:T(8,128)(2,1)S(1)}, u32[]{:S(2)}, u32[]{:S(2)}) collective-permute-start(bf16[48,512]{1,0:T(8,128)(2,1)S(1)} %get-tuple-element.82), channel_id=1, source_target_pairs={{0,9},{1,8},{2,11},{3,10},{4,13},{5,12},{6,15},{7,14},{8,1},{9,0},... | collective-permute-start | bytes 147464 | tf_op jit(solution)/shard_map/ppermute | solution.py:432
  45.5 1.6 %collective-permute-start.21 = (bf16[48,512]{1,0:T(8,128)(2,1)S(1)}, bf16[48,512]{1,0:T(8,128)(2,1)S(1)}, u32[]{:S(2)}, u32[]{:S(2)}) collective-permute-start(bf16[48,512]{1,0:T(8,128)(2,1)S(1)} %get-tuple-element.83), channel_id=1, source_target_pairs={{0,17},{1,16},{2,19},{3,18},{4,21},{5,20},{6,23},{7,22},{8,25},{9,... | collective-permute-start | bytes 147464 | tf_op jit(solution)/shard_map/ppermute | solution.py:432
  47.1 0.7 %collective-permute-start.22 = (bf16[48,512]{1,0:T(8,128)(2,1)S(1)}, bf16[48,512]{1,0:T(8,128)(2,1)S(1)}, u32[]{:S(2)}, u32[]{:S(2)}) collective-permute-start(bf16[48,512]{1,0:T(8,128)(2,1)S(1)} %get-tuple-element.84), channel_id=1, source_target_pairs={{0,25},{1,24},{2,27},{3,26},{4,29},{5,28},{6,31},{7,30},{8,17},{9,... | collective-permute-start | bytes 147464 | tf_op jit(solution)/shard_map/ppermute | solution.py:432
  47.9 0.0 collective-permute-done.19.other_ref
  47.9 1.9 %conv_back.1 = bf16[1,8,16,768]{3,2,1,0:T(8,128)(2,1)} custom-call(f32[6,8,16,128]{3,2,1,0:T(8,128)S(1)} %get-tuple-element.78.grad_ref, bf16[6,8,16,128]{3,2,1,0:T(8,128)(2,1)S(1)} %collective-permute-done.19.other_ref, f32[6,128,128]{2,1,0:T(8,128)S(1)} %get-tuple-element.69.refs_4_.taps_ref), custom_call_target="tpu_custom_call" | custom-call | flops 110000000 | bytes 1179648 | tf_op jit(solution)/shard_map/conv_back/pallas_call | solution.py:399
  49.8 0.0 collective-permute-done.20.refs_1_
  49.8 1.6 %collective-permute-done.21.refs_2_ = bf16[48,512]{1,0:T(8,128)(2,1)S(1)} collective-permute-done((bf16[48,512]{1,0:T(8,128)(2,1)S(1)}, bf16[48,512]{1,0:T(8,128)(2,1)S(1)}, u32[]{:S(2)}, u32[]{:S(2)}) %collective-permute-start.21) | collective-permute-done | bytes 49184 | tf_op jit(solution)/shard_map/ppermute | solution.py:432
  51.4 1.4 %collective-permute-done.22.refs_3_ = bf16[48,512]{1,0:T(8,128)(2,1)S(1)} collective-permute-done((bf16[48,512]{1,0:T(8,128)(2,1)S(1)}, bf16[48,512]{1,0:T(8,128)(2,1)S(1)}, u32[]{:S(2)}, u32[]{:S(2)}) %collective-permute-start.22) | collective-permute-done | bytes 49184 | tf_op jit(solution)/shard_map/ppermute | solution.py:432
  52.8 0.2 collective-permute-start.23
  53.0 1.4 %collective-permute-done.23.other_ref = f32[48,1280]{1,0:T(8,128)S(1)} collective-permute-done((f32[48,1280]{1,0:T(8,128)S(1)}, f32[48,1280]{1,0:T(8,128)S(1)}, u32[]{:S(2)}, u32[]{:S(2)}) %collective-permute-start.23) | collective-permute-done | bytes 245792 | tf_op jit(solution)/shard_map/ppermute | solution.py:444
  54.4 0.8 %finish.1 = (f32[48,1536]{1,0:T(8,128)}, f32[48,49]{1,0:T(8,128)}, f32[1,48]{1,0:T(1,128)}, f32[1,48]{1,0:T(1,128)}) custom-call(f32[48,1280]{1,0:T(8,128)S(1)} %line_sum.1.mine_ref, f32[48,1280]{1,0:T(8,128)S(1)} %collective-permute-done.23.other_ref), custom_call_target="tpu_custom_call" | custom-call | flops 550000000 | bytes 796224 | tf_op jit(solution)/shard_map/finish/pallas_call | solution.py:399
  (3 shorter events, 0.1 us)
Async XLA Ops:
  0.6 7.1 %copy-start = (bf16[1,8,16,768]{3,2,1,0:T(8,128)(2,1)S(1)}, bf16[1,8,16,768]{3,2,1,0:T(8,128)(2,1)}, u32[]{:S(2)}) copy-start(bf16[1,8,16,768]{3,2,1,0:T(8,128)(2,1)} %param.6) | copy-start | bytes 589828
  0.6 7.1 %copy-start.1 = (bf16[1,8,16,1536]{3,2,1,0:T(8,128)(2,1)S(1)}, bf16[1,8,16,1536]{3,2,1,0:T(8,128)(2,1)}, u32[]{:S(2)}) copy-start(bf16[1,8,16,1536]{3,2,1,0:T(8,128)(2,1)} %param.7) | copy-start | bytes 1179652
  2.4 10.0 %copy-start.2 = (bf16[48,512]{1,0:T(8,128)(2,1)S(1)}, bf16[48,512]{1,0:T(8,128)(2,1)}, u32[]{:S(2)}) copy-start(bf16[48,512]{1,0:T(8,128)(2,1)} %get-tuple-element.50.refs_0_) | copy-start | bytes 147460
  2.4 7.0 %collective-permute-start.1 = (bf16[48,512]{1,0:T(8,128)(2,1)}, bf16[48,512]{1,0:T(8,128)(2,1)S(1)}, u32[]{:S(2)}, u32[]{:S(2)}) collective-permute-start(bf16[48,512]{1,0:T(8,128)(2,1)} %get-tuple-element.52), channel_id=1, source_target_pairs={{0,17},{1,16},{2,19},{3,18},{4,21},{5,20},{6,23},{7,22},{8,25},{9,... | collective-permute-start | bytes 147464 | tf_op jit(solution)/shard_map/ppermute | solution.py:432
  5.9 5.6 %collective-permute-start.2 = (bf16[48,512]{1,0:T(8,128)(2,1)}, bf16[48,512]{1,0:T(8,128)(2,1)S(1)}, u32[]{:S(2)}, u32[]{:S(2)}) collective-permute-start(bf16[48,512]{1,0:T(8,128)(2,1)} %get-tuple-element.51), channel_id=1, source_target_pairs={{0,25},{1,24},{2,27},{3,26},{4,29},{5,28},{6,31},{7,30},{8,17},{9,... | collective-permute-start | bytes 147464 | tf_op jit(solution)/shard_map/ppermute | solution.py:432
  7.5 4.9 %collective-permute-start = (bf16[48,512]{1,0:T(8,128)(2,1)}, bf16[48,512]{1,0:T(8,128)(2,1)S(1)}, u32[]{:S(2)}, u32[]{:S(2)}) collective-permute-start(bf16[48,512]{1,0:T(8,128)(2,1)} %get-tuple-element.51), channel_id=1, source_target_pairs={{0,9},{1,8},{2,11},{3,10},{4,13},{5,12},{6,15},{7,14},{8,1},{9,0},... | collective-permute-start | bytes 147464 | tf_op jit(solution)/shard_map/ppermute | solution.py:432
  7.8 13.2 %collective-permute-start.9 = (bf16[256,768]{1,0:T(8,128)(2,1)S(1)}, bf16[256,768]{1,0:T(8,128)(2,1)S(1)}, u32[]{:S(2)}, u32[]{:S(2)}) collective-permute-start(bf16[256,768]{1,0:T(8,128)(2,1)S(1)} %get-tuple-element.57), channel_id=1, source_target_pairs={{0,9},{1,8},{2,11},{3,10},{4,13},{5,12},{6,15},{7,14},{8,1},{9,0},... | collective-permute-start | bytes 1179656 | tf_op jit(solution)/shard_map/ppermute | solution.py:432
  12.5 6.1 %collective-permute-start.8 = (bf16[96,128]{1,0:T(8,128)(2,1)S(1)}, bf16[96,128]{1,0:T(8,128)(2,1)S(1)}, u32[]{:S(2)}, u32[]{:S(2)}) collective-permute-start(bf16[96,128]{1,0:T(8,128)(2,1)S(1)} %get-tuple-element.54.refs_0_), channel_id=1, source_target_pairs={{0,7},{1,6},{2,5},{3,4},{4,3},{5,2},{6,1},{7,0},{8,15},{9,14},{10,... | collective-permute-start | bytes 73736 | tf_op jit(solution)/shard_map/ppermute | solution.py:432
  15.4 3.7 %collective-permute-start.7 = (bf16[96,128]{1,0:T(8,128)(2,1)S(1)}, bf16[96,128]{1,0:T(8,128)(2,1)S(1)}, u32[]{:S(2)}, u32[]{:S(2)}) collective-permute-start(bf16[96,128]{1,0:T(8,128)(2,1)S(1)} %get-tuple-element.54.refs_0_), channel_id=1, source_target_pairs={{0,5},{1,4},{2,7},{3,6},{4,1},{5,0},{6,3},{7,2},{8,13},{9,12},{10,... | collective-permute-start | bytes 73736 | tf_op jit(solution)/shard_map/ppermute | solution.py:432
  15.4 4.4 %collective-permute-start.6 = (bf16[96,128]{1,0:T(8,128)(2,1)S(1)}, bf16[96,128]{1,0:T(8,128)(2,1)S(1)}, u32[]{:S(2)}, u32[]{:S(2)}) collective-permute-start(bf16[96,128]{1,0:T(8,128)(2,1)S(1)} %get-tuple-element.54.refs_0_), channel_id=1, source_target_pairs={{0,3},{1,2},{2,1},{3,0},{4,7},{5,6},{6,5},{7,4},{8,11},{9,10},{10,... | collective-permute-start | bytes 73736 | tf_op jit(solution)/shard_map/ppermute | solution.py:432
  16.1 8.6 %collective-permute-start.5 = (bf16[192,384]{1,0:T(8,128)(2,1)S(1)}, bf16[192,384]{1,0:T(8,128)(2,1)S(1)}, u32[]{:S(2)}, u32[]{:S(2)}) collective-permute-start(bf16[192,384]{1,0:T(8,128)(2,1)S(1)} %get-tuple-element.53.refs_0_), channel_id=1, source_target_pairs={{0,6},{2,4},{4,2},{6,0},{8,14},{10,12},{12,10},{14,8},{16,22},{18,... | collective-permute-start | bytes 442376 | tf_op jit(solution)/shard_map/ppermute | solution.py:426
  18.6 7.6 %collective-permute-start.4 = (bf16[192,384]{1,0:T(8,128)(2,1)S(1)}, bf16[192,384]{1,0:T(8,128)(2,1)S(1)}, u32[]{:S(2)}, u32[]{:S(2)}) collective-permute-start(bf16[192,384]{1,0:T(8,128)(2,1)S(1)} %get-tuple-element.53.refs_0_), channel_id=1, source_target_pairs={{0,4},{2,6},{4,0},{6,2},{8,12},{10,14},{12,8},{14,10},{16,20},{18,... | collective-permute-start | bytes 442376 | tf_op jit(solution)/shard_map/ppermute | solution.py:426
  19.1 7.1 %collective-permute-start.3 = (bf16[192,384]{1,0:T(8,128)(2,1)S(1)}, bf16[192,384]{1,0:T(8,128)(2,1)S(1)}, u32[]{:S(2)}, u32[]{:S(2)}) collective-permute-start(bf16[192,384]{1,0:T(8,128)(2,1)S(1)} %get-tuple-element.53.refs_0_), channel_id=1, source_target_pairs={{0,2},{2,0},{4,6},{6,4},{8,10},{10,8},{12,14},{14,12},{16,18},{18,... | collective-permute-start | bytes 442376 | tf_op jit(solution)/shard_map/ppermute | solution.py:426
  24.2 2.6 %collective-permute-start.10 = (bf16[256,768]{1,0:T(8,128)(2,1)S(1)}, bf16[256,768]{1,0:T(8,128)(2,1)S(1)}, u32[]{:S(2)}, u32[]{:S(2)}) collective-permute-start(bf16[256,768]{1,0:T(8,128)(2,1)S(1)} %get-tuple-element.59.refs_1_), channel_id=1, source_target_pairs={{0,1},{1,0},{2,3},{3,2},{4,5},{5,4},{6,7},{7,6},{8,9},{9,8},{10,11... | collective-permute-start | bytes 1179656 | tf_op jit(solution)/shard_map/ppermute | solution.py:444
  24.6 2.2 %collective-permute-start.12 = (bf16[256,768]{1,0:T(8,128)(2,1)S(1)}, bf16[256,768]{1,0:T(8,128)(2,1)S(1)}, u32[]{:S(2)}, u32[]{:S(2)}) collective-permute-start(bf16[256,768]{1,0:T(8,128)(2,1)S(1)} %collective-permute-done.9.refs_5_.refs_6_), channel_id=1, source_target_pairs={{0,1},{1,0},{2,3},{3,2},{4,5},{5,4},{6,7},{7,6},{8,9},{9,8},{10,11... | collective-permute-start | bytes 1179656 | tf_op jit(solution)/shard_map/ppermute | solution.py:444
  24.7 2.1 %collective-permute-start.11 = (bf16[128,768]{1,0:T(8,128)(2,1)S(1)}, bf16[128,768]{1,0:T(8,128)(2,1)S(1)}, u32[]{:S(2)}, u32[]{:S(2)}) collective-permute-start(bf16[128,768]{1,0:T(8,128)(2,1)S(1)} %get-tuple-element.60), channel_id=1, source_target_pairs={{0,1},{1,0},{2,3},{3,2},{4,5},{5,4},{6,7},{7,6},{8,9},{9,8},{10,11... | collective-permute-start | bytes 589832 | tf_op jit(solution)/shard_map/ppermute | solution.py:444
  29.0 2.4 %collective-permute-start.14 = (f32[256,768]{1,0:T(8,128)S(1)}, f32[256,768]{1,0:T(8,128)S(1)}, u32[]{:S(2)}, u32[]{:S(2)}) collective-permute-start(f32[256,768]{1,0:T(8,128)S(1)} %get-tuple-element.66), channel_id=1, source_target_pairs={{0,1},{1,0},{2,3},{3,2},{4,5},{5,4},{6,7},{7,6},{8,9},{9,8},{10,11... | collective-permute-start | bytes 2359304 | tf_op jit(solution)/shard_map/ppermute | solution.py:444
  29.4 6.7 %collective-permute-start.13 = (bf16[384,384]{1,0:T(8,128)(2,1)S(1)}, bf16[384,384]{1,0:T(8,128)(2,1)S(1)}, u32[]{:S(2)}, u32[]{:S(2)}) collective-permute-start(bf16[384,384]{1,0:T(8,128)(2,1)S(1)} %get-tuple-element.63), channel_id=1, source_target_pairs={{0,2},{1,5},{2,0},{3,7},{4,6},{5,1},{6,4},{7,3},{8,10},{9,13},{10,... | collective-permute-start | bytes 884744 | tf_op jit(solution)/shard_map/ppermute | solution.py:441
  36.2 7.5 %collective-permute-start.15 = (bf16[192,384]{1,0:T(8,128)(2,1)S(1)}, bf16[192,384]{1,0:T(8,128)(2,1)S(1)}, u32[]{:S(2)}, u32[]{:S(2)}) collective-permute-start(bf16[192,384]{1,0:T(8,128)(2,1)S(1)} %relay.1), channel_id=1, source_target_pairs={{0,4},{1,3},{2,6},{3,1},{4,0},{5,7},{6,2},{7,5},{8,12},{9,11},{10,... | collective-permute-start | bytes 442376 | tf_op jit(solution)/shard_map/ppermute | solution.py:441
  37.7 10.1 %collective-permute-start.19 = (bf16[6,8,16,128]{3,2,1,0:T(8,128)(2,1)S(1)}, bf16[6,8,16,128]{3,2,1,0:T(8,128)(2,1)S(1)}, u32[]{:S(2)}, u32[]{:S(2)}) collective-permute-start(bf16[6,8,16,128]{3,2,1,0:T(8,128)(2,1)S(1)} %get-tuple-element.79), channel_id=1, source_target_pairs={{0,9},{1,8},{2,11},{3,10},{4,13},{5,12},{6,15},{7,14},{8,1},{9,0},... | collective-permute-start | bytes 589832 | tf_op jit(solution)/shard_map/ppermute | solution.py:432
  37.7 3.3 %collective-permute-start.16 = (bf16[96,128]{1,0:T(8,128)(2,1)S(1)}, bf16[96,128]{1,0:T(8,128)(2,1)S(1)}, u32[]{:S(2)}, u32[]{:S(2)}) collective-permute-start(bf16[96,128]{1,0:T(8,128)(2,1)S(1)} %get-tuple-element.74), channel_id=1, source_target_pairs={{0,3},{1,2},{2,1},{3,0},{4,7},{5,6},{6,5},{7,4},{8,11},{9,10},{10,... | collective-permute-start | bytes 73736 | tf_op jit(solution)/shard_map/ppermute | solution.py:432
  39.0 3.3 %collective-permute-start.17 = (bf16[96,128]{1,0:T(8,128)(2,1)S(1)}, bf16[96,128]{1,0:T(8,128)(2,1)S(1)}, u32[]{:S(2)}, u32[]{:S(2)}) collective-permute-start(bf16[96,128]{1,0:T(8,128)(2,1)S(1)} %get-tuple-element.75), channel_id=1, source_target_pairs={{0,5},{1,4},{2,7},{3,6},{4,1},{5,0},{6,3},{7,2},{8,13},{9,12},{10,... | collective-permute-start | bytes 73736 | tf_op jit(solution)/shard_map/ppermute | solution.py:432
  39.5 4.2 %collective-permute-start.18 = (bf16[96,128]{1,0:T(8,128)(2,1)S(1)}, bf16[96,128]{1,0:T(8,128)(2,1)S(1)}, u32[]{:S(2)}, u32[]{:S(2)}) collective-permute-start(bf16[96,128]{1,0:T(8,128)(2,1)S(1)} %get-tuple-element.76), channel_id=1, source_target_pairs={{0,7},{1,6},{2,5},{3,4},{4,3},{5,2},{6,1},{7,0},{8,15},{9,14},{10,... | collective-permute-start | bytes 73736 | tf_op jit(solution)/shard_map/ppermute | solution.py:432
  43.7 6.1 %collective-permute-start.20 = (bf16[48,512]{1,0:T(8,128)(2,1)S(1)}, bf16[48,512]{1,0:T(8,128)(2,1)S(1)}, u32[]{:S(2)}, u32[]{:S(2)}) collective-permute-start(bf16[48,512]{1,0:T(8,128)(2,1)S(1)} %get-tuple-element.82), channel_id=1, source_target_pairs={{0,9},{1,8},{2,11},{3,10},{4,13},{5,12},{6,15},{7,14},{8,1},{9,0},... | collective-permute-start | bytes 147464 | tf_op jit(solution)/shard_map/ppermute | solution.py:432
  45.5 5.9 %collective-permute-start.21 = (bf16[48,512]{1,0:T(8,128)(2,1)S(1)}, bf16[48,512]{1,0:T(8,128)(2,1)S(1)}, u32[]{:S(2)}, u32[]{:S(2)}) collective-permute-start(bf16[48,512]{1,0:T(8,128)(2,1)S(1)} %get-tuple-element.83), channel_id=1, source_target_pairs={{0,17},{1,16},{2,19},{3,18},{4,21},{5,20},{6,23},{7,22},{8,25},{9,... | collective-permute-start | bytes 147464 | tf_op jit(solution)/shard_map/ppermute | solution.py:432
  47.1 5.7 %collective-permute-start.22 = (bf16[48,512]{1,0:T(8,128)(2,1)S(1)}, bf16[48,512]{1,0:T(8,128)(2,1)S(1)}, u32[]{:S(2)}, u32[]{:S(2)}) collective-permute-start(bf16[48,512]{1,0:T(8,128)(2,1)S(1)} %get-tuple-element.84), channel_id=1, source_target_pairs={{0,25},{1,24},{2,27},{3,26},{4,29},{5,28},{6,31},{7,30},{8,17},{9,... | collective-permute-start | bytes 147464 | tf_op jit(solution)/shard_map/ppermute | solution.py:432
  52.8 1.6 %collective-permute-start.23 = (f32[48,1280]{1,0:T(8,128)S(1)}, f32[48,1280]{1,0:T(8,128)S(1)}, u32[]{:S(2)}, u32[]{:S(2)}) collective-permute-start(f32[48,1280]{1,0:T(8,128)S(1)} %line_sum.1.mine_ref), channel_id=1, source_target_pairs={{0,1},{1,0},{2,3},{3,2},{4,5},{5,4},{6,7},{7,6},{8,9},{9,8},{10,11... | collective-permute-start | bytes 737288 | tf_op jit(solution)/shard_map/ppermute | solution.py:444

commit v14 on v12

--- a/solution.py
+++ b/solution.py
@@ -243,8 +243,30 @@
     sibling_ref[...] = cot_ref[:, pl.ds(pl.multiple_of((1 - side) * half, LANES), half)]
 
 
+def join_kernel(own_ref, came_ref, out_ref):
+    rows = own_ref.shape[0]
+    out_ref[:rows, :] = own_ref[...]
+    out_ref[rows:, :] = came_ref[...]
+
+
 def order_kernel(relative, own, *refs):
-    place_rows(refs[:INNER], refs[INNER], own, relative)
+    if not relative:
+        place_rows(refs[:INNER], refs[INNER], own, relative)
+        return
+    home, first, second, out_ref = refs
+    side = lax.axis_index("rep") % 2
+    lines = home.shape[0] // own
+    for line in range(lines):
+        rows = slice(line * own, (line + 1) * own)
+        below = slice((lines + line) * own, (lines + line + 1) * own)
+        for ref, span, group in (
+            (home, rows, 0),
+            (first, rows, 1 + side),
+            (second, rows, 2 - side),
+            (second, below, INNER - 1),
+        ):
+            start = block_rows(True, group, line, own, lines)
+            out_ref[pl.ds(start, own), :] = ref[span, :]
 
 
 def project_kernel(relative, own, *refs):
@@ -413,6 +435,15 @@
         ]
         return lax.ppermute(array, ("shard", "rep"), pairs)
 
+    def hop(array, place):
+        flips = [(1, 2), (2, 1)]
+        pairs = [
+            (i * reps + r, (i ^ flips[r % 2][place]) * reps + r)
+            for i in range(shards)
+            for r in range(reps)
+        ]
+        return lax.ppermute(array, ("shard", "rep"), pairs)
+
     def over_core(array):
         return lax.ppermute(array, "rep", [(i, i ^ 1) for i in range(reps)])
 
@@ -476,15 +507,30 @@
         4.0,
         *gathered,
     )
-    weights = [weight_lines] + [over_shard(weight_lines, flip) for flip in range(1, INNER)]
+    first_lines = hop(weight_lines, 0)
+    (joined,) = call(
+        join_kernel,
+        "join",
+        [shape((2 * rows, quarter), BF16)],
+        [],
+        0.3,
+        weight_lines,
+        first_lines,
+    )
+    second_lines = hop(joined, 1)
+    weights = [weight_lines, first_lines, second_lines]
     extras = [extra_lines] + [crossing(extra_lines, flip) for flip in range(1, INNER)]
-    weights, extras = true_order(weights), true_order(extras)
+    if not relative:
+        extras = true_order(extras)
+        x_lines = jnp.where(side == 0, first_lines, second_lines[:rows])
+        y_lines = jnp.where(side == 0, second_lines[:rows], first_lines)
+        weights = true_order([weight_lines, x_lines, y_lines, second_lines[rows:]])
     (weight,) = call(
         functools.partial(order_kernel, relative, own),
         "order",
         [shape((depth, quarter), BF16)],
         [],
-        3.0,
+        1.0,
         *weights,
     )
 

time: 61.2 us -> 54.4 us (0.89)
  waiting for transfers between devices: 21.5 us -> 15.8 us
  starting transfers between devices: 25.5 us -> 24.4 us
    ppermute x14, waiting for transfers between devices: 17.4 us -> 11.1 us  [crossing(): return lax.ppermute(array, ('shard', 'rep'), pairs)]
    ppermute x6 -> x3, starting transfers between devices: 6.98 us -> 3.5 us  [over_shard(): return lax.ppermute(array, 'shard', [(i, i ^ flip) for i in range(shards)])]
    ppermute x0 -> x2, starting transfers between devices: none -> 3.4 us  [hop(): return lax.ppermute(array, ('shard', 'rep'), pairs)]
    pallas_call x12 -> x13, Pallas kernels: 13.3 us -> 13.3 us  [call(): pl.pallas_call(kernel, out_shape=outs, in_specs=[VMEM] * len(args), out_s...]
  transfers between devices with their start and end apart: 25 -> 24, of which waited for: 12 -> 12; matrix products, arithmetic and copies ran while one was open for 0% -> 0% of each run, Pallas kernels for 14% -> 16%
where the time goes in v14:
time: 54.4 us; the launch traced here: 54.3 us
  starting transfers between devices  24.4 us (45%)
  waiting for transfers between devices  15.8 us (29%)
  Pallas kernels  13.3 us (24%)
  between operations  0.75 us (1%)
    ppermute x14, starting transfers between devices, crossing(): return lax.ppermute(array, ('shard', 'rep'), pairs)  16.6 us
    pallas_call x13, Pallas kernels, call(): pl.pallas_call(kernel, out_shape=outs, in_specs=[VMEM] * len(args), out_s...  13.3 us
    ppermute x14, waiting for transfers between devices, crossing(): return lax.ppermute(array, ('shard', 'rep'), pairs)  11.1 us
    ppermute x3, starting transfers between devices, over_shard(): return lax.ppermute(array, 'shard', [(i, i ^ flip) for i in range(shards)])  3.5 us
    ppermute x2, starting transfers between devices, hop(): return lax.ppermute(array, ('shard', 'rep'), pairs)  3.4 us
    ppermute x5, waiting for transfers between devices, over_core(): return lax.ppermute(array, 'rep', [(i, i ^ 1) for i in range(reps)])  3.37 us
  transfers between devices with their start and end apart: 24, of which 12 were waited for; matrix products, arithmetic and copies ran while one was open for 0% of the time, Pallas kernels for 16%

profile of v14, /device:TPU:0, one launch (start us, length us, event | category | flops | bytes accessed | tf_op | source)
XLA Modules:
  0.0 54.3 jit_solution(2600959098589998895)
XLA Ops:
  0.6 0.0 copy-start
  0.6 0.0 copy-start.1
  0.7 1.7 %pack.1 = (bf16[48,512]{1,0:T(8,128)(2,1)}, bf16[48,512]{1,0:T(8,128)(2,1)}, bf16[48,512]{1,0:T(8,128)(2,1)}) custom-call(bf16[48,1536]{1,0:T(8,128)(2,1)} %w_ref.1, bf16[48,49]{1,0:T(8,128)(2,1)} %dw_ref.1, bf16[1,48]{1,0:T(2,128)(2,1)} %bitcast.11, bf16[1,48]{1,0:T(2,128)(2,1)} %bitcast.12), custom_call_target="tpu_custom_call" | custom-call | flops 550000000 | bytes 299808 | tf_op jit(solution)/shard_map/pack/pallas_call | solution.py:403
  2.4 0.0 copy-start.2
  2.4 3.5 %collective-permute-start.1 = (bf16[48,512]{1,0:T(8,128)(2,1)}, bf16[48,512]{1,0:T(8,128)(2,1)S(1)}, u32[]{:S(2)}, u32[]{:S(2)}) collective-permute-start(bf16[48,512]{1,0:T(8,128)(2,1)} %get-tuple-element.51), channel_id=1, source_target_pairs={{0,17},{1,16},{2,19},{3,18},{4,21},{5,20},{6,23},{7,22},{8,25},{9,... | collective-permute-start | bytes 147464 | tf_op jit(solution)/shard_map/ppermute | solution.py:436
  5.9 1.6 %collective-permute-start.2 = (bf16[48,512]{1,0:T(8,128)(2,1)}, bf16[48,512]{1,0:T(8,128)(2,1)S(1)}, u32[]{:S(2)}, u32[]{:S(2)}) collective-permute-start(bf16[48,512]{1,0:T(8,128)(2,1)} %get-tuple-element.50), channel_id=1, source_target_pairs={{0,25},{1,24},{2,27},{3,26},{4,29},{5,28},{6,31},{7,30},{8,17},{9,... | collective-permute-start | bytes 147464 | tf_op jit(solution)/shard_map/ppermute | solution.py:436
  7.5 0.2 collective-permute-start
  7.7 0.0 copy-done
  7.7 0.0 copy-done.1
  7.8 1.6 %collective-permute-start.8 = (bf16[256,768]{1,0:T(8,128)(2,1)S(1)}, bf16[256,768]{1,0:T(8,128)(2,1)S(1)}, u32[]{:S(2)}, u32[]{:S(2)}) collective-permute-start(bf16[256,768]{1,0:T(8,128)(2,1)S(1)} %get-tuple-element.56), channel_id=1, source_target_pairs={{0,9},{1,8},{2,11},{3,10},{4,13},{5,12},{6,15},{7,14},{8,1},{9,0},... | collective-permute-start | bytes 1179656 | tf_op jit(solution)/shard_map/ppermute | solution.py:436
  9.4 0.0 collective-permute-done.1.refs_2_
  9.4 2.1 %collective-permute-done.2.refs_3_ = bf16[48,512]{1,0:T(8,128)(2,1)S(1)} collective-permute-done((bf16[48,512]{1,0:T(8,128)(2,1)}, bf16[48,512]{1,0:T(8,128)(2,1)S(1)}, u32[]{:S(2)}, u32[]{:S(2)}) %collective-permute-start.2) | collective-permute-done | bytes 49184 | tf_op jit(solution)/shard_map/ppermute | solution.py:436
  11.5 0.9 %collective-permute-done.refs_1_ = bf16[48,512]{1,0:T(8,128)(2,1)S(1)} collective-permute-done((bf16[48,512]{1,0:T(8,128)(2,1)}, bf16[48,512]{1,0:T(8,128)(2,1)S(1)}, u32[]{:S(2)}, u32[]{:S(2)}) %collective-permute-start) | collective-permute-done | bytes 49184 | tf_op jit(solution)/shard_map/ppermute | solution.py:436
  12.4 0.0 copy-done.2
  12.4 0.1 assemble.1
  12.5 1.6 %collective-permute-start.3 = (bf16[192,384]{1,0:T(8,128)(2,1)S(1)}, bf16[192,384]{1,0:T(8,128)(2,1)S(1)}, u32[]{:S(2)}, u32[]{:S(2)}) collective-permute-start(bf16[192,384]{1,0:T(8,128)(2,1)S(1)} %get-tuple-element.52.own_ref.refs_0_), channel_id=1, source_target_pairs={{0,2},{1,5},{2,0},{3,7},{4,6},{5,1},{6,4},{7,3},{8,10},{9,13},{10,... | collective-permute-start | bytes 442376 | tf_op jit(solution)/shard_map/ppermute | solution.py:445
  14.0 1.6 %collective-permute-start.7 = (bf16[96,128]{1,0:T(8,128)(2,1)S(1)}, bf16[96,128]{1,0:T(8,128)(2,1)S(1)}, u32[]{:S(2)}, u32[]{:S(2)}) collective-permute-start(bf16[96,128]{1,0:T(8,128)(2,1)S(1)} %get-tuple-element.53.refs_0_), channel_id=1, source_target_pairs={{0,7},{1,6},{2,5},{3,4},{4,3},{5,2},{6,1},{7,0},{8,15},{9,14},{10,... | collective-permute-start | bytes 73736 | tf_op jit(solution)/shard_map/ppermute | solution.py:436
  15.6 0.1 collective-permute-start.6
  15.7 1.6 %collective-permute-start.5 = (bf16[96,128]{1,0:T(8,128)(2,1)S(1)}, bf16[96,128]{1,0:T(8,128)(2,1)S(1)}, u32[]{:S(2)}, u32[]{:S(2)}) collective-permute-start(bf16[96,128]{1,0:T(8,128)(2,1)S(1)} %get-tuple-element.53.refs_0_), channel_id=1, source_target_pairs={{0,3},{1,2},{2,1},{3,0},{4,7},{5,6},{6,5},{7,4},{8,11},{9,10},{10,... | collective-permute-start | bytes 73736 | tf_op jit(solution)/shard_map/ppermute | solution.py:436
  17.4 0.3 collective-permute-done.3.came_ref.refs_1_
  17.7 1.8 %collective-permute-start.4 = (bf16[384,384]{1,0:T(8,128)(2,1)S(1)}, bf16[384,384]{1,0:T(8,128)(2,1)S(1)}, u32[]{:S(2)}, u32[]{:S(2)}) collective-permute-start(bf16[384,384]{1,0:T(8,128)(2,1)S(1)} %join.1), channel_id=1, source_target_pairs={{0,4},{1,3},{2,6},{3,1},{4,0},{5,7},{6,2},{7,5},{8,12},{9,11},{10,... | collective-permute-start | bytes 884744 | tf_op jit(solution)/shard_map/ppermute | solution.py:445
  19.6 0.0 collective-permute-done.7.refs_3_
  19.6 0.0 collective-permute-done.6.refs_2_
  19.6 0.0 collective-permute-done.5.refs_1_
  19.6 1.4 %collective-permute-done.8.refs_5_.refs_6_ = bf16[256,768]{1,0:T(8,128)(2,1)S(1)} collective-permute-done((bf16[256,768]{1,0:T(8,128)(2,1)S(1)}, bf16[256,768]{1,0:T(8,128)(2,1)S(1)}, u32[]{:S(2)}, u32[]{:S(2)}) %collective-permute-start.8) | collective-permute-done | bytes 393248 | tf_op jit(solution)/shard_map/ppermute | solution.py:436
  21.0 3.2 %conv_norm.1 = (bf16[256,768]{1,0:T(8,128)(2,1)S(1)}, f32[256,768]{1,0:T(8,128)S(1)}, f32[256,128]{1,0:T(8,128)S(1)}, f32[6,128,128]{2,1,0:T(8,128)S(1)}) custom-call(bf16[96,128]{1,0:T(8,128)(2,1)S(1)} %get-tuple-element.53.refs_0_, bf16[96,128]{1,0:T(8,128)(2,1)S(1)} %collective-permute-done.5.refs_1_, bf16[96,128]{1,0:T(8,128)(2,1)S(1)} %collective-permute-done.6.refs_2_, ...), custom_call_target="tpu_custom_call" | custom-call | flops 110000000 | bytes 2392064 | tf_op jit(solution)/shard_map/conv_norm/pallas_call | solution.py:403
  24.2 0.2 collective-permute-start.9
  24.3 0.4 collective-permute-start.11
  24.7 0.1 collective-permute-start.10
  24.9 0.0 collective-permute-done.4.refs_2_
  24.9 0.1 order.1.refs_0_.weight
  24.9 1.9 %collective-permute-done.10.refs_4_ = bf16[128,768]{1,0:T(8,128)(2,1)S(1)} collective-permute-done((bf16[128,768]{1,0:T(8,128)(2,1)S(1)}, bf16[128,768]{1,0:T(8,128)(2,1)S(1)}, u32[]{:S(2)}, u32[]{:S(2)}) %collective-permute-start.10) | collective-permute-done | bytes 196640 | tf_op jit(solution)/shard_map/ppermute | solution.py:448
  26.8 0.0 collective-permute-done.9.refs_2_
  26.8 0.0 collective-permute-done.11.refs_6_
  26.8 1.5 %project.1 = (f32[192,384]{1,0:T(8,128)S(1)}, bf16[192,384]{1,0:T(8,128)(2,1)S(1)}, bf16[192,384]{1,0:T(8,128)(2,1)S(1)}, bf16[192,384]{1,0:T(8,128)(2,1)S(1)}, bf16[512,384]{1,0:T(8,128)(2,1)S(1)}) custom-call(bf16[768,384]{1,0:T(8,128)(2,1)S(1)} %order.1.refs_0_.weight, bf16[256,768]{1,0:T(8,128)(2,1)S(1)} %get-tuple-element.58.refs_1_, ...), custom_call_target="tpu_custom_call" | custom-call | flops 1760000000 | bytes 3883008 | tf_op jit(solution)/shard_map/project/pallas_call | solution.py:403
  28.3 0.6 %back_project.1 = (f32[256,768]{1,0:T(8,128)S(1)}, f32[256,768]{1,0:T(8,128)S(1)}) custom-call(bf16[768,384]{1,0:T(8,128)(2,1)S(1)} %order.1.refs_0_.weight, bf16[512,384]{1,0:T(8,128)(2,1)S(1)} %get-tuple-element.65.gp_ref), custom_call_target="tpu_custom_call" | custom-call | flops 770000000 | bytes 2555904 | tf_op jit(solution)/shard_map/back_project/pallas_call | solution.py:403
  28.9 0.2 collective-permute-start.15
  29.1 1.5 %collective-permute-start.12 = (bf16[192,384]{1,0:T(8,128)(2,1)S(1)}, bf16[192,384]{1,0:T(8,128)(2,1)S(1)}, u32[]{:S(2)}, u32[]{:S(2)}) collective-permute-start(bf16[192,384]{1,0:T(8,128)(2,1)S(1)} %get-tuple-element.62), channel_id=1, source_target_pairs={{0,2},{2,0},{4,6},{6,4},{8,10},{10,8},{12,14},{14,12},{16,18},{18,... | collective-permute-start | bytes 442376 | tf_op jit(solution)/shard_map/ppermute | solution.py:430
  30.6 1.5 %collective-permute-start.13 = (bf16[192,384]{1,0:T(8,128)(2,1)S(1)}, bf16[192,384]{1,0:T(8,128)(2,1)S(1)}, u32[]{:S(2)}, u32[]{:S(2)}) collective-permute-start(bf16[192,384]{1,0:T(8,128)(2,1)S(1)} %get-tuple-element.63), channel_id=1, source_target_pairs={{0,4},{2,6},{4,0},{6,2},{8,12},{10,14},{12,8},{14,10},{16,20},{18,... | collective-permute-start | bytes 442376 | tf_op jit(solution)/shard_map/ppermute | solution.py:430
  32.2 0.5 collective-permute-start.14
  32.6 0.0 collective-permute-done.15.refs_1_
  32.6 3.2 %norm_back.1 = (f32[96,128]{1,0:T(8,128)S(1)}, bf16[96,128]{1,0:T(8,128)(2,1)S(1)}, bf16[96,128]{1,0:T(8,128)(2,1)S(1)}, bf16[96,128]{1,0:T(8,128)(2,1)S(1)}, f3...) custom-call(f32[256,768]{1,0:T(8,128)S(1)} %get-tuple-element.66.refs_0_, ...), custom_call_target="tpu_custom_call" | custom-call | flops 110000000 | bytes 4186112 | tf_op jit(solution)/shard_map/norm_back/pallas_call | solution.py:403
  35.8 0.7 %collective-permute-start.16 = (bf16[96,128]{1,0:T(8,128)(2,1)S(1)}, bf16[96,128]{1,0:T(8,128)(2,1)S(1)}, u32[]{:S(2)}, u32[]{:S(2)}) collective-permute-start(bf16[96,128]{1,0:T(8,128)(2,1)S(1)} %get-tuple-element.72), channel_id=1, source_target_pairs={{0,3},{1,2},{2,1},{3,0},{4,7},{5,6},{6,5},{7,4},{8,11},{9,10},{10,... | collective-permute-start | bytes 73736 | tf_op jit(solution)/shard_map/ppermute | solution.py:436
  36.5 2.1 %collective-permute-start.17 = (bf16[96,128]{1,0:T(8,128)(2,1)S(1)}, bf16[96,128]{1,0:T(8,128)(2,1)S(1)}, u32[]{:S(2)}, u32[]{:S(2)}) collective-permute-start(bf16[96,128]{1,0:T(8,128)(2,1)S(1)} %get-tuple-element.73), channel_id=1, source_target_pairs={{0,5},{1,4},{2,7},{3,6},{4,1},{5,0},{6,3},{7,2},{8,13},{9,12},{10,... | collective-permute-start | bytes 73736 | tf_op jit(solution)/shard_map/ppermute | solution.py:436
  38.6 0.0 collective-permute-done.12.refs_1_
  38.6 0.0 collective-permute-start.18
  38.7 1.0 %collective-permute-done.13.refs_2_ = bf16[192,384]{1,0:T(8,128)(2,1)S(1)} collective-permute-done((bf16[192,384]{1,0:T(8,128)(2,1)S(1)}, bf16[192,384]{1,0:T(8,128)(2,1)S(1)}, u32[]{:S(2)}, u32[]{:S(2)}) %collective-permute-start.13) | collective-permute-done | bytes 147488 | tf_op jit(solution)/shard_map/ppermute | solution.py:430
  39.6 0.0 collective-permute-start.19
  39.6 0.0 collective-permute-done.14.refs_3_
  39.6 0.0 collective-permute-done.16.refs_5_
  39.7 0.5 collective-permute-done.17.refs_6_
  40.2 2.6 %collective-permute-done.18.refs_7_ = bf16[96,128]{1,0:T(8,128)(2,1)S(1)} collective-permute-done((bf16[96,128]{1,0:T(8,128)(2,1)S(1)}, bf16[96,128]{1,0:T(8,128)(2,1)S(1)}, u32[]{:S(2)}, u32[]{:S(2)}) %collective-permute-start.18) | collective-permute-done | bytes 24608 | tf_op jit(solution)/shard_map/ppermute | solution.py:436
  42.8 0.1 plane_sum.1
  42.9 0.1 collective-permute-start.20
  43.0 3.4 %collective-permute-start.21 = (bf16[48,512]{1,0:T(8,128)(2,1)S(1)}, bf16[48,512]{1,0:T(8,128)(2,1)S(1)}, u32[]{:S(2)}, u32[]{:S(2)}) collective-permute-start(bf16[48,512]{1,0:T(8,128)(2,1)S(1)} %get-tuple-element.81), channel_id=1, source_target_pairs={{0,17},{1,16},{2,19},{3,18},{4,21},{5,20},{6,23},{7,22},{8,25},{9,... | collective-permute-start | bytes 147464 | tf_op jit(solution)/shard_map/ppermute | solution.py:436
  46.3 0.0 collective-permute-start.22
  46.3 0.5 collective-permute-done.19.other_ref
  46.8 1.9 %conv_back.1 = bf16[1,8,16,768]{3,2,1,0:T(8,128)(2,1)} custom-call(f32[6,8,16,128]{3,2,1,0:T(8,128)S(1)} %get-tuple-element.76.grad_ref, bf16[6,8,16,128]{3,2,1,0:T(8,128)(2,1)S(1)} %collective-permute-done.19.other_ref, f32[6,128,128]{2,1,0:T(8,128)S(1)} %get-tuple-element.70.refs_4_.taps_ref), custom_call_target="tpu_custom_call" | custom-call | flops 110000000 | bytes 1179648 | tf_op jit(solution)/shard_map/conv_back/pallas_call | solution.py:403
  48.8 0.0 collective-permute-done.20.refs_1_
  48.8 0.1 collective-permute-done.21.refs_2_
  48.9 3.0 %collective-permute-done.22.refs_3_ = bf16[48,512]{1,0:T(8,128)(2,1)S(1)} collective-permute-done((bf16[48,512]{1,0:T(8,128)(2,1)S(1)}, bf16[48,512]{1,0:T(8,128)(2,1)S(1)}, u32[]{:S(2)}, u32[]{:S(2)}) %collective-permute-start.22) | collective-permute-done | bytes 49184 | tf_op jit(solution)/shard_map/ppermute | solution.py:436
  51.9 0.1 collective-permute-start.23
  52.0 1.5 %collective-permute-done.23.other_ref = f32[48,1280]{1,0:T(8,128)S(1)} collective-permute-done((f32[48,1280]{1,0:T(8,128)S(1)}, f32[48,1280]{1,0:T(8,128)S(1)}, u32[]{:S(2)}, u32[]{:S(2)}) %collective-permute-start.23) | collective-permute-done | bytes 245792 | tf_op jit(solution)/shard_map/ppermute | solution.py:448
  53.5 0.8 %finish.1 = (f32[48,1536]{1,0:T(8,128)}, f32[48,49]{1,0:T(8,128)}, f32[1,48]{1,0:T(1,128)}, f32[1,48]{1,0:T(1,128)}) custom-call(f32[48,1280]{1,0:T(8,128)S(1)} %line_sum.1.mine_ref, f32[48,1280]{1,0:T(8,128)S(1)} %collective-permute-done.23.other_ref), custom_call_target="tpu_custom_call" | custom-call | flops 550000000 | bytes 796224 | tf_op jit(solution)/shard_map/finish/pallas_call | solution.py:403
  (3 shorter events, 0.1 us)
Async XLA Ops:
  0.6 7.1 %copy-start = (bf16[1,8,16,768]{3,2,1,0:T(8,128)(2,1)S(1)}, bf16[1,8,16,768]{3,2,1,0:T(8,128)(2,1)}, u32[]{:S(2)}) copy-start(bf16[1,8,16,768]{3,2,1,0:T(8,128)(2,1)} %param.6) | copy-start | bytes 589828
  0.6 7.1 %copy-start.1 = (bf16[1,8,16,1536]{3,2,1,0:T(8,128)(2,1)S(1)}, bf16[1,8,16,1536]{3,2,1,0:T(8,128)(2,1)}, u32[]{:S(2)}) copy-start(bf16[1,8,16,1536]{3,2,1,0:T(8,128)(2,1)} %param.7) | copy-start | bytes 1179652
  2.4 10.0 %copy-start.2 = (bf16[48,512]{1,0:T(8,128)(2,1)S(1)}, bf16[48,512]{1,0:T(8,128)(2,1)}, u32[]{:S(2)}) copy-start(bf16[48,512]{1,0:T(8,128)(2,1)} %get-tuple-element.49.refs_0_) | copy-start | bytes 147460
  2.4 7.0 %collective-permute-start.1 = (bf16[48,512]{1,0:T(8,128)(2,1)}, bf16[48,512]{1,0:T(8,128)(2,1)S(1)}, u32[]{:S(2)}, u32[]{:S(2)}) collective-permute-start(bf16[48,512]{1,0:T(8,128)(2,1)} %get-tuple-element.51), channel_id=1, source_target_pairs={{0,17},{1,16},{2,19},{3,18},{4,21},{5,20},{6,23},{7,22},{8,25},{9,... | collective-permute-start | bytes 147464 | tf_op jit(solution)/shard_map/ppermute | solution.py:436
  5.9 5.6 %collective-permute-start.2 = (bf16[48,512]{1,0:T(8,128)(2,1)}, bf16[48,512]{1,0:T(8,128)(2,1)S(1)}, u32[]{:S(2)}, u32[]{:S(2)}) collective-permute-start(bf16[48,512]{1,0:T(8,128)(2,1)} %get-tuple-element.50), channel_id=1, source_target_pairs={{0,25},{1,24},{2,27},{3,26},{4,29},{5,28},{6,31},{7,30},{8,17},{9,... | collective-permute-start | bytes 147464 | tf_op jit(solution)/shard_map/ppermute | solution.py:436
  7.5 4.9 %collective-permute-start = (bf16[48,512]{1,0:T(8,128)(2,1)}, bf16[48,512]{1,0:T(8,128)(2,1)S(1)}, u32[]{:S(2)}, u32[]{:S(2)}) collective-permute-start(bf16[48,512]{1,0:T(8,128)(2,1)} %get-tuple-element.50), channel_id=1, source_target_pairs={{0,9},{1,8},{2,11},{3,10},{4,13},{5,12},{6,15},{7,14},{8,1},{9,0},... | collective-permute-start | bytes 147464 | tf_op jit(solution)/shard_map/ppermute | solution.py:436
  7.8 13.2 %collective-permute-start.8 = (bf16[256,768]{1,0:T(8,128)(2,1)S(1)}, bf16[256,768]{1,0:T(8,128)(2,1)S(1)}, u32[]{:S(2)}, u32[]{:S(2)}) collective-permute-start(bf16[256,768]{1,0:T(8,128)(2,1)S(1)} %get-tuple-element.56), channel_id=1, source_target_pairs={{0,9},{1,8},{2,11},{3,10},{4,13},{5,12},{6,15},{7,14},{8,1},{9,0},... | collective-permute-start | bytes 1179656 | tf_op jit(solution)/shard_map/ppermute | solution.py:436
  12.5 5.2 %collective-permute-start.3 = (bf16[192,384]{1,0:T(8,128)(2,1)S(1)}, bf16[192,384]{1,0:T(8,128)(2,1)S(1)}, u32[]{:S(2)}, u32[]{:S(2)}) collective-permute-start(bf16[192,384]{1,0:T(8,128)(2,1)S(1)} %get-tuple-element.52.own_ref.refs_0_), channel_id=1, source_target_pairs={{0,2},{1,5},{2,0},{3,7},{4,6},{5,1},{6,4},{7,3},{8,10},{9,13},{10,... | collective-permute-start | bytes 442376 | tf_op jit(solution)/shard_map/ppermute | solution.py:445
  14.0 5.5 %collective-permute-start.7 = (bf16[96,128]{1,0:T(8,128)(2,1)S(1)}, bf16[96,128]{1,0:T(8,128)(2,1)S(1)}, u32[]{:S(2)}, u32[]{:S(2)}) collective-permute-start(bf16[96,128]{1,0:T(8,128)(2,1)S(1)} %get-tuple-element.53.refs_0_), channel_id=1, source_target_pairs={{0,7},{1,6},{2,5},{3,4},{4,3},{5,2},{6,1},{7,0},{8,15},{9,14},{10,... | collective-permute-start | bytes 73736 | tf_op jit(solution)/shard_map/ppermute | solution.py:436
  15.6 4.0 %collective-permute-start.6 = (bf16[96,128]{1,0:T(8,128)(2,1)S(1)}, bf16[96,128]{1,0:T(8,128)(2,1)S(1)}, u32[]{:S(2)}, u32[]{:S(2)}) collective-permute-start(bf16[96,128]{1,0:T(8,128)(2,1)S(1)} %get-tuple-element.53.refs_0_), channel_id=1, source_target_pairs={{0,5},{1,4},{2,7},{3,6},{4,1},{5,0},{6,3},{7,2},{8,13},{9,12},{10,... | collective-permute-start | bytes 73736 | tf_op jit(solution)/shard_map/ppermute | solution.py:436
  15.7 3.8 %collective-permute-start.5 = (bf16[96,128]{1,0:T(8,128)(2,1)S(1)}, bf16[96,128]{1,0:T(8,128)(2,1)S(1)}, u32[]{:S(2)}, u32[]{:S(2)}) collective-permute-start(bf16[96,128]{1,0:T(8,128)(2,1)S(1)} %get-tuple-element.53.refs_0_), channel_id=1, source_target_pairs={{0,3},{1,2},{2,1},{3,0},{4,7},{5,6},{6,5},{7,4},{8,11},{9,10},{10,... | collective-permute-start | bytes 73736 | tf_op jit(solution)/shard_map/ppermute | solution.py:436
  17.7 7.2 %collective-permute-start.4 = (bf16[384,384]{1,0:T(8,128)(2,1)S(1)}, bf16[384,384]{1,0:T(8,128)(2,1)S(1)}, u32[]{:S(2)}, u32[]{:S(2)}) collective-permute-start(bf16[384,384]{1,0:T(8,128)(2,1)S(1)} %join.1), channel_id=1, source_target_pairs={{0,4},{1,3},{2,6},{3,1},{4,0},{5,7},{6,2},{7,5},{8,12},{9,11},{10,... | collective-permute-start | bytes 884744 | tf_op jit(solution)/shard_map/ppermute | solution.py:445
  24.2 2.6 %collective-permute-start.9 = (bf16[256,768]{1,0:T(8,128)(2,1)S(1)}, bf16[256,768]{1,0:T(8,128)(2,1)S(1)}, u32[]{:S(2)}, u32[]{:S(2)}) collective-permute-start(bf16[256,768]{1,0:T(8,128)(2,1)S(1)} %get-tuple-element.58.refs_1_), channel_id=1, source_target_pairs={{0,1},{1,0},{2,3},{3,2},{4,5},{5,4},{6,7},{7,6},{8,9},{9,8},{10,11... | collective-permute-start | bytes 1179656 | tf_op jit(solution)/shard_map/ppermute | solution.py:448
  24.3 2.5 %collective-permute-start.11 = (bf16[256,768]{1,0:T(8,128)(2,1)S(1)}, bf16[256,768]{1,0:T(8,128)(2,1)S(1)}, u32[]{:S(2)}, u32[]{:S(2)}) collective-permute-start(bf16[256,768]{1,0:T(8,128)(2,1)S(1)} %collective-permute-done.8.refs_5_.refs_6_), channel_id=1, source_target_pairs={{0,1},{1,0},{2,3},{3,2},{4,5},{5,4},{6,7},{7,6},{8,9},{9,8},{10,11... | collective-permute-start | bytes 1179656 | tf_op jit(solution)/shard_map/ppermute | solution.py:448
  24.7 2.1 %collective-permute-start.10 = (bf16[128,768]{1,0:T(8,128)(2,1)S(1)}, bf16[128,768]{1,0:T(8,128)(2,1)S(1)}, u32[]{:S(2)}, u32[]{:S(2)}) collective-permute-start(bf16[128,768]{1,0:T(8,128)(2,1)S(1)} %get-tuple-element.59), channel_id=1, source_target_pairs={{0,1},{1,0},{2,3},{3,2},{4,5},{5,4},{6,7},{7,6},{8,9},{9,8},{10,11... | collective-permute-start | bytes 589832 | tf_op jit(solution)/shard_map/ppermute | solution.py:448
  28.9 3.7 %collective-permute-start.15 = (f32[256,768]{1,0:T(8,128)S(1)}, f32[256,768]{1,0:T(8,128)S(1)}, u32[]{:S(2)}, u32[]{:S(2)}) collective-permute-start(f32[256,768]{1,0:T(8,128)S(1)} %get-tuple-element.67), channel_id=1, source_target_pairs={{0,1},{1,0},{2,3},{3,2},{4,5},{5,4},{6,7},{7,6},{8,9},{9,8},{10,11... | collective-permute-start | bytes 2359304 | tf_op jit(solution)/shard_map/ppermute | solution.py:448
  29.1 9.5 %collective-permute-start.12 = (bf16[192,384]{1,0:T(8,128)(2,1)S(1)}, bf16[192,384]{1,0:T(8,128)(2,1)S(1)}, u32[]{:S(2)}, u32[]{:S(2)}) collective-permute-start(bf16[192,384]{1,0:T(8,128)(2,1)S(1)} %get-tuple-element.62), channel_id=1, source_target_pairs={{0,2},{2,0},{4,6},{6,4},{8,10},{10,8},{12,14},{14,12},{16,18},{18,... | collective-permute-start | bytes 442376 | tf_op jit(solution)/shard_map/ppermute | solution.py:430
  30.6 9.0 %collective-permute-start.13 = (bf16[192,384]{1,0:T(8,128)(2,1)S(1)}, bf16[192,384]{1,0:T(8,128)(2,1)S(1)}, u32[]{:S(2)}, u32[]{:S(2)}) collective-permute-start(bf16[192,384]{1,0:T(8,128)(2,1)S(1)} %get-tuple-element.63), channel_id=1, source_target_pairs={{0,4},{2,6},{4,0},{6,2},{8,12},{10,14},{12,8},{14,10},{16,20},{18,... | collective-permute-start | bytes 442376 | tf_op jit(solution)/shard_map/ppermute | solution.py:430
  32.2 7.5 %collective-permute-start.14 = (bf16[192,384]{1,0:T(8,128)(2,1)S(1)}, bf16[192,384]{1,0:T(8,128)(2,1)S(1)}, u32[]{:S(2)}, u32[]{:S(2)}) collective-permute-start(bf16[192,384]{1,0:T(8,128)(2,1)S(1)} %get-tuple-element.64), channel_id=1, source_target_pairs={{0,6},{2,4},{4,2},{6,0},{8,14},{10,12},{12,10},{14,8},{16,22},{18,... | collective-permute-start | bytes 442376 | tf_op jit(solution)/shard_map/ppermute | solution.py:430
  35.8 3.8 %collective-permute-start.16 = (bf16[96,128]{1,0:T(8,128)(2,1)S(1)}, bf16[96,128]{1,0:T(8,128)(2,1)S(1)}, u32[]{:S(2)}, u32[]{:S(2)}) collective-permute-start(bf16[96,128]{1,0:T(8,128)(2,1)S(1)} %get-tuple-element.72), channel_id=1, source_target_pairs={{0,3},{1,2},{2,1},{3,0},{4,7},{5,6},{6,5},{7,4},{8,11},{9,10},{10,... | collective-permute-start | bytes 73736 | tf_op jit(solution)/shard_map/ppermute | solution.py:436
  36.5 3.6 %collective-permute-start.17 = (bf16[96,128]{1,0:T(8,128)(2,1)S(1)}, bf16[96,128]{1,0:T(8,128)(2,1)S(1)}, u32[]{:S(2)}, u32[]{:S(2)}) collective-permute-start(bf16[96,128]{1,0:T(8,128)(2,1)S(1)} %get-tuple-element.73), channel_id=1, source_target_pairs={{0,5},{1,4},{2,7},{3,6},{4,1},{5,0},{6,3},{7,2},{8,13},{9,12},{10,... | collective-permute-start | bytes 73736 | tf_op jit(solution)/shard_map/ppermute | solution.py:436
  38.6 4.2 %collective-permute-start.18 = (bf16[96,128]{1,0:T(8,128)(2,1)S(1)}, bf16[96,128]{1,0:T(8,128)(2,1)S(1)}, u32[]{:S(2)}, u32[]{:S(2)}) collective-permute-start(bf16[96,128]{1,0:T(8,128)(2,1)S(1)} %get-tuple-element.74), channel_id=1, source_target_pairs={{0,7},{1,6},{2,5},{3,4},{4,3},{5,2},{6,1},{7,0},{8,15},{9,14},{10,... | collective-permute-start | bytes 73736 | tf_op jit(solution)/shard_map/ppermute | solution.py:436
  39.6 7.2 %collective-permute-start.19 = (bf16[6,8,16,128]{3,2,1,0:T(8,128)(2,1)S(1)}, bf16[6,8,16,128]{3,2,1,0:T(8,128)(2,1)S(1)}, u32[]{:S(2)}, u32[]{:S(2)}) collective-permute-start(bf16[6,8,16,128]{3,2,1,0:T(8,128)(2,1)S(1)} %get-tuple-element.77), channel_id=1, source_target_pairs={{0,9},{1,8},{2,11},{3,10},{4,13},{5,12},{6,15},{7,14},{8,1},{9,0},... | collective-permute-start | bytes 589832 | tf_op jit(solution)/shard_map/ppermute | solution.py:436
  42.9 5.9 %collective-permute-start.20 = (bf16[48,512]{1,0:T(8,128)(2,1)S(1)}, bf16[48,512]{1,0:T(8,128)(2,1)S(1)}, u32[]{:S(2)}, u32[]{:S(2)}) collective-permute-start(bf16[48,512]{1,0:T(8,128)(2,1)S(1)} %get-tuple-element.80), channel_id=1, source_target_pairs={{0,9},{1,8},{2,11},{3,10},{4,13},{5,12},{6,15},{7,14},{8,1},{9,0},... | collective-permute-start | bytes 147464 | tf_op jit(solution)/shard_map/ppermute | solution.py:436
  43.0 5.9 %collective-permute-start.21 = (bf16[48,512]{1,0:T(8,128)(2,1)S(1)}, bf16[48,512]{1,0:T(8,128)(2,1)S(1)}, u32[]{:S(2)}, u32[]{:S(2)}) collective-permute-start(bf16[48,512]{1,0:T(8,128)(2,1)S(1)} %get-tuple-element.81), channel_id=1, source_target_pairs={{0,17},{1,16},{2,19},{3,18},{4,21},{5,20},{6,23},{7,22},{8,25},{9,... | collective-permute-start | bytes 147464 | tf_op jit(solution)/shard_map/ppermute | solution.py:436
  46.3 5.5 %collective-permute-start.22 = (bf16[48,512]{1,0:T(8,128)(2,1)S(1)}, bf16[48,512]{1,0:T(8,128)(2,1)S(1)}, u32[]{:S(2)}, u32[]{:S(2)}) collective-permute-start(bf16[48,512]{1,0:T(8,128)(2,1)S(1)} %get-tuple-element.82), channel_id=1, source_target_pairs={{0,25},{1,24},{2,27},{3,26},{4,29},{5,28},{6,31},{7,30},{8,17},{9,... | collective-permute-start | bytes 147464 | tf_op jit(solution)/shard_map/ppermute | solution.py:436
  51.9 1.6 %collective-permute-start.23 = (f32[48,1280]{1,0:T(8,128)S(1)}, f32[48,1280]{1,0:T(8,128)S(1)}, u32[]{:S(2)}, u32[]{:S(2)}) collective-permute-start(f32[48,1280]{1,0:T(8,128)S(1)} %line_sum.1.mine_ref), channel_id=1, source_target_pairs={{0,1},{1,0},{2,3},{3,2},{4,5},{5,4},{6,7},{7,6},{8,9},{9,8},{10,11... | collective-permute-start | bytes 737288 | tf_op jit(solution)/shard_map/ppermute | solution.py:448

commit v15 on v14

--- a/solution.py
+++ b/solution.py
@@ -174,9 +174,13 @@
     small = refs[:INNER]
     sources = refs[INNER : INNER + 2]
     x_ref = sources[0]
-    normed_ref, white_ref, inv_ref, taps_ref, gathered, unfolded, padded, conv = refs[INNER + 2 :]
+    normed_ref, white_ref, inv_ref, taps_ref, corner_ref, *scratch = refs[INNER + 2 :]
+    gathered, unfolded, padded, conv = scratch
     pixels, depth = x_ref.shape
     tiles = depth // LANES
+    quarter = corner_ref.shape[1]
+    start = pl.multiple_of((1 - lax.axis_index("rep") % 2) * quarter, LANES)
+    corner_ref[...] = sources[1][pixels:, pl.ds(start, quarter)]
     if relative:
         for group, piece in enumerate(small):
             unfolded[group * 2 * piece.shape[0] : (group + 1) * 2 * piece.shape[0], :] = unfold(
@@ -285,8 +289,7 @@
     cot[pixels : 2 * pixels, :] = across_ref[pixels:, pl.ds(start, quarter)]
     start = pl.multiple_of(parity * quarter, LANES)
     cot[2 * pixels : 3 * pixels, :] = sibling_ref[:, pl.ds(start, quarter)]
-    start = pl.multiple_of(side * quarter, LANES)
-    cot[3 * pixels :, :] = corner_ref[pixels:, pl.ds(start, quarter)]
+    cot[3 * pixels :, :] = corner_ref[...]
     for start in range(0, quarter, LANES):
         columns = slice(start, start + LANES)
         pre_act = jnp.dot(normed[...], weight[:, columns], preferred_element_type=F32)
@@ -535,7 +538,7 @@
     )
 
     padded = pltpu.VMEM((tiles, height, breadth + 16, LANES), F32)
-    normed, whitened, inv_std, taps = call(
+    normed, whitened, inv_std, taps, corner = call(
         functools.partial(conv_norm_kernel, relative, own, height, breadth),
         "conv_norm",
         [
@@ -543,6 +546,7 @@
             shape((2 * pixels, depth), F32),
             shape((2 * pixels, LANES), F32),
             shape((tiles, LANES, LANES), F32),
+            shape((pixels, quarter), BF16),
         ],
         [
             pltpu.VMEM((depth, LANES), F32),
@@ -555,8 +559,8 @@
         image,
         across,
     )
-    normed, across = lax.optimization_barrier((normed, across))
-    normed_sibling, corner = over_core(normed), over_core(across)
+    normed, cot_sibling = lax.optimization_barrier((normed, cot_sibling))
+    normed_sibling, corner = over_core(normed), over_core(corner)
     *pieces, grad_pre = call(
         functools.partial(project_kernel, relative, own),
         "project",
@@ -632,7 +636,7 @@
         "plane_sum",
         [shape((own, quarter + LANES), F32)] + [shape((own, quarter + LANES), BF16)] * (lines - 1),
         [],
-        2.0,
+        0.8,
         pieces[0],
         *arrived,
         small[0],

time: 54.4 us -> 54.1 us (level)
    ppermute x2, waiting for transfers between devices: 0.3 us -> 2.98 us  [hop(): return lax.ppermute(array, ('shard', 'rep'), pairs)]
    ppermute x5, waiting for transfers between devices: 3.37 us -> 1.37 us  [over_core(): return lax.ppermute(array, 'rep', [(i, i ^ 1) for i in range(reps)])]
    ppermute x14, waiting for transfers between devices: 11.1 us -> 10.1 us  [crossing(): return lax.ppermute(array, ('shard', 'rep'), pairs)]
where the time goes in v15:
time: 54.1 us; the launch traced here: 54 us
  starting transfers between devices  24.4 us (45%)
  waiting for transfers between devices  15.6 us (29%)
  Pallas kernels  13.3 us (25%)
  between operations  0.76 us (1%)
    ppermute x14, starting transfers between devices, crossing(): return lax.ppermute(array, ('shard', 'rep'), pairs)  16.3 us
    pallas_call x13, Pallas kernels, call(): pl.pallas_call(kernel, out_shape=outs, in_specs=[VMEM] * len(args), out_s...  13.3 us
    ppermute x14, waiting for transfers between devices, crossing(): return lax.ppermute(array, ('shard', 'rep'), pairs)  10.1 us
    ppermute x3, starting transfers between devices, over_shard(): return lax.ppermute(array, 'shard', [(i, i ^ flip) for i in range(shards)])  3.5 us
    ppermute x2, starting transfers between devices, hop(): return lax.ppermute(array, ('shard', 'rep'), pairs)  3.14 us
    ppermute x2, waiting for transfers between devices, hop(): return lax.ppermute(array, ('shard', 'rep'), pairs)  2.98 us
    ppermute x5, starting transfers between devices, over_core(): return lax.ppermute(array, 'rep', [(i, i ^ 1) for i in range(reps)])  1.48 us
    ppermute x5, waiting for transfers between devices, over_core(): return lax.ppermute(array, 'rep', [(i, i ^ 1) for i in range(reps)])  1.37 us
  transfers between devices with their start and end apart: 24, of which 12 were waited for; matrix products, arithmetic and copies ran while one was open for 0% of the time, Pallas kernels for 16%

profile of v15, /device:TPU:0, one launch (start us, length us, event | category | flops | bytes accessed | tf_op | source)
XLA Modules:
  0.0 54.0 jit_solution(12013449256234306178)
XLA Ops:
  0.6 0.0 copy-start
  0.6 0.0 copy-start.1
  0.7 1.7 %pack.1 = (bf16[48,512]{1,0:T(8,128)(2,1)}, bf16[48,512]{1,0:T(8,128)(2,1)}, bf16[48,512]{1,0:T(8,128)(2,1)}) custom-call(bf16[48,1536]{1,0:T(8,128)(2,1)} %w_ref.1, bf16[48,49]{1,0:T(8,128)(2,1)} %dw_ref.1, bf16[1,48]{1,0:T(2,128)(2,1)} %bitcast.11, bf16[1,48]{1,0:T(2,128)(2,1)} %bitcast.12), custom_call_target="tpu_custom_call" | custom-call | flops 550000000 | bytes 299808 | tf_op jit(solution)/shard_map/pack/pallas_call | solution.py:406
  2.4 0.0 copy-start.2
  2.4 3.5 %collective-permute-start.1 = (bf16[48,512]{1,0:T(8,128)(2,1)}, bf16[48,512]{1,0:T(8,128)(2,1)S(1)}, u32[]{:S(2)}, u32[]{:S(2)}) collective-permute-start(bf16[48,512]{1,0:T(8,128)(2,1)} %get-tuple-element.52), channel_id=1, source_target_pairs={{0,17},{1,16},{2,19},{3,18},{4,21},{5,20},{6,23},{7,22},{8,25},{9,... | collective-permute-start | bytes 147464 | tf_op jit(solution)/shard_map/ppermute | solution.py:439
  5.9 1.6 %collective-permute-start.2 = (bf16[48,512]{1,0:T(8,128)(2,1)}, bf16[48,512]{1,0:T(8,128)(2,1)S(1)}, u32[]{:S(2)}, u32[]{:S(2)}) collective-permute-start(bf16[48,512]{1,0:T(8,128)(2,1)} %get-tuple-element.51), channel_id=1, source_target_pairs={{0,25},{1,24},{2,27},{3,26},{4,29},{5,28},{6,31},{7,30},{8,17},{9,... | collective-permute-start | bytes 147464 | tf_op jit(solution)/shard_map/ppermute | solution.py:439
  7.5 0.2 collective-permute-start
  7.7 0.0 copy-done
  7.7 0.0 copy-done.1
  7.8 0.1 collective-permute-start.9
  7.9 1.7 %collective-permute-start.8 = (bf16[256,768]{1,0:T(8,128)(2,1)S(1)}, bf16[256,768]{1,0:T(8,128)(2,1)S(1)}, u32[]{:S(2)}, u32[]{:S(2)}) collective-permute-start(bf16[256,768]{1,0:T(8,128)(2,1)S(1)} %get-tuple-element.57), channel_id=1, source_target_pairs={{0,9},{1,8},{2,11},{3,10},{4,13},{5,12},{6,15},{7,14},{8,1},{9,0},... | collective-permute-start | bytes 1179656 | tf_op jit(solution)/shard_map/ppermute | solution.py:439
  9.5 0.0 collective-permute-done.1.refs_2_
  9.5 2.0 %collective-permute-done.2.refs_3_ = bf16[48,512]{1,0:T(8,128)(2,1)S(1)} collective-permute-done((bf16[48,512]{1,0:T(8,128)(2,1)}, bf16[48,512]{1,0:T(8,128)(2,1)S(1)}, u32[]{:S(2)}, u32[]{:S(2)}) %collective-permute-start.2) | collective-permute-done | bytes 49184 | tf_op jit(solution)/shard_map/ppermute | solution.py:439
  11.5 0.9 %collective-permute-done.refs_1_ = bf16[48,512]{1,0:T(8,128)(2,1)S(1)} collective-permute-done((bf16[48,512]{1,0:T(8,128)(2,1)}, bf16[48,512]{1,0:T(8,128)(2,1)S(1)}, u32[]{:S(2)}, u32[]{:S(2)}) %collective-permute-start) | collective-permute-done | bytes 49184 | tf_op jit(solution)/shard_map/ppermute | solution.py:439
  12.4 0.0 copy-done.2
  12.4 0.1 assemble.1
  12.5 1.6 %collective-permute-start.3 = (bf16[192,384]{1,0:T(8,128)(2,1)S(1)}, bf16[192,384]{1,0:T(8,128)(2,1)S(1)}, u32[]{:S(2)}, u32[]{:S(2)}) collective-permute-start(bf16[192,384]{1,0:T(8,128)(2,1)S(1)} %get-tuple-element.53.own_ref.refs_0_), channel_id=1, source_target_pairs={{0,2},{1,5},{2,0},{3,7},{4,6},{5,1},{6,4},{7,3},{8,10},{9,13},{10,... | collective-permute-start | bytes 442376 | tf_op jit(solution)/shard_map/ppermute | solution.py:448
  14.0 1.6 %collective-permute-start.7 = (bf16[96,128]{1,0:T(8,128)(2,1)S(1)}, bf16[96,128]{1,0:T(8,128)(2,1)S(1)}, u32[]{:S(2)}, u32[]{:S(2)}) collective-permute-start(bf16[96,128]{1,0:T(8,128)(2,1)S(1)} %get-tuple-element.54.refs_0_), channel_id=1, source_target_pairs={{0,7},{1,6},{2,5},{3,4},{4,3},{5,2},{6,1},{7,0},{8,15},{9,14},{10,... | collective-permute-start | bytes 73736 | tf_op jit(solution)/shard_map/ppermute | solution.py:439
  15.6 0.1 collective-permute-start.6
  15.7 1.9 %collective-permute-done.3.came_ref.refs_1_ = bf16[192,384]{1,0:T(8,128)(2,1)S(1)} collective-permute-done((bf16[192,384]{1,0:T(8,128)(2,1)S(1)}, bf16[192,384]{1,0:T(8,128)(2,1)S(1)}, u32[]{:S(2)}, u32[]{:S(2)}) %collective-permute-start.3) | collective-permute-done | bytes 147488 | tf_op jit(solution)/shard_map/ppermute | solution.py:448
  17.7 1.3 %collective-permute-start.5 = (bf16[96,128]{1,0:T(8,128)(2,1)S(1)}, bf16[96,128]{1,0:T(8,128)(2,1)S(1)}, u32[]{:S(2)}, u32[]{:S(2)}) collective-permute-start(bf16[96,128]{1,0:T(8,128)(2,1)S(1)} %get-tuple-element.54.refs_0_), channel_id=1, source_target_pairs={{0,3},{1,2},{2,1},{3,0},{4,7},{5,6},{6,5},{7,4},{8,11},{9,10},{10,... | collective-permute-start | bytes 73736 | tf_op jit(solution)/shard_map/ppermute | solution.py:439
  19.0 0.0 collective-permute-done.7.refs_3_
  19.0 1.6 %collective-permute-start.4 = (bf16[384,384]{1,0:T(8,128)(2,1)S(1)}, bf16[384,384]{1,0:T(8,128)(2,1)S(1)}, u32[]{:S(2)}, u32[]{:S(2)}) collective-permute-start(bf16[384,384]{1,0:T(8,128)(2,1)S(1)} %join.1), channel_id=1, source_target_pairs={{0,4},{1,3},{2,6},{3,1},{4,0},{5,7},{6,2},{7,5},{8,12},{9,11},{10,... | collective-permute-start | bytes 884744 | tf_op jit(solution)/shard_map/ppermute | solution.py:448
  20.6 0.0 collective-permute-done.6.refs_2_
  20.6 0.3 collective-permute-done.5.refs_1_
  20.9 0.0 collective-permute-done.8.refs_5_.refs_6_
  21.0 3.2 %conv_norm.1 = (bf16[256,768]{1,0:T(8,128)(2,1)S(1)}, f32[256,768]{1,0:T(8,128)S(1)}, f32[256,128]{1,0:T(8,128)S(1)}, f32[6,128,128]{2,1,0:T(8,128)S(1)}, bf16[128,384]{1,0:T(8,128)(2,1)S(1)}) custom-call(bf16[96,128]{1,0:T(8,128)(2,1)S(1)} %get-tuple-element.54.refs_0_, bf16[96,128]{1,0:T(8,128)(2,1)S(1)} %collective-permute-done.5.refs_1_, ...), custom_call_target="tpu_custom_call" | custom-call | flops 110000000 | bytes 2490368 | tf_op jit(solution)/shard_map/conv_norm/pallas_call | solution.py:406
  24.2 0.0 collective-permute-done.9.refs_4_
  24.2 0.2 collective-permute-start.10
  24.4 0.4 collective-permute-start.11
  24.8 1.0 %collective-permute-done.4.refs_2_ = bf16[384,384]{1,0:T(8,128)(2,1)S(1)} collective-permute-done((bf16[384,384]{1,0:T(8,128)(2,1)S(1)}, bf16[384,384]{1,0:T(8,128)(2,1)S(1)}, u32[]{:S(2)}, u32[]{:S(2)}) %collective-permute-start.4) | collective-permute-done | bytes 294944 | tf_op jit(solution)/shard_map/ppermute | solution.py:448
  25.8 0.1 order.1.refs_0_.weight
  25.9 0.2 collective-permute-done.11.refs_6_
  26.1 0.0 collective-permute-done.10.refs_2_
  26.1 1.5 %project.1 = (f32[192,384]{1,0:T(8,128)S(1)}, bf16[192,384]{1,0:T(8,128)(2,1)S(1)}, bf16[192,384]{1,0:T(8,128)(2,1)S(1)}, bf16[192,384]{1,0:T(8,128)(2,1)S(1)}, bf16[512,384]{1,0:T(8,128)(2,1)S(1)}) custom-call(bf16[768,384]{1,0:T(8,128)(2,1)S(1)} %order.1.refs_0_.weight, bf16[256,768]{1,0:T(8,128)(2,1)S(1)} %get-tuple-element.60.refs_1_, ...), custom_call_target="tpu_custom_call" | custom-call | flops 1760000000 | bytes 3588096 | tf_op jit(solution)/shard_map/project/pallas_call | solution.py:406
  27.6 0.6 %back_project.1 = (f32[256,768]{1,0:T(8,128)S(1)}, f32[256,768]{1,0:T(8,128)S(1)}) custom-call(bf16[768,384]{1,0:T(8,128)(2,1)S(1)} %order.1.refs_0_.weight, bf16[512,384]{1,0:T(8,128)(2,1)S(1)} %get-tuple-element.67.gp_ref), custom_call_target="tpu_custom_call" | custom-call | flops 770000000 | bytes 2555904 | tf_op jit(solution)/shard_map/back_project/pallas_call | solution.py:406
  28.2 0.2 collective-permute-start.15
  28.5 1.9 %collective-permute-start.12 = (bf16[192,384]{1,0:T(8,128)(2,1)S(1)}, bf16[192,384]{1,0:T(8,128)(2,1)S(1)}, u32[]{:S(2)}, u32[]{:S(2)}) collective-permute-start(bf16[192,384]{1,0:T(8,128)(2,1)S(1)} %get-tuple-element.64), channel_id=1, source_target_pairs={{0,2},{2,0},{4,6},{6,4},{8,10},{10,8},{12,14},{14,12},{16,18},{18,... | collective-permute-start | bytes 442376 | tf_op jit(solution)/shard_map/ppermute | solution.py:433
  30.4 1.3 %collective-permute-start.13 = (bf16[192,384]{1,0:T(8,128)(2,1)S(1)}, bf16[192,384]{1,0:T(8,128)(2,1)S(1)}, u32[]{:S(2)}, u32[]{:S(2)}) collective-permute-start(bf16[192,384]{1,0:T(8,128)(2,1)S(1)} %get-tuple-element.65), channel_id=1, source_target_pairs={{0,4},{2,6},{4,0},{6,2},{8,12},{10,14},{12,8},{14,10},{16,20},{18,... | collective-permute-start | bytes 442376 | tf_op jit(solution)/shard_map/ppermute | solution.py:433
  31.7 0.3 collective-permute-start.14
  32.0 0.0 collective-permute-done.15.refs_1_
  32.0 3.2 %norm_back.1 = (f32[96,128]{1,0:T(8,128)S(1)}, bf16[96,128]{1,0:T(8,128)(2,1)S(1)}, bf16[96,128]{1,0:T(8,128)(2,1)S(1)}, bf16[96,128]{1,0:T(8,128)(2,1)S(1)}, f3...) custom-call(f32[256,768]{1,0:T(8,128)S(1)} %get-tuple-element.68.refs_0_, ...), custom_call_target="tpu_custom_call" | custom-call | flops 110000000 | bytes 4186112 | tf_op jit(solution)/shard_map/norm_back/pallas_call | solution.py:406
  35.2 0.1 collective-permute-start.19
  35.2 2.0 %collective-permute-start.16 = (bf16[96,128]{1,0:T(8,128)(2,1)S(1)}, bf16[96,128]{1,0:T(8,128)(2,1)S(1)}, u32[]{:S(2)}, u32[]{:S(2)}) collective-permute-start(bf16[96,128]{1,0:T(8,128)(2,1)S(1)} %get-tuple-element.74), channel_id=1, source_target_pairs={{0,3},{1,2},{2,1},{3,0},{4,7},{5,6},{6,5},{7,4},{8,11},{9,10},{10,... | collective-permute-start | bytes 73736 | tf_op jit(solution)/shard_map/ppermute | solution.py:439
  37.2 0.0 collective-permute-done.12.refs_1_
  37.2 1.0 %collective-permute-start.17 = (bf16[96,128]{1,0:T(8,128)(2,1)S(1)}, bf16[96,128]{1,0:T(8,128)(2,1)S(1)}, u32[]{:S(2)}, u32[]{:S(2)}) collective-permute-start(bf16[96,128]{1,0:T(8,128)(2,1)S(1)} %get-tuple-element.75), channel_id=1, source_target_pairs={{0,5},{1,4},{2,7},{3,6},{4,1},{5,0},{6,3},{7,2},{8,13},{9,12},{10,... | collective-permute-start | bytes 73736 | tf_op jit(solution)/shard_map/ppermute | solution.py:439
  38.2 1.1 %collective-permute-done.13.refs_2_ = bf16[192,384]{1,0:T(8,128)(2,1)S(1)} collective-permute-done((bf16[192,384]{1,0:T(8,128)(2,1)S(1)}, bf16[192,384]{1,0:T(8,128)(2,1)S(1)}, u32[]{:S(2)}, u32[]{:S(2)}) %collective-permute-start.13) | collective-permute-done | bytes 147488 | tf_op jit(solution)/shard_map/ppermute | solution.py:433
  39.3 0.0 collective-permute-start.18
  39.3 0.0 collective-permute-done.14.refs_3_
  39.4 0.0 collective-permute-done.16.refs_5_
  39.4 1.1 %collective-permute-done.17.refs_6_ = bf16[96,128]{1,0:T(8,128)(2,1)S(1)} collective-permute-done((bf16[96,128]{1,0:T(8,128)(2,1)S(1)}, bf16[96,128]{1,0:T(8,128)(2,1)S(1)}, u32[]{:S(2)}, u32[]{:S(2)}) %collective-permute-start.17) | collective-permute-done | bytes 24608 | tf_op jit(solution)/shard_map/ppermute | solution.py:439
  40.5 3.0 %collective-permute-done.18.refs_7_ = bf16[96,128]{1,0:T(8,128)(2,1)S(1)} collective-permute-done((bf16[96,128]{1,0:T(8,128)(2,1)S(1)}, bf16[96,128]{1,0:T(8,128)(2,1)S(1)}, u32[]{:S(2)}, u32[]{:S(2)}) %collective-permute-start.18) | collective-permute-done | bytes 24608 | tf_op jit(solution)/shard_map/ppermute | solution.py:439
  43.5 0.1 plane_sum.1
  43.6 0.6 %collective-permute-start.20 = (bf16[48,512]{1,0:T(8,128)(2,1)S(1)}, bf16[48,512]{1,0:T(8,128)(2,1)S(1)}, u32[]{:S(2)}, u32[]{:S(2)}) collective-permute-start(bf16[48,512]{1,0:T(8,128)(2,1)S(1)} %get-tuple-element.82), channel_id=1, source_target_pairs={{0,9},{1,8},{2,11},{3,10},{4,13},{5,12},{6,15},{7,14},{8,1},{9,0},... | collective-permute-start | bytes 147464 | tf_op jit(solution)/shard_map/ppermute | solution.py:439
  44.2 1.8 %collective-permute-start.21 = (bf16[48,512]{1,0:T(8,128)(2,1)S(1)}, bf16[48,512]{1,0:T(8,128)(2,1)S(1)}, u32[]{:S(2)}, u32[]{:S(2)}) collective-permute-start(bf16[48,512]{1,0:T(8,128)(2,1)S(1)} %get-tuple-element.83), channel_id=1, source_target_pairs={{0,17},{1,16},{2,19},{3,18},{4,21},{5,20},{6,23},{7,22},{8,25},{9,... | collective-permute-start | bytes 147464 | tf_op jit(solution)/shard_map/ppermute | solution.py:439
  46.0 0.8 %collective-permute-start.22 = (bf16[48,512]{1,0:T(8,128)(2,1)S(1)}, bf16[48,512]{1,0:T(8,128)(2,1)S(1)}, u32[]{:S(2)}, u32[]{:S(2)}) collective-permute-start(bf16[48,512]{1,0:T(8,128)(2,1)S(1)} %get-tuple-element.84), channel_id=1, source_target_pairs={{0,25},{1,24},{2,27},{3,26},{4,29},{5,28},{6,31},{7,30},{8,17},{9,... | collective-permute-start | bytes 147464 | tf_op jit(solution)/shard_map/ppermute | solution.py:439
  46.8 0.0 collective-permute-done.19.other_ref
  46.8 1.9 %conv_back.1 = bf16[1,8,16,768]{3,2,1,0:T(8,128)(2,1)} custom-call(f32[6,8,16,128]{3,2,1,0:T(8,128)S(1)} %get-tuple-element.78.grad_ref, bf16[6,8,16,128]{3,2,1,0:T(8,128)(2,1)S(1)} %collective-permute-done.19.other_ref, f32[6,128,128]{2,1,0:T(8,128)S(1)} %get-tuple-element.72.refs_4_.taps_ref), custom_call_target="tpu_custom_call" | custom-call | flops 110000000 | bytes 1179648 | tf_op jit(solution)/shard_map/conv_back/pallas_call | solution.py:406
  48.7 0.0 collective-permute-done.20.refs_1_
  48.7 1.4 %collective-permute-done.21.refs_2_ = bf16[48,512]{1,0:T(8,128)(2,1)S(1)} collective-permute-done((bf16[48,512]{1,0:T(8,128)(2,1)S(1)}, bf16[48,512]{1,0:T(8,128)(2,1)S(1)}, u32[]{:S(2)}, u32[]{:S(2)}) %collective-permute-start.21) | collective-permute-done | bytes 49184 | tf_op jit(solution)/shard_map/ppermute | solution.py:439
  50.2 1.3 %collective-permute-done.22.refs_3_ = bf16[48,512]{1,0:T(8,128)(2,1)S(1)} collective-permute-done((bf16[48,512]{1,0:T(8,128)(2,1)S(1)}, bf16[48,512]{1,0:T(8,128)(2,1)S(1)}, u32[]{:S(2)}, u32[]{:S(2)}) %collective-permute-start.22) | collective-permute-done | bytes 49184 | tf_op jit(solution)/shard_map/ppermute | solution.py:439
  51.5 0.6 %collective-permute-start.23 = (f32[48,1280]{1,0:T(8,128)S(1)}, f32[48,1280]{1,0:T(8,128)S(1)}, u32[]{:S(2)}, u32[]{:S(2)}) collective-permute-start(f32[48,1280]{1,0:T(8,128)S(1)} %line_sum.1.mine_ref), channel_id=1, source_target_pairs={{0,1},{1,0},{2,3},{3,2},{4,5},{5,4},{6,7},{7,6},{8,9},{9,8},{10,11... | collective-permute-start | bytes 737288 | tf_op jit(solution)/shard_map/ppermute | solution.py:451
  52.1 1.1 %collective-permute-done.23.other_ref = f32[48,1280]{1,0:T(8,128)S(1)} collective-permute-done((f32[48,1280]{1,0:T(8,128)S(1)}, f32[48,1280]{1,0:T(8,128)S(1)}, u32[]{:S(2)}, u32[]{:S(2)}) %collective-permute-start.23) | collective-permute-done | bytes 245792 | tf_op jit(solution)/shard_map/ppermute | solution.py:451
  53.2 0.8 %finish.1 = (f32[48,1536]{1,0:T(8,128)}, f32[48,49]{1,0:T(8,128)}, f32[1,48]{1,0:T(1,128)}, f32[1,48]{1,0:T(1,128)}) custom-call(f32[48,1280]{1,0:T(8,128)S(1)} %line_sum.1.mine_ref, f32[48,1280]{1,0:T(8,128)S(1)} %collective-permute-done.23.other_ref), custom_call_target="tpu_custom_call" | custom-call | flops 550000000 | bytes 796224 | tf_op jit(solution)/shard_map/finish/pallas_call | solution.py:406
  (3 shorter events, 0.1 us)
Async XLA Ops:
  0.6 7.1 %copy-start = (bf16[1,8,16,768]{3,2,1,0:T(8,128)(2,1)S(1)}, bf16[1,8,16,768]{3,2,1,0:T(8,128)(2,1)}, u32[]{:S(2)}) copy-start(bf16[1,8,16,768]{3,2,1,0:T(8,128)(2,1)} %param.6) | copy-start | bytes 589828
  0.6 7.1 %copy-start.1 = (bf16[1,8,16,1536]{3,2,1,0:T(8,128)(2,1)S(1)}, bf16[1,8,16,1536]{3,2,1,0:T(8,128)(2,1)}, u32[]{:S(2)}) copy-start(bf16[1,8,16,1536]{3,2,1,0:T(8,128)(2,1)} %param.7) | copy-start | bytes 1179652
  2.4 10.0 %copy-start.2 = (bf16[48,512]{1,0:T(8,128)(2,1)S(1)}, bf16[48,512]{1,0:T(8,128)(2,1)}, u32[]{:S(2)}) copy-start(bf16[48,512]{1,0:T(8,128)(2,1)} %get-tuple-element.50.refs_0_) | copy-start | bytes 147460
  2.4 7.1 %collective-permute-start.1 = (bf16[48,512]{1,0:T(8,128)(2,1)}, bf16[48,512]{1,0:T(8,128)(2,1)S(1)}, u32[]{:S(2)}, u32[]{:S(2)}) collective-permute-start(bf16[48,512]{1,0:T(8,128)(2,1)} %get-tuple-element.52), channel_id=1, source_target_pairs={{0,17},{1,16},{2,19},{3,18},{4,21},{5,20},{6,23},{7,22},{8,25},{9,... | collective-permute-start | bytes 147464 | tf_op jit(solution)/shard_map/ppermute | solution.py:439
  5.9 5.6 %collective-permute-start.2 = (bf16[48,512]{1,0:T(8,128)(2,1)}, bf16[48,512]{1,0:T(8,128)(2,1)S(1)}, u32[]{:S(2)}, u32[]{:S(2)}) collective-permute-start(bf16[48,512]{1,0:T(8,128)(2,1)} %get-tuple-element.51), channel_id=1, source_target_pairs={{0,25},{1,24},{2,27},{3,26},{4,29},{5,28},{6,31},{7,30},{8,17},{9,... | collective-permute-start | bytes 147464 | tf_op jit(solution)/shard_map/ppermute | solution.py:439
  7.5 4.9 %collective-permute-start = (bf16[48,512]{1,0:T(8,128)(2,1)}, bf16[48,512]{1,0:T(8,128)(2,1)S(1)}, u32[]{:S(2)}, u32[]{:S(2)}) collective-permute-start(bf16[48,512]{1,0:T(8,128)(2,1)} %get-tuple-element.51), channel_id=1, source_target_pairs={{0,9},{1,8},{2,11},{3,10},{4,13},{5,12},{6,15},{7,14},{8,1},{9,0},... | collective-permute-start | bytes 147464 | tf_op jit(solution)/shard_map/ppermute | solution.py:439
  7.8 16.4 %collective-permute-start.9 = (bf16[128,768]{1,0:T(8,128)(2,1)S(1)}, bf16[128,768]{1,0:T(8,128)(2,1)S(1)}, u32[]{:S(2)}, u32[]{:S(2)}) collective-permute-start(bf16[128,768]{1,0:T(8,128)(2,1)S(1)} %get-tuple-element.59), channel_id=1, source_target_pairs={{0,1},{1,0},{2,3},{3,2},{4,5},{5,4},{6,7},{7,6},{8,9},{9,8},{10,11... | collective-permute-start | bytes 589832 | tf_op jit(solution)/shard_map/ppermute | solution.py:451
  7.9 13.1 %collective-permute-start.8 = (bf16[256,768]{1,0:T(8,128)(2,1)S(1)}, bf16[256,768]{1,0:T(8,128)(2,1)S(1)}, u32[]{:S(2)}, u32[]{:S(2)}) collective-permute-start(bf16[256,768]{1,0:T(8,128)(2,1)S(1)} %get-tuple-element.57), channel_id=1, source_target_pairs={{0,9},{1,8},{2,11},{3,10},{4,13},{5,12},{6,15},{7,14},{8,1},{9,0},... | collective-permute-start | bytes 1179656 | tf_op jit(solution)/shard_map/ppermute | solution.py:439
  12.5 5.2 %collective-permute-start.3 = (bf16[192,384]{1,0:T(8,128)(2,1)S(1)}, bf16[192,384]{1,0:T(8,128)(2,1)S(1)}, u32[]{:S(2)}, u32[]{:S(2)}) collective-permute-start(bf16[192,384]{1,0:T(8,128)(2,1)S(1)} %get-tuple-element.53.own_ref.refs_0_), channel_id=1, source_target_pairs={{0,2},{1,5},{2,0},{3,7},{4,6},{5,1},{6,4},{7,3},{8,10},{9,13},{10,... | collective-permute-start | bytes 442376 | tf_op jit(solution)/shard_map/ppermute | solution.py:448
  14.0 5.0 %collective-permute-start.7 = (bf16[96,128]{1,0:T(8,128)(2,1)S(1)}, bf16[96,128]{1,0:T(8,128)(2,1)S(1)}, u32[]{:S(2)}, u32[]{:S(2)}) collective-permute-start(bf16[96,128]{1,0:T(8,128)(2,1)S(1)} %get-tuple-element.54.refs_0_), channel_id=1, source_target_pairs={{0,7},{1,6},{2,5},{3,4},{4,3},{5,2},{6,1},{7,0},{8,15},{9,14},{10,... | collective-permute-start | bytes 73736 | tf_op jit(solution)/shard_map/ppermute | solution.py:439
  15.6 5.0 %collective-permute-start.6 = (bf16[96,128]{1,0:T(8,128)(2,1)S(1)}, bf16[96,128]{1,0:T(8,128)(2,1)S(1)}, u32[]{:S(2)}, u32[]{:S(2)}) collective-permute-start(bf16[96,128]{1,0:T(8,128)(2,1)S(1)} %get-tuple-element.54.refs_0_), channel_id=1, source_target_pairs={{0,5},{1,4},{2,7},{3,6},{4,1},{5,0},{6,3},{7,2},{8,13},{9,12},{10,... | collective-permute-start | bytes 73736 | tf_op jit(solution)/shard_map/ppermute | solution.py:439
  17.7 3.3 %collective-permute-start.5 = (bf16[96,128]{1,0:T(8,128)(2,1)S(1)}, bf16[96,128]{1,0:T(8,128)(2,1)S(1)}, u32[]{:S(2)}, u32[]{:S(2)}) collective-permute-start(bf16[96,128]{1,0:T(8,128)(2,1)S(1)} %get-tuple-element.54.refs_0_), channel_id=1, source_target_pairs={{0,3},{1,2},{2,1},{3,0},{4,7},{5,6},{6,5},{7,4},{8,11},{9,10},{10,... | collective-permute-start | bytes 73736 | tf_op jit(solution)/shard_map/ppermute | solution.py:439
  19.0 6.8 %collective-permute-start.4 = (bf16[384,384]{1,0:T(8,128)(2,1)S(1)}, bf16[384,384]{1,0:T(8,128)(2,1)S(1)}, u32[]{:S(2)}, u32[]{:S(2)}) collective-permute-start(bf16[384,384]{1,0:T(8,128)(2,1)S(1)} %join.1), channel_id=1, source_target_pairs={{0,4},{1,3},{2,6},{3,1},{4,0},{5,7},{6,2},{7,5},{8,12},{9,11},{10,... | collective-permute-start | bytes 884744 | tf_op jit(solution)/shard_map/ppermute | solution.py:448
  24.2 1.9 %collective-permute-start.10 = (bf16[256,768]{1,0:T(8,128)(2,1)S(1)}, bf16[256,768]{1,0:T(8,128)(2,1)S(1)}, u32[]{:S(2)}, u32[]{:S(2)}) collective-permute-start(bf16[256,768]{1,0:T(8,128)(2,1)S(1)} %get-tuple-element.60.refs_1_), channel_id=1, source_target_pairs={{0,1},{1,0},{2,3},{3,2},{4,5},{5,4},{6,7},{7,6},{8,9},{9,8},{10,11... | collective-permute-start | bytes 1179656 | tf_op jit(solution)/shard_map/ppermute | solution.py:451
  24.4 1.7 %collective-permute-start.11 = (bf16[128,384]{1,0:T(8,128)(2,1)S(1)}, bf16[128,384]{1,0:T(8,128)(2,1)S(1)}, u32[]{:S(2)}, u32[]{:S(2)}) collective-permute-start(bf16[128,384]{1,0:T(8,128)(2,1)S(1)} %get-tuple-element.62), channel_id=1, source_target_pairs={{0,1},{1,0},{2,3},{3,2},{4,5},{5,4},{6,7},{7,6},{8,9},{9,8},{10,11... | collective-permute-start | bytes 294920 | tf_op jit(solution)/shard_map/ppermute | solution.py:451
  28.2 3.7 %collective-permute-start.15 = (f32[256,768]{1,0:T(8,128)S(1)}, f32[256,768]{1,0:T(8,128)S(1)}, u32[]{:S(2)}, u32[]{:S(2)}) collective-permute-start(f32[256,768]{1,0:T(8,128)S(1)} %get-tuple-element.69), channel_id=1, source_target_pairs={{0,1},{1,0},{2,3},{3,2},{4,5},{5,4},{6,7},{7,6},{8,9},{9,8},{10,11... | collective-permute-start | bytes 2359304 | tf_op jit(solution)/shard_map/ppermute | solution.py:451
  28.5 8.8 %collective-permute-start.12 = (bf16[192,384]{1,0:T(8,128)(2,1)S(1)}, bf16[192,384]{1,0:T(8,128)(2,1)S(1)}, u32[]{:S(2)}, u32[]{:S(2)}) collective-permute-start(bf16[192,384]{1,0:T(8,128)(2,1)S(1)} %get-tuple-element.64), channel_id=1, source_target_pairs={{0,2},{2,0},{4,6},{6,4},{8,10},{10,8},{12,14},{14,12},{16,18},{18,... | collective-permute-start | bytes 442376 | tf_op jit(solution)/shard_map/ppermute | solution.py:433
  30.4 9.0 %collective-permute-start.13 = (bf16[192,384]{1,0:T(8,128)(2,1)S(1)}, bf16[192,384]{1,0:T(8,128)(2,1)S(1)}, u32[]{:S(2)}, u32[]{:S(2)}) collective-permute-start(bf16[192,384]{1,0:T(8,128)(2,1)S(1)} %get-tuple-element.65), channel_id=1, source_target_pairs={{0,4},{2,6},{4,0},{6,2},{8,12},{10,14},{12,8},{14,10},{16,20},{18,... | collective-permute-start | bytes 442376 | tf_op jit(solution)/shard_map/ppermute | solution.py:433
  31.7 7.7 %collective-permute-start.14 = (bf16[192,384]{1,0:T(8,128)(2,1)S(1)}, bf16[192,384]{1,0:T(8,128)(2,1)S(1)}, u32[]{:S(2)}, u32[]{:S(2)}) collective-permute-start(bf16[192,384]{1,0:T(8,128)(2,1)S(1)} %get-tuple-element.66), channel_id=1, source_target_pairs={{0,6},{2,4},{4,2},{6,0},{8,14},{10,12},{12,10},{14,8},{16,22},{18,... | collective-permute-start | bytes 442376 | tf_op jit(solution)/shard_map/ppermute | solution.py:433
  35.2 11.6 %collective-permute-start.19 = (bf16[6,8,16,128]{3,2,1,0:T(8,128)(2,1)S(1)}, bf16[6,8,16,128]{3,2,1,0:T(8,128)(2,1)S(1)}, u32[]{:S(2)}, u32[]{:S(2)}) collective-permute-start(bf16[6,8,16,128]{3,2,1,0:T(8,128)(2,1)S(1)} %get-tuple-element.79), channel_id=1, source_target_pairs={{0,9},{1,8},{2,11},{3,10},{4,13},{5,12},{6,15},{7,14},{8,1},{9,0},... | collective-permute-start | bytes 589832 | tf_op jit(solution)/shard_map/ppermute | solution.py:439
  35.2 4.1 %collective-permute-start.16 = (bf16[96,128]{1,0:T(8,128)(2,1)S(1)}, bf16[96,128]{1,0:T(8,128)(2,1)S(1)}, u32[]{:S(2)}, u32[]{:S(2)}) collective-permute-start(bf16[96,128]{1,0:T(8,128)(2,1)S(1)} %get-tuple-element.74), channel_id=1, source_target_pairs={{0,3},{1,2},{2,1},{3,0},{4,7},{5,6},{6,5},{7,4},{8,11},{9,10},{10,... | collective-permute-start | bytes 73736 | tf_op jit(solution)/shard_map/ppermute | solution.py:439
  37.2 3.3 %collective-permute-start.17 = (bf16[96,128]{1,0:T(8,128)(2,1)S(1)}, bf16[96,128]{1,0:T(8,128)(2,1)S(1)}, u32[]{:S(2)}, u32[]{:S(2)}) collective-permute-start(bf16[96,128]{1,0:T(8,128)(2,1)S(1)} %get-tuple-element.75), channel_id=1, source_target_pairs={{0,5},{1,4},{2,7},{3,6},{4,1},{5,0},{6,3},{7,2},{8,13},{9,12},{10,... | collective-permute-start | bytes 73736 | tf_op jit(solution)/shard_map/ppermute | solution.py:439
  39.3 4.2 %collective-permute-start.18 = (bf16[96,128]{1,0:T(8,128)(2,1)S(1)}, bf16[96,128]{1,0:T(8,128)(2,1)S(1)}, u32[]{:S(2)}, u32[]{:S(2)}) collective-permute-start(bf16[96,128]{1,0:T(8,128)(2,1)S(1)} %get-tuple-element.76), channel_id=1, source_target_pairs={{0,7},{1,6},{2,5},{3,4},{4,3},{5,2},{6,1},{7,0},{8,15},{9,14},{10,... | collective-permute-start | bytes 73736 | tf_op jit(solution)/shard_map/ppermute | solution.py:439
  43.6 5.2 %collective-permute-start.20 = (bf16[48,512]{1,0:T(8,128)(2,1)S(1)}, bf16[48,512]{1,0:T(8,128)(2,1)S(1)}, u32[]{:S(2)}, u32[]{:S(2)}) collective-permute-start(bf16[48,512]{1,0:T(8,128)(2,1)S(1)} %get-tuple-element.82), channel_id=1, source_target_pairs={{0,9},{1,8},{2,11},{3,10},{4,13},{5,12},{6,15},{7,14},{8,1},{9,0},... | collective-permute-start | bytes 147464 | tf_op jit(solution)/shard_map/ppermute | solution.py:439
  44.2 5.9 %collective-permute-start.21 = (bf16[48,512]{1,0:T(8,128)(2,1)S(1)}, bf16[48,512]{1,0:T(8,128)(2,1)S(1)}, u32[]{:S(2)}, u32[]{:S(2)}) collective-permute-start(bf16[48,512]{1,0:T(8,128)(2,1)S(1)} %get-tuple-element.83), channel_id=1, source_target_pairs={{0,17},{1,16},{2,19},{3,18},{4,21},{5,20},{6,23},{7,22},{8,25},{9,... | collective-permute-start | bytes 147464 | tf_op jit(solution)/shard_map/ppermute | solution.py:439
  46.0 5.4 %collective-permute-start.22 = (bf16[48,512]{1,0:T(8,128)(2,1)S(1)}, bf16[48,512]{1,0:T(8,128)(2,1)S(1)}, u32[]{:S(2)}, u32[]{:S(2)}) collective-permute-start(bf16[48,512]{1,0:T(8,128)(2,1)S(1)} %get-tuple-element.84), channel_id=1, source_target_pairs={{0,25},{1,24},{2,27},{3,26},{4,29},{5,28},{6,31},{7,30},{8,17},{9,... | collective-permute-start | bytes 147464 | tf_op jit(solution)/shard_map/ppermute | solution.py:439
  51.5 1.8 %collective-permute-start.23 = (f32[48,1280]{1,0:T(8,128)S(1)}, f32[48,1280]{1,0:T(8,128)S(1)}, u32[]{:S(2)}, u32[]{:S(2)}) collective-permute-start(f32[48,1280]{1,0:T(8,128)S(1)} %line_sum.1.mine_ref), channel_id=1, source_target_pairs={{0,1},{1,0},{2,3},{3,2},{4,5},{5,4},{6,7},{7,6},{8,9},{9,8},{10,11... | collective-permute-start | bytes 737288 | tf_op jit(solution)/shard_map/ppermute | solution.py:451

commit v16 on v15

--- a/solution.py
+++ b/solution.py
@@ -168,6 +168,12 @@
 
 def unfold(rows):
     return jnp.concatenate([rows, pltpu.roll(rows, LANES // 2, 1)], axis=0)
+
+
+def clear_borders(padded, breadth):
+    shape = padded.shape[:-2] + (8, LANES)
+    padded[..., :8, :] = jnp.zeros(shape, F32)
+    padded[..., 8 + breadth :, :] = jnp.zeros(shape, F32)
 
 
 def conv_norm_kernel(relative, own, height, breadth, *refs):
@@ -189,7 +195,7 @@
         count = unfolded.shape[0] // INNER
         small = [unfolded.at[pl.ds(group * count, count), :] for group in range(INNER)]
     place_rows(small, gathered, own, relative, F32)
-    padded[...] = jnp.zeros_like(padded)
+    clear_borders(padded, breadth)
     for tile in range(tiles):
         lanes = slice(tile * LANES, (tile + 1) * LANES)
         taps_ref[tile] = gathered[lanes, :].T
@@ -315,7 +321,7 @@
     grad_ref, sent_ref, padded, grads_ref, rows, small, unfolded = refs[7 + INNER :]
     pixels, depth = x_ref.shape
     tiles = depth // LANES
-    padded[...] = jnp.zeros_like(padded)
+    clear_borders(padded, breadth)
     rows[...] = jnp.zeros_like(rows)
     for image, source in enumerate((x_ref, far_ref)):
         span = slice(image * pixels, (image + 1) * pixels)
@@ -380,7 +386,7 @@
 
 def conv_back_kernel(grad_ref, other_ref, taps_ref, out_ref, padded):
     tiles, height, breadth, _ = grad_ref.shape
-    padded[...] = jnp.zeros_like(padded)
+    clear_borders(padded, breadth)
     padded[:, :, 8 : 8 + breadth, :] = grad_ref[...] + other_ref[...].astype(F32)
 
     def one_tile(tile, carry):
@@ -510,6 +516,7 @@
         4.0,
         *gathered,
     )
+    weight_lines, cot_sibling = lax.optimization_barrier((weight_lines, cot_sibling))
     first_lines = hop(weight_lines, 0)
     (joined,) = call(
         join_kernel,
@@ -559,7 +566,6 @@
         image,
         across,
     )
-    normed, cot_sibling = lax.optimization_barrier((normed, cot_sibling))
     normed_sibling, corner = over_core(normed), over_core(corner)
     *pieces, grad_pre = call(
         functools.partial(project_kernel, relative, own),
@@ -636,7 +642,7 @@
         "plane_sum",
         [shape((own, quarter + LANES), F32)] + [shape((own, quarter + LANES), BF16)] * (lines - 1),
         [],
-        0.8,
+        2.0,
         pieces[0],
         *arrived,
         small[0],

time: 54.1 us -> 53.8 us (level)
  waiting for transfers between devices: 15.6 us -> 15 us
    ppermute x2, waiting for transfers between devices: 2.98 us -> 0.3 us  [hop(): return lax.ppermute(array, ('shard', 'rep'), pairs)]
    ppermute x5, waiting for transfers between devices: 1.37 us -> 2.78 us  [over_core(): return lax.ppermute(array, 'rep', [(i, i ^ 1) for i in range(reps)])]
    ppermute x14, waiting for transfers between devices: 10.1 us -> 11 us  [crossing(): return lax.ppermute(array, ('shard', 'rep'), pairs)]
    ppermute x5, starting transfers between devices: 1.48 us -> 0.92 us  [over_core(): return lax.ppermute(array, 'rep', [(i, i ^ 1) for i in range(reps)])]
where the time goes in v16:
time: 53.8 us; the launch traced here: 53.6 us
  starting transfers between devices  24.4 us (45%)
  waiting for transfers between devices  15 us (28%)
  Pallas kernels  13.4 us (25%)
  between operations  0.76 us (1%)
    ppermute x14, starting transfers between devices, crossing(): return lax.ppermute(array, ('shard', 'rep'), pairs)  16.6 us
    pallas_call x13, Pallas kernels, call(): pl.pallas_call(kernel, out_shape=outs, in_specs=[VMEM] * len(args), out_s...  13.4 us
    ppermute x14, waiting for transfers between devices, crossing(): return lax.ppermute(array, ('shard', 'rep'), pairs)  11 us
    ppermute x3, starting transfers between devices, over_shard(): return lax.ppermute(array, 'shard', [(i, i ^ flip) for i in range(shards)])  3.5 us
    ppermute x2, starting transfers between devices, hop(): return lax.ppermute(array, ('shard', 'rep'), pairs)  3.4 us
    ppermute x5, waiting for transfers between devices, over_core(): return lax.ppermute(array, 'rep', [(i, i ^ 1) for i in range(reps)])  2.78 us
  transfers between devices with their start and end apart: 24, of which 12 were waited for; matrix products, arithmetic and copies ran while one was open for 0% of the time, Pallas kernels for 16%

profile of v16, /device:TPU:0, one launch (start us, length us, event | category | flops | bytes accessed | tf_op | source)
XLA Modules:
  0.0 53.6 jit_solution(12629734338367705445)
XLA Ops:
  0.6 0.0 copy-start
  0.6 0.0 copy-start.1
  0.7 1.7 %pack.1 = (bf16[48,512]{1,0:T(8,128)(2,1)}, bf16[48,512]{1,0:T(8,128)(2,1)}, bf16[48,512]{1,0:T(8,128)(2,1)}) custom-call(bf16[48,1536]{1,0:T(8,128)(2,1)} %w_ref.1, bf16[48,49]{1,0:T(8,128)(2,1)} %dw_ref.1, bf16[1,48]{1,0:T(2,128)(2,1)} %bitcast.11, bf16[1,48]{1,0:T(2,128)(2,1)} %bitcast.12), custom_call_target="tpu_custom_call" | custom-call | flops 550000000 | bytes 299808 | tf_op jit(solution)/shard_map/pack/pallas_call | solution.py:412
  2.4 0.0 copy-start.2
  2.4 3.5 %collective-permute-start.1 = (bf16[48,512]{1,0:T(8,128)(2,1)}, bf16[48,512]{1,0:T(8,128)(2,1)S(1)}, u32[]{:S(2)}, u32[]{:S(2)}) collective-permute-start(bf16[48,512]{1,0:T(8,128)(2,1)} %get-tuple-element.52), channel_id=1, source_target_pairs={{0,17},{1,16},{2,19},{3,18},{4,21},{5,20},{6,23},{7,22},{8,25},{9,... | collective-permute-start | bytes 147464 | tf_op jit(solution)/shard_map/ppermute | solution.py:445
  5.9 1.6 %collective-permute-start.2 = (bf16[48,512]{1,0:T(8,128)(2,1)}, bf16[48,512]{1,0:T(8,128)(2,1)S(1)}, u32[]{:S(2)}, u32[]{:S(2)}) collective-permute-start(bf16[48,512]{1,0:T(8,128)(2,1)} %get-tuple-element.51), channel_id=1, source_target_pairs={{0,25},{1,24},{2,27},{3,26},{4,29},{5,28},{6,31},{7,30},{8,17},{9,... | collective-permute-start | bytes 147464 | tf_op jit(solution)/shard_map/ppermute | solution.py:445
  7.5 0.2 collective-permute-start
  7.7 0.0 copy-done
  7.7 0.0 copy-done.1
  7.8 0.1 collective-permute-start.3
  7.9 1.7 %collective-permute-start.9 = (bf16[256,768]{1,0:T(8,128)(2,1)S(1)}, bf16[256,768]{1,0:T(8,128)(2,1)S(1)}, u32[]{:S(2)}, u32[]{:S(2)}) collective-permute-start(bf16[256,768]{1,0:T(8,128)(2,1)S(1)} %get-tuple-element.59), channel_id=1, source_target_pairs={{0,9},{1,8},{2,11},{3,10},{4,13},{5,12},{6,15},{7,14},{8,1},{9,0},... | collective-permute-start | bytes 1179656 | tf_op jit(solution)/shard_map/ppermute | solution.py:445
  9.5 0.0 collective-permute-done.1.refs_2_
  9.5 2.0 %collective-permute-done.2.refs_3_ = bf16[48,512]{1,0:T(8,128)(2,1)S(1)} collective-permute-done((bf16[48,512]{1,0:T(8,128)(2,1)}, bf16[48,512]{1,0:T(8,128)(2,1)S(1)}, u32[]{:S(2)}, u32[]{:S(2)}) %collective-permute-start.2) | collective-permute-done | bytes 49184 | tf_op jit(solution)/shard_map/ppermute | solution.py:445
  11.5 0.9 %collective-permute-done.refs_1_ = bf16[48,512]{1,0:T(8,128)(2,1)S(1)} collective-permute-done((bf16[48,512]{1,0:T(8,128)(2,1)}, bf16[48,512]{1,0:T(8,128)(2,1)S(1)}, u32[]{:S(2)}, u32[]{:S(2)}) %collective-permute-start) | collective-permute-done | bytes 49184 | tf_op jit(solution)/shard_map/ppermute | solution.py:445
  12.4 0.0 copy-done.2
  12.4 0.1 assemble.1
  12.5 0.0 collective-permute-done.3.refs_4_
  12.5 1.6 %collective-permute-start.4 = (bf16[192,384]{1,0:T(8,128)(2,1)S(1)}, bf16[192,384]{1,0:T(8,128)(2,1)S(1)}, u32[]{:S(2)}, u32[]{:S(2)}) collective-permute-start(bf16[192,384]{1,0:T(8,128)(2,1)S(1)} %get-tuple-element.57.own_ref.refs_0_), channel_id=1, source_target_pairs={{0,2},{1,5},{2,0},{3,7},{4,6},{5,1},{6,4},{7,3},{8,10},{9,13},{10,... | collective-permute-start | bytes 442376 | tf_op jit(solution)/shard_map/ppermute | solution.py:454
  14.0 1.6 %collective-permute-start.8 = (bf16[96,128]{1,0:T(8,128)(2,1)S(1)}, bf16[96,128]{1,0:T(8,128)(2,1)S(1)}, u32[]{:S(2)}, u32[]{:S(2)}) collective-permute-start(bf16[96,128]{1,0:T(8,128)(2,1)S(1)} %get-tuple-element.58.refs_0_), channel_id=1, source_target_pairs={{0,7},{1,6},{2,5},{3,4},{4,3},{5,2},{6,1},{7,0},{8,15},{9,14},{10,... | collective-permute-start | bytes 73736 | tf_op jit(solution)/shard_map/ppermute | solution.py:445
  15.6 0.1 collective-permute-start.7
  15.8 1.6 %collective-permute-start.6 = (bf16[96,128]{1,0:T(8,128)(2,1)S(1)}, bf16[96,128]{1,0:T(8,128)(2,1)S(1)}, u32[]{:S(2)}, u32[]{:S(2)}) collective-permute-start(bf16[96,128]{1,0:T(8,128)(2,1)S(1)} %get-tuple-element.58.refs_0_), channel_id=1, source_target_pairs={{0,3},{1,2},{2,1},{3,0},{4,7},{5,6},{6,5},{7,4},{8,11},{9,10},{10,... | collective-permute-start | bytes 73736 | tf_op jit(solution)/shard_map/ppermute | solution.py:445
  17.4 0.3 collective-permute-done.4.came_ref.refs_1_
  17.7 1.8 %collective-permute-start.5 = (bf16[384,384]{1,0:T(8,128)(2,1)S(1)}, bf16[384,384]{1,0:T(8,128)(2,1)S(1)}, u32[]{:S(2)}, u32[]{:S(2)}) collective-permute-start(bf16[384,384]{1,0:T(8,128)(2,1)S(1)} %join.1), channel_id=1, source_target_pairs={{0,4},{1,3},{2,6},{3,1},{4,0},{5,7},{6,2},{7,5},{8,12},{9,11},{10,... | collective-permute-start | bytes 884744 | tf_op jit(solution)/shard_map/ppermute | solution.py:454
  19.6 0.0 collective-permute-done.8.refs_3_
  19.6 0.0 collective-permute-done.7.refs_2_
  19.6 0.0 collective-permute-done.6.refs_1_
  19.6 1.4 %collective-permute-done.9.refs_5_.refs_6_ = bf16[256,768]{1,0:T(8,128)(2,1)S(1)} collective-permute-done((bf16[256,768]{1,0:T(8,128)(2,1)S(1)}, bf16[256,768]{1,0:T(8,128)(2,1)S(1)}, u32[]{:S(2)}, u32[]{:S(2)}) %collective-permute-start.9) | collective-permute-done | bytes 393248 | tf_op jit(solution)/shard_map/ppermute | solution.py:445
  21.0 3.2 %conv_norm.1 = (bf16[256,768]{1,0:T(8,128)(2,1)S(1)}, f32[256,768]{1,0:T(8,128)S(1)}, f32[256,128]{1,0:T(8,128)S(1)}, f32[6,128,128]{2,1,0:T(8,128)S(1)}, bf16[128,384]{1,0:T(8,128)(2,1)S(1)}) custom-call(bf16[96,128]{1,0:T(8,128)(2,1)S(1)} %get-tuple-element.58.refs_0_, bf16[96,128]{1,0:T(8,128)(2,1)S(1)} %collective-permute-done.6.refs_1_, ...), custom_call_target="tpu_custom_call" | custom-call | flops 110000000 | bytes 2490368 | tf_op jit(solution)/shard_map/conv_norm/pallas_call | solution.py:412
  24.2 0.2 collective-permute-start.10
  24.4 0.4 collective-permute-start.11
  24.8 0.0 collective-permute-done.5.refs_2_
  24.8 0.1 order.1.refs_0_.weight
  24.8 1.3 %collective-permute-done.11.refs_6_ = bf16[128,384]{1,0:T(8,128)(2,1)S(1)} collective-permute-done((bf16[128,384]{1,0:T(8,128)(2,1)S(1)}, bf16[128,384]{1,0:T(8,128)(2,1)S(1)}, u32[]{:S(2)}, u32[]{:S(2)}) %collective-permute-start.11) | collective-permute-done | bytes 98336 | tf_op jit(solution)/shard_map/ppermute | solution.py:457
  26.1 0.0 collective-permute-done.10.refs_2_
  26.1 1.5 %project.1 = (f32[192,384]{1,0:T(8,128)S(1)}, bf16[192,384]{1,0:T(8,128)(2,1)S(1)}, bf16[192,384]{1,0:T(8,128)(2,1)S(1)}, bf16[192,384]{1,0:T(8,128)(2,1)S(1)}, bf16[512,384]{1,0:T(8,128)(2,1)S(1)}) custom-call(bf16[768,384]{1,0:T(8,128)(2,1)S(1)} %order.1.refs_0_.weight, bf16[256,768]{1,0:T(8,128)(2,1)S(1)} %get-tuple-element.60.refs_1_, ...), custom_call_target="tpu_custom_call" | custom-call | flops 1760000000 | bytes 3588096 | tf_op jit(solution)/shard_map/project/pallas_call | solution.py:412
  27.7 0.6 %back_project.1 = (f32[256,768]{1,0:T(8,128)S(1)}, f32[256,768]{1,0:T(8,128)S(1)}) custom-call(bf16[768,384]{1,0:T(8,128)(2,1)S(1)} %order.1.refs_0_.weight, bf16[512,384]{1,0:T(8,128)(2,1)S(1)} %get-tuple-element.67.gp_ref), custom_call_target="tpu_custom_call" | custom-call | flops 770000000 | bytes 2555904 | tf_op jit(solution)/shard_map/back_project/pallas_call | solution.py:412
  28.3 0.2 collective-permute-start.15
  28.5 1.5 %collective-permute-start.12 = (bf16[192,384]{1,0:T(8,128)(2,1)S(1)}, bf16[192,384]{1,0:T(8,128)(2,1)S(1)}, u32[]{:S(2)}, u32[]{:S(2)}) collective-permute-start(bf16[192,384]{1,0:T(8,128)(2,1)S(1)} %get-tuple-element.64), channel_id=1, source_target_pairs={{0,2},{2,0},{4,6},{6,4},{8,10},{10,8},{12,14},{14,12},{16,18},{18,... | collective-permute-start | bytes 442376 | tf_op jit(solution)/shard_map/ppermute | solution.py:439
  30.0 1.5 %collective-permute-start.13 = (bf16[192,384]{1,0:T(8,128)(2,1)S(1)}, bf16[192,384]{1,0:T(8,128)(2,1)S(1)}, u32[]{:S(2)}, u32[]{:S(2)}) collective-permute-start(bf16[192,384]{1,0:T(8,128)(2,1)S(1)} %get-tuple-element.65), channel_id=1, source_target_pairs={{0,4},{2,6},{4,0},{6,2},{8,12},{10,14},{12,8},{14,10},{16,20},{18,... | collective-permute-start | bytes 442376 | tf_op jit(solution)/shard_map/ppermute | solution.py:439
  31.5 0.5 collective-permute-start.14
  32.0 0.0 collective-permute-done.15.refs_1_
  32.0 3.2 %norm_back.1 = (f32[96,128]{1,0:T(8,128)S(1)}, bf16[96,128]{1,0:T(8,128)(2,1)S(1)}, bf16[96,128]{1,0:T(8,128)(2,1)S(1)}, bf16[96,128]{1,0:T(8,128)(2,1)S(1)}, f3...) custom-call(f32[256,768]{1,0:T(8,128)S(1)} %get-tuple-element.68.refs_0_, ...), custom_call_target="tpu_custom_call" | custom-call | flops 110000000 | bytes 4186112 | tf_op jit(solution)/shard_map/norm_back/pallas_call | solution.py:412
  35.2 0.7 %collective-permute-start.16 = (bf16[96,128]{1,0:T(8,128)(2,1)S(1)}, bf16[96,128]{1,0:T(8,128)(2,1)S(1)}, u32[]{:S(2)}, u32[]{:S(2)}) collective-permute-start(bf16[96,128]{1,0:T(8,128)(2,1)S(1)} %get-tuple-element.74), channel_id=1, source_target_pairs={{0,3},{1,2},{2,1},{3,0},{4,7},{5,6},{6,5},{7,4},{8,11},{9,10},{10,... | collective-permute-start | bytes 73736 | tf_op jit(solution)/shard_map/ppermute | solution.py:445
  35.9 2.1 %collective-permute-start.17 = (bf16[96,128]{1,0:T(8,128)(2,1)S(1)}, bf16[96,128]{1,0:T(8,128)(2,1)S(1)}, u32[]{:S(2)}, u32[]{:S(2)}) collective-permute-start(bf16[96,128]{1,0:T(8,128)(2,1)S(1)} %get-tuple-element.75), channel_id=1, source_target_pairs={{0,5},{1,4},{2,7},{3,6},{4,1},{5,0},{6,3},{7,2},{8,13},{9,12},{10,... | collective-permute-start | bytes 73736 | tf_op jit(solution)/shard_map/ppermute | solution.py:445
  38.0 0.0 collective-permute-done.12.refs_1_
  38.0 0.0 collective-permute-start.18
  38.0 0.9 %collective-permute-done.13.refs_2_ = bf16[192,384]{1,0:T(8,128)(2,1)S(1)} collective-permute-done((bf16[192,384]{1,0:T(8,128)(2,1)S(1)}, bf16[192,384]{1,0:T(8,128)(2,1)S(1)}, u32[]{:S(2)}, u32[]{:S(2)}) %collective-permute-start.13) | collective-permute-done | bytes 147488 | tf_op jit(solution)/shard_map/ppermute | solution.py:439
  39.0 0.0 collective-permute-start.19
  39.0 0.0 collective-permute-done.14.refs_3_
  39.0 0.0 collective-permute-done.16.refs_5_
  39.0 0.6 %collective-permute-done.17.refs_6_ = bf16[96,128]{1,0:T(8,128)(2,1)S(1)} collective-permute-done((bf16[96,128]{1,0:T(8,128)(2,1)S(1)}, bf16[96,128]{1,0:T(8,128)(2,1)S(1)}, u32[]{:S(2)}, u32[]{:S(2)}) %collective-permute-start.17) | collective-permute-done | bytes 24608 | tf_op jit(solution)/shard_map/ppermute | solution.py:445
  39.5 2.6 %collective-permute-done.18.refs_7_ = bf16[96,128]{1,0:T(8,128)(2,1)S(1)} collective-permute-done((bf16[96,128]{1,0:T(8,128)(2,1)S(1)}, bf16[96,128]{1,0:T(8,128)(2,1)S(1)}, u32[]{:S(2)}, u32[]{:S(2)}) %collective-permute-start.18) | collective-permute-done | bytes 24608 | tf_op jit(solution)/shard_map/ppermute | solution.py:445
  42.2 0.1 plane_sum.1
  42.3 0.1 collective-permute-start.20
  42.3 3.4 %collective-permute-start.21 = (bf16[48,512]{1,0:T(8,128)(2,1)S(1)}, bf16[48,512]{1,0:T(8,128)(2,1)S(1)}, u32[]{:S(2)}, u32[]{:S(2)}) collective-permute-start(bf16[48,512]{1,0:T(8,128)(2,1)S(1)} %get-tuple-element.83), channel_id=1, source_target_pairs={{0,17},{1,16},{2,19},{3,18},{4,21},{5,20},{6,23},{7,22},{8,25},{9,... | collective-permute-start | bytes 147464 | tf_op jit(solution)/shard_map/ppermute | solution.py:445
  45.7 0.0 collective-permute-start.22
  45.7 0.5 collective-permute-done.19.other_ref
  46.2 2.0 %conv_back.1 = bf16[1,8,16,768]{3,2,1,0:T(8,128)(2,1)} custom-call(f32[6,8,16,128]{3,2,1,0:T(8,128)S(1)} %get-tuple-element.78.grad_ref, bf16[6,8,16,128]{3,2,1,0:T(8,128)(2,1)S(1)} %collective-permute-done.19.other_ref, f32[6,128,128]{2,1,0:T(8,128)S(1)} %get-tuple-element.72.refs_4_.taps_ref), custom_call_target="tpu_custom_call" | custom-call | flops 110000000 | bytes 1179648 | tf_op jit(solution)/shard_map/conv_back/pallas_call | solution.py:412
  48.1 0.0 collective-permute-done.20.refs_1_
  48.1 0.1 collective-permute-done.21.refs_2_
  48.2 3.0 %collective-permute-done.22.refs_3_ = bf16[48,512]{1,0:T(8,128)(2,1)S(1)} collective-permute-done((bf16[48,512]{1,0:T(8,128)(2,1)S(1)}, bf16[48,512]{1,0:T(8,128)(2,1)S(1)}, u32[]{:S(2)}, u32[]{:S(2)}) %collective-permute-start.22) | collective-permute-done | bytes 49184 | tf_op jit(solution)/shard_map/ppermute | solution.py:445
  51.3 0.1 collective-permute-start.23
  51.4 1.5 %collective-permute-done.23.other_ref = f32[48,1280]{1,0:T(8,128)S(1)} collective-permute-done((f32[48,1280]{1,0:T(8,128)S(1)}, f32[48,1280]{1,0:T(8,128)S(1)}, u32[]{:S(2)}, u32[]{:S(2)}) %collective-permute-start.23) | collective-permute-done | bytes 245792 | tf_op jit(solution)/shard_map/ppermute | solution.py:457
  52.9 0.8 %finish.1 = (f32[48,1536]{1,0:T(8,128)}, f32[48,49]{1,0:T(8,128)}, f32[1,48]{1,0:T(1,128)}, f32[1,48]{1,0:T(1,128)}) custom-call(f32[48,1280]{1,0:T(8,128)S(1)} %line_sum.1.mine_ref, f32[48,1280]{1,0:T(8,128)S(1)} %collective-permute-done.23.other_ref), custom_call_target="tpu_custom_call" | custom-call | flops 550000000 | bytes 796224 | tf_op jit(solution)/shard_map/finish/pallas_call | solution.py:412
  (3 shorter events, 0.1 us)
Async XLA Ops:
  0.6 7.1 %copy-start = (bf16[1,8,16,768]{3,2,1,0:T(8,128)(2,1)S(1)}, bf16[1,8,16,768]{3,2,1,0:T(8,128)(2,1)}, u32[]{:S(2)}) copy-start(bf16[1,8,16,768]{3,2,1,0:T(8,128)(2,1)} %param.6) | copy-start | bytes 589828
  0.6 7.1 %copy-start.1 = (bf16[1,8,16,1536]{3,2,1,0:T(8,128)(2,1)S(1)}, bf16[1,8,16,1536]{3,2,1,0:T(8,128)(2,1)}, u32[]{:S(2)}) copy-start(bf16[1,8,16,1536]{3,2,1,0:T(8,128)(2,1)} %param.7) | copy-start | bytes 1179652
  2.4 10.0 %copy-start.2 = (bf16[48,512]{1,0:T(8,128)(2,1)S(1)}, bf16[48,512]{1,0:T(8,128)(2,1)}, u32[]{:S(2)}) copy-start(bf16[48,512]{1,0:T(8,128)(2,1)} %get-tuple-element.50.refs_0_) | copy-start | bytes 147460
  2.4 7.1 %collective-permute-start.1 = (bf16[48,512]{1,0:T(8,128)(2,1)}, bf16[48,512]{1,0:T(8,128)(2,1)S(1)}, u32[]{:S(2)}, u32[]{:S(2)}) collective-permute-start(bf16[48,512]{1,0:T(8,128)(2,1)} %get-tuple-element.52), channel_id=1, source_target_pairs={{0,17},{1,16},{2,19},{3,18},{4,21},{5,20},{6,23},{7,22},{8,25},{9,... | collective-permute-start | bytes 147464 | tf_op jit(solution)/shard_map/ppermute | solution.py:445
  5.9 5.6 %collective-permute-start.2 = (bf16[48,512]{1,0:T(8,128)(2,1)}, bf16[48,512]{1,0:T(8,128)(2,1)S(1)}, u32[]{:S(2)}, u32[]{:S(2)}) collective-permute-start(bf16[48,512]{1,0:T(8,128)(2,1)} %get-tuple-element.51), channel_id=1, source_target_pairs={{0,25},{1,24},{2,27},{3,26},{4,29},{5,28},{6,31},{7,30},{8,17},{9,... | collective-permute-start | bytes 147464 | tf_op jit(solution)/shard_map/ppermute | solution.py:445
  7.5 4.9 %collective-permute-start = (bf16[48,512]{1,0:T(8,128)(2,1)}, bf16[48,512]{1,0:T(8,128)(2,1)S(1)}, u32[]{:S(2)}, u32[]{:S(2)}) collective-permute-start(bf16[48,512]{1,0:T(8,128)(2,1)} %get-tuple-element.51), channel_id=1, source_target_pairs={{0,9},{1,8},{2,11},{3,10},{4,13},{5,12},{6,15},{7,14},{8,1},{9,0},... | collective-permute-start | bytes 147464 | tf_op jit(solution)/shard_map/ppermute | solution.py:445
  7.8 4.7 %collective-permute-start.3 = (bf16[128,768]{1,0:T(8,128)(2,1)S(1)}, bf16[128,768]{1,0:T(8,128)(2,1)S(1)}, u32[]{:S(2)}, u32[]{:S(2)}) collective-permute-start(bf16[128,768]{1,0:T(8,128)(2,1)S(1)} %get-tuple-element.56), channel_id=1, source_target_pairs={{0,1},{1,0},{2,3},{3,2},{4,5},{5,4},{6,7},{7,6},{8,9},{9,8},{10,11... | collective-permute-start | bytes 589832 | tf_op jit(solution)/shard_map/ppermute | solution.py:457
  7.9 13.1 %collective-permute-start.9 = (bf16[256,768]{1,0:T(8,128)(2,1)S(1)}, bf16[256,768]{1,0:T(8,128)(2,1)S(1)}, u32[]{:S(2)}, u32[]{:S(2)}) collective-permute-start(bf16[256,768]{1,0:T(8,128)(2,1)S(1)} %get-tuple-element.59), channel_id=1, source_target_pairs={{0,9},{1,8},{2,11},{3,10},{4,13},{5,12},{6,15},{7,14},{8,1},{9,0},... | collective-permute-start | bytes 1179656 | tf_op jit(solution)/shard_map/ppermute | solution.py:445
  12.5 5.2 %collective-permute-start.4 = (bf16[192,384]{1,0:T(8,128)(2,1)S(1)}, bf16[192,384]{1,0:T(8,128)(2,1)S(1)}, u32[]{:S(2)}, u32[]{:S(2)}) collective-permute-start(bf16[192,384]{1,0:T(8,128)(2,1)S(1)} %get-tuple-element.57.own_ref.refs_0_), channel_id=1, source_target_pairs={{0,2},{1,5},{2,0},{3,7},{4,6},{5,1},{6,4},{7,3},{8,10},{9,13},{10,... | collective-permute-start | bytes 442376 | tf_op jit(solution)/shard_map/ppermute | solution.py:454
  14.0 5.5 %collective-permute-start.8 = (bf16[96,128]{1,0:T(8,128)(2,1)S(1)}, bf16[96,128]{1,0:T(8,128)(2,1)S(1)}, u32[]{:S(2)}, u32[]{:S(2)}) collective-permute-start(bf16[96,128]{1,0:T(8,128)(2,1)S(1)} %get-tuple-element.58.refs_0_), channel_id=1, source_target_pairs={{0,7},{1,6},{2,5},{3,4},{4,3},{5,2},{6,1},{7,0},{8,15},{9,14},{10,... | collective-permute-start | bytes 73736 | tf_op jit(solution)/shard_map/ppermute | solution.py:445
  15.6 4.0 %collective-permute-start.7 = (bf16[96,128]{1,0:T(8,128)(2,1)S(1)}, bf16[96,128]{1,0:T(8,128)(2,1)S(1)}, u32[]{:S(2)}, u32[]{:S(2)}) collective-permute-start(bf16[96,128]{1,0:T(8,128)(2,1)S(1)} %get-tuple-element.58.refs_0_), channel_id=1, source_target_pairs={{0,5},{1,4},{2,7},{3,6},{4,1},{5,0},{6,3},{7,2},{8,13},{9,12},{10,... | collective-permute-start | bytes 73736 | tf_op jit(solution)/shard_map/ppermute | solution.py:445
  15.8 3.8 %collective-permute-start.6 = (bf16[96,128]{1,0:T(8,128)(2,1)S(1)}, bf16[96,128]{1,0:T(8,128)(2,1)S(1)}, u32[]{:S(2)}, u32[]{:S(2)}) collective-permute-start(bf16[96,128]{1,0:T(8,128)(2,1)S(1)} %get-tuple-element.58.refs_0_), channel_id=1, source_target_pairs={{0,3},{1,2},{2,1},{3,0},{4,7},{5,6},{6,5},{7,4},{8,11},{9,10},{10,... | collective-permute-start | bytes 73736 | tf_op jit(solution)/shard_map/ppermute | solution.py:445
  17.7 7.0 %collective-permute-start.5 = (bf16[384,384]{1,0:T(8,128)(2,1)S(1)}, bf16[384,384]{1,0:T(8,128)(2,1)S(1)}, u32[]{:S(2)}, u32[]{:S(2)}) collective-permute-start(bf16[384,384]{1,0:T(8,128)(2,1)S(1)} %join.1), channel_id=1, source_target_pairs={{0,4},{1,3},{2,6},{3,1},{4,0},{5,7},{6,2},{7,5},{8,12},{9,11},{10,... | collective-permute-start | bytes 884744 | tf_op jit(solution)/shard_map/ppermute | solution.py:454
  24.2 1.9 %collective-permute-start.10 = (bf16[256,768]{1,0:T(8,128)(2,1)S(1)}, bf16[256,768]{1,0:T(8,128)(2,1)S(1)}, u32[]{:S(2)}, u32[]{:S(2)}) collective-permute-start(bf16[256,768]{1,0:T(8,128)(2,1)S(1)} %get-tuple-element.60.refs_1_), channel_id=1, source_target_pairs={{0,1},{1,0},{2,3},{3,2},{4,5},{5,4},{6,7},{7,6},{8,9},{9,8},{10,11... | collective-permute-start | bytes 1179656 | tf_op jit(solution)/shard_map/ppermute | solution.py:457
  24.4 1.7 %collective-permute-start.11 = (bf16[128,384]{1,0:T(8,128)(2,1)S(1)}, bf16[128,384]{1,0:T(8,128)(2,1)S(1)}, u32[]{:S(2)}, u32[]{:S(2)}) collective-permute-start(bf16[128,384]{1,0:T(8,128)(2,1)S(1)} %get-tuple-element.62), channel_id=1, source_target_pairs={{0,1},{1,0},{2,3},{3,2},{4,5},{5,4},{6,7},{7,6},{8,9},{9,8},{10,11... | collective-permute-start | bytes 294920 | tf_op jit(solution)/shard_map/ppermute | solution.py:457
  28.3 3.7 %collective-permute-start.15 = (f32[256,768]{1,0:T(8,128)S(1)}, f32[256,768]{1,0:T(8,128)S(1)}, u32[]{:S(2)}, u32[]{:S(2)}) collective-permute-start(f32[256,768]{1,0:T(8,128)S(1)} %get-tuple-element.69), channel_id=1, source_target_pairs={{0,1},{1,0},{2,3},{3,2},{4,5},{5,4},{6,7},{7,6},{8,9},{9,8},{10,11... | collective-permute-start | bytes 2359304 | tf_op jit(solution)/shard_map/ppermute | solution.py:457
  28.5 9.6 %collective-permute-start.12 = (bf16[192,384]{1,0:T(8,128)(2,1)S(1)}, bf16[192,384]{1,0:T(8,128)(2,1)S(1)}, u32[]{:S(2)}, u32[]{:S(2)}) collective-permute-start(bf16[192,384]{1,0:T(8,128)(2,1)S(1)} %get-tuple-element.64), channel_id=1, source_target_pairs={{0,2},{2,0},{4,6},{6,4},{8,10},{10,8},{12,14},{14,12},{16,18},{18,... | collective-permute-start | bytes 442376 | tf_op jit(solution)/shard_map/ppermute | solution.py:439
  30.0 9.0 %collective-permute-start.13 = (bf16[192,384]{1,0:T(8,128)(2,1)S(1)}, bf16[192,384]{1,0:T(8,128)(2,1)S(1)}, u32[]{:S(2)}, u32[]{:S(2)}) collective-permute-start(bf16[192,384]{1,0:T(8,128)(2,1)S(1)} %get-tuple-element.65), channel_id=1, source_target_pairs={{0,4},{2,6},{4,0},{6,2},{8,12},{10,14},{12,8},{14,10},{16,20},{18,... | collective-permute-start | bytes 442376 | tf_op jit(solution)/shard_map/ppermute | solution.py:439
  31.5 7.5 %collective-permute-start.14 = (bf16[192,384]{1,0:T(8,128)(2,1)S(1)}, bf16[192,384]{1,0:T(8,128)(2,1)S(1)}, u32[]{:S(2)}, u32[]{:S(2)}) collective-permute-start(bf16[192,384]{1,0:T(8,128)(2,1)S(1)} %get-tuple-element.66), channel_id=1, source_target_pairs={{0,6},{2,4},{4,2},{6,0},{8,14},{10,12},{12,10},{14,8},{16,22},{18,... | collective-permute-start | bytes 442376 | tf_op jit(solution)/shard_map/ppermute | solution.py:439
  35.2 3.8 %collective-permute-start.16 = (bf16[96,128]{1,0:T(8,128)(2,1)S(1)}, bf16[96,128]{1,0:T(8,128)(2,1)S(1)}, u32[]{:S(2)}, u32[]{:S(2)}) collective-permute-start(bf16[96,128]{1,0:T(8,128)(2,1)S(1)} %get-tuple-element.74), channel_id=1, source_target_pairs={{0,3},{1,2},{2,1},{3,0},{4,7},{5,6},{6,5},{7,4},{8,11},{9,10},{10,... | collective-permute-start | bytes 73736 | tf_op jit(solution)/shard_map/ppermute | solution.py:445
  35.9 3.6 %collective-permute-start.17 = (bf16[96,128]{1,0:T(8,128)(2,1)S(1)}, bf16[96,128]{1,0:T(8,128)(2,1)S(1)}, u32[]{:S(2)}, u32[]{:S(2)}) collective-permute-start(bf16[96,128]{1,0:T(8,128)(2,1)S(1)} %get-tuple-element.75), channel_id=1, source_target_pairs={{0,5},{1,4},{2,7},{3,6},{4,1},{5,0},{6,3},{7,2},{8,13},{9,12},{10,... | collective-permute-start | bytes 73736 | tf_op jit(solution)/shard_map/ppermute | solution.py:445
  38.0 4.2 %collective-permute-start.18 = (bf16[96,128]{1,0:T(8,128)(2,1)S(1)}, bf16[96,128]{1,0:T(8,128)(2,1)S(1)}, u32[]{:S(2)}, u32[]{:S(2)}) collective-permute-start(bf16[96,128]{1,0:T(8,128)(2,1)S(1)} %get-tuple-element.76), channel_id=1, source_target_pairs={{0,7},{1,6},{2,5},{3,4},{4,3},{5,2},{6,1},{7,0},{8,15},{9,14},{10,... | collective-permute-start | bytes 73736 | tf_op jit(solution)/shard_map/ppermute | solution.py:445
  39.0 7.2 %collective-permute-start.19 = (bf16[6,8,16,128]{3,2,1,0:T(8,128)(2,1)S(1)}, bf16[6,8,16,128]{3,2,1,0:T(8,128)(2,1)S(1)}, u32[]{:S(2)}, u32[]{:S(2)}) collective-permute-start(bf16[6,8,16,128]{3,2,1,0:T(8,128)(2,1)S(1)} %get-tuple-element.79), channel_id=1, source_target_pairs={{0,9},{1,8},{2,11},{3,10},{4,13},{5,12},{6,15},{7,14},{8,1},{9,0},... | collective-permute-start | bytes 589832 | tf_op jit(solution)/shard_map/ppermute | solution.py:445
  42.3 5.9 %collective-permute-start.20 = (bf16[48,512]{1,0:T(8,128)(2,1)S(1)}, bf16[48,512]{1,0:T(8,128)(2,1)S(1)}, u32[]{:S(2)}, u32[]{:S(2)}) collective-permute-start(bf16[48,512]{1,0:T(8,128)(2,1)S(1)} %get-tuple-element.82), channel_id=1, source_target_pairs={{0,9},{1,8},{2,11},{3,10},{4,13},{5,12},{6,15},{7,14},{8,1},{9,0},... | collective-permute-start | bytes 147464 | tf_op jit(solution)/shard_map/ppermute | solution.py:445
  42.3 5.9 %collective-permute-start.21 = (bf16[48,512]{1,0:T(8,128)(2,1)S(1)}, bf16[48,512]{1,0:T(8,128)(2,1)S(1)}, u32[]{:S(2)}, u32[]{:S(2)}) collective-permute-start(bf16[48,512]{1,0:T(8,128)(2,1)S(1)} %get-tuple-element.83), channel_id=1, source_target_pairs={{0,17},{1,16},{2,19},{3,18},{4,21},{5,20},{6,23},{7,22},{8,25},{9,... | collective-permute-start | bytes 147464 | tf_op jit(solution)/shard_map/ppermute | solution.py:445
  45.7 5.5 %collective-permute-start.22 = (bf16[48,512]{1,0:T(8,128)(2,1)S(1)}, bf16[48,512]{1,0:T(8,128)(2,1)S(1)}, u32[]{:S(2)}, u32[]{:S(2)}) collective-permute-start(bf16[48,512]{1,0:T(8,128)(2,1)S(1)} %get-tuple-element.84), channel_id=1, source_target_pairs={{0,25},{1,24},{2,27},{3,26},{4,29},{5,28},{6,31},{7,30},{8,17},{9,... | collective-permute-start | bytes 147464 | tf_op jit(solution)/shard_map/ppermute | solution.py:445
  51.3 1.6 %collective-permute-start.23 = (f32[48,1280]{1,0:T(8,128)S(1)}, f32[48,1280]{1,0:T(8,128)S(1)}, u32[]{:S(2)}, u32[]{:S(2)}) collective-permute-start(f32[48,1280]{1,0:T(8,128)S(1)} %line_sum.1.mine_ref), channel_id=1, source_target_pairs={{0,1},{1,0},{2,3},{3,2},{4,5},{5,4},{6,7},{7,6},{8,9},{9,8},{10,11... | collective-permute-start | bytes 737288 | tf_op jit(solution)/shard_map/ppermute | solution.py:457

commit v17 on v16

--- a/solution.py
+++ b/solution.py
@@ -78,6 +78,33 @@
     return sums
 
 
+def tight(own, quarter):
+    return own % (16 * (quarter // LANES)) == 0
+
+
+def with_small(weights, extras):
+    own, quarter = weights.shape
+    if not tight(own, quarter):
+        return jnp.concatenate([weights, extras], axis=1)
+    folded = fold(extras)
+    count = folded.shape[0] * LANES // quarter
+    parts = [folded[at : at + count] for at in range(0, folded.shape[0], count)]
+    return jnp.concatenate([weights, jnp.concatenate(parts, axis=1)], axis=0)
+
+
+def without_small(mixed, own, quarter):
+    if not tight(own, quarter):
+        return mixed[:, :quarter], mixed[:, quarter:]
+    parts = [mixed[own:, at : at + LANES] for at in range(0, quarter, LANES)]
+    return mixed[:own], unfold(jnp.concatenate(parts, axis=0))
+
+
+def mixed_shape(own, quarter):
+    if not tight(own, quarter):
+        return (own, quarter + LANES)
+    return (own + own // 2 * LANES // quarter, quarter)
+
+
 def pack_kernel(w_ref, dw_ref, gain_ref, bias_ref, home_ref, near_ref, far_ref, turned, wide):
     own, hidden = w_ref.shape
     quarter = hidden // 4
@@ -88,21 +115,21 @@
     turned[TAPS + 1 : TAPS + 2, :own] = bias_ref[...].astype(F32)
     wide[...] = jnp.zeros_like(wide)
     wide[:, :TAPS] = dw_ref[...].astype(F32)
-    extras = (wide[...] + turned[...].T[:own]).astype(BF16)
+    extras = wide[...] + turned[...].T[:own]
     kinds = ((home_ref, side, parity), (near_ref, 1 - side, parity), (far_ref, 1 - side, 1 - parity))
     for ref, place, which in kinds:
         start = pl.multiple_of(place * (2 * quarter) + which * quarter, LANES)
-        ref[:, :quarter] = w_ref[:, pl.ds(start, quarter)]
-        ref[:, quarter:] = extras
-
-
-def assemble_kernel(*refs):
+        weights = w_ref[:, pl.ds(start, quarter)].astype(F32)
+        ref[...] = with_small(weights, extras).astype(BF16)
+
+
+def assemble_kernel(own, *refs):
     pieces, (weight_ref, extra_ref) = refs[:-2], refs[-2:]
-    own = pieces[0].shape[0]
     quarter = weight_ref.shape[1]
-    for line, piece in enumerate(pieces):
-        weight_ref[line * own : (line + 1) * own, :] = piece[:, :quarter]
-    extras = jnp.concatenate([piece[:, quarter:].astype(F32) for piece in pieces], axis=0)
+    parts = [without_small(piece[...].astype(F32), own, quarter) for piece in pieces]
+    for line, (weights, _) in enumerate(parts):
+        weight_ref[line * own : (line + 1) * own, :] = weights.astype(BF16)
+    extras = jnp.concatenate([extra for _, extra in parts], axis=0)
     if extra_ref.shape[0] < extras.shape[0]:
         extras = fold(extras)
     extra_ref[...] = extras.astype(BF16)
@@ -122,13 +149,12 @@
         total = pieces[0][rows, :]
         for part in pieces[1:]:
             total = total + part[rows, :].astype(F32)
-        out[:, :quarter] = total.astype(out.dtype)
-        out[:, quarter:] = extras[rows, :].astype(out.dtype)
-
-
-def line_sum_kernel(*refs):
+        out[...] = with_small(total, extras[rows, :]).astype(out.dtype)
+
+
+def line_sum_kernel(own, *refs):
     pieces, total_ref = refs[:-1], refs[-1]
-    quarter = pieces[0].shape[1] - LANES
+    quarter = (total_ref.shape[1] - LANES) // 3
     near, far = None, None
     for line, piece in enumerate(pieces[1:], 1):
         came = piece[...].astype(F32)
@@ -136,10 +162,13 @@
             far = came if far is None else far + came
         else:
             near = came if near is None else near + came
-    total_ref[:, :quarter] = pieces[0][:, :quarter]
-    total_ref[:, quarter : 2 * quarter] = near[:, :quarter]
-    total_ref[:, 2 * quarter : 3 * quarter] = far[:, :quarter]
-    total_ref[:, 3 * quarter :] = pieces[0][:, quarter:] + near[:, quarter:] + far[:, quarter:]
+    home, extras = without_small(pieces[0][...], own, quarter)
+    total_ref[:, :quarter] = home
+    for place, part in ((1, near), (2, far)):
+        weights, more = without_small(part, own, quarter)
+        total_ref[:, place * quarter : (place + 1) * quarter] = weights
+        extras = extras + more
+    total_ref[:, 3 * quarter :] = extras
 
 
 def finish_kernel(factor, mine_ref, other_ref, up_ref, dw_ref, gain_ref, bias_ref):
@@ -476,7 +505,7 @@
     home, near, far = call(
         pack_kernel,
         "pack",
-        [shape((own, quarter + LANES), BF16)] * 3,
+        [shape(mixed_shape(own, quarter), BF16)] * 3,
         [
             pltpu.VMEM((LANES, LANES), F32),
             pltpu.VMEM((own, LANES), F32),
@@ -509,7 +538,7 @@
     rows = lines * own
     folded = rows // 2 if relative else rows
     weight_lines, extra_lines = call(
-        assemble_kernel,
+        functools.partial(assemble_kernel, own),
         "assemble",
         [shape((rows, quarter), BF16), shape((folded, LANES), BF16)],
         [],
@@ -640,7 +669,8 @@
     home, *sent = call(
         functools.partial(plane_sum_kernel, lines),
         "plane_sum",
-        [shape((own, quarter + LANES), F32)] + [shape((own, quarter + LANES), BF16)] * (lines - 1),
+        [shape(mixed_shape(own, quarter), F32)]
+        + [shape(mixed_shape(own, quarter), BF16)] * (lines - 1),
         [],
         2.0,
         pieces[0],
@@ -651,7 +681,7 @@
     home, grad_images = lax.optimization_barrier((home, grad_images))
     came = [crossing(piece, INNER * line) for line, piece in enumerate(sent, 1)]
     (total,) = call(
-        line_sum_kernel,
+        functools.partial(line_sum_kernel, own),
         "line_sum",
         [shape((own, 3 * quarter + LANES), F32)],
         [],

time: 53.8 us -> 53.2 us (0.989)
  waiting for transfers between devices: 15 us -> 14.3 us
    ppermute x14, waiting for transfers between devices: 11 us -> 10.5 us  [crossing(): return lax.ppermute(array, ('shard', 'rep'), pairs)]
  transfers between devices with their start and end apart: 24 -> 24, of which waited for: 12 -> 11; matrix products, arithmetic and copies ran while one was open for 0% -> 0% of each run, Pallas kernels for 16% -> 17%
where the time goes in v17:
time: 53.2 us; the launch traced here: 53 us
  starting transfers between devices  24.3 us (46%)
  waiting for transfers between devices  14.3 us (27%)
  Pallas kernels  13.6 us (26%)
  between operations  0.75 us (1%)
    ppermute x14, starting transfers between devices, crossing(): return lax.ppermute(array, ('shard', 'rep'), pairs)  16.6 us
    pallas_call x13, Pallas kernels, call(): pl.pallas_call(kernel, out_shape=outs, in_specs=[VMEM] * len(args), out_s...  13.6 us
    ppermute x14, waiting for transfers between devices, crossing(): return lax.ppermute(array, ('shard', 'rep'), pairs)  10.5 us
    ppermute x3, starting transfers between devices, over_shard(): return lax.ppermute(array, 'shard', [(i, i ^ flip) for i in range(shards)])  3.5 us
    ppermute x2, starting transfers between devices, hop(): return lax.ppermute(array, ('shard', 'rep'), pairs)  3.4 us
    ppermute x5, waiting for transfers between devices, over_core(): return lax.ppermute(array, 'rep', [(i, i ^ 1) for i in range(reps)])  2.78 us
  transfers between devices with their start and end apart: 24, of which 11 were waited for; matrix products, arithmetic and copies ran while one was open for 0% of the time, Pallas kernels for 17%

profile of v17, /device:TPU:0, one launch (start us, length us, event | category | flops | bytes accessed | tf_op | source)
XLA Modules:
  0.0 53.0 jit_solution(11251959461416672775)
XLA Ops:
  0.6 0.0 copy-start
  0.6 0.0 copy-start.1
  0.7 1.8 %pack.1 = (bf16[56,384]{1,0:T(8,128)(2,1)}, bf16[56,384]{1,0:T(8,128)(2,1)}, bf16[56,384]{1,0:T(8,128)(2,1)}) custom-call(bf16[48,1536]{1,0:T(8,128)(2,1)} %w_ref.1, bf16[48,49]{1,0:T(8,128)(2,1)} %dw_ref.1, bf16[1,48]{1,0:T(2,128)(2,1)} %bitcast.11, bf16[1,48]{1,0:T(2,128)(2,1)} %bitcast.12), custom_call_target="tpu_custom_call" | custom-call | flops 550000000 | bytes 281376 | tf_op jit(solution)/shard_map/pack/pallas_call | solution.py:441
  2.4 3.5 %collective-permute-start.1 = (bf16[56,384]{1,0:T(8,128)(2,1)}, bf16[56,384]{1,0:T(8,128)(2,1)S(1)}, u32[]{:S(2)}, u32[]{:S(2)}) collective-permute-start(bf16[56,384]{1,0:T(8,128)(2,1)} %get-tuple-element.52), channel_id=1, source_target_pairs={{0,17},{1,16},{2,19},{3,18},{4,21},{5,20},{6,23},{7,22},{8,25},{9,... | collective-permute-start | bytes 129032 | tf_op jit(solution)/shard_map/ppermute | solution.py:474
  5.9 1.6 %collective-permute-start.2 = (bf16[56,384]{1,0:T(8,128)(2,1)}, bf16[56,384]{1,0:T(8,128)(2,1)S(1)}, u32[]{:S(2)}, u32[]{:S(2)}) collective-permute-start(bf16[56,384]{1,0:T(8,128)(2,1)} %get-tuple-element.51), channel_id=1, source_target_pairs={{0,25},{1,24},{2,27},{3,26},{4,29},{5,28},{6,31},{7,30},{8,17},{9,... | collective-permute-start | bytes 129032 | tf_op jit(solution)/shard_map/ppermute | solution.py:474
  7.5 0.2 collective-permute-start
  7.8 0.0 copy-done
  7.8 0.0 copy-done.1
  7.8 0.1 collective-permute-start.3
  7.9 1.7 %collective-permute-start.9 = (bf16[256,768]{1,0:T(8,128)(2,1)S(1)}, bf16[256,768]{1,0:T(8,128)(2,1)S(1)}, u32[]{:S(2)}, u32[]{:S(2)}) collective-permute-start(bf16[256,768]{1,0:T(8,128)(2,1)S(1)} %get-tuple-element.59), channel_id=1, source_target_pairs={{0,9},{1,8},{2,11},{3,10},{4,13},{5,12},{6,15},{7,14},{8,1},{9,0},... | collective-permute-start | bytes 1179656 | tf_op jit(solution)/shard_map/ppermute | solution.py:474
  9.6 0.0 collective-permute-done.1.refs_2_
  9.6 1.9 %collective-permute-done.2.refs_3_ = bf16[56,384]{1,0:T(8,128)(2,1)S(1)} collective-permute-done((bf16[56,384]{1,0:T(8,128)(2,1)}, bf16[56,384]{1,0:T(8,128)(2,1)S(1)}, u32[]{:S(2)}, u32[]{:S(2)}) %collective-permute-start.2) | collective-permute-done | bytes 43040 | tf_op jit(solution)/shard_map/ppermute | solution.py:474
  11.5 0.6 %collective-permute-done.refs_1_ = bf16[56,384]{1,0:T(8,128)(2,1)S(1)} collective-permute-done((bf16[56,384]{1,0:T(8,128)(2,1)}, bf16[56,384]{1,0:T(8,128)(2,1)S(1)}, u32[]{:S(2)}, u32[]{:S(2)}) %collective-permute-start) | collective-permute-done | bytes 43040 | tf_op jit(solution)/shard_map/ppermute | solution.py:474
  12.0 0.0 copy-done.2
  12.0 0.1 assemble.1
  12.2 0.0 collective-permute-done.3.refs_4_
  12.2 1.6 %collective-permute-start.4 = (bf16[192,384]{1,0:T(8,128)(2,1)S(1)}, bf16[192,384]{1,0:T(8,128)(2,1)S(1)}, u32[]{:S(2)}, u32[]{:S(2)}) collective-permute-start(bf16[192,384]{1,0:T(8,128)(2,1)S(1)} %get-tuple-element.57.own_ref.refs_0_), channel_id=1, source_target_pairs={{0,2},{1,5},{2,0},{3,7},{4,6},{5,1},{6,4},{7,3},{8,10},{9,13},{10,... | collective-permute-start | bytes 442376 | tf_op jit(solution)/shard_map/ppermute | solution.py:483
  13.8 1.7 %collective-permute-start.8 = (bf16[96,128]{1,0:T(8,128)(2,1)S(1)}, bf16[96,128]{1,0:T(8,128)(2,1)S(1)}, u32[]{:S(2)}, u32[]{:S(2)}) collective-permute-start(bf16[96,128]{1,0:T(8,128)(2,1)S(1)} %get-tuple-element.58.refs_0_), channel_id=1, source_target_pairs={{0,7},{1,6},{2,5},{3,4},{4,3},{5,2},{6,1},{7,0},{8,15},{9,14},{10,... | collective-permute-start | bytes 73736 | tf_op jit(solution)/shard_map/ppermute | solution.py:474
  15.5 0.0 collective-permute-start.7
  15.5 1.8 %collective-permute-start.6 = (bf16[96,128]{1,0:T(8,128)(2,1)S(1)}, bf16[96,128]{1,0:T(8,128)(2,1)S(1)}, u32[]{:S(2)}, u32[]{:S(2)}) collective-permute-start(bf16[96,128]{1,0:T(8,128)(2,1)S(1)} %get-tuple-element.58.refs_0_), channel_id=1, source_target_pairs={{0,3},{1,2},{2,1},{3,0},{4,7},{5,6},{6,5},{7,4},{8,11},{9,10},{10,... | collective-permute-start | bytes 73736 | tf_op jit(solution)/shard_map/ppermute | solution.py:474
  17.2 0.2 collective-permute-done.4.came_ref.refs_1_
  17.4 1.8 %collective-permute-start.5 = (bf16[384,384]{1,0:T(8,128)(2,1)S(1)}, bf16[384,384]{1,0:T(8,128)(2,1)S(1)}, u32[]{:S(2)}, u32[]{:S(2)}) collective-permute-start(bf16[384,384]{1,0:T(8,128)(2,1)S(1)} %join.1), channel_id=1, source_target_pairs={{0,4},{1,3},{2,6},{3,1},{4,0},{5,7},{6,2},{7,5},{8,12},{9,11},{10,... | collective-permute-start | bytes 884744 | tf_op jit(solution)/shard_map/ppermute | solution.py:483
  19.3 0.0 collective-permute-done.8.refs_3_
  19.3 0.0 collective-permute-done.7.refs_2_
  19.3 0.0 collective-permute-done.6.refs_1_
  19.3 1.4 %collective-permute-done.9.refs_5_.refs_6_ = bf16[256,768]{1,0:T(8,128)(2,1)S(1)} collective-permute-done((bf16[256,768]{1,0:T(8,128)(2,1)S(1)}, bf16[256,768]{1,0:T(8,128)(2,1)S(1)}, u32[]{:S(2)}, u32[]{:S(2)}) %collective-permute-start.9) | collective-permute-done | bytes 393248 | tf_op jit(solution)/shard_map/ppermute | solution.py:474
  20.7 3.2 %conv_norm.1 = (bf16[256,768]{1,0:T(8,128)(2,1)S(1)}, f32[256,768]{1,0:T(8,128)S(1)}, f32[256,128]{1,0:T(8,128)S(1)}, f32[6,128,128]{2,1,0:T(8,128)S(1)}, bf16[128,384]{1,0:T(8,128)(2,1)S(1)}) custom-call(bf16[96,128]{1,0:T(8,128)(2,1)S(1)} %get-tuple-element.58.refs_0_, bf16[96,128]{1,0:T(8,128)(2,1)S(1)} %collective-permute-done.6.refs_1_, ...), custom_call_target="tpu_custom_call" | custom-call | flops 110000000 | bytes 2490368 | tf_op jit(solution)/shard_map/conv_norm/pallas_call | solution.py:441
  24.0 0.2 collective-permute-start.10
  24.2 0.4 collective-permute-start.11
  24.6 0.0 collective-permute-done.5.refs_2_
  24.6 0.1 order.1.refs_0_.weight
  24.6 1.3 %collective-permute-done.11.refs_6_ = bf16[128,384]{1,0:T(8,128)(2,1)S(1)} collective-permute-done((bf16[128,384]{1,0:T(8,128)(2,1)S(1)}, bf16[128,384]{1,0:T(8,128)(2,1)S(1)}, u32[]{:S(2)}, u32[]{:S(2)}) %collective-permute-start.11) | collective-permute-done | bytes 98336 | tf_op jit(solution)/shard_map/ppermute | solution.py:486
  25.9 0.0 collective-permute-done.10.refs_2_
  25.9 1.5 %project.1 = (f32[192,384]{1,0:T(8,128)S(1)}, bf16[192,384]{1,0:T(8,128)(2,1)S(1)}, bf16[192,384]{1,0:T(8,128)(2,1)S(1)}, bf16[192,384]{1,0:T(8,128)(2,1)S(1)}, bf16[512,384]{1,0:T(8,128)(2,1)S(1)}) custom-call(bf16[768,384]{1,0:T(8,128)(2,1)S(1)} %order.1.refs_0_.weight, bf16[256,768]{1,0:T(8,128)(2,1)S(1)} %get-tuple-element.60.refs_1_, ...), custom_call_target="tpu_custom_call" | custom-call | flops 1760000000 | bytes 3588096 | tf_op jit(solution)/shard_map/project/pallas_call | solution.py:441
  27.4 0.6 %back_project.1 = (f32[256,768]{1,0:T(8,128)S(1)}, f32[256,768]{1,0:T(8,128)S(1)}) custom-call(bf16[768,384]{1,0:T(8,128)(2,1)S(1)} %order.1.refs_0_.weight, bf16[512,384]{1,0:T(8,128)(2,1)S(1)} %get-tuple-element.67.gp_ref), custom_call_target="tpu_custom_call" | custom-call | flops 770000000 | bytes 2555904 | tf_op jit(solution)/shard_map/back_project/pallas_call | solution.py:441
  28.0 0.2 collective-permute-start.15
  28.2 1.5 %collective-permute-start.12 = (bf16[192,384]{1,0:T(8,128)(2,1)S(1)}, bf16[192,384]{1,0:T(8,128)(2,1)S(1)}, u32[]{:S(2)}, u32[]{:S(2)}) collective-permute-start(bf16[192,384]{1,0:T(8,128)(2,1)S(1)} %get-tuple-element.64), channel_id=1, source_target_pairs={{0,2},{2,0},{4,6},{6,4},{8,10},{10,8},{12,14},{14,12},{16,18},{18,... | collective-permute-start | bytes 442376 | tf_op jit(solution)/shard_map/ppermute | solution.py:468
  29.8 1.5 %collective-permute-start.13 = (bf16[192,384]{1,0:T(8,128)(2,1)S(1)}, bf16[192,384]{1,0:T(8,128)(2,1)S(1)}, u32[]{:S(2)}, u32[]{:S(2)}) collective-permute-start(bf16[192,384]{1,0:T(8,128)(2,1)S(1)} %get-tuple-element.65), channel_id=1, source_target_pairs={{0,4},{2,6},{4,0},{6,2},{8,12},{10,14},{12,8},{14,10},{16,20},{18,... | collective-permute-start | bytes 442376 | tf_op jit(solution)/shard_map/ppermute | solution.py:468
  31.3 0.5 collective-permute-start.14
  31.7 0.0 collective-permute-done.15.refs_1_
  31.8 3.2 %norm_back.1 = (f32[96,128]{1,0:T(8,128)S(1)}, bf16[96,128]{1,0:T(8,128)(2,1)S(1)}, bf16[96,128]{1,0:T(8,128)(2,1)S(1)}, bf16[96,128]{1,0:T(8,128)(2,1)S(1)}, f3...) custom-call(f32[256,768]{1,0:T(8,128)S(1)} %get-tuple-element.68.refs_0_, ...), custom_call_target="tpu_custom_call" | custom-call | flops 110000000 | bytes 4186112 | tf_op jit(solution)/shard_map/norm_back/pallas_call | solution.py:441
  35.0 0.7 %collective-permute-start.16 = (bf16[96,128]{1,0:T(8,128)(2,1)S(1)}, bf16[96,128]{1,0:T(8,128)(2,1)S(1)}, u32[]{:S(2)}, u32[]{:S(2)}) collective-permute-start(bf16[96,128]{1,0:T(8,128)(2,1)S(1)} %get-tuple-element.74), channel_id=1, source_target_pairs={{0,3},{1,2},{2,1},{3,0},{4,7},{5,6},{6,5},{7,4},{8,11},{9,10},{10,... | collective-permute-start | bytes 73736 | tf_op jit(solution)/shard_map/ppermute | solution.py:474
  35.7 2.1 %collective-permute-start.17 = (bf16[96,128]{1,0:T(8,128)(2,1)S(1)}, bf16[96,128]{1,0:T(8,128)(2,1)S(1)}, u32[]{:S(2)}, u32[]{:S(2)}) collective-permute-start(bf16[96,128]{1,0:T(8,128)(2,1)S(1)} %get-tuple-element.75), channel_id=1, source_target_pairs={{0,5},{1,4},{2,7},{3,6},{4,1},{5,0},{6,3},{7,2},{8,13},{9,12},{10,... | collective-permute-start | bytes 73736 | tf_op jit(solution)/shard_map/ppermute | solution.py:474
  37.8 0.0 collective-permute-done.12.refs_1_
  37.8 0.0 collective-permute-start.18
  37.8 0.9 %collective-permute-done.13.refs_2_ = bf16[192,384]{1,0:T(8,128)(2,1)S(1)} collective-permute-done((bf16[192,384]{1,0:T(8,128)(2,1)S(1)}, bf16[192,384]{1,0:T(8,128)(2,1)S(1)}, u32[]{:S(2)}, u32[]{:S(2)}) %collective-permute-start.13) | collective-permute-done | bytes 147488 | tf_op jit(solution)/shard_map/ppermute | solution.py:468
  38.8 0.0 collective-permute-start.19
  38.8 0.0 collective-permute-done.14.refs_3_
  38.8 0.0 collective-permute-done.16.refs_5_
  38.8 0.6 %collective-permute-done.17.refs_6_ = bf16[96,128]{1,0:T(8,128)(2,1)S(1)} collective-permute-done((bf16[96,128]{1,0:T(8,128)(2,1)S(1)}, bf16[96,128]{1,0:T(8,128)(2,1)S(1)}, u32[]{:S(2)}, u32[]{:S(2)}) %collective-permute-start.17) | collective-permute-done | bytes 24608 | tf_op jit(solution)/shard_map/ppermute | solution.py:474
  39.3 2.6 %collective-permute-done.18.refs_7_ = bf16[96,128]{1,0:T(8,128)(2,1)S(1)} collective-permute-done((bf16[96,128]{1,0:T(8,128)(2,1)S(1)}, bf16[96,128]{1,0:T(8,128)(2,1)S(1)}, u32[]{:S(2)}, u32[]{:S(2)}) %collective-permute-start.18) | collective-permute-done | bytes 24608 | tf_op jit(solution)/shard_map/ppermute | solution.py:474
  42.0 0.2 plane_sum.1
  42.1 0.0 collective-permute-start.20
  42.2 3.1 %collective-permute-start.21 = (bf16[56,384]{1,0:T(8,128)(2,1)S(1)}, bf16[56,384]{1,0:T(8,128)(2,1)S(1)}, u32[]{:S(2)}, u32[]{:S(2)}) collective-permute-start(bf16[56,384]{1,0:T(8,128)(2,1)S(1)} %get-tuple-element.83), channel_id=1, source_target_pairs={{0,17},{1,16},{2,19},{3,18},{4,21},{5,20},{6,23},{7,22},{8,25},{9,... | collective-permute-start | bytes 129032 | tf_op jit(solution)/shard_map/ppermute | solution.py:474
  45.3 0.1 collective-permute-start.22
  45.4 0.6 %collective-permute-done.19.other_ref = bf16[6,8,16,128]{3,2,1,0:T(8,128)(2,1)S(1)} collective-permute-done((bf16[6,8,16,128]{3,2,1,0:T(8,128)(2,1)S(1)}, bf16[6,8,16,128]{3,2,1,0:T(8,128)(2,1)S(1)}, u32[]{:S(2)}, u32[]{:S(2)}) %collective-permute-start.19) | collective-permute-done | bytes 196640 | tf_op jit(solution)/shard_map/ppermute | solution.py:474
  45.9 2.0 %conv_back.1 = bf16[1,8,16,768]{3,2,1,0:T(8,128)(2,1)} custom-call(f32[6,8,16,128]{3,2,1,0:T(8,128)S(1)} %get-tuple-element.78.grad_ref, bf16[6,8,16,128]{3,2,1,0:T(8,128)(2,1)S(1)} %collective-permute-done.19.other_ref, f32[6,128,128]{2,1,0:T(8,128)S(1)} %get-tuple-element.72.refs_4_.taps_ref), custom_call_target="tpu_custom_call" | custom-call | flops 110000000 | bytes 1179648 | tf_op jit(solution)/shard_map/conv_back/pallas_call | solution.py:441
  47.9 0.0 collective-permute-done.20.refs_1_
  47.9 0.0 collective-permute-done.21.refs_2_
  47.9 2.7 %collective-permute-done.22.refs_3_ = bf16[56,384]{1,0:T(8,128)(2,1)S(1)} collective-permute-done((bf16[56,384]{1,0:T(8,128)(2,1)S(1)}, bf16[56,384]{1,0:T(8,128)(2,1)S(1)}, u32[]{:S(2)}, u32[]{:S(2)}) %collective-permute-start.22) | collective-permute-done | bytes 43040 | tf_op jit(solution)/shard_map/ppermute | solution.py:474
  50.7 0.1 line_sum.1.mine_ref
  50.8 0.0 collective-permute-start.23
  50.8 1.5 %collective-permute-done.23.other_ref = f32[48,1280]{1,0:T(8,128)S(1)} collective-permute-done((f32[48,1280]{1,0:T(8,128)S(1)}, f32[48,1280]{1,0:T(8,128)S(1)}, u32[]{:S(2)}, u32[]{:S(2)}) %collective-permute-start.23) | collective-permute-done | bytes 245792 | tf_op jit(solution)/shard_map/ppermute | solution.py:486
  52.3 0.8 %finish.1 = (f32[48,1536]{1,0:T(8,128)}, f32[48,49]{1,0:T(8,128)}, f32[1,48]{1,0:T(1,128)}, f32[1,48]{1,0:T(1,128)}) custom-call(f32[48,1280]{1,0:T(8,128)S(1)} %line_sum.1.mine_ref, f32[48,1280]{1,0:T(8,128)S(1)} %collective-permute-done.23.other_ref), custom_call_target="tpu_custom_call" | custom-call | flops 550000000 | bytes 796224 | tf_op jit(solution)/shard_map/finish/pallas_call | solution.py:441
  (3 shorter events, 0.1 us)
Async XLA Ops:
  0.6 7.1 %copy-start = (bf16[1,8,16,768]{3,2,1,0:T(8,128)(2,1)S(1)}, bf16[1,8,16,768]{3,2,1,0:T(8,128)(2,1)}, u32[]{:S(2)}) copy-start(bf16[1,8,16,768]{3,2,1,0:T(8,128)(2,1)} %param.6) | copy-start | bytes 589828
  0.6 7.1 %copy-start.1 = (bf16[1,8,16,1536]{3,2,1,0:T(8,128)(2,1)S(1)}, bf16[1,8,16,1536]{3,2,1,0:T(8,128)(2,1)}, u32[]{:S(2)}) copy-start(bf16[1,8,16,1536]{3,2,1,0:T(8,128)(2,1)} %param.7) | copy-start | bytes 1179652
  2.4 9.6 %copy-start.2 = (bf16[56,384]{1,0:T(8,128)(2,1)S(1)}, bf16[56,384]{1,0:T(8,128)(2,1)}, u32[]{:S(2)}) copy-start(bf16[56,384]{1,0:T(8,128)(2,1)} %get-tuple-element.50.refs_0_) | copy-start | bytes 129028
  2.4 7.1 %collective-permute-start.1 = (bf16[56,384]{1,0:T(8,128)(2,1)}, bf16[56,384]{1,0:T(8,128)(2,1)S(1)}, u32[]{:S(2)}, u32[]{:S(2)}) collective-permute-start(bf16[56,384]{1,0:T(8,128)(2,1)} %get-tuple-element.52), channel_id=1, source_target_pairs={{0,17},{1,16},{2,19},{3,18},{4,21},{5,20},{6,23},{7,22},{8,25},{9,... | collective-permute-start | bytes 129032 | tf_op jit(solution)/shard_map/ppermute | solution.py:474
  5.9 5.6 %collective-permute-start.2 = (bf16[56,384]{1,0:T(8,128)(2,1)}, bf16[56,384]{1,0:T(8,128)(2,1)S(1)}, u32[]{:S(2)}, u32[]{:S(2)}) collective-permute-start(bf16[56,384]{1,0:T(8,128)(2,1)} %get-tuple-element.51), channel_id=1, source_target_pairs={{0,25},{1,24},{2,27},{3,26},{4,29},{5,28},{6,31},{7,30},{8,17},{9,... | collective-permute-start | bytes 129032 | tf_op jit(solution)/shard_map/ppermute | solution.py:474
  7.5 4.5 %collective-permute-start = (bf16[56,384]{1,0:T(8,128)(2,1)}, bf16[56,384]{1,0:T(8,128)(2,1)S(1)}, u32[]{:S(2)}, u32[]{:S(2)}) collective-permute-start(bf16[56,384]{1,0:T(8,128)(2,1)} %get-tuple-element.51), channel_id=1, source_target_pairs={{0,9},{1,8},{2,11},{3,10},{4,13},{5,12},{6,15},{7,14},{8,1},{9,0},... | collective-permute-start | bytes 129032 | tf_op jit(solution)/shard_map/ppermute | solution.py:474
  7.8 4.4 %collective-permute-start.3 = (bf16[128,768]{1,0:T(8,128)(2,1)S(1)}, bf16[128,768]{1,0:T(8,128)(2,1)S(1)}, u32[]{:S(2)}, u32[]{:S(2)}) collective-permute-start(bf16[128,768]{1,0:T(8,128)(2,1)S(1)} %get-tuple-element.56), channel_id=1, source_target_pairs={{0,1},{1,0},{2,3},{3,2},{4,5},{5,4},{6,7},{7,6},{8,9},{9,8},{10,11... | collective-permute-start | bytes 589832 | tf_op jit(solution)/shard_map/ppermute | solution.py:486
  7.9 12.8 %collective-permute-start.9 = (bf16[256,768]{1,0:T(8,128)(2,1)S(1)}, bf16[256,768]{1,0:T(8,128)(2,1)S(1)}, u32[]{:S(2)}, u32[]{:S(2)}) collective-permute-start(bf16[256,768]{1,0:T(8,128)(2,1)S(1)} %get-tuple-element.59), channel_id=1, source_target_pairs={{0,9},{1,8},{2,11},{3,10},{4,13},{5,12},{6,15},{7,14},{8,1},{9,0},... | collective-permute-start | bytes 1179656 | tf_op jit(solution)/shard_map/ppermute | solution.py:474
  12.2 5.2 %collective-permute-start.4 = (bf16[192,384]{1,0:T(8,128)(2,1)S(1)}, bf16[192,384]{1,0:T(8,128)(2,1)S(1)}, u32[]{:S(2)}, u32[]{:S(2)}) collective-permute-start(bf16[192,384]{1,0:T(8,128)(2,1)S(1)} %get-tuple-element.57.own_ref.refs_0_), channel_id=1, source_target_pairs={{0,2},{1,5},{2,0},{3,7},{4,6},{5,1},{6,4},{7,3},{8,10},{9,13},{10,... | collective-permute-start | bytes 442376 | tf_op jit(solution)/shard_map/ppermute | solution.py:483
  13.8 5.5 %collective-permute-start.8 = (bf16[96,128]{1,0:T(8,128)(2,1)S(1)}, bf16[96,128]{1,0:T(8,128)(2,1)S(1)}, u32[]{:S(2)}, u32[]{:S(2)}) collective-permute-start(bf16[96,128]{1,0:T(8,128)(2,1)S(1)} %get-tuple-element.58.refs_0_), channel_id=1, source_target_pairs={{0,7},{1,6},{2,5},{3,4},{4,3},{5,2},{6,1},{7,0},{8,15},{9,14},{10,... | collective-permute-start | bytes 73736 | tf_op jit(solution)/shard_map/ppermute | solution.py:474
  15.5 3.8 %collective-permute-start.7 = (bf16[96,128]{1,0:T(8,128)(2,1)S(1)}, bf16[96,128]{1,0:T(8,128)(2,1)S(1)}, u32[]{:S(2)}, u32[]{:S(2)}) collective-permute-start(bf16[96,128]{1,0:T(8,128)(2,1)S(1)} %get-tuple-element.58.refs_0_), channel_id=1, source_target_pairs={{0,5},{1,4},{2,7},{3,6},{4,1},{5,0},{6,3},{7,2},{8,13},{9,12},{10,... | collective-permute-start | bytes 73736 | tf_op jit(solution)/shard_map/ppermute | solution.py:474
  15.5 3.8 %collective-permute-start.6 = (bf16[96,128]{1,0:T(8,128)(2,1)S(1)}, bf16[96,128]{1,0:T(8,128)(2,1)S(1)}, u32[]{:S(2)}, u32[]{:S(2)}) collective-permute-start(bf16[96,128]{1,0:T(8,128)(2,1)S(1)} %get-tuple-element.58.refs_0_), channel_id=1, source_target_pairs={{0,3},{1,2},{2,1},{3,0},{4,7},{5,6},{6,5},{7,4},{8,11},{9,10},{10,... | collective-permute-start | bytes 73736 | tf_op jit(solution)/shard_map/ppermute | solution.py:474
  17.4 7.1 %collective-permute-start.5 = (bf16[384,384]{1,0:T(8,128)(2,1)S(1)}, bf16[384,384]{1,0:T(8,128)(2,1)S(1)}, u32[]{:S(2)}, u32[]{:S(2)}) collective-permute-start(bf16[384,384]{1,0:T(8,128)(2,1)S(1)} %join.1), channel_id=1, source_target_pairs={{0,4},{1,3},{2,6},{3,1},{4,0},{5,7},{6,2},{7,5},{8,12},{9,11},{10,... | collective-permute-start | bytes 884744 | tf_op jit(solution)/shard_map/ppermute | solution.py:483
  24.0 1.9 %collective-permute-start.10 = (bf16[256,768]{1,0:T(8,128)(2,1)S(1)}, bf16[256,768]{1,0:T(8,128)(2,1)S(1)}, u32[]{:S(2)}, u32[]{:S(2)}) collective-permute-start(bf16[256,768]{1,0:T(8,128)(2,1)S(1)} %get-tuple-element.60.refs_1_), channel_id=1, source_target_pairs={{0,1},{1,0},{2,3},{3,2},{4,5},{5,4},{6,7},{7,6},{8,9},{9,8},{10,11... | collective-permute-start | bytes 1179656 | tf_op jit(solution)/shard_map/ppermute | solution.py:486
  24.2 1.7 %collective-permute-start.11 = (bf16[128,384]{1,0:T(8,128)(2,1)S(1)}, bf16[128,384]{1,0:T(8,128)(2,1)S(1)}, u32[]{:S(2)}, u32[]{:S(2)}) collective-permute-start(bf16[128,384]{1,0:T(8,128)(2,1)S(1)} %get-tuple-element.62), channel_id=1, source_target_pairs={{0,1},{1,0},{2,3},{3,2},{4,5},{5,4},{6,7},{7,6},{8,9},{9,8},{10,11... | collective-permute-start | bytes 294920 | tf_op jit(solution)/shard_map/ppermute | solution.py:486
  28.0 3.7 %collective-permute-start.15 = (f32[256,768]{1,0:T(8,128)S(1)}, f32[256,768]{1,0:T(8,128)S(1)}, u32[]{:S(2)}, u32[]{:S(2)}) collective-permute-start(f32[256,768]{1,0:T(8,128)S(1)} %get-tuple-element.69), channel_id=1, source_target_pairs={{0,1},{1,0},{2,3},{3,2},{4,5},{5,4},{6,7},{7,6},{8,9},{9,8},{10,11... | collective-permute-start | bytes 2359304 | tf_op jit(solution)/shard_map/ppermute | solution.py:486
  28.2 9.6 %collective-permute-start.12 = (bf16[192,384]{1,0:T(8,128)(2,1)S(1)}, bf16[192,384]{1,0:T(8,128)(2,1)S(1)}, u32[]{:S(2)}, u32[]{:S(2)}) collective-permute-start(bf16[192,384]{1,0:T(8,128)(2,1)S(1)} %get-tuple-element.64), channel_id=1, source_target_pairs={{0,2},{2,0},{4,6},{6,4},{8,10},{10,8},{12,14},{14,12},{16,18},{18,... | collective-permute-start | bytes 442376 | tf_op jit(solution)/shard_map/ppermute | solution.py:468
  29.8 9.0 %collective-permute-start.13 = (bf16[192,384]{1,0:T(8,128)(2,1)S(1)}, bf16[192,384]{1,0:T(8,128)(2,1)S(1)}, u32[]{:S(2)}, u32[]{:S(2)}) collective-permute-start(bf16[192,384]{1,0:T(8,128)(2,1)S(1)} %get-tuple-element.65), channel_id=1, source_target_pairs={{0,4},{2,6},{4,0},{6,2},{8,12},{10,14},{12,8},{14,10},{16,20},{18,... | collective-permute-start | bytes 442376 | tf_op jit(solution)/shard_map/ppermute | solution.py:468
  31.3 7.5 %collective-permute-start.14 = (bf16[192,384]{1,0:T(8,128)(2,1)S(1)}, bf16[192,384]{1,0:T(8,128)(2,1)S(1)}, u32[]{:S(2)}, u32[]{:S(2)}) collective-permute-start(bf16[192,384]{1,0:T(8,128)(2,1)S(1)} %get-tuple-element.66), channel_id=1, source_target_pairs={{0,6},{2,4},{4,2},{6,0},{8,14},{10,12},{12,10},{14,8},{16,22},{18,... | collective-permute-start | bytes 442376 | tf_op jit(solution)/shard_map/ppermute | solution.py:468
  35.0 3.8 %collective-permute-start.16 = (bf16[96,128]{1,0:T(8,128)(2,1)S(1)}, bf16[96,128]{1,0:T(8,128)(2,1)S(1)}, u32[]{:S(2)}, u32[]{:S(2)}) collective-permute-start(bf16[96,128]{1,0:T(8,128)(2,1)S(1)} %get-tuple-element.74), channel_id=1, source_target_pairs={{0,3},{1,2},{2,1},{3,0},{4,7},{5,6},{6,5},{7,4},{8,11},{9,10},{10,... | collective-permute-start | bytes 73736 | tf_op jit(solution)/shard_map/ppermute | solution.py:474
  35.7 3.6 %collective-permute-start.17 = (bf16[96,128]{1,0:T(8,128)(2,1)S(1)}, bf16[96,128]{1,0:T(8,128)(2,1)S(1)}, u32[]{:S(2)}, u32[]{:S(2)}) collective-permute-start(bf16[96,128]{1,0:T(8,128)(2,1)S(1)} %get-tuple-element.75), channel_id=1, source_target_pairs={{0,5},{1,4},{2,7},{3,6},{4,1},{5,0},{6,3},{7,2},{8,13},{9,12},{10,... | collective-permute-start | bytes 73736 | tf_op jit(solution)/shard_map/ppermute | solution.py:474
  37.8 4.2 %collective-permute-start.18 = (bf16[96,128]{1,0:T(8,128)(2,1)S(1)}, bf16[96,128]{1,0:T(8,128)(2,1)S(1)}, u32[]{:S(2)}, u32[]{:S(2)}) collective-permute-start(bf16[96,128]{1,0:T(8,128)(2,1)S(1)} %get-tuple-element.76), channel_id=1, source_target_pairs={{0,7},{1,6},{2,5},{3,4},{4,3},{5,2},{6,1},{7,0},{8,15},{9,14},{10,... | collective-permute-start | bytes 73736 | tf_op jit(solution)/shard_map/ppermute | solution.py:474
  38.8 7.2 %collective-permute-start.19 = (bf16[6,8,16,128]{3,2,1,0:T(8,128)(2,1)S(1)}, bf16[6,8,16,128]{3,2,1,0:T(8,128)(2,1)S(1)}, u32[]{:S(2)}, u32[]{:S(2)}) collective-permute-start(bf16[6,8,16,128]{3,2,1,0:T(8,128)(2,1)S(1)} %get-tuple-element.79), channel_id=1, source_target_pairs={{0,9},{1,8},{2,11},{3,10},{4,13},{5,12},{6,15},{7,14},{8,1},{9,0},... | collective-permute-start | bytes 589832 | tf_op jit(solution)/shard_map/ppermute | solution.py:474
  42.1 5.8 %collective-permute-start.20 = (bf16[56,384]{1,0:T(8,128)(2,1)S(1)}, bf16[56,384]{1,0:T(8,128)(2,1)S(1)}, u32[]{:S(2)}, u32[]{:S(2)}) collective-permute-start(bf16[56,384]{1,0:T(8,128)(2,1)S(1)} %get-tuple-element.82), channel_id=1, source_target_pairs={{0,9},{1,8},{2,11},{3,10},{4,13},{5,12},{6,15},{7,14},{8,1},{9,0},... | collective-permute-start | bytes 129032 | tf_op jit(solution)/shard_map/ppermute | solution.py:474
  42.2 5.8 %collective-permute-start.21 = (bf16[56,384]{1,0:T(8,128)(2,1)S(1)}, bf16[56,384]{1,0:T(8,128)(2,1)S(1)}, u32[]{:S(2)}, u32[]{:S(2)}) collective-permute-start(bf16[56,384]{1,0:T(8,128)(2,1)S(1)} %get-tuple-element.83), channel_id=1, source_target_pairs={{0,17},{1,16},{2,19},{3,18},{4,21},{5,20},{6,23},{7,22},{8,25},{9,... | collective-permute-start | bytes 129032 | tf_op jit(solution)/shard_map/ppermute | solution.py:474
  45.3 5.4 %collective-permute-start.22 = (bf16[56,384]{1,0:T(8,128)(2,1)S(1)}, bf16[56,384]{1,0:T(8,128)(2,1)S(1)}, u32[]{:S(2)}, u32[]{:S(2)}) collective-permute-start(bf16[56,384]{1,0:T(8,128)(2,1)S(1)} %get-tuple-element.84), channel_id=1, source_target_pairs={{0,25},{1,24},{2,27},{3,26},{4,29},{5,28},{6,31},{7,30},{8,17},{9,... | collective-permute-start | bytes 129032 | tf_op jit(solution)/shard_map/ppermute | solution.py:474
  50.8 1.5 %collective-permute-start.23 = (f32[48,1280]{1,0:T(8,128)S(1)}, f32[48,1280]{1,0:T(8,128)S(1)}, u32[]{:S(2)}, u32[]{:S(2)}) collective-permute-start(f32[48,1280]{1,0:T(8,128)S(1)} %line_sum.1.mine_ref), channel_id=1, source_target_pairs={{0,1},{1,0},{2,3},{3,2},{4,5},{5,4},{6,7},{7,6},{8,9},{9,8},{10,11... | collective-permute-start | bytes 737288 | tf_op jit(solution)/shard_map/ppermute | solution.py:486

commit v18 on v17

--- a/solution.py
+++ b/solution.py
@@ -205,17 +205,52 @@
     padded[..., 8 + breadth :, :] = jnp.zeros(shape, F32)
 
 
+def conv_norm_image(source, taps_ref, outs, padded, conv, height, breadth):
+    normed_ref, white_ref, inv_ref = outs
+    pixels, depth = normed_ref.shape
+    tiles = depth // LANES
+    clear_borders(padded, breadth)
+    for tile in range(tiles):
+        lanes = slice(tile * LANES, (tile + 1) * LANES)
+        part = source[:pixels, lanes].astype(F32)
+        padded[tile, :, 8 : 8 + breadth, :] = part.reshape(height, breadth, LANES)
+
+    def one_tile(tile, carry):
+        sums = correlate(
+            padded,
+            tile,
+            lambda down, across: taps_ref[tile, pl.ds(down * KS + across, 1), :],
+            height,
+            breadth,
+        )
+        for line in range(height):
+            conv[tile, line * breadth : (line + 1) * breadth, :] = sums[line]
+        return carry
+
+    lax.fori_loop(0, tiles, one_tile, 0)
+    total = conv[0]
+    for tile in range(1, tiles):
+        total = total + conv[tile]
+    average = jnp.sum(total, axis=-1, keepdims=True) / depth
+    squares = None
+    for tile in range(tiles):
+        centered = conv[tile] - average
+        squares = centered * centered if squares is None else squares + centered * centered
+    variance = jnp.sum(squares, axis=-1, keepdims=True) / depth
+    inv_std = lax.rsqrt(variance + NORM_EPS)
+    inv_ref[...] = jnp.broadcast_to(inv_std, (pixels, LANES))
+    for tile in range(tiles):
+        lanes = slice(tile * LANES, (tile + 1) * LANES)
+        whitened = (conv[tile] - average) * inv_std
+        white_ref[:, lanes] = whitened
+        gain = taps_ref[tile, TAPS : TAPS + 1, :]
+        bias = taps_ref[tile, TAPS + 1 : TAPS + 2, :]
+        normed_ref[:, lanes] = (whitened * gain + bias).astype(BF16)
+
+
 def conv_norm_kernel(relative, own, height, breadth, *refs):
-    small = refs[:INNER]
-    sources = refs[INNER : INNER + 2]
-    x_ref = sources[0]
-    normed_ref, white_ref, inv_ref, taps_ref, corner_ref, *scratch = refs[INNER + 2 :]
-    gathered, unfolded, padded, conv = scratch
-    pixels, depth = x_ref.shape
-    tiles = depth // LANES
-    quarter = corner_ref.shape[1]
-    start = pl.multiple_of((1 - lax.axis_index("rep") % 2) * quarter, LANES)
-    corner_ref[...] = sources[1][pixels:, pl.ds(start, quarter)]
+    small, x_ref = refs[:INNER], refs[INNER]
+    *outs, taps_ref, gathered, unfolded, padded, conv = refs[INNER + 1 :]
     if relative:
         for group, piece in enumerate(small):
             unfolded[group * 2 * piece.shape[0] : (group + 1) * 2 * piece.shape[0], :] = unfold(
@@ -224,49 +259,17 @@
         count = unfolded.shape[0] // INNER
         small = [unfolded.at[pl.ds(group * count, count), :] for group in range(INNER)]
     place_rows(small, gathered, own, relative, F32)
-    clear_borders(padded, breadth)
-    for tile in range(tiles):
-        lanes = slice(tile * LANES, (tile + 1) * LANES)
-        taps_ref[tile] = gathered[lanes, :].T
-
-    for image, source in enumerate(sources):
-        for tile in range(tiles):
-            lanes = slice(tile * LANES, (tile + 1) * LANES)
-            part = source[:pixels, lanes].astype(F32)
-            padded[tile, :, 8 : 8 + breadth, :] = part.reshape(height, breadth, LANES)
-
-        def one_tile(tile, carry):
-            sums = correlate(
-                padded,
-                tile,
-                lambda down, across: taps_ref[tile, pl.ds(down * KS + across, 1), :],
-                height,
-                breadth,
-            )
-            for line in range(height):
-                conv[tile, line * breadth : (line + 1) * breadth, :] = sums[line]
-            return carry
-
-        lax.fori_loop(0, tiles, one_tile, 0)
-        total = conv[0]
-        for tile in range(1, tiles):
-            total = total + conv[tile]
-        average = jnp.sum(total, axis=-1, keepdims=True) / depth
-        squares = None
-        for tile in range(tiles):
-            centered = conv[tile] - average
-            squares = centered * centered if squares is None else squares + centered * centered
-        variance = jnp.sum(squares, axis=-1, keepdims=True) / depth
-        inv_std = lax.rsqrt(variance + NORM_EPS)
-        rows = slice(image * pixels, (image + 1) * pixels)
-        inv_ref[rows, :] = jnp.broadcast_to(inv_std, (pixels, LANES))
-        for tile in range(tiles):
-            lanes = slice(tile * LANES, (tile + 1) * LANES)
-            whitened = (conv[tile] - average) * inv_std
-            white_ref[rows, lanes] = whitened
-            gain = taps_ref[tile, TAPS : TAPS + 1, :]
-            bias = taps_ref[tile, TAPS + 1 : TAPS + 2, :]
-            normed_ref[rows, lanes] = (whitened * gain + bias).astype(BF16)
+    for tile in range(taps_ref.shape[0]):
+        taps_ref[tile] = gathered[tile * LANES : (tile + 1) * LANES, :].T
+    conv_norm_image(x_ref, taps_ref, outs, padded, conv, height, breadth)
+
+
+def far_norm_kernel(height, breadth, taps_ref, far_ref, *refs):
+    *outs, corner_ref, padded, conv = refs
+    pixels, quarter = corner_ref.shape
+    start = pl.multiple_of((1 - lax.axis_index("rep") % 2) * quarter, LANES)
+    corner_ref[...] = far_ref[pixels:, pl.ds(start, quarter)]
+    conv_norm_image(far_ref, taps_ref, outs, padded, conv, height, breadth)
 
 
 def cot_pack_kernel(image_ref, cot_ref, across_ref, sibling_ref):
@@ -309,15 +312,16 @@
 
 
 def project_kernel(relative, own, *refs):
-    weight, n_own, n_sibling, cot_ref, sibling_ref, across_ref, corner_ref = refs[:7]
-    pieces = refs[7 : 7 + INNER]
-    gp_ref, normed, cot, grad = refs[7 + INNER :]
+    weight, *parts = refs[:5]
+    cot_ref, sibling_ref, across_ref, corner_ref = refs[5:9]
+    pieces = refs[9 : 9 + INNER]
+    gp_ref, normed, cot, grad = refs[9 + INNER :]
     pixels, half = sibling_ref.shape
     quarter = half // 2
     side = lax.axis_index("rep") % 2
     parity = (lax.axis_index("shard") // INNER) % 2
-    normed[: 2 * pixels, :] = n_own[...]
-    normed[2 * pixels :, :] = n_sibling[...]
+    for place, part in enumerate(parts):
+        normed[place * pixels : (place + 1) * pixels, :] = part[...]
     start = pl.multiple_of(side * half + parity * quarter, LANES)
     cot[:pixels, :] = cot_ref[:, pl.ds(start, quarter)]
     start = pl.multiple_of(side * quarter, LANES)
@@ -345,15 +349,17 @@
 
 
 def norm_back_kernel(relative, own, height, breadth, *refs):
-    gn_own, gn_other, white_ref, inv_ref, taps_ref, x_ref, far_ref = refs[:7]
-    pieces = refs[7 : 7 + INNER]
-    grad_ref, sent_ref, padded, grads_ref, rows, small, unfolded = refs[7 + INNER :]
+    gn_own, gn_other, *norms = refs[:6]
+    taps_ref, x_ref, far_ref = refs[6:9]
+    pieces = refs[9 : 9 + INNER]
+    grad_ref, sent_ref, padded, grads_ref, rows, small, unfolded = refs[9 + INNER :]
     pixels, depth = x_ref.shape
     tiles = depth // LANES
     clear_borders(padded, breadth)
     rows[...] = jnp.zeros_like(rows)
     for image, source in enumerate((x_ref, far_ref)):
         span = slice(image * pixels, (image + 1) * pixels)
+        white_ref, inv_ref = norms[2 * image : 2 * image + 2]
         first = None
         second = None
         for tile in range(tiles):
@@ -361,7 +367,7 @@
             part = source[:pixels, lanes].astype(F32)
             padded[image, tile, :, 8 : 8 + breadth, :] = part.reshape(height, breadth, LANES)
             grad_normed = gn_own[span, lanes] + gn_other[span, lanes]
-            whitened = white_ref[span, lanes]
+            whitened = white_ref[:, lanes]
             product = grad_normed * whitened
             gain = taps_ref[tile, TAPS : TAPS + 1, :]
             rows[tile, TAPS : TAPS + 1, :] += jnp.sum(product, axis=0, keepdims=True)
@@ -375,8 +381,8 @@
             lanes = slice(tile * LANES, (tile + 1) * LANES)
             gain = taps_ref[tile, TAPS : TAPS + 1, :]
             grad_white = (gn_own[span, lanes] + gn_other[span, lanes]) * gain
-            grad_conv = inv_ref[span, :] * (
-                grad_white - mean_first - white_ref[span, lanes] * mean_second
+            grad_conv = inv_ref[...] * (
+                grad_white - mean_first - white_ref[:, lanes] * mean_second
             )
             grad_conv = grad_conv.reshape(height, breadth, LANES)
             grads_ref[image, tile] = grad_conv
@@ -569,33 +575,38 @@
         "order",
         [shape((depth, quarter), BF16)],
         [],
-        1.0,
+        0.3,
         *weights,
     )
 
     padded = pltpu.VMEM((tiles, height, breadth + 16, LANES), F32)
-    normed, whitened, inv_std, taps, corner = call(
+    norm_shapes = [
+        shape((pixels, depth), BF16),
+        shape((pixels, depth), F32),
+        shape((pixels, LANES), F32),
+    ]
+    conv = pltpu.VMEM((tiles, pixels, LANES), F32)
+    normed, whitened, inv_std, taps = call(
         functools.partial(conv_norm_kernel, relative, own, height, breadth),
         "conv_norm",
-        [
-            shape((2 * pixels, depth), BF16),
-            shape((2 * pixels, depth), F32),
-            shape((2 * pixels, LANES), F32),
-            shape((tiles, LANES, LANES), F32),
-            shape((pixels, quarter), BF16),
-        ],
-        [
-            pltpu.VMEM((depth, LANES), F32),
-            pltpu.VMEM((depth, LANES), F32),
-            padded,
-            pltpu.VMEM((tiles, pixels, LANES), F32),
-        ],
+        norm_shapes + [shape((tiles, LANES, LANES), F32)],
+        [pltpu.VMEM((depth, LANES), F32), pltpu.VMEM((depth, LANES), F32), padded, conv],
         0.1,
         *extras,
         image,
+    )
+    normed_sibling = over_core(normed)
+    far_normed, far_whitened, far_inv_std, corner = call(
+        functools.partial(far_norm_kernel, height, breadth),
+        "far_norm",
+        norm_shapes + [shape((pixels, quarter), BF16)],
+        [padded, conv],
+        1.0,
+        taps,
         across,
     )
-    normed_sibling, corner = over_core(normed), over_core(corner)
+    corner_normed, corner = over_core(far_normed), over_core(corner)
+
     *pieces, grad_pre = call(
         functools.partial(project_kernel, relative, own),
         "project",
@@ -610,7 +621,9 @@
         1.6,
         weight,
         normed,
+        far_normed,
         normed_sibling,
+        corner_normed,
         cotangent,
         cot_sibling,
         across,
@@ -648,6 +661,8 @@
         over_core(gn_sent),
         whitened,
         inv_std,
+        far_whitened,
+        far_inv_std,
         taps,
         image,
         across,

time: 53.2 us -> 52.3 us (0.983)
  waiting for transfers between devices: 14.3 us -> 11.7 us
  starting transfers between devices: 24.3 us -> 26 us
    ppermute x5 -> x6, starting transfers between devices: 0.87 us -> 2.67 us  [over_core(): return lax.ppermute(array, 'rep', [(i, i ^ 1) for i in range(reps)])]
    ppermute x14, waiting for transfers between devices: 10.5 us -> 8.94 us  [crossing(): return lax.ppermute(array, ('shard', 'rep'), pairs)]
    ppermute x3, waiting for transfers between devices: 0.93 us -> 0.18 us  [over_shard(): return lax.ppermute(array, 'shard', [(i, i ^ flip) for i in range(shards)])]
    ppermute x5 -> x6, waiting for transfers between devices: 2.78 us -> 2.41 us  [over_core(): return lax.ppermute(array, 'rep', [(i, i ^ 1) for i in range(reps)])]
    pallas_call x13 -> x14, Pallas kernels: 13.6 us -> 13.7 us  [call(): pl.pallas_call(kernel, out_shape=outs, in_specs=[VMEM] * len(args), out_s...]
  transfers between devices with their start and end apart: 24 -> 25, of which waited for: 11 -> 10; matrix products, arithmetic and copies ran while one was open for 0% -> 0% of each run, Pallas kernels for 17% -> 17%
where the time goes in v18:
time: 52.3 us; the launch traced here: 52.1 us
  starting transfers between devices  26 us (50%)
  Pallas kernels  13.7 us (26%)
  waiting for transfers between devices  11.7 us (22%)
  between operations  0.77 us (1%)
    ppermute x14, starting transfers between devices, crossing(): return lax.ppermute(array, ('shard', 'rep'), pairs)  16.4 us
    pallas_call x14, Pallas kernels, call(): pl.pallas_call(kernel, out_shape=outs, in_specs=[VMEM] * len(args), out_s...  13.7 us
    ppermute x14, waiting for transfers between devices, crossing(): return lax.ppermute(array, ('shard', 'rep'), pairs)  8.94 us
    ppermute x3, starting transfers between devices, over_shard(): return lax.ppermute(array, 'shard', [(i, i ^ flip) for i in range(shards)])  3.49 us
    ppermute x2, starting transfers between devices, hop(): return lax.ppermute(array, ('shard', 'rep'), pairs)  3.4 us
    ppermute x6, starting transfers between devices, over_core(): return lax.ppermute(array, 'rep', [(i, i ^ 1) for i in range(reps)])  2.67 us
    ppermute x6, waiting for transfers between devices, over_core(): return lax.ppermute(array, 'rep', [(i, i ^ 1) for i in range(reps)])  2.41 us
  transfers between devices with their start and end apart: 25, of which 10 were waited for; matrix products, arithmetic and copies ran while one was open for 0% of the time, Pallas kernels for 17%

profile of v18, /device:TPU:0, one launch (start us, length us, event | category | flops | bytes accessed | tf_op | source)
XLA Modules:
  0.0 52.1 jit_solution(9088930002233777595)
XLA Ops:
  0.6 0.0 copy-start
  0.6 0.0 copy-start.1
  0.7 1.8 %pack.1 = (bf16[56,384]{1,0:T(8,128)(2,1)}, bf16[56,384]{1,0:T(8,128)(2,1)}, bf16[56,384]{1,0:T(8,128)(2,1)}) custom-call(bf16[48,1536]{1,0:T(8,128)(2,1)} %w_ref.1, bf16[48,49]{1,0:T(8,128)(2,1)} %dw_ref.1, bf16[1,48]{1,0:T(2,128)(2,1)} %bitcast.11, bf16[1,48]{1,0:T(2,128)(2,1)} %bitcast.12), custom_call_target="tpu_custom_call" | custom-call | flops 550000000 | bytes 281376 | tf_op jit(solution)/shard_map/pack/pallas_call | solution.py:447
  2.4 3.5 %collective-permute-start.1 = (bf16[56,384]{1,0:T(8,128)(2,1)}, bf16[56,384]{1,0:T(8,128)(2,1)S(1)}, u32[]{:S(2)}, u32[]{:S(2)}) collective-permute-start(bf16[56,384]{1,0:T(8,128)(2,1)} %get-tuple-element.55), channel_id=1, source_target_pairs={{0,17},{1,16},{2,19},{3,18},{4,21},{5,20},{6,23},{7,22},{8,25},{9,... | collective-permute-start | bytes 129032 | tf_op jit(solution)/shard_map/ppermute | solution.py:480
  5.9 1.6 %collective-permute-start.2 = (bf16[56,384]{1,0:T(8,128)(2,1)}, bf16[56,384]{1,0:T(8,128)(2,1)S(1)}, u32[]{:S(2)}, u32[]{:S(2)}) collective-permute-start(bf16[56,384]{1,0:T(8,128)(2,1)} %get-tuple-element.54), channel_id=1, source_target_pairs={{0,25},{1,24},{2,27},{3,26},{4,29},{5,28},{6,31},{7,30},{8,17},{9,... | collective-permute-start | bytes 129032 | tf_op jit(solution)/shard_map/ppermute | solution.py:480
  7.5 0.2 collective-permute-start
  7.8 0.1 collective-permute-start.3
  7.9 1.7 %collective-permute-start.9 = (bf16[256,768]{1,0:T(8,128)(2,1)S(1)}, bf16[256,768]{1,0:T(8,128)(2,1)S(1)}, u32[]{:S(2)}, u32[]{:S(2)}) collective-permute-start(bf16[256,768]{1,0:T(8,128)(2,1)S(1)} %get-tuple-element.64), channel_id=1, source_target_pairs={{0,9},{1,8},{2,11},{3,10},{4,13},{5,12},{6,15},{7,14},{8,1},{9,0},... | collective-permute-start | bytes 1179656 | tf_op jit(solution)/shard_map/ppermute | solution.py:480
  9.6 0.0 collective-permute-done.1.refs_2_
  9.6 1.9 %collective-permute-done.2.refs_3_ = bf16[56,384]{1,0:T(8,128)(2,1)S(1)} collective-permute-done((bf16[56,384]{1,0:T(8,128)(2,1)}, bf16[56,384]{1,0:T(8,128)(2,1)S(1)}, u32[]{:S(2)}, u32[]{:S(2)}) %collective-permute-start.2) | collective-permute-done | bytes 43040 | tf_op jit(solution)/shard_map/ppermute | solution.py:480
  11.5 0.6 %collective-permute-done.refs_1_ = bf16[56,384]{1,0:T(8,128)(2,1)S(1)} collective-permute-done((bf16[56,384]{1,0:T(8,128)(2,1)}, bf16[56,384]{1,0:T(8,128)(2,1)S(1)}, u32[]{:S(2)}, u32[]{:S(2)}) %collective-permute-start) | collective-permute-done | bytes 43040 | tf_op jit(solution)/shard_map/ppermute | solution.py:480
  12.0 0.1 assemble.1
  12.2 0.0 collective-permute-done.3.refs_6_
  12.2 1.6 %collective-permute-start.4 = (bf16[192,384]{1,0:T(8,128)(2,1)S(1)}, bf16[192,384]{1,0:T(8,128)(2,1)S(1)}, u32[]{:S(2)}, u32[]{:S(2)}) collective-permute-start(bf16[192,384]{1,0:T(8,128)(2,1)S(1)} %get-tuple-element.60.own_ref.refs_0_), channel_id=1, source_target_pairs={{0,2},{1,5},{2,0},{3,7},{4,6},{5,1},{6,4},{7,3},{8,10},{9,13},{10,... | collective-permute-start | bytes 442376 | tf_op jit(solution)/shard_map/ppermute | solution.py:489
  13.8 1.7 %collective-permute-start.8 = (bf16[96,128]{1,0:T(8,128)(2,1)S(1)}, bf16[96,128]{1,0:T(8,128)(2,1)S(1)}, u32[]{:S(2)}, u32[]{:S(2)}) collective-permute-start(bf16[96,128]{1,0:T(8,128)(2,1)S(1)} %get-tuple-element.61.refs_0_), channel_id=1, source_target_pairs={{0,7},{1,6},{2,5},{3,4},{4,3},{5,2},{6,1},{7,0},{8,15},{9,14},{10,... | collective-permute-start | bytes 73736 | tf_op jit(solution)/shard_map/ppermute | solution.py:480
  15.5 0.0 collective-permute-start.7
  15.5 1.8 %collective-permute-start.6 = (bf16[96,128]{1,0:T(8,128)(2,1)S(1)}, bf16[96,128]{1,0:T(8,128)(2,1)S(1)}, u32[]{:S(2)}, u32[]{:S(2)}) collective-permute-start(bf16[96,128]{1,0:T(8,128)(2,1)S(1)} %get-tuple-element.61.refs_0_), channel_id=1, source_target_pairs={{0,3},{1,2},{2,1},{3,0},{4,7},{5,6},{6,5},{7,4},{8,11},{9,10},{10,... | collective-permute-start | bytes 73736 | tf_op jit(solution)/shard_map/ppermute | solution.py:480
  17.2 0.2 collective-permute-done.4.came_ref.refs_1_
  17.4 1.8 %collective-permute-start.5 = (bf16[384,384]{1,0:T(8,128)(2,1)S(1)}, bf16[384,384]{1,0:T(8,128)(2,1)S(1)}, u32[]{:S(2)}, u32[]{:S(2)}) collective-permute-start(bf16[384,384]{1,0:T(8,128)(2,1)S(1)} %join.1), channel_id=1, source_target_pairs={{0,4},{1,3},{2,6},{3,1},{4,0},{5,7},{6,2},{7,5},{8,12},{9,11},{10,... | collective-permute-start | bytes 884744 | tf_op jit(solution)/shard_map/ppermute | solution.py:489
  19.3 0.0 collective-permute-done.8.refs_3_
  19.3 0.0 collective-permute-done.7.refs_2_
  19.3 0.0 collective-permute-done.6.refs_1_
  19.3 1.8 %conv_norm.1 = (bf16[128,768]{1,0:T(8,128)(2,1)S(1)}, f32[128,768]{1,0:T(8,128)S(1)}, f32[128,128]{1,0:T(8,128)S(1)}, f32[6,128,128]{2,1,0:T(8,128)S(1)}) custom-call(bf16[96,128]{1,0:T(8,128)(2,1)S(1)} %get-tuple-element.61.refs_0_, bf16[96,128]{1,0:T(8,128)(2,1)S(1)} %collective-permute-done.6.refs_1_, bf16[96,128]{1,0:T(8,128)(2,1)S(1)} %collective-permute-done.7.refs_2_, ...), custom_call_target="tpu_custom_call" | custom-call | flops 110000000 | bytes 1343488 | tf_op jit(solution)/shard_map/conv_norm/pallas_call | solution.py:447
  21.1 1.6 %collective-permute-start.10 = (bf16[128,768]{1,0:T(8,128)(2,1)S(1)}, bf16[128,768]{1,0:T(8,128)(2,1)S(1)}, u32[]{:S(2)}, u32[]{:S(2)}) collective-permute-start(bf16[128,768]{1,0:T(8,128)(2,1)S(1)} %get-tuple-element.62.refs_1_), channel_id=1, source_target_pairs={{0,1},{1,0},{2,3},{3,2},{4,5},{5,4},{6,7},{7,6},{8,9},{9,8},{10,11... | collective-permute-start | bytes 589832 | tf_op jit(solution)/shard_map/ppermute | solution.py:492
  22.7 0.0 collective-permute-done.9.far_ref.refs_7_.refs_8_
  22.7 1.5 %far_norm.1 = (bf16[128,768]{1,0:T(8,128)(2,1)S(1)}, f32[128,768]{1,0:T(8,128)S(1)}, f32[128,128]{1,0:T(8,128)S(1)}, bf16[128,384]{1,0:T(8,128)(2,1)S(1)}) custom-call(f32[6,128,128]{2,1,0:T(8,128)S(1)} %get-tuple-element.63.taps_ref.refs_6_, bf16[256,768]{1,0:T(8,128)(2,1)S(1)} %collective-permute-done.9.far_ref.refs_7_.refs_8_), custom_call_target="tpu_custom_call" | custom-call | flops 1100000000 | bytes 1540096 | tf_op jit(solution)/shard_map/far_norm/pallas_call | solution.py:447
  24.2 0.1 collective-permute-start.11
  24.3 0.5 collective-permute-start.12
  24.8 0.0 collective-permute-done.5.refs_2_
  24.8 0.1 order.1.refs_0_.weight
  24.9 0.0 collective-permute-done.10.refs_3_
  24.9 1.0 %collective-permute-done.12.refs_8_ = bf16[128,384]{1,0:T(8,128)(2,1)S(1)} collective-permute-done((bf16[128,384]{1,0:T(8,128)(2,1)S(1)}, bf16[128,384]{1,0:T(8,128)(2,1)S(1)}, u32[]{:S(2)}, u32[]{:S(2)}) %collective-permute-start.12) | collective-permute-done | bytes 98336 | tf_op jit(solution)/shard_map/ppermute | solution.py:492
  25.9 0.0 collective-permute-done.11.refs_4_
  25.9 1.5 %project.1 = (f32[192,384]{1,0:T(8,128)S(1)}, bf16[192,384]{1,0:T(8,128)(2,1)S(1)}, bf16[192,384]{1,0:T(8,128)(2,1)S(1)}, bf16[192,384]{1,0:T(8,128)(2,1)S(1)}, bf16[512,384]{1,0:T(8,128)(2,1)S(1)}) custom-call(bf16[768,384]{1,0:T(8,128)(2,1)S(1)} %order.1.refs_0_.weight, bf16[128,768]{1,0:T(8,128)(2,1)S(1)} %get-tuple-element.62.refs_1_, ...), custom_call_target="tpu_custom_call" | custom-call | flops 1760000000 | bytes 3588096 | tf_op jit(solution)/shard_map/project/pallas_call | solution.py:447
  27.4 0.6 %back_project.1 = (f32[256,768]{1,0:T(8,128)S(1)}, f32[256,768]{1,0:T(8,128)S(1)}) custom-call(bf16[768,384]{1,0:T(8,128)(2,1)S(1)} %order.1.refs_0_.weight, bf16[512,384]{1,0:T(8,128)(2,1)S(1)} %get-tuple-element.72.gp_ref), custom_call_target="tpu_custom_call" | custom-call | flops 770000000 | bytes 2555904 | tf_op jit(solution)/shard_map/back_project/pallas_call | solution.py:447
  28.0 0.3 collective-permute-start.16
  28.3 0.3 collective-permute-start.13
  28.6 1.2 %collective-permute-start.14 = (bf16[192,384]{1,0:T(8,128)(2,1)S(1)}, bf16[192,384]{1,0:T(8,128)(2,1)S(1)}, u32[]{:S(2)}, u32[]{:S(2)}) collective-permute-start(bf16[192,384]{1,0:T(8,128)(2,1)S(1)} %get-tuple-element.70), channel_id=1, source_target_pairs={{0,4},{2,6},{4,0},{6,2},{8,12},{10,14},{12,8},{14,10},{16,20},{18,... | collective-permute-start | bytes 442376 | tf_op jit(solution)/shard_map/ppermute | solution.py:474
  29.8 2.0 %collective-permute-start.15 = (bf16[192,384]{1,0:T(8,128)(2,1)S(1)}, bf16[192,384]{1,0:T(8,128)(2,1)S(1)}, u32[]{:S(2)}, u32[]{:S(2)}) collective-permute-start(bf16[192,384]{1,0:T(8,128)(2,1)S(1)} %get-tuple-element.71), channel_id=1, source_target_pairs={{0,6},{2,4},{4,2},{6,0},{8,14},{10,12},{12,10},{14,8},{16,22},{18,... | collective-permute-start | bytes 442376 | tf_op jit(solution)/shard_map/ppermute | solution.py:474
  31.8 0.0 collective-permute-done.16.refs_1_
  31.8 3.2 %norm_back.1 = (f32[96,128]{1,0:T(8,128)S(1)}, bf16[96,128]{1,0:T(8,128)(2,1)S(1)}, bf16[96,128]{1,0:T(8,128)(2,1)S(1)}, bf16[96,128]{1,0:T(8,128)(2,1)S(1)}, f3...) custom-call(f32[256,768]{1,0:T(8,128)S(1)} %get-tuple-element.73.refs_0_, ...), custom_call_target="tpu_custom_call" | custom-call | flops 110000000 | bytes 4186112 | tf_op jit(solution)/shard_map/norm_back/pallas_call | solution.py:447
  35.1 0.1 collective-permute-start.17
  35.1 1.2 %collective-permute-start.18 = (bf16[96,128]{1,0:T(8,128)(2,1)S(1)}, bf16[96,128]{1,0:T(8,128)(2,1)S(1)}, u32[]{:S(2)}, u32[]{:S(2)}) collective-permute-start(bf16[96,128]{1,0:T(8,128)(2,1)S(1)} %get-tuple-element.81), channel_id=1, source_target_pairs={{0,5},{1,4},{2,7},{3,6},{4,1},{5,0},{6,3},{7,2},{8,13},{9,12},{10,... | collective-permute-start | bytes 73736 | tf_op jit(solution)/shard_map/ppermute | solution.py:480
  36.3 0.0 collective-permute-done.13.refs_1_
  36.3 1.1 %collective-permute-start.19 = (bf16[96,128]{1,0:T(8,128)(2,1)S(1)}, bf16[96,128]{1,0:T(8,128)(2,1)S(1)}, u32[]{:S(2)}, u32[]{:S(2)}) collective-permute-start(bf16[96,128]{1,0:T(8,128)(2,1)S(1)} %get-tuple-element.82), channel_id=1, source_target_pairs={{0,7},{1,6},{2,5},{3,4},{4,3},{5,2},{6,1},{7,0},{8,15},{9,14},{10,... | collective-permute-start | bytes 73736 | tf_op jit(solution)/shard_map/ppermute | solution.py:480
  37.4 0.2 collective-permute-done.14.refs_2_
  37.6 0.0 collective-permute-start.20
  37.6 0.0 collective-permute-done.15.refs_3_
  37.6 0.8 %collective-permute-done.17.refs_5_ = bf16[96,128]{1,0:T(8,128)(2,1)S(1)} collective-permute-done((bf16[96,128]{1,0:T(8,128)(2,1)S(1)}, bf16[96,128]{1,0:T(8,128)(2,1)S(1)}, u32[]{:S(2)}, u32[]{:S(2)}) %collective-permute-start.17) | collective-permute-done | bytes 24608 | tf_op jit(solution)/shard_map/ppermute | solution.py:480
  38.4 0.1 collective-permute-done.18.refs_6_
  38.5 2.1 %collective-permute-done.19.refs_7_ = bf16[96,128]{1,0:T(8,128)(2,1)S(1)} collective-permute-done((bf16[96,128]{1,0:T(8,128)(2,1)S(1)}, bf16[96,128]{1,0:T(8,128)(2,1)S(1)}, u32[]{:S(2)}, u32[]{:S(2)}) %collective-permute-start.19) | collective-permute-done | bytes 24608 | tf_op jit(solution)/shard_map/ppermute | solution.py:480
  40.5 0.2 plane_sum.1
  40.7 0.0 collective-permute-start.21
  40.7 3.4 %collective-permute-start.22 = (bf16[56,384]{1,0:T(8,128)(2,1)S(1)}, bf16[56,384]{1,0:T(8,128)(2,1)S(1)}, u32[]{:S(2)}, u32[]{:S(2)}) collective-permute-start(bf16[56,384]{1,0:T(8,128)(2,1)S(1)} %get-tuple-element.89), channel_id=1, source_target_pairs={{0,17},{1,16},{2,19},{3,18},{4,21},{5,20},{6,23},{7,22},{8,25},{9,... | collective-permute-start | bytes 129032 | tf_op jit(solution)/shard_map/ppermute | solution.py:480
  44.1 0.2 collective-permute-start.23
  44.3 0.0 collective-permute-done.20.other_ref
  44.3 2.0 %conv_back.1 = bf16[1,8,16,768]{3,2,1,0:T(8,128)(2,1)} custom-call(f32[6,8,16,128]{3,2,1,0:T(8,128)S(1)} %get-tuple-element.84.grad_ref, bf16[6,8,16,128]{3,2,1,0:T(8,128)(2,1)S(1)} %collective-permute-done.20.other_ref, f32[6,128,128]{2,1,0:T(8,128)S(1)} %get-tuple-element.63.taps_ref.refs_6_), custom_call_target="tpu_custom_call" | custom-call | flops 110000000 | bytes 1179648 | tf_op jit(solution)/shard_map/conv_back/pallas_call | solution.py:447
  46.3 0.0 collective-permute-done.21.refs_1_
  46.3 0.0 collective-permute-done.22.refs_2_
  46.3 3.5 %collective-permute-done.23.refs_3_ = bf16[56,384]{1,0:T(8,128)(2,1)S(1)} collective-permute-done((bf16[56,384]{1,0:T(8,128)(2,1)S(1)}, bf16[56,384]{1,0:T(8,128)(2,1)S(1)}, u32[]{:S(2)}, u32[]{:S(2)}) %collective-permute-start.23) | collective-permute-done | bytes 43040 | tf_op jit(solution)/shard_map/ppermute | solution.py:480
  49.8 0.1 line_sum.1.mine_ref
  49.9 0.1 collective-permute-start.24
  50.0 1.4 %collective-permute-done.24.other_ref = f32[48,1280]{1,0:T(8,128)S(1)} collective-permute-done((f32[48,1280]{1,0:T(8,128)S(1)}, f32[48,1280]{1,0:T(8,128)S(1)}, u32[]{:S(2)}, u32[]{:S(2)}) %collective-permute-start.24) | collective-permute-done | bytes 245792 | tf_op jit(solution)/shard_map/ppermute | solution.py:492
  51.4 0.8 %finish.1 = (f32[48,1536]{1,0:T(8,128)}, f32[48,49]{1,0:T(8,128)}, f32[1,48]{1,0:T(1,128)}, f32[1,48]{1,0:T(1,128)}) custom-call(f32[48,1280]{1,0:T(8,128)S(1)} %line_sum.1.mine_ref, f32[48,1280]{1,0:T(8,128)S(1)} %collective-permute-done.24.other_ref), custom_call_target="tpu_custom_call" | custom-call | flops 550000000 | bytes 796224 | tf_op jit(solution)/shard_map/finish/pallas_call | solution.py:447
  (6 shorter events, 0.1 us)
Async XLA Ops:
  0.6 7.1 %copy-start = (bf16[1,8,16,768]{3,2,1,0:T(8,128)(2,1)S(1)}, bf16[1,8,16,768]{3,2,1,0:T(8,128)(2,1)}, u32[]{:S(2)}) copy-start(bf16[1,8,16,768]{3,2,1,0:T(8,128)(2,1)} %param.6) | copy-start | bytes 589828
  0.6 7.1 %copy-start.1 = (bf16[1,8,16,1536]{3,2,1,0:T(8,128)(2,1)S(1)}, bf16[1,8,16,1536]{3,2,1,0:T(8,128)(2,1)}, u32[]{:S(2)}) copy-start(bf16[1,8,16,1536]{3,2,1,0:T(8,128)(2,1)} %param.7) | copy-start | bytes 1179652
  2.4 9.6 %copy-start.2 = (bf16[56,384]{1,0:T(8,128)(2,1)S(1)}, bf16[56,384]{1,0:T(8,128)(2,1)}, u32[]{:S(2)}) copy-start(bf16[56,384]{1,0:T(8,128)(2,1)} %get-tuple-element.53.refs_0_) | copy-start | bytes 129028
  2.4 7.1 %collective-permute-start.1 = (bf16[56,384]{1,0:T(8,128)(2,1)}, bf16[56,384]{1,0:T(8,128)(2,1)S(1)}, u32[]{:S(2)}, u32[]{:S(2)}) collective-permute-start(bf16[56,384]{1,0:T(8,128)(2,1)} %get-tuple-element.55), channel_id=1, source_target_pairs={{0,17},{1,16},{2,19},{3,18},{4,21},{5,20},{6,23},{7,22},{8,25},{9,... | collective-permute-start | bytes 129032 | tf_op jit(solution)/shard_map/ppermute | solution.py:480
  5.9 5.6 %collective-permute-start.2 = (bf16[56,384]{1,0:T(8,128)(2,1)}, bf16[56,384]{1,0:T(8,128)(2,1)S(1)}, u32[]{:S(2)}, u32[]{:S(2)}) collective-permute-start(bf16[56,384]{1,0:T(8,128)(2,1)} %get-tuple-element.54), channel_id=1, source_target_pairs={{0,25},{1,24},{2,27},{3,26},{4,29},{5,28},{6,31},{7,30},{8,17},{9,... | collective-permute-start | bytes 129032 | tf_op jit(solution)/shard_map/ppermute | solution.py:480
  7.5 4.5 %collective-permute-start = (bf16[56,384]{1,0:T(8,128)(2,1)}, bf16[56,384]{1,0:T(8,128)(2,1)S(1)}, u32[]{:S(2)}, u32[]{:S(2)}) collective-permute-start(bf16[56,384]{1,0:T(8,128)(2,1)} %get-tuple-element.54), channel_id=1, source_target_pairs={{0,9},{1,8},{2,11},{3,10},{4,13},{5,12},{6,15},{7,14},{8,1},{9,0},... | collective-permute-start | bytes 129032 | tf_op jit(solution)/shard_map/ppermute | solution.py:480
  7.8 4.4 %collective-permute-start.3 = (bf16[128,768]{1,0:T(8,128)(2,1)S(1)}, bf16[128,768]{1,0:T(8,128)(2,1)S(1)}, u32[]{:S(2)}, u32[]{:S(2)}) collective-permute-start(bf16[128,768]{1,0:T(8,128)(2,1)S(1)} %get-tuple-element.59), channel_id=1, source_target_pairs={{0,1},{1,0},{2,3},{3,2},{4,5},{5,4},{6,7},{7,6},{8,9},{9,8},{10,11... | collective-permute-start | bytes 589832 | tf_op jit(solution)/shard_map/ppermute | solution.py:492
  7.9 14.8 %collective-permute-start.9 = (bf16[256,768]{1,0:T(8,128)(2,1)S(1)}, bf16[256,768]{1,0:T(8,128)(2,1)S(1)}, u32[]{:S(2)}, u32[]{:S(2)}) collective-permute-start(bf16[256,768]{1,0:T(8,128)(2,1)S(1)} %get-tuple-element.64), channel_id=1, source_target_pairs={{0,9},{1,8},{2,11},{3,10},{4,13},{5,12},{6,15},{7,14},{8,1},{9,0},... | collective-permute-start | bytes 1179656 | tf_op jit(solution)/shard_map/ppermute | solution.py:480
  12.2 5.2 %collective-permute-start.4 = (bf16[192,384]{1,0:T(8,128)(2,1)S(1)}, bf16[192,384]{1,0:T(8,128)(2,1)S(1)}, u32[]{:S(2)}, u32[]{:S(2)}) collective-permute-start(bf16[192,384]{1,0:T(8,128)(2,1)S(1)} %get-tuple-element.60.own_ref.refs_0_), channel_id=1, source_target_pairs={{0,2},{1,5},{2,0},{3,7},{4,6},{5,1},{6,4},{7,3},{8,10},{9,13},{10,... | collective-permute-start | bytes 442376 | tf_op jit(solution)/shard_map/ppermute | solution.py:489
  13.8 5.5 %collective-permute-start.8 = (bf16[96,128]{1,0:T(8,128)(2,1)S(1)}, bf16[96,128]{1,0:T(8,128)(2,1)S(1)}, u32[]{:S(2)}, u32[]{:S(2)}) collective-permute-start(bf16[96,128]{1,0:T(8,128)(2,1)S(1)} %get-tuple-element.61.refs_0_), channel_id=1, source_target_pairs={{0,7},{1,6},{2,5},{3,4},{4,3},{5,2},{6,1},{7,0},{8,15},{9,14},{10,... | collective-permute-start | bytes 73736 | tf_op jit(solution)/shard_map/ppermute | solution.py:480
  15.5 3.8 %collective-permute-start.7 = (bf16[96,128]{1,0:T(8,128)(2,1)S(1)}, bf16[96,128]{1,0:T(8,128)(2,1)S(1)}, u32[]{:S(2)}, u32[]{:S(2)}) collective-permute-start(bf16[96,128]{1,0:T(8,128)(2,1)S(1)} %get-tuple-element.61.refs_0_), channel_id=1, source_target_pairs={{0,5},{1,4},{2,7},{3,6},{4,1},{5,0},{6,3},{7,2},{8,13},{9,12},{10,... | collective-permute-start | bytes 73736 | tf_op jit(solution)/shard_map/ppermute | solution.py:480
  15.5 3.8 %collective-permute-start.6 = (bf16[96,128]{1,0:T(8,128)(2,1)S(1)}, bf16[96,128]{1,0:T(8,128)(2,1)S(1)}, u32[]{:S(2)}, u32[]{:S(2)}) collective-permute-start(bf16[96,128]{1,0:T(8,128)(2,1)S(1)} %get-tuple-element.61.refs_0_), channel_id=1, source_target_pairs={{0,3},{1,2},{2,1},{3,0},{4,7},{5,6},{6,5},{7,4},{8,11},{9,10},{10,... | collective-permute-start | bytes 73736 | tf_op jit(solution)/shard_map/ppermute | solution.py:480
  17.4 7.4 %collective-permute-start.5 = (bf16[384,384]{1,0:T(8,128)(2,1)S(1)}, bf16[384,384]{1,0:T(8,128)(2,1)S(1)}, u32[]{:S(2)}, u32[]{:S(2)}) collective-permute-start(bf16[384,384]{1,0:T(8,128)(2,1)S(1)} %join.1), channel_id=1, source_target_pairs={{0,4},{1,3},{2,6},{3,1},{4,0},{5,7},{6,2},{7,5},{8,12},{9,11},{10,... | collective-permute-start | bytes 884744 | tf_op jit(solution)/shard_map/ppermute | solution.py:489
  21.1 3.8 %collective-permute-start.10 = (bf16[128,768]{1,0:T(8,128)(2,1)S(1)}, bf16[128,768]{1,0:T(8,128)(2,1)S(1)}, u32[]{:S(2)}, u32[]{:S(2)}) collective-permute-start(bf16[128,768]{1,0:T(8,128)(2,1)S(1)} %get-tuple-element.62.refs_1_), channel_id=1, source_target_pairs={{0,1},{1,0},{2,3},{3,2},{4,5},{5,4},{6,7},{7,6},{8,9},{9,8},{10,11... | collective-permute-start | bytes 589832 | tf_op jit(solution)/shard_map/ppermute | solution.py:492
  24.2 1.7 %collective-permute-start.11 = (bf16[128,768]{1,0:T(8,128)(2,1)S(1)}, bf16[128,768]{1,0:T(8,128)(2,1)S(1)}, u32[]{:S(2)}, u32[]{:S(2)}) collective-permute-start(bf16[128,768]{1,0:T(8,128)(2,1)S(1)} %get-tuple-element.65.refs_2_), channel_id=1, source_target_pairs={{0,1},{1,0},{2,3},{3,2},{4,5},{5,4},{6,7},{7,6},{8,9},{9,8},{10,11... | collective-permute-start | bytes 589832 | tf_op jit(solution)/shard_map/ppermute | solution.py:492
  24.3 1.6 %collective-permute-start.12 = (bf16[128,384]{1,0:T(8,128)(2,1)S(1)}, bf16[128,384]{1,0:T(8,128)(2,1)S(1)}, u32[]{:S(2)}, u32[]{:S(2)}) collective-permute-start(bf16[128,384]{1,0:T(8,128)(2,1)S(1)} %get-tuple-element.67), channel_id=1, source_target_pairs={{0,1},{1,0},{2,3},{3,2},{4,5},{5,4},{6,7},{7,6},{8,9},{9,8},{10,11... | collective-permute-start | bytes 294920 | tf_op jit(solution)/shard_map/ppermute | solution.py:492
  28.0 3.8 %collective-permute-start.16 = (f32[256,768]{1,0:T(8,128)S(1)}, f32[256,768]{1,0:T(8,128)S(1)}, u32[]{:S(2)}, u32[]{:S(2)}) collective-permute-start(f32[256,768]{1,0:T(8,128)S(1)} %get-tuple-element.74), channel_id=1, source_target_pairs={{0,1},{1,0},{2,3},{3,2},{4,5},{5,4},{6,7},{7,6},{8,9},{9,8},{10,11... | collective-permute-start | bytes 2359304 | tf_op jit(solution)/shard_map/ppermute | solution.py:492
  28.3 8.0 %collective-permute-start.13 = (bf16[192,384]{1,0:T(8,128)(2,1)S(1)}, bf16[192,384]{1,0:T(8,128)(2,1)S(1)}, u32[]{:S(2)}, u32[]{:S(2)}) collective-permute-start(bf16[192,384]{1,0:T(8,128)(2,1)S(1)} %get-tuple-element.69), channel_id=1, source_target_pairs={{0,2},{2,0},{4,6},{6,4},{8,10},{10,8},{12,14},{14,12},{16,18},{18,... | collective-permute-start | bytes 442376 | tf_op jit(solution)/shard_map/ppermute | solution.py:474
  28.6 8.9 %collective-permute-start.14 = (bf16[192,384]{1,0:T(8,128)(2,1)S(1)}, bf16[192,384]{1,0:T(8,128)(2,1)S(1)}, u32[]{:S(2)}, u32[]{:S(2)}) collective-permute-start(bf16[192,384]{1,0:T(8,128)(2,1)S(1)} %get-tuple-element.70), channel_id=1, source_target_pairs={{0,4},{2,6},{4,0},{6,2},{8,12},{10,14},{12,8},{14,10},{16,20},{18,... | collective-permute-start | bytes 442376 | tf_op jit(solution)/shard_map/ppermute | solution.py:474
  29.8 7.8 %collective-permute-start.15 = (bf16[192,384]{1,0:T(8,128)(2,1)S(1)}, bf16[192,384]{1,0:T(8,128)(2,1)S(1)}, u32[]{:S(2)}, u32[]{:S(2)}) collective-permute-start(bf16[192,384]{1,0:T(8,128)(2,1)S(1)} %get-tuple-element.71), channel_id=1, source_target_pairs={{0,6},{2,4},{4,2},{6,0},{8,14},{10,12},{12,10},{14,8},{16,22},{18,... | collective-permute-start | bytes 442376 | tf_op jit(solution)/shard_map/ppermute | solution.py:474
  35.1 3.3 %collective-permute-start.17 = (bf16[96,128]{1,0:T(8,128)(2,1)S(1)}, bf16[96,128]{1,0:T(8,128)(2,1)S(1)}, u32[]{:S(2)}, u32[]{:S(2)}) collective-permute-start(bf16[96,128]{1,0:T(8,128)(2,1)S(1)} %get-tuple-element.80), channel_id=1, source_target_pairs={{0,3},{1,2},{2,1},{3,0},{4,7},{5,6},{6,5},{7,4},{8,11},{9,10},{10,... | collective-permute-start | bytes 73736 | tf_op jit(solution)/shard_map/ppermute | solution.py:480
  35.1 3.3 %collective-permute-start.18 = (bf16[96,128]{1,0:T(8,128)(2,1)S(1)}, bf16[96,128]{1,0:T(8,128)(2,1)S(1)}, u32[]{:S(2)}, u32[]{:S(2)}) collective-permute-start(bf16[96,128]{1,0:T(8,128)(2,1)S(1)} %get-tuple-element.81), channel_id=1, source_target_pairs={{0,5},{1,4},{2,7},{3,6},{4,1},{5,0},{6,3},{7,2},{8,13},{9,12},{10,... | collective-permute-start | bytes 73736 | tf_op jit(solution)/shard_map/ppermute | solution.py:480
  36.3 4.2 %collective-permute-start.19 = (bf16[96,128]{1,0:T(8,128)(2,1)S(1)}, bf16[96,128]{1,0:T(8,128)(2,1)S(1)}, u32[]{:S(2)}, u32[]{:S(2)}) collective-permute-start(bf16[96,128]{1,0:T(8,128)(2,1)S(1)} %get-tuple-element.82), channel_id=1, source_target_pairs={{0,7},{1,6},{2,5},{3,4},{4,3},{5,2},{6,1},{7,0},{8,15},{9,14},{10,... | collective-permute-start | bytes 73736 | tf_op jit(solution)/shard_map/ppermute | solution.py:480
  37.6 6.8 %collective-permute-start.20 = (bf16[6,8,16,128]{3,2,1,0:T(8,128)(2,1)S(1)}, bf16[6,8,16,128]{3,2,1,0:T(8,128)(2,1)S(1)}, u32[]{:S(2)}, u32[]{:S(2)}) collective-permute-start(bf16[6,8,16,128]{3,2,1,0:T(8,128)(2,1)S(1)} %get-tuple-element.85), channel_id=1, source_target_pairs={{0,9},{1,8},{2,11},{3,10},{4,13},{5,12},{6,15},{7,14},{8,1},{9,0},... | collective-permute-start | bytes 589832 | tf_op jit(solution)/shard_map/ppermute | solution.py:480
  40.7 5.6 %collective-permute-start.21 = (bf16[56,384]{1,0:T(8,128)(2,1)S(1)}, bf16[56,384]{1,0:T(8,128)(2,1)S(1)}, u32[]{:S(2)}, u32[]{:S(2)}) collective-permute-start(bf16[56,384]{1,0:T(8,128)(2,1)S(1)} %get-tuple-element.88), channel_id=1, source_target_pairs={{0,9},{1,8},{2,11},{3,10},{4,13},{5,12},{6,15},{7,14},{8,1},{9,0},... | collective-permute-start | bytes 129032 | tf_op jit(solution)/shard_map/ppermute | solution.py:480
  40.7 5.6 %collective-permute-start.22 = (bf16[56,384]{1,0:T(8,128)(2,1)S(1)}, bf16[56,384]{1,0:T(8,128)(2,1)S(1)}, u32[]{:S(2)}, u32[]{:S(2)}) collective-permute-start(bf16[56,384]{1,0:T(8,128)(2,1)S(1)} %get-tuple-element.89), channel_id=1, source_target_pairs={{0,17},{1,16},{2,19},{3,18},{4,21},{5,20},{6,23},{7,22},{8,25},{9,... | collective-permute-start | bytes 129032 | tf_op jit(solution)/shard_map/ppermute | solution.py:480
  44.1 5.7 %collective-permute-start.23 = (bf16[56,384]{1,0:T(8,128)(2,1)S(1)}, bf16[56,384]{1,0:T(8,128)(2,1)S(1)}, u32[]{:S(2)}, u32[]{:S(2)}) collective-permute-start(bf16[56,384]{1,0:T(8,128)(2,1)S(1)} %get-tuple-element.90), channel_id=1, source_target_pairs={{0,25},{1,24},{2,27},{3,26},{4,29},{5,28},{6,31},{7,30},{8,17},{9,... | collective-permute-start | bytes 129032 | tf_op jit(solution)/shard_map/ppermute | solution.py:480
  49.9 1.5 %collective-permute-start.24 = (f32[48,1280]{1,0:T(8,128)S(1)}, f32[48,1280]{1,0:T(8,128)S(1)}, u32[]{:S(2)}, u32[]{:S(2)}) collective-permute-start(f32[48,1280]{1,0:T(8,128)S(1)} %line_sum.1.mine_ref), channel_id=1, source_target_pairs={{0,1},{1,0},{2,3},{3,2},{4,5},{5,4},{6,7},{7,6},{8,9},{9,8},{10,11... | collective-permute-start | bytes 737288 | tf_op jit(solution)/shard_map/ppermute | solution.py:492

commit v19 on v18

--- a/solution.py
+++ b/solution.py
@@ -156,7 +156,7 @@
     pieces, total_ref = refs[:-1], refs[-1]
     quarter = (total_ref.shape[1] - LANES) // 3
     near, far = None, None
-    for line, piece in enumerate(pieces[1:], 1):
+    for line, piece in zip(range(len(pieces) - 1, 0, -1), pieces[1:]):
         came = piece[...].astype(F32)
         if line % 2:
             far = came if far is None else far + came
@@ -639,7 +639,7 @@
         grad_pre,
     )
     pieces = relative_order(pieces)
-    arrived = [over_shard(piece, flip) for flip, piece in enumerate(pieces) if flip]
+    arrived = [over_shard(pieces[flip], flip) for flip in range(INNER - 1, 0, -1)]
     *small, grad_conv, grad_sent = call(
         functools.partial(norm_back_kernel, relative, own, height, breadth),
         "norm_back",
@@ -668,7 +668,7 @@
         across,
     )
     small = relative_order(small)
-    small_arrived = [crossing(piece, flip) for flip, piece in enumerate(small) if flip]
+    small_arrived = [crossing(small[flip], flip) for flip in range(INNER - 1, 0, -1)]
     grad_other = crossing(grad_sent, INNER)
     (grad_images,) = call(
         conv_back_kernel,
@@ -694,7 +694,7 @@
         *small_arrived,
     )
     home, grad_images = lax.optimization_barrier((home, grad_images))
-    came = [crossing(piece, INNER * line) for line, piece in enumerate(sent, 1)]
+    came = [crossing(sent[line - 1], INNER * line) for line in range(lines - 1, 0, -1)]
     (total,) = call(
         functools.partial(line_sum_kernel, own),
         "line_sum",

time: 52.3 us -> 51.5 us (0.985)
  waiting for transfers between devices: 11.7 us -> 10.6 us
    ppermute x14, waiting for transfers between devices: 8.94 us -> 7.12 us  [crossing(): return lax.ppermute(array, ('shard', 'rep'), pairs)]
    ppermute x3, waiting for transfers between devices: 0.18 us -> 0.95 us  [over_shard(): return lax.ppermute(array, 'shard', [(i, i ^ flip) for i in range(shards)])]
where the time goes in v19:
time: 51.5 us; the launch traced here: 51.3 us
  starting transfers between devices  26.2 us (51%)
  Pallas kernels  13.7 us (27%)
  waiting for transfers between devices  10.6 us (21%)
  between operations  0.75 us (1%)
    ppermute x14, starting transfers between devices, crossing(): return lax.ppermute(array, ('shard', 'rep'), pairs)  16.7 us
    pallas_call x14, Pallas kernels, call(): pl.pallas_call(kernel, out_shape=outs, in_specs=[VMEM] * len(args), out_s...  13.7 us
    ppermute x14, waiting for transfers between devices, crossing(): return lax.ppermute(array, ('shard', 'rep'), pairs)  7.12 us
    ppermute x3, starting transfers between devices, over_shard(): return lax.ppermute(array, 'shard', [(i, i ^ flip) for i in range(shards)])  3.49 us
    ppermute x2, starting transfers between devices, hop(): return lax.ppermute(array, ('shard', 'rep'), pairs)  3.4 us
    ppermute x6, starting transfers between devices, over_core(): return lax.ppermute(array, 'rep', [(i, i ^ 1) for i in range(reps)])  2.69 us
    ppermute x6, waiting for transfers between devices, over_core(): return lax.ppermute(array, 'rep', [(i, i ^ 1) for i in range(reps)])  2.39 us
  transfers between devices with their start and end apart: 25, of which 10 were waited for; matrix products, arithmetic and copies ran while one was open for 0% of the time, Pallas kernels for 17%

profile of v19, /device:TPU:0, one launch (start us, length us, event | category | flops | bytes accessed | tf_op | source)
XLA Modules:
  0.0 51.3 jit_solution(3450728450007867785)
XLA Ops:
  0.6 0.0 copy-start
  0.7 1.8 %pack.1 = (bf16[56,384]{1,0:T(8,128)(2,1)}, bf16[56,384]{1,0:T(8,128)(2,1)}, bf16[56,384]{1,0:T(8,128)(2,1)}) custom-call(bf16[48,1536]{1,0:T(8,128)(2,1)} %w_ref.1, bf16[48,49]{1,0:T(8,128)(2,1)} %dw_ref.1, bf16[1,48]{1,0:T(2,128)(2,1)} %bitcast.11, bf16[1,48]{1,0:T(2,128)(2,1)} %bitcast.12), custom_call_target="tpu_custom_call" | custom-call | flops 550000000 | bytes 281376 | tf_op jit(solution)/shard_map/pack/pallas_call | solution.py:447
  2.4 3.5 %collective-permute-start.1 = (bf16[56,384]{1,0:T(8,128)(2,1)}, bf16[56,384]{1,0:T(8,128)(2,1)S(1)}, u32[]{:S(2)}, u32[]{:S(2)}) collective-permute-start(bf16[56,384]{1,0:T(8,128)(2,1)} %get-tuple-element.55), channel_id=1, source_target_pairs={{0,17},{1,16},{2,19},{3,18},{4,21},{5,20},{6,23},{7,22},{8,25},{9,... | collective-permute-start | bytes 129032 | tf_op jit(solution)/shard_map/ppermute | solution.py:480
  5.9 1.6 %collective-permute-start.2 = (bf16[56,384]{1,0:T(8,128)(2,1)}, bf16[56,384]{1,0:T(8,128)(2,1)S(1)}, u32[]{:S(2)}, u32[]{:S(2)}) collective-permute-start(bf16[56,384]{1,0:T(8,128)(2,1)} %get-tuple-element.54), channel_id=1, source_target_pairs={{0,25},{1,24},{2,27},{3,26},{4,29},{5,28},{6,31},{7,30},{8,17},{9,... | collective-permute-start | bytes 129032 | tf_op jit(solution)/shard_map/ppermute | solution.py:480
  7.5 0.2 collective-permute-start
  7.8 0.0 copy-done.1
  7.8 0.1 collective-permute-start.3
  7.9 1.7 %collective-permute-start.9 = (bf16[256,768]{1,0:T(8,128)(2,1)S(1)}, bf16[256,768]{1,0:T(8,128)(2,1)S(1)}, u32[]{:S(2)}, u32[]{:S(2)}) collective-permute-start(bf16[256,768]{1,0:T(8,128)(2,1)S(1)} %get-tuple-element.64), channel_id=1, source_target_pairs={{0,9},{1,8},{2,11},{3,10},{4,13},{5,12},{6,15},{7,14},{8,1},{9,0},... | collective-permute-start | bytes 1179656 | tf_op jit(solution)/shard_map/ppermute | solution.py:480
  9.6 0.0 collective-permute-done.1.refs_2_
  9.6 1.9 %collective-permute-done.2.refs_3_ = bf16[56,384]{1,0:T(8,128)(2,1)S(1)} collective-permute-done((bf16[56,384]{1,0:T(8,128)(2,1)}, bf16[56,384]{1,0:T(8,128)(2,1)S(1)}, u32[]{:S(2)}, u32[]{:S(2)}) %collective-permute-start.2) | collective-permute-done | bytes 43040 | tf_op jit(solution)/shard_map/ppermute | solution.py:480
  11.5 0.6 %collective-permute-done.refs_1_ = bf16[56,384]{1,0:T(8,128)(2,1)S(1)} collective-permute-done((bf16[56,384]{1,0:T(8,128)(2,1)}, bf16[56,384]{1,0:T(8,128)(2,1)S(1)}, u32[]{:S(2)}, u32[]{:S(2)}) %collective-permute-start) | collective-permute-done | bytes 43040 | tf_op jit(solution)/shard_map/ppermute | solution.py:480
  12.0 0.1 assemble.1
  12.2 0.0 collective-permute-done.3.refs_6_
  12.2 1.6 %collective-permute-start.4 = (bf16[192,384]{1,0:T(8,128)(2,1)S(1)}, bf16[192,384]{1,0:T(8,128)(2,1)S(1)}, u32[]{:S(2)}, u32[]{:S(2)}) collective-permute-start(bf16[192,384]{1,0:T(8,128)(2,1)S(1)} %get-tuple-element.60.own_ref.refs_0_), channel_id=1, source_target_pairs={{0,2},{1,5},{2,0},{3,7},{4,6},{5,1},{6,4},{7,3},{8,10},{9,13},{10,... | collective-permute-start | bytes 442376 | tf_op jit(solution)/shard_map/ppermute | solution.py:489
  13.8 1.7 %collective-permute-start.8 = (bf16[96,128]{1,0:T(8,128)(2,1)S(1)}, bf16[96,128]{1,0:T(8,128)(2,1)S(1)}, u32[]{:S(2)}, u32[]{:S(2)}) collective-permute-start(bf16[96,128]{1,0:T(8,128)(2,1)S(1)} %get-tuple-element.61.refs_0_), channel_id=1, source_target_pairs={{0,7},{1,6},{2,5},{3,4},{4,3},{5,2},{6,1},{7,0},{8,15},{9,14},{10,... | collective-permute-start | bytes 73736 | tf_op jit(solution)/shard_map/ppermute | solution.py:480
  15.5 0.0 collective-permute-start.7
  15.5 1.8 %collective-permute-start.6 = (bf16[96,128]{1,0:T(8,128)(2,1)S(1)}, bf16[96,128]{1,0:T(8,128)(2,1)S(1)}, u32[]{:S(2)}, u32[]{:S(2)}) collective-permute-start(bf16[96,128]{1,0:T(8,128)(2,1)S(1)} %get-tuple-element.61.refs_0_), channel_id=1, source_target_pairs={{0,3},{1,2},{2,1},{3,0},{4,7},{5,6},{6,5},{7,4},{8,11},{9,10},{10,... | collective-permute-start | bytes 73736 | tf_op jit(solution)/shard_map/ppermute | solution.py:480
  17.2 0.2 collective-permute-done.4.came_ref.refs_1_
  17.4 1.8 %collective-permute-start.5 = (bf16[384,384]{1,0:T(8,128)(2,1)S(1)}, bf16[384,384]{1,0:T(8,128)(2,1)S(1)}, u32[]{:S(2)}, u32[]{:S(2)}) collective-permute-start(bf16[384,384]{1,0:T(8,128)(2,1)S(1)} %join.1), channel_id=1, source_target_pairs={{0,4},{1,3},{2,6},{3,1},{4,0},{5,7},{6,2},{7,5},{8,12},{9,11},{10,... | collective-permute-start | bytes 884744 | tf_op jit(solution)/shard_map/ppermute | solution.py:489
  19.3 0.0 collective-permute-done.8.refs_3_
  19.3 0.0 collective-permute-done.7.refs_2_
  19.3 0.0 collective-permute-done.6.refs_1_
  19.3 1.8 %conv_norm.1 = (bf16[128,768]{1,0:T(8,128)(2,1)S(1)}, f32[128,768]{1,0:T(8,128)S(1)}, f32[128,128]{1,0:T(8,128)S(1)}, f32[6,128,128]{2,1,0:T(8,128)S(1)}) custom-call(bf16[96,128]{1,0:T(8,128)(2,1)S(1)} %get-tuple-element.61.refs_0_, bf16[96,128]{1,0:T(8,128)(2,1)S(1)} %collective-permute-done.6.refs_1_, bf16[96,128]{1,0:T(8,128)(2,1)S(1)} %collective-permute-done.7.refs_2_, ...), custom_call_target="tpu_custom_call" | custom-call | flops 110000000 | bytes 1343488 | tf_op jit(solution)/shard_map/conv_norm/pallas_call | solution.py:447
  21.1 1.6 %collective-permute-start.10 = (bf16[128,768]{1,0:T(8,128)(2,1)S(1)}, bf16[128,768]{1,0:T(8,128)(2,1)S(1)}, u32[]{:S(2)}, u32[]{:S(2)}) collective-permute-start(bf16[128,768]{1,0:T(8,128)(2,1)S(1)} %get-tuple-element.62.refs_1_), channel_id=1, source_target_pairs={{0,1},{1,0},{2,3},{3,2},{4,5},{5,4},{6,7},{7,6},{8,9},{9,8},{10,11... | collective-permute-start | bytes 589832 | tf_op jit(solution)/shard_map/ppermute | solution.py:492
  22.7 0.0 collective-permute-done.9.far_ref.refs_7_.refs_8_
  22.7 1.5 %far_norm.1 = (bf16[128,768]{1,0:T(8,128)(2,1)S(1)}, f32[128,768]{1,0:T(8,128)S(1)}, f32[128,128]{1,0:T(8,128)S(1)}, bf16[128,384]{1,0:T(8,128)(2,1)S(1)}) custom-call(f32[6,128,128]{2,1,0:T(8,128)S(1)} %get-tuple-element.63.taps_ref.refs_6_, bf16[256,768]{1,0:T(8,128)(2,1)S(1)} %collective-permute-done.9.far_ref.refs_7_.refs_8_), custom_call_target="tpu_custom_call" | custom-call | flops 1100000000 | bytes 1540096 | tf_op jit(solution)/shard_map/far_norm/pallas_call | solution.py:447
  24.2 0.1 collective-permute-start.11
  24.3 0.5 collective-permute-start.12
  24.8 0.0 collective-permute-done.5.refs_2_
  24.8 0.1 order.1.refs_0_.weight
  24.9 0.0 collective-permute-done.10.refs_3_
  24.9 1.0 %collective-permute-done.12.refs_8_ = bf16[128,384]{1,0:T(8,128)(2,1)S(1)} collective-permute-done((bf16[128,384]{1,0:T(8,128)(2,1)S(1)}, bf16[128,384]{1,0:T(8,128)(2,1)S(1)}, u32[]{:S(2)}, u32[]{:S(2)}) %collective-permute-start.12) | collective-permute-done | bytes 98336 | tf_op jit(solution)/shard_map/ppermute | solution.py:492
  25.9 0.0 collective-permute-done.11.refs_4_
  25.9 1.5 %project.1 = (f32[192,384]{1,0:T(8,128)S(1)}, bf16[192,384]{1,0:T(8,128)(2,1)S(1)}, bf16[192,384]{1,0:T(8,128)(2,1)S(1)}, bf16[192,384]{1,0:T(8,128)(2,1)S(1)}, bf16[512,384]{1,0:T(8,128)(2,1)S(1)}) custom-call(bf16[768,384]{1,0:T(8,128)(2,1)S(1)} %order.1.refs_0_.weight, bf16[128,768]{1,0:T(8,128)(2,1)S(1)} %get-tuple-element.62.refs_1_, ...), custom_call_target="tpu_custom_call" | custom-call | flops 1760000000 | bytes 3588096 | tf_op jit(solution)/shard_map/project/pallas_call | solution.py:447
  27.4 0.6 %back_project.1 = (f32[256,768]{1,0:T(8,128)S(1)}, f32[256,768]{1,0:T(8,128)S(1)}) custom-call(bf16[768,384]{1,0:T(8,128)(2,1)S(1)} %order.1.refs_0_.weight, bf16[512,384]{1,0:T(8,128)(2,1)S(1)} %get-tuple-element.72.gp_ref), custom_call_target="tpu_custom_call" | custom-call | flops 770000000 | bytes 2555904 | tf_op jit(solution)/shard_map/back_project/pallas_call | solution.py:447
  28.0 0.3 collective-permute-start.16
  28.3 0.9 %collective-permute-start.13 = (bf16[192,384]{1,0:T(8,128)(2,1)S(1)}, bf16[192,384]{1,0:T(8,128)(2,1)S(1)}, u32[]{:S(2)}, u32[]{:S(2)}) collective-permute-start(bf16[192,384]{1,0:T(8,128)(2,1)S(1)} %get-tuple-element.69), channel_id=1, source_target_pairs={{0,6},{2,4},{4,2},{6,0},{8,14},{10,12},{12,10},{14,8},{16,22},{18,... | collective-permute-start | bytes 442376 | tf_op jit(solution)/shard_map/ppermute | solution.py:474
  29.2 0.9 %collective-permute-start.14 = (bf16[192,384]{1,0:T(8,128)(2,1)S(1)}, bf16[192,384]{1,0:T(8,128)(2,1)S(1)}, u32[]{:S(2)}, u32[]{:S(2)}) collective-permute-start(bf16[192,384]{1,0:T(8,128)(2,1)S(1)} %get-tuple-element.70), channel_id=1, source_target_pairs={{0,4},{2,6},{4,0},{6,2},{8,12},{10,14},{12,8},{14,10},{16,20},{18,... | collective-permute-start | bytes 442376 | tf_op jit(solution)/shard_map/ppermute | solution.py:474
  30.1 1.7 %collective-permute-start.15 = (bf16[192,384]{1,0:T(8,128)(2,1)S(1)}, bf16[192,384]{1,0:T(8,128)(2,1)S(1)}, u32[]{:S(2)}, u32[]{:S(2)}) collective-permute-start(bf16[192,384]{1,0:T(8,128)(2,1)S(1)} %get-tuple-element.71), channel_id=1, source_target_pairs={{0,2},{2,0},{4,6},{6,4},{8,10},{10,8},{12,14},{14,12},{16,18},{18,... | collective-permute-start | bytes 442376 | tf_op jit(solution)/shard_map/ppermute | solution.py:474
  31.8 0.0 collective-permute-done.16.refs_1_
  31.8 3.2 %norm_back.1 = (f32[96,128]{1,0:T(8,128)S(1)}, bf16[96,128]{1,0:T(8,128)(2,1)S(1)}, bf16[96,128]{1,0:T(8,128)(2,1)S(1)}, bf16[96,128]{1,0:T(8,128)(2,1)S(1)}, f3...) custom-call(f32[256,768]{1,0:T(8,128)S(1)} %get-tuple-element.73.refs_0_, ...), custom_call_target="tpu_custom_call" | custom-call | flops 110000000 | bytes 4186112 | tf_op jit(solution)/shard_map/norm_back/pallas_call | solution.py:447
  35.1 0.2 collective-permute-start.17
  35.2 1.4 %collective-permute-start.18 = (bf16[96,128]{1,0:T(8,128)(2,1)S(1)}, bf16[96,128]{1,0:T(8,128)(2,1)S(1)}, u32[]{:S(2)}, u32[]{:S(2)}) collective-permute-start(bf16[96,128]{1,0:T(8,128)(2,1)S(1)} %get-tuple-element.81), channel_id=1, source_target_pairs={{0,5},{1,4},{2,7},{3,6},{4,1},{5,0},{6,3},{7,2},{8,13},{9,12},{10,... | collective-permute-start | bytes 73736 | tf_op jit(solution)/shard_map/ppermute | solution.py:480
  36.6 0.0 collective-permute-done.13.refs_1_
  36.6 0.8 %collective-permute-start.19 = (bf16[96,128]{1,0:T(8,128)(2,1)S(1)}, bf16[96,128]{1,0:T(8,128)(2,1)S(1)}, u32[]{:S(2)}, u32[]{:S(2)}) collective-permute-start(bf16[96,128]{1,0:T(8,128)(2,1)S(1)} %get-tuple-element.82), channel_id=1, source_target_pairs={{0,3},{1,2},{2,1},{3,0},{4,7},{5,6},{6,5},{7,4},{8,11},{9,10},{10,... | collective-permute-start | bytes 73736 | tf_op jit(solution)/shard_map/ppermute | solution.py:480
  37.4 0.9 %collective-permute-done.14.refs_2_ = bf16[192,384]{1,0:T(8,128)(2,1)S(1)} collective-permute-done((bf16[192,384]{1,0:T(8,128)(2,1)S(1)}, bf16[192,384]{1,0:T(8,128)(2,1)S(1)}, u32[]{:S(2)}, u32[]{:S(2)}) %collective-permute-start.14) | collective-permute-done | bytes 147488 | tf_op jit(solution)/shard_map/ppermute | solution.py:474
  38.3 0.0 collective-permute-start.20
  38.3 0.0 collective-permute-done.15.refs_3_
  38.3 0.9 %collective-permute-done.17.refs_5_ = bf16[96,128]{1,0:T(8,128)(2,1)S(1)} collective-permute-done((bf16[96,128]{1,0:T(8,128)(2,1)S(1)}, bf16[96,128]{1,0:T(8,128)(2,1)S(1)}, u32[]{:S(2)}, u32[]{:S(2)}) %collective-permute-start.17) | collective-permute-done | bytes 24608 | tf_op jit(solution)/shard_map/ppermute | solution.py:480
  39.3 0.0 collective-permute-done.18.refs_6_
  39.3 0.6 %collective-permute-done.19.refs_7_ = bf16[96,128]{1,0:T(8,128)(2,1)S(1)} collective-permute-done((bf16[96,128]{1,0:T(8,128)(2,1)S(1)}, bf16[96,128]{1,0:T(8,128)(2,1)S(1)}, u32[]{:S(2)}, u32[]{:S(2)}) %collective-permute-start.19) | collective-permute-done | bytes 24608 | tf_op jit(solution)/shard_map/ppermute | solution.py:480
  39.9 0.2 plane_sum.1
  40.0 2.7 %collective-permute-start.21 = (bf16[56,384]{1,0:T(8,128)(2,1)S(1)}, bf16[56,384]{1,0:T(8,128)(2,1)S(1)}, u32[]{:S(2)}, u32[]{:S(2)}) collective-permute-start(bf16[56,384]{1,0:T(8,128)(2,1)S(1)} %get-tuple-element.88), channel_id=1, source_target_pairs={{0,25},{1,24},{2,27},{3,26},{4,29},{5,28},{6,31},{7,30},{8,17},{9,... | collective-permute-start | bytes 129032 | tf_op jit(solution)/shard_map/ppermute | solution.py:480
  42.8 0.0 collective-permute-start.22
  42.8 1.1 %collective-permute-start.23 = (bf16[56,384]{1,0:T(8,128)(2,1)S(1)}, bf16[56,384]{1,0:T(8,128)(2,1)S(1)}, u32[]{:S(2)}, u32[]{:S(2)}) collective-permute-start(bf16[56,384]{1,0:T(8,128)(2,1)S(1)} %get-tuple-element.90), channel_id=1, source_target_pairs={{0,9},{1,8},{2,11},{3,10},{4,13},{5,12},{6,15},{7,14},{8,1},{9,0},... | collective-permute-start | bytes 129032 | tf_op jit(solution)/shard_map/ppermute | solution.py:480
  43.9 1.3 %collective-permute-done.20.other_ref = bf16[6,8,16,128]{3,2,1,0:T(8,128)(2,1)S(1)} collective-permute-done((bf16[6,8,16,128]{3,2,1,0:T(8,128)(2,1)S(1)}, bf16[6,8,16,128]{3,2,1,0:T(8,128)(2,1)S(1)}, u32[]{:S(2)}, u32[]{:S(2)}) %collective-permute-start.20) | collective-permute-done | bytes 196640 | tf_op jit(solution)/shard_map/ppermute | solution.py:480
  45.2 2.0 %conv_back.1 = bf16[1,8,16,768]{3,2,1,0:T(8,128)(2,1)} custom-call(f32[6,8,16,128]{3,2,1,0:T(8,128)S(1)} %get-tuple-element.84.grad_ref, bf16[6,8,16,128]{3,2,1,0:T(8,128)(2,1)S(1)} %collective-permute-done.20.other_ref, f32[6,128,128]{2,1,0:T(8,128)S(1)} %get-tuple-element.63.taps_ref.refs_6_), custom_call_target="tpu_custom_call" | custom-call | flops 110000000 | bytes 1179648 | tf_op jit(solution)/shard_map/conv_back/pallas_call | solution.py:447
  47.2 0.0 collective-permute-done.21.refs_1_
  47.2 1.8 %collective-permute-done.22.refs_2_ = bf16[56,384]{1,0:T(8,128)(2,1)S(1)} collective-permute-done((bf16[56,384]{1,0:T(8,128)(2,1)S(1)}, bf16[56,384]{1,0:T(8,128)(2,1)S(1)}, u32[]{:S(2)}, u32[]{:S(2)}) %collective-permute-start.22) | collective-permute-done | bytes 43040 | tf_op jit(solution)/shard_map/ppermute | solution.py:480
  48.9 0.0 collective-permute-done.23.refs_3_
  48.9 0.1 line_sum.1.mine_ref
  49.0 0.1 collective-permute-start.24
  49.2 1.4 %collective-permute-done.24.other_ref = f32[48,1280]{1,0:T(8,128)S(1)} collective-permute-done((f32[48,1280]{1,0:T(8,128)S(1)}, f32[48,1280]{1,0:T(8,128)S(1)}, u32[]{:S(2)}, u32[]{:S(2)}) %collective-permute-start.24) | collective-permute-done | bytes 245792 | tf_op jit(solution)/shard_map/ppermute | solution.py:492
  50.6 0.8 %finish.1 = (f32[48,1536]{1,0:T(8,128)}, f32[48,49]{1,0:T(8,128)}, f32[1,48]{1,0:T(1,128)}, f32[1,48]{1,0:T(1,128)}) custom-call(f32[48,1280]{1,0:T(8,128)S(1)} %line_sum.1.mine_ref, f32[48,1280]{1,0:T(8,128)S(1)} %collective-permute-done.24.other_ref), custom_call_target="tpu_custom_call" | custom-call | flops 550000000 | bytes 796224 | tf_op jit(solution)/shard_map/finish/pallas_call | solution.py:447
  (6 shorter events, 0.1 us)
Async XLA Ops:
  0.6 7.1 %copy-start = (bf16[1,8,16,768]{3,2,1,0:T(8,128)(2,1)S(1)}, bf16[1,8,16,768]{3,2,1,0:T(8,128)(2,1)}, u32[]{:S(2)}) copy-start(bf16[1,8,16,768]{3,2,1,0:T(8,128)(2,1)} %param.6) | copy-start | bytes 589828
  0.6 7.1 %copy-start.1 = (bf16[1,8,16,1536]{3,2,1,0:T(8,128)(2,1)S(1)}, bf16[1,8,16,1536]{3,2,1,0:T(8,128)(2,1)}, u32[]{:S(2)}) copy-start(bf16[1,8,16,1536]{3,2,1,0:T(8,128)(2,1)} %param.7) | copy-start | bytes 1179652
  2.4 9.6 %copy-start.2 = (bf16[56,384]{1,0:T(8,128)(2,1)S(1)}, bf16[56,384]{1,0:T(8,128)(2,1)}, u32[]{:S(2)}) copy-start(bf16[56,384]{1,0:T(8,128)(2,1)} %get-tuple-element.53.refs_0_) | copy-start | bytes 129028
  2.4 7.1 %collective-permute-start.1 = (bf16[56,384]{1,0:T(8,128)(2,1)}, bf16[56,384]{1,0:T(8,128)(2,1)S(1)}, u32[]{:S(2)}, u32[]{:S(2)}) collective-permute-start(bf16[56,384]{1,0:T(8,128)(2,1)} %get-tuple-element.55), channel_id=1, source_target_pairs={{0,17},{1,16},{2,19},{3,18},{4,21},{5,20},{6,23},{7,22},{8,25},{9,... | collective-permute-start | bytes 129032 | tf_op jit(solution)/shard_map/ppermute | solution.py:480
  5.9 5.6 %collective-permute-start.2 = (bf16[56,384]{1,0:T(8,128)(2,1)}, bf16[56,384]{1,0:T(8,128)(2,1)S(1)}, u32[]{:S(2)}, u32[]{:S(2)}) collective-permute-start(bf16[56,384]{1,0:T(8,128)(2,1)} %get-tuple-element.54), channel_id=1, source_target_pairs={{0,25},{1,24},{2,27},{3,26},{4,29},{5,28},{6,31},{7,30},{8,17},{9,... | collective-permute-start | bytes 129032 | tf_op jit(solution)/shard_map/ppermute | solution.py:480
  7.5 4.5 %collective-permute-start = (bf16[56,384]{1,0:T(8,128)(2,1)}, bf16[56,384]{1,0:T(8,128)(2,1)S(1)}, u32[]{:S(2)}, u32[]{:S(2)}) collective-permute-start(bf16[56,384]{1,0:T(8,128)(2,1)} %get-tuple-element.54), channel_id=1, source_target_pairs={{0,9},{1,8},{2,11},{3,10},{4,13},{5,12},{6,15},{7,14},{8,1},{9,0},... | collective-permute-start | bytes 129032 | tf_op jit(solution)/shard_map/ppermute | solution.py:480
  7.8 4.4 %collective-permute-start.3 = (bf16[128,768]{1,0:T(8,128)(2,1)S(1)}, bf16[128,768]{1,0:T(8,128)(2,1)S(1)}, u32[]{:S(2)}, u32[]{:S(2)}) collective-permute-start(bf16[128,768]{1,0:T(8,128)(2,1)S(1)} %get-tuple-element.59), channel_id=1, source_target_pairs={{0,1},{1,0},{2,3},{3,2},{4,5},{5,4},{6,7},{7,6},{8,9},{9,8},{10,11... | collective-permute-start | bytes 589832 | tf_op jit(solution)/shard_map/ppermute | solution.py:492
  7.9 14.8 %collective-permute-start.9 = (bf16[256,768]{1,0:T(8,128)(2,1)S(1)}, bf16[256,768]{1,0:T(8,128)(2,1)S(1)}, u32[]{:S(2)}, u32[]{:S(2)}) collective-permute-start(bf16[256,768]{1,0:T(8,128)(2,1)S(1)} %get-tuple-element.64), channel_id=1, source_target_pairs={{0,9},{1,8},{2,11},{3,10},{4,13},{5,12},{6,15},{7,14},{8,1},{9,0},... | collective-permute-start | bytes 1179656 | tf_op jit(solution)/shard_map/ppermute | solution.py:480
  12.2 5.2 %collective-permute-start.4 = (bf16[192,384]{1,0:T(8,128)(2,1)S(1)}, bf16[192,384]{1,0:T(8,128)(2,1)S(1)}, u32[]{:S(2)}, u32[]{:S(2)}) collective-permute-start(bf16[192,384]{1,0:T(8,128)(2,1)S(1)} %get-tuple-element.60.own_ref.refs_0_), channel_id=1, source_target_pairs={{0,2},{1,5},{2,0},{3,7},{4,6},{5,1},{6,4},{7,3},{8,10},{9,13},{10,... | collective-permute-start | bytes 442376 | tf_op jit(solution)/shard_map/ppermute | solution.py:489
  13.8 5.5 %collective-permute-start.8 = (bf16[96,128]{1,0:T(8,128)(2,1)S(1)}, bf16[96,128]{1,0:T(8,128)(2,1)S(1)}, u32[]{:S(2)}, u32[]{:S(2)}) collective-permute-start(bf16[96,128]{1,0:T(8,128)(2,1)S(1)} %get-tuple-element.61.refs_0_), channel_id=1, source_target_pairs={{0,7},{1,6},{2,5},{3,4},{4,3},{5,2},{6,1},{7,0},{8,15},{9,14},{10,... | collective-permute-start | bytes 73736 | tf_op jit(solution)/shard_map/ppermute | solution.py:480
  15.5 3.8 %collective-permute-start.7 = (bf16[96,128]{1,0:T(8,128)(2,1)S(1)}, bf16[96,128]{1,0:T(8,128)(2,1)S(1)}, u32[]{:S(2)}, u32[]{:S(2)}) collective-permute-start(bf16[96,128]{1,0:T(8,128)(2,1)S(1)} %get-tuple-element.61.refs_0_), channel_id=1, source_target_pairs={{0,5},{1,4},{2,7},{3,6},{4,1},{5,0},{6,3},{7,2},{8,13},{9,12},{10,... | collective-permute-start | bytes 73736 | tf_op jit(solution)/shard_map/ppermute | solution.py:480
  15.5 3.8 %collective-permute-start.6 = (bf16[96,128]{1,0:T(8,128)(2,1)S(1)}, bf16[96,128]{1,0:T(8,128)(2,1)S(1)}, u32[]{:S(2)}, u32[]{:S(2)}) collective-permute-start(bf16[96,128]{1,0:T(8,128)(2,1)S(1)} %get-tuple-element.61.refs_0_), channel_id=1, source_target_pairs={{0,3},{1,2},{2,1},{3,0},{4,7},{5,6},{6,5},{7,4},{8,11},{9,10},{10,... | collective-permute-start | bytes 73736 | tf_op jit(solution)/shard_map/ppermute | solution.py:480
  17.4 7.4 %collective-permute-start.5 = (bf16[384,384]{1,0:T(8,128)(2,1)S(1)}, bf16[384,384]{1,0:T(8,128)(2,1)S(1)}, u32[]{:S(2)}, u32[]{:S(2)}) collective-permute-start(bf16[384,384]{1,0:T(8,128)(2,1)S(1)} %join.1), channel_id=1, source_target_pairs={{0,4},{1,3},{2,6},{3,1},{4,0},{5,7},{6,2},{7,5},{8,12},{9,11},{10,... | collective-permute-start | bytes 884744 | tf_op jit(solution)/shard_map/ppermute | solution.py:489
  21.1 3.8 %collective-permute-start.10 = (bf16[128,768]{1,0:T(8,128)(2,1)S(1)}, bf16[128,768]{1,0:T(8,128)(2,1)S(1)}, u32[]{:S(2)}, u32[]{:S(2)}) collective-permute-start(bf16[128,768]{1,0:T(8,128)(2,1)S(1)} %get-tuple-element.62.refs_1_), channel_id=1, source_target_pairs={{0,1},{1,0},{2,3},{3,2},{4,5},{5,4},{6,7},{7,6},{8,9},{9,8},{10,11... | collective-permute-start | bytes 589832 | tf_op jit(solution)/shard_map/ppermute | solution.py:492
  24.2 1.7 %collective-permute-start.11 = (bf16[128,768]{1,0:T(8,128)(2,1)S(1)}, bf16[128,768]{1,0:T(8,128)(2,1)S(1)}, u32[]{:S(2)}, u32[]{:S(2)}) collective-permute-start(bf16[128,768]{1,0:T(8,128)(2,1)S(1)} %get-tuple-element.65.refs_2_), channel_id=1, source_target_pairs={{0,1},{1,0},{2,3},{3,2},{4,5},{5,4},{6,7},{7,6},{8,9},{9,8},{10,11... | collective-permute-start | bytes 589832 | tf_op jit(solution)/shard_map/ppermute | solution.py:492
  24.3 1.6 %collective-permute-start.12 = (bf16[128,384]{1,0:T(8,128)(2,1)S(1)}, bf16[128,384]{1,0:T(8,128)(2,1)S(1)}, u32[]{:S(2)}, u32[]{:S(2)}) collective-permute-start(bf16[128,384]{1,0:T(8,128)(2,1)S(1)} %get-tuple-element.67), channel_id=1, source_target_pairs={{0,1},{1,0},{2,3},{3,2},{4,5},{5,4},{6,7},{7,6},{8,9},{9,8},{10,11... | collective-permute-start | bytes 294920 | tf_op jit(solution)/shard_map/ppermute | solution.py:492
  28.0 3.8 %collective-permute-start.16 = (f32[256,768]{1,0:T(8,128)S(1)}, f32[256,768]{1,0:T(8,128)S(1)}, u32[]{:S(2)}, u32[]{:S(2)}) collective-permute-start(f32[256,768]{1,0:T(8,128)S(1)} %get-tuple-element.74), channel_id=1, source_target_pairs={{0,1},{1,0},{2,3},{3,2},{4,5},{5,4},{6,7},{7,6},{8,9},{9,8},{10,11... | collective-permute-start | bytes 2359304 | tf_op jit(solution)/shard_map/ppermute | solution.py:492
  28.3 8.3 %collective-permute-start.13 = (bf16[192,384]{1,0:T(8,128)(2,1)S(1)}, bf16[192,384]{1,0:T(8,128)(2,1)S(1)}, u32[]{:S(2)}, u32[]{:S(2)}) collective-permute-start(bf16[192,384]{1,0:T(8,128)(2,1)S(1)} %get-tuple-element.69), channel_id=1, source_target_pairs={{0,6},{2,4},{4,2},{6,0},{8,14},{10,12},{12,10},{14,8},{16,22},{18,... | collective-permute-start | bytes 442376 | tf_op jit(solution)/shard_map/ppermute | solution.py:474
  29.2 9.1 %collective-permute-start.14 = (bf16[192,384]{1,0:T(8,128)(2,1)S(1)}, bf16[192,384]{1,0:T(8,128)(2,1)S(1)}, u32[]{:S(2)}, u32[]{:S(2)}) collective-permute-start(bf16[192,384]{1,0:T(8,128)(2,1)S(1)} %get-tuple-element.70), channel_id=1, source_target_pairs={{0,4},{2,6},{4,0},{6,2},{8,12},{10,14},{12,8},{14,10},{16,20},{18,... | collective-permute-start | bytes 442376 | tf_op jit(solution)/shard_map/ppermute | solution.py:474
  30.1 8.2 %collective-permute-start.15 = (bf16[192,384]{1,0:T(8,128)(2,1)S(1)}, bf16[192,384]{1,0:T(8,128)(2,1)S(1)}, u32[]{:S(2)}, u32[]{:S(2)}) collective-permute-start(bf16[192,384]{1,0:T(8,128)(2,1)S(1)} %get-tuple-element.71), channel_id=1, source_target_pairs={{0,2},{2,0},{4,6},{6,4},{8,10},{10,8},{12,14},{14,12},{16,18},{18,... | collective-permute-start | bytes 442376 | tf_op jit(solution)/shard_map/ppermute | solution.py:474
  35.1 4.2 %collective-permute-start.17 = (bf16[96,128]{1,0:T(8,128)(2,1)S(1)}, bf16[96,128]{1,0:T(8,128)(2,1)S(1)}, u32[]{:S(2)}, u32[]{:S(2)}) collective-permute-start(bf16[96,128]{1,0:T(8,128)(2,1)S(1)} %get-tuple-element.80), channel_id=1, source_target_pairs={{0,7},{1,6},{2,5},{3,4},{4,3},{5,2},{6,1},{7,0},{8,15},{9,14},{10,... | collective-permute-start | bytes 73736 | tf_op jit(solution)/shard_map/ppermute | solution.py:480
  35.2 4.0 %collective-permute-start.18 = (bf16[96,128]{1,0:T(8,128)(2,1)S(1)}, bf16[96,128]{1,0:T(8,128)(2,1)S(1)}, u32[]{:S(2)}, u32[]{:S(2)}) collective-permute-start(bf16[96,128]{1,0:T(8,128)(2,1)S(1)} %get-tuple-element.81), channel_id=1, source_target_pairs={{0,5},{1,4},{2,7},{3,6},{4,1},{5,0},{6,3},{7,2},{8,13},{9,12},{10,... | collective-permute-start | bytes 73736 | tf_op jit(solution)/shard_map/ppermute | solution.py:480
  36.6 3.3 %collective-permute-start.19 = (bf16[96,128]{1,0:T(8,128)(2,1)S(1)}, bf16[96,128]{1,0:T(8,128)(2,1)S(1)}, u32[]{:S(2)}, u32[]{:S(2)}) collective-permute-start(bf16[96,128]{1,0:T(8,128)(2,1)S(1)} %get-tuple-element.82), channel_id=1, source_target_pairs={{0,3},{1,2},{2,1},{3,0},{4,7},{5,6},{6,5},{7,4},{8,11},{9,10},{10,... | collective-permute-start | bytes 73736 | tf_op jit(solution)/shard_map/ppermute | solution.py:480
  38.3 6.9 %collective-permute-start.20 = (bf16[6,8,16,128]{3,2,1,0:T(8,128)(2,1)S(1)}, bf16[6,8,16,128]{3,2,1,0:T(8,128)(2,1)S(1)}, u32[]{:S(2)}, u32[]{:S(2)}) collective-permute-start(bf16[6,8,16,128]{3,2,1,0:T(8,128)(2,1)S(1)} %get-tuple-element.85), channel_id=1, source_target_pairs={{0,9},{1,8},{2,11},{3,10},{4,13},{5,12},{6,15},{7,14},{8,1},{9,0},... | collective-permute-start | bytes 589832 | tf_op jit(solution)/shard_map/ppermute | solution.py:480
  40.0 7.2 %collective-permute-start.21 = (bf16[56,384]{1,0:T(8,128)(2,1)S(1)}, bf16[56,384]{1,0:T(8,128)(2,1)S(1)}, u32[]{:S(2)}, u32[]{:S(2)}) collective-permute-start(bf16[56,384]{1,0:T(8,128)(2,1)S(1)} %get-tuple-element.88), channel_id=1, source_target_pairs={{0,25},{1,24},{2,27},{3,26},{4,29},{5,28},{6,31},{7,30},{8,17},{9,... | collective-permute-start | bytes 129032 | tf_op jit(solution)/shard_map/ppermute | solution.py:480
  42.8 6.2 %collective-permute-start.22 = (bf16[56,384]{1,0:T(8,128)(2,1)S(1)}, bf16[56,384]{1,0:T(8,128)(2,1)S(1)}, u32[]{:S(2)}, u32[]{:S(2)}) collective-permute-start(bf16[56,384]{1,0:T(8,128)(2,1)S(1)} %get-tuple-element.89), channel_id=1, source_target_pairs={{0,17},{1,16},{2,19},{3,18},{4,21},{5,20},{6,23},{7,22},{8,25},{9,... | collective-permute-start | bytes 129032 | tf_op jit(solution)/shard_map/ppermute | solution.py:480
  42.8 6.2 %collective-permute-start.23 = (bf16[56,384]{1,0:T(8,128)(2,1)S(1)}, bf16[56,384]{1,0:T(8,128)(2,1)S(1)}, u32[]{:S(2)}, u32[]{:S(2)}) collective-permute-start(bf16[56,384]{1,0:T(8,128)(2,1)S(1)} %get-tuple-element.90), channel_id=1, source_target_pairs={{0,9},{1,8},{2,11},{3,10},{4,13},{5,12},{6,15},{7,14},{8,1},{9,0},... | collective-permute-start | bytes 129032 | tf_op jit(solution)/shard_map/ppermute | solution.py:480
  49.0 1.5 %collective-permute-start.24 = (f32[48,1280]{1,0:T(8,128)S(1)}, f32[48,1280]{1,0:T(8,128)S(1)}, u32[]{:S(2)}, u32[]{:S(2)}) collective-permute-start(f32[48,1280]{1,0:T(8,128)S(1)} %line_sum.1.mine_ref), channel_id=1, source_target_pairs={{0,1},{1,0},{2,3},{3,2},{4,5},{5,4},{6,7},{7,6},{8,9},{9,8},{10,11... | collective-permute-start | bytes 737288 | tf_op jit(solution)/shard_map/ppermute | solution.py:492

commit v20 on v19

--- a/solution.py
+++ b/solution.py
@@ -152,11 +152,15 @@
         out[...] = with_small(total, extras[rows, :]).astype(out.dtype)
 
 
+def line_order(lines):
+    return [*range(2, lines), 1]
+
+
 def line_sum_kernel(own, *refs):
     pieces, total_ref = refs[:-1], refs[-1]
     quarter = (total_ref.shape[1] - LANES) // 3
     near, far = None, None
-    for line, piece in zip(range(len(pieces) - 1, 0, -1), pieces[1:]):
+    for line, piece in zip(line_order(len(pieces)), pieces[1:]):
         came = piece[...].astype(F32)
         if line % 2:
             far = came if far is None else far + came
@@ -694,7 +698,7 @@
         *small_arrived,
     )
     home, grad_images = lax.optimization_barrier((home, grad_images))
-    came = [crossing(sent[line - 1], INNER * line) for line in range(lines - 1, 0, -1)]
+    came = [crossing(sent[line - 1], INNER * line) for line in line_order(lines)]
     (total,) = call(
         functools.partial(line_sum_kernel, own),
         "line_sum",

time: 51.5 us -> 51 us (level)
  waiting for transfers between devices: 10.6 us -> 10 us
    ppermute x6, starting transfers between devices: 2.69 us -> 3.3 us  [over_core(): return lax.ppermute(array, 'rep', [(i, i ^ 1) for i in range(reps)])]
  transfers between devices with their start and end apart: 25 -> 25, of which waited for: 10 -> 9; matrix products, arithmetic and copies ran while one was open for 0% -> 0% of each run, Pallas kernels for 17% -> 18%
where the time goes in v20:
time: 51 us; the launch traced here: 50.8 us
  starting transfers between devices  26.4 us (52%)
  Pallas kernels  13.7 us (27%)
  waiting for transfers between devices  10 us (20%)
  between operations  0.75 us (1%)
    ppermute x14, starting transfers between devices, crossing(): return lax.ppermute(array, ('shard', 'rep'), pairs)  16.2 us
    pallas_call x14, Pallas kernels, call(): pl.pallas_call(kernel, out_shape=outs, in_specs=[VMEM] * len(args), out_s...  13.7 us
    ppermute x14, waiting for transfers between devices, crossing(): return lax.ppermute(array, ('shard', 'rep'), pairs)  6.75 us
    ppermute x3, starting transfers between devices, over_shard(): return lax.ppermute(array, 'shard', [(i, i ^ flip) for i in range(shards)])  3.49 us
    ppermute x2, starting transfers between devices, hop(): return lax.ppermute(array, ('shard', 'rep'), pairs)  3.4 us
    ppermute x6, starting transfers between devices, over_core(): return lax.ppermute(array, 'rep', [(i, i ^ 1) for i in range(reps)])  3.3 us
    ppermute x6, waiting for transfers between devices, over_core(): return lax.ppermute(array, 'rep', [(i, i ^ 1) for i in range(reps)])  2.13 us
  transfers between devices with their start and end apart: 25, of which 9 were waited for; matrix products, arithmetic and copies ran while one was open for 0% of the time, Pallas kernels for 18%

profile of v20, /device:TPU:0, one launch (start us, length us, event | category | flops | bytes accessed | tf_op | source)
XLA Modules:
  0.0 50.8 jit_solution(15939919490032118618)
XLA Ops:
  0.7 1.8 %pack.1 = (bf16[56,384]{1,0:T(8,128)(2,1)}, bf16[56,384]{1,0:T(8,128)(2,1)}, bf16[56,384]{1,0:T(8,128)(2,1)}) custom-call(bf16[48,1536]{1,0:T(8,128)(2,1)} %w_ref.1, bf16[48,49]{1,0:T(8,128)(2,1)} %dw_ref.1, bf16[1,48]{1,0:T(2,128)(2,1)} %bitcast.11, bf16[1,48]{1,0:T(2,128)(2,1)} %bitcast.12), custom_call_target="tpu_custom_call" | custom-call | flops 550000000 | bytes 281376 | tf_op jit(solution)/shard_map/pack/pallas_call | solution.py:451
  2.4 3.5 %collective-permute-start.1 = (bf16[56,384]{1,0:T(8,128)(2,1)}, bf16[56,384]{1,0:T(8,128)(2,1)S(1)}, u32[]{:S(2)}, u32[]{:S(2)}) collective-permute-start(bf16[56,384]{1,0:T(8,128)(2,1)} %get-tuple-element.55), channel_id=1, source_target_pairs={{0,17},{1,16},{2,19},{3,18},{4,21},{5,20},{6,23},{7,22},{8,25},{9,... | collective-permute-start | bytes 129032 | tf_op jit(solution)/shard_map/ppermute | solution.py:484
  5.9 1.6 %collective-permute-start.2 = (bf16[56,384]{1,0:T(8,128)(2,1)}, bf16[56,384]{1,0:T(8,128)(2,1)S(1)}, u32[]{:S(2)}, u32[]{:S(2)}) collective-permute-start(bf16[56,384]{1,0:T(8,128)(2,1)} %get-tuple-element.54), channel_id=1, source_target_pairs={{0,25},{1,24},{2,27},{3,26},{4,29},{5,28},{6,31},{7,30},{8,17},{9,... | collective-permute-start | bytes 129032 | tf_op jit(solution)/shard_map/ppermute | solution.py:484
  7.5 0.2 collective-permute-start
  7.8 0.0 copy-done.1
  7.8 0.1 collective-permute-start.3
  7.9 1.7 %collective-permute-start.9 = (bf16[256,768]{1,0:T(8,128)(2,1)S(1)}, bf16[256,768]{1,0:T(8,128)(2,1)S(1)}, u32[]{:S(2)}, u32[]{:S(2)}) collective-permute-start(bf16[256,768]{1,0:T(8,128)(2,1)S(1)} %get-tuple-element.64), channel_id=1, source_target_pairs={{0,9},{1,8},{2,11},{3,10},{4,13},{5,12},{6,15},{7,14},{8,1},{9,0},... | collective-permute-start | bytes 1179656 | tf_op jit(solution)/shard_map/ppermute | solution.py:484
  9.6 0.0 collective-permute-done.1.refs_2_
  9.6 1.9 %collective-permute-done.2.refs_3_ = bf16[56,384]{1,0:T(8,128)(2,1)S(1)} collective-permute-done((bf16[56,384]{1,0:T(8,128)(2,1)}, bf16[56,384]{1,0:T(8,128)(2,1)S(1)}, u32[]{:S(2)}, u32[]{:S(2)}) %collective-permute-start.2) | collective-permute-done | bytes 43040 | tf_op jit(solution)/shard_map/ppermute | solution.py:484
  11.5 0.6 %collective-permute-done.refs_1_ = bf16[56,384]{1,0:T(8,128)(2,1)S(1)} collective-permute-done((bf16[56,384]{1,0:T(8,128)(2,1)}, bf16[56,384]{1,0:T(8,128)(2,1)S(1)}, u32[]{:S(2)}, u32[]{:S(2)}) %collective-permute-start) | collective-permute-done | bytes 43040 | tf_op jit(solution)/shard_map/ppermute | solution.py:484
  12.0 0.0 copy-done.2
  12.0 0.1 assemble.1
  12.2 0.0 collective-permute-done.3.refs_6_
  12.2 1.6 %collective-permute-start.4 = (bf16[192,384]{1,0:T(8,128)(2,1)S(1)}, bf16[192,384]{1,0:T(8,128)(2,1)S(1)}, u32[]{:S(2)}, u32[]{:S(2)}) collective-permute-start(bf16[192,384]{1,0:T(8,128)(2,1)S(1)} %get-tuple-element.60.own_ref.refs_0_), channel_id=1, source_target_pairs={{0,2},{1,5},{2,0},{3,7},{4,6},{5,1},{6,4},{7,3},{8,10},{9,13},{10,... | collective-permute-start | bytes 442376 | tf_op jit(solution)/shard_map/ppermute | solution.py:493
  13.8 1.7 %collective-permute-start.8 = (bf16[96,128]{1,0:T(8,128)(2,1)S(1)}, bf16[96,128]{1,0:T(8,128)(2,1)S(1)}, u32[]{:S(2)}, u32[]{:S(2)}) collective-permute-start(bf16[96,128]{1,0:T(8,128)(2,1)S(1)} %get-tuple-element.61.refs_0_), channel_id=1, source_target_pairs={{0,7},{1,6},{2,5},{3,4},{4,3},{5,2},{6,1},{7,0},{8,15},{9,14},{10,... | collective-permute-start | bytes 73736 | tf_op jit(solution)/shard_map/ppermute | solution.py:484
  15.5 0.0 collective-permute-start.7
  15.5 1.8 %collective-permute-start.6 = (bf16[96,128]{1,0:T(8,128)(2,1)S(1)}, bf16[96,128]{1,0:T(8,128)(2,1)S(1)}, u32[]{:S(2)}, u32[]{:S(2)}) collective-permute-start(bf16[96,128]{1,0:T(8,128)(2,1)S(1)} %get-tuple-element.61.refs_0_), channel_id=1, source_target_pairs={{0,3},{1,2},{2,1},{3,0},{4,7},{5,6},{6,5},{7,4},{8,11},{9,10},{10,... | collective-permute-start | bytes 73736 | tf_op jit(solution)/shard_map/ppermute | solution.py:484
  17.2 0.2 collective-permute-done.4.came_ref.refs_1_
  17.4 1.8 %collective-permute-start.5 = (bf16[384,384]{1,0:T(8,128)(2,1)S(1)}, bf16[384,384]{1,0:T(8,128)(2,1)S(1)}, u32[]{:S(2)}, u32[]{:S(2)}) collective-permute-start(bf16[384,384]{1,0:T(8,128)(2,1)S(1)} %join.1), channel_id=1, source_target_pairs={{0,4},{1,3},{2,6},{3,1},{4,0},{5,7},{6,2},{7,5},{8,12},{9,11},{10,... | collective-permute-start | bytes 884744 | tf_op jit(solution)/shard_map/ppermute | solution.py:493
  19.3 0.0 collective-permute-done.8.refs_3_
  19.3 0.0 collective-permute-done.7.refs_2_
  19.3 0.0 collective-permute-done.6.refs_1_
  19.3 1.8 %conv_norm.1 = (bf16[128,768]{1,0:T(8,128)(2,1)S(1)}, f32[128,768]{1,0:T(8,128)S(1)}, f32[128,128]{1,0:T(8,128)S(1)}, f32[6,128,128]{2,1,0:T(8,128)S(1)}) custom-call(bf16[96,128]{1,0:T(8,128)(2,1)S(1)} %get-tuple-element.61.refs_0_, bf16[96,128]{1,0:T(8,128)(2,1)S(1)} %collective-permute-done.6.refs_1_, bf16[96,128]{1,0:T(8,128)(2,1)S(1)} %collective-permute-done.7.refs_2_, ...), custom_call_target="tpu_custom_call" | custom-call | flops 110000000 | bytes 1343488 | tf_op jit(solution)/shard_map/conv_norm/pallas_call | solution.py:451
  21.1 1.6 %collective-permute-start.10 = (bf16[128,768]{1,0:T(8,128)(2,1)S(1)}, bf16[128,768]{1,0:T(8,128)(2,1)S(1)}, u32[]{:S(2)}, u32[]{:S(2)}) collective-permute-start(bf16[128,768]{1,0:T(8,128)(2,1)S(1)} %get-tuple-element.62.refs_1_), channel_id=1, source_target_pairs={{0,1},{1,0},{2,3},{3,2},{4,5},{5,4},{6,7},{7,6},{8,9},{9,8},{10,11... | collective-permute-start | bytes 589832 | tf_op jit(solution)/shard_map/ppermute | solution.py:496
  22.7 0.0 collective-permute-done.9.far_ref.refs_7_.refs_8_
  22.7 1.5 %far_norm.1 = (bf16[128,768]{1,0:T(8,128)(2,1)S(1)}, f32[128,768]{1,0:T(8,128)S(1)}, f32[128,128]{1,0:T(8,128)S(1)}, bf16[128,384]{1,0:T(8,128)(2,1)S(1)}) custom-call(f32[6,128,128]{2,1,0:T(8,128)S(1)} %get-tuple-element.63.taps_ref.refs_6_, bf16[256,768]{1,0:T(8,128)(2,1)S(1)} %collective-permute-done.9.far_ref.refs_7_.refs_8_), custom_call_target="tpu_custom_call" | custom-call | flops 1100000000 | bytes 1540096 | tf_op jit(solution)/shard_map/far_norm/pallas_call | solution.py:451
  24.2 0.1 collective-permute-start.11
  24.3 0.5 collective-permute-start.12
  24.8 0.0 collective-permute-done.5.refs_2_
  24.8 0.1 order.1.refs_0_.weight
  24.9 0.0 collective-permute-done.10.refs_3_
  24.9 1.0 %collective-permute-done.12.refs_8_ = bf16[128,384]{1,0:T(8,128)(2,1)S(1)} collective-permute-done((bf16[128,384]{1,0:T(8,128)(2,1)S(1)}, bf16[128,384]{1,0:T(8,128)(2,1)S(1)}, u32[]{:S(2)}, u32[]{:S(2)}) %collective-permute-start.12) | collective-permute-done | bytes 98336 | tf_op jit(solution)/shard_map/ppermute | solution.py:496
  25.9 0.0 collective-permute-done.11.refs_4_
  25.9 1.5 %project.1 = (f32[192,384]{1,0:T(8,128)S(1)}, bf16[192,384]{1,0:T(8,128)(2,1)S(1)}, bf16[192,384]{1,0:T(8,128)(2,1)S(1)}, bf16[192,384]{1,0:T(8,128)(2,1)S(1)}, bf16[512,384]{1,0:T(8,128)(2,1)S(1)}) custom-call(bf16[768,384]{1,0:T(8,128)(2,1)S(1)} %order.1.refs_0_.weight, bf16[128,768]{1,0:T(8,128)(2,1)S(1)} %get-tuple-element.62.refs_1_, ...), custom_call_target="tpu_custom_call" | custom-call | flops 1760000000 | bytes 3588096 | tf_op jit(solution)/shard_map/project/pallas_call | solution.py:451
  27.4 0.6 %back_project.1 = (f32[256,768]{1,0:T(8,128)S(1)}, f32[256,768]{1,0:T(8,128)S(1)}) custom-call(bf16[768,384]{1,0:T(8,128)(2,1)S(1)} %order.1.refs_0_.weight, bf16[512,384]{1,0:T(8,128)(2,1)S(1)} %get-tuple-element.72.gp_ref), custom_call_target="tpu_custom_call" | custom-call | flops 770000000 | bytes 2555904 | tf_op jit(solution)/shard_map/back_project/pallas_call | solution.py:451
  28.0 0.3 collective-permute-start.16
  28.3 0.9 %collective-permute-start.13 = (bf16[192,384]{1,0:T(8,128)(2,1)S(1)}, bf16[192,384]{1,0:T(8,128)(2,1)S(1)}, u32[]{:S(2)}, u32[]{:S(2)}) collective-permute-start(bf16[192,384]{1,0:T(8,128)(2,1)S(1)} %get-tuple-element.69), channel_id=1, source_target_pairs={{0,6},{2,4},{4,2},{6,0},{8,14},{10,12},{12,10},{14,8},{16,22},{18,... | collective-permute-start | bytes 442376 | tf_op jit(solution)/shard_map/ppermute | solution.py:478
  29.2 0.9 %collective-permute-start.14 = (bf16[192,384]{1,0:T(8,128)(2,1)S(1)}, bf16[192,384]{1,0:T(8,128)(2,1)S(1)}, u32[]{:S(2)}, u32[]{:S(2)}) collective-permute-start(bf16[192,384]{1,0:T(8,128)(2,1)S(1)} %get-tuple-element.70), channel_id=1, source_target_pairs={{0,4},{2,6},{4,0},{6,2},{8,12},{10,14},{12,8},{14,10},{16,20},{18,... | collective-permute-start | bytes 442376 | tf_op jit(solution)/shard_map/ppermute | solution.py:478
  30.1 1.7 %collective-permute-start.15 = (bf16[192,384]{1,0:T(8,128)(2,1)S(1)}, bf16[192,384]{1,0:T(8,128)(2,1)S(1)}, u32[]{:S(2)}, u32[]{:S(2)}) collective-permute-start(bf16[192,384]{1,0:T(8,128)(2,1)S(1)} %get-tuple-element.71), channel_id=1, source_target_pairs={{0,2},{2,0},{4,6},{6,4},{8,10},{10,8},{12,14},{14,12},{16,18},{18,... | collective-permute-start | bytes 442376 | tf_op jit(solution)/shard_map/ppermute | solution.py:478
  31.8 0.0 collective-permute-done.16.refs_1_
  31.8 3.2 %norm_back.1 = (f32[96,128]{1,0:T(8,128)S(1)}, bf16[96,128]{1,0:T(8,128)(2,1)S(1)}, bf16[96,128]{1,0:T(8,128)(2,1)S(1)}, bf16[96,128]{1,0:T(8,128)(2,1)S(1)}, f3...) custom-call(f32[256,768]{1,0:T(8,128)S(1)} %get-tuple-element.73.refs_0_, ...), custom_call_target="tpu_custom_call" | custom-call | flops 110000000 | bytes 4186112 | tf_op jit(solution)/shard_map/norm_back/pallas_call | solution.py:451
  35.1 0.2 collective-permute-start.17
  35.2 1.4 %collective-permute-start.18 = (bf16[96,128]{1,0:T(8,128)(2,1)S(1)}, bf16[96,128]{1,0:T(8,128)(2,1)S(1)}, u32[]{:S(2)}, u32[]{:S(2)}) collective-permute-start(bf16[96,128]{1,0:T(8,128)(2,1)S(1)} %get-tuple-element.81), channel_id=1, source_target_pairs={{0,5},{1,4},{2,7},{3,6},{4,1},{5,0},{6,3},{7,2},{8,13},{9,12},{10,... | collective-permute-start | bytes 73736 | tf_op jit(solution)/shard_map/ppermute | solution.py:484
  36.6 0.0 collective-permute-done.13.refs_1_
  36.6 0.8 %collective-permute-start.19 = (bf16[96,128]{1,0:T(8,128)(2,1)S(1)}, bf16[96,128]{1,0:T(8,128)(2,1)S(1)}, u32[]{:S(2)}, u32[]{:S(2)}) collective-permute-start(bf16[96,128]{1,0:T(8,128)(2,1)S(1)} %get-tuple-element.82), channel_id=1, source_target_pairs={{0,3},{1,2},{2,1},{3,0},{4,7},{5,6},{6,5},{7,4},{8,11},{9,10},{10,... | collective-permute-start | bytes 73736 | tf_op jit(solution)/shard_map/ppermute | solution.py:484
  37.4 0.9 %collective-permute-done.14.refs_2_ = bf16[192,384]{1,0:T(8,128)(2,1)S(1)} collective-permute-done((bf16[192,384]{1,0:T(8,128)(2,1)S(1)}, bf16[192,384]{1,0:T(8,128)(2,1)S(1)}, u32[]{:S(2)}, u32[]{:S(2)}) %collective-permute-start.14) | collective-permute-done | bytes 147488 | tf_op jit(solution)/shard_map/ppermute | solution.py:478
  38.3 0.0 collective-permute-start.20
  38.3 0.0 collective-permute-done.15.refs_3_
  38.3 0.9 %collective-permute-done.17.refs_5_ = bf16[96,128]{1,0:T(8,128)(2,1)S(1)} collective-permute-done((bf16[96,128]{1,0:T(8,128)(2,1)S(1)}, bf16[96,128]{1,0:T(8,128)(2,1)S(1)}, u32[]{:S(2)}, u32[]{:S(2)}) %collective-permute-start.17) | collective-permute-done | bytes 24608 | tf_op jit(solution)/shard_map/ppermute | solution.py:484
  39.3 0.0 collective-permute-done.18.refs_6_
  39.3 0.6 %collective-permute-done.19.refs_7_ = bf16[96,128]{1,0:T(8,128)(2,1)S(1)} collective-permute-done((bf16[96,128]{1,0:T(8,128)(2,1)S(1)}, bf16[96,128]{1,0:T(8,128)(2,1)S(1)}, u32[]{:S(2)}, u32[]{:S(2)}) %collective-permute-start.19) | collective-permute-done | bytes 24608 | tf_op jit(solution)/shard_map/ppermute | solution.py:484
  39.9 0.2 plane_sum.1
  40.0 1.8 %collective-permute-start.21 = (bf16[56,384]{1,0:T(8,128)(2,1)S(1)}, bf16[56,384]{1,0:T(8,128)(2,1)S(1)}, u32[]{:S(2)}, u32[]{:S(2)}) collective-permute-start(bf16[56,384]{1,0:T(8,128)(2,1)S(1)} %get-tuple-element.88), channel_id=1, source_target_pairs={{0,17},{1,16},{2,19},{3,18},{4,21},{5,20},{6,23},{7,22},{8,25},{9,... | collective-permute-start | bytes 129032 | tf_op jit(solution)/shard_map/ppermute | solution.py:484
  41.9 1.0 %collective-permute-start.22 = (bf16[56,384]{1,0:T(8,128)(2,1)S(1)}, bf16[56,384]{1,0:T(8,128)(2,1)S(1)}, u32[]{:S(2)}, u32[]{:S(2)}) collective-permute-start(bf16[56,384]{1,0:T(8,128)(2,1)S(1)} %get-tuple-element.89), channel_id=1, source_target_pairs={{0,25},{1,24},{2,27},{3,26},{4,29},{5,28},{6,31},{7,30},{8,17},{9,... | collective-permute-start | bytes 129032 | tf_op jit(solution)/shard_map/ppermute | solution.py:484
  42.9 0.6 %collective-permute-start.23 = (bf16[56,384]{1,0:T(8,128)(2,1)S(1)}, bf16[56,384]{1,0:T(8,128)(2,1)S(1)}, u32[]{:S(2)}, u32[]{:S(2)}) collective-permute-start(bf16[56,384]{1,0:T(8,128)(2,1)S(1)} %get-tuple-element.90), channel_id=1, source_target_pairs={{0,9},{1,8},{2,11},{3,10},{4,13},{5,12},{6,15},{7,14},{8,1},{9,0},... | collective-permute-start | bytes 129032 | tf_op jit(solution)/shard_map/ppermute | solution.py:484
  43.4 2.7 %collective-permute-done.20.other_ref = bf16[6,8,16,128]{3,2,1,0:T(8,128)(2,1)S(1)} collective-permute-done((bf16[6,8,16,128]{3,2,1,0:T(8,128)(2,1)S(1)}, bf16[6,8,16,128]{3,2,1,0:T(8,128)(2,1)S(1)}, u32[]{:S(2)}, u32[]{:S(2)}) %collective-permute-start.20) | collective-permute-done | bytes 196640 | tf_op jit(solution)/shard_map/ppermute | solution.py:484
  46.1 2.0 %conv_back.1 = bf16[1,8,16,768]{3,2,1,0:T(8,128)(2,1)} custom-call(f32[6,8,16,128]{3,2,1,0:T(8,128)S(1)} %get-tuple-element.84.grad_ref, bf16[6,8,16,128]{3,2,1,0:T(8,128)(2,1)S(1)} %collective-permute-done.20.other_ref, f32[6,128,128]{2,1,0:T(8,128)S(1)} %get-tuple-element.63.taps_ref.refs_6_), custom_call_target="tpu_custom_call" | custom-call | flops 110000000 | bytes 1179648 | tf_op jit(solution)/shard_map/conv_back/pallas_call | solution.py:451
  48.1 0.0 collective-permute-done.21.refs_1_
  48.1 0.0 collective-permute-done.22.refs_2_
  48.1 0.0 collective-permute-done.23.refs_3_
  48.1 0.1 line_sum.1.mine_ref
  48.2 0.7 %collective-permute-start.24 = (f32[48,1280]{1,0:T(8,128)S(1)}, f32[48,1280]{1,0:T(8,128)S(1)}, u32[]{:S(2)}, u32[]{:S(2)}) collective-permute-start(f32[48,1280]{1,0:T(8,128)S(1)} %line_sum.1.mine_ref), channel_id=1, source_target_pairs={{0,1},{1,0},{2,3},{3,2},{4,5},{5,4},{6,7},{7,6},{8,9},{9,8},{10,11... | collective-permute-start | bytes 737288 | tf_op jit(solution)/shard_map/ppermute | solution.py:496
  48.9 1.1 %collective-permute-done.24.other_ref = f32[48,1280]{1,0:T(8,128)S(1)} collective-permute-done((f32[48,1280]{1,0:T(8,128)S(1)}, f32[48,1280]{1,0:T(8,128)S(1)}, u32[]{:S(2)}, u32[]{:S(2)}) %collective-permute-start.24) | collective-permute-done | bytes 245792 | tf_op jit(solution)/shard_map/ppermute | solution.py:496
  50.1 0.8 %finish.1 = (f32[48,1536]{1,0:T(8,128)}, f32[48,49]{1,0:T(8,128)}, f32[1,48]{1,0:T(1,128)}, f32[1,48]{1,0:T(1,128)}) custom-call(f32[48,1280]{1,0:T(8,128)S(1)} %line_sum.1.mine_ref, f32[48,1280]{1,0:T(8,128)S(1)} %collective-permute-done.24.other_ref), custom_call_target="tpu_custom_call" | custom-call | flops 550000000 | bytes 796224 | tf_op jit(solution)/shard_map/finish/pallas_call | solution.py:451
  (6 shorter events, 0.1 us)
Async XLA Ops:
  0.6 7.1 %copy-start = (bf16[1,8,16,768]{3,2,1,0:T(8,128)(2,1)S(1)}, bf16[1,8,16,768]{3,2,1,0:T(8,128)(2,1)}, u32[]{:S(2)}) copy-start(bf16[1,8,16,768]{3,2,1,0:T(8,128)(2,1)} %param.6) | copy-start | bytes 589828
  0.6 7.1 %copy-start.1 = (bf16[1,8,16,1536]{3,2,1,0:T(8,128)(2,1)S(1)}, bf16[1,8,16,1536]{3,2,1,0:T(8,128)(2,1)}, u32[]{:S(2)}) copy-start(bf16[1,8,16,1536]{3,2,1,0:T(8,128)(2,1)} %param.7) | copy-start | bytes 1179652
  2.4 9.6 %copy-start.2 = (bf16[56,384]{1,0:T(8,128)(2,1)S(1)}, bf16[56,384]{1,0:T(8,128)(2,1)}, u32[]{:S(2)}) copy-start(bf16[56,384]{1,0:T(8,128)(2,1)} %get-tuple-element.53.refs_0_) | copy-start | bytes 129028
  2.4 7.1 %collective-permute-start.1 = (bf16[56,384]{1,0:T(8,128)(2,1)}, bf16[56,384]{1,0:T(8,128)(2,1)S(1)}, u32[]{:S(2)}, u32[]{:S(2)}) collective-permute-start(bf16[56,384]{1,0:T(8,128)(2,1)} %get-tuple-element.55), channel_id=1, source_target_pairs={{0,17},{1,16},{2,19},{3,18},{4,21},{5,20},{6,23},{7,22},{8,25},{9,... | collective-permute-start | bytes 129032 | tf_op jit(solution)/shard_map/ppermute | solution.py:484
  5.9 5.6 %collective-permute-start.2 = (bf16[56,384]{1,0:T(8,128)(2,1)}, bf16[56,384]{1,0:T(8,128)(2,1)S(1)}, u32[]{:S(2)}, u32[]{:S(2)}) collective-permute-start(bf16[56,384]{1,0:T(8,128)(2,1)} %get-tuple-element.54), channel_id=1, source_target_pairs={{0,25},{1,24},{2,27},{3,26},{4,29},{5,28},{6,31},{7,30},{8,17},{9,... | collective-permute-start | bytes 129032 | tf_op jit(solution)/shard_map/ppermute | solution.py:484
  7.5 4.5 %collective-permute-start = (bf16[56,384]{1,0:T(8,128)(2,1)}, bf16[56,384]{1,0:T(8,128)(2,1)S(1)}, u32[]{:S(2)}, u32[]{:S(2)}) collective-permute-start(bf16[56,384]{1,0:T(8,128)(2,1)} %get-tuple-element.54), channel_id=1, source_target_pairs={{0,9},{1,8},{2,11},{3,10},{4,13},{5,12},{6,15},{7,14},{8,1},{9,0},... | collective-permute-start | bytes 129032 | tf_op jit(solution)/shard_map/ppermute | solution.py:484
  7.8 4.4 %collective-permute-start.3 = (bf16[128,768]{1,0:T(8,128)(2,1)S(1)}, bf16[128,768]{1,0:T(8,128)(2,1)S(1)}, u32[]{:S(2)}, u32[]{:S(2)}) collective-permute-start(bf16[128,768]{1,0:T(8,128)(2,1)S(1)} %get-tuple-element.59), channel_id=1, source_target_pairs={{0,1},{1,0},{2,3},{3,2},{4,5},{5,4},{6,7},{7,6},{8,9},{9,8},{10,11... | collective-permute-start | bytes 589832 | tf_op jit(solution)/shard_map/ppermute | solution.py:496
  7.9 14.8 %collective-permute-start.9 = (bf16[256,768]{1,0:T(8,128)(2,1)S(1)}, bf16[256,768]{1,0:T(8,128)(2,1)S(1)}, u32[]{:S(2)}, u32[]{:S(2)}) collective-permute-start(bf16[256,768]{1,0:T(8,128)(2,1)S(1)} %get-tuple-element.64), channel_id=1, source_target_pairs={{0,9},{1,8},{2,11},{3,10},{4,13},{5,12},{6,15},{7,14},{8,1},{9,0},... | collective-permute-start | bytes 1179656 | tf_op jit(solution)/shard_map/ppermute | solution.py:484
  12.2 5.2 %collective-permute-start.4 = (bf16[192,384]{1,0:T(8,128)(2,1)S(1)}, bf16[192,384]{1,0:T(8,128)(2,1)S(1)}, u32[]{:S(2)}, u32[]{:S(2)}) collective-permute-start(bf16[192,384]{1,0:T(8,128)(2,1)S(1)} %get-tuple-element.60.own_ref.refs_0_), channel_id=1, source_target_pairs={{0,2},{1,5},{2,0},{3,7},{4,6},{5,1},{6,4},{7,3},{8,10},{9,13},{10,... | collective-permute-start | bytes 442376 | tf_op jit(solution)/shard_map/ppermute | solution.py:493
  13.8 5.5 %collective-permute-start.8 = (bf16[96,128]{1,0:T(8,128)(2,1)S(1)}, bf16[96,128]{1,0:T(8,128)(2,1)S(1)}, u32[]{:S(2)}, u32[]{:S(2)}) collective-permute-start(bf16[96,128]{1,0:T(8,128)(2,1)S(1)} %get-tuple-element.61.refs_0_), channel_id=1, source_target_pairs={{0,7},{1,6},{2,5},{3,4},{4,3},{5,2},{6,1},{7,0},{8,15},{9,14},{10,... | collective-permute-start | bytes 73736 | tf_op jit(solution)/shard_map/ppermute | solution.py:484
  15.5 3.8 %collective-permute-start.7 = (bf16[96,128]{1,0:T(8,128)(2,1)S(1)}, bf16[96,128]{1,0:T(8,128)(2,1)S(1)}, u32[]{:S(2)}, u32[]{:S(2)}) collective-permute-start(bf16[96,128]{1,0:T(8,128)(2,1)S(1)} %get-tuple-element.61.refs_0_), channel_id=1, source_target_pairs={{0,5},{1,4},{2,7},{3,6},{4,1},{5,0},{6,3},{7,2},{8,13},{9,12},{10,... | collective-permute-start | bytes 73736 | tf_op jit(solution)/shard_map/ppermute | solution.py:484
  15.5 3.8 %collective-permute-start.6 = (bf16[96,128]{1,0:T(8,128)(2,1)S(1)}, bf16[96,128]{1,0:T(8,128)(2,1)S(1)}, u32[]{:S(2)}, u32[]{:S(2)}) collective-permute-start(bf16[96,128]{1,0:T(8,128)(2,1)S(1)} %get-tuple-element.61.refs_0_), channel_id=1, source_target_pairs={{0,3},{1,2},{2,1},{3,0},{4,7},{5,6},{6,5},{7,4},{8,11},{9,10},{10,... | collective-permute-start | bytes 73736 | tf_op jit(solution)/shard_map/ppermute | solution.py:484
  17.4 7.4 %collective-permute-start.5 = (bf16[384,384]{1,0:T(8,128)(2,1)S(1)}, bf16[384,384]{1,0:T(8,128)(2,1)S(1)}, u32[]{:S(2)}, u32[]{:S(2)}) collective-permute-start(bf16[384,384]{1,0:T(8,128)(2,1)S(1)} %join.1), channel_id=1, source_target_pairs={{0,4},{1,3},{2,6},{3,1},{4,0},{5,7},{6,2},{7,5},{8,12},{9,11},{10,... | collective-permute-start | bytes 884744 | tf_op jit(solution)/shard_map/ppermute | solution.py:493
  21.1 3.8 %collective-permute-start.10 = (bf16[128,768]{1,0:T(8,128)(2,1)S(1)}, bf16[128,768]{1,0:T(8,128)(2,1)S(1)}, u32[]{:S(2)}, u32[]{:S(2)}) collective-permute-start(bf16[128,768]{1,0:T(8,128)(2,1)S(1)} %get-tuple-element.62.refs_1_), channel_id=1, source_target_pairs={{0,1},{1,0},{2,3},{3,2},{4,5},{5,4},{6,7},{7,6},{8,9},{9,8},{10,11... | collective-permute-start | bytes 589832 | tf_op jit(solution)/shard_map/ppermute | solution.py:496
  24.2 1.7 %collective-permute-start.11 = (bf16[128,768]{1,0:T(8,128)(2,1)S(1)}, bf16[128,768]{1,0:T(8,128)(2,1)S(1)}, u32[]{:S(2)}, u32[]{:S(2)}) collective-permute-start(bf16[128,768]{1,0:T(8,128)(2,1)S(1)} %get-tuple-element.65.refs_2_), channel_id=1, source_target_pairs={{0,1},{1,0},{2,3},{3,2},{4,5},{5,4},{6,7},{7,6},{8,9},{9,8},{10,11... | collective-permute-start | bytes 589832 | tf_op jit(solution)/shard_map/ppermute | solution.py:496
  24.3 1.6 %collective-permute-start.12 = (bf16[128,384]{1,0:T(8,128)(2,1)S(1)}, bf16[128,384]{1,0:T(8,128)(2,1)S(1)}, u32[]{:S(2)}, u32[]{:S(2)}) collective-permute-start(bf16[128,384]{1,0:T(8,128)(2,1)S(1)} %get-tuple-element.67), channel_id=1, source_target_pairs={{0,1},{1,0},{2,3},{3,2},{4,5},{5,4},{6,7},{7,6},{8,9},{9,8},{10,11... | collective-permute-start | bytes 294920 | tf_op jit(solution)/shard_map/ppermute | solution.py:496
  28.0 3.8 %collective-permute-start.16 = (f32[256,768]{1,0:T(8,128)S(1)}, f32[256,768]{1,0:T(8,128)S(1)}, u32[]{:S(2)}, u32[]{:S(2)}) collective-permute-start(f32[256,768]{1,0:T(8,128)S(1)} %get-tuple-element.74), channel_id=1, source_target_pairs={{0,1},{1,0},{2,3},{3,2},{4,5},{5,4},{6,7},{7,6},{8,9},{9,8},{10,11... | collective-permute-start | bytes 2359304 | tf_op jit(solution)/shard_map/ppermute | solution.py:496
  28.3 8.3 %collective-permute-start.13 = (bf16[192,384]{1,0:T(8,128)(2,1)S(1)}, bf16[192,384]{1,0:T(8,128)(2,1)S(1)}, u32[]{:S(2)}, u32[]{:S(2)}) collective-permute-start(bf16[192,384]{1,0:T(8,128)(2,1)S(1)} %get-tuple-element.69), channel_id=1, source_target_pairs={{0,6},{2,4},{4,2},{6,0},{8,14},{10,12},{12,10},{14,8},{16,22},{18,... | collective-permute-start | bytes 442376 | tf_op jit(solution)/shard_map/ppermute | solution.py:478
  29.2 9.1 %collective-permute-start.14 = (bf16[192,384]{1,0:T(8,128)(2,1)S(1)}, bf16[192,384]{1,0:T(8,128)(2,1)S(1)}, u32[]{:S(2)}, u32[]{:S(2)}) collective-permute-start(bf16[192,384]{1,0:T(8,128)(2,1)S(1)} %get-tuple-element.70), channel_id=1, source_target_pairs={{0,4},{2,6},{4,0},{6,2},{8,12},{10,14},{12,8},{14,10},{16,20},{18,... | collective-permute-start | bytes 442376 | tf_op jit(solution)/shard_map/ppermute | solution.py:478
  30.1 8.2 %collective-permute-start.15 = (bf16[192,384]{1,0:T(8,128)(2,1)S(1)}, bf16[192,384]{1,0:T(8,128)(2,1)S(1)}, u32[]{:S(2)}, u32[]{:S(2)}) collective-permute-start(bf16[192,384]{1,0:T(8,128)(2,1)S(1)} %get-tuple-element.71), channel_id=1, source_target_pairs={{0,2},{2,0},{4,6},{6,4},{8,10},{10,8},{12,14},{14,12},{16,18},{18,... | collective-permute-start | bytes 442376 | tf_op jit(solution)/shard_map/ppermute | solution.py:478
  35.1 4.2 %collective-permute-start.17 = (bf16[96,128]{1,0:T(8,128)(2,1)S(1)}, bf16[96,128]{1,0:T(8,128)(2,1)S(1)}, u32[]{:S(2)}, u32[]{:S(2)}) collective-permute-start(bf16[96,128]{1,0:T(8,128)(2,1)S(1)} %get-tuple-element.80), channel_id=1, source_target_pairs={{0,7},{1,6},{2,5},{3,4},{4,3},{5,2},{6,1},{7,0},{8,15},{9,14},{10,... | collective-permute-start | bytes 73736 | tf_op jit(solution)/shard_map/ppermute | solution.py:484
  35.2 4.0 %collective-permute-start.18 = (bf16[96,128]{1,0:T(8,128)(2,1)S(1)}, bf16[96,128]{1,0:T(8,128)(2,1)S(1)}, u32[]{:S(2)}, u32[]{:S(2)}) collective-permute-start(bf16[96,128]{1,0:T(8,128)(2,1)S(1)} %get-tuple-element.81), channel_id=1, source_target_pairs={{0,5},{1,4},{2,7},{3,6},{4,1},{5,0},{6,3},{7,2},{8,13},{9,12},{10,... | collective-permute-start | bytes 73736 | tf_op jit(solution)/shard_map/ppermute | solution.py:484
  36.6 3.3 %collective-permute-start.19 = (bf16[96,128]{1,0:T(8,128)(2,1)S(1)}, bf16[96,128]{1,0:T(8,128)(2,1)S(1)}, u32[]{:S(2)}, u32[]{:S(2)}) collective-permute-start(bf16[96,128]{1,0:T(8,128)(2,1)S(1)} %get-tuple-element.82), channel_id=1, source_target_pairs={{0,3},{1,2},{2,1},{3,0},{4,7},{5,6},{6,5},{7,4},{8,11},{9,10},{10,... | collective-permute-start | bytes 73736 | tf_op jit(solution)/shard_map/ppermute | solution.py:484
  38.3 7.8 %collective-permute-start.20 = (bf16[6,8,16,128]{3,2,1,0:T(8,128)(2,1)S(1)}, bf16[6,8,16,128]{3,2,1,0:T(8,128)(2,1)S(1)}, u32[]{:S(2)}, u32[]{:S(2)}) collective-permute-start(bf16[6,8,16,128]{3,2,1,0:T(8,128)(2,1)S(1)} %get-tuple-element.85), channel_id=1, source_target_pairs={{0,9},{1,8},{2,11},{3,10},{4,13},{5,12},{6,15},{7,14},{8,1},{9,0},... | collective-permute-start | bytes 589832 | tf_op jit(solution)/shard_map/ppermute | solution.py:484
  40.0 8.1 %collective-permute-start.21 = (bf16[56,384]{1,0:T(8,128)(2,1)S(1)}, bf16[56,384]{1,0:T(8,128)(2,1)S(1)}, u32[]{:S(2)}, u32[]{:S(2)}) collective-permute-start(bf16[56,384]{1,0:T(8,128)(2,1)S(1)} %get-tuple-element.88), channel_id=1, source_target_pairs={{0,17},{1,16},{2,19},{3,18},{4,21},{5,20},{6,23},{7,22},{8,25},{9,... | collective-permute-start | bytes 129032 | tf_op jit(solution)/shard_map/ppermute | solution.py:484
  41.9 6.3 %collective-permute-start.22 = (bf16[56,384]{1,0:T(8,128)(2,1)S(1)}, bf16[56,384]{1,0:T(8,128)(2,1)S(1)}, u32[]{:S(2)}, u32[]{:S(2)}) collective-permute-start(bf16[56,384]{1,0:T(8,128)(2,1)S(1)} %get-tuple-element.89), channel_id=1, source_target_pairs={{0,25},{1,24},{2,27},{3,26},{4,29},{5,28},{6,31},{7,30},{8,17},{9,... | collective-permute-start | bytes 129032 | tf_op jit(solution)/shard_map/ppermute | solution.py:484
  42.9 5.3 %collective-permute-start.23 = (bf16[56,384]{1,0:T(8,128)(2,1)S(1)}, bf16[56,384]{1,0:T(8,128)(2,1)S(1)}, u32[]{:S(2)}, u32[]{:S(2)}) collective-permute-start(bf16[56,384]{1,0:T(8,128)(2,1)S(1)} %get-tuple-element.90), channel_id=1, source_target_pairs={{0,9},{1,8},{2,11},{3,10},{4,13},{5,12},{6,15},{7,14},{8,1},{9,0},... | collective-permute-start | bytes 129032 | tf_op jit(solution)/shard_map/ppermute | solution.py:484
  48.2 1.9 %collective-permute-start.24 = (f32[48,1280]{1,0:T(8,128)S(1)}, f32[48,1280]{1,0:T(8,128)S(1)}, u32[]{:S(2)}, u32[]{:S(2)}) collective-permute-start(f32[48,1280]{1,0:T(8,128)S(1)} %line_sum.1.mine_ref), channel_id=1, source_target_pairs={{0,1},{1,0},{2,3},{3,2},{4,5},{5,4},{6,7},{7,6},{8,9},{9,8},{10,11... | collective-permute-start | bytes 737288 | tf_op jit(solution)/shard_map/ppermute | solution.py:496

commit v21 on v20

--- a/solution.py
+++ b/solution.py
@@ -643,7 +643,7 @@
         grad_pre,
     )
     pieces = relative_order(pieces)
-    arrived = [over_shard(pieces[flip], flip) for flip in range(INNER - 1, 0, -1)]
+    arrived = [over_shard(pieces[flip], flip) for flip in range(1, INNER)]
     *small, grad_conv, grad_sent = call(
         functools.partial(norm_back_kernel, relative, own, height, breadth),
         "norm_back",

time: 51 us -> 50.6 us (level)
  starting transfers between devices: 26.4 us -> 25.8 us
    ppermute x3, waiting for transfers between devices: 0.95 us -> 0.18 us  [over_shard(): return lax.ppermute(array, 'shard', [(i, i ^ flip) for i in range(shards)])]
    ppermute x14, waiting for transfers between devices: 6.75 us -> 7.49 us  [crossing(): return lax.ppermute(array, ('shard', 'rep'), pairs)]
    ppermute x6, starting transfers between devices: 3.3 us -> 2.66 us  [over_core(): return lax.ppermute(array, 'rep', [(i, i ^ 1) for i in range(reps)])]
  transfers between devices with their start and end apart: 25 -> 25, of which waited for: 9 -> 10; matrix products, arithmetic and copies ran while one was open for 0% -> 0% of each run, Pallas kernels for 18% -> 18%
where the time goes in v21:
time: 50.6 us; the launch traced here: 50.5 us
  starting transfers between devices  25.8 us (51%)
  Pallas kernels  13.7 us (27%)
  waiting for transfers between devices  10.3 us (20%)
  between operations  0.75 us (1%)
    ppermute x14, starting transfers between devices, crossing(): return lax.ppermute(array, ('shard', 'rep'), pairs)  16.2 us
    pallas_call x14, Pallas kernels, call(): pl.pallas_call(kernel, out_shape=outs, in_specs=[VMEM] * len(args), out_s...  13.7 us
    ppermute x14, waiting for transfers between devices, crossing(): return lax.ppermute(array, ('shard', 'rep'), pairs)  7.49 us
    ppermute x3, starting transfers between devices, over_shard(): return lax.ppermute(array, 'shard', [(i, i ^ flip) for i in range(shards)])  3.49 us
    ppermute x2, starting transfers between devices, hop(): return lax.ppermute(array, ('shard', 'rep'), pairs)  3.4 us
    ppermute x6, starting transfers between devices, over_core(): return lax.ppermute(array, 'rep', [(i, i ^ 1) for i in range(reps)])  2.66 us
    ppermute x6, waiting for transfers between devices, over_core(): return lax.ppermute(array, 'rep', [(i, i ^ 1) for i in range(reps)])  2.41 us
  transfers between devices with their start and end apart: 25, of which 10 were waited for; matrix products, arithmetic and copies ran while one was open for 0% of the time, Pallas kernels for 18%

profile of v21, /device:TPU:0, one launch (start us, length us, event | category | flops | bytes accessed | tf_op | source)
XLA Modules:
  0.0 50.5 jit_solution(15180542412370563241)
XLA Ops:
  0.6 0.0 copy-start
  0.6 0.0 copy-start.1
  0.7 1.8 %pack.1 = (bf16[56,384]{1,0:T(8,128)(2,1)}, bf16[56,384]{1,0:T(8,128)(2,1)}, bf16[56,384]{1,0:T(8,128)(2,1)}) custom-call(bf16[48,1536]{1,0:T(8,128)(2,1)} %w_ref.1, bf16[48,49]{1,0:T(8,128)(2,1)} %dw_ref.1, bf16[1,48]{1,0:T(2,128)(2,1)} %bitcast.11, bf16[1,48]{1,0:T(2,128)(2,1)} %bitcast.12), custom_call_target="tpu_custom_call" | custom-call | flops 550000000 | bytes 281376 | tf_op jit(solution)/shard_map/pack/pallas_call | solution.py:451
  2.4 3.5 %collective-permute-start.1 = (bf16[56,384]{1,0:T(8,128)(2,1)}, bf16[56,384]{1,0:T(8,128)(2,1)S(1)}, u32[]{:S(2)}, u32[]{:S(2)}) collective-permute-start(bf16[56,384]{1,0:T(8,128)(2,1)} %get-tuple-element.55), channel_id=1, source_target_pairs={{0,17},{1,16},{2,19},{3,18},{4,21},{5,20},{6,23},{7,22},{8,25},{9,... | collective-permute-start | bytes 129032 | tf_op jit(solution)/shard_map/ppermute | solution.py:484
  5.9 1.6 %collective-permute-start.2 = (bf16[56,384]{1,0:T(8,128)(2,1)}, bf16[56,384]{1,0:T(8,128)(2,1)S(1)}, u32[]{:S(2)}, u32[]{:S(2)}) collective-permute-start(bf16[56,384]{1,0:T(8,128)(2,1)} %get-tuple-element.54), channel_id=1, source_target_pairs={{0,25},{1,24},{2,27},{3,26},{4,29},{5,28},{6,31},{7,30},{8,17},{9,... | collective-permute-start | bytes 129032 | tf_op jit(solution)/shard_map/ppermute | solution.py:484
  7.5 0.2 collective-permute-start
  7.8 0.1 collective-permute-start.3
  7.9 1.7 %collective-permute-start.9 = (bf16[256,768]{1,0:T(8,128)(2,1)S(1)}, bf16[256,768]{1,0:T(8,128)(2,1)S(1)}, u32[]{:S(2)}, u32[]{:S(2)}) collective-permute-start(bf16[256,768]{1,0:T(8,128)(2,1)S(1)} %get-tuple-element.64), channel_id=1, source_target_pairs={{0,9},{1,8},{2,11},{3,10},{4,13},{5,12},{6,15},{7,14},{8,1},{9,0},... | collective-permute-start | bytes 1179656 | tf_op jit(solution)/shard_map/ppermute | solution.py:484
  9.6 0.0 collective-permute-done.1.refs_2_
  9.6 1.9 %collective-permute-done.2.refs_3_ = bf16[56,384]{1,0:T(8,128)(2,1)S(1)} collective-permute-done((bf16[56,384]{1,0:T(8,128)(2,1)}, bf16[56,384]{1,0:T(8,128)(2,1)S(1)}, u32[]{:S(2)}, u32[]{:S(2)}) %collective-permute-start.2) | collective-permute-done | bytes 43040 | tf_op jit(solution)/shard_map/ppermute | solution.py:484
  11.5 0.6 %collective-permute-done.refs_1_ = bf16[56,384]{1,0:T(8,128)(2,1)S(1)} collective-permute-done((bf16[56,384]{1,0:T(8,128)(2,1)}, bf16[56,384]{1,0:T(8,128)(2,1)S(1)}, u32[]{:S(2)}, u32[]{:S(2)}) %collective-permute-start) | collective-permute-done | bytes 43040 | tf_op jit(solution)/shard_map/ppermute | solution.py:484
  12.0 0.1 assemble.1
  12.2 0.0 collective-permute-done.3.refs_6_
  12.2 1.6 %collective-permute-start.4 = (bf16[192,384]{1,0:T(8,128)(2,1)S(1)}, bf16[192,384]{1,0:T(8,128)(2,1)S(1)}, u32[]{:S(2)}, u32[]{:S(2)}) collective-permute-start(bf16[192,384]{1,0:T(8,128)(2,1)S(1)} %get-tuple-element.60.own_ref.refs_0_), channel_id=1, source_target_pairs={{0,2},{1,5},{2,0},{3,7},{4,6},{5,1},{6,4},{7,3},{8,10},{9,13},{10,... | collective-permute-start | bytes 442376 | tf_op jit(solution)/shard_map/ppermute | solution.py:493
  13.8 1.7 %collective-permute-start.8 = (bf16[96,128]{1,0:T(8,128)(2,1)S(1)}, bf16[96,128]{1,0:T(8,128)(2,1)S(1)}, u32[]{:S(2)}, u32[]{:S(2)}) collective-permute-start(bf16[96,128]{1,0:T(8,128)(2,1)S(1)} %get-tuple-element.61.refs_0_), channel_id=1, source_target_pairs={{0,7},{1,6},{2,5},{3,4},{4,3},{5,2},{6,1},{7,0},{8,15},{9,14},{10,... | collective-permute-start | bytes 73736 | tf_op jit(solution)/shard_map/ppermute | solution.py:484
  15.5 0.0 collective-permute-start.7
  15.5 1.8 %collective-permute-start.6 = (bf16[96,128]{1,0:T(8,128)(2,1)S(1)}, bf16[96,128]{1,0:T(8,128)(2,1)S(1)}, u32[]{:S(2)}, u32[]{:S(2)}) collective-permute-start(bf16[96,128]{1,0:T(8,128)(2,1)S(1)} %get-tuple-element.61.refs_0_), channel_id=1, source_target_pairs={{0,3},{1,2},{2,1},{3,0},{4,7},{5,6},{6,5},{7,4},{8,11},{9,10},{10,... | collective-permute-start | bytes 73736 | tf_op jit(solution)/shard_map/ppermute | solution.py:484
  17.2 0.2 collective-permute-done.4.came_ref.refs_1_
  17.4 1.8 %collective-permute-start.5 = (bf16[384,384]{1,0:T(8,128)(2,1)S(1)}, bf16[384,384]{1,0:T(8,128)(2,1)S(1)}, u32[]{:S(2)}, u32[]{:S(2)}) collective-permute-start(bf16[384,384]{1,0:T(8,128)(2,1)S(1)} %join.1), channel_id=1, source_target_pairs={{0,4},{1,3},{2,6},{3,1},{4,0},{5,7},{6,2},{7,5},{8,12},{9,11},{10,... | collective-permute-start | bytes 884744 | tf_op jit(solution)/shard_map/ppermute | solution.py:493
  19.3 0.0 collective-permute-done.8.refs_3_
  19.3 0.0 collective-permute-done.7.refs_2_
  19.3 0.0 collective-permute-done.6.refs_1_
  19.3 1.8 %conv_norm.1 = (bf16[128,768]{1,0:T(8,128)(2,1)S(1)}, f32[128,768]{1,0:T(8,128)S(1)}, f32[128,128]{1,0:T(8,128)S(1)}, f32[6,128,128]{2,1,0:T(8,128)S(1)}) custom-call(bf16[96,128]{1,0:T(8,128)(2,1)S(1)} %get-tuple-element.61.refs_0_, bf16[96,128]{1,0:T(8,128)(2,1)S(1)} %collective-permute-done.6.refs_1_, bf16[96,128]{1,0:T(8,128)(2,1)S(1)} %collective-permute-done.7.refs_2_, ...), custom_call_target="tpu_custom_call" | custom-call | flops 110000000 | bytes 1343488 | tf_op jit(solution)/shard_map/conv_norm/pallas_call | solution.py:451
  21.1 1.6 %collective-permute-start.10 = (bf16[128,768]{1,0:T(8,128)(2,1)S(1)}, bf16[128,768]{1,0:T(8,128)(2,1)S(1)}, u32[]{:S(2)}, u32[]{:S(2)}) collective-permute-start(bf16[128,768]{1,0:T(8,128)(2,1)S(1)} %get-tuple-element.62.refs_1_), channel_id=1, source_target_pairs={{0,1},{1,0},{2,3},{3,2},{4,5},{5,4},{6,7},{7,6},{8,9},{9,8},{10,11... | collective-permute-start | bytes 589832 | tf_op jit(solution)/shard_map/ppermute | solution.py:496
  22.7 0.0 collective-permute-done.9.far_ref.refs_7_.refs_8_
  22.7 1.5 %far_norm.1 = (bf16[128,768]{1,0:T(8,128)(2,1)S(1)}, f32[128,768]{1,0:T(8,128)S(1)}, f32[128,128]{1,0:T(8,128)S(1)}, bf16[128,384]{1,0:T(8,128)(2,1)S(1)}) custom-call(f32[6,128,128]{2,1,0:T(8,128)S(1)} %get-tuple-element.63.taps_ref.refs_6_, bf16[256,768]{1,0:T(8,128)(2,1)S(1)} %collective-permute-done.9.far_ref.refs_7_.refs_8_), custom_call_target="tpu_custom_call" | custom-call | flops 1100000000 | bytes 1540096 | tf_op jit(solution)/shard_map/far_norm/pallas_call | solution.py:451
  24.2 0.1 collective-permute-start.11
  24.3 0.5 collective-permute-start.12
  24.8 0.0 collective-permute-done.5.refs_2_
  24.8 0.1 order.1.refs_0_.weight
  24.9 0.0 collective-permute-done.10.refs_3_
  24.9 1.0 %collective-permute-done.12.refs_8_ = bf16[128,384]{1,0:T(8,128)(2,1)S(1)} collective-permute-done((bf16[128,384]{1,0:T(8,128)(2,1)S(1)}, bf16[128,384]{1,0:T(8,128)(2,1)S(1)}, u32[]{:S(2)}, u32[]{:S(2)}) %collective-permute-start.12) | collective-permute-done | bytes 98336 | tf_op jit(solution)/shard_map/ppermute | solution.py:496
  25.9 0.0 collective-permute-done.11.refs_4_
  25.9 1.5 %project.1 = (f32[192,384]{1,0:T(8,128)S(1)}, bf16[192,384]{1,0:T(8,128)(2,1)S(1)}, bf16[192,384]{1,0:T(8,128)(2,1)S(1)}, bf16[192,384]{1,0:T(8,128)(2,1)S(1)}, bf16[512,384]{1,0:T(8,128)(2,1)S(1)}) custom-call(bf16[768,384]{1,0:T(8,128)(2,1)S(1)} %order.1.refs_0_.weight, bf16[128,768]{1,0:T(8,128)(2,1)S(1)} %get-tuple-element.62.refs_1_, ...), custom_call_target="tpu_custom_call" | custom-call | flops 1760000000 | bytes 3588096 | tf_op jit(solution)/shard_map/project/pallas_call | solution.py:451
  27.4 0.6 %back_project.1 = (f32[256,768]{1,0:T(8,128)S(1)}, f32[256,768]{1,0:T(8,128)S(1)}) custom-call(bf16[768,384]{1,0:T(8,128)(2,1)S(1)} %order.1.refs_0_.weight, bf16[512,384]{1,0:T(8,128)(2,1)S(1)} %get-tuple-element.72.gp_ref), custom_call_target="tpu_custom_call" | custom-call | flops 770000000 | bytes 2555904 | tf_op jit(solution)/shard_map/back_project/pallas_call | solution.py:451
  28.0 0.3 collective-permute-start.16
  28.3 0.3 collective-permute-start.13
  28.6 1.2 %collective-permute-start.14 = (bf16[192,384]{1,0:T(8,128)(2,1)S(1)}, bf16[192,384]{1,0:T(8,128)(2,1)S(1)}, u32[]{:S(2)}, u32[]{:S(2)}) collective-permute-start(bf16[192,384]{1,0:T(8,128)(2,1)S(1)} %get-tuple-element.70), channel_id=1, source_target_pairs={{0,4},{2,6},{4,0},{6,2},{8,12},{10,14},{12,8},{14,10},{16,20},{18,... | collective-permute-start | bytes 442376 | tf_op jit(solution)/shard_map/ppermute | solution.py:478
  29.8 2.0 %collective-permute-start.15 = (bf16[192,384]{1,0:T(8,128)(2,1)S(1)}, bf16[192,384]{1,0:T(8,128)(2,1)S(1)}, u32[]{:S(2)}, u32[]{:S(2)}) collective-permute-start(bf16[192,384]{1,0:T(8,128)(2,1)S(1)} %get-tuple-element.71), channel_id=1, source_target_pairs={{0,6},{2,4},{4,2},{6,0},{8,14},{10,12},{12,10},{14,8},{16,22},{18,... | collective-permute-start | bytes 442376 | tf_op jit(solution)/shard_map/ppermute | solution.py:478
  31.8 0.0 collective-permute-done.16.refs_1_
  31.8 3.2 %norm_back.1 = (f32[96,128]{1,0:T(8,128)S(1)}, bf16[96,128]{1,0:T(8,128)(2,1)S(1)}, bf16[96,128]{1,0:T(8,128)(2,1)S(1)}, bf16[96,128]{1,0:T(8,128)(2,1)S(1)}, f3...) custom-call(f32[256,768]{1,0:T(8,128)S(1)} %get-tuple-element.73.refs_0_, ...), custom_call_target="tpu_custom_call" | custom-call | flops 110000000 | bytes 4186112 | tf_op jit(solution)/shard_map/norm_back/pallas_call | solution.py:451
  35.1 0.2 collective-permute-start.17
  35.2 1.4 %collective-permute-start.18 = (bf16[96,128]{1,0:T(8,128)(2,1)S(1)}, bf16[96,128]{1,0:T(8,128)(2,1)S(1)}, u32[]{:S(2)}, u32[]{:S(2)}) collective-permute-start(bf16[96,128]{1,0:T(8,128)(2,1)S(1)} %get-tuple-element.81), channel_id=1, source_target_pairs={{0,5},{1,4},{2,7},{3,6},{4,1},{5,0},{6,3},{7,2},{8,13},{9,12},{10,... | collective-permute-start | bytes 73736 | tf_op jit(solution)/shard_map/ppermute | solution.py:484
  36.6 0.0 collective-permute-done.13.refs_1_
  36.6 0.7 %collective-permute-start.19 = (bf16[96,128]{1,0:T(8,128)(2,1)S(1)}, bf16[96,128]{1,0:T(8,128)(2,1)S(1)}, u32[]{:S(2)}, u32[]{:S(2)}) collective-permute-start(bf16[96,128]{1,0:T(8,128)(2,1)S(1)} %get-tuple-element.82), channel_id=1, source_target_pairs={{0,3},{1,2},{2,1},{3,0},{4,7},{5,6},{6,5},{7,4},{8,11},{9,10},{10,... | collective-permute-start | bytes 73736 | tf_op jit(solution)/shard_map/ppermute | solution.py:484
  37.4 0.2 collective-permute-done.14.refs_2_
  37.6 0.0 collective-permute-start.20
  37.6 0.0 collective-permute-done.15.refs_3_
  37.6 1.7 %collective-permute-done.17.refs_5_ = bf16[96,128]{1,0:T(8,128)(2,1)S(1)} collective-permute-done((bf16[96,128]{1,0:T(8,128)(2,1)S(1)}, bf16[96,128]{1,0:T(8,128)(2,1)S(1)}, u32[]{:S(2)}, u32[]{:S(2)}) %collective-permute-start.17) | collective-permute-done | bytes 24608 | tf_op jit(solution)/shard_map/ppermute | solution.py:484
  39.3 0.0 collective-permute-done.18.refs_6_
  39.3 0.6 %collective-permute-done.19.refs_7_ = bf16[96,128]{1,0:T(8,128)(2,1)S(1)} collective-permute-done((bf16[96,128]{1,0:T(8,128)(2,1)S(1)}, bf16[96,128]{1,0:T(8,128)(2,1)S(1)}, u32[]{:S(2)}, u32[]{:S(2)}) %collective-permute-start.19) | collective-permute-done | bytes 24608 | tf_op jit(solution)/shard_map/ppermute | solution.py:484
  39.9 0.2 plane_sum.1
  40.0 1.8 %collective-permute-start.21 = (bf16[56,384]{1,0:T(8,128)(2,1)S(1)}, bf16[56,384]{1,0:T(8,128)(2,1)S(1)}, u32[]{:S(2)}, u32[]{:S(2)}) collective-permute-start(bf16[56,384]{1,0:T(8,128)(2,1)S(1)} %get-tuple-element.88), channel_id=1, source_target_pairs={{0,17},{1,16},{2,19},{3,18},{4,21},{5,20},{6,23},{7,22},{8,25},{9,... | collective-permute-start | bytes 129032 | tf_op jit(solution)/shard_map/ppermute | solution.py:484
  41.9 1.0 %collective-permute-start.22 = (bf16[56,384]{1,0:T(8,128)(2,1)S(1)}, bf16[56,384]{1,0:T(8,128)(2,1)S(1)}, u32[]{:S(2)}, u32[]{:S(2)}) collective-permute-start(bf16[56,384]{1,0:T(8,128)(2,1)S(1)} %get-tuple-element.89), channel_id=1, source_target_pairs={{0,25},{1,24},{2,27},{3,26},{4,29},{5,28},{6,31},{7,30},{8,17},{9,... | collective-permute-start | bytes 129032 | tf_op jit(solution)/shard_map/ppermute | solution.py:484
  42.9 0.6 %collective-permute-start.23 = (bf16[56,384]{1,0:T(8,128)(2,1)S(1)}, bf16[56,384]{1,0:T(8,128)(2,1)S(1)}, u32[]{:S(2)}, u32[]{:S(2)}) collective-permute-start(bf16[56,384]{1,0:T(8,128)(2,1)S(1)} %get-tuple-element.90), channel_id=1, source_target_pairs={{0,9},{1,8},{2,11},{3,10},{4,13},{5,12},{6,15},{7,14},{8,1},{9,0},... | collective-permute-start | bytes 129032 | tf_op jit(solution)/shard_map/ppermute | solution.py:484
  43.4 0.2 collective-permute-done.20.other_ref
  43.7 2.0 %conv_back.1 = bf16[1,8,16,768]{3,2,1,0:T(8,128)(2,1)} custom-call(f32[6,8,16,128]{3,2,1,0:T(8,128)S(1)} %get-tuple-element.84.grad_ref, bf16[6,8,16,128]{3,2,1,0:T(8,128)(2,1)S(1)} %collective-permute-done.20.other_ref, f32[6,128,128]{2,1,0:T(8,128)S(1)} %get-tuple-element.63.taps_ref.refs_6_), custom_call_target="tpu_custom_call" | custom-call | flops 110000000 | bytes 1179648 | tf_op jit(solution)/shard_map/conv_back/pallas_call | solution.py:451
  45.6 0.0 collective-permute-done.21.refs_1_
  45.6 2.4 %collective-permute-done.22.refs_2_ = bf16[56,384]{1,0:T(8,128)(2,1)S(1)} collective-permute-done((bf16[56,384]{1,0:T(8,128)(2,1)S(1)}, bf16[56,384]{1,0:T(8,128)(2,1)S(1)}, u32[]{:S(2)}, u32[]{:S(2)}) %collective-permute-start.22) | collective-permute-done | bytes 43040 | tf_op jit(solution)/shard_map/ppermute | solution.py:484
  48.1 0.0 collective-permute-done.23.refs_3_
  48.1 0.1 line_sum.1.mine_ref
  48.2 0.1 collective-permute-start.24
  48.3 1.4 %collective-permute-done.24.other_ref = f32[48,1280]{1,0:T(8,128)S(1)} collective-permute-done((f32[48,1280]{1,0:T(8,128)S(1)}, f32[48,1280]{1,0:T(8,128)S(1)}, u32[]{:S(2)}, u32[]{:S(2)}) %collective-permute-start.24) | collective-permute-done | bytes 245792 | tf_op jit(solution)/shard_map/ppermute | solution.py:496
  49.7 0.8 %finish.1 = (f32[48,1536]{1,0:T(8,128)}, f32[48,49]{1,0:T(8,128)}, f32[1,48]{1,0:T(1,128)}, f32[1,48]{1,0:T(1,128)}) custom-call(f32[48,1280]{1,0:T(8,128)S(1)} %line_sum.1.mine_ref, f32[48,1280]{1,0:T(8,128)S(1)} %collective-permute-done.24.other_ref), custom_call_target="tpu_custom_call" | custom-call | flops 550000000 | bytes 796224 | tf_op jit(solution)/shard_map/finish/pallas_call | solution.py:451
  (6 shorter events, 0.1 us)
Async XLA Ops:
  0.6 7.1 %copy-start = (bf16[1,8,16,768]{3,2,1,0:T(8,128)(2,1)S(1)}, bf16[1,8,16,768]{3,2,1,0:T(8,128)(2,1)}, u32[]{:S(2)}) copy-start(bf16[1,8,16,768]{3,2,1,0:T(8,128)(2,1)} %param.6) | copy-start | bytes 589828
  0.6 7.1 %copy-start.1 = (bf16[1,8,16,1536]{3,2,1,0:T(8,128)(2,1)S(1)}, bf16[1,8,16,1536]{3,2,1,0:T(8,128)(2,1)}, u32[]{:S(2)}) copy-start(bf16[1,8,16,1536]{3,2,1,0:T(8,128)(2,1)} %param.7) | copy-start | bytes 1179652
  2.4 9.6 %copy-start.2 = (bf16[56,384]{1,0:T(8,128)(2,1)S(1)}, bf16[56,384]{1,0:T(8,128)(2,1)}, u32[]{:S(2)}) copy-start(bf16[56,384]{1,0:T(8,128)(2,1)} %get-tuple-element.53.refs_0_) | copy-start | bytes 129028
  2.4 7.1 %collective-permute-start.1 = (bf16[56,384]{1,0:T(8,128)(2,1)}, bf16[56,384]{1,0:T(8,128)(2,1)S(1)}, u32[]{:S(2)}, u32[]{:S(2)}) collective-permute-start(bf16[56,384]{1,0:T(8,128)(2,1)} %get-tuple-element.55), channel_id=1, source_target_pairs={{0,17},{1,16},{2,19},{3,18},{4,21},{5,20},{6,23},{7,22},{8,25},{9,... | collective-permute-start | bytes 129032 | tf_op jit(solution)/shard_map/ppermute | solution.py:484
  5.9 5.6 %collective-permute-start.2 = (bf16[56,384]{1,0:T(8,128)(2,1)}, bf16[56,384]{1,0:T(8,128)(2,1)S(1)}, u32[]{:S(2)}, u32[]{:S(2)}) collective-permute-start(bf16[56,384]{1,0:T(8,128)(2,1)} %get-tuple-element.54), channel_id=1, source_target_pairs={{0,25},{1,24},{2,27},{3,26},{4,29},{5,28},{6,31},{7,30},{8,17},{9,... | collective-permute-start | bytes 129032 | tf_op jit(solution)/shard_map/ppermute | solution.py:484
  7.5 4.5 %collective-permute-start = (bf16[56,384]{1,0:T(8,128)(2,1)}, bf16[56,384]{1,0:T(8,128)(2,1)S(1)}, u32[]{:S(2)}, u32[]{:S(2)}) collective-permute-start(bf16[56,384]{1,0:T(8,128)(2,1)} %get-tuple-element.54), channel_id=1, source_target_pairs={{0,9},{1,8},{2,11},{3,10},{4,13},{5,12},{6,15},{7,14},{8,1},{9,0},... | collective-permute-start | bytes 129032 | tf_op jit(solution)/shard_map/ppermute | solution.py:484
  7.8 4.4 %collective-permute-start.3 = (bf16[128,768]{1,0:T(8,128)(2,1)S(1)}, bf16[128,768]{1,0:T(8,128)(2,1)S(1)}, u32[]{:S(2)}, u32[]{:S(2)}) collective-permute-start(bf16[128,768]{1,0:T(8,128)(2,1)S(1)} %get-tuple-element.59), channel_id=1, source_target_pairs={{0,1},{1,0},{2,3},{3,2},{4,5},{5,4},{6,7},{7,6},{8,9},{9,8},{10,11... | collective-permute-start | bytes 589832 | tf_op jit(solution)/shard_map/ppermute | solution.py:496
  7.9 14.8 %collective-permute-start.9 = (bf16[256,768]{1,0:T(8,128)(2,1)S(1)}, bf16[256,768]{1,0:T(8,128)(2,1)S(1)}, u32[]{:S(2)}, u32[]{:S(2)}) collective-permute-start(bf16[256,768]{1,0:T(8,128)(2,1)S(1)} %get-tuple-element.64), channel_id=1, source_target_pairs={{0,9},{1,8},{2,11},{3,10},{4,13},{5,12},{6,15},{7,14},{8,1},{9,0},... | collective-permute-start | bytes 1179656 | tf_op jit(solution)/shard_map/ppermute | solution.py:484
  12.2 5.2 %collective-permute-start.4 = (bf16[192,384]{1,0:T(8,128)(2,1)S(1)}, bf16[192,384]{1,0:T(8,128)(2,1)S(1)}, u32[]{:S(2)}, u32[]{:S(2)}) collective-permute-start(bf16[192,384]{1,0:T(8,128)(2,1)S(1)} %get-tuple-element.60.own_ref.refs_0_), channel_id=1, source_target_pairs={{0,2},{1,5},{2,0},{3,7},{4,6},{5,1},{6,4},{7,3},{8,10},{9,13},{10,... | collective-permute-start | bytes 442376 | tf_op jit(solution)/shard_map/ppermute | solution.py:493
  13.8 5.5 %collective-permute-start.8 = (bf16[96,128]{1,0:T(8,128)(2,1)S(1)}, bf16[96,128]{1,0:T(8,128)(2,1)S(1)}, u32[]{:S(2)}, u32[]{:S(2)}) collective-permute-start(bf16[96,128]{1,0:T(8,128)(2,1)S(1)} %get-tuple-element.61.refs_0_), channel_id=1, source_target_pairs={{0,7},{1,6},{2,5},{3,4},{4,3},{5,2},{6,1},{7,0},{8,15},{9,14},{10,... | collective-permute-start | bytes 73736 | tf_op jit(solution)/shard_map/ppermute | solution.py:484
  15.5 3.8 %collective-permute-start.7 = (bf16[96,128]{1,0:T(8,128)(2,1)S(1)}, bf16[96,128]{1,0:T(8,128)(2,1)S(1)}, u32[]{:S(2)}, u32[]{:S(2)}) collective-permute-start(bf16[96,128]{1,0:T(8,128)(2,1)S(1)} %get-tuple-element.61.refs_0_), channel_id=1, source_target_pairs={{0,5},{1,4},{2,7},{3,6},{4,1},{5,0},{6,3},{7,2},{8,13},{9,12},{10,... | collective-permute-start | bytes 73736 | tf_op jit(solution)/shard_map/ppermute | solution.py:484
  15.5 3.8 %collective-permute-start.6 = (bf16[96,128]{1,0:T(8,128)(2,1)S(1)}, bf16[96,128]{1,0:T(8,128)(2,1)S(1)}, u32[]{:S(2)}, u32[]{:S(2)}) collective-permute-start(bf16[96,128]{1,0:T(8,128)(2,1)S(1)} %get-tuple-element.61.refs_0_), channel_id=1, source_target_pairs={{0,3},{1,2},{2,1},{3,0},{4,7},{5,6},{6,5},{7,4},{8,11},{9,10},{10,... | collective-permute-start | bytes 73736 | tf_op jit(solution)/shard_map/ppermute | solution.py:484
  17.4 7.4 %collective-permute-start.5 = (bf16[384,384]{1,0:T(8,128)(2,1)S(1)}, bf16[384,384]{1,0:T(8,128)(2,1)S(1)}, u32[]{:S(2)}, u32[]{:S(2)}) collective-permute-start(bf16[384,384]{1,0:T(8,128)(2,1)S(1)} %join.1), channel_id=1, source_target_pairs={{0,4},{1,3},{2,6},{3,1},{4,0},{5,7},{6,2},{7,5},{8,12},{9,11},{10,... | collective-permute-start | bytes 884744 | tf_op jit(solution)/shard_map/ppermute | solution.py:493
  21.1 3.8 %collective-permute-start.10 = (bf16[128,768]{1,0:T(8,128)(2,1)S(1)}, bf16[128,768]{1,0:T(8,128)(2,1)S(1)}, u32[]{:S(2)}, u32[]{:S(2)}) collective-permute-start(bf16[128,768]{1,0:T(8,128)(2,1)S(1)} %get-tuple-element.62.refs_1_), channel_id=1, source_target_pairs={{0,1},{1,0},{2,3},{3,2},{4,5},{5,4},{6,7},{7,6},{8,9},{9,8},{10,11... | collective-permute-start | bytes 589832 | tf_op jit(solution)/shard_map/ppermute | solution.py:496
  24.2 1.7 %collective-permute-start.11 = (bf16[128,768]{1,0:T(8,128)(2,1)S(1)}, bf16[128,768]{1,0:T(8,128)(2,1)S(1)}, u32[]{:S(2)}, u32[]{:S(2)}) collective-permute-start(bf16[128,768]{1,0:T(8,128)(2,1)S(1)} %get-tuple-element.65.refs_2_), channel_id=1, source_target_pairs={{0,1},{1,0},{2,3},{3,2},{4,5},{5,4},{6,7},{7,6},{8,9},{9,8},{10,11... | collective-permute-start | bytes 589832 | tf_op jit(solution)/shard_map/ppermute | solution.py:496
  24.3 1.6 %collective-permute-start.12 = (bf16[128,384]{1,0:T(8,128)(2,1)S(1)}, bf16[128,384]{1,0:T(8,128)(2,1)S(1)}, u32[]{:S(2)}, u32[]{:S(2)}) collective-permute-start(bf16[128,384]{1,0:T(8,128)(2,1)S(1)} %get-tuple-element.67), channel_id=1, source_target_pairs={{0,1},{1,0},{2,3},{3,2},{4,5},{5,4},{6,7},{7,6},{8,9},{9,8},{10,11... | collective-permute-start | bytes 294920 | tf_op jit(solution)/shard_map/ppermute | solution.py:496
  28.0 3.8 %collective-permute-start.16 = (f32[256,768]{1,0:T(8,128)S(1)}, f32[256,768]{1,0:T(8,128)S(1)}, u32[]{:S(2)}, u32[]{:S(2)}) collective-permute-start(f32[256,768]{1,0:T(8,128)S(1)} %get-tuple-element.74), channel_id=1, source_target_pairs={{0,1},{1,0},{2,3},{3,2},{4,5},{5,4},{6,7},{7,6},{8,9},{9,8},{10,11... | collective-permute-start | bytes 2359304 | tf_op jit(solution)/shard_map/ppermute | solution.py:496
  28.3 8.3 %collective-permute-start.13 = (bf16[192,384]{1,0:T(8,128)(2,1)S(1)}, bf16[192,384]{1,0:T(8,128)(2,1)S(1)}, u32[]{:S(2)}, u32[]{:S(2)}) collective-permute-start(bf16[192,384]{1,0:T(8,128)(2,1)S(1)} %get-tuple-element.69), channel_id=1, source_target_pairs={{0,2},{2,0},{4,6},{6,4},{8,10},{10,8},{12,14},{14,12},{16,18},{18,... | collective-permute-start | bytes 442376 | tf_op jit(solution)/shard_map/ppermute | solution.py:478
  28.6 8.9 %collective-permute-start.14 = (bf16[192,384]{1,0:T(8,128)(2,1)S(1)}, bf16[192,384]{1,0:T(8,128)(2,1)S(1)}, u32[]{:S(2)}, u32[]{:S(2)}) collective-permute-start(bf16[192,384]{1,0:T(8,128)(2,1)S(1)} %get-tuple-element.70), channel_id=1, source_target_pairs={{0,4},{2,6},{4,0},{6,2},{8,12},{10,14},{12,8},{14,10},{16,20},{18,... | collective-permute-start | bytes 442376 | tf_op jit(solution)/shard_map/ppermute | solution.py:478
  29.8 7.8 %collective-permute-start.15 = (bf16[192,384]{1,0:T(8,128)(2,1)S(1)}, bf16[192,384]{1,0:T(8,128)(2,1)S(1)}, u32[]{:S(2)}, u32[]{:S(2)}) collective-permute-start(bf16[192,384]{1,0:T(8,128)(2,1)S(1)} %get-tuple-element.71), channel_id=1, source_target_pairs={{0,6},{2,4},{4,2},{6,0},{8,14},{10,12},{12,10},{14,8},{16,22},{18,... | collective-permute-start | bytes 442376 | tf_op jit(solution)/shard_map/ppermute | solution.py:478
  35.1 4.2 %collective-permute-start.17 = (bf16[96,128]{1,0:T(8,128)(2,1)S(1)}, bf16[96,128]{1,0:T(8,128)(2,1)S(1)}, u32[]{:S(2)}, u32[]{:S(2)}) collective-permute-start(bf16[96,128]{1,0:T(8,128)(2,1)S(1)} %get-tuple-element.80), channel_id=1, source_target_pairs={{0,7},{1,6},{2,5},{3,4},{4,3},{5,2},{6,1},{7,0},{8,15},{9,14},{10,... | collective-permute-start | bytes 73736 | tf_op jit(solution)/shard_map/ppermute | solution.py:484
  35.2 4.0 %collective-permute-start.18 = (bf16[96,128]{1,0:T(8,128)(2,1)S(1)}, bf16[96,128]{1,0:T(8,128)(2,1)S(1)}, u32[]{:S(2)}, u32[]{:S(2)}) collective-permute-start(bf16[96,128]{1,0:T(8,128)(2,1)S(1)} %get-tuple-element.81), channel_id=1, source_target_pairs={{0,5},{1,4},{2,7},{3,6},{4,1},{5,0},{6,3},{7,2},{8,13},{9,12},{10,... | collective-permute-start | bytes 73736 | tf_op jit(solution)/shard_map/ppermute | solution.py:484
  36.6 3.3 %collective-permute-start.19 = (bf16[96,128]{1,0:T(8,128)(2,1)S(1)}, bf16[96,128]{1,0:T(8,128)(2,1)S(1)}, u32[]{:S(2)}, u32[]{:S(2)}) collective-permute-start(bf16[96,128]{1,0:T(8,128)(2,1)S(1)} %get-tuple-element.82), channel_id=1, source_target_pairs={{0,3},{1,2},{2,1},{3,0},{4,7},{5,6},{6,5},{7,4},{8,11},{9,10},{10,... | collective-permute-start | bytes 73736 | tf_op jit(solution)/shard_map/ppermute | solution.py:484
  37.6 6.1 %collective-permute-start.20 = (bf16[6,8,16,128]{3,2,1,0:T(8,128)(2,1)S(1)}, bf16[6,8,16,128]{3,2,1,0:T(8,128)(2,1)S(1)}, u32[]{:S(2)}, u32[]{:S(2)}) collective-permute-start(bf16[6,8,16,128]{3,2,1,0:T(8,128)(2,1)S(1)} %get-tuple-element.85), channel_id=1, source_target_pairs={{0,9},{1,8},{2,11},{3,10},{4,13},{5,12},{6,15},{7,14},{8,1},{9,0},... | collective-permute-start | bytes 589832 | tf_op jit(solution)/shard_map/ppermute | solution.py:484
  40.0 5.6 %collective-permute-start.21 = (bf16[56,384]{1,0:T(8,128)(2,1)S(1)}, bf16[56,384]{1,0:T(8,128)(2,1)S(1)}, u32[]{:S(2)}, u32[]{:S(2)}) collective-permute-start(bf16[56,384]{1,0:T(8,128)(2,1)S(1)} %get-tuple-element.88), channel_id=1, source_target_pairs={{0,17},{1,16},{2,19},{3,18},{4,21},{5,20},{6,23},{7,22},{8,25},{9,... | collective-permute-start | bytes 129032 | tf_op jit(solution)/shard_map/ppermute | solution.py:484
  41.9 6.2 %collective-permute-start.22 = (bf16[56,384]{1,0:T(8,128)(2,1)S(1)}, bf16[56,384]{1,0:T(8,128)(2,1)S(1)}, u32[]{:S(2)}, u32[]{:S(2)}) collective-permute-start(bf16[56,384]{1,0:T(8,128)(2,1)S(1)} %get-tuple-element.89), channel_id=1, source_target_pairs={{0,25},{1,24},{2,27},{3,26},{4,29},{5,28},{6,31},{7,30},{8,17},{9,... | collective-permute-start | bytes 129032 | tf_op jit(solution)/shard_map/ppermute | solution.py:484
  42.9 5.2 %collective-permute-start.23 = (bf16[56,384]{1,0:T(8,128)(2,1)S(1)}, bf16[56,384]{1,0:T(8,128)(2,1)S(1)}, u32[]{:S(2)}, u32[]{:S(2)}) collective-permute-start(bf16[56,384]{1,0:T(8,128)(2,1)S(1)} %get-tuple-element.90), channel_id=1, source_target_pairs={{0,9},{1,8},{2,11},{3,10},{4,13},{5,12},{6,15},{7,14},{8,1},{9,0},... | collective-permute-start | bytes 129032 | tf_op jit(solution)/shard_map/ppermute | solution.py:484
  48.2 1.5 %collective-permute-start.24 = (f32[48,1280]{1,0:T(8,128)S(1)}, f32[48,1280]{1,0:T(8,128)S(1)}, u32[]{:S(2)}, u32[]{:S(2)}) collective-permute-start(f32[48,1280]{1,0:T(8,128)S(1)} %line_sum.1.mine_ref), channel_id=1, source_target_pairs={{0,1},{1,0},{2,3},{3,2},{4,5},{5,4},{6,7},{7,6},{8,9},{9,8},{10,11... | collective-permute-start | bytes 737288 | tf_op jit(solution)/shard_map/ppermute | solution.py:496

commit v22 on v21

--- a/solution.py
+++ b/solution.py
@@ -349,7 +349,7 @@
         gp_ref[...], weight[...], (((1,), (1,)), ((), ())), preferred_element_type=F32
     )
     own_ref[...] = grad_normed[:rows]
-    other_ref[...] = grad_normed[rows:]
+    other_ref[...] = grad_normed[rows:].astype(BF16)
 
 
 def norm_back_kernel(relative, own, height, breadth, *refs):
@@ -370,7 +370,7 @@
             lanes = slice(tile * LANES, (tile + 1) * LANES)
             part = source[:pixels, lanes].astype(F32)
             padded[image, tile, :, 8 : 8 + breadth, :] = part.reshape(height, breadth, LANES)
-            grad_normed = gn_own[span, lanes] + gn_other[span, lanes]
+            grad_normed = gn_own[span, lanes] + gn_other[span, lanes].astype(F32)
             whitened = white_ref[:, lanes]
             product = grad_normed * whitened
             gain = taps_ref[tile, TAPS : TAPS + 1, :]
@@ -384,7 +384,7 @@
         for tile in range(tiles):
             lanes = slice(tile * LANES, (tile + 1) * LANES)
             gain = taps_ref[tile, TAPS : TAPS + 1, :]
-            grad_white = (gn_own[span, lanes] + gn_other[span, lanes]) * gain
+            grad_white = (gn_own[span, lanes] + gn_other[span, lanes].astype(F32)) * gain
             grad_conv = inv_ref[...] * (
                 grad_white - mean_first - white_ref[:, lanes] * mean_second
             )
@@ -636,7 +636,7 @@
     gn_kept, gn_sent = call(
         back_project_kernel,
         "back_project",
-        [shape((2 * pixels, depth), F32)] * 2,
+        [shape((2 * pixels, depth), F32), shape((2 * pixels, depth), BF16)],
         [],
         0.7,
         weight,

time: 50.6 us -> 50.6 us (level)
  no operation moved by 1% of the time
where the time goes in v22:
time: 50.6 us; the launch traced here: 50.5 us
  starting transfers between devices  25.8 us (51%)
  Pallas kernels  13.7 us (27%)
  waiting for transfers between devices  10.2 us (20%)
  between operations  0.76 us (2%)
    ppermute x14, starting transfers between devices, crossing(): return lax.ppermute(array, ('shard', 'rep'), pairs)  16.2 us
    pallas_call x14, Pallas kernels, call(): pl.pallas_call(kernel, out_shape=outs, in_specs=[VMEM] * len(args), out_s...  13.7 us
    ppermute x14, waiting for transfers between devices, crossing(): return lax.ppermute(array, ('shard', 'rep'), pairs)  7.48 us
    ppermute x3, starting transfers between devices, over_shard(): return lax.ppermute(array, 'shard', [(i, i ^ flip) for i in range(shards)])  3.49 us
    ppermute x2, starting transfers between devices, hop(): return lax.ppermute(array, ('shard', 'rep'), pairs)  3.4 us
    ppermute x6, starting transfers between devices, over_core(): return lax.ppermute(array, 'rep', [(i, i ^ 1) for i in range(reps)])  2.68 us
    ppermute x6, waiting for transfers between devices, over_core(): return lax.ppermute(array, 'rep', [(i, i ^ 1) for i in range(reps)])  2.4 us
  transfers between devices with their start and end apart: 25, of which 10 were waited for; matrix products, arithmetic and copies ran while one was open for 0% of the time, Pallas kernels for 18%

profile of v22, /device:TPU:0, one launch (start us, length us, event | category | flops | bytes accessed | tf_op | source)
XLA Modules:
  0.0 50.5 jit_solution(18091228517146090087)
XLA Ops:
  0.6 0.0 copy-start
  0.6 0.0 copy-start.1
  0.7 1.8 %pack.1 = (bf16[56,384]{1,0:T(8,128)(2,1)}, bf16[56,384]{1,0:T(8,128)(2,1)}, bf16[56,384]{1,0:T(8,128)(2,1)}) custom-call(bf16[48,1536]{1,0:T(8,128)(2,1)} %w_ref.1, bf16[48,49]{1,0:T(8,128)(2,1)} %dw_ref.1, bf16[1,48]{1,0:T(2,128)(2,1)} %bitcast.11, bf16[1,48]{1,0:T(2,128)(2,1)} %bitcast.12), custom_call_target="tpu_custom_call" | custom-call | flops 550000000 | bytes 281376 | tf_op jit(solution)/shard_map/pack/pallas_call | solution.py:451
  2.4 3.5 %collective-permute-start.1 = (bf16[56,384]{1,0:T(8,128)(2,1)}, bf16[56,384]{1,0:T(8,128)(2,1)S(1)}, u32[]{:S(2)}, u32[]{:S(2)}) collective-permute-start(bf16[56,384]{1,0:T(8,128)(2,1)} %get-tuple-element.55), channel_id=1, source_target_pairs={{0,17},{1,16},{2,19},{3,18},{4,21},{5,20},{6,23},{7,22},{8,25},{9,... | collective-permute-start | bytes 129032 | tf_op jit(solution)/shard_map/ppermute | solution.py:484
  5.9 1.6 %collective-permute-start.2 = (bf16[56,384]{1,0:T(8,128)(2,1)}, bf16[56,384]{1,0:T(8,128)(2,1)S(1)}, u32[]{:S(2)}, u32[]{:S(2)}) collective-permute-start(bf16[56,384]{1,0:T(8,128)(2,1)} %get-tuple-element.54), channel_id=1, source_target_pairs={{0,25},{1,24},{2,27},{3,26},{4,29},{5,28},{6,31},{7,30},{8,17},{9,... | collective-permute-start | bytes 129032 | tf_op jit(solution)/shard_map/ppermute | solution.py:484
  7.5 0.2 collective-permute-start
  7.8 0.1 collective-permute-start.3
  7.9 1.7 %collective-permute-start.9 = (bf16[256,768]{1,0:T(8,128)(2,1)S(1)}, bf16[256,768]{1,0:T(8,128)(2,1)S(1)}, u32[]{:S(2)}, u32[]{:S(2)}) collective-permute-start(bf16[256,768]{1,0:T(8,128)(2,1)S(1)} %get-tuple-element.64), channel_id=1, source_target_pairs={{0,9},{1,8},{2,11},{3,10},{4,13},{5,12},{6,15},{7,14},{8,1},{9,0},... | collective-permute-start | bytes 1179656 | tf_op jit(solution)/shard_map/ppermute | solution.py:484
  9.6 0.0 collective-permute-done.1.refs_2_
  9.6 1.9 %collective-permute-done.2.refs_3_ = bf16[56,384]{1,0:T(8,128)(2,1)S(1)} collective-permute-done((bf16[56,384]{1,0:T(8,128)(2,1)}, bf16[56,384]{1,0:T(8,128)(2,1)S(1)}, u32[]{:S(2)}, u32[]{:S(2)}) %collective-permute-start.2) | collective-permute-done | bytes 43040 | tf_op jit(solution)/shard_map/ppermute | solution.py:484
  11.5 0.6 %collective-permute-done.refs_1_ = bf16[56,384]{1,0:T(8,128)(2,1)S(1)} collective-permute-done((bf16[56,384]{1,0:T(8,128)(2,1)}, bf16[56,384]{1,0:T(8,128)(2,1)S(1)}, u32[]{:S(2)}, u32[]{:S(2)}) %collective-permute-start) | collective-permute-done | bytes 43040 | tf_op jit(solution)/shard_map/ppermute | solution.py:484
  12.0 0.1 assemble.1
  12.2 0.0 collective-permute-done.3.refs_6_
  12.2 1.6 %collective-permute-start.4 = (bf16[192,384]{1,0:T(8,128)(2,1)S(1)}, bf16[192,384]{1,0:T(8,128)(2,1)S(1)}, u32[]{:S(2)}, u32[]{:S(2)}) collective-permute-start(bf16[192,384]{1,0:T(8,128)(2,1)S(1)} %get-tuple-element.60.own_ref.refs_0_), channel_id=1, source_target_pairs={{0,2},{1,5},{2,0},{3,7},{4,6},{5,1},{6,4},{7,3},{8,10},{9,13},{10,... | collective-permute-start | bytes 442376 | tf_op jit(solution)/shard_map/ppermute | solution.py:493
  13.8 1.7 %collective-permute-start.8 = (bf16[96,128]{1,0:T(8,128)(2,1)S(1)}, bf16[96,128]{1,0:T(8,128)(2,1)S(1)}, u32[]{:S(2)}, u32[]{:S(2)}) collective-permute-start(bf16[96,128]{1,0:T(8,128)(2,1)S(1)} %get-tuple-element.61.refs_0_), channel_id=1, source_target_pairs={{0,7},{1,6},{2,5},{3,4},{4,3},{5,2},{6,1},{7,0},{8,15},{9,14},{10,... | collective-permute-start | bytes 73736 | tf_op jit(solution)/shard_map/ppermute | solution.py:484
  15.5 0.0 collective-permute-start.7
  15.5 1.8 %collective-permute-start.6 = (bf16[96,128]{1,0:T(8,128)(2,1)S(1)}, bf16[96,128]{1,0:T(8,128)(2,1)S(1)}, u32[]{:S(2)}, u32[]{:S(2)}) collective-permute-start(bf16[96,128]{1,0:T(8,128)(2,1)S(1)} %get-tuple-element.61.refs_0_), channel_id=1, source_target_pairs={{0,3},{1,2},{2,1},{3,0},{4,7},{5,6},{6,5},{7,4},{8,11},{9,10},{10,... | collective-permute-start | bytes 73736 | tf_op jit(solution)/shard_map/ppermute | solution.py:484
  17.2 0.2 collective-permute-done.4.came_ref.refs_1_
  17.4 1.8 %collective-permute-start.5 = (bf16[384,384]{1,0:T(8,128)(2,1)S(1)}, bf16[384,384]{1,0:T(8,128)(2,1)S(1)}, u32[]{:S(2)}, u32[]{:S(2)}) collective-permute-start(bf16[384,384]{1,0:T(8,128)(2,1)S(1)} %join.1), channel_id=1, source_target_pairs={{0,4},{1,3},{2,6},{3,1},{4,0},{5,7},{6,2},{7,5},{8,12},{9,11},{10,... | collective-permute-start | bytes 884744 | tf_op jit(solution)/shard_map/ppermute | solution.py:493
  19.3 0.0 collective-permute-done.8.refs_3_
  19.3 0.0 collective-permute-done.7.refs_2_
  19.3 0.0 collective-permute-done.6.refs_1_
  19.3 1.8 %conv_norm.1 = (bf16[128,768]{1,0:T(8,128)(2,1)S(1)}, f32[128,768]{1,0:T(8,128)S(1)}, f32[128,128]{1,0:T(8,128)S(1)}, f32[6,128,128]{2,1,0:T(8,128)S(1)}) custom-call(bf16[96,128]{1,0:T(8,128)(2,1)S(1)} %get-tuple-element.61.refs_0_, bf16[96,128]{1,0:T(8,128)(2,1)S(1)} %collective-permute-done.6.refs_1_, bf16[96,128]{1,0:T(8,128)(2,1)S(1)} %collective-permute-done.7.refs_2_, ...), custom_call_target="tpu_custom_call" | custom-call | flops 110000000 | bytes 1343488 | tf_op jit(solution)/shard_map/conv_norm/pallas_call | solution.py:451
  21.1 1.6 %collective-permute-start.10 = (bf16[128,768]{1,0:T(8,128)(2,1)S(1)}, bf16[128,768]{1,0:T(8,128)(2,1)S(1)}, u32[]{:S(2)}, u32[]{:S(2)}) collective-permute-start(bf16[128,768]{1,0:T(8,128)(2,1)S(1)} %get-tuple-element.62.refs_1_), channel_id=1, source_target_pairs={{0,1},{1,0},{2,3},{3,2},{4,5},{5,4},{6,7},{7,6},{8,9},{9,8},{10,11... | collective-permute-start | bytes 589832 | tf_op jit(solution)/shard_map/ppermute | solution.py:496
  22.7 0.0 collective-permute-done.9.far_ref.refs_7_.refs_8_
  22.7 1.5 %far_norm.1 = (bf16[128,768]{1,0:T(8,128)(2,1)S(1)}, f32[128,768]{1,0:T(8,128)S(1)}, f32[128,128]{1,0:T(8,128)S(1)}, bf16[128,384]{1,0:T(8,128)(2,1)S(1)}) custom-call(f32[6,128,128]{2,1,0:T(8,128)S(1)} %get-tuple-element.63.taps_ref.refs_6_, bf16[256,768]{1,0:T(8,128)(2,1)S(1)} %collective-permute-done.9.far_ref.refs_7_.refs_8_), custom_call_target="tpu_custom_call" | custom-call | flops 1100000000 | bytes 1540096 | tf_op jit(solution)/shard_map/far_norm/pallas_call | solution.py:451
  24.2 0.1 collective-permute-start.11
  24.3 0.5 collective-permute-start.12
  24.8 0.0 collective-permute-done.5.refs_2_
  24.8 0.1 order.1.refs_0_.weight
  24.9 0.0 collective-permute-done.10.refs_3_
  24.9 1.0 %collective-permute-done.12.refs_8_ = bf16[128,384]{1,0:T(8,128)(2,1)S(1)} collective-permute-done((bf16[128,384]{1,0:T(8,128)(2,1)S(1)}, bf16[128,384]{1,0:T(8,128)(2,1)S(1)}, u32[]{:S(2)}, u32[]{:S(2)}) %collective-permute-start.12) | collective-permute-done | bytes 98336 | tf_op jit(solution)/shard_map/ppermute | solution.py:496
  25.9 0.0 collective-permute-done.11.refs_4_
  25.9 1.5 %project.1 = (f32[192,384]{1,0:T(8,128)S(1)}, bf16[192,384]{1,0:T(8,128)(2,1)S(1)}, bf16[192,384]{1,0:T(8,128)(2,1)S(1)}, bf16[192,384]{1,0:T(8,128)(2,1)S(1)}, bf16[512,384]{1,0:T(8,128)(2,1)S(1)}) custom-call(bf16[768,384]{1,0:T(8,128)(2,1)S(1)} %order.1.refs_0_.weight, bf16[128,768]{1,0:T(8,128)(2,1)S(1)} %get-tuple-element.62.refs_1_, ...), custom_call_target="tpu_custom_call" | custom-call | flops 1760000000 | bytes 3588096 | tf_op jit(solution)/shard_map/project/pallas_call | solution.py:451
  27.4 0.6 %back_project.1 = (f32[256,768]{1,0:T(8,128)S(1)}, bf16[256,768]{1,0:T(8,128)(2,1)S(1)}) custom-call(bf16[768,384]{1,0:T(8,128)(2,1)S(1)} %order.1.refs_0_.weight, bf16[512,384]{1,0:T(8,128)(2,1)S(1)} %get-tuple-element.72.gp_ref), custom_call_target="tpu_custom_call" | custom-call | flops 770000000 | bytes 2162688 | tf_op jit(solution)/shard_map/back_project/pallas_call | solution.py:451
  28.0 0.3 collective-permute-start.16
  28.3 0.3 collective-permute-start.13
  28.6 1.2 %collective-permute-start.14 = (bf16[192,384]{1,0:T(8,128)(2,1)S(1)}, bf16[192,384]{1,0:T(8,128)(2,1)S(1)}, u32[]{:S(2)}, u32[]{:S(2)}) collective-permute-start(bf16[192,384]{1,0:T(8,128)(2,1)S(1)} %get-tuple-element.70), channel_id=1, source_target_pairs={{0,4},{2,6},{4,0},{6,2},{8,12},{10,14},{12,8},{14,10},{16,20},{18,... | collective-permute-start | bytes 442376 | tf_op jit(solution)/shard_map/ppermute | solution.py:478
  29.8 2.0 %collective-permute-start.15 = (bf16[192,384]{1,0:T(8,128)(2,1)S(1)}, bf16[192,384]{1,0:T(8,128)(2,1)S(1)}, u32[]{:S(2)}, u32[]{:S(2)}) collective-permute-start(bf16[192,384]{1,0:T(8,128)(2,1)S(1)} %get-tuple-element.71), channel_id=1, source_target_pairs={{0,6},{2,4},{4,2},{6,0},{8,14},{10,12},{12,10},{14,8},{16,22},{18,... | collective-permute-start | bytes 442376 | tf_op jit(solution)/shard_map/ppermute | solution.py:478
  31.8 0.0 collective-permute-done.16.refs_1_
  31.8 3.2 %norm_back.1 = (f32[96,128]{1,0:T(8,128)S(1)}, bf16[96,128]{1,0:T(8,128)(2,1)S(1)}, bf16[96,128]{1,0:T(8,128)(2,1)S(1)}, bf16[96,128]{1,0:T(8,128)(2,1)S(1)}, f3...) custom-call(f32[256,768]{1,0:T(8,128)S(1)} %get-tuple-element.73.refs_0_, ...), custom_call_target="tpu_custom_call" | custom-call | flops 110000000 | bytes 3792896 | tf_op jit(solution)/shard_map/norm_back/pallas_call | solution.py:451
  35.1 0.2 collective-permute-start.17
  35.3 1.4 %collective-permute-start.18 = (bf16[96,128]{1,0:T(8,128)(2,1)S(1)}, bf16[96,128]{1,0:T(8,128)(2,1)S(1)}, u32[]{:S(2)}, u32[]{:S(2)}) collective-permute-start(bf16[96,128]{1,0:T(8,128)(2,1)S(1)} %get-tuple-element.81), channel_id=1, source_target_pairs={{0,5},{1,4},{2,7},{3,6},{4,1},{5,0},{6,3},{7,2},{8,13},{9,12},{10,... | collective-permute-start | bytes 73736 | tf_op jit(solution)/shard_map/ppermute | solution.py:484
  36.6 0.0 collective-permute-done.13.refs_1_
  36.6 0.7 %collective-permute-start.19 = (bf16[96,128]{1,0:T(8,128)(2,1)S(1)}, bf16[96,128]{1,0:T(8,128)(2,1)S(1)}, u32[]{:S(2)}, u32[]{:S(2)}) collective-permute-start(bf16[96,128]{1,0:T(8,128)(2,1)S(1)} %get-tuple-element.82), channel_id=1, source_target_pairs={{0,3},{1,2},{2,1},{3,0},{4,7},{5,6},{6,5},{7,4},{8,11},{9,10},{10,... | collective-permute-start | bytes 73736 | tf_op jit(solution)/shard_map/ppermute | solution.py:484
  37.4 0.2 collective-permute-done.14.refs_2_
  37.6 0.0 collective-permute-start.20
  37.6 0.0 collective-permute-done.15.refs_3_
  37.6 1.7 %collective-permute-done.17.refs_5_ = bf16[96,128]{1,0:T(8,128)(2,1)S(1)} collective-permute-done((bf16[96,128]{1,0:T(8,128)(2,1)S(1)}, bf16[96,128]{1,0:T(8,128)(2,1)S(1)}, u32[]{:S(2)}, u32[]{:S(2)}) %collective-permute-start.17) | collective-permute-done | bytes 24608 | tf_op jit(solution)/shard_map/ppermute | solution.py:484
  39.3 0.0 collective-permute-done.18.refs_6_
  39.3 0.6 %collective-permute-done.19.refs_7_ = bf16[96,128]{1,0:T(8,128)(2,1)S(1)} collective-permute-done((bf16[96,128]{1,0:T(8,128)(2,1)S(1)}, bf16[96,128]{1,0:T(8,128)(2,1)S(1)}, u32[]{:S(2)}, u32[]{:S(2)}) %collective-permute-start.19) | collective-permute-done | bytes 24608 | tf_op jit(solution)/shard_map/ppermute | solution.py:484
  39.9 0.2 plane_sum.1
  40.1 1.8 %collective-permute-start.21 = (bf16[56,384]{1,0:T(8,128)(2,1)S(1)}, bf16[56,384]{1,0:T(8,128)(2,1)S(1)}, u32[]{:S(2)}, u32[]{:S(2)}) collective-permute-start(bf16[56,384]{1,0:T(8,128)(2,1)S(1)} %get-tuple-element.88), channel_id=1, source_target_pairs={{0,17},{1,16},{2,19},{3,18},{4,21},{5,20},{6,23},{7,22},{8,25},{9,... | collective-permute-start | bytes 129032 | tf_op jit(solution)/shard_map/ppermute | solution.py:484
  41.9 1.0 %collective-permute-start.22 = (bf16[56,384]{1,0:T(8,128)(2,1)S(1)}, bf16[56,384]{1,0:T(8,128)(2,1)S(1)}, u32[]{:S(2)}, u32[]{:S(2)}) collective-permute-start(bf16[56,384]{1,0:T(8,128)(2,1)S(1)} %get-tuple-element.89), channel_id=1, source_target_pairs={{0,25},{1,24},{2,27},{3,26},{4,29},{5,28},{6,31},{7,30},{8,17},{9,... | collective-permute-start | bytes 129032 | tf_op jit(solution)/shard_map/ppermute | solution.py:484
  42.9 0.6 %collective-permute-start.23 = (bf16[56,384]{1,0:T(8,128)(2,1)S(1)}, bf16[56,384]{1,0:T(8,128)(2,1)S(1)}, u32[]{:S(2)}, u32[]{:S(2)}) collective-permute-start(bf16[56,384]{1,0:T(8,128)(2,1)S(1)} %get-tuple-element.90), channel_id=1, source_target_pairs={{0,9},{1,8},{2,11},{3,10},{4,13},{5,12},{6,15},{7,14},{8,1},{9,0},... | collective-permute-start | bytes 129032 | tf_op jit(solution)/shard_map/ppermute | solution.py:484
  43.5 0.2 collective-permute-done.20.other_ref
  43.7 2.0 %conv_back.1 = bf16[1,8,16,768]{3,2,1,0:T(8,128)(2,1)} custom-call(f32[6,8,16,128]{3,2,1,0:T(8,128)S(1)} %get-tuple-element.84.grad_ref, bf16[6,8,16,128]{3,2,1,0:T(8,128)(2,1)S(1)} %collective-permute-done.20.other_ref, f32[6,128,128]{2,1,0:T(8,128)S(1)} %get-tuple-element.63.taps_ref.refs_6_), custom_call_target="tpu_custom_call" | custom-call | flops 110000000 | bytes 1179648 | tf_op jit(solution)/shard_map/conv_back/pallas_call | solution.py:451
  45.6 0.0 collective-permute-done.21.refs_1_
  45.6 2.4 %collective-permute-done.22.refs_2_ = bf16[56,384]{1,0:T(8,128)(2,1)S(1)} collective-permute-done((bf16[56,384]{1,0:T(8,128)(2,1)S(1)}, bf16[56,384]{1,0:T(8,128)(2,1)S(1)}, u32[]{:S(2)}, u32[]{:S(2)}) %collective-permute-start.22) | collective-permute-done | bytes 43040 | tf_op jit(solution)/shard_map/ppermute | solution.py:484
  48.1 0.0 collective-permute-done.23.refs_3_
  48.1 0.1 line_sum.1.mine_ref
  48.2 0.1 collective-permute-start.24
  48.3 1.4 %collective-permute-done.24.other_ref = f32[48,1280]{1,0:T(8,128)S(1)} collective-permute-done((f32[48,1280]{1,0:T(8,128)S(1)}, f32[48,1280]{1,0:T(8,128)S(1)}, u32[]{:S(2)}, u32[]{:S(2)}) %collective-permute-start.24) | collective-permute-done | bytes 245792 | tf_op jit(solution)/shard_map/ppermute | solution.py:496
  49.7 0.8 %finish.1 = (f32[48,1536]{1,0:T(8,128)}, f32[48,49]{1,0:T(8,128)}, f32[1,48]{1,0:T(1,128)}, f32[1,48]{1,0:T(1,128)}) custom-call(f32[48,1280]{1,0:T(8,128)S(1)} %line_sum.1.mine_ref, f32[48,1280]{1,0:T(8,128)S(1)} %collective-permute-done.24.other_ref), custom_call_target="tpu_custom_call" | custom-call | flops 550000000 | bytes 796224 | tf_op jit(solution)/shard_map/finish/pallas_call | solution.py:451
  (6 shorter events, 0.1 us)
Async XLA Ops:
  0.6 7.1 %copy-start = (bf16[1,8,16,768]{3,2,1,0:T(8,128)(2,1)S(1)}, bf16[1,8,16,768]{3,2,1,0:T(8,128)(2,1)}, u32[]{:S(2)}) copy-start(bf16[1,8,16,768]{3,2,1,0:T(8,128)(2,1)} %param.6) | copy-start | bytes 589828
  0.6 7.1 %copy-start.1 = (bf16[1,8,16,1536]{3,2,1,0:T(8,128)(2,1)S(1)}, bf16[1,8,16,1536]{3,2,1,0:T(8,128)(2,1)}, u32[]{:S(2)}) copy-start(bf16[1,8,16,1536]{3,2,1,0:T(8,128)(2,1)} %param.7) | copy-start | bytes 1179652
  2.4 9.6 %copy-start.2 = (bf16[56,384]{1,0:T(8,128)(2,1)S(1)}, bf16[56,384]{1,0:T(8,128)(2,1)}, u32[]{:S(2)}) copy-start(bf16[56,384]{1,0:T(8,128)(2,1)} %get-tuple-element.53.refs_0_) | copy-start | bytes 129028
  2.4 7.1 %collective-permute-start.1 = (bf16[56,384]{1,0:T(8,128)(2,1)}, bf16[56,384]{1,0:T(8,128)(2,1)S(1)}, u32[]{:S(2)}, u32[]{:S(2)}) collective-permute-start(bf16[56,384]{1,0:T(8,128)(2,1)} %get-tuple-element.55), channel_id=1, source_target_pairs={{0,17},{1,16},{2,19},{3,18},{4,21},{5,20},{6,23},{7,22},{8,25},{9,... | collective-permute-start | bytes 129032 | tf_op jit(solution)/shard_map/ppermute | solution.py:484
  5.9 5.6 %collective-permute-start.2 = (bf16[56,384]{1,0:T(8,128)(2,1)}, bf16[56,384]{1,0:T(8,128)(2,1)S(1)}, u32[]{:S(2)}, u32[]{:S(2)}) collective-permute-start(bf16[56,384]{1,0:T(8,128)(2,1)} %get-tuple-element.54), channel_id=1, source_target_pairs={{0,25},{1,24},{2,27},{3,26},{4,29},{5,28},{6,31},{7,30},{8,17},{9,... | collective-permute-start | bytes 129032 | tf_op jit(solution)/shard_map/ppermute | solution.py:484
  7.5 4.5 %collective-permute-start = (bf16[56,384]{1,0:T(8,128)(2,1)}, bf16[56,384]{1,0:T(8,128)(2,1)S(1)}, u32[]{:S(2)}, u32[]{:S(2)}) collective-permute-start(bf16[56,384]{1,0:T(8,128)(2,1)} %get-tuple-element.54), channel_id=1, source_target_pairs={{0,9},{1,8},{2,11},{3,10},{4,13},{5,12},{6,15},{7,14},{8,1},{9,0},... | collective-permute-start | bytes 129032 | tf_op jit(solution)/shard_map/ppermute | solution.py:484
  7.8 4.4 %collective-permute-start.3 = (bf16[128,768]{1,0:T(8,128)(2,1)S(1)}, bf16[128,768]{1,0:T(8,128)(2,1)S(1)}, u32[]{:S(2)}, u32[]{:S(2)}) collective-permute-start(bf16[128,768]{1,0:T(8,128)(2,1)S(1)} %get-tuple-element.59), channel_id=1, source_target_pairs={{0,1},{1,0},{2,3},{3,2},{4,5},{5,4},{6,7},{7,6},{8,9},{9,8},{10,11... | collective-permute-start | bytes 589832 | tf_op jit(solution)/shard_map/ppermute | solution.py:496
  7.9 14.8 %collective-permute-start.9 = (bf16[256,768]{1,0:T(8,128)(2,1)S(1)}, bf16[256,768]{1,0:T(8,128)(2,1)S(1)}, u32[]{:S(2)}, u32[]{:S(2)}) collective-permute-start(bf16[256,768]{1,0:T(8,128)(2,1)S(1)} %get-tuple-element.64), channel_id=1, source_target_pairs={{0,9},{1,8},{2,11},{3,10},{4,13},{5,12},{6,15},{7,14},{8,1},{9,0},... | collective-permute-start | bytes 1179656 | tf_op jit(solution)/shard_map/ppermute | solution.py:484
  12.2 5.2 %collective-permute-start.4 = (bf16[192,384]{1,0:T(8,128)(2,1)S(1)}, bf16[192,384]{1,0:T(8,128)(2,1)S(1)}, u32[]{:S(2)}, u32[]{:S(2)}) collective-permute-start(bf16[192,384]{1,0:T(8,128)(2,1)S(1)} %get-tuple-element.60.own_ref.refs_0_), channel_id=1, source_target_pairs={{0,2},{1,5},{2,0},{3,7},{4,6},{5,1},{6,4},{7,3},{8,10},{9,13},{10,... | collective-permute-start | bytes 442376 | tf_op jit(solution)/shard_map/ppermute | solution.py:493
  13.8 5.5 %collective-permute-start.8 = (bf16[96,128]{1,0:T(8,128)(2,1)S(1)}, bf16[96,128]{1,0:T(8,128)(2,1)S(1)}, u32[]{:S(2)}, u32[]{:S(2)}) collective-permute-start(bf16[96,128]{1,0:T(8,128)(2,1)S(1)} %get-tuple-element.61.refs_0_), channel_id=1, source_target_pairs={{0,7},{1,6},{2,5},{3,4},{4,3},{5,2},{6,1},{7,0},{8,15},{9,14},{10,... | collective-permute-start | bytes 73736 | tf_op jit(solution)/shard_map/ppermute | solution.py:484
  15.5 3.8 %collective-permute-start.7 = (bf16[96,128]{1,0:T(8,128)(2,1)S(1)}, bf16[96,128]{1,0:T(8,128)(2,1)S(1)}, u32[]{:S(2)}, u32[]{:S(2)}) collective-permute-start(bf16[96,128]{1,0:T(8,128)(2,1)S(1)} %get-tuple-element.61.refs_0_), channel_id=1, source_target_pairs={{0,5},{1,4},{2,7},{3,6},{4,1},{5,0},{6,3},{7,2},{8,13},{9,12},{10,... | collective-permute-start | bytes 73736 | tf_op jit(solution)/shard_map/ppermute | solution.py:484
  15.5 3.8 %collective-permute-start.6 = (bf16[96,128]{1,0:T(8,128)(2,1)S(1)}, bf16[96,128]{1,0:T(8,128)(2,1)S(1)}, u32[]{:S(2)}, u32[]{:S(2)}) collective-permute-start(bf16[96,128]{1,0:T(8,128)(2,1)S(1)} %get-tuple-element.61.refs_0_), channel_id=1, source_target_pairs={{0,3},{1,2},{2,1},{3,0},{4,7},{5,6},{6,5},{7,4},{8,11},{9,10},{10,... | collective-permute-start | bytes 73736 | tf_op jit(solution)/shard_map/ppermute | solution.py:484
  17.4 7.4 %collective-permute-start.5 = (bf16[384,384]{1,0:T(8,128)(2,1)S(1)}, bf16[384,384]{1,0:T(8,128)(2,1)S(1)}, u32[]{:S(2)}, u32[]{:S(2)}) collective-permute-start(bf16[384,384]{1,0:T(8,128)(2,1)S(1)} %join.1), channel_id=1, source_target_pairs={{0,4},{1,3},{2,6},{3,1},{4,0},{5,7},{6,2},{7,5},{8,12},{9,11},{10,... | collective-permute-start | bytes 884744 | tf_op jit(solution)/shard_map/ppermute | solution.py:493
  21.1 3.8 %collective-permute-start.10 = (bf16[128,768]{1,0:T(8,128)(2,1)S(1)}, bf16[128,768]{1,0:T(8,128)(2,1)S(1)}, u32[]{:S(2)}, u32[]{:S(2)}) collective-permute-start(bf16[128,768]{1,0:T(8,128)(2,1)S(1)} %get-tuple-element.62.refs_1_), channel_id=1, source_target_pairs={{0,1},{1,0},{2,3},{3,2},{4,5},{5,4},{6,7},{7,6},{8,9},{9,8},{10,11... | collective-permute-start | bytes 589832 | tf_op jit(solution)/shard_map/ppermute | solution.py:496
  24.2 1.7 %collective-permute-start.11 = (bf16[128,768]{1,0:T(8,128)(2,1)S(1)}, bf16[128,768]{1,0:T(8,128)(2,1)S(1)}, u32[]{:S(2)}, u32[]{:S(2)}) collective-permute-start(bf16[128,768]{1,0:T(8,128)(2,1)S(1)} %get-tuple-element.65.refs_2_), channel_id=1, source_target_pairs={{0,1},{1,0},{2,3},{3,2},{4,5},{5,4},{6,7},{7,6},{8,9},{9,8},{10,11... | collective-permute-start | bytes 589832 | tf_op jit(solution)/shard_map/ppermute | solution.py:496
  24.3 1.6 %collective-permute-start.12 = (bf16[128,384]{1,0:T(8,128)(2,1)S(1)}, bf16[128,384]{1,0:T(8,128)(2,1)S(1)}, u32[]{:S(2)}, u32[]{:S(2)}) collective-permute-start(bf16[128,384]{1,0:T(8,128)(2,1)S(1)} %get-tuple-element.67), channel_id=1, source_target_pairs={{0,1},{1,0},{2,3},{3,2},{4,5},{5,4},{6,7},{7,6},{8,9},{9,8},{10,11... | collective-permute-start | bytes 294920 | tf_op jit(solution)/shard_map/ppermute | solution.py:496
  28.0 3.8 %collective-permute-start.16 = (bf16[256,768]{1,0:T(8,128)(2,1)S(1)}, bf16[256,768]{1,0:T(8,128)(2,1)S(1)}, u32[]{:S(2)}, u32[]{:S(2)}) collective-permute-start(bf16[256,768]{1,0:T(8,128)(2,1)S(1)} %get-tuple-element.74), channel_id=1, source_target_pairs={{0,1},{1,0},{2,3},{3,2},{4,5},{5,4},{6,7},{7,6},{8,9},{9,8},{10,11... | collective-permute-start | bytes 1179656 | tf_op jit(solution)/shard_map/ppermute | solution.py:496
  28.3 8.3 %collective-permute-start.13 = (bf16[192,384]{1,0:T(8,128)(2,1)S(1)}, bf16[192,384]{1,0:T(8,128)(2,1)S(1)}, u32[]{:S(2)}, u32[]{:S(2)}) collective-permute-start(bf16[192,384]{1,0:T(8,128)(2,1)S(1)} %get-tuple-element.69), channel_id=1, source_target_pairs={{0,2},{2,0},{4,6},{6,4},{8,10},{10,8},{12,14},{14,12},{16,18},{18,... | collective-permute-start | bytes 442376 | tf_op jit(solution)/shard_map/ppermute | solution.py:478
  28.6 8.9 %collective-permute-start.14 = (bf16[192,384]{1,0:T(8,128)(2,1)S(1)}, bf16[192,384]{1,0:T(8,128)(2,1)S(1)}, u32[]{:S(2)}, u32[]{:S(2)}) collective-permute-start(bf16[192,384]{1,0:T(8,128)(2,1)S(1)} %get-tuple-element.70), channel_id=1, source_target_pairs={{0,4},{2,6},{4,0},{6,2},{8,12},{10,14},{12,8},{14,10},{16,20},{18,... | collective-permute-start | bytes 442376 | tf_op jit(solution)/shard_map/ppermute | solution.py:478
  29.8 7.8 %collective-permute-start.15 = (bf16[192,384]{1,0:T(8,128)(2,1)S(1)}, bf16[192,384]{1,0:T(8,128)(2,1)S(1)}, u32[]{:S(2)}, u32[]{:S(2)}) collective-permute-start(bf16[192,384]{1,0:T(8,128)(2,1)S(1)} %get-tuple-element.71), channel_id=1, source_target_pairs={{0,6},{2,4},{4,2},{6,0},{8,14},{10,12},{12,10},{14,8},{16,22},{18,... | collective-permute-start | bytes 442376 | tf_op jit(solution)/shard_map/ppermute | solution.py:478
  35.1 4.2 %collective-permute-start.17 = (bf16[96,128]{1,0:T(8,128)(2,1)S(1)}, bf16[96,128]{1,0:T(8,128)(2,1)S(1)}, u32[]{:S(2)}, u32[]{:S(2)}) collective-permute-start(bf16[96,128]{1,0:T(8,128)(2,1)S(1)} %get-tuple-element.80), channel_id=1, source_target_pairs={{0,7},{1,6},{2,5},{3,4},{4,3},{5,2},{6,1},{7,0},{8,15},{9,14},{10,... | collective-permute-start | bytes 73736 | tf_op jit(solution)/shard_map/ppermute | solution.py:484
  35.3 4.0 %collective-permute-start.18 = (bf16[96,128]{1,0:T(8,128)(2,1)S(1)}, bf16[96,128]{1,0:T(8,128)(2,1)S(1)}, u32[]{:S(2)}, u32[]{:S(2)}) collective-permute-start(bf16[96,128]{1,0:T(8,128)(2,1)S(1)} %get-tuple-element.81), channel_id=1, source_target_pairs={{0,5},{1,4},{2,7},{3,6},{4,1},{5,0},{6,3},{7,2},{8,13},{9,12},{10,... | collective-permute-start | bytes 73736 | tf_op jit(solution)/shard_map/ppermute | solution.py:484
  36.6 3.3 %collective-permute-start.19 = (bf16[96,128]{1,0:T(8,128)(2,1)S(1)}, bf16[96,128]{1,0:T(8,128)(2,1)S(1)}, u32[]{:S(2)}, u32[]{:S(2)}) collective-permute-start(bf16[96,128]{1,0:T(8,128)(2,1)S(1)} %get-tuple-element.82), channel_id=1, source_target_pairs={{0,3},{1,2},{2,1},{3,0},{4,7},{5,6},{6,5},{7,4},{8,11},{9,10},{10,... | collective-permute-start | bytes 73736 | tf_op jit(solution)/shard_map/ppermute | solution.py:484
  37.6 6.1 %collective-permute-start.20 = (bf16[6,8,16,128]{3,2,1,0:T(8,128)(2,1)S(1)}, bf16[6,8,16,128]{3,2,1,0:T(8,128)(2,1)S(1)}, u32[]{:S(2)}, u32[]{:S(2)}) collective-permute-start(bf16[6,8,16,128]{3,2,1,0:T(8,128)(2,1)S(1)} %get-tuple-element.85), channel_id=1, source_target_pairs={{0,9},{1,8},{2,11},{3,10},{4,13},{5,12},{6,15},{7,14},{8,1},{9,0},... | collective-permute-start | bytes 589832 | tf_op jit(solution)/shard_map/ppermute | solution.py:484
  40.1 5.6 %collective-permute-start.21 = (bf16[56,384]{1,0:T(8,128)(2,1)S(1)}, bf16[56,384]{1,0:T(8,128)(2,1)S(1)}, u32[]{:S(2)}, u32[]{:S(2)}) collective-permute-start(bf16[56,384]{1,0:T(8,128)(2,1)S(1)} %get-tuple-element.88), channel_id=1, source_target_pairs={{0,17},{1,16},{2,19},{3,18},{4,21},{5,20},{6,23},{7,22},{8,25},{9,... | collective-permute-start | bytes 129032 | tf_op jit(solution)/shard_map/ppermute | solution.py:484
  41.9 6.2 %collective-permute-start.22 = (bf16[56,384]{1,0:T(8,128)(2,1)S(1)}, bf16[56,384]{1,0:T(8,128)(2,1)S(1)}, u32[]{:S(2)}, u32[]{:S(2)}) collective-permute-start(bf16[56,384]{1,0:T(8,128)(2,1)S(1)} %get-tuple-element.89), channel_id=1, source_target_pairs={{0,25},{1,24},{2,27},{3,26},{4,29},{5,28},{6,31},{7,30},{8,17},{9,... | collective-permute-start | bytes 129032 | tf_op jit(solution)/shard_map/ppermute | solution.py:484
  42.9 5.2 %collective-permute-start.23 = (bf16[56,384]{1,0:T(8,128)(2,1)S(1)}, bf16[56,384]{1,0:T(8,128)(2,1)S(1)}, u32[]{:S(2)}, u32[]{:S(2)}) collective-permute-start(bf16[56,384]{1,0:T(8,128)(2,1)S(1)} %get-tuple-element.90), channel_id=1, source_target_pairs={{0,9},{1,8},{2,11},{3,10},{4,13},{5,12},{6,15},{7,14},{8,1},{9,0},... | collective-permute-start | bytes 129032 | tf_op jit(solution)/shard_map/ppermute | solution.py:484
  48.2 1.5 %collective-permute-start.24 = (f32[48,1280]{1,0:T(8,128)S(1)}, f32[48,1280]{1,0:T(8,128)S(1)}, u32[]{:S(2)}, u32[]{:S(2)}) collective-permute-start(f32[48,1280]{1,0:T(8,128)S(1)} %line_sum.1.mine_ref), channel_id=1, source_target_pairs={{0,1},{1,0},{2,3},{3,2},{4,5},{5,4},{6,7},{7,6},{8,9},{9,8},{10,11... | collective-permute-start | bytes 737288 | tf_op jit(solution)/shard_map/ppermute | solution.py:496
